TPU v7x, 32 devices: a whole 2x2x4 slice. The times are simulated.
32 devices in a mesh: groups: 2 (over y), ep: 8 (over z, x), tp: 2 (over core).
Axes of the slice: x: 2, y: 2, z: 4, core: 2. Of those that a mesh axis runs over, the one named last changes fastest.
Arguments:
- tokens: bfloat16 [1024, 2880], P(('groups', 'ep'), 'tp'), parts along dimension 0, may hold values from -6 to 6
- expert_ids: int32 [1024, 4], P(('groups', 'ep')), parts along dimension 0, may hold values from 0 to 7, all different within a row; in each aligned block of 64 rows (0 to 63, 64 to 127, ...) at most 48 rows name the same one
- gate_probs: float32 [1024, 4], P(('groups', 'ep')), parts along dimension 0, may hold values from 0.05 to 1
- w_gate: bfloat16 [8, 2880, 1440], P('ep', None, 'tp'), may hold values from -0.109375 to 0.109375
- w_up: bfloat16 [8, 2880, 1440], P('ep', None, 'tp'), may hold values from -0.109375 to 0.109375
- w_down: bfloat16 [8, 1440, 2880], P('ep', 'tp'), may hold values from -0.15625 to 0.15625
Outputs:
- mixed: bfloat16 [1024, 2880], P(('groups', 'ep'), 'tp'), parts along dimension 0
There are 2 independent parts, one for each index of `groups`. A program takes and returns all parts, laid end to end along the dimension named above; an argument that names none is the same for every part. Nothing has to cross between parts.
Inputs may be any that keep to these rules, and one draw needn't show every extreme that they name: `expert_ids`: within each block of 64 rows that one index of ep holds, no expert is named by more than 48 rows, and in every draw some expert is named by exactly 48 rows of some block; the numbers of one row differ.
All inputs are finite; a program needn't handle non-finite values.
Results may differ from a plain program's by a relative error of at most 0.0058.
Values may be sent and summed in bfloat16 or wider, within the bound.
No kernel may reach another device: no remote copies, remote signals or barrier semaphores. Data moves between devices by JAX's collectives and lax.ppermute only.
A program may use at most 128 MiB of HBM per device.

v0:
```python
import jax
import jax.numpy as jnp
from jax import lax
from jax.sharding import PartitionSpec as P


def swiglu_expert(rows, gate_part, up_part, down_part):
    gated = jnp.dot(rows, gate_part, preferred_element_type=jnp.float32)
    lifted = jnp.dot(rows, up_part, preferred_element_type=jnp.float32)
    hidden = (jax.nn.silu(gated) * lifted).astype(jnp.bfloat16)
    return jnp.dot(hidden, down_part, preferred_element_type=jnp.float32)


def slot_table(expert_ids, n_experts):
    routed = expert_ids.reshape(-1)
    pair_count = routed.shape[0]
    onehot = (routed[:, None] == jnp.arange(n_experts, dtype=jnp.int32)[None, :]).astype(
        jnp.bfloat16
    )
    row_index = lax.broadcasted_iota(jnp.int32, (pair_count, pair_count), 0)
    col_index = lax.broadcasted_iota(jnp.int32, (pair_count, pair_count), 1)
    earlier = (row_index > col_index).astype(jnp.bfloat16)
    before = jnp.dot(earlier, onehot, preferred_element_type=jnp.float32)
    slots = jnp.sum(before * onehot.astype(jnp.float32), axis=1).astype(jnp.int32)
    return (routed, slots)


def body(tokens, expert_ids, gate_probs, w_gate, w_up, w_down):
    n_experts = lax.axis_size("ep")
    tok_rows, top_count = expert_ids.shape
    capacity = 3 * tok_rows * top_count // (2 * n_experts)
    routed, slots = slot_table(expert_ids, n_experts)
    positions = routed * capacity + slots
    pair_token = jnp.repeat(jnp.arange(tok_rows, dtype=jnp.int32), top_count)
    buffer_rows = n_experts * capacity
    owners = jnp.full((buffer_rows,), tok_rows, jnp.int32).at[positions].set(pair_token)
    half_slots = capacity // 2
    whole_tokens = lax.all_gather(tokens, "tp", axis=1, tiled=True)
    width = whole_tokens.shape[1]
    gate_full, up_full = (
        lax.all_gather(w_gate, "tp", axis=2, tiled=True),
        lax.all_gather(w_up, "tp", axis=2, tiled=True),
    )
    down_full = lax.all_gather(w_down, "tp", axis=1, tiled=True)
    padded = jnp.concatenate([whole_tokens, jnp.zeros((1, width), whole_tokens.dtype)], 0)
    outgoing = padded[owners].reshape(n_experts, capacity, width)
    lane = lax.axis_index("tp")
    mine = lax.dynamic_slice_in_dim(outgoing, lane * half_slots, half_slots, 1)
    block = lax.all_to_all(mine, "ep", split_axis=0, concat_axis=0, tiled=True)
    sources, items, columns = block.shape
    result = swiglu_expert(
        block.reshape(sources * items, columns), gate_full[0], up_full[0], down_full[0]
    )
    result = result.astype(jnp.bfloat16).reshape(sources, items, columns)
    returned = lax.all_to_all(result, "ep", split_axis=0, concat_axis=0, tiled=True)
    received = returned.reshape(n_experts * half_slots, width)
    in_half = slots // half_slots == lane
    local_pos = routed * half_slots + slots % half_slots
    picked = received[local_pos].astype(jnp.float32).reshape(tok_rows, top_count, width)
    weighted = jnp.where(in_half.reshape(tok_rows, top_count), gate_probs, 0.0)
    partial_value = jnp.sum(weighted[:, :, None] * picked, axis=1)
    return lax.psum_scatter(partial_value, "tp", scatter_dimension=1, tiled=True).astype(
        jnp.bfloat16
    )


def solution(mesh):
    in_specs = (
        P(("groups", "ep"), "tp"),
        P(("groups", "ep"), None),
        P(("groups", "ep"), None),
        P("ep", None, "tp"),
        P("ep", None, "tp"),
        P("ep", "tp", None),
    )
    out_specs = P(("groups", "ep"), "tp")
    return jax.shard_map(body, mesh=mesh, in_specs=in_specs, out_specs=out_specs, check_vma=False)
```

profile of v0, /device:TPU:0, one launch (start us, length us, event | category | flops | bytes accessed | tf_op | source)
XLA Modules:
  0.0 152.5 jit_solution(289677251777825991)
XLA Ops:
  6.5 0.0 all-gather.5.cloned.1.call-start
  6.5 0.7 all-gather.5.cloned.1.call-update
  7.3 0.0 all-gather.7.cloned.1.call-start
  7.3 0.7 all-gather.7.cloned.1.call-update
  8.0 0.0 copy-start.1
  8.0 0.0 copy-start
  8.0 0.0 all-gather.9.cloned.1.call-start
  8.1 0.7 all-gather.9.cloned.1.call-update
  8.8 0.0 copy-done.1
  8.8 0.1 copy.23
  8.9 0.1 eq.24
  9.0 0.2 fusion.15
  9.2 0.1 copy.29
  9.3 0.1 mul.55
  9.4 0.1 copy.30
  9.5 0.1 mul.60
  9.6 0.1 reshape.139
  9.7 0.0 copy-done
  9.7 2.2 %all-gather = bf16[2,1440,64]{1,2,0:T(8,128)(2,1)S(1)} all-gather(bf16[1,1440,64]{1,2,0:T(8,128)(2,1)S(1)} %bitcast.41), channel_id=1, replica_groups=mesh['groups'=2,'ep'=8,'tp'=2] {'tp'}, dimensions={0}, use_global_device_ids=true | all-gather | bytes 552960 | tf_op jit(solution)/shard_map/all_gather | solution.py:38
  11.9 0.4 copy.28
  12.3 0.3 reshape.145
  12.7 1.4 scatter_custom_fusion
  14.1 2.9 %gather_fusion = bf16[384,2880]{1,0:T(8,128)(2,1)S(1)} fusion(bf16[65,2880]{1,0:T(8,128)(2,1)S(1)} %concatenate.3, s32[1024]{0:T(1024)S(1)} %pad_clamp_fusion.1), kind=kCustom, calls=%fused_computation | custom fusion | bytes 4425216 | tf_op jit(solution)/shard_map/gather | solution.py:46
  17.0 0.1 constant_dynamic-slice_fusion
  17.1 35.3 %all_to_all.10 = bf16[8,24,2880]{2,1,0:T(8,128)(2,1)S(1)} all-to-all(bf16[8,24,2880]{2,1,0:T(8,128)(2,1)S(1)} %constant_dynamic-slice_fusion), channel_id=1, replica_groups=mesh['groups'=2,'ep'=8,'tp'=2] {'ep'}, dimensions={0} | all-to-all | bytes 2211840 | tf_op jit(solution)/shard_map/all_to_all | solution.py:49
  52.4 0.0 all-gather.5.cloned.1.call-done
  52.4 6.2 %fusion.4 = f32[192,1440]{1,0:T(8,128)S(1)} fusion(bf16[192,2880]{1,0:T(8,128)(2,1)S(1)} %bitcast.38, bf16[1,2880,1440]{1,2,0:T(8,128)(2,1)} %all-gather.5.cloned.1.call-done), kind=kOutput, calls=%fused_computation.7 | convolution fusion | flops 1592524800 | bytes 10506240 | tf_op jit(solution)/shard_map/dot_general | solution.py:8
  58.6 0.0 all-gather.7.cloned.1.call-done
  58.7 20.6 %all-gather.9.cloned.1.call-done = bf16[1,1440,2880]{2,1,0:T(8,128)(2,1)} async-done(((bf16[1,720,2880]{2,1,0:T(8,128)(2,1)}), bf16[1,1440,2880]{2,1,0:T(8,128)(2,1)}) %all-gather.9.cloned.1.call-update) | async-done | bytes 8294416 | tf_op jit(solution)/shard_map/all_gather | solution.py:44
  79.3 11.6 %fusion.6 = bf16[192,2880]{1,0:T(8,128)(2,1)} fusion(bf16[1,1440,2880]{2,1,0:T(8,128)(2,1)} %all-gather.9.cloned.1.call-done, bf16[192,2880]{1,0:T(8,128)(2,1)S(1)} %bitcast.39, bf16[1,2880,1440]{1,2,0:T(8,128)(2,1)} %all-gather.7.cloned.1.call-done, f32[192,1440]{1,0:T(8,128)S(1)} %fusion.4), kind=kOutput, calls=%fused_computation.9 | convolution fusion | flops 3187261440 | bytes 19906560 | tf_op jit(solution)/shard_map/dot_general | solution.py:11
  90.9 0.0 copy-start.2
  90.9 5.9 %all-to-all-start.1 = ((bf16[8,24,2880]{2,1,0:T(8,128)(2,1)}), bf16[8,24,2880]{2,1,0:T(8,128)(2,1)S(1)}, u32[]{:S(2)}, u32[]{:S(2)}) async-start(bf16[8,24,2880]{2,1,0:T(8,128)(2,1)} %bitcast.10), calls=%async_computation.1 | async-start | bytes 2260992 | tf_op jit(solution)/shard_map/all_to_all | solution.py:55
  96.8 0.2 reduce-scatter.4.cloned.1.call-start
  97.0 0.1 div.15
  97.2 0.1 copy.24
  97.3 0.1 and.21
  97.4 0.1 copy.25
  97.5 0.0 copy-done.2
  97.5 0.1 copy.27
  97.6 27.2 %all-to-all-done.1 = bf16[8,24,2880]{2,1,0:T(8,128)(2,1)S(1)} async-done(((bf16[8,24,2880]{2,1,0:T(8,128)(2,1)}), bf16[8,24,2880]{2,1,0:T(8,128)(2,1)S(1)}, u32[]{:S(2)}, u32[]{:S(2)}) %all-to-all-start.1) | async-done | bytes 1105952 | tf_op jit(solution)/shard_map/all_to_all | solution.py:55
  124.8 2.7 %gather_fusion.1 = bf16[256,2880]{1,0:T(8,128)(2,1)} fusion(bf16[192,2880]{1,0:T(8,128)(2,1)S(1)} %bitcast.34, s32[1024]{0:T(1024)S(1)} %pad_clamp_fusion), kind=kCustom, calls=%fused_computation.1 | custom fusion | bytes 2950144 | tf_op jit(solution)/shard_map/gather | solution.py:59
  127.5 2.8 %reshape.118 = f32[64,4,2880]{2,1,0:T(4,128)S(1)} reshape(bf16[256,2880]{1,0:T(8,128)(2,1)} %gather_fusion.1) | data formatting | bytes 4423680 | tf_op jit(solution)/shard_map/convert_element_type | solution.py:59
  130.2 2.9 %multiply_reduce_fusion = f32[64,2880]{1,0:T(8,128)} fusion(f32[64,4,2880]{2,1,0:T(4,128)S(1)} %reshape.118, f32[64,4]{1,0:T(8,128)S(1)} %copy.27), kind=kLoop, calls=%fused_computation.10 | loop fusion | flops 1290240 | bytes 3687424 | tf_op jit(solution)/shard_map/reduce_sum | solution.py:61
  133.2 2.7 %copy.31 = f32[64,2880]{0,1:T(8,128)} copy(f32[64,2880]{1,0:T(8,128)} %multiply_reduce_fusion) | data formatting | bytes 1474560
  135.9 0.0 reduce-scatter.4.cloned.1.call-update
  135.9 8.2 %reduce-scatter.4.cloned.1.call-done = f32[1440,64]{1,0:T(8,128)} async-done(((f32[2880,64]{1,0:T(8,128)}), f32[1440,64]{1,0:T(8,128)}) %reduce-scatter.4.cloned.1.call-update) | async-done | bytes 368656
  144.1 1.9 %copy.32 = bf16[64,1440]{1,0:T(8,128)(2,1)} copy(f32[64,1440]{0,1:T(8,128)} %bitcast.40) | data formatting | bytes 552960
  (11 shorter events, 0.1 us)
Async XLA Ops:
  6.5 45.9 %all-gather.5.cloned.1.call-start = ((), (), s32[]{:S(2)}) async-start(), calls=%async_computation.3 | async-start | bytes 12718080 | tf_op jit(solution)/shard_map/all_gather | solution.py:41
  7.3 51.4 %all-gather.7.cloned.1.call-start = ((), (), s32[]{:S(2)}) async-start(), calls=%async_computation.4 | async-start | bytes 12718080 | tf_op jit(solution)/shard_map/all_gather | solution.py:42
  8.0 0.8 copy-start.1
  8.0 1.7 %copy-start = (bf16[64,1440]{1,0:T(8,128)(2,1)S(1)}, bf16[64,1440]{1,0:T(8,128)(2,1)}, u32[]{:S(2)}) copy-start(bf16[64,1440]{1,0:T(8,128)(2,1)} %param.6) | copy-start | bytes 552964
  8.0 71.3 %all-gather.9.cloned.1.call-start = ((), (), s32[]{:S(2)}) async-start(), calls=%async_computation.5 | async-start | bytes 12718080 | tf_op jit(solution)/shard_map/all_gather | solution.py:44
  90.9 6.6 %copy-start.2 = (f32[64,4]{0,1:T(4,128)S(1)}, f32[64,4]{0,1:T(4,128)}, u32[]{:S(2)}) copy-start(f32[64,4]{0,1:T(4,128)} %param.8) | copy-start | bytes 3076
  90.9 33.9 %all-to-all-start.1 = ((bf16[8,24,2880]{2,1,0:T(8,128)(2,1)}), bf16[8,24,2880]{2,1,0:T(8,128)(2,1)S(1)}, u32[]{:S(2)}, u32[]{:S(2)}) async-start(bf16[8,24,2880]{2,1,0:T(8,128)(2,1)} %bitcast.10), calls=%async_computation.1 | async-start | bytes 2260992 | tf_op jit(solution)/shard_map/all_to_all | solution.py:55
  96.8 47.3 %reduce-scatter.4.cloned.1.call-start = ((), (), s32[]{:S(2)}) async-start(), calls=%async_computation.6 | async-start | bytes 2211840
Sparse Core Ops, SparseCore 0:
  8.9 23.4 all-gather.4
  33.9 21.8 all-gather.6
  57.4 21.8 all-gather.8
  136.0 7.9 reduce-scatter.3
where the time goes:
time: 153 us
  waiting for transfers between devices  58.1 us (38%)
  blocking collectives  37.5 us (25%)
  matrix products  18 us (12%)
  local copies, waits for them, and re-layouts  16.4 us (11%)
  between operations  13.3 us (9%)
  starting transfers between devices  6.19 us (4%)
  other arithmetic  2.99 us (2%)
    all_to_all x1, blocking collectives, body(): block = lax.all_to_all(mine, 'ep', split_axis=0, concat_axis=0, tiled=True)  35.3 us
    all_to_all x1, waiting for transfers between devices, body(): lax.all_to_all(result, 'ep', split_axis=0, concat_axis=0, tiled=True)  27.2 us
    all_gather x1, waiting for transfers between devices, body(): down_full = lax.all_gather(w_down, 'tp', axis=1, tiled=True)  20.6 us
    dot_general x1, matrix products, swiglu_expert(): return jnp.dot(hidden, down_part, preferred_element_type=jnp.float32)  11.6 us
    unnamed x5, waiting for transfers between devices  10.3 us
    dot_general x1, matrix products, swiglu_expert(): gated = jnp.dot(rows, gate_part, preferred_element_type=jnp.float32)  6.2 us
    all_to_all x1, starting transfers between devices, body(): lax.all_to_all(result, 'ep', split_axis=0, concat_axis=0, tiled=True)  5.9 us
    unnamed x10, local copies, waits for them, and re-layouts  5.07 us
  transfers between devices with their start and end apart: 5, of which 3 were waited for; matrix products, arithmetic and copies ran while one was open for 8% of the time, Pallas kernels for 0%

commit v1 on v0

--- a/solution.py
+++ b/solution.py
@@ -1,7 +1,133 @@
+import functools
+
 import jax
 import jax.numpy as jnp
 from jax import lax
+from jax.experimental import pallas as pl
+from jax.experimental.pallas import tpu as pltpu
 from jax.sharding import PartitionSpec as P
+
+ROWS_BY_ROWS = (((1,), (1,)), ((), ()))
+SPLITS = 3
+
+
+def split_gates(expert_ids, gate_probs, n_experts):
+    chosen = expert_ids[:, :, None] == jnp.arange(n_experts, dtype=jnp.int32)[None, None, :]
+    rest = jnp.sum(jnp.where(chosen, gate_probs[:, :, None], 0.0), axis=1)
+    terms = []
+    for _ in range(SPLITS):
+        term = lax.reduce_precision(rest, 8, 7)
+        terms.append(term.astype(jnp.bfloat16))
+        rest = rest - term
+    return jnp.concatenate(terms, axis=1)
+
+
+def expert_kernel(n_blocks, n_experts, place, *refs):
+    own, across = refs[:n_blocks], refs[n_blocks : 2 * n_blocks]
+    w_gate, w_up, w_down, mine, theirs, x = refs[2 * n_blocks :]
+    lane, expert = place[0], place[1]
+    half = mine.shape[1]
+    start = 0
+    for a, b in zip(own, across):
+        span = slice(start, start + a.shape[0])
+        start += a.shape[0]
+
+        @pl.when(lane == 0)
+        def _():
+            x[span, :half] = a[:, :half]
+            x[span, half:] = b[:, :half]
+
+        @pl.when(lane != 0)
+        def _():
+            x[span, :half] = b[:, :half]
+            x[span, half:] = a[:, :half]
+
+    gated = lax.dot_general(x[...], w_gate[...], ROWS_BY_ROWS, preferred_element_type=jnp.float32)
+    lifted = lax.dot_general(x[...], w_up[...], ROWS_BY_ROWS, preferred_element_type=jnp.float32)
+    hidden = (gated / (1.0 + jnp.exp(-gated)) * lifted).astype(jnp.bfloat16)
+    out = jnp.dot(hidden, w_down[...], preferred_element_type=jnp.float32)
+    start = 0
+    for a in own:
+        span = slice(start, start + a.shape[0])
+        start += a.shape[0]
+        terms = a[:, half:].astype(jnp.float32)
+        column = lax.broadcasted_iota(jnp.int32, terms.shape, 1)
+        weight = jnp.sum(jnp.where(lax.rem(column, n_experts) == expert, terms, 0.0), axis=1, keepdims=True)
+        low = (out[span, :half] * weight).astype(jnp.bfloat16)
+        high = (out[span, half:] * weight).astype(jnp.bfloat16)
+
+        @pl.when(lane == 0)
+        def _():
+            mine[span] = low
+            theirs[span] = high
+
+        @pl.when(lane != 0)
+        def _():
+            mine[span] = high
+            theirs[span] = low
+
+
+def run_expert(place, own, across, weights, n_experts):
+    hidden, width = weights[0].shape
+    rows = sum(a.shape[0] for a in own)
+    vmem = pl.BlockSpec(memory_space=pltpu.VMEM)
+    held = [pltpu.with_memory_space_constraint(w, pltpu.VMEM) for w in weights]
+    return pl.pallas_call(
+        functools.partial(expert_kernel, len(own), n_experts),
+        out_shape=[jax.ShapeDtypeStruct((rows, width // 2), jnp.bfloat16)] * 2,
+        in_specs=[pl.BlockSpec(memory_space=pltpu.SMEM)] + [vmem] * (2 * len(own) + 3),
+        out_specs=[vmem] * 2,
+        scratch_shapes=[pltpu.VMEM((rows, width), jnp.bfloat16)],
+        compiler_params=pltpu.CompilerParams(vmem_limit_bytes=24 << 20),
+        cost_estimate=pl.CostEstimate(flops=6 * rows * hidden * width, bytes_accessed=6 * hidden * width, transcendentals=0),
+    )(place, *own, *across, *held)
+
+
+def ring_body(tokens, expert_ids, gate_probs, w_gate, w_up, w_down):
+    n = lax.axis_size("ep")
+    rows, half = tokens.shape
+    order = list(range(0, n, 2)) + list(range(n - 1, 0, -2))
+    ahead = [(order[i], order[(i + 1) % n]) for i in range(n)]
+    back = [(b, a) for a, b in ahead]
+    swap = functools.partial(lax.ppermute, axis_name="tp", perm=[(0, 1), (1, 0)])
+    far = n // 2
+    place = jnp.stack([lax.axis_index("tp"), lax.axis_index("ep")]).astype(jnp.int32)
+    weights = (w_gate[0].T, w_up[0].T, w_down[0])
+    packed = jnp.concatenate([tokens, split_gates(expert_ids, gate_probs, n)], axis=1)
+
+    came = {0: packed}
+    for k in range(1, far):
+        came[k] = lax.ppermute(came[k - 1], "ep", ahead)
+        came[-k] = lax.ppermute(came[1 - k], "ep", back)
+    far_low = lax.ppermute(came[far - 1][: rows // 2], "ep", ahead)
+    far_high = lax.ppermute(came[1 - far][rows // 2 :], "ep", back)
+
+    def expert(blocks):
+        mine, theirs = run_expert(place, blocks, [swap(b) for b in blocks], weights, n)
+        return mine.astype(jnp.float32) + swap(theirs).astype(jnp.float32)
+
+    near = [0] + [s * k for k in range(1, far - 1) for s in (1, -1)]
+    value = {}
+    for group in (near[:3], near[3:]):
+        out = expert([came[k] for k in group])
+        for i, k in enumerate(group):
+            value[k] = out[i * rows : (i + 1) * rows]
+    out = expert([came[far - 1], came[1 - far], far_low, far_high])
+    value[far - 1], value[1 - far] = out[:rows], out[rows : 2 * rows]
+    far_value = out[2 * rows :]
+
+    to_ahead = far_value[: rows // 2].astype(jnp.bfloat16)
+    to_back = far_value[rows // 2 :].astype(jnp.bfloat16)
+    pad_low, pad_high = ((0, rows - rows // 2), (0, 0)), ((rows // 2, 0), (0, 0))
+    for k in range(far - 1, -1, -1):
+        from_behind = lax.ppermute(to_ahead, "ep", ahead).astype(jnp.float32)
+        from_front = lax.ppermute(to_back, "ep", back).astype(jnp.float32)
+        if k == far - 1:
+            from_behind, from_front = jnp.pad(from_behind, pad_low), jnp.pad(from_front, pad_high)
+        if k:
+            to_ahead = (value[-k] + from_behind).astype(jnp.bfloat16)
+            to_back = (value[k] + from_front).astype(jnp.bfloat16)
+    return (value[0] + from_behind + from_front).astype(jnp.bfloat16)
 
 
 def swiglu_expert(rows, gate_part, up_part, down_part):
@@ -25,7 +151,7 @@
     return (routed, slots)
 
 
-def body(tokens, expert_ids, gate_probs, w_gate, w_up, w_down):
+def slot_body(tokens, expert_ids, gate_probs, w_gate, w_up, w_down):
     n_experts = lax.axis_size("ep")
     tok_rows, top_count = expert_ids.shape
     capacity = 3 * tok_rows * top_count // (2 * n_experts)
@@ -74,4 +200,10 @@
         P("ep", "tp", None),
     )
     out_specs = P(("groups", "ep"), "tp")
+
+    def body(tokens, expert_ids, *rest):
+        n, top = lax.axis_size("ep"), expert_ids.shape[1]
+        small = n <= 4 * top and n % 2 == 0 and n >= 6 and lax.axis_size("tp") == 2
+        return (ring_body if small else slot_body)(tokens, expert_ids, *rest)
+
     return jax.shard_map(body, mesh=mesh, in_specs=in_specs, out_specs=out_specs, check_vma=False)

time: 153 us -> 82.6 us (0.54)
  blocking collectives: 37.5 us -> 0 us
  waiting for transfers between devices: 58.1 us -> 36.3 us
  matrix products: 18 us -> 0 us
  Pallas kernels: 0 us -> 15.6 us
  starting transfers between devices: 6.19 us -> 20.1 us
  between operations: 13.3 us -> 0.14 us
  local copies, waits for them, and re-layouts: 16.4 us -> 7.93 us
    ppermute x0 -> x28, waiting for transfers between devices: none -> 36.3 us  [the longest x4 12.8 us: ring_body(): from_behind = lax.ppermute(to_ahead, 'ep', ahead).astype(jnp.float32)]
    all_to_all x1 -> x0, blocking collectives: 35.3 us -> none  [body(): block = lax.all_to_all(mine, 'ep', split_axis=0, concat_axis=0, tiled=True)]
    all_to_all x1 -> x0, waiting for transfers between devices: 27.2 us -> none  [body(): lax.all_to_all(result, 'ep', split_axis=0, concat_axis=0, tiled=True)]
    all_gather x3 -> x0, waiting for transfers between devices: 20.7 us -> none  [the longest x1 20.6 us: body(): down_full = lax.all_gather(w_down, 'tp', axis=1, tiled=True)]
    ppermute x0 -> x28, starting transfers between devices: none -> 20.1 us  [the longest x4 6.43 us: ring_body(): from_behind = lax.ppermute(to_ahead, 'ep', ahead).astype(jnp.float32)]
    dot_general x3 -> x0, matrix products: 18 us -> none  [the longest x1 11.6 us: swiglu_expert(): return jnp.dot(hidden, down_part, preferred_element_type=jnp.float32)]
    pallas_call x0 -> x3, Pallas kernels: none -> 15.6 us  [run_expert(): pl.pallas_call(functools.partial(expert_kernel, len(own), n_experts), out...]
    unnamed x5 -> x0, waiting for transfers between devices: 10.3 us -> none
  transfers between devices with their start and end apart: 5 -> 28, of which waited for: 3 -> 15; matrix products, arithmetic and copies ran while one was open for 8% -> 1% of each run, Pallas kernels for 0% -> 12%
where the time goes in v1:
time: 82.6 us; the launch traced here: 82.3 us
  waiting for transfers between devices  36.3 us (44%)
  starting transfers between devices  20.1 us (24%)
  Pallas kernels  15.6 us (19%)
  local copies, waits for them, and re-layouts  7.93 us (10%)
  other arithmetic  2.24 us (3%)
    pallas_call x3, Pallas kernels, run_expert(): pl.pallas_call(functools.partial(expert_kernel, len(own), n_experts), out...  15.6 us
    ppermute x4, waiting for transfers between devices, ring_body(): from_behind = lax.ppermute(to_ahead, 'ep', ahead).astype(jnp.float32)  12.8 us
    ppermute x3, waiting for transfers between devices, ring_body(): came[k] = lax.ppermute(came[k - 1], 'ep', ahead)  12.6 us
    unnamed x10, local copies, waits for them, and re-layouts  6.61 us
    ppermute x4, starting transfers between devices, ring_body(): from_behind = lax.ppermute(to_ahead, 'ep', ahead).astype(jnp.float32)  6.43 us
    ppermute x3, starting transfers between devices, ring_body(): came[k] = lax.ppermute(came[k - 1], 'ep', ahead)  6.41 us
    ppermute x4, waiting for transfers between devices, ring_body(): from_front = lax.ppermute(to_back, 'ep', back).astype(jnp.float32)  4.09 us
    ppermute x9, waiting for transfers between devices, expert(): swap(b)  3.06 us
  transfers between devices with their start and end apart: 28, of which 15 were waited for; matrix products, arithmetic and copies ran while one was open for 1% of the time, Pallas kernels for 12%

profile of v1, /device:TPU:0, one launch (start us, length us, event | category | flops | bytes accessed | tf_op | source)
XLA Modules:
  0.0 82.3 jit_solution(6485494507167541298)
XLA Ops:
  0.0 0.7 select_reduce_fusion
  0.7 0.1 copy.11
  0.8 0.1 copy.12
  0.9 0.1 copy.13
  1.0 1.0 %concatenate.3.refs_0_ = bf16[64,1464]{1,0:T(8,128)(2,1)S(1)} concatenate(bf16[64,1440]{1,0:T(8,128)(2,1)} %param.6, bf16[64,8]{1,0:T(8,128)(2,1)S(1)} %copy.13, bf16[64,8]{1,0:T(8,128)(2,1)S(1)} %get-tuple-element.28, bf16[64,8]{1,0:T(8,128)(2,1)S(1)} %get-tuple-element.27), dimensions={1} | concatenate | bytes 374784 | tf_op jit(solution)/shard_map/concatenate | solution.py:96
  2.0 3.1 %collective-permute-start = (bf16[64,1464]{1,0:T(8,128)(2,1)S(1)}, bf16[64,1464]{1,0:T(8,128)(2,1)S(1)}, u32[]{:S(2)}, u32[]{:S(2)}) collective-permute-start(bf16[64,1464]{1,0:T(8,128)(2,1)S(1)} %concatenate.3.refs_0_), channel_id=1, source_target_pairs={{0,4},{4,8},{8,12},{12,14},{14,10},{10,6},{6,2},{2,0},{1,5},{5,9},... | collective-permute-start | bytes 562184 | tf_op jit(solution)/shard_map/ppermute | solution.py:100
  5.1 4.8 %collective-permute-done.refs_1_ = bf16[64,1464]{1,0:T(8,128)(2,1)S(1)} collective-permute-done((bf16[64,1464]{1,0:T(8,128)(2,1)S(1)}, bf16[64,1464]{1,0:T(8,128)(2,1)S(1)}, u32[]{:S(2)}, u32[]{:S(2)}) %collective-permute-start) | collective-permute-done | bytes 187424 | tf_op jit(solution)/shard_map/ppermute | solution.py:100
  9.9 1.8 %collective-permute-start.6 = (bf16[64,1464]{1,0:T(8,128)(2,1)S(1)}, bf16[64,1464]{1,0:T(8,128)(2,1)S(1)}, u32[]{:S(2)}, u32[]{:S(2)}) collective-permute-start(bf16[64,1464]{1,0:T(8,128)(2,1)S(1)} %collective-permute-done.refs_1_), channel_id=1, source_target_pairs={{0,4},{4,8},{8,12},{12,14},{14,10},{10,6},{6,2},{2,0},{1,5},{5,9},... | collective-permute-start | bytes 562184 | tf_op jit(solution)/shard_map/ppermute | solution.py:100
  11.7 0.2 collective-permute-start.7
  11.9 4.1 %collective-permute-done.6.refs_0_ = bf16[64,1464]{1,0:T(8,128)(2,1)S(1)} collective-permute-done((bf16[64,1464]{1,0:T(8,128)(2,1)S(1)}, bf16[64,1464]{1,0:T(8,128)(2,1)S(1)}, u32[]{:S(2)}, u32[]{:S(2)}) %collective-permute-start.6) | collective-permute-done | bytes 187424 | tf_op jit(solution)/shard_map/ppermute | solution.py:100
  16.0 1.5 %collective-permute-start.11 = (bf16[64,1464]{1,0:T(8,128)(2,1)S(1)}, bf16[64,1464]{1,0:T(8,128)(2,1)S(1)}, u32[]{:S(2)}, u32[]{:S(2)}) collective-permute-start(bf16[64,1464]{1,0:T(8,128)(2,1)S(1)} %collective-permute-done.6.refs_0_), channel_id=1, source_target_pairs={{0,4},{4,8},{8,12},{12,14},{14,10},{10,6},{6,2},{2,0},{1,5},{5,9},... | collective-permute-start | bytes 562184 | tf_op jit(solution)/shard_map/ppermute | solution.py:100
  17.5 0.0 collective-permute-done.7.refs_1_
  17.5 0.5 collective-permute-start.12
  18.0 3.7 %collective-permute-done.11.refs_0_ = bf16[64,1464]{1,0:T(8,128)(2,1)S(1)} collective-permute-done((bf16[64,1464]{1,0:T(8,128)(2,1)S(1)}, bf16[64,1464]{1,0:T(8,128)(2,1)S(1)}, u32[]{:S(2)}, u32[]{:S(2)}) %collective-permute-start.11) | collective-permute-done | bytes 187424 | tf_op jit(solution)/shard_map/ppermute | solution.py:100
  21.8 1.9 %collective-permute-start.13 = (bf16[32,1464]{1,0:T(8,128)(2,1)S(1)}, bf16[32,1464]{1,0:T(8,128)(2,1)S(1)}, u32[]{:S(2)}, u32[]{:S(2)}) collective-permute-start(bf16[32,1464]{1,0:T(8,128)(2,1)S(1)} %slice.52), channel_id=1, source_target_pairs={{0,4},{4,8},{8,12},{12,14},{14,10},{10,6},{6,2},{2,0},{1,5},{5,9},... | collective-permute-start | bytes 281096 | tf_op jit(solution)/shard_map/ppermute | solution.py:102
  23.6 0.4 collective-permute-start.14
  24.1 0.0 collective-permute-start.15
  24.1 0.5 collective-permute-start.16
  24.6 1.9 %collective-permute-done.13.refs_2_ = bf16[32,1464]{1,0:T(8,128)(2,1)S(1)} collective-permute-done((bf16[32,1464]{1,0:T(8,128)(2,1)S(1)}, bf16[32,1464]{1,0:T(8,128)(2,1)S(1)}, u32[]{:S(2)}, u32[]{:S(2)}) %collective-permute-start.13) | collective-permute-done | bytes 93728 | tf_op jit(solution)/shard_map/ppermute | solution.py:102
  26.4 0.0 collective-permute-start.17
  26.4 1.9 %collective-permute-done.14.refs_3_ = bf16[32,1464]{1,0:T(8,128)(2,1)S(1)} collective-permute-done((bf16[32,1464]{1,0:T(8,128)(2,1)S(1)}, bf16[32,1464]{1,0:T(8,128)(2,1)S(1)}, u32[]{:S(2)}, u32[]{:S(2)}) %collective-permute-start.14) | collective-permute-done | bytes 93728 | tf_op jit(solution)/shard_map/ppermute | solution.py:103
  28.3 0.0 collective-permute-start.18
  28.3 0.1 pad_add_fusion.place
  28.4 0.0 collective-permute-done.17.refs_6_
  28.4 1.2 %collective-permute-done.18.refs_7_ = bf16[32,1464]{1,0:T(8,128)(2,1)S(1)} collective-permute-done((bf16[32,1464]{1,0:T(8,128)(2,1)S(1)}, bf16[32,1464]{1,0:T(8,128)(2,1)S(1)}, u32[]{:S(2)}, u32[]{:S(2)}) %collective-permute-start.18) | collective-permute-done | bytes 93728 | tf_op jit(solution)/shard_map/ppermute | solution.py:106
  29.6 2.2 %copy-done = bf16[1,2880,720]{1,2,0:T(8,128)(2,1)S(1)} copy-done((bf16[1,2880,720]{1,2,0:T(8,128)(2,1)S(1)}, bf16[1,2880,720]{1,2,0:T(8,128)(2,1)}, u32[]{:S(2)}) %copy-start) | copy-done | bytes 4147224
  31.8 2.2 %copy-done.1 = bf16[1,2880,720]{1,2,0:T(8,128)(2,1)S(1)} copy-done((bf16[1,2880,720]{1,2,0:T(8,128)(2,1)S(1)}, bf16[1,2880,720]{1,2,0:T(8,128)(2,1)}, u32[]{:S(2)}) %copy-start.1) | copy-done | bytes 4147224
  34.0 2.2 %copy-done.2 = bf16[1,720,2880]{2,1,0:T(8,128)(2,1)S(1)} copy-done((bf16[1,720,2880]{2,1,0:T(8,128)(2,1)S(1)}, bf16[1,720,2880]{2,1,0:T(8,128)(2,1)}, u32[]{:S(2)}) %copy-start.2) | copy-done | bytes 4147224
  36.2 5.6 %shard_map.66 = (bf16[192,1440]{1,0:T(8,128)(2,1)S(1)}, bf16[192,1440]{1,0:T(8,128)(2,1)S(1)}) custom-call(s32[2]{0:T(128)S(1)} %pad_add_fusion.place, bf16[64,1464]{1,0:T(8,128)(2,1)S(1)} %collective-permute-done.11.refs_0_, bf16[64,1464]{1,0:T(8,128)(2,1)S(1)} %collective-permute-done.12.refs_1_, bf16[32,1464]{1,0:T(8,128)(2,1)S(1)} %collective-permute-done.13.refs_2_, ...), custom_call_target="tpu_custom_call" | custom-call | flops 2388787200 | bytes 12441600 | tf_op jit(solution)/shard_map/pallas_call | solution.py:75
  41.8 0.2 collective-permute-start.19
  42.0 0.3 collective-permute-start.2
  42.4 0.2 collective-permute-start.3
  42.5 0.3 collective-permute-start.4
  42.9 1.3 %collective-permute-done.2.refs_3_ = bf16[64,1464]{1,0:T(8,128)(2,1)S(1)} collective-permute-done((bf16[64,1464]{1,0:T(8,128)(2,1)S(1)}, bf16[64,1464]{1,0:T(8,128)(2,1)S(1)}, u32[]{:S(2)}, u32[]{:S(2)}) %collective-permute-start.2) | collective-permute-done | bytes 187424 | tf_op jit(solution)/shard_map/ppermute | solution.py:106
  44.2 0.3 collective-permute-done.3.refs_4_
  44.4 0.3 collective-permute-done.4.refs_5_
  44.7 5.3 %shard_map.64 = (bf16[192,1440]{1,0:T(8,128)(2,1)S(1)}, bf16[192,1440]{1,0:T(8,128)(2,1)S(1)}) custom-call(s32[2]{0:T(128)S(1)} %pad_add_fusion.place, bf16[64,1464]{1,0:T(8,128)(2,1)S(1)} %concatenate.3.refs_0_, bf16[64,1464]{1,0:T(8,128)(2,1)S(1)} %collective-permute-done.refs_1_, bf16[64,1464]{1,0:T(8,128)(2,1)S(1)} %collective-permute-done.1.refs_2_, ...), custom_call_target="tpu_custom_call" | custom-call | flops 2388787200 | bytes 12441600 | tf_op jit(solution)/shard_map/pallas_call | solution.py:75
  50.0 0.2 collective-permute-start.5
  50.2 0.3 collective-permute-start.8
  50.6 0.2 collective-permute-start.9
  50.8 0.2 fusion.10
  51.0 1.6 %collective-permute-start.20 = (bf16[32,1440]{1,0:T(8,128)(2,1)S(1)}, bf16[32,1440]{1,0:T(8,128)(2,1)S(1)}, u32[]{:S(2)}, u32[]{:S(2)}) collective-permute-start(bf16[32,1440]{1,0:T(8,128)(2,1)S(1)} %get-tuple-element.25), channel_id=1, source_target_pairs={{0,4},{4,8},{8,12},{12,14},{14,10},{10,6},{6,2},{2,0},{1,5},{5,9},... | collective-permute-start | bytes 276488 | tf_op jit(solution)/shard_map/ppermute | solution.py:123
  52.6 0.4 collective-permute-start.24
  53.1 0.0 collective-permute-done.8.refs_2_
  53.1 4.8 %shard_map.65 = (bf16[128,1440]{1,0:T(8,128)(2,1)S(1)}, bf16[128,1440]{1,0:T(8,128)(2,1)S(1)}) custom-call(s32[2]{0:T(128)S(1)} %pad_add_fusion.place, bf16[64,1464]{1,0:T(8,128)(2,1)S(1)} %collective-permute-done.6.refs_0_, bf16[64,1464]{1,0:T(8,128)(2,1)S(1)} %collective-permute-done.7.refs_1_, bf16[64,1464]{1,0:T(8,128)(2,1)S(1)} %collective-permute-done.8.refs_2_, ...), custom_call_target="tpu_custom_call" | custom-call | flops 1592524800 | bytes 12441600 | tf_op jit(solution)/shard_map/pallas_call | solution.py:75
  57.8 0.1 collective-permute-start.10
  57.9 0.1 fusion.3
  58.0 1.6 %collective-permute-start.21 = (bf16[64,1440]{1,0:T(8,128)(2,1)S(1)}, bf16[64,1440]{1,0:T(8,128)(2,1)S(1)}, u32[]{:S(2)}, u32[]{:S(2)}) collective-permute-start(bf16[64,1440]{1,0:T(8,128)(2,1)S(1)} %get-tuple-element.19), channel_id=1, source_target_pairs={{0,4},{4,8},{8,12},{12,14},{14,10},{10,6},{6,2},{2,0},{1,5},{5,9},... | collective-permute-start | bytes 552968 | tf_op jit(solution)/shard_map/ppermute | solution.py:123
  59.6 0.4 collective-permute-start.25
  60.1 0.1 convert_add_fusion.2
  60.2 5.2 %collective-permute-done.21 = bf16[64,1440]{1,0:T(8,128)(2,1)S(1)} collective-permute-done((bf16[64,1440]{1,0:T(8,128)(2,1)S(1)}, bf16[64,1440]{1,0:T(8,128)(2,1)S(1)}, u32[]{:S(2)}, u32[]{:S(2)}) %collective-permute-start.21) | collective-permute-done | bytes 184352 | tf_op jit(solution)/shard_map/ppermute | solution.py:123
  65.3 1.3 %collective-permute-done.25 = bf16[64,1440]{1,0:T(8,128)(2,1)S(1)} collective-permute-done((bf16[64,1440]{1,0:T(8,128)(2,1)S(1)}, bf16[64,1440]{1,0:T(8,128)(2,1)S(1)}, u32[]{:S(2)}, u32[]{:S(2)}) %collective-permute-start.25) | collective-permute-done | bytes 184352 | tf_op jit(solution)/shard_map/ppermute | solution.py:124
  66.6 0.1 fusion.4
  66.7 1.6 %collective-permute-start.22 = (bf16[64,1440]{1,0:T(8,128)(2,1)S(1)}, bf16[64,1440]{1,0:T(8,128)(2,1)S(1)}, u32[]{:S(2)}, u32[]{:S(2)}) collective-permute-start(bf16[64,1440]{1,0:T(8,128)(2,1)S(1)} %get-tuple-element.23), channel_id=1, source_target_pairs={{0,4},{4,8},{8,12},{12,14},{14,10},{10,6},{6,2},{2,0},{1,5},{5,9},... | collective-permute-start | bytes 552968 | tf_op jit(solution)/shard_map/ppermute | solution.py:123
  68.4 0.4 collective-permute-start.26
  68.8 0.2 convert_add_fusion.1
  69.0 4.0 %collective-permute-done.22 = bf16[64,1440]{1,0:T(8,128)(2,1)S(1)} collective-permute-done((bf16[64,1440]{1,0:T(8,128)(2,1)S(1)}, bf16[64,1440]{1,0:T(8,128)(2,1)S(1)}, u32[]{:S(2)}, u32[]{:S(2)}) %collective-permute-start.22) | collective-permute-done | bytes 184352 | tf_op jit(solution)/shard_map/ppermute | solution.py:123
  73.0 1.3 %collective-permute-done.26 = bf16[64,1440]{1,0:T(8,128)(2,1)S(1)} collective-permute-done((bf16[64,1440]{1,0:T(8,128)(2,1)S(1)}, bf16[64,1440]{1,0:T(8,128)(2,1)S(1)}, u32[]{:S(2)}, u32[]{:S(2)}) %collective-permute-start.26) | collective-permute-done | bytes 184352 | tf_op jit(solution)/shard_map/ppermute | solution.py:124
  74.3 0.1 fusion.5
  74.4 1.5 %collective-permute-start.23 = (bf16[64,1440]{1,0:T(8,128)(2,1)S(1)}, bf16[64,1440]{1,0:T(8,128)(2,1)S(1)}, u32[]{:S(2)}, u32[]{:S(2)}) collective-permute-start(bf16[64,1440]{1,0:T(8,128)(2,1)S(1)} %get-tuple-element.17), channel_id=1, source_target_pairs={{0,4},{4,8},{8,12},{12,14},{14,10},{10,6},{6,2},{2,0},{1,5},{5,9},... | collective-permute-start | bytes 552968 | tf_op jit(solution)/shard_map/ppermute | solution.py:123
  75.9 0.5 collective-permute-start.27
  76.4 3.6 %collective-permute-done.23 = bf16[64,1440]{1,0:T(8,128)(2,1)S(1)} collective-permute-done((bf16[64,1440]{1,0:T(8,128)(2,1)S(1)}, bf16[64,1440]{1,0:T(8,128)(2,1)S(1)}, u32[]{:S(2)}, u32[]{:S(2)}) %collective-permute-start.23) | collective-permute-done | bytes 184352 | tf_op jit(solution)/shard_map/ppermute | solution.py:123
  80.1 1.5 %collective-permute-done.27 = bf16[64,1440]{1,0:T(8,128)(2,1)S(1)} collective-permute-done((bf16[64,1440]{1,0:T(8,128)(2,1)S(1)}, bf16[64,1440]{1,0:T(8,128)(2,1)S(1)}, u32[]{:S(2)}, u32[]{:S(2)}) %collective-permute-start.27) | collective-permute-done | bytes 184352 | tf_op jit(solution)/shard_map/ppermute | solution.py:124
  81.6 0.8 fusion.7
  (24 shorter events, 0.1 us)
Async XLA Ops:
  2.0 7.9 %collective-permute-start = (bf16[64,1464]{1,0:T(8,128)(2,1)S(1)}, bf16[64,1464]{1,0:T(8,128)(2,1)S(1)}, u32[]{:S(2)}, u32[]{:S(2)}) collective-permute-start(bf16[64,1464]{1,0:T(8,128)(2,1)S(1)} %concatenate.3.refs_0_), channel_id=1, source_target_pairs={{0,4},{4,8},{8,12},{12,14},{14,10},{10,6},{6,2},{2,0},{1,5},{5,9},... | collective-permute-start | bytes 562184 | tf_op jit(solution)/shard_map/ppermute | solution.py:100
  5.1 6.6 %collective-permute-start.1 = (bf16[64,1464]{1,0:T(8,128)(2,1)S(1)}, bf16[64,1464]{1,0:T(8,128)(2,1)S(1)}, u32[]{:S(2)}, u32[]{:S(2)}) collective-permute-start(bf16[64,1464]{1,0:T(8,128)(2,1)S(1)} %concatenate.3.refs_0_), channel_id=1, source_target_pairs={{4,0},{8,4},{12,8},{14,12},{10,14},{6,10},{2,6},{0,2},{5,1},{9,5},... | collective-permute-start | bytes 562184 | tf_op jit(solution)/shard_map/ppermute | solution.py:101
  9.9 6.1 %collective-permute-start.6 = (bf16[64,1464]{1,0:T(8,128)(2,1)S(1)}, bf16[64,1464]{1,0:T(8,128)(2,1)S(1)}, u32[]{:S(2)}, u32[]{:S(2)}) collective-permute-start(bf16[64,1464]{1,0:T(8,128)(2,1)S(1)} %collective-permute-done.refs_1_), channel_id=1, source_target_pairs={{0,4},{4,8},{8,12},{12,14},{14,10},{10,6},{6,2},{2,0},{1,5},{5,9},... | collective-permute-start | bytes 562184 | tf_op jit(solution)/shard_map/ppermute | solution.py:100
  11.7 5.8 %collective-permute-start.7 = (bf16[64,1464]{1,0:T(8,128)(2,1)S(1)}, bf16[64,1464]{1,0:T(8,128)(2,1)S(1)}, u32[]{:S(2)}, u32[]{:S(2)}) collective-permute-start(bf16[64,1464]{1,0:T(8,128)(2,1)S(1)} %collective-permute-done.1.refs_2_), channel_id=1, source_target_pairs={{4,0},{8,4},{12,8},{14,12},{10,14},{6,10},{2,6},{0,2},{5,1},{9,5},... | collective-permute-start | bytes 562184 | tf_op jit(solution)/shard_map/ppermute | solution.py:101
  16.0 5.7 %collective-permute-start.11 = (bf16[64,1464]{1,0:T(8,128)(2,1)S(1)}, bf16[64,1464]{1,0:T(8,128)(2,1)S(1)}, u32[]{:S(2)}, u32[]{:S(2)}) collective-permute-start(bf16[64,1464]{1,0:T(8,128)(2,1)S(1)} %collective-permute-done.6.refs_0_), channel_id=1, source_target_pairs={{0,4},{4,8},{8,12},{12,14},{14,10},{10,6},{6,2},{2,0},{1,5},{5,9},... | collective-permute-start | bytes 562184 | tf_op jit(solution)/shard_map/ppermute | solution.py:100
  17.5 6.1 %collective-permute-start.12 = (bf16[64,1464]{1,0:T(8,128)(2,1)S(1)}, bf16[64,1464]{1,0:T(8,128)(2,1)S(1)}, u32[]{:S(2)}, u32[]{:S(2)}) collective-permute-start(bf16[64,1464]{1,0:T(8,128)(2,1)S(1)} %collective-permute-done.7.refs_1_), channel_id=1, source_target_pairs={{4,0},{8,4},{12,8},{14,12},{10,14},{6,10},{2,6},{0,2},{5,1},{9,5},... | collective-permute-start | bytes 562184 | tf_op jit(solution)/shard_map/ppermute | solution.py:101
  21.8 4.7 %collective-permute-start.13 = (bf16[32,1464]{1,0:T(8,128)(2,1)S(1)}, bf16[32,1464]{1,0:T(8,128)(2,1)S(1)}, u32[]{:S(2)}, u32[]{:S(2)}) collective-permute-start(bf16[32,1464]{1,0:T(8,128)(2,1)S(1)} %slice.52), channel_id=1, source_target_pairs={{0,4},{4,8},{8,12},{12,14},{14,10},{10,6},{6,2},{2,0},{1,5},{5,9},... | collective-permute-start | bytes 281096 | tf_op jit(solution)/shard_map/ppermute | solution.py:102
  23.6 21.1 %slice-start = ((s8[4239360]{0:T(1024)(128)(4,1)}), s8[45056]{0:T(1024)(128)(4,1)S(1)}, s32[]{:S(2)}) async-start(s8[4239360]{0:T(1024)(128)(4,1)} %bitcast.10), calls=%async_computation | async-start | bytes 90112
  23.6 4.7 %collective-permute-start.14 = (bf16[32,1464]{1,0:T(8,128)(2,1)S(1)}, bf16[32,1464]{1,0:T(8,128)(2,1)S(1)}, u32[]{:S(2)}, u32[]{:S(2)}) collective-permute-start(bf16[32,1464]{1,0:T(8,128)(2,1)S(1)} %slice.53), channel_id=1, source_target_pairs={{4,0},{8,4},{12,8},{14,12},{10,14},{6,10},{2,6},{0,2},{5,1},{9,5},... | collective-permute-start | bytes 281096 | tf_op jit(solution)/shard_map/ppermute | solution.py:103
  24.1 5.6 %collective-permute-start.15 = (bf16[64,1464]{1,0:T(8,128)(2,1)S(1)}, bf16[64,1464]{1,0:T(8,128)(2,1)S(1)}, u32[]{:S(2)}, u32[]{:S(2)}) collective-permute-start(bf16[64,1464]{1,0:T(8,128)(2,1)S(1)} %collective-permute-done.11.refs_0_), channel_id=1, source_target_pairs={{0,1},{1,0},{2,3},{3,2},{4,5},{5,4},{6,7},{7,6},{8,9},{9,8},{10,11... | collective-permute-start | bytes 562184 | tf_op jit(solution)/shard_map/ppermute | solution.py:106
  24.1 5.6 %collective-permute-start.16 = (bf16[64,1464]{1,0:T(8,128)(2,1)S(1)}, bf16[64,1464]{1,0:T(8,128)(2,1)S(1)}, u32[]{:S(2)}, u32[]{:S(2)}) collective-permute-start(bf16[64,1464]{1,0:T(8,128)(2,1)S(1)} %collective-permute-done.12.refs_1_), channel_id=1, source_target_pairs={{0,1},{1,0},{2,3},{3,2},{4,5},{5,4},{6,7},{7,6},{8,9},{9,8},{10,11... | collective-permute-start | bytes 562184 | tf_op jit(solution)/shard_map/ppermute | solution.py:106
  26.4 2.0 %collective-permute-start.17 = (bf16[32,1464]{1,0:T(8,128)(2,1)S(1)}, bf16[32,1464]{1,0:T(8,128)(2,1)S(1)}, u32[]{:S(2)}, u32[]{:S(2)}) collective-permute-start(bf16[32,1464]{1,0:T(8,128)(2,1)S(1)} %collective-permute-done.13.refs_2_), channel_id=1, source_target_pairs={{0,1},{1,0},{2,3},{3,2},{4,5},{5,4},{6,7},{7,6},{8,9},{9,8},{10,11... | collective-permute-start | bytes 281096 | tf_op jit(solution)/shard_map/ppermute | solution.py:106
  28.3 1.3 %collective-permute-start.18 = (bf16[32,1464]{1,0:T(8,128)(2,1)S(1)}, bf16[32,1464]{1,0:T(8,128)(2,1)S(1)}, u32[]{:S(2)}, u32[]{:S(2)}) collective-permute-start(bf16[32,1464]{1,0:T(8,128)(2,1)S(1)} %collective-permute-done.14.refs_3_), channel_id=1, source_target_pairs={{0,1},{1,0},{2,3},{3,2},{4,5},{5,4},{6,7},{7,6},{8,9},{9,8},{10,11... | collective-permute-start | bytes 281096 | tf_op jit(solution)/shard_map/ppermute | solution.py:106
  29.6 2.2 %copy-start = (bf16[1,2880,720]{1,2,0:T(8,128)(2,1)S(1)}, bf16[1,2880,720]{1,2,0:T(8,128)(2,1)}, u32[]{:S(2)}) copy-start(bf16[1,2880,720]{1,2,0:T(8,128)(2,1)} %param.9) | copy-start | bytes 12441604
  31.8 2.2 %copy-start.1 = (bf16[1,2880,720]{1,2,0:T(8,128)(2,1)S(1)}, bf16[1,2880,720]{1,2,0:T(8,128)(2,1)}, u32[]{:S(2)}) copy-start(bf16[1,2880,720]{1,2,0:T(8,128)(2,1)} %param.10) | copy-start | bytes 12441604
  34.0 2.2 %copy-start.2 = (bf16[1,720,2880]{2,1,0:T(8,128)(2,1)S(1)}, bf16[1,720,2880]{2,1,0:T(8,128)(2,1)}, u32[]{:S(2)}) copy-start(bf16[1,720,2880]{2,1,0:T(8,128)(2,1)} %param.11) | copy-start | bytes 12441604
  36.2 8.5 %slice-start.1 = ((s8[4239360]{0:T(1024)(128)(4,1)}), s8[4194304]{0:T(1024)(128)(4,1)S(1)}, s32[]{:S(2)}) async-start(s8[4239360]{0:T(1024)(128)(4,1)} %bitcast.10), calls=%async_computation.1 | async-start | bytes 8388608
  41.8 9.0 %collective-permute-start.19 = (bf16[192,1440]{1,0:T(8,128)(2,1)S(1)}, bf16[192,1440]{1,0:T(8,128)(2,1)S(1)}, u32[]{:S(2)}, u32[]{:S(2)}) collective-permute-start(bf16[192,1440]{1,0:T(8,128)(2,1)S(1)} %get-tuple-element.16), channel_id=1, source_target_pairs={{0,1},{1,0},{2,3},{3,2},{4,5},{5,4},{6,7},{7,6},{8,9},{9,8},{10,11... | collective-permute-start | bytes 1658888 | tf_op jit(solution)/shard_map/ppermute | solution.py:107
  42.0 2.1 %collective-permute-start.2 = (bf16[64,1464]{1,0:T(8,128)(2,1)S(1)}, bf16[64,1464]{1,0:T(8,128)(2,1)S(1)}, u32[]{:S(2)}, u32[]{:S(2)}) collective-permute-start(bf16[64,1464]{1,0:T(8,128)(2,1)S(1)} %concatenate.3.refs_0_), channel_id=1, source_target_pairs={{0,1},{1,0},{2,3},{3,2},{4,5},{5,4},{6,7},{7,6},{8,9},{9,8},{10,11... | collective-permute-start | bytes 562184 | tf_op jit(solution)/shard_map/ppermute | solution.py:106
  42.4 2.1 %collective-permute-start.3 = (bf16[64,1464]{1,0:T(8,128)(2,1)S(1)}, bf16[64,1464]{1,0:T(8,128)(2,1)S(1)}, u32[]{:S(2)}, u32[]{:S(2)}) collective-permute-start(bf16[64,1464]{1,0:T(8,128)(2,1)S(1)} %collective-permute-done.refs_1_), channel_id=1, source_target_pairs={{0,1},{1,0},{2,3},{3,2},{4,5},{5,4},{6,7},{7,6},{8,9},{9,8},{10,11... | collective-permute-start | bytes 562184 | tf_op jit(solution)/shard_map/ppermute | solution.py:106
  42.5 2.2 %collective-permute-start.4 = (bf16[64,1464]{1,0:T(8,128)(2,1)S(1)}, bf16[64,1464]{1,0:T(8,128)(2,1)S(1)}, u32[]{:S(2)}, u32[]{:S(2)}) collective-permute-start(bf16[64,1464]{1,0:T(8,128)(2,1)S(1)} %collective-permute-done.1.refs_2_), channel_id=1, source_target_pairs={{0,1},{1,0},{2,3},{3,2},{4,5},{5,4},{6,7},{7,6},{8,9},{9,8},{10,11... | collective-permute-start | bytes 562184 | tf_op jit(solution)/shard_map/ppermute | solution.py:106
  50.0 18.8 %collective-permute-start.5 = (bf16[192,1440]{1,0:T(8,128)(2,1)S(1)}, bf16[192,1440]{1,0:T(8,128)(2,1)S(1)}, u32[]{:S(2)}, u32[]{:S(2)}) collective-permute-start(bf16[192,1440]{1,0:T(8,128)(2,1)S(1)} %get-tuple-element.12), channel_id=1, source_target_pairs={{0,1},{1,0},{2,3},{3,2},{4,5},{5,4},{6,7},{7,6},{8,9},{9,8},{10,11... | collective-permute-start | bytes 1658888 | tf_op jit(solution)/shard_map/ppermute | solution.py:107
  50.2 2.8 %collective-permute-start.8 = (bf16[64,1464]{1,0:T(8,128)(2,1)S(1)}, bf16[64,1464]{1,0:T(8,128)(2,1)S(1)}, u32[]{:S(2)}, u32[]{:S(2)}) collective-permute-start(bf16[64,1464]{1,0:T(8,128)(2,1)S(1)} %collective-permute-done.6.refs_0_), channel_id=1, source_target_pairs={{0,1},{1,0},{2,3},{3,2},{4,5},{5,4},{6,7},{7,6},{8,9},{9,8},{10,11... | collective-permute-start | bytes 562184 | tf_op jit(solution)/shard_map/ppermute | solution.py:106
  50.6 2.5 %collective-permute-start.9 = (bf16[64,1464]{1,0:T(8,128)(2,1)S(1)}, bf16[64,1464]{1,0:T(8,128)(2,1)S(1)}, u32[]{:S(2)}, u32[]{:S(2)}) collective-permute-start(bf16[64,1464]{1,0:T(8,128)(2,1)S(1)} %collective-permute-done.7.refs_1_), channel_id=1, source_target_pairs={{0,1},{1,0},{2,3},{3,2},{4,5},{5,4},{6,7},{7,6},{8,9},{9,8},{10,11... | collective-permute-start | bytes 562184 | tf_op jit(solution)/shard_map/ppermute | solution.py:106
  51.0 6.9 %collective-permute-start.20 = (bf16[32,1440]{1,0:T(8,128)(2,1)S(1)}, bf16[32,1440]{1,0:T(8,128)(2,1)S(1)}, u32[]{:S(2)}, u32[]{:S(2)}) collective-permute-start(bf16[32,1440]{1,0:T(8,128)(2,1)S(1)} %get-tuple-element.25), channel_id=1, source_target_pairs={{0,4},{4,8},{8,12},{12,14},{14,10},{10,6},{6,2},{2,0},{1,5},{5,9},... | collective-permute-start | bytes 276488 | tf_op jit(solution)/shard_map/ppermute | solution.py:123
  52.6 5.3 %collective-permute-start.24 = (bf16[32,1440]{1,0:T(8,128)(2,1)S(1)}, bf16[32,1440]{1,0:T(8,128)(2,1)S(1)}, u32[]{:S(2)}, u32[]{:S(2)}) collective-permute-start(bf16[32,1440]{1,0:T(8,128)(2,1)S(1)} %get-tuple-element.26), channel_id=1, source_target_pairs={{4,0},{8,4},{12,8},{14,12},{10,14},{6,10},{2,6},{0,2},{5,1},{9,5},... | collective-permute-start | bytes 276488 | tf_op jit(solution)/shard_map/ppermute | solution.py:124
  57.8 2.3 %collective-permute-start.10 = (bf16[128,1440]{1,0:T(8,128)(2,1)S(1)}, bf16[128,1440]{1,0:T(8,128)(2,1)S(1)}, u32[]{:S(2)}, u32[]{:S(2)}) collective-permute-start(bf16[128,1440]{1,0:T(8,128)(2,1)S(1)} %get-tuple-element.14), channel_id=1, source_target_pairs={{0,1},{1,0},{2,3},{3,2},{4,5},{5,4},{6,7},{7,6},{8,9},{9,8},{10,11... | collective-permute-start | bytes 1105928 | tf_op jit(solution)/shard_map/ppermute | solution.py:107
  58.0 7.3 %collective-permute-start.21 = (bf16[64,1440]{1,0:T(8,128)(2,1)S(1)}, bf16[64,1440]{1,0:T(8,128)(2,1)S(1)}, u32[]{:S(2)}, u32[]{:S(2)}) collective-permute-start(bf16[64,1440]{1,0:T(8,128)(2,1)S(1)} %get-tuple-element.19), channel_id=1, source_target_pairs={{0,4},{4,8},{8,12},{12,14},{14,10},{10,6},{6,2},{2,0},{1,5},{5,9},... | collective-permute-start | bytes 552968 | tf_op jit(solution)/shard_map/ppermute | solution.py:123
  59.6 7.0 %collective-permute-start.25 = (bf16[64,1440]{1,0:T(8,128)(2,1)S(1)}, bf16[64,1440]{1,0:T(8,128)(2,1)S(1)}, u32[]{:S(2)}, u32[]{:S(2)}) collective-permute-start(bf16[64,1440]{1,0:T(8,128)(2,1)S(1)} %get-tuple-element.20), channel_id=1, source_target_pairs={{4,0},{8,4},{12,8},{14,12},{10,14},{6,10},{2,6},{0,2},{5,1},{9,5},... | collective-permute-start | bytes 552968 | tf_op jit(solution)/shard_map/ppermute | solution.py:124
  66.7 6.2 %collective-permute-start.22 = (bf16[64,1440]{1,0:T(8,128)(2,1)S(1)}, bf16[64,1440]{1,0:T(8,128)(2,1)S(1)}, u32[]{:S(2)}, u32[]{:S(2)}) collective-permute-start(bf16[64,1440]{1,0:T(8,128)(2,1)S(1)} %get-tuple-element.23), channel_id=1, source_target_pairs={{0,4},{4,8},{8,12},{12,14},{14,10},{10,6},{6,2},{2,0},{1,5},{5,9},... | collective-permute-start | bytes 552968 | tf_op jit(solution)/shard_map/ppermute | solution.py:123
  68.4 5.9 %collective-permute-start.26 = (bf16[64,1440]{1,0:T(8,128)(2,1)S(1)}, bf16[64,1440]{1,0:T(8,128)(2,1)S(1)}, u32[]{:S(2)}, u32[]{:S(2)}) collective-permute-start(bf16[64,1440]{1,0:T(8,128)(2,1)S(1)} %get-tuple-element.24), channel_id=1, source_target_pairs={{4,0},{8,4},{12,8},{14,12},{10,14},{6,10},{2,6},{0,2},{5,1},{9,5},... | collective-permute-start | bytes 552968 | tf_op jit(solution)/shard_map/ppermute | solution.py:124
  74.4 5.7 %collective-permute-start.23 = (bf16[64,1440]{1,0:T(8,128)(2,1)S(1)}, bf16[64,1440]{1,0:T(8,128)(2,1)S(1)}, u32[]{:S(2)}, u32[]{:S(2)}) collective-permute-start(bf16[64,1440]{1,0:T(8,128)(2,1)S(1)} %get-tuple-element.17), channel_id=1, source_target_pairs={{0,4},{4,8},{8,12},{12,14},{14,10},{10,6},{6,2},{2,0},{1,5},{5,9},... | collective-permute-start | bytes 552968 | tf_op jit(solution)/shard_map/ppermute | solution.py:123
  75.9 5.7 %collective-permute-start.27 = (bf16[64,1440]{1,0:T(8,128)(2,1)S(1)}, bf16[64,1440]{1,0:T(8,128)(2,1)S(1)}, u32[]{:S(2)}, u32[]{:S(2)}) collective-permute-start(bf16[64,1440]{1,0:T(8,128)(2,1)S(1)} %get-tuple-element.18), channel_id=1, source_target_pairs={{4,0},{8,4},{12,8},{14,12},{10,14},{6,10},{2,6},{0,2},{5,1},{9,5},... | collective-permute-start | bytes 552968 | tf_op jit(solution)/shard_map/ppermute | solution.py:124

commit v2 on v0

--- a/solution.py
+++ b/solution.py
@@ -1,7 +1,196 @@
+import functools
+
 import jax
 import jax.numpy as jnp
 from jax import lax
+from jax.experimental import pallas as pl
+from jax.experimental.pallas import tpu as pltpu
 from jax.sharding import PartitionSpec as P
+
+SPLITS = 3
+
+
+def in_vmem(shape, dtype=jnp.bfloat16):
+    return pltpu.MemorySpace.VMEM(shape, dtype)
+
+
+def hold(x):
+    return pltpu.with_memory_space_constraint(x, pltpu.VMEM)
+
+
+def after(x, done):
+    return lax.optimization_barrier((x, done))[0]
+
+
+def pack_kernel(n_experts, tokens, ids, probs, packed):
+    top, rows = ids.shape
+    half = tokens.shape[1]
+    packed[:, :half] = tokens[...]
+    expert = lax.broadcasted_iota(jnp.int32, (n_experts, rows), 0)
+    rest = jnp.zeros((n_experts, rows), jnp.float32)
+    for k in range(top):
+        rest += jnp.where(ids[k : k + 1, :] == expert, probs[k : k + 1, :], 0.0)
+    terms = []
+    for _ in range(SPLITS):
+        term = rest.astype(jnp.bfloat16).astype(jnp.float32)
+        terms.append(term)
+        rest = rest - term
+    packed[:, half:] = jnp.concatenate(terms, axis=0).T.astype(jnp.bfloat16)
+
+
+def pack(tokens, expert_ids, gate_probs, n_experts):
+    rows, half = tokens.shape
+    return pl.pallas_call(
+        functools.partial(pack_kernel, n_experts),
+        out_shape=in_vmem((rows, half + SPLITS * n_experts)),
+        compiler_params=pltpu.CompilerParams(vmem_limit_bytes=8 << 20),
+    )(tokens, expert_ids.T, gate_probs.T)
+
+
+def load_kernel(place, gate_in, up_in, down_in, gate, up, down_mine, down_theirs, done, gate_buf, up_buf, down_buf, sems):
+    lane = place[0]
+    half = down_mine.shape[1]
+    copies = [
+        pltpu.make_async_copy(src, dst, sems.at[i])
+        for i, (src, dst) in enumerate(((gate_in, gate_buf), (up_in, up_buf), (down_in, down_buf)))
+    ]
+    for copy in copies:
+        copy.start()
+    copies[0].wait()
+    gate[...] = gate_buf[...].T
+    copies[1].wait()
+    up[...] = up_buf[...].T
+    copies[2].wait()
+
+    @pl.when(lane == 0)
+    def _():
+        down_mine[...] = down_buf[:, :half]
+        down_theirs[...] = down_buf[:, half:]
+
+    @pl.when(lane != 0)
+    def _():
+        down_mine[...] = down_buf[:, half:]
+        down_theirs[...] = down_buf[:, :half]
+
+    done[...] = jnp.zeros_like(done)
+
+
+def load_weights(place, w_gate, w_up, w_down):
+    hidden, width = w_down.shape
+    return pl.pallas_call(
+        load_kernel,
+        out_shape=[in_vmem((width, hidden))] * 2 + [in_vmem((hidden, width // 2))] * 2 + [in_vmem((8, 128), jnp.float32)],
+        in_specs=[pl.BlockSpec(memory_space=pltpu.SMEM)] + [pl.BlockSpec(memory_space=pltpu.HBM)] * 3,
+        out_specs=[pl.BlockSpec(memory_space=pltpu.VMEM)] * 5,
+        scratch_shapes=[pltpu.VMEM((hidden, width), jnp.bfloat16)] * 3 + [pltpu.SemaphoreType.DMA((3,))],
+        compiler_params=pltpu.CompilerParams(vmem_limit_bytes=32 << 20),
+        cost_estimate=pl.CostEstimate(flops=0, bytes_accessed=12 * hidden * width, transcendentals=0),
+    )(place, *[pltpu.with_memory_space_constraint(w, pltpu.HBM) for w in (w_gate.T, w_up.T, w_down)])
+
+
+def expert_kernel(n_blocks, n_experts, place, *refs):
+    own, across = refs[:n_blocks], refs[n_blocks : 2 * n_blocks]
+    w_gate, w_up, down_mine, down_theirs, mine, theirs, x_own, x_across = refs[2 * n_blocks :]
+    lane, expert = place[0], place[1]
+    half = mine.shape[1]
+    spans, start = [], 0
+    for a, b in zip(own, across):
+        spans.append(slice(start, start + a.shape[0]))
+        x_own[spans[-1], :] = a[:, :half]
+        x_across[spans[-1], :] = b[:, :half]
+        start += a.shape[0]
+    here = pl.ds(pl.multiple_of(lane * half, 16), half)
+    there = pl.ds(pl.multiple_of((1 - lane) * half, 16), half)
+
+    def project(w):
+        near = jnp.dot(x_own[...], w[here, :], preferred_element_type=jnp.float32)
+        return near + jnp.dot(x_across[...], w[there, :], preferred_element_type=jnp.float32)
+
+    gated = project(w_gate)
+    lifted = project(w_up)
+    hidden = (gated / (1.0 + jnp.exp(-gated)) * lifted).astype(jnp.bfloat16)
+    weights = []
+    for a in own:
+        terms = a[:, half:].astype(jnp.float32)
+        column = lax.broadcasted_iota(jnp.int32, terms.shape, 1)
+        weights.append(jnp.sum(jnp.where(lax.rem(column, n_experts) == expert, terms, 0.0), axis=1, keepdims=True))
+    for w, out in ((down_theirs, theirs), (down_mine, mine)):
+        value = jnp.dot(hidden, w[...], preferred_element_type=jnp.float32)
+        for span, weight in zip(spans, weights):
+            out[span] = (value[span] * weight).astype(jnp.bfloat16)
+
+
+def run_expert(place, own, across, weights, n_experts):
+    width, hidden = weights[0].shape
+    rows = sum(a.shape[0] for a in own)
+    vmem = pl.BlockSpec(memory_space=pltpu.VMEM)
+    return pl.pallas_call(
+        functools.partial(expert_kernel, len(own), n_experts),
+        out_shape=[in_vmem((rows, width // 2))] * 2,
+        in_specs=[pl.BlockSpec(memory_space=pltpu.SMEM)] + [vmem] * (2 * len(own) + 4),
+        out_specs=[vmem] * 2,
+        scratch_shapes=[pltpu.VMEM((rows, width // 2), jnp.bfloat16)] * 2,
+        compiler_params=pltpu.CompilerParams(vmem_limit_bytes=16 << 20),
+        cost_estimate=pl.CostEstimate(flops=6 * rows * hidden * width, bytes_accessed=6 * hidden * width, transcendentals=0),
+    )(place, *[hold(a) for a in own], *[hold(a) for a in across], *[hold(w) for w in weights])
+
+
+def ring_body(tokens, expert_ids, gate_probs, w_gate, w_up, w_down):
+    n = lax.axis_size("ep")
+    rows = tokens.shape[0]
+    order = list(range(0, n, 2)) + list(range(n - 1, 0, -2))
+    ahead = [(order[i], order[(i + 1) % n]) for i in range(n)]
+    back = [(b, a) for a, b in ahead]
+    swap = functools.partial(lax.ppermute, axis_name="tp", perm=[(0, 1), (1, 0)])
+    far = n // 2
+    place = jnp.stack([lax.axis_index("tp"), lax.axis_index("ep")]).astype(jnp.int32)
+    packed = pack(tokens, expert_ids, gate_probs, n)
+    *weights, loaded = load_weights(after(place, packed), w_gate[0], w_up[0], w_down[0])
+
+    came, across, value = {0: packed}, {}, {}
+
+    def run(keys, wait_for=None):
+        at = place if wait_for is None else after(place, wait_for)
+        mine, theirs = run_expert(at, [came[k] for k in keys], [across[k] for k in keys], weights, n)
+        theirs = swap(theirs)
+        start = 0
+        for k in keys:
+            span = slice(start, start + came[k].shape[0])
+            start = span.stop
+            value[k] = mine[span].astype(jnp.float32) + theirs[span].astype(jnp.float32)
+        return mine
+
+    hidden_work = loaded
+    for k in range(1, far):
+        came[k] = lax.ppermute(after(came[k - 1], hidden_work) if k > 1 else packed, "ep", ahead)
+        came[-k] = lax.ppermute(after(came[1 - k], hidden_work) if k > 1 else packed, "ep", back)
+        across[k - 1] = swap(came[k - 1])
+        if k > 1:
+            across[1 - k] = swap(came[1 - k])
+            hidden_work = run([0] if k == 2 else [k - 2, 2 - k])
+    far_keys = ("low", "high")
+    came["low"] = lax.ppermute(after(came[far - 1], hidden_work)[: rows // 2], "ep", ahead)
+    came["high"] = lax.ppermute(after(came[1 - far], hidden_work)[rows // 2 :], "ep", back)
+    for k in (far - 1, 1 - far, *far_keys):
+        across[k] = swap(came[k])
+    run(far_keys)
+
+    to_ahead = value["low"].astype(jnp.bfloat16)
+    to_back = value["high"].astype(jnp.bfloat16)
+    run([far - 1, 1 - far], (to_ahead, to_back))
+    pad_low, pad_high = ((0, rows - rows // 2), (0, 0)), ((rows // 2, 0), (0, 0))
+    for k in range(far - 1, -1, -1):
+        behind = lax.ppermute(to_ahead, "ep", ahead)
+        front = lax.ppermute(to_back, "ep", back)
+        if k == far - 1:
+            run([far - 2, 2 - far], (behind, front))
+        behind, front = behind.astype(jnp.float32), front.astype(jnp.float32)
+        if k == far - 1:
+            behind, front = jnp.pad(behind, pad_low), jnp.pad(front, pad_high)
+        if k:
+            to_ahead = (value[-k] + behind).astype(jnp.bfloat16)
+            to_back = (value[k] + front).astype(jnp.bfloat16)
+    return (value[0] + behind + front).astype(jnp.bfloat16)
 
 
 def swiglu_expert(rows, gate_part, up_part, down_part):
@@ -25,7 +214,7 @@
     return (routed, slots)
 
 
-def body(tokens, expert_ids, gate_probs, w_gate, w_up, w_down):
+def slot_body(tokens, expert_ids, gate_probs, w_gate, w_up, w_down):
     n_experts = lax.axis_size("ep")
     tok_rows, top_count = expert_ids.shape
     capacity = 3 * tok_rows * top_count // (2 * n_experts)
@@ -74,4 +263,10 @@
         P("ep", "tp", None),
     )
     out_specs = P(("groups", "ep"), "tp")
+
+    def body(tokens, expert_ids, *rest):
+        n, top = lax.axis_size("ep"), expert_ids.shape[1]
+        small = n <= 4 * top and n % 2 == 0 and n >= 6 and lax.axis_size("tp") == 2
+        return (ring_body if small else slot_body)(tokens, expert_ids, *rest)
+
     return jax.shard_map(body, mesh=mesh, in_specs=in_specs, out_specs=out_specs, check_vma=False)

time: 153 us -> 75.8 us (0.50)
  blocking collectives: 37.5 us -> 0 us
  waiting for transfers between devices: 58.1 us -> 31.1 us
  Pallas kernels: 0 us -> 20.9 us
  matrix products: 18 us -> 0 us
  local copies, waits for them, and re-layouts: 16.4 us -> 2.3 us
  starting transfers between devices: 6.19 us -> 19.8 us
  between operations: 13.3 us -> 0.13 us
  other arithmetic: 2.99 us -> 1.32 us
    all_to_all x1 -> x0, blocking collectives: 35.3 us -> none  [body(): block = lax.all_to_all(mine, 'ep', split_axis=0, concat_axis=0, tiled=True)]
    ppermute x0 -> x30, waiting for transfers between devices: none -> 31.1 us  [the longest x4 12.9 us: ring_body(): behind = lax.ppermute(to_ahead, 'ep', ahead)]
    all_to_all x1 -> x0, waiting for transfers between devices: 27.2 us -> none  [body(): lax.all_to_all(result, 'ep', split_axis=0, concat_axis=0, tiled=True)]
    pallas_call x0 -> x7, Pallas kernels: none -> 20.9 us  [the longest x5 14.2 us: run_expert(): pl.pallas_call(functools.partial(expert_kernel, len(own), n_experts), out...]
    all_gather x3 -> x0, waiting for transfers between devices: 20.7 us -> none  [the longest x1 20.6 us: body(): down_full = lax.all_gather(w_down, 'tp', axis=1, tiled=True)]
    ppermute x0 -> x30, starting transfers between devices: none -> 19.8 us  [the longest x3 6.94 us: ring_body(): lax.ppermute(after(came[k - 1], hidden_work) if k > 1 else packed, 'ep',...]
    dot_general x3 -> x0, matrix products: 18 us -> none  [the longest x1 11.6 us: swiglu_expert(): return jnp.dot(hidden, down_part, preferred_element_type=jnp.float32)]
    unnamed x5 -> x0, waiting for transfers between devices: 10.3 us -> none
  transfers between devices with their start and end apart: 5 -> 30, of which waited for: 3 -> 16; matrix products, arithmetic and copies ran while one was open for 8% -> 1% of each run, Pallas kernels for 0% -> 20%
where the time goes in v2:
time: 75.8 us; the launch traced here: 75.6 us
  waiting for transfers between devices  31.1 us (41%)
  Pallas kernels  20.9 us (28%)
  starting transfers between devices  19.8 us (26%)
  local copies, waits for them, and re-layouts  2.3 us (3%)
  other arithmetic  1.32 us (2%)
    pallas_call x5, Pallas kernels, run_expert(): pl.pallas_call(functools.partial(expert_kernel, len(own), n_experts), out...  14.2 us
    ppermute x4, waiting for transfers between devices, ring_body(): behind = lax.ppermute(to_ahead, 'ep', ahead)  12.9 us
    ppermute x4, waiting for transfers between devices, ring_body(): front = lax.ppermute(to_back, 'ep', back)  7.45 us
    ppermute x3, starting transfers between devices, ring_body(): lax.ppermute(after(came[k - 1], hidden_work) if k > 1 else packed, 'ep',...  6.94 us
    pallas_call x1, Pallas kernels, load_weights(): pl.pallas_call(load_kernel, out_shape=[in_vmem((width, hidden))] * 2 + [i...  6.61 us
    ppermute x4, starting transfers between devices, ring_body(): behind = lax.ppermute(to_ahead, 'ep', ahead)  6.25 us
    ppermute x3, waiting for transfers between devices, ring_body(): lax.ppermute(after(came[k - 1], hidden_work) if k > 1 else packed, 'ep',...  3.84 us
    ppermute x1, waiting for transfers between devices, ring_body(): lax.ppermute(after(came[far - 1], hidden_work)[:rows // 2], 'ep', ahead)  2.34 us
  transfers between devices with their start and end apart: 30, of which 16 were waited for; matrix products, arithmetic and copies ran while one was open for 1% of the time, Pallas kernels for 20%

profile of v2, /device:TPU:0, one launch (start us, length us, event | category | flops | bytes accessed | tf_op | source)
XLA Modules:
  0.0 75.6 jit_solution(6015588732810064652)
XLA Ops:
  0.0 0.9 %copy-done = bf16[64,1440]{1,0:T(8,128)(2,1)S(1)} copy-done((bf16[64,1440]{1,0:T(8,128)(2,1)S(1)}, bf16[64,1440]{1,0:T(8,128)(2,1)}, u32[]{:S(2)}) %copy-start) | copy-done | bytes 184344
  0.9 0.7 copy-done.1
  1.6 0.7 copy-done.2
  2.3 0.2 shard_map.64.refs_0_
  2.5 3.0 %collective-permute-start.2 = (bf16[64,1464]{1,0:T(8,128)(2,1)S(1)}, bf16[64,1464]{1,0:T(8,128)(2,1)S(1)}, u32[]{:S(2)}, u32[]{:S(2)}) collective-permute-start(bf16[64,1464]{1,0:T(8,128)(2,1)S(1)} %shard_map.64.refs_0_), channel_id=1, source_target_pairs={{0,4},{4,8},{8,12},{12,14},{14,10},{10,6},{6,2},{2,0},{1,5},{5,9},... | collective-permute-start | bytes 562184 | tf_op jit(solution)/shard_map/ppermute | solution.py:165
  5.5 0.0 collective-permute-start.3
  5.5 0.0 collective-permute-start
  5.5 0.1 pad_add_fusion.place
  5.6 6.6 %shard_map.65 = (bf16[2880,720]{1,0:T(8,128)(2,1)S(1)}, bf16[2880,720]{1,0:T(8,128)(2,1)S(1)}, bf16[720,1440]{1,0:T(8,128)(2,1)S(1)}, bf16[720,1440]{1,0:T(8,128)(2,1)S(1)}, f32[8,128]{1,0:T(8,128)}) custom-call(s32[2]{0:T(128)S(1)} %pad_add_fusion.place, bf16[720,2880]{1,0:T(8,128)(2,1)} %bitcast.13, bf16[720,2880]{1,0:T(8,128)(2,1)} %bitcast.14, ...), custom_call_target="tpu_custom_call" | custom-call | bytes 24883200 | tf_op jit(solution)/shard_map/pallas_call | solution.py:80
  12.2 2.1 %collective-permute-start.7 = (bf16[64,1464]{1,0:T(8,128)(2,1)S(1)}, bf16[64,1464]{1,0:T(8,128)(2,1)S(1)}, u32[]{:S(2)}, u32[]{:S(2)}) collective-permute-start(bf16[64,1464]{1,0:T(8,128)(2,1)S(1)} %collective-permute-done.2.refs_0_), channel_id=1, source_target_pairs={{0,4},{4,8},{8,12},{12,14},{14,10},{10,6},{6,2},{2,0},{1,5},{5,9},... | collective-permute-start | bytes 562184 | tf_op jit(solution)/shard_map/ppermute | solution.py:165
  14.3 0.0 collective-permute-done.3.refs_1_
  14.3 0.0 collective-permute-start.10
  14.3 0.2 collective-permute-start.4
  14.5 0.3 collective-permute-start.5
  14.8 0.0 collective-permute-done.refs_1_
  14.8 3.0 %shard_map.66 = (bf16[64,1440]{1,0:T(8,128)(2,1)S(1)}, bf16[64,1440]{1,0:T(8,128)(2,1)S(1)}) custom-call(s32[2]{0:T(128)S(1)} %pad_add_fusion.place, bf16[64,1464]{1,0:T(8,128)(2,1)S(1)} %shard_map.64.refs_0_, bf16[64,1464]{1,0:T(8,128)(2,1)S(1)} %collective-permute-done.refs_1_, bf16[2880,720]{1,0:T(8,128)(2,1)S(1)} %get-tuple-element.30.refs_2_.refs_4_, ...), custom_call_target="tpu_custom_call" | custom-call | flops 796262400 | bytes 12441600 | tf_op jit(solution)/shard_map/pallas_call | solution.py:127
  17.8 1.9 %collective-permute-done.7.refs_0_ = bf16[64,1464]{1,0:T(8,128)(2,1)S(1)} collective-permute-done((bf16[64,1464]{1,0:T(8,128)(2,1)S(1)}, bf16[64,1464]{1,0:T(8,128)(2,1)S(1)}, u32[]{:S(2)}, u32[]{:S(2)}) %collective-permute-start.7) | collective-permute-done | bytes 187424 | tf_op jit(solution)/shard_map/ppermute | solution.py:165
  19.8 1.8 %collective-permute-start.8 = (bf16[64,1464]{1,0:T(8,128)(2,1)S(1)}, bf16[64,1464]{1,0:T(8,128)(2,1)S(1)}, u32[]{:S(2)}, u32[]{:S(2)}) collective-permute-start(bf16[64,1464]{1,0:T(8,128)(2,1)S(1)} %collective-permute-done.7.refs_0_), channel_id=1, source_target_pairs={{0,4},{4,8},{8,12},{12,14},{14,10},{10,6},{6,2},{2,0},{1,5},{5,9},... | collective-permute-start | bytes 562184 | tf_op jit(solution)/shard_map/ppermute | solution.py:165
  21.6 0.0 collective-permute-done.10.refs_1_
  21.6 0.2 collective-permute-start.11
  21.8 0.0 collective-permute-done.4.refs_2_
  21.8 2.7 %shard_map.67 = (bf16[128,1440]{1,0:T(8,128)(2,1)S(1)}, bf16[128,1440]{1,0:T(8,128)(2,1)S(1)}) custom-call(s32[2]{0:T(128)S(1)} %pad_add_fusion.place, bf16[64,1464]{1,0:T(8,128)(2,1)S(1)} %collective-permute-done.2.refs_0_, bf16[64,1464]{1,0:T(8,128)(2,1)S(1)} %collective-permute-done.3.refs_1_, bf16[64,1464]{1,0:T(8,128)(2,1)S(1)} %collective-permute-done.4.refs_2_, ...), custom_call_target="tpu_custom_call" | custom-call | flops 1592524800 | bytes 12441600 | tf_op jit(solution)/shard_map/pallas_call | solution.py:127
  24.5 1.9 %collective-permute-done.8.refs_0_ = bf16[64,1464]{1,0:T(8,128)(2,1)S(1)} collective-permute-done((bf16[64,1464]{1,0:T(8,128)(2,1)S(1)}, bf16[64,1464]{1,0:T(8,128)(2,1)S(1)}, u32[]{:S(2)}, u32[]{:S(2)}) %collective-permute-start.8) | collective-permute-done | bytes 187424 | tf_op jit(solution)/shard_map/ppermute | solution.py:165
  26.4 1.8 %collective-permute-start.9 = (bf16[32,1464]{1,0:T(8,128)(2,1)S(1)}, bf16[32,1464]{1,0:T(8,128)(2,1)S(1)}, u32[]{:S(2)}, u32[]{:S(2)}) collective-permute-start(bf16[32,1464]{1,0:T(8,128)(2,1)S(1)} %slice.56), channel_id=1, source_target_pairs={{0,4},{4,8},{8,12},{12,14},{14,10},{10,6},{6,2},{2,0},{1,5},{5,9},... | collective-permute-start | bytes 281096 | tf_op jit(solution)/shard_map/ppermute | solution.py:172
  28.2 0.6 collective-permute-start.12
  28.8 2.3 %collective-permute-done.9.refs_0_ = bf16[32,1464]{1,0:T(8,128)(2,1)S(1)} collective-permute-done((bf16[32,1464]{1,0:T(8,128)(2,1)S(1)}, bf16[32,1464]{1,0:T(8,128)(2,1)S(1)}, u32[]{:S(2)}, u32[]{:S(2)}) %collective-permute-start.9) | collective-permute-done | bytes 93728 | tf_op jit(solution)/shard_map/ppermute | solution.py:172
  31.1 1.9 %collective-permute-done.12.refs_1_ = bf16[32,1464]{1,0:T(8,128)(2,1)S(1)} collective-permute-done((bf16[32,1464]{1,0:T(8,128)(2,1)S(1)}, bf16[32,1464]{1,0:T(8,128)(2,1)S(1)}, u32[]{:S(2)}, u32[]{:S(2)}) %collective-permute-start.12) | collective-permute-done | bytes 93728 | tf_op jit(solution)/shard_map/ppermute | solution.py:173
  33.1 0.0 collective-permute-start.14
  33.1 0.0 collective-permute-done.13.refs_2_
  33.1 1.3 %collective-permute-done.14.refs_3_ = bf16[32,1464]{1,0:T(8,128)(2,1)S(1)} collective-permute-done((bf16[32,1464]{1,0:T(8,128)(2,1)S(1)}, bf16[32,1464]{1,0:T(8,128)(2,1)S(1)}, u32[]{:S(2)}, u32[]{:S(2)}) %collective-permute-start.14) | collective-permute-done | bytes 93728 | tf_op jit(solution)/shard_map/ppermute | solution.py:175
  34.4 3.0 %shard_map.68 = (bf16[64,1440]{1,0:T(8,128)(2,1)S(1)}, bf16[64,1440]{1,0:T(8,128)(2,1)S(1)}) custom-call(s32[2]{0:T(128)S(1)} %pad_add_fusion.place, bf16[32,1464]{1,0:T(8,128)(2,1)S(1)} %collective-permute-done.9.refs_0_, bf16[32,1464]{1,0:T(8,128)(2,1)S(1)} %collective-permute-done.12.refs_1_, bf16[32,1464]{1,0:T(8,128)(2,1)S(1)} %collective-permute-done.13.refs_2_, ...), custom_call_target="tpu_custom_call" | custom-call | flops 796262400 | bytes 12441600 | tf_op jit(solution)/shard_map/pallas_call | solution.py:127
  37.4 0.2 collective-permute-start.15
  37.6 0.4 collective-permute-start.21
  38.0 0.1 collective-permute-start.22
  38.1 0.8 %collective-permute-done.15 = bf16[64,1440]{1,0:T(8,128)(2,1)S(1)} collective-permute-done((bf16[64,1440]{1,0:T(8,128)(2,1)S(1)}, bf16[64,1440]{1,0:T(8,128)(2,1)S(1)}, u32[]{:S(2)}, u32[]{:S(2)}) %collective-permute-start.15) | collective-permute-done | bytes 184352 | tf_op jit(solution)/shard_map/ppermute | solution.py:155
  38.9 0.1 add_convert_fusion.7
  39.0 0.2 collective-permute-done.21.refs_2_
  39.2 0.3 collective-permute-done.22.refs_3_
  39.5 2.7 %shard_map.70 = (bf16[128,1440]{1,0:T(8,128)(2,1)S(1)}, bf16[128,1440]{1,0:T(8,128)(2,1)S(1)}) custom-call(s32[2]{0:T(128)S(1)} %pad_add_fusion.place, bf16[64,1464]{1,0:T(8,128)(2,1)S(1)} %collective-permute-done.8.refs_0_, bf16[64,1464]{1,0:T(8,128)(2,1)S(1)} %collective-permute-done.11.refs_1_, bf16[64,1464]{1,0:T(8,128)(2,1)S(1)} %collective-permute-done.21.refs_2_, ...), custom_call_target="tpu_custom_call" | custom-call | flops 1592524800 | bytes 12441600 | tf_op jit(solution)/shard_map/pallas_call | solution.py:127
  42.2 0.3 collective-permute-start.23
  42.5 0.3 collective-permute-start.18
  42.7 0.2 collective-permute-start.19
  43.0 1.6 %collective-permute-start.16 = (bf16[32,1440]{1,0:T(8,128)(2,1)S(1)}, bf16[32,1440]{1,0:T(8,128)(2,1)S(1)}, u32[]{:S(2)}, u32[]{:S(2)}) collective-permute-start(bf16[32,1440]{1,0:T(8,128)(2,1)S(1)} %get-tuple-element.60), channel_id=1, source_target_pairs={{0,4},{4,8},{8,12},{12,14},{14,10},{10,6},{6,2},{2,0},{1,5},{5,9},... | collective-permute-start | bytes 276488 | tf_op jit(solution)/shard_map/ppermute | solution.py:183
  44.5 0.4 collective-permute-start.17
  45.0 3.0 %collective-permute-done.16 = bf16[32,1440]{1,0:T(8,128)(2,1)S(1)} collective-permute-done((bf16[32,1440]{1,0:T(8,128)(2,1)S(1)}, bf16[32,1440]{1,0:T(8,128)(2,1)S(1)}, u32[]{:S(2)}, u32[]{:S(2)}) %collective-permute-start.16) | collective-permute-done | bytes 92192 | tf_op jit(solution)/shard_map/ppermute | solution.py:183
  48.0 1.3 %collective-permute-done.17 = bf16[32,1440]{1,0:T(8,128)(2,1)S(1)} collective-permute-done((bf16[32,1440]{1,0:T(8,128)(2,1)S(1)}, bf16[32,1440]{1,0:T(8,128)(2,1)S(1)}, u32[]{:S(2)}, u32[]{:S(2)}) %collective-permute-start.17) | collective-permute-done | bytes 92192 | tf_op jit(solution)/shard_map/ppermute | solution.py:184
  49.3 2.7 %shard_map.69 = (bf16[128,1440]{1,0:T(8,128)(2,1)S(1)}, bf16[128,1440]{1,0:T(8,128)(2,1)S(1)}) custom-call(s32[2]{0:T(128)S(1)} %pad_add_fusion.place, bf16[64,1464]{1,0:T(8,128)(2,1)S(1)} %collective-permute-done.7.refs_0_, bf16[64,1464]{1,0:T(8,128)(2,1)S(1)} %collective-permute-done.10.refs_1_, bf16[64,1464]{1,0:T(8,128)(2,1)S(1)} %collective-permute-done.18.refs_2_, ...), custom_call_target="tpu_custom_call" | custom-call | flops 1592524800 | bytes 12441600 | tf_op jit(solution)/shard_map/pallas_call | solution.py:127
  52.0 0.1 collective-permute-start.20
  52.1 0.1 add_convert_fusion.6
  52.2 1.6 %collective-permute-start.24 = (bf16[64,1440]{1,0:T(8,128)(2,1)S(1)}, bf16[64,1440]{1,0:T(8,128)(2,1)S(1)}, u32[]{:S(2)}, u32[]{:S(2)}) collective-permute-start(bf16[64,1440]{1,0:T(8,128)(2,1)S(1)} %get-tuple-element.57), channel_id=1, source_target_pairs={{0,4},{4,8},{8,12},{12,14},{14,10},{10,6},{6,2},{2,0},{1,5},{5,9},... | collective-permute-start | bytes 552968 | tf_op jit(solution)/shard_map/ppermute | solution.py:183
  53.8 0.4 collective-permute-start.27
  54.3 5.3 %collective-permute-done.24 = bf16[64,1440]{1,0:T(8,128)(2,1)S(1)} collective-permute-done((bf16[64,1440]{1,0:T(8,128)(2,1)S(1)}, bf16[64,1440]{1,0:T(8,128)(2,1)S(1)}, u32[]{:S(2)}, u32[]{:S(2)}) %collective-permute-start.24) | collective-permute-done | bytes 184352 | tf_op jit(solution)/shard_map/ppermute | solution.py:183
  59.5 1.3 %collective-permute-done.27 = bf16[64,1440]{1,0:T(8,128)(2,1)S(1)} collective-permute-done((bf16[64,1440]{1,0:T(8,128)(2,1)S(1)}, bf16[64,1440]{1,0:T(8,128)(2,1)S(1)}, u32[]{:S(2)}, u32[]{:S(2)}) %collective-permute-start.27) | collective-permute-done | bytes 184352 | tf_op jit(solution)/shard_map/ppermute | solution.py:184
  60.8 0.1 add_convert_fusion.5
  61.0 1.5 %collective-permute-start.25 = (bf16[64,1440]{1,0:T(8,128)(2,1)S(1)}, bf16[64,1440]{1,0:T(8,128)(2,1)S(1)}, u32[]{:S(2)}, u32[]{:S(2)}) collective-permute-start(bf16[64,1440]{1,0:T(8,128)(2,1)S(1)} %get-tuple-element.55), channel_id=1, source_target_pairs={{0,4},{4,8},{8,12},{12,14},{14,10},{10,6},{6,2},{2,0},{1,5},{5,9},... | collective-permute-start | bytes 552968 | tf_op jit(solution)/shard_map/ppermute | solution.py:183
  62.5 0.5 collective-permute-start.28
  63.1 4.2 %collective-permute-done.25 = bf16[64,1440]{1,0:T(8,128)(2,1)S(1)} collective-permute-done((bf16[64,1440]{1,0:T(8,128)(2,1)S(1)}, bf16[64,1440]{1,0:T(8,128)(2,1)S(1)}, u32[]{:S(2)}, u32[]{:S(2)}) %collective-permute-start.25) | collective-permute-done | bytes 184352 | tf_op jit(solution)/shard_map/ppermute | solution.py:183
  67.2 1.2 %collective-permute-done.28 = bf16[64,1440]{1,0:T(8,128)(2,1)S(1)} collective-permute-done((bf16[64,1440]{1,0:T(8,128)(2,1)S(1)}, bf16[64,1440]{1,0:T(8,128)(2,1)S(1)}, u32[]{:S(2)}, u32[]{:S(2)}) %collective-permute-start.28) | collective-permute-done | bytes 184352 | tf_op jit(solution)/shard_map/ppermute | solution.py:184
  68.4 0.1 add_convert_fusion.4
  68.6 0.6 collective-permute-start.29
  69.2 1.5 %collective-permute-start.26 = (bf16[64,1440]{1,0:T(8,128)(2,1)S(1)}, bf16[64,1440]{1,0:T(8,128)(2,1)S(1)}, u32[]{:S(2)}, u32[]{:S(2)}) collective-permute-start(bf16[64,1440]{1,0:T(8,128)(2,1)S(1)} %get-tuple-element.53), channel_id=1, source_target_pairs={{0,4},{4,8},{8,12},{12,14},{14,10},{10,6},{6,2},{2,0},{1,5},{5,9},... | collective-permute-start | bytes 552968 | tf_op jit(solution)/shard_map/ppermute | solution.py:183
  70.7 3.6 %collective-permute-done.29 = bf16[64,1440]{1,0:T(8,128)(2,1)S(1)} collective-permute-done((bf16[64,1440]{1,0:T(8,128)(2,1)S(1)}, bf16[64,1440]{1,0:T(8,128)(2,1)S(1)}, u32[]{:S(2)}, u32[]{:S(2)}) %collective-permute-start.29) | collective-permute-done | bytes 184352 | tf_op jit(solution)/shard_map/ppermute | solution.py:184
  74.3 0.5 collective-permute-done.26
  74.8 0.8 %add_convert_fusion = bf16[64,1440]{1,0:T(8,128)(2,1)} fusion(bf16[64,1440]{1,0:T(8,128)(2,1)S(1)} %collective-permute-done.29, bf16[64,1440]{1,0:T(8,128)(2,1)S(1)} %collective-permute-done.26, bf16[64,1440]{1,0:T(8,128)(2,1)S(1)} %collective-permute-done.1, bf16[64,1440]{1,0:T(8,128)(2,1)S(1)} %get-tuple-element.34), kind=kLoop, calls=%fused_computation | loop fusion | flops 737280 | bytes 921600 | tf_op jit(solution)/shard_map/convert_element_type | solution.py:193
  (17 shorter events, 0.1 us)
Async XLA Ops:
  0.0 0.9 %copy-start = (bf16[64,1440]{1,0:T(8,128)(2,1)S(1)}, bf16[64,1440]{1,0:T(8,128)(2,1)}, u32[]{:S(2)}) copy-start(bf16[64,1440]{1,0:T(8,128)(2,1)} %tokens.1) | copy-start | bytes 552964
  0.9 0.7 copy-start.1
  1.6 0.7 copy-start.2
  2.5 9.7 %collective-permute-start.2 = (bf16[64,1464]{1,0:T(8,128)(2,1)S(1)}, bf16[64,1464]{1,0:T(8,128)(2,1)S(1)}, u32[]{:S(2)}, u32[]{:S(2)}) collective-permute-start(bf16[64,1464]{1,0:T(8,128)(2,1)S(1)} %shard_map.64.refs_0_), channel_id=1, source_target_pairs={{0,4},{4,8},{8,12},{12,14},{14,10},{10,6},{6,2},{2,0},{1,5},{5,9},... | collective-permute-start | bytes 562184 | tf_op jit(solution)/shard_map/ppermute | solution.py:165
  5.5 8.8 %collective-permute-start.3 = (bf16[64,1464]{1,0:T(8,128)(2,1)S(1)}, bf16[64,1464]{1,0:T(8,128)(2,1)S(1)}, u32[]{:S(2)}, u32[]{:S(2)}) collective-permute-start(bf16[64,1464]{1,0:T(8,128)(2,1)S(1)} %shard_map.64.refs_0_), channel_id=1, source_target_pairs={{4,0},{8,4},{12,8},{14,12},{10,14},{6,10},{2,6},{0,2},{5,1},{9,5},... | collective-permute-start | bytes 562184 | tf_op jit(solution)/shard_map/ppermute | solution.py:166
  5.5 9.3 %collective-permute-start = (bf16[64,1464]{1,0:T(8,128)(2,1)S(1)}, bf16[64,1464]{1,0:T(8,128)(2,1)S(1)}, u32[]{:S(2)}, u32[]{:S(2)}) collective-permute-start(bf16[64,1464]{1,0:T(8,128)(2,1)S(1)} %shard_map.64.refs_0_), channel_id=1, source_target_pairs={{0,1},{1,0},{2,3},{3,2},{4,5},{5,4},{6,7},{7,6},{8,9},{9,8},{10,11... | collective-permute-start | bytes 562184 | tf_op jit(solution)/shard_map/ppermute | solution.py:167
  12.2 7.6 %collective-permute-start.7 = (bf16[64,1464]{1,0:T(8,128)(2,1)S(1)}, bf16[64,1464]{1,0:T(8,128)(2,1)S(1)}, u32[]{:S(2)}, u32[]{:S(2)}) collective-permute-start(bf16[64,1464]{1,0:T(8,128)(2,1)S(1)} %collective-permute-done.2.refs_0_), channel_id=1, source_target_pairs={{0,4},{4,8},{8,12},{12,14},{14,10},{10,6},{6,2},{2,0},{1,5},{5,9},... | collective-permute-start | bytes 562184 | tf_op jit(solution)/shard_map/ppermute | solution.py:165
  14.3 7.3 %collective-permute-start.10 = (bf16[64,1464]{1,0:T(8,128)(2,1)S(1)}, bf16[64,1464]{1,0:T(8,128)(2,1)S(1)}, u32[]{:S(2)}, u32[]{:S(2)}) collective-permute-start(bf16[64,1464]{1,0:T(8,128)(2,1)S(1)} %collective-permute-done.3.refs_1_), channel_id=1, source_target_pairs={{4,0},{8,4},{12,8},{14,12},{10,14},{6,10},{2,6},{0,2},{5,1},{9,5},... | collective-permute-start | bytes 562184 | tf_op jit(solution)/shard_map/ppermute | solution.py:166
  14.3 7.5 %collective-permute-start.4 = (bf16[64,1464]{1,0:T(8,128)(2,1)S(1)}, bf16[64,1464]{1,0:T(8,128)(2,1)S(1)}, u32[]{:S(2)}, u32[]{:S(2)}) collective-permute-start(bf16[64,1464]{1,0:T(8,128)(2,1)S(1)} %collective-permute-done.2.refs_0_), channel_id=1, source_target_pairs={{0,1},{1,0},{2,3},{3,2},{4,5},{5,4},{6,7},{7,6},{8,9},{9,8},{10,11... | collective-permute-start | bytes 562184 | tf_op jit(solution)/shard_map/ppermute | solution.py:167
  14.5 7.3 %collective-permute-start.5 = (bf16[64,1464]{1,0:T(8,128)(2,1)S(1)}, bf16[64,1464]{1,0:T(8,128)(2,1)S(1)}, u32[]{:S(2)}, u32[]{:S(2)}) collective-permute-start(bf16[64,1464]{1,0:T(8,128)(2,1)S(1)} %collective-permute-done.3.refs_1_), channel_id=1, source_target_pairs={{0,1},{1,0},{2,3},{3,2},{4,5},{5,4},{6,7},{7,6},{8,9},{9,8},{10,11... | collective-permute-start | bytes 562184 | tf_op jit(solution)/shard_map/ppermute | solution.py:169
  19.8 6.7 %collective-permute-start.8 = (bf16[64,1464]{1,0:T(8,128)(2,1)S(1)}, bf16[64,1464]{1,0:T(8,128)(2,1)S(1)}, u32[]{:S(2)}, u32[]{:S(2)}) collective-permute-start(bf16[64,1464]{1,0:T(8,128)(2,1)S(1)} %collective-permute-done.7.refs_0_), channel_id=1, source_target_pairs={{0,4},{4,8},{8,12},{12,14},{14,10},{10,6},{6,2},{2,0},{1,5},{5,9},... | collective-permute-start | bytes 562184 | tf_op jit(solution)/shard_map/ppermute | solution.py:165
  21.6 6.6 %collective-permute-start.11 = (bf16[64,1464]{1,0:T(8,128)(2,1)S(1)}, bf16[64,1464]{1,0:T(8,128)(2,1)S(1)}, u32[]{:S(2)}, u32[]{:S(2)}) collective-permute-start(bf16[64,1464]{1,0:T(8,128)(2,1)S(1)} %collective-permute-done.10.refs_1_), channel_id=1, source_target_pairs={{4,0},{8,4},{12,8},{14,12},{10,14},{6,10},{2,6},{0,2},{5,1},{9,5},... | collective-permute-start | bytes 562184 | tf_op jit(solution)/shard_map/ppermute | solution.py:166
  26.4 4.7 %collective-permute-start.9 = (bf16[32,1464]{1,0:T(8,128)(2,1)S(1)}, bf16[32,1464]{1,0:T(8,128)(2,1)S(1)}, u32[]{:S(2)}, u32[]{:S(2)}) collective-permute-start(bf16[32,1464]{1,0:T(8,128)(2,1)S(1)} %slice.56), channel_id=1, source_target_pairs={{0,4},{4,8},{8,12},{12,14},{14,10},{10,6},{6,2},{2,0},{1,5},{5,9},... | collective-permute-start | bytes 281096 | tf_op jit(solution)/shard_map/ppermute | solution.py:172
  28.2 4.8 %collective-permute-start.12 = (bf16[32,1464]{1,0:T(8,128)(2,1)S(1)}, bf16[32,1464]{1,0:T(8,128)(2,1)S(1)}, u32[]{:S(2)}, u32[]{:S(2)}) collective-permute-start(bf16[32,1464]{1,0:T(8,128)(2,1)S(1)} %slice.57), channel_id=1, source_target_pairs={{4,0},{8,4},{12,8},{14,12},{10,14},{6,10},{2,6},{0,2},{5,1},{9,5},... | collective-permute-start | bytes 281096 | tf_op jit(solution)/shard_map/ppermute | solution.py:173
  31.1 2.0 %collective-permute-start.13 = (bf16[32,1464]{1,0:T(8,128)(2,1)S(1)}, bf16[32,1464]{1,0:T(8,128)(2,1)S(1)}, u32[]{:S(2)}, u32[]{:S(2)}) collective-permute-start(bf16[32,1464]{1,0:T(8,128)(2,1)S(1)} %collective-permute-done.9.refs_0_), channel_id=1, source_target_pairs={{0,1},{1,0},{2,3},{3,2},{4,5},{5,4},{6,7},{7,6},{8,9},{9,8},{10,11... | collective-permute-start | bytes 281096 | tf_op jit(solution)/shard_map/ppermute | solution.py:175
  33.1 1.3 %collective-permute-start.14 = (bf16[32,1464]{1,0:T(8,128)(2,1)S(1)}, bf16[32,1464]{1,0:T(8,128)(2,1)S(1)}, u32[]{:S(2)}, u32[]{:S(2)}) collective-permute-start(bf16[32,1464]{1,0:T(8,128)(2,1)S(1)} %collective-permute-done.12.refs_1_), channel_id=1, source_target_pairs={{0,1},{1,0},{2,3},{3,2},{4,5},{5,4},{6,7},{7,6},{8,9},{9,8},{10,11... | collective-permute-start | bytes 281096 | tf_op jit(solution)/shard_map/ppermute | solution.py:175
  37.4 1.5 %collective-permute-start.15 = (bf16[64,1440]{1,0:T(8,128)(2,1)S(1)}, bf16[64,1440]{1,0:T(8,128)(2,1)S(1)}, u32[]{:S(2)}, u32[]{:S(2)}) collective-permute-start(bf16[64,1440]{1,0:T(8,128)(2,1)S(1)} %get-tuple-element.46), channel_id=1, source_target_pairs={{0,1},{1,0},{2,3},{3,2},{4,5},{5,4},{6,7},{7,6},{8,9},{9,8},{10,11... | collective-permute-start | bytes 552968 | tf_op jit(solution)/shard_map/ppermute | solution.py:155
  37.6 1.6 %collective-permute-start.21 = (bf16[64,1464]{1,0:T(8,128)(2,1)S(1)}, bf16[64,1464]{1,0:T(8,128)(2,1)S(1)}, u32[]{:S(2)}, u32[]{:S(2)}) collective-permute-start(bf16[64,1464]{1,0:T(8,128)(2,1)S(1)} %collective-permute-done.8.refs_0_), channel_id=1, source_target_pairs={{0,1},{1,0},{2,3},{3,2},{4,5},{5,4},{6,7},{7,6},{8,9},{9,8},{10,11... | collective-permute-start | bytes 562184 | tf_op jit(solution)/shard_map/ppermute | solution.py:175
  38.0 1.5 %collective-permute-start.22 = (bf16[64,1464]{1,0:T(8,128)(2,1)S(1)}, bf16[64,1464]{1,0:T(8,128)(2,1)S(1)}, u32[]{:S(2)}, u32[]{:S(2)}) collective-permute-start(bf16[64,1464]{1,0:T(8,128)(2,1)S(1)} %collective-permute-done.11.refs_1_), channel_id=1, source_target_pairs={{0,1},{1,0},{2,3},{3,2},{4,5},{5,4},{6,7},{7,6},{8,9},{9,8},{10,11... | collective-permute-start | bytes 562184 | tf_op jit(solution)/shard_map/ppermute | solution.py:175
  42.2 9.9 %collective-permute-start.23 = (bf16[128,1440]{1,0:T(8,128)(2,1)S(1)}, bf16[128,1440]{1,0:T(8,128)(2,1)S(1)}, u32[]{:S(2)}, u32[]{:S(2)}) collective-permute-start(bf16[128,1440]{1,0:T(8,128)(2,1)S(1)} %get-tuple-element.52), channel_id=1, source_target_pairs={{0,1},{1,0},{2,3},{3,2},{4,5},{5,4},{6,7},{7,6},{8,9},{9,8},{10,11... | collective-permute-start | bytes 1105928 | tf_op jit(solution)/shard_map/ppermute | solution.py:155
  42.5 6.8 %collective-permute-start.18 = (bf16[64,1464]{1,0:T(8,128)(2,1)S(1)}, bf16[64,1464]{1,0:T(8,128)(2,1)S(1)}, u32[]{:S(2)}, u32[]{:S(2)}) collective-permute-start(bf16[64,1464]{1,0:T(8,128)(2,1)S(1)} %collective-permute-done.7.refs_0_), channel_id=1, source_target_pairs={{0,1},{1,0},{2,3},{3,2},{4,5},{5,4},{6,7},{7,6},{8,9},{9,8},{10,11... | collective-permute-start | bytes 562184 | tf_op jit(solution)/shard_map/ppermute | solution.py:167
  42.7 6.5 %collective-permute-start.19 = (bf16[64,1464]{1,0:T(8,128)(2,1)S(1)}, bf16[64,1464]{1,0:T(8,128)(2,1)S(1)}, u32[]{:S(2)}, u32[]{:S(2)}) collective-permute-start(bf16[64,1464]{1,0:T(8,128)(2,1)S(1)} %collective-permute-done.10.refs_1_), channel_id=1, source_target_pairs={{0,1},{1,0},{2,3},{3,2},{4,5},{5,4},{6,7},{7,6},{8,9},{9,8},{10,11... | collective-permute-start | bytes 562184 | tf_op jit(solution)/shard_map/ppermute | solution.py:169
  43.0 5.0 %collective-permute-start.16 = (bf16[32,1440]{1,0:T(8,128)(2,1)S(1)}, bf16[32,1440]{1,0:T(8,128)(2,1)S(1)}, u32[]{:S(2)}, u32[]{:S(2)}) collective-permute-start(bf16[32,1440]{1,0:T(8,128)(2,1)S(1)} %get-tuple-element.60), channel_id=1, source_target_pairs={{0,4},{4,8},{8,12},{12,14},{14,10},{10,6},{6,2},{2,0},{1,5},{5,9},... | collective-permute-start | bytes 276488 | tf_op jit(solution)/shard_map/ppermute | solution.py:183
  44.5 4.7 %collective-permute-start.17 = (bf16[32,1440]{1,0:T(8,128)(2,1)S(1)}, bf16[32,1440]{1,0:T(8,128)(2,1)S(1)}, u32[]{:S(2)}, u32[]{:S(2)}) collective-permute-start(bf16[32,1440]{1,0:T(8,128)(2,1)S(1)} %get-tuple-element.59), channel_id=1, source_target_pairs={{4,0},{8,4},{12,8},{14,12},{10,14},{6,10},{2,6},{0,2},{5,1},{9,5},... | collective-permute-start | bytes 276488 | tf_op jit(solution)/shard_map/ppermute | solution.py:184
  52.0 2.3 %collective-permute-start.20 = (bf16[128,1440]{1,0:T(8,128)(2,1)S(1)}, bf16[128,1440]{1,0:T(8,128)(2,1)S(1)}, u32[]{:S(2)}, u32[]{:S(2)}) collective-permute-start(bf16[128,1440]{1,0:T(8,128)(2,1)S(1)} %get-tuple-element.49), channel_id=1, source_target_pairs={{0,1},{1,0},{2,3},{3,2},{4,5},{5,4},{6,7},{7,6},{8,9},{9,8},{10,11... | collective-permute-start | bytes 1105928 | tf_op jit(solution)/shard_map/ppermute | solution.py:155
  52.2 7.3 %collective-permute-start.24 = (bf16[64,1440]{1,0:T(8,128)(2,1)S(1)}, bf16[64,1440]{1,0:T(8,128)(2,1)S(1)}, u32[]{:S(2)}, u32[]{:S(2)}) collective-permute-start(bf16[64,1440]{1,0:T(8,128)(2,1)S(1)} %get-tuple-element.57), channel_id=1, source_target_pairs={{0,4},{4,8},{8,12},{12,14},{14,10},{10,6},{6,2},{2,0},{1,5},{5,9},... | collective-permute-start | bytes 552968 | tf_op jit(solution)/shard_map/ppermute | solution.py:183
  53.8 7.0 %collective-permute-start.27 = (bf16[64,1440]{1,0:T(8,128)(2,1)S(1)}, bf16[64,1440]{1,0:T(8,128)(2,1)S(1)}, u32[]{:S(2)}, u32[]{:S(2)}) collective-permute-start(bf16[64,1440]{1,0:T(8,128)(2,1)S(1)} %get-tuple-element.58), channel_id=1, source_target_pairs={{4,0},{8,4},{12,8},{14,12},{10,14},{6,10},{2,6},{0,2},{5,1},{9,5},... | collective-permute-start | bytes 552968 | tf_op jit(solution)/shard_map/ppermute | solution.py:184
  54.3 8.8 %collective-permute-start.6 = (bf16[128,1440]{1,0:T(8,128)(2,1)S(1)}, bf16[128,1440]{1,0:T(8,128)(2,1)S(1)}, u32[]{:S(2)}, u32[]{:S(2)}) collective-permute-start(bf16[128,1440]{1,0:T(8,128)(2,1)S(1)} %get-tuple-element.37), channel_id=1, source_target_pairs={{0,1},{1,0},{2,3},{3,2},{4,5},{5,4},{6,7},{7,6},{8,9},{9,8},{10,11... | collective-permute-start | bytes 1105928 | tf_op jit(solution)/shard_map/ppermute | solution.py:155
  61.0 6.2 %collective-permute-start.25 = (bf16[64,1440]{1,0:T(8,128)(2,1)S(1)}, bf16[64,1440]{1,0:T(8,128)(2,1)S(1)}, u32[]{:S(2)}, u32[]{:S(2)}) collective-permute-start(bf16[64,1440]{1,0:T(8,128)(2,1)S(1)} %get-tuple-element.55), channel_id=1, source_target_pairs={{0,4},{4,8},{8,12},{12,14},{14,10},{10,6},{6,2},{2,0},{1,5},{5,9},... | collective-permute-start | bytes 552968 | tf_op jit(solution)/shard_map/ppermute | solution.py:183
  62.5 5.9 %collective-permute-start.28 = (bf16[64,1440]{1,0:T(8,128)(2,1)S(1)}, bf16[64,1440]{1,0:T(8,128)(2,1)S(1)}, u32[]{:S(2)}, u32[]{:S(2)}) collective-permute-start(bf16[64,1440]{1,0:T(8,128)(2,1)S(1)} %get-tuple-element.56), channel_id=1, source_target_pairs={{4,0},{8,4},{12,8},{14,12},{10,14},{6,10},{2,6},{0,2},{5,1},{9,5},... | collective-permute-start | bytes 552968 | tf_op jit(solution)/shard_map/ppermute | solution.py:184
  63.1 7.6 %collective-permute-start.1 = (bf16[64,1440]{1,0:T(8,128)(2,1)S(1)}, bf16[64,1440]{1,0:T(8,128)(2,1)S(1)}, u32[]{:S(2)}, u32[]{:S(2)}) collective-permute-start(bf16[64,1440]{1,0:T(8,128)(2,1)S(1)} %get-tuple-element.35), channel_id=1, source_target_pairs={{0,1},{1,0},{2,3},{3,2},{4,5},{5,4},{6,7},{7,6},{8,9},{9,8},{10,11... | collective-permute-start | bytes 552968 | tf_op jit(solution)/shard_map/ppermute | solution.py:155
  68.6 5.7 %collective-permute-start.29 = (bf16[64,1440]{1,0:T(8,128)(2,1)S(1)}, bf16[64,1440]{1,0:T(8,128)(2,1)S(1)}, u32[]{:S(2)}, u32[]{:S(2)}) collective-permute-start(bf16[64,1440]{1,0:T(8,128)(2,1)S(1)} %get-tuple-element.54), channel_id=1, source_target_pairs={{4,0},{8,4},{12,8},{14,12},{10,14},{6,10},{2,6},{0,2},{5,1},{9,5},... | collective-permute-start | bytes 552968 | tf_op jit(solution)/shard_map/ppermute | solution.py:184
  69.2 5.7 %collective-permute-start.26 = (bf16[64,1440]{1,0:T(8,128)(2,1)S(1)}, bf16[64,1440]{1,0:T(8,128)(2,1)S(1)}, u32[]{:S(2)}, u32[]{:S(2)}) collective-permute-start(bf16[64,1440]{1,0:T(8,128)(2,1)S(1)} %get-tuple-element.53), channel_id=1, source_target_pairs={{0,4},{4,8},{8,12},{12,14},{14,10},{10,6},{6,2},{2,0},{1,5},{5,9},... | collective-permute-start | bytes 552968 | tf_op jit(solution)/shard_map/ppermute | solution.py:183

commit v3 on v2

--- a/solution.py
+++ b/solution.py
@@ -22,10 +22,17 @@
     return lax.optimization_barrier((x, done))[0]
 
 
-def pack_kernel(n_experts, tokens, ids, probs, packed):
+def pack_kernel(n_experts, tokens_in, ids_in, probs_in, packed, tokens, ids, probs, sems):
+    copies = [
+        pltpu.make_async_copy(src, dst, sems.at[i])
+        for i, (src, dst) in enumerate(((ids_in, ids), (probs_in, probs), (tokens_in, tokens)))
+    ]
+    for copy in copies:
+        copy.start()
     top, rows = ids.shape
     half = tokens.shape[1]
-    packed[:, :half] = tokens[...]
+    copies[0].wait()
+    copies[1].wait()
     expert = lax.broadcasted_iota(jnp.int32, (n_experts, rows), 0)
     rest = jnp.zeros((n_experts, rows), jnp.float32)
     for k in range(top):
@@ -36,31 +43,54 @@
         terms.append(term)
         rest = rest - term
     packed[:, half:] = jnp.concatenate(terms, axis=0).T.astype(jnp.bfloat16)
+    copies[2].wait()
+    packed[:, :half] = tokens[...]
 
 
 def pack(tokens, expert_ids, gate_probs, n_experts):
     rows, half = tokens.shape
+    args = (tokens, expert_ids.T, gate_probs.T)
     return pl.pallas_call(
         functools.partial(pack_kernel, n_experts),
         out_shape=in_vmem((rows, half + SPLITS * n_experts)),
+        in_specs=[pl.BlockSpec(memory_space=pltpu.HBM)] * 3,
+        out_specs=pl.BlockSpec(memory_space=pltpu.VMEM),
+        scratch_shapes=[pltpu.VMEM(a.shape, a.dtype) for a in args] + [pltpu.SemaphoreType.DMA((3,))],
         compiler_params=pltpu.CompilerParams(vmem_limit_bytes=8 << 20),
-    )(tokens, expert_ids.T, gate_probs.T)
-
-
-def load_kernel(place, gate_in, up_in, down_in, gate, up, down_mine, down_theirs, done, gate_buf, up_buf, down_buf, sems):
-    lane = place[0]
-    half = down_mine.shape[1]
+    )(*[pltpu.with_memory_space_constraint(a, pltpu.HBM) for a in args])
+
+
+def turn_kernel(after_this, gate_in, up_in, gate, up, gate_buf, up_buf, sems):
     copies = [
         pltpu.make_async_copy(src, dst, sems.at[i])
-        for i, (src, dst) in enumerate(((gate_in, gate_buf), (up_in, up_buf), (down_in, down_buf)))
+        for i, (src, dst) in enumerate(((gate_in, gate_buf), (up_in, up_buf)))
     ]
     for copy in copies:
         copy.start()
-    copies[0].wait()
-    gate[...] = gate_buf[...].T
-    copies[1].wait()
-    up[...] = up_buf[...].T
-    copies[2].wait()
+    for copy, buf, out in zip(copies, (gate_buf, up_buf), (gate, up)):
+        copy.wait()
+        out[...] = buf[...].T
+
+
+def turn_weights(after_this, *weights):
+    hidden, width = weights[0].shape
+    return pl.pallas_call(
+        turn_kernel,
+        out_shape=[in_vmem((width, hidden))] * 2,
+        in_specs=[pl.BlockSpec(memory_space=pltpu.SMEM)] + [pl.BlockSpec(memory_space=pltpu.HBM)] * 2,
+        out_specs=[pl.BlockSpec(memory_space=pltpu.VMEM)] * 2,
+        scratch_shapes=[pltpu.VMEM((hidden, width), jnp.bfloat16)] * 2 + [pltpu.SemaphoreType.DMA((2,))],
+        compiler_params=pltpu.CompilerParams(vmem_limit_bytes=32 << 20),
+        cost_estimate=pl.CostEstimate(flops=0, bytes_accessed=8 * hidden * width, transcendentals=0),
+    )(after_this, *[pltpu.with_memory_space_constraint(w, pltpu.HBM) for w in weights])
+
+
+def halve_kernel(place, down_in, down_mine, down_theirs, down_buf, sem):
+    lane = place[0]
+    half = down_mine.shape[1]
+    copy = pltpu.make_async_copy(down_in, down_buf, sem)
+    copy.start()
+    copy.wait()
 
     @pl.when(lane == 0)
     def _():
@@ -72,20 +102,18 @@
         down_mine[...] = down_buf[:, half:]
         down_theirs[...] = down_buf[:, :half]
 
-    done[...] = jnp.zeros_like(done)
-
-
-def load_weights(place, w_gate, w_up, w_down):
+
+def halve_weights(place, w_down):
     hidden, width = w_down.shape
     return pl.pallas_call(
-        load_kernel,
-        out_shape=[in_vmem((width, hidden))] * 2 + [in_vmem((hidden, width // 2))] * 2 + [in_vmem((8, 128), jnp.float32)],
-        in_specs=[pl.BlockSpec(memory_space=pltpu.SMEM)] + [pl.BlockSpec(memory_space=pltpu.HBM)] * 3,
-        out_specs=[pl.BlockSpec(memory_space=pltpu.VMEM)] * 5,
-        scratch_shapes=[pltpu.VMEM((hidden, width), jnp.bfloat16)] * 3 + [pltpu.SemaphoreType.DMA((3,))],
+        halve_kernel,
+        out_shape=[in_vmem((hidden, width // 2))] * 2,
+        in_specs=[pl.BlockSpec(memory_space=pltpu.SMEM), pl.BlockSpec(memory_space=pltpu.HBM)],
+        out_specs=[pl.BlockSpec(memory_space=pltpu.VMEM)] * 2,
+        scratch_shapes=[pltpu.VMEM((hidden, width), jnp.bfloat16), pltpu.SemaphoreType.DMA],
         compiler_params=pltpu.CompilerParams(vmem_limit_bytes=32 << 20),
-        cost_estimate=pl.CostEstimate(flops=0, bytes_accessed=12 * hidden * width, transcendentals=0),
-    )(place, *[pltpu.with_memory_space_constraint(w, pltpu.HBM) for w in (w_gate.T, w_up.T, w_down)])
+        cost_estimate=pl.CostEstimate(flops=0, bytes_accessed=8 * hidden * width, transcendentals=0),
+    )(place, pltpu.with_memory_space_constraint(w_down, pltpu.HBM))
 
 
 def expert_kernel(n_blocks, n_experts, place, *refs):
@@ -145,45 +173,52 @@
     far = n // 2
     place = jnp.stack([lax.axis_index("tp"), lax.axis_index("ep")]).astype(jnp.int32)
     packed = pack(tokens, expert_ids, gate_probs, n)
-    *weights, loaded = load_weights(after(place, packed), w_gate[0], w_up[0], w_down[0])
+    gate, up = turn_weights(after(place, packed), w_gate[0].T, w_up[0].T)
 
     came, across, value = {0: packed}, {}, {}
 
     def run(keys, wait_for=None):
         at = place if wait_for is None else after(place, wait_for)
         mine, theirs = run_expert(at, [came[k] for k in keys], [across[k] for k in keys], weights, n)
-        theirs = swap(theirs)
+        done, theirs = theirs, swap(theirs)
         start = 0
         for k in keys:
             span = slice(start, start + came[k].shape[0])
             start = span.stop
             value[k] = mine[span].astype(jnp.float32) + theirs[span].astype(jnp.float32)
-        return mine
-
-    hidden_work = loaded
-    for k in range(1, far):
-        came[k] = lax.ppermute(after(came[k - 1], hidden_work) if k > 1 else packed, "ep", ahead)
-        came[-k] = lax.ppermute(after(came[1 - k], hidden_work) if k > 1 else packed, "ep", back)
-        across[k - 1] = swap(came[k - 1])
-        if k > 1:
-            across[1 - k] = swap(came[1 - k])
-            hidden_work = run([0] if k == 2 else [k - 2, 2 - k])
-    far_keys = ("low", "high")
-    came["low"] = lax.ppermute(after(came[far - 1], hidden_work)[: rows // 2], "ep", ahead)
-    came["high"] = lax.ppermute(after(came[1 - far], hidden_work)[rows // 2 :], "ep", back)
-    for k in (far - 1, 1 - far, *far_keys):
-        across[k] = swap(came[k])
-    run(far_keys)
+        return done
+
+    came[1] = lax.ppermute(packed, "ep", ahead)
+    came[-1] = lax.ppermute(packed, "ep", back)
+    across[0] = swap(packed)
+    weights, done = [gate, up], up
+    for k in range(2, far):
+        came[k - 1], came[1 - k] = after((came[k - 1], came[1 - k]), done)
+        came[k] = lax.ppermute(came[k - 1], "ep", ahead)
+        came[-k] = lax.ppermute(came[1 - k], "ep", back)
+        across[k - 1], across[1 - k] = swap(came[k - 1]), swap(came[1 - k])
+        if k == 2:
+            weights += halve_weights(after(place, came[1]), w_down[0])
+            done = weights[-1]
+        else:
+            done = run([k - 2, 2 - k])
+    came[far - 1], came[1 - far] = after((came[far - 1], came[1 - far]), done)
+    came["low"] = lax.ppermute(came[far - 1][: rows // 2], "ep", ahead)
+    came["high"] = lax.ppermute(came[1 - far][rows // 2 :], "ep", back)
+    across[far - 1], across[1 - far] = swap(came[far - 1]), swap(came[1 - far])
+    done = run([far - 1, 1 - far])
+    came["low"], came["high"] = after((came["low"], came["high"]), done)
+    across["low"], across["high"] = swap(came["low"]), swap(came["high"])
+    done = run(["low", "high"])
+    run([far - 2, 2 - far], done)
+    run([0], done)
 
     to_ahead = value["low"].astype(jnp.bfloat16)
     to_back = value["high"].astype(jnp.bfloat16)
-    run([far - 1, 1 - far], (to_ahead, to_back))
     pad_low, pad_high = ((0, rows - rows // 2), (0, 0)), ((rows // 2, 0), (0, 0))
     for k in range(far - 1, -1, -1):
         behind = lax.ppermute(to_ahead, "ep", ahead)
         front = lax.ppermute(to_back, "ep", back)
-        if k == far - 1:
-            run([far - 2, 2 - far], (behind, front))
         behind, front = behind.astype(jnp.float32), front.astype(jnp.float32)
         if k == far - 1:
             behind, front = jnp.pad(behind, pad_low), jnp.pad(front, pad_high)

time: 75.8 us -> 65.8 us (0.87)
  waiting for transfers between devices: 31.1 us -> 19.4 us
  Pallas kernels: 20.9 us -> 23.9 us
  local copies, waits for them, and re-layouts: 2.3 us -> 0.01 us
  starting transfers between devices: 19.8 us -> 20.8 us
    ppermute x4, waiting for transfers between devices: 12.9 us -> 5.19 us  [ring_body(): behind = lax.ppermute(to_ahead, 'ep', ahead)]
    ppermute x22, waiting for transfers between devices: 10.7 us -> 7.47 us  [the longest x2 2.8 us: ring_body(): came[-k] = lax.ppermute(came[1 - k], 'ep', back)]
    unnamed x6 -> x0, local copies, waits for them, and re-layouts: 2.29 us -> none
    pallas_call x1 -> x2, Pallas kernels: 6.61 us -> 8.75 us  [the longest x1 5.28 us: turn_weights(): pl.pallas_call(turn_kernel, out_shape=[in_vmem((width, hidden))] * 2, in_...]
    ppermute x4, starting transfers between devices: 2.01 us -> 3.55 us  [ring_body(): front = lax.ppermute(to_back, 'ep', back)]
    ppermute x4, starting transfers between devices: 6.25 us -> 4.78 us  [ring_body(): behind = lax.ppermute(to_ahead, 'ep', ahead)]
    ppermute x22, starting transfers between devices: 11.6 us -> 12.5 us  [the longest x2 3.15 us: ring_body(): came[k] = lax.ppermute(came[k - 1], 'ep', ahead)]
    pallas_call x1, Pallas kernels: 0.16 us -> 1 us  [pack(): pl.pallas_call(functools.partial(pack_kernel, n_experts), out_shape=in_vm...]
  transfers between devices with their start and end apart: 30 -> 30, of which waited for: 16 -> 16; matrix products, arithmetic and copies ran while one was open for 1% -> 1% of each run, Pallas kernels for 20% -> 30%
where the time goes in v3:
time: 65.8 us; the launch traced here: 65.6 us
  Pallas kernels  23.9 us (36%)
  starting transfers between devices  20.8 us (32%)
  waiting for transfers between devices  19.4 us (29%)
  other arithmetic  1.31 us (2%)
    pallas_call x5, Pallas kernels, run_expert(): pl.pallas_call(functools.partial(expert_kernel, len(own), n_experts), out...  14.2 us
    ppermute x4, waiting for transfers between devices, ring_body(): front = lax.ppermute(to_back, 'ep', back)  6.75 us
    pallas_call x1, Pallas kernels, turn_weights(): pl.pallas_call(turn_kernel, out_shape=[in_vmem((width, hidden))] * 2, in_...  5.28 us
    ppermute x4, waiting for transfers between devices, ring_body(): behind = lax.ppermute(to_ahead, 'ep', ahead)  5.19 us
    ppermute x4, starting transfers between devices, ring_body(): behind = lax.ppermute(to_ahead, 'ep', ahead)  4.78 us
    ppermute x4, starting transfers between devices, ring_body(): front = lax.ppermute(to_back, 'ep', back)  3.55 us
    pallas_call x1, Pallas kernels, halve_weights(): pl.pallas_call(halve_kernel, out_shape=[in_vmem((hidden, width // 2))] *...  3.47 us
    ppermute x2, starting transfers between devices, ring_body(): came[k] = lax.ppermute(came[k - 1], 'ep', ahead)  3.15 us
  transfers between devices with their start and end apart: 30, of which 16 were waited for; matrix products, arithmetic and copies ran while one was open for 1% of the time, Pallas kernels for 30%

profile of v3, /device:TPU:0, one launch (start us, length us, event | category | flops | bytes accessed | tf_op | source)
XLA Modules:
  0.0 65.6 jit_solution(7470500721713228993)
XLA Ops:
  0.0 1.0 %shard_map.64.refs_0_ = bf16[64,1464]{1,0:T(8,128)(2,1)S(1)} custom-call(bf16[64,1440]{1,0:T(8,128)(2,1)} %tokens_in.1, s32[4,64]{1,0:T(4,128)} %bitcast.14, f32[4,64]{1,0:T(4,128)} %bitcast.15), custom_call_target="tpu_custom_call" | custom-call | tf_op jit(solution)/shard_map/pallas_call | solution.py:53
  1.0 3.1 %collective-permute-start = (bf16[64,1464]{1,0:T(8,128)(2,1)S(1)}, bf16[64,1464]{1,0:T(8,128)(2,1)S(1)}, u32[]{:S(2)}, u32[]{:S(2)}) collective-permute-start(bf16[64,1464]{1,0:T(8,128)(2,1)S(1)} %shard_map.64.refs_0_), channel_id=1, source_target_pairs={{0,4},{4,8},{8,12},{12,14},{14,10},{10,6},{6,2},{2,0},{1,5},{5,9},... | collective-permute-start | bytes 562184 | tf_op jit(solution)/shard_map/ppermute | solution.py:191
  4.1 0.1 pad_add_fusion.after_this.place
  4.2 5.3 %shard_map.65 = (bf16[2880,720]{1,0:T(8,128)(2,1)S(1)}, bf16[2880,720]{1,0:T(8,128)(2,1)S(1)}) custom-call(s32[2]{0:T(128)S(1)} %pad_add_fusion.after_this.place, bf16[720,2880]{1,0:T(8,128)(2,1)} %bitcast.11, bf16[720,2880]{1,0:T(8,128)(2,1)} %bitcast.12), custom_call_target="tpu_custom_call" | custom-call | bytes 16588800 | tf_op jit(solution)/shard_map/pallas_call | solution.py:77
  9.5 1.0 %collective-permute-done.1.refs_1_ = bf16[64,1464]{1,0:T(8,128)(2,1)S(1)} collective-permute-done((bf16[64,1464]{1,0:T(8,128)(2,1)S(1)}, bf16[64,1464]{1,0:T(8,128)(2,1)S(1)}, u32[]{:S(2)}, u32[]{:S(2)}) %collective-permute-start.1) | collective-permute-done | bytes 187424 | tf_op jit(solution)/shard_map/ppermute | solution.py:192
  10.4 1.6 %collective-permute-start.2 = (bf16[64,1464]{1,0:T(8,128)(2,1)S(1)}, bf16[64,1464]{1,0:T(8,128)(2,1)S(1)}, u32[]{:S(2)}, u32[]{:S(2)}) collective-permute-start(bf16[64,1464]{1,0:T(8,128)(2,1)S(1)} %collective-permute-done.refs_0_), channel_id=1, source_target_pairs={{0,4},{4,8},{8,12},{12,14},{14,10},{10,6},{6,2},{2,0},{1,5},{5,9},... | collective-permute-start | bytes 562184 | tf_op jit(solution)/shard_map/ppermute | solution.py:197
  12.0 0.4 collective-permute-start.3
  12.5 0.0 collective-permute-start.6
  12.5 0.5 collective-permute-start.7
  13.0 3.5 %shard_map.66 = (bf16[720,1440]{1,0:T(8,128)(2,1)S(1)}, bf16[720,1440]{1,0:T(8,128)(2,1)S(1)}) custom-call(s32[2]{0:T(128)S(1)} %pad_add_fusion.after_this.place, bf16[720,2880]{1,0:T(8,128)(2,1)} %bitcast.13), custom_call_target="tpu_custom_call" | custom-call | bytes 16588800 | tf_op jit(solution)/shard_map/pallas_call | solution.py:108
  16.5 0.0 collective-permute-done.2.refs_0_
  16.5 1.2 %collective-permute-done.3.refs_1_ = bf16[64,1464]{1,0:T(8,128)(2,1)S(1)} collective-permute-done((bf16[64,1464]{1,0:T(8,128)(2,1)S(1)}, bf16[64,1464]{1,0:T(8,128)(2,1)S(1)}, u32[]{:S(2)}, u32[]{:S(2)}) %collective-permute-start.3) | collective-permute-done | bytes 187424 | tf_op jit(solution)/shard_map/ppermute | solution.py:198
  17.7 1.6 %collective-permute-start.4 = (bf16[64,1464]{1,0:T(8,128)(2,1)S(1)}, bf16[64,1464]{1,0:T(8,128)(2,1)S(1)}, u32[]{:S(2)}, u32[]{:S(2)}) collective-permute-start(bf16[64,1464]{1,0:T(8,128)(2,1)S(1)} %collective-permute-done.2.refs_0_), channel_id=1, source_target_pairs={{0,4},{4,8},{8,12},{12,14},{14,10},{10,6},{6,2},{2,0},{1,5},{5,9},... | collective-permute-start | bytes 562184 | tf_op jit(solution)/shard_map/ppermute | solution.py:197
  19.3 0.4 collective-permute-start.5
  19.7 0.0 collective-permute-done.6.refs_2_
  19.7 2.7 %shard_map.67 = (bf16[128,1440]{1,0:T(8,128)(2,1)S(1)}, bf16[128,1440]{1,0:T(8,128)(2,1)S(1)}) custom-call(s32[2]{0:T(128)S(1)} %pad_add_fusion.after_this.place, bf16[64,1464]{1,0:T(8,128)(2,1)S(1)} %collective-permute-done.refs_0_, bf16[64,1464]{1,0:T(8,128)(2,1)S(1)} %collective-permute-done.1.refs_1_, ...), custom_call_target="tpu_custom_call" | custom-call | flops 1592524800 | bytes 12441600 | tf_op jit(solution)/shard_map/pallas_call | solution.py:155
  22.4 0.9 %collective-permute-done.4.refs_0_ = bf16[64,1464]{1,0:T(8,128)(2,1)S(1)} collective-permute-done((bf16[64,1464]{1,0:T(8,128)(2,1)S(1)}, bf16[64,1464]{1,0:T(8,128)(2,1)S(1)}, u32[]{:S(2)}, u32[]{:S(2)}) %collective-permute-start.4) | collective-permute-done | bytes 187424 | tf_op jit(solution)/shard_map/ppermute | solution.py:197
  23.4 1.6 %collective-permute-done.5.refs_1_ = bf16[64,1464]{1,0:T(8,128)(2,1)S(1)} collective-permute-done((bf16[64,1464]{1,0:T(8,128)(2,1)S(1)}, bf16[64,1464]{1,0:T(8,128)(2,1)S(1)}, u32[]{:S(2)}, u32[]{:S(2)}) %collective-permute-start.5) | collective-permute-done | bytes 187424 | tf_op jit(solution)/shard_map/ppermute | solution.py:198
  24.9 0.0 collective-permute-start.10
  24.9 0.5 collective-permute-start.11
  25.5 1.5 %collective-permute-start.8 = (bf16[32,1464]{1,0:T(8,128)(2,1)S(1)}, bf16[32,1464]{1,0:T(8,128)(2,1)S(1)}, u32[]{:S(2)}, u32[]{:S(2)}) collective-permute-start(bf16[32,1464]{1,0:T(8,128)(2,1)S(1)} %slice.54), channel_id=1, source_target_pairs={{0,4},{4,8},{8,12},{12,14},{14,10},{10,6},{6,2},{2,0},{1,5},{5,9},... | collective-permute-start | bytes 281096 | tf_op jit(solution)/shard_map/ppermute | solution.py:206
  27.0 0.5 collective-permute-start.9
  27.5 0.0 collective-permute-done.10.refs_2_
  27.6 2.7 %shard_map.68 = (bf16[128,1440]{1,0:T(8,128)(2,1)S(1)}, bf16[128,1440]{1,0:T(8,128)(2,1)S(1)}) custom-call(s32[2]{0:T(128)S(1)} %pad_add_fusion.after_this.place, bf16[64,1464]{1,0:T(8,128)(2,1)S(1)} %collective-permute-done.4.refs_0_, bf16[64,1464]{1,0:T(8,128)(2,1)S(1)} %collective-permute-done.5.refs_1_, ...), custom_call_target="tpu_custom_call" | custom-call | flops 1592524800 | bytes 12441600 | tf_op jit(solution)/shard_map/pallas_call | solution.py:155
  30.3 0.0 collective-permute-done.8.refs_0_
  30.3 1.4 %collective-permute-done.9.refs_1_ = bf16[32,1464]{1,0:T(8,128)(2,1)S(1)} collective-permute-done((bf16[32,1464]{1,0:T(8,128)(2,1)S(1)}, bf16[32,1464]{1,0:T(8,128)(2,1)S(1)}, u32[]{:S(2)}, u32[]{:S(2)}) %collective-permute-start.9) | collective-permute-done | bytes 93728 | tf_op jit(solution)/shard_map/ppermute | solution.py:207
  31.6 0.0 collective-permute-start.12
  31.6 0.5 collective-permute-start.13
  32.1 0.8 %collective-permute-done.12.refs_2_ = bf16[32,1464]{1,0:T(8,128)(2,1)S(1)} collective-permute-done((bf16[32,1464]{1,0:T(8,128)(2,1)S(1)}, bf16[32,1464]{1,0:T(8,128)(2,1)S(1)}, u32[]{:S(2)}, u32[]{:S(2)}) %collective-permute-start.12) | collective-permute-done | bytes 93728 | tf_op jit(solution)/shard_map/ppermute | solution.py:211
  32.9 0.2 collective-permute-done.13.refs_3_
  33.1 3.0 %shard_map.69 = (bf16[64,1440]{1,0:T(8,128)(2,1)S(1)}, bf16[64,1440]{1,0:T(8,128)(2,1)S(1)}) custom-call(s32[2]{0:T(128)S(1)} %pad_add_fusion.after_this.place, bf16[32,1464]{1,0:T(8,128)(2,1)S(1)} %collective-permute-done.8.refs_0_, bf16[32,1464]{1,0:T(8,128)(2,1)S(1)} %collective-permute-done.9.refs_1_, ...), custom_call_target="tpu_custom_call" | custom-call | flops 796262400 | bytes 12441600 | tf_op jit(solution)/shard_map/pallas_call | solution.py:155
  36.1 0.4 collective-permute-start.21
  36.5 0.2 collective-permute-start.17
  36.7 0.4 collective-permute-start.18
  37.1 0.2 collective-permute-start.20
  37.2 0.4 collective-permute-done.21
  37.7 1.3 %collective-permute-start.22 = (bf16[32,1440]{1,0:T(8,128)(2,1)S(1)}, bf16[32,1440]{1,0:T(8,128)(2,1)S(1)}, u32[]{:S(2)}, u32[]{:S(2)}) collective-permute-start(bf16[32,1440]{1,0:T(8,128)(2,1)S(1)} %get-tuple-element.61), channel_id=1, source_target_pairs={{0,4},{4,8},{8,12},{12,14},{14,10},{10,6},{6,2},{2,0},{1,5},{5,9},... | collective-permute-start | bytes 276488 | tf_op jit(solution)/shard_map/ppermute | solution.py:220
  39.0 0.8 %collective-permute-start.26 = (bf16[32,1440]{1,0:T(8,128)(2,1)S(1)}, bf16[32,1440]{1,0:T(8,128)(2,1)S(1)}, u32[]{:S(2)}, u32[]{:S(2)}) collective-permute-start(bf16[32,1440]{1,0:T(8,128)(2,1)S(1)} %get-tuple-element.62), channel_id=1, source_target_pairs={{4,0},{8,4},{12,8},{14,12},{10,14},{6,10},{2,6},{0,2},{5,1},{9,5},... | collective-permute-start | bytes 276488 | tf_op jit(solution)/shard_map/ppermute | solution.py:221
  39.8 2.7 %shard_map.71 = (bf16[128,1440]{1,0:T(8,128)(2,1)S(1)}, bf16[128,1440]{1,0:T(8,128)(2,1)S(1)}) custom-call(s32[2]{0:T(128)S(1)} %pad_add_fusion.after_this.place, bf16[64,1464]{1,0:T(8,128)(2,1)S(1)} %collective-permute-done.2.refs_0_, bf16[64,1464]{1,0:T(8,128)(2,1)S(1)} %collective-permute-done.3.refs_1_, ...), custom_call_target="tpu_custom_call" | custom-call | flops 1592524800 | bytes 12441600 | tf_op jit(solution)/shard_map/pallas_call | solution.py:155
  42.5 0.1 collective-permute-start.19
  42.6 0.0 collective-permute-done.20
  42.6 0.2 collective-permute-done.22
  42.8 1.0 %collective-permute-done.26 = bf16[32,1440]{1,0:T(8,128)(2,1)S(1)} collective-permute-done((bf16[32,1440]{1,0:T(8,128)(2,1)S(1)}, bf16[32,1440]{1,0:T(8,128)(2,1)S(1)}, u32[]{:S(2)}, u32[]{:S(2)}) %collective-permute-start.26) | collective-permute-done | bytes 92192 | tf_op jit(solution)/shard_map/ppermute | solution.py:221
  43.8 0.1 add_convert_fusion.6
  43.9 1.2 %collective-permute-start.23 = (bf16[64,1440]{1,0:T(8,128)(2,1)S(1)}, bf16[64,1440]{1,0:T(8,128)(2,1)S(1)}, u32[]{:S(2)}, u32[]{:S(2)}) collective-permute-start(bf16[64,1440]{1,0:T(8,128)(2,1)S(1)} %get-tuple-element.59), channel_id=1, source_target_pairs={{0,4},{4,8},{8,12},{12,14},{14,10},{10,6},{6,2},{2,0},{1,5},{5,9},... | collective-permute-start | bytes 552968 | tf_op jit(solution)/shard_map/ppermute | solution.py:220
  45.1 0.9 %collective-permute-start.27 = (bf16[64,1440]{1,0:T(8,128)(2,1)S(1)}, bf16[64,1440]{1,0:T(8,128)(2,1)S(1)}, u32[]{:S(2)}, u32[]{:S(2)}) collective-permute-start(bf16[64,1440]{1,0:T(8,128)(2,1)S(1)} %get-tuple-element.60), channel_id=1, source_target_pairs={{4,0},{8,4},{12,8},{14,12},{10,14},{6,10},{2,6},{0,2},{5,1},{9,5},... | collective-permute-start | bytes 552968 | tf_op jit(solution)/shard_map/ppermute | solution.py:221
  46.0 0.0 collective-permute-start.14
  46.0 0.5 collective-permute-start.16
  46.5 0.0 collective-permute-done.19
  46.5 3.6 %collective-permute-done.23 = bf16[64,1440]{1,0:T(8,128)(2,1)S(1)} collective-permute-done((bf16[64,1440]{1,0:T(8,128)(2,1)S(1)}, bf16[64,1440]{1,0:T(8,128)(2,1)S(1)}, u32[]{:S(2)}, u32[]{:S(2)}) %collective-permute-start.23) | collective-permute-done | bytes 184352 | tf_op jit(solution)/shard_map/ppermute | solution.py:220
  50.1 1.0 %collective-permute-done.27 = bf16[64,1440]{1,0:T(8,128)(2,1)S(1)} collective-permute-done((bf16[64,1440]{1,0:T(8,128)(2,1)S(1)}, bf16[64,1440]{1,0:T(8,128)(2,1)S(1)}, u32[]{:S(2)}, u32[]{:S(2)}) %collective-permute-start.27) | collective-permute-done | bytes 184352 | tf_op jit(solution)/shard_map/ppermute | solution.py:221
  51.1 0.1 add_convert_fusion.5
  51.2 1.2 %collective-permute-start.24 = (bf16[64,1440]{1,0:T(8,128)(2,1)S(1)}, bf16[64,1440]{1,0:T(8,128)(2,1)S(1)}, u32[]{:S(2)}, u32[]{:S(2)}) collective-permute-start(bf16[64,1440]{1,0:T(8,128)(2,1)S(1)} %get-tuple-element.57), channel_id=1, source_target_pairs={{0,4},{4,8},{8,12},{12,14},{14,10},{10,6},{6,2},{2,0},{1,5},{5,9},... | collective-permute-start | bytes 552968 | tf_op jit(solution)/shard_map/ppermute | solution.py:220
  52.4 0.9 %collective-permute-start.28 = (bf16[64,1440]{1,0:T(8,128)(2,1)S(1)}, bf16[64,1440]{1,0:T(8,128)(2,1)S(1)}, u32[]{:S(2)}, u32[]{:S(2)}) collective-permute-start(bf16[64,1440]{1,0:T(8,128)(2,1)S(1)} %get-tuple-element.58), channel_id=1, source_target_pairs={{4,0},{8,4},{12,8},{14,12},{10,14},{6,10},{2,6},{0,2},{5,1},{9,5},... | collective-permute-start | bytes 552968 | tf_op jit(solution)/shard_map/ppermute | solution.py:221
  53.3 3.0 %shard_map.70 = (bf16[64,1440]{1,0:T(8,128)(2,1)S(1)}, bf16[64,1440]{1,0:T(8,128)(2,1)S(1)}) custom-call(s32[2]{0:T(128)S(1)} %pad_add_fusion.after_this.place, bf16[64,1464]{1,0:T(8,128)(2,1)S(1)} %shard_map.64.refs_0_, bf16[64,1464]{1,0:T(8,128)(2,1)S(1)} %collective-permute-done.14.refs_1_, bf16[2880,720]{1,0:T(8,128)(2,1)S(1)} %get-tuple-element.38.refs_4_.refs_2_, ...), custom_call_target="tpu_custom_call" | custom-call | flops 796262400 | bytes 12441600 | tf_op jit(solution)/shard_map/pallas_call | solution.py:155
  56.3 0.1 collective-permute-start.15
  56.4 0.5 collective-permute-done.24
  56.9 1.1 %collective-permute-done.28 = bf16[64,1440]{1,0:T(8,128)(2,1)S(1)} collective-permute-done((bf16[64,1440]{1,0:T(8,128)(2,1)S(1)}, bf16[64,1440]{1,0:T(8,128)(2,1)S(1)}, u32[]{:S(2)}, u32[]{:S(2)}) %collective-permute-start.28) | collective-permute-done | bytes 184352 | tf_op jit(solution)/shard_map/ppermute | solution.py:221
  58.0 0.1 add_convert_fusion.4
  58.2 1.0 %collective-permute-start.29 = (bf16[64,1440]{1,0:T(8,128)(2,1)S(1)}, bf16[64,1440]{1,0:T(8,128)(2,1)S(1)}, u32[]{:S(2)}, u32[]{:S(2)}) collective-permute-start(bf16[64,1440]{1,0:T(8,128)(2,1)S(1)} %get-tuple-element.56), channel_id=1, source_target_pairs={{4,0},{8,4},{12,8},{14,12},{10,14},{6,10},{2,6},{0,2},{5,1},{9,5},... | collective-permute-start | bytes 552968 | tf_op jit(solution)/shard_map/ppermute | solution.py:221
  59.2 1.1 %collective-permute-start.25 = (bf16[64,1440]{1,0:T(8,128)(2,1)S(1)}, bf16[64,1440]{1,0:T(8,128)(2,1)S(1)}, u32[]{:S(2)}, u32[]{:S(2)}) collective-permute-start(bf16[64,1440]{1,0:T(8,128)(2,1)S(1)} %get-tuple-element.55), channel_id=1, source_target_pairs={{0,4},{4,8},{8,12},{12,14},{14,10},{10,6},{6,2},{2,0},{1,5},{5,9},... | collective-permute-start | bytes 552968 | tf_op jit(solution)/shard_map/ppermute | solution.py:220
  60.3 3.6 %collective-permute-done.29 = bf16[64,1440]{1,0:T(8,128)(2,1)S(1)} collective-permute-done((bf16[64,1440]{1,0:T(8,128)(2,1)S(1)}, bf16[64,1440]{1,0:T(8,128)(2,1)S(1)}, u32[]{:S(2)}, u32[]{:S(2)}) %collective-permute-start.29) | collective-permute-done | bytes 184352 | tf_op jit(solution)/shard_map/ppermute | solution.py:221
  63.9 0.9 %collective-permute-done.25 = bf16[64,1440]{1,0:T(8,128)(2,1)S(1)} collective-permute-done((bf16[64,1440]{1,0:T(8,128)(2,1)S(1)}, bf16[64,1440]{1,0:T(8,128)(2,1)S(1)}, u32[]{:S(2)}, u32[]{:S(2)}) %collective-permute-start.25) | collective-permute-done | bytes 184352 | tf_op jit(solution)/shard_map/ppermute | solution.py:220
  64.8 0.8 %add_convert_fusion = bf16[64,1440]{1,0:T(8,128)(2,1)} fusion(bf16[64,1440]{1,0:T(8,128)(2,1)S(1)} %collective-permute-done.29, bf16[64,1440]{1,0:T(8,128)(2,1)S(1)} %collective-permute-done.25, bf16[64,1440]{1,0:T(8,128)(2,1)S(1)} %collective-permute-done.15, bf16[64,1440]{1,0:T(8,128)(2,1)S(1)} %get-tuple-element.48), kind=kLoop, calls=%fused_computation | loop fusion | flops 737280 | bytes 921600 | tf_op jit(solution)/shard_map/convert_element_type | solution.py:228
  (12 shorter events, 0.1 us)
Async XLA Ops:
  1.0 8.4 %collective-permute-start = (bf16[64,1464]{1,0:T(8,128)(2,1)S(1)}, bf16[64,1464]{1,0:T(8,128)(2,1)S(1)}, u32[]{:S(2)}, u32[]{:S(2)}) collective-permute-start(bf16[64,1464]{1,0:T(8,128)(2,1)S(1)} %shard_map.64.refs_0_), channel_id=1, source_target_pairs={{0,4},{4,8},{8,12},{12,14},{14,10},{10,6},{6,2},{2,0},{1,5},{5,9},... | collective-permute-start | bytes 562184 | tf_op jit(solution)/shard_map/ppermute | solution.py:191
  4.1 6.4 %collective-permute-start.1 = (bf16[64,1464]{1,0:T(8,128)(2,1)S(1)}, bf16[64,1464]{1,0:T(8,128)(2,1)S(1)}, u32[]{:S(2)}, u32[]{:S(2)}) collective-permute-start(bf16[64,1464]{1,0:T(8,128)(2,1)S(1)} %shard_map.64.refs_0_), channel_id=1, source_target_pairs={{4,0},{8,4},{12,8},{14,12},{10,14},{6,10},{2,6},{0,2},{5,1},{9,5},... | collective-permute-start | bytes 562184 | tf_op jit(solution)/shard_map/ppermute | solution.py:192
  10.4 6.0 %collective-permute-start.2 = (bf16[64,1464]{1,0:T(8,128)(2,1)S(1)}, bf16[64,1464]{1,0:T(8,128)(2,1)S(1)}, u32[]{:S(2)}, u32[]{:S(2)}) collective-permute-start(bf16[64,1464]{1,0:T(8,128)(2,1)S(1)} %collective-permute-done.refs_0_), channel_id=1, source_target_pairs={{0,4},{4,8},{8,12},{12,14},{14,10},{10,6},{6,2},{2,0},{1,5},{5,9},... | collective-permute-start | bytes 562184 | tf_op jit(solution)/shard_map/ppermute | solution.py:197
  12.0 5.7 %collective-permute-start.3 = (bf16[64,1464]{1,0:T(8,128)(2,1)S(1)}, bf16[64,1464]{1,0:T(8,128)(2,1)S(1)}, u32[]{:S(2)}, u32[]{:S(2)}) collective-permute-start(bf16[64,1464]{1,0:T(8,128)(2,1)S(1)} %collective-permute-done.1.refs_1_), channel_id=1, source_target_pairs={{4,0},{8,4},{12,8},{14,12},{10,14},{6,10},{2,6},{0,2},{5,1},{9,5},... | collective-permute-start | bytes 562184 | tf_op jit(solution)/shard_map/ppermute | solution.py:198
  12.5 7.3 %collective-permute-start.6 = (bf16[64,1464]{1,0:T(8,128)(2,1)S(1)}, bf16[64,1464]{1,0:T(8,128)(2,1)S(1)}, u32[]{:S(2)}, u32[]{:S(2)}) collective-permute-start(bf16[64,1464]{1,0:T(8,128)(2,1)S(1)} %collective-permute-done.refs_0_), channel_id=1, source_target_pairs={{0,1},{1,0},{2,3},{3,2},{4,5},{5,4},{6,7},{7,6},{8,9},{9,8},{10,11... | collective-permute-start | bytes 562184 | tf_op jit(solution)/shard_map/ppermute | solution.py:199
  12.5 7.3 %collective-permute-start.7 = (bf16[64,1464]{1,0:T(8,128)(2,1)S(1)}, bf16[64,1464]{1,0:T(8,128)(2,1)S(1)}, u32[]{:S(2)}, u32[]{:S(2)}) collective-permute-start(bf16[64,1464]{1,0:T(8,128)(2,1)S(1)} %collective-permute-done.1.refs_1_), channel_id=1, source_target_pairs={{0,1},{1,0},{2,3},{3,2},{4,5},{5,4},{6,7},{7,6},{8,9},{9,8},{10,11... | collective-permute-start | bytes 562184 | tf_op jit(solution)/shard_map/ppermute | solution.py:199
  17.7 5.7 %collective-permute-start.4 = (bf16[64,1464]{1,0:T(8,128)(2,1)S(1)}, bf16[64,1464]{1,0:T(8,128)(2,1)S(1)}, u32[]{:S(2)}, u32[]{:S(2)}) collective-permute-start(bf16[64,1464]{1,0:T(8,128)(2,1)S(1)} %collective-permute-done.2.refs_0_), channel_id=1, source_target_pairs={{0,4},{4,8},{8,12},{12,14},{14,10},{10,6},{6,2},{2,0},{1,5},{5,9},... | collective-permute-start | bytes 562184 | tf_op jit(solution)/shard_map/ppermute | solution.py:197
  19.3 5.7 %collective-permute-start.5 = (bf16[64,1464]{1,0:T(8,128)(2,1)S(1)}, bf16[64,1464]{1,0:T(8,128)(2,1)S(1)}, u32[]{:S(2)}, u32[]{:S(2)}) collective-permute-start(bf16[64,1464]{1,0:T(8,128)(2,1)S(1)} %collective-permute-done.3.refs_1_), channel_id=1, source_target_pairs={{4,0},{8,4},{12,8},{14,12},{10,14},{6,10},{2,6},{0,2},{5,1},{9,5},... | collective-permute-start | bytes 562184 | tf_op jit(solution)/shard_map/ppermute | solution.py:198
  24.9 2.6 %collective-permute-start.10 = (bf16[64,1464]{1,0:T(8,128)(2,1)S(1)}, bf16[64,1464]{1,0:T(8,128)(2,1)S(1)}, u32[]{:S(2)}, u32[]{:S(2)}) collective-permute-start(bf16[64,1464]{1,0:T(8,128)(2,1)S(1)} %collective-permute-done.4.refs_0_), channel_id=1, source_target_pairs={{0,1},{1,0},{2,3},{3,2},{4,5},{5,4},{6,7},{7,6},{8,9},{9,8},{10,11... | collective-permute-start | bytes 562184 | tf_op jit(solution)/shard_map/ppermute | solution.py:208
  24.9 2.6 %collective-permute-start.11 = (bf16[64,1464]{1,0:T(8,128)(2,1)S(1)}, bf16[64,1464]{1,0:T(8,128)(2,1)S(1)}, u32[]{:S(2)}, u32[]{:S(2)}) collective-permute-start(bf16[64,1464]{1,0:T(8,128)(2,1)S(1)} %collective-permute-done.5.refs_1_), channel_id=1, source_target_pairs={{0,1},{1,0},{2,3},{3,2},{4,5},{5,4},{6,7},{7,6},{8,9},{9,8},{10,11... | collective-permute-start | bytes 562184 | tf_op jit(solution)/shard_map/ppermute | solution.py:208
  25.5 4.8 %collective-permute-start.8 = (bf16[32,1464]{1,0:T(8,128)(2,1)S(1)}, bf16[32,1464]{1,0:T(8,128)(2,1)S(1)}, u32[]{:S(2)}, u32[]{:S(2)}) collective-permute-start(bf16[32,1464]{1,0:T(8,128)(2,1)S(1)} %slice.54), channel_id=1, source_target_pairs={{0,4},{4,8},{8,12},{12,14},{14,10},{10,6},{6,2},{2,0},{1,5},{5,9},... | collective-permute-start | bytes 281096 | tf_op jit(solution)/shard_map/ppermute | solution.py:206
  27.0 4.6 %collective-permute-start.9 = (bf16[32,1464]{1,0:T(8,128)(2,1)S(1)}, bf16[32,1464]{1,0:T(8,128)(2,1)S(1)}, u32[]{:S(2)}, u32[]{:S(2)}) collective-permute-start(bf16[32,1464]{1,0:T(8,128)(2,1)S(1)} %slice.55), channel_id=1, source_target_pairs={{4,0},{8,4},{12,8},{14,12},{10,14},{6,10},{2,6},{0,2},{5,1},{9,5},... | collective-permute-start | bytes 281096 | tf_op jit(solution)/shard_map/ppermute | solution.py:207
  31.6 1.3 %collective-permute-start.12 = (bf16[32,1464]{1,0:T(8,128)(2,1)S(1)}, bf16[32,1464]{1,0:T(8,128)(2,1)S(1)}, u32[]{:S(2)}, u32[]{:S(2)}) collective-permute-start(bf16[32,1464]{1,0:T(8,128)(2,1)S(1)} %collective-permute-done.8.refs_0_), channel_id=1, source_target_pairs={{0,1},{1,0},{2,3},{3,2},{4,5},{5,4},{6,7},{7,6},{8,9},{9,8},{10,11... | collective-permute-start | bytes 281096 | tf_op jit(solution)/shard_map/ppermute | solution.py:211
  31.6 1.5 %collective-permute-start.13 = (bf16[32,1464]{1,0:T(8,128)(2,1)S(1)}, bf16[32,1464]{1,0:T(8,128)(2,1)S(1)}, u32[]{:S(2)}, u32[]{:S(2)}) collective-permute-start(bf16[32,1464]{1,0:T(8,128)(2,1)S(1)} %collective-permute-done.9.refs_1_), channel_id=1, source_target_pairs={{0,1},{1,0},{2,3},{3,2},{4,5},{5,4},{6,7},{7,6},{8,9},{9,8},{10,11... | collective-permute-start | bytes 281096 | tf_op jit(solution)/shard_map/ppermute | solution.py:211
  36.1 1.5 %collective-permute-start.21 = (bf16[64,1440]{1,0:T(8,128)(2,1)S(1)}, bf16[64,1440]{1,0:T(8,128)(2,1)S(1)}, u32[]{:S(2)}, u32[]{:S(2)}) collective-permute-start(bf16[64,1440]{1,0:T(8,128)(2,1)S(1)} %get-tuple-element.46), channel_id=1, source_target_pairs={{0,1},{1,0},{2,3},{3,2},{4,5},{5,4},{6,7},{7,6},{8,9},{9,8},{10,11... | collective-permute-start | bytes 552968 | tf_op jit(solution)/shard_map/ppermute | solution.py:183
  36.5 3.2 %collective-permute-start.17 = (bf16[64,1464]{1,0:T(8,128)(2,1)S(1)}, bf16[64,1464]{1,0:T(8,128)(2,1)S(1)}, u32[]{:S(2)}, u32[]{:S(2)}) collective-permute-start(bf16[64,1464]{1,0:T(8,128)(2,1)S(1)} %collective-permute-done.2.refs_0_), channel_id=1, source_target_pairs={{0,1},{1,0},{2,3},{3,2},{4,5},{5,4},{6,7},{7,6},{8,9},{9,8},{10,11... | collective-permute-start | bytes 562184 | tf_op jit(solution)/shard_map/ppermute | solution.py:199
  36.7 3.1 %collective-permute-start.18 = (bf16[64,1464]{1,0:T(8,128)(2,1)S(1)}, bf16[64,1464]{1,0:T(8,128)(2,1)S(1)}, u32[]{:S(2)}, u32[]{:S(2)}) collective-permute-start(bf16[64,1464]{1,0:T(8,128)(2,1)S(1)} %collective-permute-done.3.refs_1_), channel_id=1, source_target_pairs={{0,1},{1,0},{2,3},{3,2},{4,5},{5,4},{6,7},{7,6},{8,9},{9,8},{10,11... | collective-permute-start | bytes 562184 | tf_op jit(solution)/shard_map/ppermute | solution.py:199
  37.1 5.5 %collective-permute-start.20 = (bf16[128,1440]{1,0:T(8,128)(2,1)S(1)}, bf16[128,1440]{1,0:T(8,128)(2,1)S(1)}, u32[]{:S(2)}, u32[]{:S(2)}) collective-permute-start(bf16[128,1440]{1,0:T(8,128)(2,1)S(1)} %get-tuple-element.43), channel_id=1, source_target_pairs={{0,1},{1,0},{2,3},{3,2},{4,5},{5,4},{6,7},{7,6},{8,9},{9,8},{10,11... | collective-permute-start | bytes 1105928 | tf_op jit(solution)/shard_map/ppermute | solution.py:183
  37.7 5.1 %collective-permute-start.22 = (bf16[32,1440]{1,0:T(8,128)(2,1)S(1)}, bf16[32,1440]{1,0:T(8,128)(2,1)S(1)}, u32[]{:S(2)}, u32[]{:S(2)}) collective-permute-start(bf16[32,1440]{1,0:T(8,128)(2,1)S(1)} %get-tuple-element.61), channel_id=1, source_target_pairs={{0,4},{4,8},{8,12},{12,14},{14,10},{10,6},{6,2},{2,0},{1,5},{5,9},... | collective-permute-start | bytes 276488 | tf_op jit(solution)/shard_map/ppermute | solution.py:220
  39.0 4.8 %collective-permute-start.26 = (bf16[32,1440]{1,0:T(8,128)(2,1)S(1)}, bf16[32,1440]{1,0:T(8,128)(2,1)S(1)}, u32[]{:S(2)}, u32[]{:S(2)}) collective-permute-start(bf16[32,1440]{1,0:T(8,128)(2,1)S(1)} %get-tuple-element.62), channel_id=1, source_target_pairs={{4,0},{8,4},{12,8},{14,12},{10,14},{6,10},{2,6},{0,2},{5,1},{9,5},... | collective-permute-start | bytes 276488 | tf_op jit(solution)/shard_map/ppermute | solution.py:221
  42.5 4.0 %collective-permute-start.19 = (bf16[128,1440]{1,0:T(8,128)(2,1)S(1)}, bf16[128,1440]{1,0:T(8,128)(2,1)S(1)}, u32[]{:S(2)}, u32[]{:S(2)}) collective-permute-start(bf16[128,1440]{1,0:T(8,128)(2,1)S(1)} %get-tuple-element.52), channel_id=1, source_target_pairs={{0,1},{1,0},{2,3},{3,2},{4,5},{5,4},{6,7},{7,6},{8,9},{9,8},{10,11... | collective-permute-start | bytes 1105928 | tf_op jit(solution)/shard_map/ppermute | solution.py:183
  43.9 6.2 %collective-permute-start.23 = (bf16[64,1440]{1,0:T(8,128)(2,1)S(1)}, bf16[64,1440]{1,0:T(8,128)(2,1)S(1)}, u32[]{:S(2)}, u32[]{:S(2)}) collective-permute-start(bf16[64,1440]{1,0:T(8,128)(2,1)S(1)} %get-tuple-element.59), channel_id=1, source_target_pairs={{0,4},{4,8},{8,12},{12,14},{14,10},{10,6},{6,2},{2,0},{1,5},{5,9},... | collective-permute-start | bytes 552968 | tf_op jit(solution)/shard_map/ppermute | solution.py:220
  45.1 6.0 %collective-permute-start.27 = (bf16[64,1440]{1,0:T(8,128)(2,1)S(1)}, bf16[64,1440]{1,0:T(8,128)(2,1)S(1)}, u32[]{:S(2)}, u32[]{:S(2)}) collective-permute-start(bf16[64,1440]{1,0:T(8,128)(2,1)S(1)} %get-tuple-element.60), channel_id=1, source_target_pairs={{4,0},{8,4},{12,8},{14,12},{10,14},{6,10},{2,6},{0,2},{5,1},{9,5},... | collective-permute-start | bytes 552968 | tf_op jit(solution)/shard_map/ppermute | solution.py:221
  46.0 7.3 %collective-permute-start.14 = (bf16[64,1464]{1,0:T(8,128)(2,1)S(1)}, bf16[64,1464]{1,0:T(8,128)(2,1)S(1)}, u32[]{:S(2)}, u32[]{:S(2)}) collective-permute-start(bf16[64,1464]{1,0:T(8,128)(2,1)S(1)} %shard_map.64.refs_0_), channel_id=1, source_target_pairs={{0,1},{1,0},{2,3},{3,2},{4,5},{5,4},{6,7},{7,6},{8,9},{9,8},{10,11... | collective-permute-start | bytes 562184 | tf_op jit(solution)/shard_map/ppermute | solution.py:193
  46.0 10.4 %collective-permute-start.16 = (bf16[128,1440]{1,0:T(8,128)(2,1)S(1)}, bf16[128,1440]{1,0:T(8,128)(2,1)S(1)}, u32[]{:S(2)}, u32[]{:S(2)}) collective-permute-start(bf16[128,1440]{1,0:T(8,128)(2,1)S(1)} %get-tuple-element.40), channel_id=1, source_target_pairs={{0,1},{1,0},{2,3},{3,2},{4,5},{5,4},{6,7},{7,6},{8,9},{9,8},{10,11... | collective-permute-start | bytes 1105928 | tf_op jit(solution)/shard_map/ppermute | solution.py:183
  51.2 5.7 %collective-permute-start.24 = (bf16[64,1440]{1,0:T(8,128)(2,1)S(1)}, bf16[64,1440]{1,0:T(8,128)(2,1)S(1)}, u32[]{:S(2)}, u32[]{:S(2)}) collective-permute-start(bf16[64,1440]{1,0:T(8,128)(2,1)S(1)} %get-tuple-element.57), channel_id=1, source_target_pairs={{0,4},{4,8},{8,12},{12,14},{14,10},{10,6},{6,2},{2,0},{1,5},{5,9},... | collective-permute-start | bytes 552968 | tf_op jit(solution)/shard_map/ppermute | solution.py:220
  52.4 5.7 %collective-permute-start.28 = (bf16[64,1440]{1,0:T(8,128)(2,1)S(1)}, bf16[64,1440]{1,0:T(8,128)(2,1)S(1)}, u32[]{:S(2)}, u32[]{:S(2)}) collective-permute-start(bf16[64,1440]{1,0:T(8,128)(2,1)S(1)} %get-tuple-element.58), channel_id=1, source_target_pairs={{4,0},{8,4},{12,8},{14,12},{10,14},{6,10},{2,6},{0,2},{5,1},{9,5},... | collective-permute-start | bytes 552968 | tf_op jit(solution)/shard_map/ppermute | solution.py:221
  56.3 4.0 %collective-permute-start.15 = (bf16[64,1440]{1,0:T(8,128)(2,1)S(1)}, bf16[64,1440]{1,0:T(8,128)(2,1)S(1)}, u32[]{:S(2)}, u32[]{:S(2)}) collective-permute-start(bf16[64,1440]{1,0:T(8,128)(2,1)S(1)} %get-tuple-element.49), channel_id=1, source_target_pairs={{0,1},{1,0},{2,3},{3,2},{4,5},{5,4},{6,7},{7,6},{8,9},{9,8},{10,11... | collective-permute-start | bytes 552968 | tf_op jit(solution)/shard_map/ppermute | solution.py:183
  58.2 5.7 %collective-permute-start.29 = (bf16[64,1440]{1,0:T(8,128)(2,1)S(1)}, bf16[64,1440]{1,0:T(8,128)(2,1)S(1)}, u32[]{:S(2)}, u32[]{:S(2)}) collective-permute-start(bf16[64,1440]{1,0:T(8,128)(2,1)S(1)} %get-tuple-element.56), channel_id=1, source_target_pairs={{4,0},{8,4},{12,8},{14,12},{10,14},{6,10},{2,6},{0,2},{5,1},{9,5},... | collective-permute-start | bytes 552968 | tf_op jit(solution)/shard_map/ppermute | solution.py:221
  59.2 5.7 %collective-permute-start.25 = (bf16[64,1440]{1,0:T(8,128)(2,1)S(1)}, bf16[64,1440]{1,0:T(8,128)(2,1)S(1)}, u32[]{:S(2)}, u32[]{:S(2)}) collective-permute-start(bf16[64,1440]{1,0:T(8,128)(2,1)S(1)} %get-tuple-element.55), channel_id=1, source_target_pairs={{0,4},{4,8},{8,12},{12,14},{14,10},{10,6},{6,2},{2,0},{1,5},{5,9},... | collective-permute-start | bytes 552968 | tf_op jit(solution)/shard_map/ppermute | solution.py:220

commit v4 on v3

--- a/solution.py
+++ b/solution.py
@@ -186,6 +186,7 @@
             span = slice(start, start + came[k].shape[0])
             start = span.stop
             value[k] = mine[span].astype(jnp.float32) + theirs[span].astype(jnp.float32)
+            mine, theirs = lax.optimization_barrier((mine, theirs))
         return done
 
     came[1] = lax.ppermute(packed, "ep", ahead)
@@ -193,7 +194,7 @@
     across[0] = swap(packed)
     weights, done = [gate, up], up
     for k in range(2, far):
-        came[k - 1], came[1 - k] = after((came[k - 1], came[1 - k]), done)
+        came[k - 1], came[1 - k] = after(came[k - 1], done), after(came[1 - k], done)
         came[k] = lax.ppermute(came[k - 1], "ep", ahead)
         came[-k] = lax.ppermute(came[1 - k], "ep", back)
         across[k - 1], across[1 - k] = swap(came[k - 1]), swap(came[1 - k])
@@ -202,16 +203,14 @@
             done = weights[-1]
         else:
             done = run([k - 2, 2 - k])
-    came[far - 1], came[1 - far] = after((came[far - 1], came[1 - far]), done)
+    came[far - 1], came[1 - far] = after(came[far - 1], done), after(came[1 - far], done)
     came["low"] = lax.ppermute(came[far - 1][: rows // 2], "ep", ahead)
     came["high"] = lax.ppermute(came[1 - far][rows // 2 :], "ep", back)
     across[far - 1], across[1 - far] = swap(came[far - 1]), swap(came[1 - far])
     done = run([far - 1, 1 - far])
     came["low"], came["high"] = after((came["low"], came["high"]), done)
     across["low"], across["high"] = swap(came["low"]), swap(came["high"])
-    done = run(["low", "high"])
-    run([far - 2, 2 - far], done)
-    run([0], done)
+    run(["low", "high"])
 
     to_ahead = value["low"].astype(jnp.bfloat16)
     to_back = value["high"].astype(jnp.bfloat16)
@@ -219,12 +218,16 @@
     for k in range(far - 1, -1, -1):
         behind = lax.ppermute(to_ahead, "ep", ahead)
         front = lax.ppermute(to_back, "ep", back)
+        if k >= far - 2:
+            done = run([far - 2, 2 - far] if k == far - 1 else [0], (to_ahead, to_back))
         behind, front = behind.astype(jnp.float32), front.astype(jnp.float32)
         if k == far - 1:
             behind, front = jnp.pad(behind, pad_low), jnp.pad(front, pad_high)
         if k:
             to_ahead = (value[-k] + behind).astype(jnp.bfloat16)
             to_back = (value[k] + front).astype(jnp.bfloat16)
+        if k >= far - 2:
+            to_ahead, to_back = after(to_ahead, done), after(to_back, done)
     return (value[0] + behind + front).astype(jnp.bfloat16)
 
 

time: 65.8 us -> 63.1 us (0.959)
  waiting for transfers between devices: 19.4 us -> 16.6 us
    ppermute x4, waiting for transfers between devices: 6.75 us -> 0.58 us  [ring_body(): front = lax.ppermute(to_back, 'ep', back)]
    ppermute x4, waiting for transfers between devices: 5.19 us -> 9.73 us  [ring_body(): behind = lax.ppermute(to_ahead, 'ep', ahead)]
    ppermute x1, starting transfers between devices: 0.01 us -> 2.99 us  [ring_body(): came[-1] = lax.ppermute(packed, 'ep', back)]
    ppermute x1, starting transfers between devices: 3.08 us -> 0.15 us  [ring_body(): came[1] = lax.ppermute(packed, 'ep', ahead)]
    ppermute x4, starting transfers between devices: 3.55 us -> 6.47 us  [ring_body(): front = lax.ppermute(to_back, 'ep', back)]
    ppermute x4, starting transfers between devices: 4.78 us -> 2.02 us  [ring_body(): behind = lax.ppermute(to_ahead, 'ep', ahead)]
    ppermute x2, starting transfers between devices: 0.9 us -> 3.52 us  [ring_body(): came[-k] = lax.ppermute(came[1 - k], 'ep', back)]
    ppermute x2, starting transfers between devices: 3.15 us -> 0.59 us  [ring_body(): came[k] = lax.ppermute(came[k - 1], 'ep', ahead)]
  transfers between devices with their start and end apart: 30 -> 30, of which waited for: 16 -> 13; matrix products, arithmetic and copies ran while one was open for 1% -> 1% of each run, Pallas kernels for 30% -> 36%
where the time goes in v4:
time: 63.1 us; the launch traced here: 62.9 us
  Pallas kernels  23.9 us (38%)
  starting transfers between devices  20.9 us (33%)
  waiting for transfers between devices  16.6 us (26%)
  other arithmetic  1.32 us (2%)
    pallas_call x5, Pallas kernels, run_expert(): pl.pallas_call(functools.partial(expert_kernel, len(own), n_experts), out...  14.1 us
    ppermute x4, waiting for transfers between devices, ring_body(): behind = lax.ppermute(to_ahead, 'ep', ahead)  9.73 us
    ppermute x4, starting transfers between devices, ring_body(): front = lax.ppermute(to_back, 'ep', back)  6.47 us
    pallas_call x1, Pallas kernels, turn_weights(): pl.pallas_call(turn_kernel, out_shape=[in_vmem((width, hidden))] * 2, in_...  5.28 us
    ppermute x2, starting transfers between devices, ring_body(): came[-k] = lax.ppermute(came[1 - k], 'ep', back)  3.52 us
    pallas_call x1, Pallas kernels, halve_weights(): pl.pallas_call(halve_kernel, out_shape=[in_vmem((hidden, width // 2))] *...  3.47 us
    ppermute x1, starting transfers between devices, ring_body(): came[-1] = lax.ppermute(packed, 'ep', back)  2.99 us
    ppermute x2, waiting for transfers between devices, ring_body(): came[-k] = lax.ppermute(came[1 - k], 'ep', back)  2.35 us
  transfers between devices with their start and end apart: 30, of which 13 were waited for; matrix products, arithmetic and copies ran while one was open for 1% of the time, Pallas kernels for 36%

profile of v4, /device:TPU:0, one launch (start us, length us, event | category | flops | bytes accessed | tf_op | source)
XLA Modules:
  0.0 62.9 jit_solution(14672057479556120047)
XLA Ops:
  0.0 1.0 %shard_map.64.refs_0_ = bf16[64,1464]{1,0:T(8,128)(2,1)S(1)} custom-call(bf16[64,1440]{1,0:T(8,128)(2,1)} %tokens_in.1, s32[4,64]{1,0:T(4,128)} %bitcast.14, f32[4,64]{1,0:T(4,128)} %bitcast.15), custom_call_target="tpu_custom_call" | custom-call | tf_op jit(solution)/shard_map/pallas_call | solution.py:53
  1.0 3.0 %collective-permute-start.3 = (bf16[64,1464]{1,0:T(8,128)(2,1)S(1)}, bf16[64,1464]{1,0:T(8,128)(2,1)S(1)}, u32[]{:S(2)}, u32[]{:S(2)}) collective-permute-start(bf16[64,1464]{1,0:T(8,128)(2,1)S(1)} %shard_map.64.refs_0_), channel_id=1, source_target_pairs={{4,0},{8,4},{12,8},{14,12},{10,14},{6,10},{2,6},{0,2},{5,1},{9,5},... | collective-permute-start | bytes 562184 | tf_op jit(solution)/shard_map/ppermute | solution.py:193
  4.0 0.2 collective-permute-start
  4.1 0.1 pad_add_fusion.after_this.place
  4.2 5.3 %shard_map.65 = (bf16[2880,720]{1,0:T(8,128)(2,1)S(1)}, bf16[2880,720]{1,0:T(8,128)(2,1)S(1)}) custom-call(s32[2]{0:T(128)S(1)} %pad_add_fusion.after_this.place, bf16[720,2880]{1,0:T(8,128)(2,1)} %bitcast.11, bf16[720,2880]{1,0:T(8,128)(2,1)} %bitcast.12), custom_call_target="tpu_custom_call" | custom-call | bytes 16588800 | tf_op jit(solution)/shard_map/pallas_call | solution.py:77
  9.5 1.9 %collective-permute-start.6 = (bf16[64,1464]{1,0:T(8,128)(2,1)S(1)}, bf16[64,1464]{1,0:T(8,128)(2,1)S(1)}, u32[]{:S(2)}, u32[]{:S(2)}) collective-permute-start(bf16[64,1464]{1,0:T(8,128)(2,1)S(1)} %collective-permute-done.3.refs_1_), channel_id=1, source_target_pairs={{4,0},{8,4},{12,8},{14,12},{10,14},{6,10},{2,6},{0,2},{5,1},{9,5},... | collective-permute-start | bytes 562184 | tf_op jit(solution)/shard_map/ppermute | solution.py:199
  11.5 0.2 collective-permute-start.1
  11.6 0.5 collective-permute-start.5
  12.1 3.5 %shard_map.66 = (bf16[720,1440]{1,0:T(8,128)(2,1)S(1)}, bf16[720,1440]{1,0:T(8,128)(2,1)S(1)}) custom-call(s32[2]{0:T(128)S(1)} %pad_add_fusion.after_this.place, bf16[720,2880]{1,0:T(8,128)(2,1)} %bitcast.13), custom_call_target="tpu_custom_call" | custom-call | bytes 16588800 | tf_op jit(solution)/shard_map/pallas_call | solution.py:108
  15.6 0.3 collective-permute-done.6.refs_1_
  15.9 1.6 %collective-permute-start.7 = (bf16[64,1464]{1,0:T(8,128)(2,1)S(1)}, bf16[64,1464]{1,0:T(8,128)(2,1)S(1)}, u32[]{:S(2)}, u32[]{:S(2)}) collective-permute-start(bf16[64,1464]{1,0:T(8,128)(2,1)S(1)} %collective-permute-done.6.refs_1_), channel_id=1, source_target_pairs={{4,0},{8,4},{12,8},{14,12},{10,14},{6,10},{2,6},{0,2},{5,1},{9,5},... | collective-permute-start | bytes 562184 | tf_op jit(solution)/shard_map/ppermute | solution.py:199
  17.5 0.0 collective-permute-done.1.refs_0_
  17.5 0.4 collective-permute-start.2
  18.0 2.7 %shard_map.67 = (bf16[128,1440]{1,0:T(8,128)(2,1)S(1)}, bf16[128,1440]{1,0:T(8,128)(2,1)S(1)}) custom-call(s32[2]{0:T(128)S(1)} %pad_add_fusion.after_this.place, bf16[64,1464]{1,0:T(8,128)(2,1)S(1)} %collective-permute-done.refs_0_, bf16[64,1464]{1,0:T(8,128)(2,1)S(1)} %collective-permute-done.3.refs_1_, ...), custom_call_target="tpu_custom_call" | custom-call | flops 1592524800 | bytes 12441600 | tf_op jit(solution)/shard_map/pallas_call | solution.py:155
  20.7 2.0 %collective-permute-done.7.refs_1_ = bf16[64,1464]{1,0:T(8,128)(2,1)S(1)} collective-permute-done((bf16[64,1464]{1,0:T(8,128)(2,1)S(1)}, bf16[64,1464]{1,0:T(8,128)(2,1)S(1)}, u32[]{:S(2)}, u32[]{:S(2)}) %collective-permute-start.7) | collective-permute-done | bytes 187424 | tf_op jit(solution)/shard_map/ppermute | solution.py:199
  22.7 0.0 collective-permute-start.9
  22.7 1.4 %collective-permute-done.2.refs_0_ = bf16[64,1464]{1,0:T(8,128)(2,1)S(1)} collective-permute-done((bf16[64,1464]{1,0:T(8,128)(2,1)S(1)}, bf16[64,1464]{1,0:T(8,128)(2,1)S(1)}, u32[]{:S(2)}, u32[]{:S(2)}) %collective-permute-start.2) | collective-permute-done | bytes 187424 | tf_op jit(solution)/shard_map/ppermute | solution.py:198
  24.1 0.0 collective-permute-start.8
  24.1 0.5 collective-permute-start.22
  24.6 1.6 %collective-permute-start.12 = (bf16[32,1464]{1,0:T(8,128)(2,1)S(1)}, bf16[32,1464]{1,0:T(8,128)(2,1)S(1)}, u32[]{:S(2)}, u32[]{:S(2)}) collective-permute-start(bf16[32,1464]{1,0:T(8,128)(2,1)S(1)} %slice.57), channel_id=1, source_target_pairs={{4,0},{8,4},{12,8},{14,12},{10,14},{6,10},{2,6},{0,2},{5,1},{9,5},... | collective-permute-start | bytes 281096 | tf_op jit(solution)/shard_map/ppermute | solution.py:208
  26.2 0.4 collective-permute-start.11
  26.7 0.0 collective-permute-done.9.refs_3_
  26.7 2.7 %shard_map.68 = (bf16[128,1440]{1,0:T(8,128)(2,1)S(1)}, bf16[128,1440]{1,0:T(8,128)(2,1)S(1)}) custom-call(s32[2]{0:T(128)S(1)} %pad_add_fusion.after_this.place, bf16[64,1464]{1,0:T(8,128)(2,1)S(1)} %collective-permute-done.2.refs_0_, bf16[64,1464]{1,0:T(8,128)(2,1)S(1)} %collective-permute-done.7.refs_1_, ...), custom_call_target="tpu_custom_call" | custom-call | flops 1592524800 | bytes 12441600 | tf_op jit(solution)/shard_map/pallas_call | solution.py:155
  29.4 0.0 collective-permute-done.12.refs_1_
  29.4 1.4 %collective-permute-done.11.refs_0_ = bf16[32,1464]{1,0:T(8,128)(2,1)S(1)} collective-permute-done((bf16[32,1464]{1,0:T(8,128)(2,1)S(1)}, bf16[32,1464]{1,0:T(8,128)(2,1)S(1)}, u32[]{:S(2)}, u32[]{:S(2)}) %collective-permute-start.11) | collective-permute-done | bytes 93728 | tf_op jit(solution)/shard_map/ppermute | solution.py:207
  30.8 0.0 collective-permute-start.13
  30.8 0.5 collective-permute-start.14
  31.4 0.8 %collective-permute-done.13.refs_2_ = bf16[32,1464]{1,0:T(8,128)(2,1)S(1)} collective-permute-done((bf16[32,1464]{1,0:T(8,128)(2,1)S(1)}, bf16[32,1464]{1,0:T(8,128)(2,1)S(1)}, u32[]{:S(2)}, u32[]{:S(2)}) %collective-permute-start.13) | collective-permute-done | bytes 93728 | tf_op jit(solution)/shard_map/ppermute | solution.py:212
  32.1 0.2 collective-permute-done.14.refs_3_
  32.3 3.0 %shard_map.69 = (bf16[64,1440]{1,0:T(8,128)(2,1)S(1)}, bf16[64,1440]{1,0:T(8,128)(2,1)S(1)}) custom-call(s32[2]{0:T(128)S(1)} %pad_add_fusion.after_this.place, bf16[32,1464]{1,0:T(8,128)(2,1)S(1)} %collective-permute-done.11.refs_0_, bf16[32,1464]{1,0:T(8,128)(2,1)S(1)} %collective-permute-done.12.refs_1_, ...), custom_call_target="tpu_custom_call" | custom-call | flops 796262400 | bytes 12441600 | tf_op jit(solution)/shard_map/pallas_call | solution.py:155
  35.3 0.4 collective-permute-start.15
  35.8 0.2 collective-permute-start.20
  35.9 0.4 collective-permute-start.17
  36.3 0.2 collective-permute-start.18
  36.4 0.0 collective-permute-done.22
  36.4 0.4 collective-permute-start.10
  36.8 0.1 collective-permute-done.15
  36.9 0.5 collective-permute-start.16
  37.4 0.1 collective-permute-done.17.refs_2_
  37.5 1.6 %collective-permute-start.19 = (bf16[32,1440]{1,0:T(8,128)(2,1)S(1)}, bf16[32,1440]{1,0:T(8,128)(2,1)S(1)}, u32[]{:S(2)}, u32[]{:S(2)}) collective-permute-start(bf16[32,1440]{1,0:T(8,128)(2,1)S(1)} %get-tuple-element.81), channel_id=1, source_target_pairs={{4,0},{8,4},{12,8},{14,12},{10,14},{6,10},{2,6},{0,2},{5,1},{9,5},... | collective-permute-start | bytes 276488 | tf_op jit(solution)/shard_map/ppermute | solution.py:220
  39.1 0.0 collective-permute-done.18.refs_3_
  39.1 2.7 %shard_map.70 = (bf16[128,1440]{1,0:T(8,128)(2,1)S(1)}, bf16[128,1440]{1,0:T(8,128)(2,1)S(1)}) custom-call(s32[2]{0:T(128)S(1)} %pad_add_fusion.after_this.place, bf16[64,1464]{1,0:T(8,128)(2,1)S(1)} %collective-permute-done.1.refs_0_, bf16[64,1464]{1,0:T(8,128)(2,1)S(1)} %collective-permute-done.6.refs_1_, ...), custom_call_target="tpu_custom_call" | custom-call | flops 1592524800 | bytes 12441600 | tf_op jit(solution)/shard_map/pallas_call | solution.py:155
  41.8 0.1 collective-permute-start.23
  41.8 0.0 collective-permute-done.10
  41.9 0.1 collective-permute-done.16
  42.0 0.1 add_convert_fusion.6
  42.1 0.5 collective-permute-start.24
  42.6 0.1 add_convert_fusion.5
  42.6 1.6 %collective-permute-start.27 = (bf16[64,1440]{1,0:T(8,128)(2,1)S(1)}, bf16[64,1440]{1,0:T(8,128)(2,1)S(1)}, u32[]{:S(2)}, u32[]{:S(2)}) collective-permute-start(bf16[64,1440]{1,0:T(8,128)(2,1)S(1)} %add_convert_fusion.5), channel_id=1, source_target_pairs={{4,0},{8,4},{12,8},{14,12},{10,14},{6,10},{2,6},{0,2},{5,1},{9,5},... | collective-permute-start | bytes 552968 | tf_op jit(solution)/shard_map/ppermute | solution.py:220
  44.3 3.0 %shard_map.71 = (bf16[64,1440]{1,0:T(8,128)(2,1)S(1)}, bf16[64,1440]{1,0:T(8,128)(2,1)S(1)}) custom-call(s32[2]{0:T(128)S(1)} %pad_add_fusion.after_this.place, bf16[64,1464]{1,0:T(8,128)(2,1)S(1)} %shard_map.64.refs_0_, bf16[64,1464]{1,0:T(8,128)(2,1)S(1)} %collective-permute-done.20.refs_1_, bf16[2880,720]{1,0:T(8,128)(2,1)S(1)} %get-tuple-element.50.refs_4_.refs_2_, ...), custom_call_target="tpu_custom_call" | custom-call | flops 796262400 | bytes 12441600 | tf_op jit(solution)/shard_map/pallas_call | solution.py:155
  47.3 0.1 collective-permute-start.21
  47.4 1.9 %collective-permute-done.24 = bf16[64,1440]{1,0:T(8,128)(2,1)S(1)} collective-permute-done((bf16[64,1440]{1,0:T(8,128)(2,1)S(1)}, bf16[64,1440]{1,0:T(8,128)(2,1)S(1)}, u32[]{:S(2)}, u32[]{:S(2)}) %collective-permute-start.24) | collective-permute-done | bytes 184352 | tf_op jit(solution)/shard_map/ppermute | solution.py:219
  49.3 0.1 add_convert_fusion.4
  49.4 0.5 collective-permute-start.25
  49.9 0.1 add_convert_fusion.2
  49.9 1.6 %collective-permute-start.28 = (bf16[64,1440]{1,0:T(8,128)(2,1)S(1)}, bf16[64,1440]{1,0:T(8,128)(2,1)S(1)}, u32[]{:S(2)}, u32[]{:S(2)}) collective-permute-start(bf16[64,1440]{1,0:T(8,128)(2,1)S(1)} %add_convert_fusion.2), channel_id=1, source_target_pairs={{4,0},{8,4},{12,8},{14,12},{10,14},{6,10},{2,6},{0,2},{5,1},{9,5},... | collective-permute-start | bytes 552968 | tf_op jit(solution)/shard_map/ppermute | solution.py:220
  51.6 4.2 %collective-permute-done.25 = bf16[64,1440]{1,0:T(8,128)(2,1)S(1)} collective-permute-done((bf16[64,1440]{1,0:T(8,128)(2,1)S(1)}, bf16[64,1440]{1,0:T(8,128)(2,1)S(1)}, u32[]{:S(2)}, u32[]{:S(2)}) %collective-permute-start.25) | collective-permute-done | bytes 184352 | tf_op jit(solution)/shard_map/ppermute | solution.py:219
  55.8 0.1 add_convert_fusion.3
  55.8 0.5 collective-permute-start.26
  56.3 0.1 add_convert_fusion.1
  56.4 1.6 %collective-permute-start.29 = (bf16[64,1440]{1,0:T(8,128)(2,1)S(1)}, bf16[64,1440]{1,0:T(8,128)(2,1)S(1)}, u32[]{:S(2)}, u32[]{:S(2)}) collective-permute-start(bf16[64,1440]{1,0:T(8,128)(2,1)S(1)} %add_convert_fusion.1), channel_id=1, source_target_pairs={{4,0},{8,4},{12,8},{14,12},{10,14},{6,10},{2,6},{0,2},{5,1},{9,5},... | collective-permute-start | bytes 552968 | tf_op jit(solution)/shard_map/ppermute | solution.py:220
  58.1 3.5 %collective-permute-done.26 = bf16[64,1440]{1,0:T(8,128)(2,1)S(1)} collective-permute-done((bf16[64,1440]{1,0:T(8,128)(2,1)S(1)}, bf16[64,1440]{1,0:T(8,128)(2,1)S(1)}, u32[]{:S(2)}, u32[]{:S(2)}) %collective-permute-start.26) | collective-permute-done | bytes 184352 | tf_op jit(solution)/shard_map/ppermute | solution.py:219
  61.6 0.6 collective-permute-done.29
  62.1 0.8 %add_convert_fusion = bf16[64,1440]{1,0:T(8,128)(2,1)} fusion(bf16[64,1440]{1,0:T(8,128)(2,1)S(1)} %collective-permute-done.29, bf16[64,1440]{1,0:T(8,128)(2,1)S(1)} %collective-permute-done.26, bf16[64,1440]{1,0:T(8,128)(2,1)S(1)} %collective-permute-done.21, bf16[64,1440]{1,0:T(8,128)(2,1)S(1)} %get-tuple-element.71), kind=kLoop, calls=%fused_computation | loop fusion | flops 737280 | bytes 921600 | tf_op jit(solution)/shard_map/convert_element_type | solution.py:231
  (15 shorter events, 0.1 us)
Async XLA Ops:
  1.0 8.5 %collective-permute-start.3 = (bf16[64,1464]{1,0:T(8,128)(2,1)S(1)}, bf16[64,1464]{1,0:T(8,128)(2,1)S(1)}, u32[]{:S(2)}, u32[]{:S(2)}) collective-permute-start(bf16[64,1464]{1,0:T(8,128)(2,1)S(1)} %shard_map.64.refs_0_), channel_id=1, source_target_pairs={{4,0},{8,4},{12,8},{14,12},{10,14},{6,10},{2,6},{0,2},{5,1},{9,5},... | collective-permute-start | bytes 562184 | tf_op jit(solution)/shard_map/ppermute | solution.py:193
  4.0 7.5 %collective-permute-start = (bf16[64,1464]{1,0:T(8,128)(2,1)S(1)}, bf16[64,1464]{1,0:T(8,128)(2,1)S(1)}, u32[]{:S(2)}, u32[]{:S(2)}) collective-permute-start(bf16[64,1464]{1,0:T(8,128)(2,1)S(1)} %shard_map.64.refs_0_), channel_id=1, source_target_pairs={{0,4},{4,8},{8,12},{12,14},{14,10},{10,6},{6,2},{2,0},{1,5},{5,9},... | collective-permute-start | bytes 562184 | tf_op jit(solution)/shard_map/ppermute | solution.py:192
  9.5 6.4 %collective-permute-start.6 = (bf16[64,1464]{1,0:T(8,128)(2,1)S(1)}, bf16[64,1464]{1,0:T(8,128)(2,1)S(1)}, u32[]{:S(2)}, u32[]{:S(2)}) collective-permute-start(bf16[64,1464]{1,0:T(8,128)(2,1)S(1)} %collective-permute-done.3.refs_1_), channel_id=1, source_target_pairs={{4,0},{8,4},{12,8},{14,12},{10,14},{6,10},{2,6},{0,2},{5,1},{9,5},... | collective-permute-start | bytes 562184 | tf_op jit(solution)/shard_map/ppermute | solution.py:199
  11.5 6.1 %collective-permute-start.1 = (bf16[64,1464]{1,0:T(8,128)(2,1)S(1)}, bf16[64,1464]{1,0:T(8,128)(2,1)S(1)}, u32[]{:S(2)}, u32[]{:S(2)}) collective-permute-start(bf16[64,1464]{1,0:T(8,128)(2,1)S(1)} %collective-permute-done.refs_0_), channel_id=1, source_target_pairs={{0,4},{4,8},{8,12},{12,14},{14,10},{10,6},{6,2},{2,0},{1,5},{5,9},... | collective-permute-start | bytes 562184 | tf_op jit(solution)/shard_map/ppermute | solution.py:198
  11.6 6.4 %collective-permute-start.4 = (bf16[64,1464]{1,0:T(8,128)(2,1)S(1)}, bf16[64,1464]{1,0:T(8,128)(2,1)S(1)}, u32[]{:S(2)}, u32[]{:S(2)}) collective-permute-start(bf16[64,1464]{1,0:T(8,128)(2,1)S(1)} %collective-permute-done.refs_0_), channel_id=1, source_target_pairs={{0,1},{1,0},{2,3},{3,2},{4,5},{5,4},{6,7},{7,6},{8,9},{9,8},{10,11... | collective-permute-start | bytes 562184 | tf_op jit(solution)/shard_map/ppermute | solution.py:200
  11.6 6.4 %collective-permute-start.5 = (bf16[64,1464]{1,0:T(8,128)(2,1)S(1)}, bf16[64,1464]{1,0:T(8,128)(2,1)S(1)}, u32[]{:S(2)}, u32[]{:S(2)}) collective-permute-start(bf16[64,1464]{1,0:T(8,128)(2,1)S(1)} %collective-permute-done.3.refs_1_), channel_id=1, source_target_pairs={{0,1},{1,0},{2,3},{3,2},{4,5},{5,4},{6,7},{7,6},{8,9},{9,8},{10,11... | collective-permute-start | bytes 562184 | tf_op jit(solution)/shard_map/ppermute | solution.py:200
  15.9 6.7 %collective-permute-start.7 = (bf16[64,1464]{1,0:T(8,128)(2,1)S(1)}, bf16[64,1464]{1,0:T(8,128)(2,1)S(1)}, u32[]{:S(2)}, u32[]{:S(2)}) collective-permute-start(bf16[64,1464]{1,0:T(8,128)(2,1)S(1)} %collective-permute-done.6.refs_1_), channel_id=1, source_target_pairs={{4,0},{8,4},{12,8},{14,12},{10,14},{6,10},{2,6},{0,2},{5,1},{9,5},... | collective-permute-start | bytes 562184 | tf_op jit(solution)/shard_map/ppermute | solution.py:199
  17.5 6.5 %collective-permute-start.2 = (bf16[64,1464]{1,0:T(8,128)(2,1)S(1)}, bf16[64,1464]{1,0:T(8,128)(2,1)S(1)}, u32[]{:S(2)}, u32[]{:S(2)}) collective-permute-start(bf16[64,1464]{1,0:T(8,128)(2,1)S(1)} %collective-permute-done.1.refs_0_), channel_id=1, source_target_pairs={{0,4},{4,8},{8,12},{12,14},{14,10},{10,6},{6,2},{2,0},{1,5},{5,9},... | collective-permute-start | bytes 562184 | tf_op jit(solution)/shard_map/ppermute | solution.py:198
  22.7 4.0 %collective-permute-start.9 = (bf16[64,1464]{1,0:T(8,128)(2,1)S(1)}, bf16[64,1464]{1,0:T(8,128)(2,1)S(1)}, u32[]{:S(2)}, u32[]{:S(2)}) collective-permute-start(bf16[64,1464]{1,0:T(8,128)(2,1)S(1)} %collective-permute-done.7.refs_1_), channel_id=1, source_target_pairs={{0,1},{1,0},{2,3},{3,2},{4,5},{5,4},{6,7},{7,6},{8,9},{9,8},{10,11... | collective-permute-start | bytes 562184 | tf_op jit(solution)/shard_map/ppermute | solution.py:209
  24.1 2.6 %collective-permute-start.8 = (bf16[64,1464]{1,0:T(8,128)(2,1)S(1)}, bf16[64,1464]{1,0:T(8,128)(2,1)S(1)}, u32[]{:S(2)}, u32[]{:S(2)}) collective-permute-start(bf16[64,1464]{1,0:T(8,128)(2,1)S(1)} %collective-permute-done.2.refs_0_), channel_id=1, source_target_pairs={{0,1},{1,0},{2,3},{3,2},{4,5},{5,4},{6,7},{7,6},{8,9},{9,8},{10,11... | collective-permute-start | bytes 562184 | tf_op jit(solution)/shard_map/ppermute | solution.py:209
  24.1 12.4 %collective-permute-start.22 = (bf16[128,1440]{1,0:T(8,128)(2,1)S(1)}, bf16[128,1440]{1,0:T(8,128)(2,1)S(1)}, u32[]{:S(2)}, u32[]{:S(2)}) collective-permute-start(bf16[128,1440]{1,0:T(8,128)(2,1)S(1)} %get-tuple-element.52), channel_id=1, source_target_pairs={{0,1},{1,0},{2,3},{3,2},{4,5},{5,4},{6,7},{7,6},{8,9},{9,8},{10,11... | collective-permute-start | bytes 1105928 | tf_op jit(solution)/shard_map/ppermute | solution.py:183
  24.6 4.8 %collective-permute-start.12 = (bf16[32,1464]{1,0:T(8,128)(2,1)S(1)}, bf16[32,1464]{1,0:T(8,128)(2,1)S(1)}, u32[]{:S(2)}, u32[]{:S(2)}) collective-permute-start(bf16[32,1464]{1,0:T(8,128)(2,1)S(1)} %slice.57), channel_id=1, source_target_pairs={{4,0},{8,4},{12,8},{14,12},{10,14},{6,10},{2,6},{0,2},{5,1},{9,5},... | collective-permute-start | bytes 281096 | tf_op jit(solution)/shard_map/ppermute | solution.py:208
  26.2 4.6 %collective-permute-start.11 = (bf16[32,1464]{1,0:T(8,128)(2,1)S(1)}, bf16[32,1464]{1,0:T(8,128)(2,1)S(1)}, u32[]{:S(2)}, u32[]{:S(2)}) collective-permute-start(bf16[32,1464]{1,0:T(8,128)(2,1)S(1)} %slice.56), channel_id=1, source_target_pairs={{0,4},{4,8},{8,12},{12,14},{14,10},{10,6},{6,2},{2,0},{1,5},{5,9},... | collective-permute-start | bytes 281096 | tf_op jit(solution)/shard_map/ppermute | solution.py:207
  30.8 1.3 %collective-permute-start.13 = (bf16[32,1464]{1,0:T(8,128)(2,1)S(1)}, bf16[32,1464]{1,0:T(8,128)(2,1)S(1)}, u32[]{:S(2)}, u32[]{:S(2)}) collective-permute-start(bf16[32,1464]{1,0:T(8,128)(2,1)S(1)} %collective-permute-done.11.refs_0_), channel_id=1, source_target_pairs={{0,1},{1,0},{2,3},{3,2},{4,5},{5,4},{6,7},{7,6},{8,9},{9,8},{10,11... | collective-permute-start | bytes 281096 | tf_op jit(solution)/shard_map/ppermute | solution.py:212
  30.8 1.5 %collective-permute-start.14 = (bf16[32,1464]{1,0:T(8,128)(2,1)S(1)}, bf16[32,1464]{1,0:T(8,128)(2,1)S(1)}, u32[]{:S(2)}, u32[]{:S(2)}) collective-permute-start(bf16[32,1464]{1,0:T(8,128)(2,1)S(1)} %collective-permute-done.12.refs_1_), channel_id=1, source_target_pairs={{0,1},{1,0},{2,3},{3,2},{4,5},{5,4},{6,7},{7,6},{8,9},{9,8},{10,11... | collective-permute-start | bytes 281096 | tf_op jit(solution)/shard_map/ppermute | solution.py:212
  35.3 1.5 %collective-permute-start.15 = (bf16[64,1440]{1,0:T(8,128)(2,1)S(1)}, bf16[64,1440]{1,0:T(8,128)(2,1)S(1)}, u32[]{:S(2)}, u32[]{:S(2)}) collective-permute-start(bf16[64,1440]{1,0:T(8,128)(2,1)S(1)} %get-tuple-element.63), channel_id=1, source_target_pairs={{0,1},{1,0},{2,3},{3,2},{4,5},{5,4},{6,7},{7,6},{8,9},{9,8},{10,11... | collective-permute-start | bytes 552968 | tf_op jit(solution)/shard_map/ppermute | solution.py:183
  35.8 8.5 %collective-permute-start.20 = (bf16[64,1464]{1,0:T(8,128)(2,1)S(1)}, bf16[64,1464]{1,0:T(8,128)(2,1)S(1)}, u32[]{:S(2)}, u32[]{:S(2)}) collective-permute-start(bf16[64,1464]{1,0:T(8,128)(2,1)S(1)} %shard_map.64.refs_0_), channel_id=1, source_target_pairs={{0,1},{1,0},{2,3},{3,2},{4,5},{5,4},{6,7},{7,6},{8,9},{9,8},{10,11... | collective-permute-start | bytes 562184 | tf_op jit(solution)/shard_map/ppermute | solution.py:194
  35.9 1.6 %collective-permute-start.17 = (bf16[64,1464]{1,0:T(8,128)(2,1)S(1)}, bf16[64,1464]{1,0:T(8,128)(2,1)S(1)}, u32[]{:S(2)}, u32[]{:S(2)}) collective-permute-start(bf16[64,1464]{1,0:T(8,128)(2,1)S(1)} %collective-permute-done.1.refs_0_), channel_id=1, source_target_pairs={{0,1},{1,0},{2,3},{3,2},{4,5},{5,4},{6,7},{7,6},{8,9},{9,8},{10,11... | collective-permute-start | bytes 562184 | tf_op jit(solution)/shard_map/ppermute | solution.py:200
  36.3 2.8 %collective-permute-start.18 = (bf16[64,1464]{1,0:T(8,128)(2,1)S(1)}, bf16[64,1464]{1,0:T(8,128)(2,1)S(1)}, u32[]{:S(2)}, u32[]{:S(2)}) collective-permute-start(bf16[64,1464]{1,0:T(8,128)(2,1)S(1)} %collective-permute-done.6.refs_1_), channel_id=1, source_target_pairs={{0,1},{1,0},{2,3},{3,2},{4,5},{5,4},{6,7},{7,6},{8,9},{9,8},{10,11... | collective-permute-start | bytes 562184 | tf_op jit(solution)/shard_map/ppermute | solution.py:200
  36.4 5.4 %collective-permute-start.10 = (bf16[128,1440]{1,0:T(8,128)(2,1)S(1)}, bf16[128,1440]{1,0:T(8,128)(2,1)S(1)}, u32[]{:S(2)}, u32[]{:S(2)}) collective-permute-start(bf16[128,1440]{1,0:T(8,128)(2,1)S(1)} %get-tuple-element.57), channel_id=1, source_target_pairs={{0,1},{1,0},{2,3},{3,2},{4,5},{5,4},{6,7},{7,6},{8,9},{9,8},{10,11... | collective-permute-start | bytes 1105928 | tf_op jit(solution)/shard_map/ppermute | solution.py:183
  36.9 5.1 %collective-permute-start.16 = (bf16[32,1440]{1,0:T(8,128)(2,1)S(1)}, bf16[32,1440]{1,0:T(8,128)(2,1)S(1)}, u32[]{:S(2)}, u32[]{:S(2)}) collective-permute-start(bf16[32,1440]{1,0:T(8,128)(2,1)S(1)} %get-tuple-element.82), channel_id=1, source_target_pairs={{0,4},{4,8},{8,12},{12,14},{14,10},{10,6},{6,2},{2,0},{1,5},{5,9},... | collective-permute-start | bytes 276488 | tf_op jit(solution)/shard_map/ppermute | solution.py:219
  37.5 5.1 %collective-permute-start.19 = (bf16[32,1440]{1,0:T(8,128)(2,1)S(1)}, bf16[32,1440]{1,0:T(8,128)(2,1)S(1)}, u32[]{:S(2)}, u32[]{:S(2)}) collective-permute-start(bf16[32,1440]{1,0:T(8,128)(2,1)S(1)} %get-tuple-element.81), channel_id=1, source_target_pairs={{4,0},{8,4},{12,8},{14,12},{10,14},{6,10},{2,6},{0,2},{5,1},{9,5},... | collective-permute-start | bytes 276488 | tf_op jit(solution)/shard_map/ppermute | solution.py:220
  41.8 5.6 %collective-permute-start.23 = (bf16[128,1440]{1,0:T(8,128)(2,1)S(1)}, bf16[128,1440]{1,0:T(8,128)(2,1)S(1)}, u32[]{:S(2)}, u32[]{:S(2)}) collective-permute-start(bf16[128,1440]{1,0:T(8,128)(2,1)S(1)} %get-tuple-element.67), channel_id=1, source_target_pairs={{0,1},{1,0},{2,3},{3,2},{4,5},{5,4},{6,7},{7,6},{8,9},{9,8},{10,11... | collective-permute-start | bytes 1105928 | tf_op jit(solution)/shard_map/ppermute | solution.py:183
  42.1 7.2 %collective-permute-start.24 = (bf16[64,1440]{1,0:T(8,128)(2,1)S(1)}, bf16[64,1440]{1,0:T(8,128)(2,1)S(1)}, u32[]{:S(2)}, u32[]{:S(2)}) collective-permute-start(bf16[64,1440]{1,0:T(8,128)(2,1)S(1)} %add_convert_fusion.6), channel_id=1, source_target_pairs={{0,4},{4,8},{8,12},{12,14},{14,10},{10,6},{6,2},{2,0},{1,5},{5,9},... | collective-permute-start | bytes 552968 | tf_op jit(solution)/shard_map/ppermute | solution.py:219
  42.6 7.2 %collective-permute-start.27 = (bf16[64,1440]{1,0:T(8,128)(2,1)S(1)}, bf16[64,1440]{1,0:T(8,128)(2,1)S(1)}, u32[]{:S(2)}, u32[]{:S(2)}) collective-permute-start(bf16[64,1440]{1,0:T(8,128)(2,1)S(1)} %add_convert_fusion.5), channel_id=1, source_target_pairs={{4,0},{8,4},{12,8},{14,12},{10,14},{6,10},{2,6},{0,2},{5,1},{9,5},... | collective-permute-start | bytes 552968 | tf_op jit(solution)/shard_map/ppermute | solution.py:220
  47.3 10.8 %collective-permute-start.21 = (bf16[64,1440]{1,0:T(8,128)(2,1)S(1)}, bf16[64,1440]{1,0:T(8,128)(2,1)S(1)}, u32[]{:S(2)}, u32[]{:S(2)}) collective-permute-start(bf16[64,1440]{1,0:T(8,128)(2,1)S(1)} %get-tuple-element.72), channel_id=1, source_target_pairs={{0,1},{1,0},{2,3},{3,2},{4,5},{5,4},{6,7},{7,6},{8,9},{9,8},{10,11... | collective-permute-start | bytes 552968 | tf_op jit(solution)/shard_map/ppermute | solution.py:183
  49.4 6.4 %collective-permute-start.25 = (bf16[64,1440]{1,0:T(8,128)(2,1)S(1)}, bf16[64,1440]{1,0:T(8,128)(2,1)S(1)}, u32[]{:S(2)}, u32[]{:S(2)}) collective-permute-start(bf16[64,1440]{1,0:T(8,128)(2,1)S(1)} %add_convert_fusion.4), channel_id=1, source_target_pairs={{0,4},{4,8},{8,12},{12,14},{14,10},{10,6},{6,2},{2,0},{1,5},{5,9},... | collective-permute-start | bytes 552968 | tf_op jit(solution)/shard_map/ppermute | solution.py:219
  49.9 6.4 %collective-permute-start.28 = (bf16[64,1440]{1,0:T(8,128)(2,1)S(1)}, bf16[64,1440]{1,0:T(8,128)(2,1)S(1)}, u32[]{:S(2)}, u32[]{:S(2)}) collective-permute-start(bf16[64,1440]{1,0:T(8,128)(2,1)S(1)} %add_convert_fusion.2), channel_id=1, source_target_pairs={{4,0},{8,4},{12,8},{14,12},{10,14},{6,10},{2,6},{0,2},{5,1},{9,5},... | collective-permute-start | bytes 552968 | tf_op jit(solution)/shard_map/ppermute | solution.py:220
  55.8 5.7 %collective-permute-start.26 = (bf16[64,1440]{1,0:T(8,128)(2,1)S(1)}, bf16[64,1440]{1,0:T(8,128)(2,1)S(1)}, u32[]{:S(2)}, u32[]{:S(2)}) collective-permute-start(bf16[64,1440]{1,0:T(8,128)(2,1)S(1)} %add_convert_fusion.3), channel_id=1, source_target_pairs={{0,4},{4,8},{8,12},{12,14},{14,10},{10,6},{6,2},{2,0},{1,5},{5,9},... | collective-permute-start | bytes 552968 | tf_op jit(solution)/shard_map/ppermute | solution.py:219
  56.4 5.7 %collective-permute-start.29 = (bf16[64,1440]{1,0:T(8,128)(2,1)S(1)}, bf16[64,1440]{1,0:T(8,128)(2,1)S(1)}, u32[]{:S(2)}, u32[]{:S(2)}) collective-permute-start(bf16[64,1440]{1,0:T(8,128)(2,1)S(1)} %add_convert_fusion.1), channel_id=1, source_target_pairs={{4,0},{8,4},{12,8},{14,12},{10,14},{6,10},{2,6},{0,2},{5,1},{9,5},... | collective-permute-start | bytes 552968 | tf_op jit(solution)/shard_map/ppermute | solution.py:220

commit v5 on v4

--- a/solution.py
+++ b/solution.py
@@ -60,16 +60,22 @@
     )(*[pltpu.with_memory_space_constraint(a, pltpu.HBM) for a in args])
 
 
+def pieces(hidden):
+    first = -(-hidden // 256) * 128
+    return ((0, first), (first, hidden))
+
+
 def turn_kernel(after_this, gate_in, up_in, gate, up, gate_buf, up_buf, sems):
-    copies = [
-        pltpu.make_async_copy(src, dst, sems.at[i])
-        for i, (src, dst) in enumerate(((gate_in, gate_buf), (up_in, up_buf)))
-    ]
-    for copy in copies:
+    steps = []
+    for i, (src, buf, out) in enumerate(((gate_in, gate_buf, gate), (up_in, up_buf, up))):
+        for j, (start, stop) in enumerate(pieces(src.shape[0])):
+            span = pl.ds(start, stop - start)
+            steps.append((pltpu.make_async_copy(src.at[span], buf.at[span], sems.at[i, j]), buf, out, start, stop))
+    for copy, *_ in steps:
         copy.start()
-    for copy, buf, out in zip(copies, (gate_buf, up_buf), (gate, up)):
+    for copy, buf, out, start, stop in steps:
         copy.wait()
-        out[...] = buf[...].T
+        out[:, start:stop] = buf[start:stop, :].T
 
 
 def turn_weights(after_this, *weights):
@@ -79,28 +85,34 @@
         out_shape=[in_vmem((width, hidden))] * 2,
         in_specs=[pl.BlockSpec(memory_space=pltpu.SMEM)] + [pl.BlockSpec(memory_space=pltpu.HBM)] * 2,
         out_specs=[pl.BlockSpec(memory_space=pltpu.VMEM)] * 2,
-        scratch_shapes=[pltpu.VMEM((hidden, width), jnp.bfloat16)] * 2 + [pltpu.SemaphoreType.DMA((2,))],
+        scratch_shapes=[pltpu.VMEM((hidden, width), jnp.bfloat16)] * 2 + [pltpu.SemaphoreType.DMA((2, 2))],
         compiler_params=pltpu.CompilerParams(vmem_limit_bytes=32 << 20),
         cost_estimate=pl.CostEstimate(flops=0, bytes_accessed=8 * hidden * width, transcendentals=0),
     )(after_this, *[pltpu.with_memory_space_constraint(w, pltpu.HBM) for w in weights])
 
 
-def halve_kernel(place, down_in, down_mine, down_theirs, down_buf, sem):
+def halve_kernel(place, down_in, down_mine, down_theirs, down_buf, sems):
     lane = place[0]
     half = down_mine.shape[1]
-    copy = pltpu.make_async_copy(down_in, down_buf, sem)
-    copy.start()
-    copy.wait()
-
-    @pl.when(lane == 0)
-    def _():
-        down_mine[...] = down_buf[:, :half]
-        down_theirs[...] = down_buf[:, half:]
-
-    @pl.when(lane != 0)
-    def _():
-        down_mine[...] = down_buf[:, half:]
-        down_theirs[...] = down_buf[:, :half]
+    spans = [slice(start, stop) for start, stop in pieces(down_in.shape[0])]
+    copies = [
+        pltpu.make_async_copy(down_in.at[pl.ds(s.start, s.stop - s.start)], down_buf.at[pl.ds(s.start, s.stop - s.start)], sems.at[i])
+        for i, s in enumerate(spans)
+    ]
+    for copy in copies:
+        copy.start()
+    for copy, s in zip(copies, spans):
+        copy.wait()
+
+        @pl.when(lane == 0)
+        def _():
+            down_mine[s, :] = down_buf[s, :half]
+            down_theirs[s, :] = down_buf[s, half:]
+
+        @pl.when(lane != 0)
+        def _():
+            down_mine[s, :] = down_buf[s, half:]
+            down_theirs[s, :] = down_buf[s, :half]
 
 
 def halve_weights(place, w_down):
@@ -110,7 +122,7 @@
         out_shape=[in_vmem((hidden, width // 2))] * 2,
         in_specs=[pl.BlockSpec(memory_space=pltpu.SMEM), pl.BlockSpec(memory_space=pltpu.HBM)],
         out_specs=[pl.BlockSpec(memory_space=pltpu.VMEM)] * 2,
-        scratch_shapes=[pltpu.VMEM((hidden, width), jnp.bfloat16), pltpu.SemaphoreType.DMA],
+        scratch_shapes=[pltpu.VMEM((hidden, width), jnp.bfloat16), pltpu.SemaphoreType.DMA((2,))],
         compiler_params=pltpu.CompilerParams(vmem_limit_bytes=32 << 20),
         cost_estimate=pl.CostEstimate(flops=0, bytes_accessed=8 * hidden * width, transcendentals=0),
     )(place, pltpu.with_memory_space_constraint(w_down, pltpu.HBM))
@@ -169,9 +181,17 @@
     order = list(range(0, n, 2)) + list(range(n - 1, 0, -2))
     ahead = [(order[i], order[(i + 1) % n]) for i in range(n)]
     back = [(b, a) for a, b in ahead]
+    levels = n // 2
+    middle = (levels // 2 - 1, levels // 2)
+    opposite = [(i, i ^ 1 if i // 2 in middle else n - 1 - i) for i in range(n)]
     swap = functools.partial(lax.ppermute, axis_name="tp", perm=[(0, 1), (1, 0)])
     far = n // 2
-    place = jnp.stack([lax.axis_index("tp"), lax.axis_index("ep")]).astype(jnp.int32)
+    me = lax.axis_index("ep")
+    level, side = me // 2, me % 2
+    relays = (level == middle[0]) | (level == middle[1])
+    relays_ahead = relays & ((level == middle[0]) == (side == 0))
+    relays_back = relays & ~relays_ahead
+    place = jnp.stack([lax.axis_index("tp"), me]).astype(jnp.int32)
     packed = pack(tokens, expert_ids, gate_probs, n)
     gate, up = turn_weights(after(place, packed), w_gate[0].T, w_up[0].T)
 
@@ -199,36 +219,33 @@
         came[-k] = lax.ppermute(came[1 - k], "ep", back)
         across[k - 1], across[1 - k] = swap(came[k - 1]), swap(came[1 - k])
         if k == 2:
+            passed = jnp.where(relays_ahead, came[-1], jnp.where(relays_back, came[1], packed))
+            came[far] = lax.ppermute(passed, "ep", opposite)
             weights += halve_weights(after(place, came[1]), w_down[0])
             done = weights[-1]
         else:
-            done = run([k - 2, 2 - k])
+            done = run([k - 1, 1 - k])
     came[far - 1], came[1 - far] = after(came[far - 1], done), after(came[1 - far], done)
-    came["low"] = lax.ppermute(came[far - 1][: rows // 2], "ep", ahead)
-    came["high"] = lax.ppermute(came[1 - far][rows // 2 :], "ep", back)
     across[far - 1], across[1 - far] = swap(came[far - 1]), swap(came[1 - far])
-    done = run([far - 1, 1 - far])
-    came["low"], came["high"] = after((came["low"], came["high"]), done)
-    across["low"], across["high"] = swap(came["low"]), swap(came["high"])
-    run(["low", "high"])
-
-    to_ahead = value["low"].astype(jnp.bfloat16)
-    to_back = value["high"].astype(jnp.bfloat16)
-    pad_low, pad_high = ((0, rows - rows // 2), (0, 0)), ((rows // 2, 0), (0, 0))
-    for k in range(far - 1, -1, -1):
+    across[far] = swap(came[far])
+    run([far - 1, 1 - far, far])
+    returned = lax.ppermute(value[far].astype(jnp.bfloat16), "ep", opposite)
+
+    to_ahead, to_back = value[1 - far].astype(jnp.bfloat16), value[far - 1].astype(jnp.bfloat16)
+    for k in range(far - 1, 0, -1):
         behind = lax.ppermute(to_ahead, "ep", ahead)
         front = lax.ppermute(to_back, "ep", back)
         if k >= far - 2:
-            done = run([far - 2, 2 - far] if k == far - 1 else [0], (to_ahead, to_back))
-        behind, front = behind.astype(jnp.float32), front.astype(jnp.float32)
-        if k == far - 1:
-            behind, front = jnp.pad(behind, pad_low), jnp.pad(front, pad_high)
-        if k:
-            to_ahead = (value[-k] + behind).astype(jnp.bfloat16)
-            to_back = (value[k] + front).astype(jnp.bfloat16)
-        if k >= far - 2:
-            to_ahead, to_back = after(to_ahead, done), after(to_back, done)
-    return (value[0] + behind + front).astype(jnp.bfloat16)
+            done = run([1, -1] if k == far - 1 else [0], (to_ahead, to_back))
+        if k > 1:
+            to_ahead, to_back = value[1 - k] + behind.astype(jnp.float32), value[k - 1] + front.astype(jnp.float32)
+            if k == 2:
+                for_back = lax.optimization_barrier(returned).astype(jnp.float32)
+                to_ahead += jnp.where(relays_ahead, returned.astype(jnp.float32), 0.0)
+                to_back += jnp.where(relays_back, for_back, 0.0)
+            to_ahead, to_back = after(to_ahead.astype(jnp.bfloat16), done), after(to_back.astype(jnp.bfloat16), done)
+    total = value[0] + behind.astype(jnp.float32) + front.astype(jnp.float32)
+    return (total + jnp.where(relays, 0.0, returned.astype(jnp.float32))).astype(jnp.bfloat16)
 
 
 def swiglu_expert(rows, gate_part, up_part, down_part):
@@ -304,7 +321,7 @@
 
     def body(tokens, expert_ids, *rest):
         n, top = lax.axis_size("ep"), expert_ids.shape[1]
-        small = n <= 4 * top and n % 2 == 0 and n >= 6 and lax.axis_size("tp") == 2
+        small = n <= 4 * top and n % 4 == 0 and n >= 8 and lax.axis_size("tp") == 2
         return (ring_body if small else slot_body)(tokens, expert_ids, *rest)
 
     return jax.shard_map(body, mesh=mesh, in_specs=in_specs, out_specs=out_specs, check_vma=False)

time: 63.1 us -> 64.6 us (1.024)
  starting transfers between devices: 20.9 us -> 28.2 us
  waiting for transfers between devices: 16.6 us -> 13.7 us
  Pallas kernels: 23.9 us -> 21 us
    ppermute x4 -> x3, waiting for transfers between devices: 9.73 us -> 1.37 us  [ring_body(): behind = lax.ppermute(to_ahead, 'ep', ahead)]
    ppermute x4 -> x3, waiting for transfers between devices: 0.58 us -> 7.06 us  [ring_body(): front = lax.ppermute(to_back, 'ep', back)]
    ppermute x4 -> x3, starting transfers between devices: 2.59 us -> 8.07 us  [the longest x1 5.04 us: ring_body(): came[far] = lax.ppermute(passed, 'ep', opposite)]
    ppermute x4 -> x3, starting transfers between devices: 2.02 us -> 5.76 us  [ring_body(): behind = lax.ppermute(to_ahead, 'ep', ahead)]
    ppermute x1, starting transfers between devices: 2.99 us -> 0.01 us  [ring_body(): came[-1] = lax.ppermute(packed, 'ep', back)]
    ppermute x1, starting transfers between devices: 0.15 us -> 3.08 us  [ring_body(): came[1] = lax.ppermute(packed, 'ep', ahead)]
    pallas_call x5 -> x4, Pallas kernels: 14.1 us -> 12 us  [run_expert(): pl.pallas_call(functools.partial(expert_kernel, len(own), n_experts), out...]
    ppermute x2, waiting for transfers between devices: 2.35 us -> 0.42 us  [ring_body(): came[-k] = lax.ppermute(came[1 - k], 'ep', back)]
  transfers between devices with their start and end apart: 30 -> 26, of which waited for: 13 -> 9; matrix products, arithmetic and copies ran while one was open for 1% -> 1% of each run, Pallas kernels for 36% -> 25%
where the time goes in v5:
time: 64.6 us; the launch traced here: 64.5 us
  starting transfers between devices  28.2 us (44%)
  Pallas kernels  21 us (33%)
  waiting for transfers between devices  13.7 us (21%)
  other arithmetic  1.44 us (2%)
    pallas_call x4, Pallas kernels, run_expert(): pl.pallas_call(functools.partial(expert_kernel, len(own), n_experts), out...  12 us
    ppermute x3, waiting for transfers between devices, ring_body(): front = lax.ppermute(to_back, 'ep', back)  7.06 us
    ppermute x3, starting transfers between devices, ring_body(): behind = lax.ppermute(to_ahead, 'ep', ahead)  5.76 us
    ppermute x1, starting transfers between devices, ring_body(): came[far] = lax.ppermute(passed, 'ep', opposite)  5.04 us
    pallas_call x1, Pallas kernels, turn_weights(): pl.pallas_call(turn_kernel, out_shape=[in_vmem((width, hidden))] * 2, in_...  4.79 us
    ppermute x3, starting transfers between devices, ring_body(): front = lax.ppermute(to_back, 'ep', back)  4.62 us
    pallas_call x1, Pallas kernels, halve_weights(): pl.pallas_call(halve_kernel, out_shape=[in_vmem((hidden, width // 2))] *...  3.13 us
    ppermute x1, starting transfers between devices, ring_body(): came[1] = lax.ppermute(packed, 'ep', ahead)  3.08 us
  transfers between devices with their start and end apart: 26, of which 9 were waited for; matrix products, arithmetic and copies ran while one was open for 1% of the time, Pallas kernels for 25%

profile of v5, /device:TPU:0, one launch (start us, length us, event | category | flops | bytes accessed | tf_op | source)
XLA Modules:
  0.0 64.5 jit_solution(3337258120040390138)
XLA Ops:
  0.0 1.0 %shard_map.64.refs_0_ = bf16[64,1464]{1,0:T(8,128)(2,1)S(1)} custom-call(bf16[64,1440]{1,0:T(8,128)(2,1)} %tokens_in.1, s32[4,64]{1,0:T(4,128)} %bitcast.14, f32[4,64]{1,0:T(4,128)} %bitcast.15), custom_call_target="tpu_custom_call" | custom-call | tf_op jit(solution)/shard_map/pallas_call | solution.py:53
  1.0 3.1 %collective-permute-start = (bf16[64,1464]{1,0:T(8,128)(2,1)S(1)}, bf16[64,1464]{1,0:T(8,128)(2,1)S(1)}, u32[]{:S(2)}, u32[]{:S(2)}) collective-permute-start(bf16[64,1464]{1,0:T(8,128)(2,1)S(1)} %shard_map.64.refs_0_), channel_id=1, source_target_pairs={{0,4},{4,8},{8,12},{12,14},{14,10},{10,6},{6,2},{2,0},{1,5},{5,9},... | collective-permute-start | bytes 562184 | tf_op jit(solution)/shard_map/ppermute | solution.py:212
  4.1 0.0 collective-permute-start.2
  4.1 0.1 pad_add_fusion.after_this.place
  4.2 4.8 %shard_map.65 = (bf16[2880,720]{1,0:T(8,128)(2,1)S(1)}, bf16[2880,720]{1,0:T(8,128)(2,1)S(1)}) custom-call(s32[2]{0:T(128)S(1)} %pad_add_fusion.after_this.place, bf16[720,2880]{1,0:T(8,128)(2,1)} %bitcast.11, bf16[720,2880]{1,0:T(8,128)(2,1)} %bitcast.12), custom_call_target="tpu_custom_call" | custom-call | bytes 16588800 | tf_op jit(solution)/shard_map/pallas_call | solution.py:83
  9.0 0.0 collective-permute-done.refs_0_
  9.0 2.1 %collective-permute-start.1 = (bf16[64,1464]{1,0:T(8,128)(2,1)S(1)}, bf16[64,1464]{1,0:T(8,128)(2,1)S(1)}, u32[]{:S(2)}, u32[]{:S(2)}) collective-permute-start(bf16[64,1464]{1,0:T(8,128)(2,1)S(1)} %collective-permute-done.refs_0_), channel_id=1, source_target_pairs={{0,4},{4,8},{8,12},{12,14},{14,10},{10,6},{6,2},{2,0},{1,5},{5,9},... | collective-permute-start | bytes 562184 | tf_op jit(solution)/shard_map/ppermute | solution.py:218
  11.0 0.0 collective-permute-done.2.refs_1_
  11.1 0.0 collective-permute-start.3
  11.1 5.0 %collective-permute-start.9 = (bf16[64,1464]{1,0:T(8,128)(2,1)S(1)}, bf16[64,1464]{1,0:T(8,128)(2,1)S(1)}, u32[]{:S(2)}, u32[]{:S(2)}) collective-permute-start(bf16[64,1464]{1,0:T(8,128)(2,1)S(1)} %select_select_fusion), channel_id=1, source_target_pairs={{0,14},{2,12},{4,6},{6,4},{8,10},{10,8},{12,2},{14,0},{1,15},{3,13... | collective-permute-start | bytes 562184 | tf_op jit(solution)/shard_map/ppermute | solution.py:223
  16.1 3.1 %shard_map.66 = (bf16[720,1440]{1,0:T(8,128)(2,1)S(1)}, bf16[720,1440]{1,0:T(8,128)(2,1)S(1)}) custom-call(s32[2]{0:T(128)S(1)} %pad_add_fusion.after_this.place, bf16[720,2880]{1,0:T(8,128)(2,1)} %bitcast.13), custom_call_target="tpu_custom_call" | custom-call | bytes 16588800 | tf_op jit(solution)/shard_map/pallas_call | solution.py:120
  19.3 0.0 collective-permute-done.1.refs_0_
  19.3 0.0 collective-permute-done.3.refs_1_
  19.3 0.1 collective-permute-start.4
  19.4 0.5 collective-permute-start.5
  19.9 0.1 collective-permute-start.7
  20.0 1.9 %collective-permute-start.8 = (bf16[64,1464]{1,0:T(8,128)(2,1)S(1)}, bf16[64,1464]{1,0:T(8,128)(2,1)S(1)}, u32[]{:S(2)}, u32[]{:S(2)}) collective-permute-start(bf16[64,1464]{1,0:T(8,128)(2,1)S(1)} %collective-permute-done.3.refs_1_), channel_id=1, source_target_pairs={{4,0},{8,4},{12,8},{14,12},{10,14},{6,10},{2,6},{0,2},{5,1},{9,5},... | collective-permute-start | bytes 562184 | tf_op jit(solution)/shard_map/ppermute | solution.py:219
  21.9 0.8 %collective-permute-done.9.refs_2_ = bf16[64,1464]{1,0:T(8,128)(2,1)S(1)} collective-permute-done((bf16[64,1464]{1,0:T(8,128)(2,1)S(1)}, bf16[64,1464]{1,0:T(8,128)(2,1)S(1)}, u32[]{:S(2)}, u32[]{:S(2)}) %collective-permute-start.9) | collective-permute-done | bytes 187424 | tf_op jit(solution)/shard_map/ppermute | solution.py:223
  22.7 0.0 collective-permute-start.12
  22.7 0.0 collective-permute-done.4.refs_2_
  22.7 0.0 collective-permute-done.5.refs_3_
  22.8 2.7 %shard_map.67 = (bf16[128,1440]{1,0:T(8,128)(2,1)S(1)}, bf16[128,1440]{1,0:T(8,128)(2,1)S(1)}) custom-call(s32[2]{0:T(128)S(1)} %pad_add_fusion.after_this.place, bf16[64,1464]{1,0:T(8,128)(2,1)S(1)} %collective-permute-done.1.refs_0_, bf16[64,1464]{1,0:T(8,128)(2,1)S(1)} %collective-permute-done.3.refs_1_, ...), custom_call_target="tpu_custom_call" | custom-call | flops 1592524800 | bytes 12441600 | tf_op jit(solution)/shard_map/pallas_call | solution.py:167
  25.5 1.5 %collective-permute-done.7.refs_0_ = bf16[64,1464]{1,0:T(8,128)(2,1)S(1)} collective-permute-done((bf16[64,1464]{1,0:T(8,128)(2,1)S(1)}, bf16[64,1464]{1,0:T(8,128)(2,1)S(1)}, u32[]{:S(2)}, u32[]{:S(2)}) %collective-permute-start.7) | collective-permute-done | bytes 187424 | tf_op jit(solution)/shard_map/ppermute | solution.py:218
  26.9 0.4 collective-permute-done.8.refs_1_
  27.3 0.0 collective-permute-start.10
  27.3 0.5 collective-permute-start.11
  27.9 0.0 collective-permute-done.12.refs_5_
  27.9 0.9 %collective-permute-done.10.refs_3_ = bf16[64,1464]{1,0:T(8,128)(2,1)S(1)} collective-permute-done((bf16[64,1464]{1,0:T(8,128)(2,1)S(1)}, bf16[64,1464]{1,0:T(8,128)(2,1)S(1)}, u32[]{:S(2)}, u32[]{:S(2)}) %collective-permute-start.10) | collective-permute-done | bytes 187424 | tf_op jit(solution)/shard_map/ppermute | solution.py:229
  28.8 0.3 collective-permute-done.11.refs_4_
  29.1 3.6 %shard_map.68 = (bf16[192,1440]{1,0:T(8,128)(2,1)S(1)}, bf16[192,1440]{1,0:T(8,128)(2,1)S(1)}) custom-call(s32[2]{0:T(128)S(1)} %pad_add_fusion.after_this.place, bf16[64,1464]{1,0:T(8,128)(2,1)S(1)} %collective-permute-done.7.refs_0_, bf16[64,1464]{1,0:T(8,128)(2,1)S(1)} %collective-permute-done.8.refs_1_, ...), custom_call_target="tpu_custom_call" | custom-call | flops 2388787200 | bytes 12441600 | tf_op jit(solution)/shard_map/pallas_call | solution.py:167
  32.7 0.3 collective-permute-start.13
  33.0 0.3 collective-permute-start.6
  33.3 0.2 collective-permute-start.18
  33.5 0.3 collective-permute-start.15
  33.8 0.2 collective-permute-start.16
  34.0 1.3 %collective-permute-done.6 = bf16[128,1440]{1,0:T(8,128)(2,1)S(1)} collective-permute-done((bf16[128,1440]{1,0:T(8,128)(2,1)S(1)}, bf16[128,1440]{1,0:T(8,128)(2,1)S(1)}, u32[]{:S(2)}, u32[]{:S(2)}) %collective-permute-start.6) | collective-permute-done | bytes 368672 | tf_op jit(solution)/shard_map/ppermute | solution.py:203
  35.3 0.0 collective-permute-done.13
  35.4 1.5 %collective-permute-start.17 = (bf16[64,1440]{1,0:T(8,128)(2,1)S(1)}, bf16[64,1440]{1,0:T(8,128)(2,1)S(1)}, u32[]{:S(2)}, u32[]{:S(2)}) collective-permute-start(bf16[64,1440]{1,0:T(8,128)(2,1)S(1)} %add_convert_fusion.3), channel_id=1, source_target_pairs={{4,0},{8,4},{12,8},{14,12},{10,14},{6,10},{2,6},{0,2},{5,1},{9,5},... | collective-permute-start | bytes 552968 | tf_op jit(solution)/shard_map/ppermute | solution.py:237
  36.9 2.5 %collective-permute-start.14 = (bf16[64,1440]{1,0:T(8,128)(2,1)S(1)}, bf16[64,1440]{1,0:T(8,128)(2,1)S(1)}, u32[]{:S(2)}, u32[]{:S(2)}) collective-permute-start(bf16[64,1440]{1,0:T(8,128)(2,1)S(1)} %add_convert_fusion.5), channel_id=1, source_target_pairs={{0,4},{4,8},{8,12},{12,14},{14,10},{10,6},{6,2},{2,0},{1,5},{5,9},... | collective-permute-start | bytes 552968 | tf_op jit(solution)/shard_map/ppermute | solution.py:236
  39.4 0.0 collective-permute-done.15.refs_2_
  39.4 3.0 %collective-permute-start.22 = (bf16[64,1440]{1,0:T(8,128)(2,1)S(1)}, bf16[64,1440]{1,0:T(8,128)(2,1)S(1)}, u32[]{:S(2)}, u32[]{:S(2)}) collective-permute-start(bf16[64,1440]{1,0:T(8,128)(2,1)S(1)} %add_convert_fusion.1), channel_id=1, source_target_pairs={{0,14},{2,12},{4,6},{6,4},{8,10},{10,8},{12,2},{14,0},{1,15},{3,13... | collective-permute-start | bytes 552968 | tf_op jit(solution)/shard_map/ppermute | solution.py:232
  42.5 0.0 collective-permute-done.16.refs_3_
  42.5 2.7 %shard_map.69 = (bf16[128,1440]{1,0:T(8,128)(2,1)S(1)}, bf16[128,1440]{1,0:T(8,128)(2,1)S(1)}) custom-call(s32[2]{0:T(128)S(1)} %pad_add_fusion.after_this.place, bf16[64,1464]{1,0:T(8,128)(2,1)S(1)} %collective-permute-done.refs_0_, bf16[64,1464]{1,0:T(8,128)(2,1)S(1)} %collective-permute-done.2.refs_1_, ...), custom_call_target="tpu_custom_call" | custom-call | flops 1592524800 | bytes 12441600 | tf_op jit(solution)/shard_map/pallas_call | solution.py:167
  45.2 0.1 collective-permute-start.20
  45.3 0.0 collective-permute-done.17
  45.3 0.1 add_convert_fusion.2
  45.4 1.6 %collective-permute-start.24 = (bf16[64,1440]{1,0:T(8,128)(2,1)S(1)}, bf16[64,1440]{1,0:T(8,128)(2,1)S(1)}, u32[]{:S(2)}, u32[]{:S(2)}) collective-permute-start(bf16[64,1440]{1,0:T(8,128)(2,1)S(1)} %add_convert_fusion.2), channel_id=1, source_target_pairs={{4,0},{8,4},{12,8},{14,12},{10,14},{6,10},{2,6},{0,2},{5,1},{9,5},... | collective-permute-start | bytes 552968 | tf_op jit(solution)/shard_map/ppermute | solution.py:237
  47.0 0.0 collective-permute-done.14
  47.0 0.1 add_convert_fusion.4
  47.1 2.7 %collective-permute-start.21 = (bf16[64,1440]{1,0:T(8,128)(2,1)S(1)}, bf16[64,1440]{1,0:T(8,128)(2,1)S(1)}, u32[]{:S(2)}, u32[]{:S(2)}) collective-permute-start(bf16[64,1440]{1,0:T(8,128)(2,1)S(1)} %add_convert_fusion.4), channel_id=1, source_target_pairs={{0,4},{4,8},{8,12},{12,14},{14,10},{10,6},{6,2},{2,0},{1,5},{5,9},... | collective-permute-start | bytes 552968 | tf_op jit(solution)/shard_map/ppermute | solution.py:236
  49.7 0.0 collective-permute-done.18.refs_1_
  49.7 3.0 %shard_map.70 = (bf16[64,1440]{1,0:T(8,128)(2,1)S(1)}, bf16[64,1440]{1,0:T(8,128)(2,1)S(1)}) custom-call(s32[2]{0:T(128)S(1)} %pad_add_fusion.after_this.place, bf16[64,1464]{1,0:T(8,128)(2,1)S(1)} %shard_map.64.refs_0_, bf16[64,1464]{1,0:T(8,128)(2,1)S(1)} %collective-permute-done.18.refs_1_, ...), custom_call_target="tpu_custom_call" | custom-call | flops 796262400 | bytes 12441600 | tf_op jit(solution)/shard_map/pallas_call | solution.py:167
  52.8 0.1 collective-permute-start.19
  52.8 0.0 collective-permute-done.22
  52.9 2.4 %collective-permute-done.24 = bf16[64,1440]{1,0:T(8,128)(2,1)S(1)} collective-permute-done((bf16[64,1440]{1,0:T(8,128)(2,1)S(1)}, bf16[64,1440]{1,0:T(8,128)(2,1)S(1)}, u32[]{:S(2)}, u32[]{:S(2)}) %collective-permute-start.24) | collective-permute-done | bytes 184352 | tf_op jit(solution)/shard_map/ppermute | solution.py:237
  55.2 0.1 add_convert_fusion
  55.4 1.5 %collective-permute-start.25 = (bf16[64,1440]{1,0:T(8,128)(2,1)S(1)}, bf16[64,1440]{1,0:T(8,128)(2,1)S(1)}, u32[]{:S(2)}, u32[]{:S(2)}) collective-permute-start(bf16[64,1440]{1,0:T(8,128)(2,1)S(1)} %add_convert_fusion), channel_id=1, source_target_pairs={{4,0},{8,4},{12,8},{14,12},{10,14},{6,10},{2,6},{0,2},{5,1},{9,5},... | collective-permute-start | bytes 552968 | tf_op jit(solution)/shard_map/ppermute | solution.py:237
  56.9 0.0 collective-permute-done.21
  56.9 0.1 fusion.1
  57.0 0.6 collective-permute-start.23
  57.6 0.0 collective-permute-done.19
  57.6 4.7 %collective-permute-done.25 = bf16[64,1440]{1,0:T(8,128)(2,1)S(1)} collective-permute-done((bf16[64,1440]{1,0:T(8,128)(2,1)S(1)}, bf16[64,1440]{1,0:T(8,128)(2,1)S(1)}, u32[]{:S(2)}, u32[]{:S(2)}) %collective-permute-start.25) | collective-permute-done | bytes 184352 | tf_op jit(solution)/shard_map/ppermute | solution.py:237
  62.3 1.4 %collective-permute-done.23 = bf16[64,1440]{1,0:T(8,128)(2,1)S(1)} collective-permute-done((bf16[64,1440]{1,0:T(8,128)(2,1)S(1)}, bf16[64,1440]{1,0:T(8,128)(2,1)S(1)}, u32[]{:S(2)}, u32[]{:S(2)}) %collective-permute-start.23) | collective-permute-done | bytes 184352 | tf_op jit(solution)/shard_map/ppermute | solution.py:236
  63.6 0.8 %fusion.3 = bf16[64,1440]{1,0:T(8,128)(2,1)} fusion(bf16[64,1440]{1,0:T(8,128)(2,1)S(1)} %collective-permute-done.22, bf16[64,1440]{1,0:T(8,128)(2,1)S(1)} %collective-permute-done.25, bf16[64,1440]{1,0:T(8,128)(2,1)S(1)} %collective-permute-done.23, bf16[64,1440]{1,0:T(8,128)(2,1)S(1)} %collective-permute-done.19, ...), kind=kLoop, calls=%fused_computation.5 | loop fusion | flops 1013760 | bytes 1105921 | tf_op jit(solution)/shard_map/convert_element_type | solution.py:248
  (5 shorter events, 0.2 us)
Async XLA Ops:
  1.0 8.0 %collective-permute-start = (bf16[64,1464]{1,0:T(8,128)(2,1)S(1)}, bf16[64,1464]{1,0:T(8,128)(2,1)S(1)}, u32[]{:S(2)}, u32[]{:S(2)}) collective-permute-start(bf16[64,1464]{1,0:T(8,128)(2,1)S(1)} %shard_map.64.refs_0_), channel_id=1, source_target_pairs={{0,4},{4,8},{8,12},{12,14},{14,10},{10,6},{6,2},{2,0},{1,5},{5,9},... | collective-permute-start | bytes 562184 | tf_op jit(solution)/shard_map/ppermute | solution.py:212
  4.1 7.0 %collective-permute-start.2 = (bf16[64,1464]{1,0:T(8,128)(2,1)S(1)}, bf16[64,1464]{1,0:T(8,128)(2,1)S(1)}, u32[]{:S(2)}, u32[]{:S(2)}) collective-permute-start(bf16[64,1464]{1,0:T(8,128)(2,1)S(1)} %shard_map.64.refs_0_), channel_id=1, source_target_pairs={{4,0},{8,4},{12,8},{14,12},{10,14},{6,10},{2,6},{0,2},{5,1},{9,5},... | collective-permute-start | bytes 562184 | tf_op jit(solution)/shard_map/ppermute | solution.py:213
  9.0 10.3 %collective-permute-start.1 = (bf16[64,1464]{1,0:T(8,128)(2,1)S(1)}, bf16[64,1464]{1,0:T(8,128)(2,1)S(1)}, u32[]{:S(2)}, u32[]{:S(2)}) collective-permute-start(bf16[64,1464]{1,0:T(8,128)(2,1)S(1)} %collective-permute-done.refs_0_), channel_id=1, source_target_pairs={{0,4},{4,8},{8,12},{12,14},{14,10},{10,6},{6,2},{2,0},{1,5},{5,9},... | collective-permute-start | bytes 562184 | tf_op jit(solution)/shard_map/ppermute | solution.py:218
  11.1 8.2 %collective-permute-start.3 = (bf16[64,1464]{1,0:T(8,128)(2,1)S(1)}, bf16[64,1464]{1,0:T(8,128)(2,1)S(1)}, u32[]{:S(2)}, u32[]{:S(2)}) collective-permute-start(bf16[64,1464]{1,0:T(8,128)(2,1)S(1)} %collective-permute-done.2.refs_1_), channel_id=1, source_target_pairs={{4,0},{8,4},{12,8},{14,12},{10,14},{6,10},{2,6},{0,2},{5,1},{9,5},... | collective-permute-start | bytes 562184 | tf_op jit(solution)/shard_map/ppermute | solution.py:219
  11.1 11.7 %collective-permute-start.9 = (bf16[64,1464]{1,0:T(8,128)(2,1)S(1)}, bf16[64,1464]{1,0:T(8,128)(2,1)S(1)}, u32[]{:S(2)}, u32[]{:S(2)}) collective-permute-start(bf16[64,1464]{1,0:T(8,128)(2,1)S(1)} %select_select_fusion), channel_id=1, source_target_pairs={{0,14},{2,12},{4,6},{6,4},{8,10},{10,8},{12,2},{14,0},{1,15},{3,13... | collective-permute-start | bytes 562184 | tf_op jit(solution)/shard_map/ppermute | solution.py:223
  19.3 3.5 %collective-permute-start.4 = (bf16[64,1464]{1,0:T(8,128)(2,1)S(1)}, bf16[64,1464]{1,0:T(8,128)(2,1)S(1)}, u32[]{:S(2)}, u32[]{:S(2)}) collective-permute-start(bf16[64,1464]{1,0:T(8,128)(2,1)S(1)} %collective-permute-done.1.refs_0_), channel_id=1, source_target_pairs={{0,1},{1,0},{2,3},{3,2},{4,5},{5,4},{6,7},{7,6},{8,9},{9,8},{10,11... | collective-permute-start | bytes 562184 | tf_op jit(solution)/shard_map/ppermute | solution.py:220
  19.4 3.4 %collective-permute-start.5 = (bf16[64,1464]{1,0:T(8,128)(2,1)S(1)}, bf16[64,1464]{1,0:T(8,128)(2,1)S(1)}, u32[]{:S(2)}, u32[]{:S(2)}) collective-permute-start(bf16[64,1464]{1,0:T(8,128)(2,1)S(1)} %collective-permute-done.3.refs_1_), channel_id=1, source_target_pairs={{0,1},{1,0},{2,3},{3,2},{4,5},{5,4},{6,7},{7,6},{8,9},{9,8},{10,11... | collective-permute-start | bytes 562184 | tf_op jit(solution)/shard_map/ppermute | solution.py:220
  19.9 7.1 %collective-permute-start.7 = (bf16[64,1464]{1,0:T(8,128)(2,1)S(1)}, bf16[64,1464]{1,0:T(8,128)(2,1)S(1)}, u32[]{:S(2)}, u32[]{:S(2)}) collective-permute-start(bf16[64,1464]{1,0:T(8,128)(2,1)S(1)} %collective-permute-done.1.refs_0_), channel_id=1, source_target_pairs={{0,4},{4,8},{8,12},{12,14},{14,10},{10,6},{6,2},{2,0},{1,5},{5,9},... | collective-permute-start | bytes 562184 | tf_op jit(solution)/shard_map/ppermute | solution.py:218
  20.0 7.4 %collective-permute-start.8 = (bf16[64,1464]{1,0:T(8,128)(2,1)S(1)}, bf16[64,1464]{1,0:T(8,128)(2,1)S(1)}, u32[]{:S(2)}, u32[]{:S(2)}) collective-permute-start(bf16[64,1464]{1,0:T(8,128)(2,1)S(1)} %collective-permute-done.3.refs_1_), channel_id=1, source_target_pairs={{4,0},{8,4},{12,8},{14,12},{10,14},{6,10},{2,6},{0,2},{5,1},{9,5},... | collective-permute-start | bytes 562184 | tf_op jit(solution)/shard_map/ppermute | solution.py:219
  22.7 5.1 %collective-permute-start.12 = (bf16[64,1464]{1,0:T(8,128)(2,1)S(1)}, bf16[64,1464]{1,0:T(8,128)(2,1)S(1)}, u32[]{:S(2)}, u32[]{:S(2)}) collective-permute-start(bf16[64,1464]{1,0:T(8,128)(2,1)S(1)} %collective-permute-done.9.refs_2_), channel_id=1, source_target_pairs={{0,1},{1,0},{2,3},{3,2},{4,5},{5,4},{6,7},{7,6},{8,9},{9,8},{10,11... | collective-permute-start | bytes 562184 | tf_op jit(solution)/shard_map/ppermute | solution.py:230
  27.3 1.4 %collective-permute-start.10 = (bf16[64,1464]{1,0:T(8,128)(2,1)S(1)}, bf16[64,1464]{1,0:T(8,128)(2,1)S(1)}, u32[]{:S(2)}, u32[]{:S(2)}) collective-permute-start(bf16[64,1464]{1,0:T(8,128)(2,1)S(1)} %collective-permute-done.7.refs_0_), channel_id=1, source_target_pairs={{0,1},{1,0},{2,3},{3,2},{4,5},{5,4},{6,7},{7,6},{8,9},{9,8},{10,11... | collective-permute-start | bytes 562184 | tf_op jit(solution)/shard_map/ppermute | solution.py:229
  27.3 1.7 %collective-permute-start.11 = (bf16[64,1464]{1,0:T(8,128)(2,1)S(1)}, bf16[64,1464]{1,0:T(8,128)(2,1)S(1)}, u32[]{:S(2)}, u32[]{:S(2)}) collective-permute-start(bf16[64,1464]{1,0:T(8,128)(2,1)S(1)} %collective-permute-done.8.refs_1_), channel_id=1, source_target_pairs={{0,1},{1,0},{2,3},{3,2},{4,5},{5,4},{6,7},{7,6},{8,9},{9,8},{10,11... | collective-permute-start | bytes 562184 | tf_op jit(solution)/shard_map/ppermute | solution.py:229
  32.7 2.6 %collective-permute-start.13 = (bf16[192,1440]{1,0:T(8,128)(2,1)S(1)}, bf16[192,1440]{1,0:T(8,128)(2,1)S(1)}, u32[]{:S(2)}, u32[]{:S(2)}) collective-permute-start(bf16[192,1440]{1,0:T(8,128)(2,1)S(1)} %get-tuple-element.56), channel_id=1, source_target_pairs={{0,1},{1,0},{2,3},{3,2},{4,5},{5,4},{6,7},{7,6},{8,9},{9,8},{10,11... | collective-permute-start | bytes 1658888 | tf_op jit(solution)/shard_map/ppermute | solution.py:203
  33.0 2.3 %collective-permute-start.6 = (bf16[128,1440]{1,0:T(8,128)(2,1)S(1)}, bf16[128,1440]{1,0:T(8,128)(2,1)S(1)}, u32[]{:S(2)}, u32[]{:S(2)}) collective-permute-start(bf16[128,1440]{1,0:T(8,128)(2,1)S(1)} %get-tuple-element.50), channel_id=1, source_target_pairs={{0,1},{1,0},{2,3},{3,2},{4,5},{5,4},{6,7},{7,6},{8,9},{9,8},{10,11... | collective-permute-start | bytes 1105928 | tf_op jit(solution)/shard_map/ppermute | solution.py:203
  33.3 16.5 %collective-permute-start.18 = (bf16[64,1464]{1,0:T(8,128)(2,1)S(1)}, bf16[64,1464]{1,0:T(8,128)(2,1)S(1)}, u32[]{:S(2)}, u32[]{:S(2)}) collective-permute-start(bf16[64,1464]{1,0:T(8,128)(2,1)S(1)} %shard_map.64.refs_0_), channel_id=1, source_target_pairs={{0,1},{1,0},{2,3},{3,2},{4,5},{5,4},{6,7},{7,6},{8,9},{9,8},{10,11... | collective-permute-start | bytes 562184 | tf_op jit(solution)/shard_map/ppermute | solution.py:214
  33.5 6.0 %collective-permute-start.15 = (bf16[64,1464]{1,0:T(8,128)(2,1)S(1)}, bf16[64,1464]{1,0:T(8,128)(2,1)S(1)}, u32[]{:S(2)}, u32[]{:S(2)}) collective-permute-start(bf16[64,1464]{1,0:T(8,128)(2,1)S(1)} %collective-permute-done.refs_0_), channel_id=1, source_target_pairs={{0,1},{1,0},{2,3},{3,2},{4,5},{5,4},{6,7},{7,6},{8,9},{9,8},{10,11... | collective-permute-start | bytes 562184 | tf_op jit(solution)/shard_map/ppermute | solution.py:220
  33.8 8.7 %collective-permute-start.16 = (bf16[64,1464]{1,0:T(8,128)(2,1)S(1)}, bf16[64,1464]{1,0:T(8,128)(2,1)S(1)}, u32[]{:S(2)}, u32[]{:S(2)}) collective-permute-start(bf16[64,1464]{1,0:T(8,128)(2,1)S(1)} %collective-permute-done.2.refs_1_), channel_id=1, source_target_pairs={{0,1},{1,0},{2,3},{3,2},{4,5},{5,4},{6,7},{7,6},{8,9},{9,8},{10,11... | collective-permute-start | bytes 562184 | tf_op jit(solution)/shard_map/ppermute | solution.py:220
  35.4 9.9 %collective-permute-start.17 = (bf16[64,1440]{1,0:T(8,128)(2,1)S(1)}, bf16[64,1440]{1,0:T(8,128)(2,1)S(1)}, u32[]{:S(2)}, u32[]{:S(2)}) collective-permute-start(bf16[64,1440]{1,0:T(8,128)(2,1)S(1)} %add_convert_fusion.3), channel_id=1, source_target_pairs={{4,0},{8,4},{12,8},{14,12},{10,14},{6,10},{2,6},{0,2},{5,1},{9,5},... | collective-permute-start | bytes 552968 | tf_op jit(solution)/shard_map/ppermute | solution.py:237
  36.9 10.1 %collective-permute-start.14 = (bf16[64,1440]{1,0:T(8,128)(2,1)S(1)}, bf16[64,1440]{1,0:T(8,128)(2,1)S(1)}, u32[]{:S(2)}, u32[]{:S(2)}) collective-permute-start(bf16[64,1440]{1,0:T(8,128)(2,1)S(1)} %add_convert_fusion.5), channel_id=1, source_target_pairs={{0,4},{4,8},{8,12},{12,14},{14,10},{10,6},{6,2},{2,0},{1,5},{5,9},... | collective-permute-start | bytes 552968 | tf_op jit(solution)/shard_map/ppermute | solution.py:236
  39.4 13.4 %collective-permute-start.22 = (bf16[64,1440]{1,0:T(8,128)(2,1)S(1)}, bf16[64,1440]{1,0:T(8,128)(2,1)S(1)}, u32[]{:S(2)}, u32[]{:S(2)}) collective-permute-start(bf16[64,1440]{1,0:T(8,128)(2,1)S(1)} %add_convert_fusion.1), channel_id=1, source_target_pairs={{0,14},{2,12},{4,6},{6,4},{8,10},{10,8},{12,2},{14,0},{1,15},{3,13... | collective-permute-start | bytes 552968 | tf_op jit(solution)/shard_map/ppermute | solution.py:232
  45.2 10.1 %collective-permute-start.20 = (bf16[128,1440]{1,0:T(8,128)(2,1)S(1)}, bf16[128,1440]{1,0:T(8,128)(2,1)S(1)}, u32[]{:S(2)}, u32[]{:S(2)}) collective-permute-start(bf16[128,1440]{1,0:T(8,128)(2,1)S(1)} %get-tuple-element.60), channel_id=1, source_target_pairs={{0,1},{1,0},{2,3},{3,2},{4,5},{5,4},{6,7},{7,6},{8,9},{9,8},{10,11... | collective-permute-start | bytes 1105928 | tf_op jit(solution)/shard_map/ppermute | solution.py:203
  45.4 9.9 %collective-permute-start.24 = (bf16[64,1440]{1,0:T(8,128)(2,1)S(1)}, bf16[64,1440]{1,0:T(8,128)(2,1)S(1)}, u32[]{:S(2)}, u32[]{:S(2)}) collective-permute-start(bf16[64,1440]{1,0:T(8,128)(2,1)S(1)} %add_convert_fusion.2), channel_id=1, source_target_pairs={{4,0},{8,4},{12,8},{14,12},{10,14},{6,10},{2,6},{0,2},{5,1},{9,5},... | collective-permute-start | bytes 552968 | tf_op jit(solution)/shard_map/ppermute | solution.py:237
  47.1 9.8 %collective-permute-start.21 = (bf16[64,1440]{1,0:T(8,128)(2,1)S(1)}, bf16[64,1440]{1,0:T(8,128)(2,1)S(1)}, u32[]{:S(2)}, u32[]{:S(2)}) collective-permute-start(bf16[64,1440]{1,0:T(8,128)(2,1)S(1)} %add_convert_fusion.4), channel_id=1, source_target_pairs={{0,4},{4,8},{8,12},{12,14},{14,10},{10,6},{6,2},{2,0},{1,5},{5,9},... | collective-permute-start | bytes 552968 | tf_op jit(solution)/shard_map/ppermute | solution.py:236
  52.8 4.8 %collective-permute-start.19 = (bf16[64,1440]{1,0:T(8,128)(2,1)S(1)}, bf16[64,1440]{1,0:T(8,128)(2,1)S(1)}, u32[]{:S(2)}, u32[]{:S(2)}) collective-permute-start(bf16[64,1440]{1,0:T(8,128)(2,1)S(1)} %get-tuple-element.65), channel_id=1, source_target_pairs={{0,1},{1,0},{2,3},{3,2},{4,5},{5,4},{6,7},{7,6},{8,9},{9,8},{10,11... | collective-permute-start | bytes 552968 | tf_op jit(solution)/shard_map/ppermute | solution.py:203
  55.4 6.9 %collective-permute-start.25 = (bf16[64,1440]{1,0:T(8,128)(2,1)S(1)}, bf16[64,1440]{1,0:T(8,128)(2,1)S(1)}, u32[]{:S(2)}, u32[]{:S(2)}) collective-permute-start(bf16[64,1440]{1,0:T(8,128)(2,1)S(1)} %add_convert_fusion), channel_id=1, source_target_pairs={{4,0},{8,4},{12,8},{14,12},{10,14},{6,10},{2,6},{0,2},{5,1},{9,5},... | collective-permute-start | bytes 552968 | tf_op jit(solution)/shard_map/ppermute | solution.py:237
  57.0 6.6 %collective-permute-start.23 = (bf16[64,1440]{1,0:T(8,128)(2,1)S(1)}, bf16[64,1440]{1,0:T(8,128)(2,1)S(1)}, u32[]{:S(2)}, u32[]{:S(2)}) collective-permute-start(bf16[64,1440]{1,0:T(8,128)(2,1)S(1)} %fusion.1), channel_id=1, source_target_pairs={{0,4},{4,8},{8,12},{12,14},{14,10},{10,6},{6,2},{2,0},{1,5},{5,9},... | collective-permute-start | bytes 552968 | tf_op jit(solution)/shard_map/ppermute | solution.py:236

commit v6 on v5

--- a/solution.py
+++ b/solution.py
@@ -128,51 +128,140 @@
     )(place, pltpu.with_memory_space_constraint(w_down, pltpu.HBM))
 
 
+def gather_rows(blocks, x, width):
+    start = 0
+    for block in blocks:
+        x[start : start + block.shape[0], :] = block[:, :width]
+        start += block.shape[0]
+    if start < x.shape[0]:
+        x[start:, :] = jnp.zeros((x.shape[0] - start, width), x.dtype)
+
+
+def project(x, lane, w):
+    half = x.shape[1]
+    return jnp.dot(x[...], w[pl.ds(pl.multiple_of(lane * half, 16), half), :], preferred_element_type=jnp.float32)
+
+
+def activate(gated, lifted):
+    return (gated / (1.0 + jnp.exp(-gated)) * lifted).astype(jnp.bfloat16)
+
+
+def gate_weights(blocks, half, expert, n_experts):
+    weights = []
+    for block in blocks:
+        terms = block[:, half:].astype(jnp.float32)
+        column = lax.broadcasted_iota(jnp.int32, terms.shape, 1)
+        weights.append(jnp.sum(jnp.where(lax.rem(column, n_experts) == expert, terms, 0.0), axis=1, keepdims=True))
+    return weights
+
+
+def lower(hidden, w, weights, out):
+    value = jnp.dot(hidden, w[...], preferred_element_type=jnp.float32)
+    start = 0
+    for weight in weights:
+        span = slice(start, start + weight.shape[0])
+        start = span.stop
+        out[span] = (value[span] * weight).astype(jnp.bfloat16)
+
+
 def expert_kernel(n_blocks, n_experts, place, *refs):
     own, across = refs[:n_blocks], refs[n_blocks : 2 * n_blocks]
     w_gate, w_up, down_mine, down_theirs, mine, theirs, x_own, x_across = refs[2 * n_blocks :]
     lane, expert = place[0], place[1]
     half = mine.shape[1]
-    spans, start = [], 0
-    for a, b in zip(own, across):
-        spans.append(slice(start, start + a.shape[0]))
-        x_own[spans[-1], :] = a[:, :half]
-        x_across[spans[-1], :] = b[:, :half]
-        start += a.shape[0]
-    here = pl.ds(pl.multiple_of(lane * half, 16), half)
-    there = pl.ds(pl.multiple_of((1 - lane) * half, 16), half)
-
-    def project(w):
-        near = jnp.dot(x_own[...], w[here, :], preferred_element_type=jnp.float32)
-        return near + jnp.dot(x_across[...], w[there, :], preferred_element_type=jnp.float32)
-
-    gated = project(w_gate)
-    lifted = project(w_up)
-    hidden = (gated / (1.0 + jnp.exp(-gated)) * lifted).astype(jnp.bfloat16)
-    weights = []
-    for a in own:
-        terms = a[:, half:].astype(jnp.float32)
-        column = lax.broadcasted_iota(jnp.int32, terms.shape, 1)
-        weights.append(jnp.sum(jnp.where(lax.rem(column, n_experts) == expert, terms, 0.0), axis=1, keepdims=True))
-    for w, out in ((down_theirs, theirs), (down_mine, mine)):
-        value = jnp.dot(hidden, w[...], preferred_element_type=jnp.float32)
-        for span, weight in zip(spans, weights):
-            out[span] = (value[span] * weight).astype(jnp.bfloat16)
+    gather_rows(own, x_own, half)
+    gather_rows(across, x_across, half)
+    gated = project(x_own, lane, w_gate) + project(x_across, 1 - lane, w_gate)
+    lifted = project(x_own, lane, w_up) + project(x_across, 1 - lane, w_up)
+    hidden = activate(gated, lifted)
+    weights = gate_weights(own, half, expert, n_experts)
+    lower(hidden, down_theirs, weights, theirs)
+    lower(hidden, down_mine, weights, mine)
+
+
+def first_kernel(n_blocks, place, *refs):
+    own = refs[:n_blocks]
+    w_gate, w_up, gated, lifted, x = refs[n_blocks:]
+    gather_rows(own, x, x.shape[1])
+    gated[...] = project(x, place[0], w_gate)
+    lifted[...] = project(x, place[0], w_up)
+
+
+def second_kernel(n_blocks, n_experts, place, *refs):
+    own, across = refs[:n_blocks], refs[n_blocks : 2 * n_blocks]
+    gated, lifted, w_gate, w_up, down_theirs, hidden, theirs, x = refs[2 * n_blocks :]
+    half = x.shape[1]
+    gather_rows(across, x, half)
+    there = 1 - place[0]
+    hidden[...] = activate(gated[...] + project(x, there, w_gate), lifted[...] + project(x, there, w_up))
+    lower(hidden[...], down_theirs, gate_weights(own, half, place[1], n_experts), theirs)
+
+
+def third_kernel(n_blocks, n_experts, place, *refs):
+    own = refs[:n_blocks]
+    hidden, down_mine, mine = refs[n_blocks:]
+    lower(hidden[...], down_mine, gate_weights(own, mine.shape[1], place[1], n_experts), mine)
+
+
+def call(kernel, place, args, out_shape, scratch_shapes, flops):
+    vmem = pl.BlockSpec(memory_space=pltpu.VMEM)
+    return pl.pallas_call(
+        kernel,
+        out_shape=out_shape,
+        in_specs=[pl.BlockSpec(memory_space=pltpu.SMEM)] + [vmem] * len(args),
+        out_specs=[vmem] * len(out_shape),
+        scratch_shapes=scratch_shapes,
+        compiler_params=pltpu.CompilerParams(vmem_limit_bytes=16 << 20),
+        cost_estimate=pl.CostEstimate(flops=flops, bytes_accessed=flops // 128, transcendentals=0),
+    )(place, *[hold(a) for a in args])
+
+
+def padded(rows):
+    return -(-rows // 128) * 128
 
 
 def run_expert(place, own, across, weights, n_experts):
     width, hidden = weights[0].shape
+    half = width // 2
     rows = sum(a.shape[0] for a in own)
-    vmem = pl.BlockSpec(memory_space=pltpu.VMEM)
-    return pl.pallas_call(
+    return call(
         functools.partial(expert_kernel, len(own), n_experts),
-        out_shape=[in_vmem((rows, width // 2))] * 2,
-        in_specs=[pl.BlockSpec(memory_space=pltpu.SMEM)] + [vmem] * (2 * len(own) + 4),
-        out_specs=[vmem] * 2,
-        scratch_shapes=[pltpu.VMEM((rows, width // 2), jnp.bfloat16)] * 2,
-        compiler_params=pltpu.CompilerParams(vmem_limit_bytes=16 << 20),
-        cost_estimate=pl.CostEstimate(flops=6 * rows * hidden * width, bytes_accessed=6 * hidden * width, transcendentals=0),
-    )(place, *[hold(a) for a in own], *[hold(a) for a in across], *[hold(w) for w in weights])
+        place,
+        (*own, *across, *weights),
+        [in_vmem((rows, half))] * 2,
+        [pltpu.VMEM((padded(rows), half), jnp.bfloat16)] * 2,
+        6 * padded(rows) * hidden * width,
+    )
+
+
+def run_expert_in_stages(place, own, swap, weights, n_experts):
+    gate, up, down_mine, down_theirs = weights
+    width, hidden = gate.shape
+    half = width // 2
+    rows, n_blocks = sum(a.shape[0] for a in own), len(own)
+    across = [swap(a) for a in own]
+    products = [in_vmem((padded(rows), hidden), jnp.float32)] * 2
+    x = [pltpu.VMEM((padded(rows), half), jnp.bfloat16)]
+    flops = 2 * padded(rows) * hidden * width
+    gated, lifted = call(functools.partial(first_kernel, n_blocks), place, (*own, gate, up), products, x, flops)
+    units, theirs = call(
+        functools.partial(second_kernel, n_blocks, n_experts),
+        place,
+        (*own, *across, gated, lifted, gate, up, down_theirs),
+        [in_vmem((padded(rows), hidden)), in_vmem((rows, half))],
+        x,
+        flops + flops // 2,
+    )
+    theirs = swap(theirs)
+    (mine,) = call(
+        functools.partial(third_kernel, n_blocks, n_experts),
+        place,
+        (*own, units, down_mine),
+        [in_vmem((rows, half))],
+        [],
+        flops // 2,
+    )
+    return mine, theirs
 
 
 def ring_body(tokens, expert_ids, gate_probs, w_gate, w_up, w_down):
@@ -181,17 +270,9 @@
     order = list(range(0, n, 2)) + list(range(n - 1, 0, -2))
     ahead = [(order[i], order[(i + 1) % n]) for i in range(n)]
     back = [(b, a) for a, b in ahead]
-    levels = n // 2
-    middle = (levels // 2 - 1, levels // 2)
-    opposite = [(i, i ^ 1 if i // 2 in middle else n - 1 - i) for i in range(n)]
     swap = functools.partial(lax.ppermute, axis_name="tp", perm=[(0, 1), (1, 0)])
     far = n // 2
-    me = lax.axis_index("ep")
-    level, side = me // 2, me % 2
-    relays = (level == middle[0]) | (level == middle[1])
-    relays_ahead = relays & ((level == middle[0]) == (side == 0))
-    relays_back = relays & ~relays_ahead
-    place = jnp.stack([lax.axis_index("tp"), me]).astype(jnp.int32)
+    place = jnp.stack([lax.axis_index("tp"), lax.axis_index("ep")]).astype(jnp.int32)
     packed = pack(tokens, expert_ids, gate_probs, n)
     gate, up = turn_weights(after(place, packed), w_gate[0].T, w_up[0].T)
 
@@ -200,14 +281,16 @@
     def run(keys, wait_for=None):
         at = place if wait_for is None else after(place, wait_for)
         mine, theirs = run_expert(at, [came[k] for k in keys], [across[k] for k in keys], weights, n)
-        done, theirs = theirs, swap(theirs)
+        keep(keys, mine, swap(theirs))
+        return theirs
+
+    def keep(keys, mine, theirs):
         start = 0
         for k in keys:
             span = slice(start, start + came[k].shape[0])
             start = span.stop
             value[k] = mine[span].astype(jnp.float32) + theirs[span].astype(jnp.float32)
             mine, theirs = lax.optimization_barrier((mine, theirs))
-        return done
 
     came[1] = lax.ppermute(packed, "ep", ahead)
     came[-1] = lax.ppermute(packed, "ep", back)
@@ -219,33 +302,36 @@
         came[-k] = lax.ppermute(came[1 - k], "ep", back)
         across[k - 1], across[1 - k] = swap(came[k - 1]), swap(came[1 - k])
         if k == 2:
-            passed = jnp.where(relays_ahead, came[-1], jnp.where(relays_back, came[1], packed))
-            came[far] = lax.ppermute(passed, "ep", opposite)
             weights += halve_weights(after(place, came[1]), w_down[0])
             done = weights[-1]
         else:
-            done = run([k - 1, 1 - k])
+            done = run([k - 2, 2 - k], across[0] if k == 3 else None)
     came[far - 1], came[1 - far] = after(came[far - 1], done), after(came[1 - far], done)
+    came["low"] = lax.ppermute(came[far - 1][: rows // 2], "ep", ahead)
+    came["high"] = lax.ppermute(came[1 - far][rows // 2 :], "ep", back)
     across[far - 1], across[1 - far] = swap(came[far - 1]), swap(came[1 - far])
-    across[far] = swap(came[far])
-    run([far - 1, 1 - far, far])
-    returned = lax.ppermute(value[far].astype(jnp.bfloat16), "ep", opposite)
-
-    to_ahead, to_back = value[1 - far].astype(jnp.bfloat16), value[far - 1].astype(jnp.bfloat16)
-    for k in range(far - 1, 0, -1):
+    done = run([far - 1, 1 - far], (across[far - 2], across[2 - far]))
+    came["low"], came["high"] = after((came["low"], came["high"]), done)
+    far_keys = ["low", "high"]
+    keep(far_keys, *run_expert_in_stages(place, [came[k] for k in far_keys], swap, weights, n))
+
+    to_ahead = value["low"].astype(jnp.bfloat16)
+    to_back = value["high"].astype(jnp.bfloat16)
+    pad_low, pad_high = ((0, rows - rows // 2), (0, 0)), ((rows // 2, 0), (0, 0))
+    for k in range(far - 1, -1, -1):
         behind = lax.ppermute(to_ahead, "ep", ahead)
         front = lax.ppermute(to_back, "ep", back)
         if k >= far - 2:
-            done = run([1, -1] if k == far - 1 else [0], (to_ahead, to_back))
-        if k > 1:
-            to_ahead, to_back = value[1 - k] + behind.astype(jnp.float32), value[k - 1] + front.astype(jnp.float32)
-            if k == 2:
-                for_back = lax.optimization_barrier(returned).astype(jnp.float32)
-                to_ahead += jnp.where(relays_ahead, returned.astype(jnp.float32), 0.0)
-                to_back += jnp.where(relays_back, for_back, 0.0)
-            to_ahead, to_back = after(to_ahead.astype(jnp.bfloat16), done), after(to_back.astype(jnp.bfloat16), done)
-    total = value[0] + behind.astype(jnp.float32) + front.astype(jnp.float32)
-    return (total + jnp.where(relays, 0.0, returned.astype(jnp.float32))).astype(jnp.bfloat16)
+            done = run([far - 2, 2 - far] if k == far - 1 else [0], (to_ahead, to_back))
+        behind, front = behind.astype(jnp.float32), front.astype(jnp.float32)
+        if k == far - 1:
+            behind, front = jnp.pad(behind, pad_low), jnp.pad(front, pad_high)
+        if k:
+            to_ahead = (value[-k] + behind).astype(jnp.bfloat16)
+            to_back = (value[k] + front).astype(jnp.bfloat16)
+        if k >= far - 2:
+            to_ahead, to_back = after(to_ahead, done), after(to_back, done)
+    return (value[0] + behind + front).astype(jnp.bfloat16)
 
 
 def swiglu_expert(rows, gate_part, up_part, down_part):
@@ -321,7 +407,7 @@
 
     def body(tokens, expert_ids, *rest):
         n, top = lax.axis_size("ep"), expert_ids.shape[1]
-        small = n <= 4 * top and n % 4 == 0 and n >= 8 and lax.axis_size("tp") == 2
+        small = n <= 4 * top and n % 2 == 0 and n >= 6 and lax.axis_size("tp") == 2
         return (ring_body if small else slot_body)(tokens, expert_ids, *rest)
 
     return jax.shard_map(body, mesh=mesh, in_specs=in_specs, out_specs=out_specs, check_vma=False)

time: 64.6 us -> 63 us (0.975)
  starting transfers between devices: 28.2 us -> 20.5 us
  waiting for transfers between devices: 13.7 us -> 17 us
  Pallas kernels: 21 us -> 23.8 us
    ppermute x3 -> x4, waiting for transfers between devices: 1.37 us -> 9.99 us  [ring_body(): behind = lax.ppermute(to_ahead, 'ep', ahead)]
    ppermute x3 -> x4, waiting for transfers between devices: 7.06 us -> 1.72 us  [ring_body(): front = lax.ppermute(to_back, 'ep', back)]
    ppermute x7 -> x9, starting transfers between devices: 8.79 us -> 3.8 us  [the longest x1 1.63 us: ring_body(): came['low'] = lax.ppermute(came[far - 1][:rows // 2], 'ep', ahead)]
    pallas_call x4 -> x7, Pallas kernels: 12 us -> 14.9 us  [call(): pl.pallas_call(kernel, out_shape=out_shape, in_specs=[pl.BlockSpec(memory...]
    ppermute x3 -> x4, starting transfers between devices: 4.62 us -> 2 us  [ring_body(): front = lax.ppermute(to_back, 'ep', back)]
    ppermute x2, starting transfers between devices: 2.18 us -> 3.82 us  [ring_body(): came[k] = lax.ppermute(came[k - 1], 'ep', ahead)]
    ppermute x2, starting transfers between devices: 1.93 us -> 0.29 us  [ring_body(): came[-k] = lax.ppermute(came[1 - k], 'ep', back)]
    ppermute x2, waiting for transfers between devices: 0.42 us -> 1.55 us  [ring_body(): came[-k] = lax.ppermute(came[1 - k], 'ep', back)]
  transfers between devices with their start and end apart: 26 -> 30, of which waited for: 9 -> 9; matrix products, arithmetic and copies ran while one was open for 1% -> 1% of each run, Pallas kernels for 25% -> 36%
where the time goes in v6:
time: 63 us; the launch traced here: 62.9 us
  Pallas kernels  23.8 us (38%)
  starting transfers between devices  20.5 us (33%)
  waiting for transfers between devices  17 us (27%)
  other arithmetic  1.32 us (2%)
    pallas_call x7, Pallas kernels, call(): pl.pallas_call(kernel, out_shape=out_shape, in_specs=[pl.BlockSpec(memory...  14.9 us
    ppermute x4, waiting for transfers between devices, ring_body(): behind = lax.ppermute(to_ahead, 'ep', ahead)  9.99 us
    ppermute x4, starting transfers between devices, ring_body(): behind = lax.ppermute(to_ahead, 'ep', ahead)  6.47 us
    pallas_call x1, Pallas kernels, turn_weights(): pl.pallas_call(turn_kernel, out_shape=[in_vmem((width, hidden))] * 2, in_...  4.79 us
    ppermute x2, starting transfers between devices, ring_body(): came[k] = lax.ppermute(came[k - 1], 'ep', ahead)  3.82 us
    pallas_call x1, Pallas kernels, halve_weights(): pl.pallas_call(halve_kernel, out_shape=[in_vmem((hidden, width // 2))] *...  3.13 us
    ppermute x1, starting transfers between devices, ring_body(): came[1] = lax.ppermute(packed, 'ep', ahead)  3.08 us
    ppermute x2, waiting for transfers between devices, ring_body(): came[k] = lax.ppermute(came[k - 1], 'ep', ahead)  2.24 us
  transfers between devices with their start and end apart: 30, of which 9 were waited for; matrix products, arithmetic and copies ran while one was open for 1% of the time, Pallas kernels for 36%

profile of v6, /device:TPU:0, one launch (start us, length us, event | category | flops | bytes accessed | tf_op | source)
XLA Modules:
  0.0 62.9 jit_solution(5685544002527151782)
XLA Ops:
  0.0 1.0 %shard_map.64.refs_0_ = bf16[64,1464]{1,0:T(8,128)(2,1)S(1)} custom-call(bf16[64,1440]{1,0:T(8,128)(2,1)} %tokens_in.1, s32[4,64]{1,0:T(4,128)} %bitcast.14, f32[4,64]{1,0:T(4,128)} %bitcast.15), custom_call_target="tpu_custom_call" | custom-call | tf_op jit(solution)/shard_map/pallas_call | solution.py:53
  1.0 3.1 %collective-permute-start = (bf16[64,1464]{1,0:T(8,128)(2,1)S(1)}, bf16[64,1464]{1,0:T(8,128)(2,1)S(1)}, u32[]{:S(2)}, u32[]{:S(2)}) collective-permute-start(bf16[64,1464]{1,0:T(8,128)(2,1)S(1)} %shard_map.64.refs_0_), channel_id=1, source_target_pairs={{0,4},{4,8},{8,12},{12,14},{14,10},{10,6},{6,2},{2,0},{1,5},{5,9},... | collective-permute-start | bytes 562184 | tf_op jit(solution)/shard_map/ppermute | solution.py:295
  4.1 0.0 collective-permute-start.3
  4.1 0.1 pad_add_fusion.after_this.place
  4.2 4.8 %shard_map.65 = (bf16[2880,720]{1,0:T(8,128)(2,1)S(1)}, bf16[2880,720]{1,0:T(8,128)(2,1)S(1)}) custom-call(s32[2]{0:T(128)S(1)} %pad_add_fusion.after_this.place, bf16[720,2880]{1,0:T(8,128)(2,1)} %bitcast.11, bf16[720,2880]{1,0:T(8,128)(2,1)} %bitcast.12), custom_call_target="tpu_custom_call" | custom-call | bytes 16588800 | tf_op jit(solution)/shard_map/pallas_call | solution.py:83
  9.0 0.0 collective-permute-done.refs_0_
  9.0 2.1 %collective-permute-start.1 = (bf16[64,1464]{1,0:T(8,128)(2,1)S(1)}, bf16[64,1464]{1,0:T(8,128)(2,1)S(1)}, u32[]{:S(2)}, u32[]{:S(2)}) collective-permute-start(bf16[64,1464]{1,0:T(8,128)(2,1)S(1)} %collective-permute-done.refs_0_), channel_id=1, source_target_pairs={{0,4},{4,8},{8,12},{12,14},{14,10},{10,6},{6,2},{2,0},{1,5},{5,9},... | collective-permute-start | bytes 562184 | tf_op jit(solution)/shard_map/ppermute | solution.py:301
  11.0 0.0 collective-permute-done.3.refs_1_
  11.1 0.0 collective-permute-start.4
  11.1 0.5 collective-permute-start.8
  11.6 0.1 collective-permute-start.9
  11.6 3.1 %shard_map.66 = (bf16[720,1440]{1,0:T(8,128)(2,1)S(1)}, bf16[720,1440]{1,0:T(8,128)(2,1)S(1)}) custom-call(s32[2]{0:T(128)S(1)} %pad_add_fusion.after_this.place, bf16[720,2880]{1,0:T(8,128)(2,1)} %bitcast.13), custom_call_target="tpu_custom_call" | custom-call | bytes 16588800 | tf_op jit(solution)/shard_map/pallas_call | solution.py:120
  14.8 0.6 collective-permute-done.1.refs_0_
  15.4 1.7 %collective-permute-start.6 = (bf16[64,1464]{1,0:T(8,128)(2,1)S(1)}, bf16[64,1464]{1,0:T(8,128)(2,1)S(1)}, u32[]{:S(2)}, u32[]{:S(2)}) collective-permute-start(bf16[64,1464]{1,0:T(8,128)(2,1)S(1)} %collective-permute-done.1.refs_0_), channel_id=1, source_target_pairs={{0,4},{4,8},{8,12},{12,14},{14,10},{10,6},{6,2},{2,0},{1,5},{5,9},... | collective-permute-start | bytes 562184 | tf_op jit(solution)/shard_map/ppermute | solution.py:301
  17.1 0.3 collective-permute-start.10
  17.4 0.0 collective-permute-done.7.refs_1_
  17.4 0.5 collective-permute-start.5
  17.9 0.0 collective-permute-done.9.refs_3_
  17.9 2.7 %shard_map.67 = (bf16[128,1440]{1,0:T(8,128)(2,1)S(1)}, bf16[128,1440]{1,0:T(8,128)(2,1)S(1)}) custom-call(s32[2]{0:T(128)S(1)} %pad_add_fusion.after_this.place, bf16[64,1464]{1,0:T(8,128)(2,1)S(1)} %collective-permute-done.refs_0_, bf16[64,1464]{1,0:T(8,128)(2,1)S(1)} %collective-permute-done.3.refs_1_, ...), custom_call_target="tpu_custom_call" | custom-call | flops 1592524800 | bytes 12441600 | tf_op jit(solution)/shard_map/pallas_call | solution.py:208
  20.6 1.6 %collective-permute-done.6.refs_0_ = bf16[64,1464]{1,0:T(8,128)(2,1)S(1)} collective-permute-done((bf16[64,1464]{1,0:T(8,128)(2,1)S(1)}, bf16[64,1464]{1,0:T(8,128)(2,1)S(1)}, u32[]{:S(2)}, u32[]{:S(2)}) %collective-permute-start.6) | collective-permute-done | bytes 187424 | tf_op jit(solution)/shard_map/ppermute | solution.py:301
  22.3 0.0 collective-permute-start.11
  22.3 1.5 %collective-permute-done.10.refs_1_ = bf16[64,1464]{1,0:T(8,128)(2,1)S(1)} collective-permute-done((bf16[64,1464]{1,0:T(8,128)(2,1)S(1)}, bf16[64,1464]{1,0:T(8,128)(2,1)S(1)}, u32[]{:S(2)}, u32[]{:S(2)}) %collective-permute-start.10) | collective-permute-done | bytes 187424 | tf_op jit(solution)/shard_map/ppermute | solution.py:302
  23.8 0.5 collective-permute-start.22
  24.4 0.0 collective-permute-done.2.refs_2_
  24.4 1.6 %collective-permute-start.14 = (bf16[32,1464]{1,0:T(8,128)(2,1)S(1)}, bf16[32,1464]{1,0:T(8,128)(2,1)S(1)}, u32[]{:S(2)}, u32[]{:S(2)}) collective-permute-start(bf16[32,1464]{1,0:T(8,128)(2,1)S(1)} %slice.56), channel_id=1, source_target_pairs={{0,4},{4,8},{8,12},{12,14},{14,10},{10,6},{6,2},{2,0},{1,5},{5,9},... | collective-permute-start | bytes 281096 | tf_op jit(solution)/shard_map/ppermute | solution.py:310
  26.0 0.4 collective-permute-start.15
  26.5 0.0 collective-permute-done.11.refs_2_
  26.5 2.7 %shard_map.68 = (bf16[128,1440]{1,0:T(8,128)(2,1)S(1)}, bf16[128,1440]{1,0:T(8,128)(2,1)S(1)}) custom-call(s32[2]{0:T(128)S(1)} %pad_add_fusion.after_this.place, bf16[64,1464]{1,0:T(8,128)(2,1)S(1)} %collective-permute-done.6.refs_0_, bf16[64,1464]{1,0:T(8,128)(2,1)S(1)} %collective-permute-done.10.refs_1_, ...), custom_call_target="tpu_custom_call" | custom-call | flops 1592524800 | bytes 12441600 | tf_op jit(solution)/shard_map/pallas_call | solution.py:208
  29.2 0.0 collective-permute-done.14.refs_0_
  29.2 1.4 %collective-permute-done.15.refs_1_ = bf16[32,1464]{1,0:T(8,128)(2,1)S(1)} collective-permute-done((bf16[32,1464]{1,0:T(8,128)(2,1)S(1)}, bf16[32,1464]{1,0:T(8,128)(2,1)S(1)}, u32[]{:S(2)}, u32[]{:S(2)}) %collective-permute-start.15) | collective-permute-done | bytes 93728 | tf_op jit(solution)/shard_map/ppermute | solution.py:311
  30.6 0.0 collective-permute-start.16
  30.6 0.5 collective-permute-start.17
  31.1 1.3 %shard_map.69 = (f32[128,720]{1,0:T(8,128)S(1)}, f32[128,720]{1,0:T(8,128)S(1)}) custom-call(s32[2]{0:T(128)S(1)} %pad_add_fusion.after_this.place, bf16[32,1464]{1,0:T(8,128)(2,1)S(1)} %collective-permute-done.14.refs_0_, bf16[32,1464]{1,0:T(8,128)(2,1)S(1)} %collective-permute-done.15.refs_1_, ...), custom_call_target="tpu_custom_call" | custom-call | flops 530841600 | bytes 4147200 | tf_op jit(solution)/shard_map/pallas_call | solution.py:208
  32.5 0.0 collective-permute-done.16.refs_2_
  32.5 1.8 %shard_map.70 = (bf16[128,720]{1,0:T(8,128)(2,1)S(1)}, bf16[64,1440]{1,0:T(8,128)(2,1)S(1)}) custom-call(s32[2]{0:T(128)S(1)} %pad_add_fusion.after_this.place, bf16[32,1464]{1,0:T(8,128)(2,1)S(1)} %collective-permute-done.14.refs_0_, bf16[32,1464]{1,0:T(8,128)(2,1)S(1)} %collective-permute-done.15.refs_1_, ...), custom_call_target="tpu_custom_call" | custom-call | flops 796262400 | bytes 6220800 | tf_op jit(solution)/shard_map/pallas_call | solution.py:208
  34.2 0.1 collective-permute-start.18
  34.3 0.5 collective-permute-start.13
  34.8 1.0 %shard_map.71 = bf16[64,1440]{1,0:T(8,128)(2,1)S(1)} custom-call(s32[2]{0:T(128)S(1)} %pad_add_fusion.after_this.place, bf16[32,1464]{1,0:T(8,128)(2,1)S(1)} %collective-permute-done.14.refs_0_, bf16[32,1464]{1,0:T(8,128)(2,1)S(1)} %collective-permute-done.15.refs_1_, bf16[128,720]{1,0:T(8,128)(2,1)S(1)} %get-tuple-element.70.refs_2_, ...), custom_call_target="tpu_custom_call" | custom-call | flops 265420800 | bytes 2073600 | tf_op jit(solution)/shard_map/pallas_call | solution.py:208
  35.9 0.5 collective-permute-start.20
  36.4 1.6 %collective-permute-start.19 = (bf16[32,1440]{1,0:T(8,128)(2,1)S(1)}, bf16[32,1440]{1,0:T(8,128)(2,1)S(1)}, u32[]{:S(2)}, u32[]{:S(2)}) collective-permute-start(bf16[32,1440]{1,0:T(8,128)(2,1)S(1)} %get-tuple-element.90), channel_id=1, source_target_pairs={{0,4},{4,8},{8,12},{12,14},{14,10},{10,6},{6,2},{2,0},{1,5},{5,9},... | collective-permute-start | bytes 276488 | tf_op jit(solution)/shard_map/ppermute | solution.py:322
  38.0 2.7 %shard_map.72 = (bf16[128,1440]{1,0:T(8,128)(2,1)S(1)}, bf16[128,1440]{1,0:T(8,128)(2,1)S(1)}) custom-call(s32[2]{0:T(128)S(1)} %pad_add_fusion.after_this.place, bf16[64,1464]{1,0:T(8,128)(2,1)S(1)} %collective-permute-done.1.refs_0_, bf16[64,1464]{1,0:T(8,128)(2,1)S(1)} %collective-permute-done.4.refs_1_, ...), custom_call_target="tpu_custom_call" | custom-call | flops 1592524800 | bytes 12441600 | tf_op jit(solution)/shard_map/pallas_call | solution.py:208
  40.7 0.1 collective-permute-start.23
  40.8 0.2 collective-permute-done.19
  41.0 0.1 add_convert_fusion.6
  41.1 1.6 %collective-permute-start.24 = (bf16[64,1440]{1,0:T(8,128)(2,1)S(1)}, bf16[64,1440]{1,0:T(8,128)(2,1)S(1)}, u32[]{:S(2)}, u32[]{:S(2)}) collective-permute-start(bf16[64,1440]{1,0:T(8,128)(2,1)S(1)} %add_convert_fusion.6), channel_id=1, source_target_pairs={{0,4},{4,8},{8,12},{12,14},{14,10},{10,6},{6,2},{2,0},{1,5},{5,9},... | collective-permute-start | bytes 552968 | tf_op jit(solution)/shard_map/ppermute | solution.py:322
  42.7 0.0 collective-permute-done.20
  42.7 0.1 add_convert_fusion.5
  42.8 0.5 collective-permute-start.27
  43.3 2.7 %shard_map.73 = (bf16[64,1440]{1,0:T(8,128)(2,1)S(1)}, bf16[64,1440]{1,0:T(8,128)(2,1)S(1)}) custom-call(s32[2]{0:T(128)S(1)} %pad_add_fusion.after_this.place, bf16[64,1464]{1,0:T(8,128)(2,1)S(1)} %shard_map.64.refs_0_, bf16[64,1464]{1,0:T(8,128)(2,1)S(1)} %collective-permute-done.7.refs_1_, ...), custom_call_target="tpu_custom_call" | custom-call | flops 1592524800 | bytes 12441600 | tf_op jit(solution)/shard_map/pallas_call | solution.py:208
  46.0 0.1 collective-permute-start.21
  46.1 2.2 %collective-permute-done.24 = bf16[64,1440]{1,0:T(8,128)(2,1)S(1)} collective-permute-done((bf16[64,1440]{1,0:T(8,128)(2,1)S(1)}, bf16[64,1440]{1,0:T(8,128)(2,1)S(1)}, u32[]{:S(2)}, u32[]{:S(2)}) %collective-permute-start.24) | collective-permute-done | bytes 184352 | tf_op jit(solution)/shard_map/ppermute | solution.py:322
  48.2 0.1 add_convert_fusion.4
  48.3 1.6 %collective-permute-start.25 = (bf16[64,1440]{1,0:T(8,128)(2,1)S(1)}, bf16[64,1440]{1,0:T(8,128)(2,1)S(1)}, u32[]{:S(2)}, u32[]{:S(2)}) collective-permute-start(bf16[64,1440]{1,0:T(8,128)(2,1)S(1)} %add_convert_fusion.4), channel_id=1, source_target_pairs={{0,4},{4,8},{8,12},{12,14},{14,10},{10,6},{6,2},{2,0},{1,5},{5,9},... | collective-permute-start | bytes 552968 | tf_op jit(solution)/shard_map/ppermute | solution.py:322
  49.9 0.0 collective-permute-done.27
  49.9 0.1 add_convert_fusion.2
  50.0 0.5 collective-permute-start.28
  50.5 4.1 %collective-permute-done.25 = bf16[64,1440]{1,0:T(8,128)(2,1)S(1)} collective-permute-done((bf16[64,1440]{1,0:T(8,128)(2,1)S(1)}, bf16[64,1440]{1,0:T(8,128)(2,1)S(1)}, u32[]{:S(2)}, u32[]{:S(2)}) %collective-permute-start.25) | collective-permute-done | bytes 184352 | tf_op jit(solution)/shard_map/ppermute | solution.py:322
  54.6 0.1 add_convert_fusion.3
  54.7 1.6 %collective-permute-start.26 = (bf16[64,1440]{1,0:T(8,128)(2,1)S(1)}, bf16[64,1440]{1,0:T(8,128)(2,1)S(1)}, u32[]{:S(2)}, u32[]{:S(2)}) collective-permute-start(bf16[64,1440]{1,0:T(8,128)(2,1)S(1)} %add_convert_fusion.3), channel_id=1, source_target_pairs={{0,4},{4,8},{8,12},{12,14},{14,10},{10,6},{6,2},{2,0},{1,5},{5,9},... | collective-permute-start | bytes 552968 | tf_op jit(solution)/shard_map/ppermute | solution.py:322
  56.3 0.1 add_convert_fusion.1
  56.4 0.5 collective-permute-start.29
  56.9 3.5 %collective-permute-done.26 = bf16[64,1440]{1,0:T(8,128)(2,1)S(1)} collective-permute-done((bf16[64,1440]{1,0:T(8,128)(2,1)S(1)}, bf16[64,1440]{1,0:T(8,128)(2,1)S(1)}, u32[]{:S(2)}, u32[]{:S(2)}) %collective-permute-start.26) | collective-permute-done | bytes 184352 | tf_op jit(solution)/shard_map/ppermute | solution.py:322
  60.4 1.7 %collective-permute-done.29 = bf16[64,1440]{1,0:T(8,128)(2,1)S(1)} collective-permute-done((bf16[64,1440]{1,0:T(8,128)(2,1)S(1)}, bf16[64,1440]{1,0:T(8,128)(2,1)S(1)}, u32[]{:S(2)}, u32[]{:S(2)}) %collective-permute-start.29) | collective-permute-done | bytes 184352 | tf_op jit(solution)/shard_map/ppermute | solution.py:323
  62.1 0.8 %add_convert_fusion = bf16[64,1440]{1,0:T(8,128)(2,1)} fusion(bf16[64,1440]{1,0:T(8,128)(2,1)S(1)} %collective-permute-done.29, bf16[64,1440]{1,0:T(8,128)(2,1)S(1)} %collective-permute-done.26, bf16[64,1440]{1,0:T(8,128)(2,1)S(1)} %collective-permute-done.21, bf16[64,1440]{1,0:T(8,128)(2,1)S(1)} %get-tuple-element.79), kind=kLoop, calls=%fused_computation | loop fusion | flops 737280 | bytes 921600 | tf_op jit(solution)/shard_map/convert_element_type | solution.py:334
  (17 shorter events, 0.1 us)
Async XLA Ops:
  1.0 8.0 %collective-permute-start = (bf16[64,1464]{1,0:T(8,128)(2,1)S(1)}, bf16[64,1464]{1,0:T(8,128)(2,1)S(1)}, u32[]{:S(2)}, u32[]{:S(2)}) collective-permute-start(bf16[64,1464]{1,0:T(8,128)(2,1)S(1)} %shard_map.64.refs_0_), channel_id=1, source_target_pairs={{0,4},{4,8},{8,12},{12,14},{14,10},{10,6},{6,2},{2,0},{1,5},{5,9},... | collective-permute-start | bytes 562184 | tf_op jit(solution)/shard_map/ppermute | solution.py:295
  4.1 7.0 %collective-permute-start.3 = (bf16[64,1464]{1,0:T(8,128)(2,1)S(1)}, bf16[64,1464]{1,0:T(8,128)(2,1)S(1)}, u32[]{:S(2)}, u32[]{:S(2)}) collective-permute-start(bf16[64,1464]{1,0:T(8,128)(2,1)S(1)} %shard_map.64.refs_0_), channel_id=1, source_target_pairs={{4,0},{8,4},{12,8},{14,12},{10,14},{6,10},{2,6},{0,2},{5,1},{9,5},... | collective-permute-start | bytes 562184 | tf_op jit(solution)/shard_map/ppermute | solution.py:296
  9.0 6.4 %collective-permute-start.1 = (bf16[64,1464]{1,0:T(8,128)(2,1)S(1)}, bf16[64,1464]{1,0:T(8,128)(2,1)S(1)}, u32[]{:S(2)}, u32[]{:S(2)}) collective-permute-start(bf16[64,1464]{1,0:T(8,128)(2,1)S(1)} %collective-permute-done.refs_0_), channel_id=1, source_target_pairs={{0,4},{4,8},{8,12},{12,14},{14,10},{10,6},{6,2},{2,0},{1,5},{5,9},... | collective-permute-start | bytes 562184 | tf_op jit(solution)/shard_map/ppermute | solution.py:301
  11.1 6.1 %collective-permute-start.4 = (bf16[64,1464]{1,0:T(8,128)(2,1)S(1)}, bf16[64,1464]{1,0:T(8,128)(2,1)S(1)}, u32[]{:S(2)}, u32[]{:S(2)}) collective-permute-start(bf16[64,1464]{1,0:T(8,128)(2,1)S(1)} %collective-permute-done.3.refs_1_), channel_id=1, source_target_pairs={{4,0},{8,4},{12,8},{14,12},{10,14},{6,10},{2,6},{0,2},{5,1},{9,5},... | collective-permute-start | bytes 562184 | tf_op jit(solution)/shard_map/ppermute | solution.py:302
  11.1 6.4 %collective-permute-start.7 = (bf16[64,1464]{1,0:T(8,128)(2,1)S(1)}, bf16[64,1464]{1,0:T(8,128)(2,1)S(1)}, u32[]{:S(2)}, u32[]{:S(2)}) collective-permute-start(bf16[64,1464]{1,0:T(8,128)(2,1)S(1)} %shard_map.64.refs_0_), channel_id=1, source_target_pairs={{0,1},{1,0},{2,3},{3,2},{4,5},{5,4},{6,7},{7,6},{8,9},{9,8},{10,11... | collective-permute-start | bytes 562184 | tf_op jit(solution)/shard_map/ppermute | solution.py:297
  11.1 6.4 %collective-permute-start.8 = (bf16[64,1464]{1,0:T(8,128)(2,1)S(1)}, bf16[64,1464]{1,0:T(8,128)(2,1)S(1)}, u32[]{:S(2)}, u32[]{:S(2)}) collective-permute-start(bf16[64,1464]{1,0:T(8,128)(2,1)S(1)} %collective-permute-done.refs_0_), channel_id=1, source_target_pairs={{0,1},{1,0},{2,3},{3,2},{4,5},{5,4},{6,7},{7,6},{8,9},{9,8},{10,11... | collective-permute-start | bytes 562184 | tf_op jit(solution)/shard_map/ppermute | solution.py:303
  11.6 6.4 %collective-permute-start.9 = (bf16[64,1464]{1,0:T(8,128)(2,1)S(1)}, bf16[64,1464]{1,0:T(8,128)(2,1)S(1)}, u32[]{:S(2)}, u32[]{:S(2)}) collective-permute-start(bf16[64,1464]{1,0:T(8,128)(2,1)S(1)} %collective-permute-done.3.refs_1_), channel_id=1, source_target_pairs={{0,1},{1,0},{2,3},{3,2},{4,5},{5,4},{6,7},{7,6},{8,9},{9,8},{10,11... | collective-permute-start | bytes 562184 | tf_op jit(solution)/shard_map/ppermute | solution.py:303
  15.4 6.9 %collective-permute-start.6 = (bf16[64,1464]{1,0:T(8,128)(2,1)S(1)}, bf16[64,1464]{1,0:T(8,128)(2,1)S(1)}, u32[]{:S(2)}, u32[]{:S(2)}) collective-permute-start(bf16[64,1464]{1,0:T(8,128)(2,1)S(1)} %collective-permute-done.1.refs_0_), channel_id=1, source_target_pairs={{0,4},{4,8},{8,12},{12,14},{14,10},{10,6},{6,2},{2,0},{1,5},{5,9},... | collective-permute-start | bytes 562184 | tf_op jit(solution)/shard_map/ppermute | solution.py:301
  17.1 6.7 %collective-permute-start.10 = (bf16[64,1464]{1,0:T(8,128)(2,1)S(1)}, bf16[64,1464]{1,0:T(8,128)(2,1)S(1)}, u32[]{:S(2)}, u32[]{:S(2)}) collective-permute-start(bf16[64,1464]{1,0:T(8,128)(2,1)S(1)} %collective-permute-done.4.refs_1_), channel_id=1, source_target_pairs={{4,0},{8,4},{12,8},{14,12},{10,14},{6,10},{2,6},{0,2},{5,1},{9,5},... | collective-permute-start | bytes 562184 | tf_op jit(solution)/shard_map/ppermute | solution.py:302
  17.4 6.9 %collective-permute-start.2 = (bf16[64,1464]{1,0:T(8,128)(2,1)S(1)}, bf16[64,1464]{1,0:T(8,128)(2,1)S(1)}, u32[]{:S(2)}, u32[]{:S(2)}) collective-permute-start(bf16[64,1464]{1,0:T(8,128)(2,1)S(1)} %collective-permute-done.1.refs_0_), channel_id=1, source_target_pairs={{0,1},{1,0},{2,3},{3,2},{4,5},{5,4},{6,7},{7,6},{8,9},{9,8},{10,11... | collective-permute-start | bytes 562184 | tf_op jit(solution)/shard_map/ppermute | solution.py:303
  17.4 8.6 %collective-permute-start.5 = (bf16[64,1464]{1,0:T(8,128)(2,1)S(1)}, bf16[64,1464]{1,0:T(8,128)(2,1)S(1)}, u32[]{:S(2)}, u32[]{:S(2)}) collective-permute-start(bf16[64,1464]{1,0:T(8,128)(2,1)S(1)} %collective-permute-done.4.refs_1_), channel_id=1, source_target_pairs={{0,1},{1,0},{2,3},{3,2},{4,5},{5,4},{6,7},{7,6},{8,9},{9,8},{10,11... | collective-permute-start | bytes 562184 | tf_op jit(solution)/shard_map/ppermute | solution.py:303
  22.3 4.2 %collective-permute-start.11 = (bf16[64,1464]{1,0:T(8,128)(2,1)S(1)}, bf16[64,1464]{1,0:T(8,128)(2,1)S(1)}, u32[]{:S(2)}, u32[]{:S(2)}) collective-permute-start(bf16[64,1464]{1,0:T(8,128)(2,1)S(1)} %collective-permute-done.6.refs_0_), channel_id=1, source_target_pairs={{0,1},{1,0},{2,3},{3,2},{4,5},{5,4},{6,7},{7,6},{8,9},{9,8},{10,11... | collective-permute-start | bytes 562184 | tf_op jit(solution)/shard_map/ppermute | solution.py:312
  23.8 2.6 %collective-permute-start.12 = (bf16[64,1464]{1,0:T(8,128)(2,1)S(1)}, bf16[64,1464]{1,0:T(8,128)(2,1)S(1)}, u32[]{:S(2)}, u32[]{:S(2)}) collective-permute-start(bf16[64,1464]{1,0:T(8,128)(2,1)S(1)} %collective-permute-done.10.refs_1_), channel_id=1, source_target_pairs={{0,1},{1,0},{2,3},{3,2},{4,5},{5,4},{6,7},{7,6},{8,9},{9,8},{10,11... | collective-permute-start | bytes 562184 | tf_op jit(solution)/shard_map/ppermute | solution.py:312
  23.8 10.5 %collective-permute-start.22 = (bf16[128,1440]{1,0:T(8,128)(2,1)S(1)}, bf16[128,1440]{1,0:T(8,128)(2,1)S(1)}, u32[]{:S(2)}, u32[]{:S(2)}) collective-permute-start(bf16[128,1440]{1,0:T(8,128)(2,1)S(1)} %get-tuple-element.59), channel_id=1, source_target_pairs={{0,1},{1,0},{2,3},{3,2},{4,5},{5,4},{6,7},{7,6},{8,9},{9,8},{10,11... | collective-permute-start | bytes 1105928 | tf_op jit(solution)/shard_map/ppermute | solution.py:284
  24.4 4.8 %collective-permute-start.14 = (bf16[32,1464]{1,0:T(8,128)(2,1)S(1)}, bf16[32,1464]{1,0:T(8,128)(2,1)S(1)}, u32[]{:S(2)}, u32[]{:S(2)}) collective-permute-start(bf16[32,1464]{1,0:T(8,128)(2,1)S(1)} %slice.56), channel_id=1, source_target_pairs={{0,4},{4,8},{8,12},{12,14},{14,10},{10,6},{6,2},{2,0},{1,5},{5,9},... | collective-permute-start | bytes 281096 | tf_op jit(solution)/shard_map/ppermute | solution.py:310
  26.0 4.6 %collective-permute-start.15 = (bf16[32,1464]{1,0:T(8,128)(2,1)S(1)}, bf16[32,1464]{1,0:T(8,128)(2,1)S(1)}, u32[]{:S(2)}, u32[]{:S(2)}) collective-permute-start(bf16[32,1464]{1,0:T(8,128)(2,1)S(1)} %slice.57), channel_id=1, source_target_pairs={{4,0},{8,4},{12,8},{14,12},{10,14},{6,10},{2,6},{0,2},{5,1},{9,5},... | collective-permute-start | bytes 281096 | tf_op jit(solution)/shard_map/ppermute | solution.py:311
  30.6 1.8 %collective-permute-start.16 = (bf16[32,1464]{1,0:T(8,128)(2,1)S(1)}, bf16[32,1464]{1,0:T(8,128)(2,1)S(1)}, u32[]{:S(2)}, u32[]{:S(2)}) collective-permute-start(bf16[32,1464]{1,0:T(8,128)(2,1)S(1)} %collective-permute-done.14.refs_0_), channel_id=1, source_target_pairs={{0,1},{1,0},{2,3},{3,2},{4,5},{5,4},{6,7},{7,6},{8,9},{9,8},{10,11... | collective-permute-start | bytes 281096 | tf_op jit(solution)/shard_map/ppermute | solution.py:242
  30.6 1.9 %collective-permute-start.17 = (bf16[32,1464]{1,0:T(8,128)(2,1)S(1)}, bf16[32,1464]{1,0:T(8,128)(2,1)S(1)}, u32[]{:S(2)}, u32[]{:S(2)}) collective-permute-start(bf16[32,1464]{1,0:T(8,128)(2,1)S(1)} %collective-permute-done.15.refs_1_), channel_id=1, source_target_pairs={{0,1},{1,0},{2,3},{3,2},{4,5},{5,4},{6,7},{7,6},{8,9},{9,8},{10,11... | collective-permute-start | bytes 281096 | tf_op jit(solution)/shard_map/ppermute | solution.py:242
  34.2 1.6 %collective-permute-start.18 = (bf16[64,1440]{1,0:T(8,128)(2,1)S(1)}, bf16[64,1440]{1,0:T(8,128)(2,1)S(1)}, u32[]{:S(2)}, u32[]{:S(2)}) collective-permute-start(bf16[64,1440]{1,0:T(8,128)(2,1)S(1)} %get-tuple-element.71), channel_id=1, source_target_pairs={{0,1},{1,0},{2,3},{3,2},{4,5},{5,4},{6,7},{7,6},{8,9},{9,8},{10,11... | collective-permute-start | bytes 552968 | tf_op jit(solution)/shard_map/ppermute | solution.py:255
  34.3 6.4 %collective-permute-start.13 = (bf16[128,1440]{1,0:T(8,128)(2,1)S(1)}, bf16[128,1440]{1,0:T(8,128)(2,1)S(1)}, u32[]{:S(2)}, u32[]{:S(2)}) collective-permute-start(bf16[128,1440]{1,0:T(8,128)(2,1)S(1)} %get-tuple-element.63), channel_id=1, source_target_pairs={{0,1},{1,0},{2,3},{3,2},{4,5},{5,4},{6,7},{7,6},{8,9},{9,8},{10,11... | collective-permute-start | bytes 1105928 | tf_op jit(solution)/shard_map/ppermute | solution.py:284
  35.9 6.8 %collective-permute-start.20 = (bf16[32,1440]{1,0:T(8,128)(2,1)S(1)}, bf16[32,1440]{1,0:T(8,128)(2,1)S(1)}, u32[]{:S(2)}, u32[]{:S(2)}) collective-permute-start(bf16[32,1440]{1,0:T(8,128)(2,1)S(1)} %get-tuple-element.89), channel_id=1, source_target_pairs={{4,0},{8,4},{12,8},{14,12},{10,14},{6,10},{2,6},{0,2},{5,1},{9,5},... | collective-permute-start | bytes 276488 | tf_op jit(solution)/shard_map/ppermute | solution.py:323
  36.4 4.6 %collective-permute-start.19 = (bf16[32,1440]{1,0:T(8,128)(2,1)S(1)}, bf16[32,1440]{1,0:T(8,128)(2,1)S(1)}, u32[]{:S(2)}, u32[]{:S(2)}) collective-permute-start(bf16[32,1440]{1,0:T(8,128)(2,1)S(1)} %get-tuple-element.90), channel_id=1, source_target_pairs={{0,4},{4,8},{8,12},{12,14},{14,10},{10,6},{6,2},{2,0},{1,5},{5,9},... | collective-permute-start | bytes 276488 | tf_op jit(solution)/shard_map/ppermute | solution.py:322
  40.7 5.3 %collective-permute-start.23 = (bf16[128,1440]{1,0:T(8,128)(2,1)S(1)}, bf16[128,1440]{1,0:T(8,128)(2,1)S(1)}, u32[]{:S(2)}, u32[]{:S(2)}) collective-permute-start(bf16[128,1440]{1,0:T(8,128)(2,1)S(1)} %get-tuple-element.75), channel_id=1, source_target_pairs={{0,1},{1,0},{2,3},{3,2},{4,5},{5,4},{6,7},{7,6},{8,9},{9,8},{10,11... | collective-permute-start | bytes 1105928 | tf_op jit(solution)/shard_map/ppermute | solution.py:284
  41.1 7.1 %collective-permute-start.24 = (bf16[64,1440]{1,0:T(8,128)(2,1)S(1)}, bf16[64,1440]{1,0:T(8,128)(2,1)S(1)}, u32[]{:S(2)}, u32[]{:S(2)}) collective-permute-start(bf16[64,1440]{1,0:T(8,128)(2,1)S(1)} %add_convert_fusion.6), channel_id=1, source_target_pairs={{0,4},{4,8},{8,12},{12,14},{14,10},{10,6},{6,2},{2,0},{1,5},{5,9},... | collective-permute-start | bytes 552968 | tf_op jit(solution)/shard_map/ppermute | solution.py:322
  42.8 7.1 %collective-permute-start.27 = (bf16[64,1440]{1,0:T(8,128)(2,1)S(1)}, bf16[64,1440]{1,0:T(8,128)(2,1)S(1)}, u32[]{:S(2)}, u32[]{:S(2)}) collective-permute-start(bf16[64,1440]{1,0:T(8,128)(2,1)S(1)} %add_convert_fusion.5), channel_id=1, source_target_pairs={{4,0},{8,4},{12,8},{14,12},{10,14},{6,10},{2,6},{0,2},{5,1},{9,5},... | collective-permute-start | bytes 552968 | tf_op jit(solution)/shard_map/ppermute | solution.py:323
  46.0 10.9 %collective-permute-start.21 = (bf16[64,1440]{1,0:T(8,128)(2,1)S(1)}, bf16[64,1440]{1,0:T(8,128)(2,1)S(1)}, u32[]{:S(2)}, u32[]{:S(2)}) collective-permute-start(bf16[64,1440]{1,0:T(8,128)(2,1)S(1)} %get-tuple-element.80), channel_id=1, source_target_pairs={{0,1},{1,0},{2,3},{3,2},{4,5},{5,4},{6,7},{7,6},{8,9},{9,8},{10,11... | collective-permute-start | bytes 552968 | tf_op jit(solution)/shard_map/ppermute | solution.py:284
  48.3 6.3 %collective-permute-start.25 = (bf16[64,1440]{1,0:T(8,128)(2,1)S(1)}, bf16[64,1440]{1,0:T(8,128)(2,1)S(1)}, u32[]{:S(2)}, u32[]{:S(2)}) collective-permute-start(bf16[64,1440]{1,0:T(8,128)(2,1)S(1)} %add_convert_fusion.4), channel_id=1, source_target_pairs={{0,4},{4,8},{8,12},{12,14},{14,10},{10,6},{6,2},{2,0},{1,5},{5,9},... | collective-permute-start | bytes 552968 | tf_op jit(solution)/shard_map/ppermute | solution.py:322
  50.0 6.3 %collective-permute-start.28 = (bf16[64,1440]{1,0:T(8,128)(2,1)S(1)}, bf16[64,1440]{1,0:T(8,128)(2,1)S(1)}, u32[]{:S(2)}, u32[]{:S(2)}) collective-permute-start(bf16[64,1440]{1,0:T(8,128)(2,1)S(1)} %add_convert_fusion.2), channel_id=1, source_target_pairs={{4,0},{8,4},{12,8},{14,12},{10,14},{6,10},{2,6},{0,2},{5,1},{9,5},... | collective-permute-start | bytes 552968 | tf_op jit(solution)/shard_map/ppermute | solution.py:323
  54.7 5.7 %collective-permute-start.26 = (bf16[64,1440]{1,0:T(8,128)(2,1)S(1)}, bf16[64,1440]{1,0:T(8,128)(2,1)S(1)}, u32[]{:S(2)}, u32[]{:S(2)}) collective-permute-start(bf16[64,1440]{1,0:T(8,128)(2,1)S(1)} %add_convert_fusion.3), channel_id=1, source_target_pairs={{0,4},{4,8},{8,12},{12,14},{14,10},{10,6},{6,2},{2,0},{1,5},{5,9},... | collective-permute-start | bytes 552968 | tf_op jit(solution)/shard_map/ppermute | solution.py:322
  56.4 5.7 %collective-permute-start.29 = (bf16[64,1440]{1,0:T(8,128)(2,1)S(1)}, bf16[64,1440]{1,0:T(8,128)(2,1)S(1)}, u32[]{:S(2)}, u32[]{:S(2)}) collective-permute-start(bf16[64,1440]{1,0:T(8,128)(2,1)S(1)} %add_convert_fusion.1), channel_id=1, source_target_pairs={{4,0},{8,4},{12,8},{14,12},{10,14},{6,10},{2,6},{0,2},{5,1},{9,5},... | collective-permute-start | bytes 552968 | tf_op jit(solution)/shard_map/ppermute | solution.py:323

commit v7 on v6

--- a/solution.py
+++ b/solution.py
@@ -155,28 +155,30 @@
     return weights
 
 
-def lower(hidden, w, weights, out):
+def lower(hidden, w, weights, *outs):
     value = jnp.dot(hidden, w[...], preferred_element_type=jnp.float32)
-    start = 0
+    start, rows = 0, outs[0].shape[0]
     for weight in weights:
-        span = slice(start, start + weight.shape[0])
-        start = span.stop
-        out[span] = (value[span] * weight).astype(jnp.bfloat16)
+        stop = start + weight.shape[0]
+        out, at = outs[start // rows], start % rows
+        out[at : at + weight.shape[0]] = (value[start:stop] * weight).astype(jnp.bfloat16)
+        start = stop
 
 
 def expert_kernel(n_blocks, n_experts, place, *refs):
     own, across = refs[:n_blocks], refs[n_blocks : 2 * n_blocks]
-    w_gate, w_up, down_mine, down_theirs, mine, theirs, x_own, x_across = refs[2 * n_blocks :]
+    w_gate, w_up, down_mine, down_theirs, *outs, x_own, x_across = refs[2 * n_blocks :]
     lane, expert = place[0], place[1]
-    half = mine.shape[1]
+    half = x_own.shape[1]
     gather_rows(own, x_own, half)
     gather_rows(across, x_across, half)
     gated = project(x_own, lane, w_gate) + project(x_across, 1 - lane, w_gate)
     lifted = project(x_own, lane, w_up) + project(x_across, 1 - lane, w_up)
     hidden = activate(gated, lifted)
     weights = gate_weights(own, half, expert, n_experts)
-    lower(hidden, down_theirs, weights, theirs)
-    lower(hidden, down_mine, weights, mine)
+    mine, theirs = outs[: len(outs) // 2], outs[len(outs) // 2 :]
+    lower(hidden, down_theirs, weights, *theirs)
+    lower(hidden, down_mine, weights, *mine)
 
 
 def first_kernel(n_blocks, place, *refs):
@@ -223,15 +225,16 @@
 def run_expert(place, own, across, weights, n_experts):
     width, hidden = weights[0].shape
     half = width // 2
-    rows = sum(a.shape[0] for a in own)
-    return call(
+    rows, pairs = sum(a.shape[0] for a in own), max(1, len(own) // 2)
+    outs = call(
         functools.partial(expert_kernel, len(own), n_experts),
         place,
         (*own, *across, *weights),
-        [in_vmem((rows, half))] * 2,
+        [in_vmem((rows // pairs, half))] * (2 * pairs),
         [pltpu.VMEM((padded(rows), half), jnp.bfloat16)] * 2,
         6 * padded(rows) * hidden * width,
     )
+    return outs[:pairs], outs[pairs:]
 
 
 def run_expert_in_stages(place, own, swap, weights, n_experts):
@@ -281,16 +284,18 @@
     def run(keys, wait_for=None):
         at = place if wait_for is None else after(place, wait_for)
         mine, theirs = run_expert(at, [came[k] for k in keys], [across[k] for k in keys], weights, n)
-        keep(keys, mine, swap(theirs))
-        return theirs
+        for i, pair in enumerate(zip(mine, theirs)):
+            keep(keys[2 * i : 2 * i + 2], pair[0], swap(pair[1]))
+        return theirs[0]
 
     def keep(keys, mine, theirs):
+        pairs = ((mine, theirs), lax.optimization_barrier((mine, theirs)))
         start = 0
-        for k in keys:
+        for i, k in enumerate(keys):
+            mine, theirs = pairs[i % 2]
             span = slice(start, start + came[k].shape[0])
             start = span.stop
             value[k] = mine[span].astype(jnp.float32) + theirs[span].astype(jnp.float32)
-            mine, theirs = lax.optimization_barrier((mine, theirs))
 
     came[1] = lax.ppermute(packed, "ep", ahead)
     came[-1] = lax.ppermute(packed, "ep", back)
@@ -304,13 +309,11 @@
         if k == 2:
             weights += halve_weights(after(place, came[1]), w_down[0])
             done = weights[-1]
-        else:
-            done = run([k - 2, 2 - k], across[0] if k == 3 else None)
     came[far - 1], came[1 - far] = after(came[far - 1], done), after(came[1 - far], done)
     came["low"] = lax.ppermute(came[far - 1][: rows // 2], "ep", ahead)
     came["high"] = lax.ppermute(came[1 - far][rows // 2 :], "ep", back)
     across[far - 1], across[1 - far] = swap(came[far - 1]), swap(came[1 - far])
-    done = run([far - 1, 1 - far], (across[far - 2], across[2 - far]))
+    done = run([far - 1, 1 - far], [across[k] for k in range(2 - far, far - 1)])
     came["low"], came["high"] = after((came["low"], came["high"]), done)
     far_keys = ["low", "high"]
     keep(far_keys, *run_expert_in_stages(place, [came[k] for k in far_keys], swap, weights, n))
@@ -321,15 +324,17 @@
     for k in range(far - 1, -1, -1):
         behind = lax.ppermute(to_ahead, "ep", ahead)
         front = lax.ppermute(to_back, "ep", back)
-        if k >= far - 2:
-            done = run([far - 2, 2 - far] if k == far - 1 else [0], (to_ahead, to_back))
+        if k == far - 1:
+            done = run([j for i in range(1, far - 1) for j in (i, -i)], (to_ahead, to_back))
+        elif k == 1:
+            done = run([0], (to_ahead, to_back))
         behind, front = behind.astype(jnp.float32), front.astype(jnp.float32)
         if k == far - 1:
             behind, front = jnp.pad(behind, pad_low), jnp.pad(front, pad_high)
         if k:
             to_ahead = (value[-k] + behind).astype(jnp.bfloat16)
             to_back = (value[k] + front).astype(jnp.bfloat16)
-        if k >= far - 2:
+        if k in (far - 1, 1):
             to_ahead, to_back = after(to_ahead, done), after(to_back, done)
     return (value[0] + behind + front).astype(jnp.bfloat16)
 

time: 63 us -> 64.2 us (1.019)
  waiting for transfers between devices: 17 us -> 19.1 us
  Pallas kernels: 23.8 us -> 22.9 us
    ppermute x4, waiting for transfers between devices: 9.99 us -> 4.16 us  [ring_body(): behind = lax.ppermute(to_ahead, 'ep', ahead)]
    ppermute x4, waiting for transfers between devices: 1.72 us -> 7.16 us  [ring_body(): front = lax.ppermute(to_back, 'ep', back)]
    ppermute x2, waiting for transfers between devices: 2.24 us -> 4.32 us  [ring_body(): came[k] = lax.ppermute(came[k - 1], 'ep', ahead)]
    pallas_call x7 -> x6, Pallas kernels: 14.9 us -> 13.9 us  [call(): pl.pallas_call(kernel, out_shape=out_shape, in_specs=[pl.BlockSpec(memory...]
  transfers between devices with their start and end apart: 30 -> 30, of which waited for: 9 -> 10; matrix products, arithmetic and copies ran while one was open for 1% -> 1% of each run, Pallas kernels for 36% -> 31%
where the time goes in v7:
time: 64.2 us; the launch traced here: 64 us
  Pallas kernels  22.9 us (36%)
  starting transfers between devices  20.5 us (32%)
  waiting for transfers between devices  19.1 us (30%)
  other arithmetic  1.32 us (2%)
    pallas_call x6, Pallas kernels, call(): pl.pallas_call(kernel, out_shape=out_shape, in_specs=[pl.BlockSpec(memory...  13.9 us
    ppermute x4, waiting for transfers between devices, ring_body(): front = lax.ppermute(to_back, 'ep', back)  7.16 us
    ppermute x4, starting transfers between devices, ring_body(): behind = lax.ppermute(to_ahead, 'ep', ahead)  6.48 us
    pallas_call x1, Pallas kernels, turn_weights(): pl.pallas_call(turn_kernel, out_shape=[in_vmem((width, hidden))] * 2, in_...  4.79 us
    ppermute x2, waiting for transfers between devices, ring_body(): came[k] = lax.ppermute(came[k - 1], 'ep', ahead)  4.32 us
    ppermute x4, waiting for transfers between devices, ring_body(): behind = lax.ppermute(to_ahead, 'ep', ahead)  4.16 us
    ppermute x2, starting transfers between devices, ring_body(): came[k] = lax.ppermute(came[k - 1], 'ep', ahead)  3.82 us
    pallas_call x1, Pallas kernels, halve_weights(): pl.pallas_call(halve_kernel, out_shape=[in_vmem((hidden, width // 2))] *...  3.13 us
  transfers between devices with their start and end apart: 30, of which 10 were waited for; matrix products, arithmetic and copies ran while one was open for 1% of the time, Pallas kernels for 31%

profile of v7, /device:TPU:0, one launch (start us, length us, event | category | flops | bytes accessed | tf_op | source)
XLA Modules:
  0.0 64.0 jit_solution(3095819264052263440)
XLA Ops:
  0.0 1.0 %shard_map.64.refs_0_ = bf16[64,1464]{1,0:T(8,128)(2,1)S(1)} custom-call(bf16[64,1440]{1,0:T(8,128)(2,1)} %tokens_in.1, s32[4,64]{1,0:T(4,128)} %bitcast.14, f32[4,64]{1,0:T(4,128)} %bitcast.15), custom_call_target="tpu_custom_call" | custom-call | tf_op jit(solution)/shard_map/pallas_call | solution.py:53
  1.0 3.1 %collective-permute-start = (bf16[64,1464]{1,0:T(8,128)(2,1)S(1)}, bf16[64,1464]{1,0:T(8,128)(2,1)S(1)}, u32[]{:S(2)}, u32[]{:S(2)}) collective-permute-start(bf16[64,1464]{1,0:T(8,128)(2,1)S(1)} %shard_map.64.refs_0_), channel_id=1, source_target_pairs={{0,4},{4,8},{8,12},{12,14},{14,10},{10,6},{6,2},{2,0},{1,5},{5,9},... | collective-permute-start | bytes 562184 | tf_op jit(solution)/shard_map/ppermute | solution.py:300
  4.1 0.0 collective-permute-start.4
  4.1 0.1 pad_add_fusion.after_this.place
  4.2 4.8 %shard_map.65 = (bf16[2880,720]{1,0:T(8,128)(2,1)S(1)}, bf16[2880,720]{1,0:T(8,128)(2,1)S(1)}) custom-call(s32[2]{0:T(128)S(1)} %pad_add_fusion.after_this.place, bf16[720,2880]{1,0:T(8,128)(2,1)} %bitcast.11, bf16[720,2880]{1,0:T(8,128)(2,1)} %bitcast.12), custom_call_target="tpu_custom_call" | custom-call | bytes 16588800 | tf_op jit(solution)/shard_map/pallas_call | solution.py:83
  9.0 0.0 collective-permute-done.refs_0_
  9.0 2.1 %collective-permute-start.1 = (bf16[64,1464]{1,0:T(8,128)(2,1)S(1)}, bf16[64,1464]{1,0:T(8,128)(2,1)S(1)}, u32[]{:S(2)}, u32[]{:S(2)}) collective-permute-start(bf16[64,1464]{1,0:T(8,128)(2,1)S(1)} %collective-permute-done.refs_0_), channel_id=1, source_target_pairs={{0,4},{4,8},{8,12},{12,14},{14,10},{10,6},{6,2},{2,0},{1,5},{5,9},... | collective-permute-start | bytes 562184 | tf_op jit(solution)/shard_map/ppermute | solution.py:306
  11.1 0.0 collective-permute-start.5
  11.1 3.1 %shard_map.66 = (bf16[720,1440]{1,0:T(8,128)(2,1)S(1)}, bf16[720,1440]{1,0:T(8,128)(2,1)S(1)}) custom-call(s32[2]{0:T(128)S(1)} %pad_add_fusion.after_this.place, bf16[720,2880]{1,0:T(8,128)(2,1)} %bitcast.13), custom_call_target="tpu_custom_call" | custom-call | bytes 16588800 | tf_op jit(solution)/shard_map/pallas_call | solution.py:120
  14.2 1.2 %collective-permute-done.1.refs_2_ = bf16[64,1464]{1,0:T(8,128)(2,1)S(1)} collective-permute-done((bf16[64,1464]{1,0:T(8,128)(2,1)S(1)}, bf16[64,1464]{1,0:T(8,128)(2,1)S(1)}, u32[]{:S(2)}, u32[]{:S(2)}) %collective-permute-start.1) | collective-permute-done | bytes 187424 | tf_op jit(solution)/shard_map/ppermute | solution.py:306
  15.4 1.7 %collective-permute-start.2 = (bf16[64,1464]{1,0:T(8,128)(2,1)S(1)}, bf16[64,1464]{1,0:T(8,128)(2,1)S(1)}, u32[]{:S(2)}, u32[]{:S(2)}) collective-permute-start(bf16[64,1464]{1,0:T(8,128)(2,1)S(1)} %collective-permute-done.1.refs_2_), channel_id=1, source_target_pairs={{0,4},{4,8},{8,12},{12,14},{14,10},{10,6},{6,2},{2,0},{1,5},{5,9},... | collective-permute-start | bytes 562184 | tf_op jit(solution)/shard_map/ppermute | solution.py:306
  17.1 0.0 collective-permute-done.5.refs_3_
  17.1 0.3 collective-permute-start.6
  17.4 0.5 collective-permute-start.11
  17.9 0.0 collective-permute-start.9
  17.9 3.1 %collective-permute-done.2.refs_0_ = bf16[64,1464]{1,0:T(8,128)(2,1)S(1)} collective-permute-done((bf16[64,1464]{1,0:T(8,128)(2,1)S(1)}, bf16[64,1464]{1,0:T(8,128)(2,1)S(1)}, u32[]{:S(2)}, u32[]{:S(2)}) %collective-permute-start.2) | collective-permute-done | bytes 187424 | tf_op jit(solution)/shard_map/ppermute | solution.py:306
  21.1 1.7 %collective-permute-done.6.refs_1_ = bf16[64,1464]{1,0:T(8,128)(2,1)S(1)} collective-permute-done((bf16[64,1464]{1,0:T(8,128)(2,1)S(1)}, bf16[64,1464]{1,0:T(8,128)(2,1)S(1)}, u32[]{:S(2)}, u32[]{:S(2)}) %collective-permute-start.6) | collective-permute-done | bytes 187424 | tf_op jit(solution)/shard_map/ppermute | solution.py:307
  22.8 0.5 collective-permute-start.13
  23.3 0.1 collective-permute-start.14
  23.4 0.0 collective-permute-done.9.refs_5_
  23.4 1.6 %collective-permute-start.3 = (bf16[32,1464]{1,0:T(8,128)(2,1)S(1)}, bf16[32,1464]{1,0:T(8,128)(2,1)S(1)}, u32[]{:S(2)}, u32[]{:S(2)}) collective-permute-start(bf16[32,1464]{1,0:T(8,128)(2,1)S(1)} %slice.54), channel_id=1, source_target_pairs={{0,4},{4,8},{8,12},{12,14},{14,10},{10,6},{6,2},{2,0},{1,5},{5,9},... | collective-permute-start | bytes 281096 | tf_op jit(solution)/shard_map/ppermute | solution.py:313
  25.1 0.5 collective-permute-start.7
  25.5 2.7 %shard_map.67 = (bf16[128,1440]{1,0:T(8,128)(2,1)S(1)}, bf16[128,1440]{1,0:T(8,128)(2,1)S(1)}) custom-call(s32[2]{0:T(128)S(1)} %pad_add_fusion.after_this.place, bf16[64,1464]{1,0:T(8,128)(2,1)S(1)} %collective-permute-done.2.refs_0_, bf16[64,1464]{1,0:T(8,128)(2,1)S(1)} %collective-permute-done.6.refs_1_, ...), custom_call_target="tpu_custom_call" | custom-call | flops 1592524800 | bytes 12441600 | tf_op jit(solution)/shard_map/pallas_call | solution.py:210
  28.2 0.4 collective-permute-done.3.refs_0_
  28.6 1.3 %collective-permute-done.7.refs_1_ = bf16[32,1464]{1,0:T(8,128)(2,1)S(1)} collective-permute-done((bf16[32,1464]{1,0:T(8,128)(2,1)S(1)}, bf16[32,1464]{1,0:T(8,128)(2,1)S(1)}, u32[]{:S(2)}, u32[]{:S(2)}) %collective-permute-start.7) | collective-permute-done | bytes 93728 | tf_op jit(solution)/shard_map/ppermute | solution.py:314
  29.9 0.0 collective-permute-start.15
  29.9 0.5 collective-permute-start.16
  30.4 1.3 %shard_map.68 = (f32[128,720]{1,0:T(8,128)S(1)}, f32[128,720]{1,0:T(8,128)S(1)}) custom-call(s32[2]{0:T(128)S(1)} %pad_add_fusion.after_this.place, bf16[32,1464]{1,0:T(8,128)(2,1)S(1)} %collective-permute-done.3.refs_0_, bf16[32,1464]{1,0:T(8,128)(2,1)S(1)} %collective-permute-done.7.refs_1_, ...), custom_call_target="tpu_custom_call" | custom-call | flops 530841600 | bytes 4147200 | tf_op jit(solution)/shard_map/pallas_call | solution.py:210
  31.8 0.0 collective-permute-done.16.refs_3_
  31.8 1.8 %shard_map.69 = (bf16[128,720]{1,0:T(8,128)(2,1)S(1)}, bf16[64,1440]{1,0:T(8,128)(2,1)S(1)}) custom-call(s32[2]{0:T(128)S(1)} %pad_add_fusion.after_this.place, bf16[32,1464]{1,0:T(8,128)(2,1)S(1)} %collective-permute-done.3.refs_0_, bf16[32,1464]{1,0:T(8,128)(2,1)S(1)} %collective-permute-done.7.refs_1_, ...), custom_call_target="tpu_custom_call" | custom-call | flops 796262400 | bytes 6220800 | tf_op jit(solution)/shard_map/pallas_call | solution.py:210
  33.5 0.1 collective-permute-start.17
  33.6 0.5 collective-permute-start.19
  34.1 1.0 %shard_map.70 = bf16[64,1440]{1,0:T(8,128)(2,1)S(1)} custom-call(s32[2]{0:T(128)S(1)} %pad_add_fusion.after_this.place, bf16[32,1464]{1,0:T(8,128)(2,1)S(1)} %collective-permute-done.3.refs_0_, bf16[32,1464]{1,0:T(8,128)(2,1)S(1)} %collective-permute-done.7.refs_1_, bf16[128,720]{1,0:T(8,128)(2,1)S(1)} %get-tuple-element.64.refs_2_, ...), custom_call_target="tpu_custom_call" | custom-call | flops 265420800 | bytes 2073600 | tf_op jit(solution)/shard_map/pallas_call | solution.py:210
  35.1 0.0 collective-permute-done.17
  35.2 0.5 collective-permute-start.22
  35.7 1.6 %collective-permute-start.20 = (bf16[32,1440]{1,0:T(8,128)(2,1)S(1)}, bf16[32,1440]{1,0:T(8,128)(2,1)S(1)}, u32[]{:S(2)}, u32[]{:S(2)}) collective-permute-start(bf16[32,1440]{1,0:T(8,128)(2,1)S(1)} %get-tuple-element.88), channel_id=1, source_target_pairs={{0,4},{4,8},{8,12},{12,14},{14,10},{10,6},{6,2},{2,0},{1,5},{5,9},... | collective-permute-start | bytes 276488 | tf_op jit(solution)/shard_map/ppermute | solution.py:325
  37.3 4.5 %shard_map.71 = (bf16[128,1440]{1,0:T(8,128)(2,1)S(1)}, bf16[128,1440]{1,0:T(8,128)(2,1)S(1)}, bf16[128,1440]{1,0:T(8,128)(2,1)S(1)}, bf16[128,1440]{1,0:T(8,128)(2,1)S(1)}) custom-call(s32[2]{0:T(128)S(1)} %pad_add_fusion.after_this.place, bf16[64,1464]{1,0:T(8,128)(2,1)S(1)} %collective-permute-done.refs_0_, ...), custom_call_target="tpu_custom_call" | custom-call | flops 3185049600 | bytes 24883200 | tf_op jit(solution)/shard_map/pallas_call | solution.py:210
  41.8 0.1 collective-permute-start.18
  41.9 0.5 collective-permute-start.25
  42.4 0.0 collective-permute-done.19
  42.4 0.1 add_convert_fusion.4
  42.4 0.5 collective-permute-start.23
  42.9 0.0 collective-permute-done.20
  42.9 0.1 add_convert_fusion.6
  43.0 1.6 %collective-permute-start.21 = (bf16[64,1440]{1,0:T(8,128)(2,1)S(1)}, bf16[64,1440]{1,0:T(8,128)(2,1)S(1)}, u32[]{:S(2)}, u32[]{:S(2)}) collective-permute-start(bf16[64,1440]{1,0:T(8,128)(2,1)S(1)} %add_convert_fusion.6), channel_id=1, source_target_pairs={{0,4},{4,8},{8,12},{12,14},{14,10},{10,6},{6,2},{2,0},{1,5},{5,9},... | collective-permute-start | bytes 552968 | tf_op jit(solution)/shard_map/ppermute | solution.py:325
  44.6 4.7 %collective-permute-done.23 = bf16[64,1440]{1,0:T(8,128)(2,1)S(1)} collective-permute-done((bf16[64,1440]{1,0:T(8,128)(2,1)S(1)}, bf16[64,1440]{1,0:T(8,128)(2,1)S(1)}, u32[]{:S(2)}, u32[]{:S(2)}) %collective-permute-start.23) | collective-permute-done | bytes 184352 | tf_op jit(solution)/shard_map/ppermute | solution.py:326
  49.4 0.0 collective-permute-done.18
  49.4 0.1 add_convert_fusion.3
  49.5 0.5 collective-permute-start.28
  50.0 0.1 add_convert_fusion.5
  50.0 1.6 %collective-permute-start.26 = (bf16[64,1440]{1,0:T(8,128)(2,1)S(1)}, bf16[64,1440]{1,0:T(8,128)(2,1)S(1)}, u32[]{:S(2)}, u32[]{:S(2)}) collective-permute-start(bf16[64,1440]{1,0:T(8,128)(2,1)S(1)} %add_convert_fusion.5), channel_id=1, source_target_pairs={{0,4},{4,8},{8,12},{12,14},{14,10},{10,6},{6,2},{2,0},{1,5},{5,9},... | collective-permute-start | bytes 552968 | tf_op jit(solution)/shard_map/ppermute | solution.py:325
  51.7 2.7 %shard_map.72 = (bf16[64,1440]{1,0:T(8,128)(2,1)S(1)}, bf16[64,1440]{1,0:T(8,128)(2,1)S(1)}) custom-call(s32[2]{0:T(128)S(1)} %pad_add_fusion.after_this.place, bf16[64,1464]{1,0:T(8,128)(2,1)S(1)} %shard_map.64.refs_0_, bf16[64,1464]{1,0:T(8,128)(2,1)S(1)} %collective-permute-done.10.refs_1_, ...), custom_call_target="tpu_custom_call" | custom-call | flops 1592524800 | bytes 12441600 | tf_op jit(solution)/shard_map/pallas_call | solution.py:210
  54.3 0.1 collective-permute-start.24
  54.4 0.0 collective-permute-done.25
  54.4 1.1 %collective-permute-done.28 = bf16[64,1440]{1,0:T(8,128)(2,1)S(1)} collective-permute-done((bf16[64,1440]{1,0:T(8,128)(2,1)S(1)}, bf16[64,1440]{1,0:T(8,128)(2,1)S(1)}, u32[]{:S(2)}, u32[]{:S(2)}) %collective-permute-start.28) | collective-permute-done | bytes 184352 | tf_op jit(solution)/shard_map/ppermute | solution.py:326
  55.6 0.1 add_convert_fusion.1
  55.6 0.2 collective-permute-done.26
  55.9 0.1 add_convert_fusion.2
  55.9 1.6 %collective-permute-start.27 = (bf16[64,1440]{1,0:T(8,128)(2,1)S(1)}, bf16[64,1440]{1,0:T(8,128)(2,1)S(1)}, u32[]{:S(2)}, u32[]{:S(2)}) collective-permute-start(bf16[64,1440]{1,0:T(8,128)(2,1)S(1)} %add_convert_fusion.2), channel_id=1, source_target_pairs={{0,4},{4,8},{8,12},{12,14},{14,10},{10,6},{6,2},{2,0},{1,5},{5,9},... | collective-permute-start | bytes 552968 | tf_op jit(solution)/shard_map/ppermute | solution.py:325
  57.6 0.4 collective-permute-start.29
  58.0 0.0 collective-permute-done.24
  58.0 3.9 %collective-permute-done.27 = bf16[64,1440]{1,0:T(8,128)(2,1)S(1)} collective-permute-done((bf16[64,1440]{1,0:T(8,128)(2,1)S(1)}, bf16[64,1440]{1,0:T(8,128)(2,1)S(1)}, u32[]{:S(2)}, u32[]{:S(2)}) %collective-permute-start.27) | collective-permute-done | bytes 184352 | tf_op jit(solution)/shard_map/ppermute | solution.py:325
  62.0 1.3 %collective-permute-done.29 = bf16[64,1440]{1,0:T(8,128)(2,1)S(1)} collective-permute-done((bf16[64,1440]{1,0:T(8,128)(2,1)S(1)}, bf16[64,1440]{1,0:T(8,128)(2,1)S(1)}, u32[]{:S(2)}, u32[]{:S(2)}) %collective-permute-start.29) | collective-permute-done | bytes 184352 | tf_op jit(solution)/shard_map/ppermute | solution.py:326
  63.3 0.8 %add_convert_fusion = bf16[64,1440]{1,0:T(8,128)(2,1)} fusion(bf16[64,1440]{1,0:T(8,128)(2,1)S(1)} %collective-permute-done.29, bf16[64,1440]{1,0:T(8,128)(2,1)S(1)} %collective-permute-done.27, bf16[64,1440]{1,0:T(8,128)(2,1)S(1)} %collective-permute-done.24, bf16[64,1440]{1,0:T(8,128)(2,1)S(1)} %get-tuple-element.80), kind=kLoop, calls=%fused_computation | loop fusion | flops 737280 | bytes 921600 | tf_op jit(solution)/shard_map/convert_element_type | solution.py:339
  (16 shorter events, 0.1 us)
Async XLA Ops:
  1.0 8.0 %collective-permute-start = (bf16[64,1464]{1,0:T(8,128)(2,1)S(1)}, bf16[64,1464]{1,0:T(8,128)(2,1)S(1)}, u32[]{:S(2)}, u32[]{:S(2)}) collective-permute-start(bf16[64,1464]{1,0:T(8,128)(2,1)S(1)} %shard_map.64.refs_0_), channel_id=1, source_target_pairs={{0,4},{4,8},{8,12},{12,14},{14,10},{10,6},{6,2},{2,0},{1,5},{5,9},... | collective-permute-start | bytes 562184 | tf_op jit(solution)/shard_map/ppermute | solution.py:300
  4.1 7.0 %collective-permute-start.4 = (bf16[64,1464]{1,0:T(8,128)(2,1)S(1)}, bf16[64,1464]{1,0:T(8,128)(2,1)S(1)}, u32[]{:S(2)}, u32[]{:S(2)}) collective-permute-start(bf16[64,1464]{1,0:T(8,128)(2,1)S(1)} %shard_map.64.refs_0_), channel_id=1, source_target_pairs={{4,0},{8,4},{12,8},{14,12},{10,14},{6,10},{2,6},{0,2},{5,1},{9,5},... | collective-permute-start | bytes 562184 | tf_op jit(solution)/shard_map/ppermute | solution.py:301
  9.0 6.4 %collective-permute-start.1 = (bf16[64,1464]{1,0:T(8,128)(2,1)S(1)}, bf16[64,1464]{1,0:T(8,128)(2,1)S(1)}, u32[]{:S(2)}, u32[]{:S(2)}) collective-permute-start(bf16[64,1464]{1,0:T(8,128)(2,1)S(1)} %collective-permute-done.refs_0_), channel_id=1, source_target_pairs={{0,4},{4,8},{8,12},{12,14},{14,10},{10,6},{6,2},{2,0},{1,5},{5,9},... | collective-permute-start | bytes 562184 | tf_op jit(solution)/shard_map/ppermute | solution.py:306
  11.1 6.1 %collective-permute-start.5 = (bf16[64,1464]{1,0:T(8,128)(2,1)S(1)}, bf16[64,1464]{1,0:T(8,128)(2,1)S(1)}, u32[]{:S(2)}, u32[]{:S(2)}) collective-permute-start(bf16[64,1464]{1,0:T(8,128)(2,1)S(1)} %collective-permute-done.4.refs_1_), channel_id=1, source_target_pairs={{4,0},{8,4},{12,8},{14,12},{10,14},{6,10},{2,6},{0,2},{5,1},{9,5},... | collective-permute-start | bytes 562184 | tf_op jit(solution)/shard_map/ppermute | solution.py:307
  15.4 5.7 %collective-permute-start.2 = (bf16[64,1464]{1,0:T(8,128)(2,1)S(1)}, bf16[64,1464]{1,0:T(8,128)(2,1)S(1)}, u32[]{:S(2)}, u32[]{:S(2)}) collective-permute-start(bf16[64,1464]{1,0:T(8,128)(2,1)S(1)} %collective-permute-done.1.refs_2_), channel_id=1, source_target_pairs={{0,4},{4,8},{8,12},{12,14},{14,10},{10,6},{6,2},{2,0},{1,5},{5,9},... | collective-permute-start | bytes 562184 | tf_op jit(solution)/shard_map/ppermute | solution.py:306
  17.1 5.7 %collective-permute-start.6 = (bf16[64,1464]{1,0:T(8,128)(2,1)S(1)}, bf16[64,1464]{1,0:T(8,128)(2,1)S(1)}, u32[]{:S(2)}, u32[]{:S(2)}) collective-permute-start(bf16[64,1464]{1,0:T(8,128)(2,1)S(1)} %collective-permute-done.5.refs_3_), channel_id=1, source_target_pairs={{4,0},{8,4},{12,8},{14,12},{10,14},{6,10},{2,6},{0,2},{5,1},{9,5},... | collective-permute-start | bytes 562184 | tf_op jit(solution)/shard_map/ppermute | solution.py:307
  17.4 5.4 %collective-permute-start.10 = (bf16[64,1464]{1,0:T(8,128)(2,1)S(1)}, bf16[64,1464]{1,0:T(8,128)(2,1)S(1)}, u32[]{:S(2)}, u32[]{:S(2)}) collective-permute-start(bf16[64,1464]{1,0:T(8,128)(2,1)S(1)} %shard_map.64.refs_0_), channel_id=1, source_target_pairs={{0,1},{1,0},{2,3},{3,2},{4,5},{5,4},{6,7},{7,6},{8,9},{9,8},{10,11... | collective-permute-start | bytes 562184 | tf_op jit(solution)/shard_map/ppermute | solution.py:302
  17.4 5.9 %collective-permute-start.11 = (bf16[64,1464]{1,0:T(8,128)(2,1)S(1)}, bf16[64,1464]{1,0:T(8,128)(2,1)S(1)}, u32[]{:S(2)}, u32[]{:S(2)}) collective-permute-start(bf16[64,1464]{1,0:T(8,128)(2,1)S(1)} %collective-permute-done.refs_0_), channel_id=1, source_target_pairs={{0,1},{1,0},{2,3},{3,2},{4,5},{5,4},{6,7},{7,6},{8,9},{9,8},{10,11... | collective-permute-start | bytes 562184 | tf_op jit(solution)/shard_map/ppermute | solution.py:308
  17.9 5.5 %collective-permute-start.9 = (bf16[64,1464]{1,0:T(8,128)(2,1)S(1)}, bf16[64,1464]{1,0:T(8,128)(2,1)S(1)}, u32[]{:S(2)}, u32[]{:S(2)}) collective-permute-start(bf16[64,1464]{1,0:T(8,128)(2,1)S(1)} %collective-permute-done.4.refs_1_), channel_id=1, source_target_pairs={{0,1},{1,0},{2,3},{3,2},{4,5},{5,4},{6,7},{7,6},{8,9},{9,8},{10,11... | collective-permute-start | bytes 562184 | tf_op jit(solution)/shard_map/ppermute | solution.py:308
  21.1 4.0 %collective-permute-start.12 = (bf16[64,1464]{1,0:T(8,128)(2,1)S(1)}, bf16[64,1464]{1,0:T(8,128)(2,1)S(1)}, u32[]{:S(2)}, u32[]{:S(2)}) collective-permute-start(bf16[64,1464]{1,0:T(8,128)(2,1)S(1)} %collective-permute-done.1.refs_2_), channel_id=1, source_target_pairs={{0,1},{1,0},{2,3},{3,2},{4,5},{5,4},{6,7},{7,6},{8,9},{9,8},{10,11... | collective-permute-start | bytes 562184 | tf_op jit(solution)/shard_map/ppermute | solution.py:308
  22.8 2.3 %collective-permute-start.8 = (bf16[64,1464]{1,0:T(8,128)(2,1)S(1)}, bf16[64,1464]{1,0:T(8,128)(2,1)S(1)}, u32[]{:S(2)}, u32[]{:S(2)}) collective-permute-start(bf16[64,1464]{1,0:T(8,128)(2,1)S(1)} %collective-permute-done.5.refs_3_), channel_id=1, source_target_pairs={{0,1},{1,0},{2,3},{3,2},{4,5},{5,4},{6,7},{7,6},{8,9},{9,8},{10,11... | collective-permute-start | bytes 562184 | tf_op jit(solution)/shard_map/ppermute | solution.py:308
  22.8 2.7 %collective-permute-start.13 = (bf16[64,1464]{1,0:T(8,128)(2,1)S(1)}, bf16[64,1464]{1,0:T(8,128)(2,1)S(1)}, u32[]{:S(2)}, u32[]{:S(2)}) collective-permute-start(bf16[64,1464]{1,0:T(8,128)(2,1)S(1)} %collective-permute-done.2.refs_0_), channel_id=1, source_target_pairs={{0,1},{1,0},{2,3},{3,2},{4,5},{5,4},{6,7},{7,6},{8,9},{9,8},{10,11... | collective-permute-start | bytes 562184 | tf_op jit(solution)/shard_map/ppermute | solution.py:315
  23.3 2.2 %collective-permute-start.14 = (bf16[64,1464]{1,0:T(8,128)(2,1)S(1)}, bf16[64,1464]{1,0:T(8,128)(2,1)S(1)}, u32[]{:S(2)}, u32[]{:S(2)}) collective-permute-start(bf16[64,1464]{1,0:T(8,128)(2,1)S(1)} %collective-permute-done.6.refs_1_), channel_id=1, source_target_pairs={{0,1},{1,0},{2,3},{3,2},{4,5},{5,4},{6,7},{7,6},{8,9},{9,8},{10,11... | collective-permute-start | bytes 562184 | tf_op jit(solution)/shard_map/ppermute | solution.py:315
  23.4 5.2 %collective-permute-start.3 = (bf16[32,1464]{1,0:T(8,128)(2,1)S(1)}, bf16[32,1464]{1,0:T(8,128)(2,1)S(1)}, u32[]{:S(2)}, u32[]{:S(2)}) collective-permute-start(bf16[32,1464]{1,0:T(8,128)(2,1)S(1)} %slice.54), channel_id=1, source_target_pairs={{0,4},{4,8},{8,12},{12,14},{14,10},{10,6},{6,2},{2,0},{1,5},{5,9},... | collective-permute-start | bytes 281096 | tf_op jit(solution)/shard_map/ppermute | solution.py:313
  25.1 4.9 %collective-permute-start.7 = (bf16[32,1464]{1,0:T(8,128)(2,1)S(1)}, bf16[32,1464]{1,0:T(8,128)(2,1)S(1)}, u32[]{:S(2)}, u32[]{:S(2)}) collective-permute-start(bf16[32,1464]{1,0:T(8,128)(2,1)S(1)} %slice.55), channel_id=1, source_target_pairs={{4,0},{8,4},{12,8},{14,12},{10,14},{6,10},{2,6},{0,2},{5,1},{9,5},... | collective-permute-start | bytes 281096 | tf_op jit(solution)/shard_map/ppermute | solution.py:314
  29.9 1.8 %collective-permute-start.15 = (bf16[32,1464]{1,0:T(8,128)(2,1)S(1)}, bf16[32,1464]{1,0:T(8,128)(2,1)S(1)}, u32[]{:S(2)}, u32[]{:S(2)}) collective-permute-start(bf16[32,1464]{1,0:T(8,128)(2,1)S(1)} %collective-permute-done.3.refs_0_), channel_id=1, source_target_pairs={{0,1},{1,0},{2,3},{3,2},{4,5},{5,4},{6,7},{7,6},{8,9},{9,8},{10,11... | collective-permute-start | bytes 281096 | tf_op jit(solution)/shard_map/ppermute | solution.py:245
  29.9 1.9 %collective-permute-start.16 = (bf16[32,1464]{1,0:T(8,128)(2,1)S(1)}, bf16[32,1464]{1,0:T(8,128)(2,1)S(1)}, u32[]{:S(2)}, u32[]{:S(2)}) collective-permute-start(bf16[32,1464]{1,0:T(8,128)(2,1)S(1)} %collective-permute-done.7.refs_1_), channel_id=1, source_target_pairs={{0,1},{1,0},{2,3},{3,2},{4,5},{5,4},{6,7},{7,6},{8,9},{9,8},{10,11... | collective-permute-start | bytes 281096 | tf_op jit(solution)/shard_map/ppermute | solution.py:245
  33.5 1.6 %collective-permute-start.17 = (bf16[64,1440]{1,0:T(8,128)(2,1)S(1)}, bf16[64,1440]{1,0:T(8,128)(2,1)S(1)}, u32[]{:S(2)}, u32[]{:S(2)}) collective-permute-start(bf16[64,1440]{1,0:T(8,128)(2,1)S(1)} %get-tuple-element.65), channel_id=1, source_target_pairs={{0,1},{1,0},{2,3},{3,2},{4,5},{5,4},{6,7},{7,6},{8,9},{9,8},{10,11... | collective-permute-start | bytes 552968 | tf_op jit(solution)/shard_map/ppermute | solution.py:258
  33.6 8.8 %collective-permute-start.19 = (bf16[128,1440]{1,0:T(8,128)(2,1)S(1)}, bf16[128,1440]{1,0:T(8,128)(2,1)S(1)}, u32[]{:S(2)}, u32[]{:S(2)}) collective-permute-start(bf16[128,1440]{1,0:T(8,128)(2,1)S(1)} %get-tuple-element.59), channel_id=1, source_target_pairs={{0,1},{1,0},{2,3},{3,2},{4,5},{5,4},{6,7},{7,6},{8,9},{9,8},{10,11... | collective-permute-start | bytes 1105928 | tf_op jit(solution)/shard_map/ppermute | solution.py:288
  35.2 7.2 %collective-permute-start.22 = (bf16[32,1440]{1,0:T(8,128)(2,1)S(1)}, bf16[32,1440]{1,0:T(8,128)(2,1)S(1)}, u32[]{:S(2)}, u32[]{:S(2)}) collective-permute-start(bf16[32,1440]{1,0:T(8,128)(2,1)S(1)} %get-tuple-element.87), channel_id=1, source_target_pairs={{4,0},{8,4},{12,8},{14,12},{10,14},{6,10},{2,6},{0,2},{5,1},{9,5},... | collective-permute-start | bytes 276488 | tf_op jit(solution)/shard_map/ppermute | solution.py:326
  35.7 7.2 %collective-permute-start.20 = (bf16[32,1440]{1,0:T(8,128)(2,1)S(1)}, bf16[32,1440]{1,0:T(8,128)(2,1)S(1)}, u32[]{:S(2)}, u32[]{:S(2)}) collective-permute-start(bf16[32,1440]{1,0:T(8,128)(2,1)S(1)} %get-tuple-element.88), channel_id=1, source_target_pairs={{0,4},{4,8},{8,12},{12,14},{14,10},{10,6},{6,2},{2,0},{1,5},{5,9},... | collective-permute-start | bytes 276488 | tf_op jit(solution)/shard_map/ppermute | solution.py:325
  41.8 7.6 %collective-permute-start.18 = (bf16[128,1440]{1,0:T(8,128)(2,1)S(1)}, bf16[128,1440]{1,0:T(8,128)(2,1)S(1)}, u32[]{:S(2)}, u32[]{:S(2)}) collective-permute-start(bf16[128,1440]{1,0:T(8,128)(2,1)S(1)} %get-tuple-element.70), channel_id=1, source_target_pairs={{0,1},{1,0},{2,3},{3,2},{4,5},{5,4},{6,7},{7,6},{8,9},{9,8},{10,11... | collective-permute-start | bytes 1105928 | tf_op jit(solution)/shard_map/ppermute | solution.py:288
  41.9 12.6 %collective-permute-start.25 = (bf16[128,1440]{1,0:T(8,128)(2,1)S(1)}, bf16[128,1440]{1,0:T(8,128)(2,1)S(1)}, u32[]{:S(2)}, u32[]{:S(2)}) collective-permute-start(bf16[128,1440]{1,0:T(8,128)(2,1)S(1)} %get-tuple-element.76), channel_id=1, source_target_pairs={{0,1},{1,0},{2,3},{3,2},{4,5},{5,4},{6,7},{7,6},{8,9},{9,8},{10,11... | collective-permute-start | bytes 1105928 | tf_op jit(solution)/shard_map/ppermute | solution.py:288
  42.4 6.9 %collective-permute-start.23 = (bf16[64,1440]{1,0:T(8,128)(2,1)S(1)}, bf16[64,1440]{1,0:T(8,128)(2,1)S(1)}, u32[]{:S(2)}, u32[]{:S(2)}) collective-permute-start(bf16[64,1440]{1,0:T(8,128)(2,1)S(1)} %add_convert_fusion.4), channel_id=1, source_target_pairs={{4,0},{8,4},{12,8},{14,12},{10,14},{6,10},{2,6},{0,2},{5,1},{9,5},... | collective-permute-start | bytes 552968 | tf_op jit(solution)/shard_map/ppermute | solution.py:326
  43.0 7.0 %collective-permute-start.21 = (bf16[64,1440]{1,0:T(8,128)(2,1)S(1)}, bf16[64,1440]{1,0:T(8,128)(2,1)S(1)}, u32[]{:S(2)}, u32[]{:S(2)}) collective-permute-start(bf16[64,1440]{1,0:T(8,128)(2,1)S(1)} %add_convert_fusion.6), channel_id=1, source_target_pairs={{0,4},{4,8},{8,12},{12,14},{14,10},{10,6},{6,2},{2,0},{1,5},{5,9},... | collective-permute-start | bytes 552968 | tf_op jit(solution)/shard_map/ppermute | solution.py:325
  49.5 6.1 %collective-permute-start.28 = (bf16[64,1440]{1,0:T(8,128)(2,1)S(1)}, bf16[64,1440]{1,0:T(8,128)(2,1)S(1)}, u32[]{:S(2)}, u32[]{:S(2)}) collective-permute-start(bf16[64,1440]{1,0:T(8,128)(2,1)S(1)} %add_convert_fusion.3), channel_id=1, source_target_pairs={{4,0},{8,4},{12,8},{14,12},{10,14},{6,10},{2,6},{0,2},{5,1},{9,5},... | collective-permute-start | bytes 552968 | tf_op jit(solution)/shard_map/ppermute | solution.py:326
  50.0 5.8 %collective-permute-start.26 = (bf16[64,1440]{1,0:T(8,128)(2,1)S(1)}, bf16[64,1440]{1,0:T(8,128)(2,1)S(1)}, u32[]{:S(2)}, u32[]{:S(2)}) collective-permute-start(bf16[64,1440]{1,0:T(8,128)(2,1)S(1)} %add_convert_fusion.5), channel_id=1, source_target_pairs={{0,4},{4,8},{8,12},{12,14},{14,10},{10,6},{6,2},{2,0},{1,5},{5,9},... | collective-permute-start | bytes 552968 | tf_op jit(solution)/shard_map/ppermute | solution.py:325
  54.3 3.7 %collective-permute-start.24 = (bf16[64,1440]{1,0:T(8,128)(2,1)S(1)}, bf16[64,1440]{1,0:T(8,128)(2,1)S(1)}, u32[]{:S(2)}, u32[]{:S(2)}) collective-permute-start(bf16[64,1440]{1,0:T(8,128)(2,1)S(1)} %get-tuple-element.81), channel_id=1, source_target_pairs={{0,1},{1,0},{2,3},{3,2},{4,5},{5,4},{6,7},{7,6},{8,9},{9,8},{10,11... | collective-permute-start | bytes 552968 | tf_op jit(solution)/shard_map/ppermute | solution.py:288
  55.9 6.0 %collective-permute-start.27 = (bf16[64,1440]{1,0:T(8,128)(2,1)S(1)}, bf16[64,1440]{1,0:T(8,128)(2,1)S(1)}, u32[]{:S(2)}, u32[]{:S(2)}) collective-permute-start(bf16[64,1440]{1,0:T(8,128)(2,1)S(1)} %add_convert_fusion.2), channel_id=1, source_target_pairs={{0,4},{4,8},{8,12},{12,14},{14,10},{10,6},{6,2},{2,0},{1,5},{5,9},... | collective-permute-start | bytes 552968 | tf_op jit(solution)/shard_map/ppermute | solution.py:325
  57.6 5.7 %collective-permute-start.29 = (bf16[64,1440]{1,0:T(8,128)(2,1)S(1)}, bf16[64,1440]{1,0:T(8,128)(2,1)S(1)}, u32[]{:S(2)}, u32[]{:S(2)}) collective-permute-start(bf16[64,1440]{1,0:T(8,128)(2,1)S(1)} %add_convert_fusion.1), channel_id=1, source_target_pairs={{4,0},{8,4},{12,8},{14,12},{10,14},{6,10},{2,6},{0,2},{5,1},{9,5},... | collective-permute-start | bytes 552968 | tf_op jit(solution)/shard_map/ppermute | solution.py:326

commit v8 on v7

--- a/solution.py
+++ b/solution.py
@@ -157,12 +157,12 @@
 
 def lower(hidden, w, weights, *outs):
     value = jnp.dot(hidden, w[...], preferred_element_type=jnp.float32)
-    start, rows = 0, outs[0].shape[0]
-    for weight in weights:
-        stop = start + weight.shape[0]
-        out, at = outs[start // rows], start % rows
-        out[at : at + weight.shape[0]] = (value[start:stop] * weight).astype(jnp.bfloat16)
-        start = stop
+    places = [(out, at) for out in outs for at in range(0, out.shape[0], weights[0].shape[0])]
+    start = 0
+    for weight, (out, at) in zip(weights, places):
+        rows = weight.shape[0]
+        out[at : at + rows] = (value[start : start + rows] * weight).astype(jnp.bfloat16)
+        start += rows
 
 
 def expert_kernel(n_blocks, n_experts, place, *refs):
@@ -191,18 +191,18 @@
 
 def second_kernel(n_blocks, n_experts, place, *refs):
     own, across = refs[:n_blocks], refs[n_blocks : 2 * n_blocks]
-    gated, lifted, w_gate, w_up, down_theirs, hidden, theirs, x = refs[2 * n_blocks :]
+    gated, lifted, w_gate, w_up, down_theirs, hidden, *theirs, x = refs[2 * n_blocks :]
     half = x.shape[1]
     gather_rows(across, x, half)
     there = 1 - place[0]
     hidden[...] = activate(gated[...] + project(x, there, w_gate), lifted[...] + project(x, there, w_up))
-    lower(hidden[...], down_theirs, gate_weights(own, half, place[1], n_experts), theirs)
+    lower(hidden[...], down_theirs, gate_weights(own, half, place[1], n_experts), *theirs)
 
 
 def third_kernel(n_blocks, n_experts, place, *refs):
     own = refs[:n_blocks]
-    hidden, down_mine, mine = refs[n_blocks:]
-    lower(hidden[...], down_mine, gate_weights(own, mine.shape[1], place[1], n_experts), mine)
+    hidden, down_mine, *mine = refs[n_blocks:]
+    lower(hidden[...], down_mine, gate_weights(own, mine[0].shape[1], place[1], n_experts), *mine)
 
 
 def call(kernel, place, args, out_shape, scratch_shapes, flops):
@@ -219,7 +219,7 @@
 
 
 def padded(rows):
-    return -(-rows // 128) * 128
+    return max(rows, 128)
 
 
 def run_expert(place, own, across, weights, n_experts):
@@ -237,30 +237,31 @@
     return outs[:pairs], outs[pairs:]
 
 
-def run_expert_in_stages(place, own, swap, weights, n_experts):
+def run_expert_in_stages(place, own, across, swap, weights, n_experts):
     gate, up, down_mine, down_theirs = weights
     width, hidden = gate.shape
     half = width // 2
     rows, n_blocks = sum(a.shape[0] for a in own), len(own)
-    across = [swap(a) for a in own]
+    first = own[0].shape[0]
     products = [in_vmem((padded(rows), hidden), jnp.float32)] * 2
+    outs = [in_vmem((first, half)), in_vmem((rows - first, half))]
     x = [pltpu.VMEM((padded(rows), half), jnp.bfloat16)]
     flops = 2 * padded(rows) * hidden * width
     gated, lifted = call(functools.partial(first_kernel, n_blocks), place, (*own, gate, up), products, x, flops)
-    units, theirs = call(
+    units, *theirs = call(
         functools.partial(second_kernel, n_blocks, n_experts),
         place,
         (*own, *across, gated, lifted, gate, up, down_theirs),
-        [in_vmem((padded(rows), hidden)), in_vmem((rows, half))],
+        [in_vmem((padded(rows), hidden)), *outs],
         x,
         flops + flops // 2,
     )
-    theirs = swap(theirs)
-    (mine,) = call(
+    theirs = [swap(a) for a in theirs]
+    mine = call(
         functools.partial(third_kernel, n_blocks, n_experts),
         place,
         (*own, units, down_mine),
-        [in_vmem((rows, half))],
+        outs,
         [],
         flops // 2,
     )
@@ -284,9 +285,7 @@
     def run(keys, wait_for=None):
         at = place if wait_for is None else after(place, wait_for)
         mine, theirs = run_expert(at, [came[k] for k in keys], [across[k] for k in keys], weights, n)
-        for i, pair in enumerate(zip(mine, theirs)):
-            keep(keys[2 * i : 2 * i + 2], pair[0], swap(pair[1]))
-        return theirs[0]
+        return [(keys[2 * i : 2 * i + 2], *pair) for i, pair in enumerate(zip(mine, theirs))]
 
     def keep(keys, mine, theirs):
         pairs = ((mine, theirs), lax.optimization_barrier((mine, theirs)))
@@ -300,41 +299,41 @@
     came[1] = lax.ppermute(packed, "ep", ahead)
     came[-1] = lax.ppermute(packed, "ep", back)
     across[0] = swap(packed)
-    weights, done = [gate, up], up
+    weights, done = [gate, up], [up]
     for k in range(2, far):
         came[k - 1], came[1 - k] = after(came[k - 1], done), after(came[1 - k], done)
         came[k] = lax.ppermute(came[k - 1], "ep", ahead)
         came[-k] = lax.ppermute(came[1 - k], "ep", back)
         across[k - 1], across[1 - k] = swap(came[k - 1]), swap(came[1 - k])
+        done = [across[k - 1], across[1 - k]]
         if k == 2:
-            weights += halve_weights(after(place, came[1]), w_down[0])
-            done = weights[-1]
-    came[far - 1], came[1 - far] = after(came[far - 1], done), after(came[1 - far], done)
-    came["low"] = lax.ppermute(came[far - 1][: rows // 2], "ep", ahead)
-    came["high"] = lax.ppermute(came[1 - far][rows // 2 :], "ep", back)
-    across[far - 1], across[1 - far] = swap(came[far - 1]), swap(came[1 - far])
-    done = run([far - 1, 1 - far], [across[k] for k in range(2 - far, far - 1)])
-    came["low"], came["high"] = after((came["low"], came["high"]), done)
-    far_keys = ["low", "high"]
-    keep(far_keys, *run_expert_in_stages(place, [came[k] for k in far_keys], swap, weights, n))
-
-    to_ahead = value["low"].astype(jnp.bfloat16)
-    to_back = value["high"].astype(jnp.bfloat16)
-    pad_low, pad_high = ((0, rows - rows // 2), (0, 0)), ((rows // 2, 0), (0, 0))
+            weights += halve_weights(after(place, (came[1], across[0])), w_down[0])
+            done.append(weights[-1])
+    came[far - 1] = after(came[far - 1], done)
+    came[far] = lax.ppermute(came[far - 1], "ep", ahead)
+    across[far - 1] = swap(came[far - 1])
+    near = run([j for i in range(1, far - 1) for j in (i, -i)])
+    done = near[0][-1]
+    came[far], came[1 - far] = after(came[far], done), after(came[1 - far], done)
+    across[far], across[1 - far] = swap(came[far]), swap(came[1 - far])
+    last = [far, far - 1, 1 - far]
+    for keys, mine, theirs in zip(([far], last[1:]), *run_expert_in_stages(place, [came[k] for k in last], [across[k] for k in last], swap, weights, n)):
+        keep(keys, mine, theirs)
+    for keys, mine, theirs in near:
+        keep(keys, mine, swap(after(theirs, value[far])))
+
+    to_ahead, to_back = value[far].astype(jnp.bfloat16), None
     for k in range(far - 1, -1, -1):
-        behind = lax.ppermute(to_ahead, "ep", ahead)
-        front = lax.ppermute(to_back, "ep", back)
-        if k == far - 1:
-            done = run([j for i in range(1, far - 1) for j in (i, -i)], (to_ahead, to_back))
-        elif k == 1:
-            done = run([0], (to_ahead, to_back))
-        behind, front = behind.astype(jnp.float32), front.astype(jnp.float32)
-        if k == far - 1:
-            behind, front = jnp.pad(behind, pad_low), jnp.pad(front, pad_high)
+        behind = lax.ppermute(to_ahead, "ep", ahead).astype(jnp.float32)
+        front = 0.0 if to_back is None else lax.ppermute(to_back, "ep", back).astype(jnp.float32)
+        done = None
+        if k == 1:
+            ((keys, mine, done),) = run([0], (to_ahead, to_back))
+            keep(keys, mine, swap(done))
         if k:
             to_ahead = (value[-k] + behind).astype(jnp.bfloat16)
             to_back = (value[k] + front).astype(jnp.bfloat16)
-        if k in (far - 1, 1):
+        if done is not None:
             to_ahead, to_back = after(to_ahead, done), after(to_back, done)
     return (value[0] + behind + front).astype(jnp.bfloat16)
 

time: 64.2 us -> 63.2 us (0.984)
  waiting for transfers between devices: 19.1 us -> 21.2 us
  Pallas kernels: 22.9 us -> 21.1 us
  starting transfers between devices: 20.5 us -> 19.2 us
    ppermute x19 -> x16, waiting for transfers between devices: 13 us -> 15.2 us  [the longest x4 9.73 us: ring_body(): behind = lax.ppermute(to_ahead, 'ep', ahead).astype(jnp.float32)]
    pallas_call x6 -> x5, Pallas kernels: 13.9 us -> 12.2 us  [call(): pl.pallas_call(kernel, out_shape=out_shape, in_specs=[pl.BlockSpec(memory...]
    ppermute x19 -> x16, starting transfers between devices: 12.8 us -> 11.4 us  [the longest x4 6.8 us: ring_body(): behind = lax.ppermute(to_ahead, 'ep', ahead).astype(jnp.float32)]
    ppermute x2, waiting for transfers between devices: 1.75 us -> 0.44 us  [ring_body(): came[-k] = lax.ppermute(came[1 - k], 'ep', back)]
    ppermute x2, waiting for transfers between devices: 4.32 us -> 5.52 us  [ring_body(): came[k] = lax.ppermute(came[k - 1], 'ep', ahead)]
  transfers between devices with their start and end apart: 30 -> 27, of which waited for: 10 -> 10; matrix products, arithmetic and copies ran while one was open for 1% -> 1% of each run, Pallas kernels for 31% -> 28%
where the time goes in v8:
time: 63.2 us; the launch traced here: 63 us
  waiting for transfers between devices  21.2 us (34%)
  Pallas kernels  21.1 us (33%)
  starting transfers between devices  19.2 us (30%)
  other arithmetic  1.32 us (2%)
    pallas_call x5, Pallas kernels, call(): pl.pallas_call(kernel, out_shape=out_shape, in_specs=[pl.BlockSpec(memory...  12.2 us
    ppermute x4, waiting for transfers between devices, ring_body(): behind = lax.ppermute(to_ahead, 'ep', ahead).astype(jnp.float32)  9.73 us
    ppermute x4, starting transfers between devices, ring_body(): behind = lax.ppermute(to_ahead, 'ep', ahead).astype(jnp.float32)  6.8 us
    ppermute x2, waiting for transfers between devices, ring_body(): came[k] = lax.ppermute(came[k - 1], 'ep', ahead)  5.52 us
    pallas_call x1, Pallas kernels, turn_weights(): pl.pallas_call(turn_kernel, out_shape=[in_vmem((width, hidden))] * 2, in_...  4.79 us
    ppermute x3, waiting for transfers between devices, ring_body(): lax.ppermute(to_back, 'ep', back).astype(jnp.float32)  4.59 us
    ppermute x2, starting transfers between devices, ring_body(): came[k] = lax.ppermute(came[k - 1], 'ep', ahead)  3.85 us
    pallas_call x1, Pallas kernels, halve_weights(): pl.pallas_call(halve_kernel, out_shape=[in_vmem((hidden, width // 2))] *...  3.13 us
  transfers between devices with their start and end apart: 27, of which 10 were waited for; matrix products, arithmetic and copies ran while one was open for 1% of the time, Pallas kernels for 28%

profile of v8, /device:TPU:0, one launch (start us, length us, event | category | flops | bytes accessed | tf_op | source)
XLA Modules:
  0.0 63.0 jit_solution(12727484076232172382)
XLA Ops:
  0.0 1.0 %shard_map.64.refs_0_ = bf16[64,1464]{1,0:T(8,128)(2,1)S(1)} custom-call(bf16[64,1440]{1,0:T(8,128)(2,1)} %tokens_in.1, s32[4,64]{1,0:T(4,128)} %bitcast.14, f32[4,64]{1,0:T(4,128)} %bitcast.15), custom_call_target="tpu_custom_call" | custom-call | tf_op jit(solution)/shard_map/pallas_call | solution.py:53
  1.0 3.1 %collective-permute-start = (bf16[64,1464]{1,0:T(8,128)(2,1)S(1)}, bf16[64,1464]{1,0:T(8,128)(2,1)S(1)}, u32[]{:S(2)}, u32[]{:S(2)}) collective-permute-start(bf16[64,1464]{1,0:T(8,128)(2,1)S(1)} %shard_map.64.refs_0_), channel_id=1, source_target_pairs={{0,4},{4,8},{8,12},{12,14},{14,10},{10,6},{6,2},{2,0},{1,5},{5,9},... | collective-permute-start | bytes 562184 | tf_op jit(solution)/shard_map/ppermute | solution.py:299
  4.1 0.0 collective-permute-start.1
  4.1 0.0 collective-permute-start.5
  4.1 0.1 pad_add_fusion.after_this.place
  4.2 4.8 %shard_map.65 = (bf16[2880,720]{1,0:T(8,128)(2,1)S(1)}, bf16[2880,720]{1,0:T(8,128)(2,1)S(1)}) custom-call(s32[2]{0:T(128)S(1)} %pad_add_fusion.after_this.place, bf16[720,2880]{1,0:T(8,128)(2,1)} %bitcast.11, bf16[720,2880]{1,0:T(8,128)(2,1)} %bitcast.12), custom_call_target="tpu_custom_call" | custom-call | bytes 16588800 | tf_op jit(solution)/shard_map/pallas_call | solution.py:83
  9.0 0.0 collective-permute-done.refs_0_
  9.0 0.6 collective-permute-start.3
  9.5 2.0 %collective-permute-start.2 = (bf16[64,1464]{1,0:T(8,128)(2,1)S(1)}, bf16[64,1464]{1,0:T(8,128)(2,1)S(1)}, u32[]{:S(2)}, u32[]{:S(2)}) collective-permute-start(bf16[64,1464]{1,0:T(8,128)(2,1)S(1)} %collective-permute-done.refs_0_), channel_id=1, source_target_pairs={{0,4},{4,8},{8,12},{12,14},{14,10},{10,6},{6,2},{2,0},{1,5},{5,9},... | collective-permute-start | bytes 562184 | tf_op jit(solution)/shard_map/ppermute | solution.py:305
  11.6 0.0 collective-permute-done.1.refs_1_
  11.6 0.0 collective-permute-start.4
  11.6 0.1 collective-permute-start.6
  11.6 0.0 collective-permute-done.5.refs_1_
  11.6 3.1 %shard_map.66 = (bf16[720,1440]{1,0:T(8,128)(2,1)S(1)}, bf16[720,1440]{1,0:T(8,128)(2,1)S(1)}) custom-call(s32[2]{0:T(128)S(1)} %pad_add_fusion.after_this.place, bf16[720,2880]{1,0:T(8,128)(2,1)} %bitcast.13), custom_call_target="tpu_custom_call" | custom-call | bytes 16588800 | tf_op jit(solution)/shard_map/pallas_call | solution.py:120
  14.8 0.0 collective-permute-done.3.refs_4_
  14.8 1.8 %collective-permute-done.2.refs_2_ = bf16[64,1464]{1,0:T(8,128)(2,1)S(1)} collective-permute-done((bf16[64,1464]{1,0:T(8,128)(2,1)S(1)}, bf16[64,1464]{1,0:T(8,128)(2,1)S(1)}, u32[]{:S(2)}, u32[]{:S(2)}) %collective-permute-start.2) | collective-permute-done | bytes 187424 | tf_op jit(solution)/shard_map/ppermute | solution.py:305
  16.6 0.0 collective-permute-done.4.refs_5_
  16.6 1.8 %collective-permute-start.9 = (bf16[64,1464]{1,0:T(8,128)(2,1)S(1)}, bf16[64,1464]{1,0:T(8,128)(2,1)S(1)}, u32[]{:S(2)}, u32[]{:S(2)}) collective-permute-start(bf16[64,1464]{1,0:T(8,128)(2,1)S(1)} %collective-permute-done.2.refs_2_), channel_id=1, source_target_pairs={{0,4},{4,8},{8,12},{12,14},{14,10},{10,6},{6,2},{2,0},{1,5},{5,9},... | collective-permute-start | bytes 562184 | tf_op jit(solution)/shard_map/ppermute | solution.py:305
  18.5 0.4 collective-permute-done.6.refs_3_
  18.9 0.1 collective-permute-start.8
  19.0 0.2 collective-permute-start.11
  19.2 3.7 %collective-permute-done.9.refs_1_ = bf16[64,1464]{1,0:T(8,128)(2,1)S(1)} collective-permute-done((bf16[64,1464]{1,0:T(8,128)(2,1)S(1)}, bf16[64,1464]{1,0:T(8,128)(2,1)S(1)}, u32[]{:S(2)}, u32[]{:S(2)}) %collective-permute-start.9) | collective-permute-done | bytes 187424 | tf_op jit(solution)/shard_map/ppermute | solution.py:305
  22.9 0.0 collective-permute-done.7.refs_6_
  22.9 0.0 collective-permute-done.8.refs_7_
  22.9 0.0 collective-permute-start.13
  22.9 1.7 %collective-permute-start.10 = (bf16[64,1464]{1,0:T(8,128)(2,1)S(1)}, bf16[64,1464]{1,0:T(8,128)(2,1)S(1)}, u32[]{:S(2)}, u32[]{:S(2)}) collective-permute-start(bf16[64,1464]{1,0:T(8,128)(2,1)S(1)} %collective-permute-done.9.refs_1_), channel_id=1, source_target_pairs={{0,4},{4,8},{8,12},{12,14},{14,10},{10,6},{6,2},{2,0},{1,5},{5,9},... | collective-permute-start | bytes 562184 | tf_op jit(solution)/shard_map/ppermute | solution.py:313
  24.6 4.5 %shard_map.67 = (bf16[128,1440]{1,0:T(8,128)(2,1)S(1)}, bf16[128,1440]{1,0:T(8,128)(2,1)S(1)}, bf16[128,1440]{1,0:T(8,128)(2,1)S(1)}, bf16[128,1440]{1,0:T(8,128)(2,1)S(1)}) custom-call(s32[2]{0:T(128)S(1)} %pad_add_fusion.after_this.place, bf16[64,1464]{1,0:T(8,128)(2,1)S(1)} %collective-permute-done.refs_0_, ...), custom_call_target="tpu_custom_call" | custom-call | flops 3185049600 | bytes 24883200 | tf_op jit(solution)/shard_map/pallas_call | solution.py:210
  29.1 0.2 collective-permute-start.14
  29.3 0.9 %collective-permute-done.10.refs_0_ = bf16[64,1464]{1,0:T(8,128)(2,1)S(1)} collective-permute-done((bf16[64,1464]{1,0:T(8,128)(2,1)S(1)}, bf16[64,1464]{1,0:T(8,128)(2,1)S(1)}, u32[]{:S(2)}, u32[]{:S(2)}) %collective-permute-start.10) | collective-permute-done | bytes 187424 | tf_op jit(solution)/shard_map/ppermute | solution.py:313
  30.2 0.0 collective-permute-start.12
  30.2 1.6 %shard_map.68 = (f32[192,720]{1,0:T(8,128)S(1)}, f32[192,720]{1,0:T(8,128)S(1)}) custom-call(s32[2]{0:T(128)S(1)} %pad_add_fusion.after_this.place, bf16[64,1464]{1,0:T(8,128)(2,1)S(1)} %collective-permute-done.10.refs_0_, bf16[64,1464]{1,0:T(8,128)(2,1)S(1)} %collective-permute-done.9.refs_1_, bf16[64,1464]{1,0:T(8,128)(2,1)S(1)} %collective-permute-done.11.refs_2_, ...), custom_call_target="tpu_custom_call" | custom-call | flops 796262400 | bytes 6220800 | tf_op jit(solution)/shard_map/pallas_call | solution.py:210
  31.9 0.0 collective-permute-done.14.refs_5_
  31.9 0.0 collective-permute-done.12.refs_3_
  31.9 2.2 %shard_map.69 = (bf16[192,720]{1,0:T(8,128)(2,1)S(1)}, bf16[64,1440]{1,0:T(8,128)(2,1)S(1)}, bf16[128,1440]{1,0:T(8,128)(2,1)S(1)}) custom-call(s32[2]{0:T(128)S(1)} %pad_add_fusion.after_this.place, bf16[64,1464]{1,0:T(8,128)(2,1)S(1)} %collective-permute-done.10.refs_0_, bf16[64,1464]{1,0:T(8,128)(2,1)S(1)} %collective-permute-done.9.refs_1_, ...), custom_call_target="tpu_custom_call" | custom-call | flops 1194393600 | bytes 9331200 | tf_op jit(solution)/shard_map/pallas_call | solution.py:210
  34.1 0.6 collective-permute-start.15
  34.7 0.1 collective-permute-start.17
  34.7 1.2 %shard_map.70 = (bf16[64,1440]{1,0:T(8,128)(2,1)S(1)}, bf16[128,1440]{1,0:T(8,128)(2,1)S(1)}) custom-call(s32[2]{0:T(128)S(1)} %pad_add_fusion.after_this.place, bf16[64,1464]{1,0:T(8,128)(2,1)S(1)} %collective-permute-done.10.refs_0_, bf16[64,1464]{1,0:T(8,128)(2,1)S(1)} %collective-permute-done.9.refs_1_, ...), custom_call_target="tpu_custom_call" | custom-call | flops 398131200 | bytes 3110400 | tf_op jit(solution)/shard_map/pallas_call | solution.py:210
  36.0 1.7 %collective-permute-start.18 = (bf16[64,1440]{1,0:T(8,128)(2,1)S(1)}, bf16[64,1440]{1,0:T(8,128)(2,1)S(1)}, u32[]{:S(2)}, u32[]{:S(2)}) collective-permute-start(bf16[64,1440]{1,0:T(8,128)(2,1)S(1)} %fusion), channel_id=1, source_target_pairs={{0,4},{4,8},{8,12},{12,14},{14,10},{10,6},{6,2},{2,0},{1,5},{5,9},... | collective-permute-start | bytes 552968 | tf_op jit(solution)/shard_map/ppermute | solution.py:327
  37.6 0.2 collective-permute-start.16
  37.8 0.3 collective-permute-start.22
  38.2 0.0 collective-permute-done.17
  38.2 0.5 collective-permute-start.20
  38.7 4.6 %collective-permute-done.18 = bf16[64,1440]{1,0:T(8,128)(2,1)S(1)} collective-permute-done((bf16[64,1440]{1,0:T(8,128)(2,1)S(1)}, bf16[64,1440]{1,0:T(8,128)(2,1)S(1)}, u32[]{:S(2)}, u32[]{:S(2)}) %collective-permute-start.18) | collective-permute-done | bytes 184352 | tf_op jit(solution)/shard_map/ppermute | solution.py:327
  43.3 0.1 add_convert_fusion.6
  43.4 1.7 %collective-permute-start.19 = (bf16[64,1440]{1,0:T(8,128)(2,1)S(1)}, bf16[64,1440]{1,0:T(8,128)(2,1)S(1)}, u32[]{:S(2)}, u32[]{:S(2)}) collective-permute-start(bf16[64,1440]{1,0:T(8,128)(2,1)S(1)} %add_convert_fusion.6), channel_id=1, source_target_pairs={{0,4},{4,8},{8,12},{12,14},{14,10},{10,6},{6,2},{2,0},{1,5},{5,9},... | collective-permute-start | bytes 552968 | tf_op jit(solution)/shard_map/ppermute | solution.py:327
  45.0 0.0 collective-permute-done.16
  45.0 0.2 collective-permute-done.20
  45.2 0.1 add_convert_fusion.3
  45.3 0.5 collective-permute-start.25
  45.8 4.1 %collective-permute-done.19 = bf16[64,1440]{1,0:T(8,128)(2,1)S(1)} collective-permute-done((bf16[64,1440]{1,0:T(8,128)(2,1)S(1)}, bf16[64,1440]{1,0:T(8,128)(2,1)S(1)}, u32[]{:S(2)}, u32[]{:S(2)}) %collective-permute-start.19) | collective-permute-done | bytes 184352 | tf_op jit(solution)/shard_map/ppermute | solution.py:327
  49.9 0.1 add_convert_fusion.5
  50.0 1.8 %collective-permute-start.23 = (bf16[64,1440]{1,0:T(8,128)(2,1)S(1)}, bf16[64,1440]{1,0:T(8,128)(2,1)S(1)}, u32[]{:S(2)}, u32[]{:S(2)}) collective-permute-start(bf16[64,1440]{1,0:T(8,128)(2,1)S(1)} %add_convert_fusion.5), channel_id=1, source_target_pairs={{0,4},{4,8},{8,12},{12,14},{14,10},{10,6},{6,2},{2,0},{1,5},{5,9},... | collective-permute-start | bytes 552968 | tf_op jit(solution)/shard_map/ppermute | solution.py:327
  51.8 2.7 %shard_map.71 = (bf16[64,1440]{1,0:T(8,128)(2,1)S(1)}, bf16[64,1440]{1,0:T(8,128)(2,1)S(1)}) custom-call(s32[2]{0:T(128)S(1)} %pad_add_fusion.after_this.place, bf16[64,1464]{1,0:T(8,128)(2,1)S(1)} %shard_map.64.refs_0_, bf16[64,1464]{1,0:T(8,128)(2,1)S(1)} %collective-permute-done.5.refs_1_, ...), custom_call_target="tpu_custom_call" | custom-call | flops 1592524800 | bytes 12441600 | tf_op jit(solution)/shard_map/pallas_call | solution.py:210
  54.5 0.1 collective-permute-start.21
  54.5 0.0 collective-permute-done.25
  54.6 0.1 add_convert_fusion.1
  54.6 0.5 collective-permute-start.26
  55.1 0.7 %collective-permute-done.23 = bf16[64,1440]{1,0:T(8,128)(2,1)S(1)} collective-permute-done((bf16[64,1440]{1,0:T(8,128)(2,1)S(1)}, bf16[64,1440]{1,0:T(8,128)(2,1)S(1)}, u32[]{:S(2)}, u32[]{:S(2)}) %collective-permute-start.23) | collective-permute-done | bytes 184352 | tf_op jit(solution)/shard_map/ppermute | solution.py:327
  55.9 0.1 add_convert_fusion.2
  55.9 1.7 %collective-permute-start.24 = (bf16[64,1440]{1,0:T(8,128)(2,1)S(1)}, bf16[64,1440]{1,0:T(8,128)(2,1)S(1)}, u32[]{:S(2)}, u32[]{:S(2)}) collective-permute-start(bf16[64,1440]{1,0:T(8,128)(2,1)S(1)} %add_convert_fusion.2), channel_id=1, source_target_pairs={{0,4},{4,8},{8,12},{12,14},{14,10},{10,6},{6,2},{2,0},{1,5},{5,9},... | collective-permute-start | bytes 552968 | tf_op jit(solution)/shard_map/ppermute | solution.py:327
  57.6 0.0 collective-permute-done.21
  57.6 4.4 %collective-permute-done.26 = bf16[64,1440]{1,0:T(8,128)(2,1)S(1)} collective-permute-done((bf16[64,1440]{1,0:T(8,128)(2,1)S(1)}, bf16[64,1440]{1,0:T(8,128)(2,1)S(1)}, u32[]{:S(2)}, u32[]{:S(2)}) %collective-permute-start.26) | collective-permute-done | bytes 184352 | tf_op jit(solution)/shard_map/ppermute | solution.py:328
  62.0 0.3 collective-permute-done.24
  62.3 0.8 %add_convert_fusion = bf16[64,1440]{1,0:T(8,128)(2,1)} fusion(bf16[64,1440]{1,0:T(8,128)(2,1)S(1)} %collective-permute-done.26, bf16[64,1440]{1,0:T(8,128)(2,1)S(1)} %collective-permute-done.24, bf16[64,1440]{1,0:T(8,128)(2,1)S(1)} %collective-permute-done.21, bf16[64,1440]{1,0:T(8,128)(2,1)S(1)} %get-tuple-element.71), kind=kLoop, calls=%fused_computation | loop fusion | flops 737280 | bytes 921600 | tf_op jit(solution)/shard_map/convert_element_type | solution.py:338
  (7 shorter events, 0.1 us)
Async XLA Ops:
  1.0 8.0 %collective-permute-start = (bf16[64,1464]{1,0:T(8,128)(2,1)S(1)}, bf16[64,1464]{1,0:T(8,128)(2,1)S(1)}, u32[]{:S(2)}, u32[]{:S(2)}) collective-permute-start(bf16[64,1464]{1,0:T(8,128)(2,1)S(1)} %shard_map.64.refs_0_), channel_id=1, source_target_pairs={{0,4},{4,8},{8,12},{12,14},{14,10},{10,6},{6,2},{2,0},{1,5},{5,9},... | collective-permute-start | bytes 562184 | tf_op jit(solution)/shard_map/ppermute | solution.py:299
  4.1 7.5 %collective-permute-start.1 = (bf16[64,1464]{1,0:T(8,128)(2,1)S(1)}, bf16[64,1464]{1,0:T(8,128)(2,1)S(1)}, u32[]{:S(2)}, u32[]{:S(2)}) collective-permute-start(bf16[64,1464]{1,0:T(8,128)(2,1)S(1)} %shard_map.64.refs_0_), channel_id=1, source_target_pairs={{4,0},{8,4},{12,8},{14,12},{10,14},{6,10},{2,6},{0,2},{5,1},{9,5},... | collective-permute-start | bytes 562184 | tf_op jit(solution)/shard_map/ppermute | solution.py:300
  4.1 7.6 %collective-permute-start.5 = (bf16[64,1464]{1,0:T(8,128)(2,1)S(1)}, bf16[64,1464]{1,0:T(8,128)(2,1)S(1)}, u32[]{:S(2)}, u32[]{:S(2)}) collective-permute-start(bf16[64,1464]{1,0:T(8,128)(2,1)S(1)} %shard_map.64.refs_0_), channel_id=1, source_target_pairs={{0,1},{1,0},{2,3},{3,2},{4,5},{5,4},{6,7},{7,6},{8,9},{9,8},{10,11... | collective-permute-start | bytes 562184 | tf_op jit(solution)/shard_map/ppermute | solution.py:301
  9.0 5.8 %collective-permute-start.3 = (bf16[64,1464]{1,0:T(8,128)(2,1)S(1)}, bf16[64,1464]{1,0:T(8,128)(2,1)S(1)}, u32[]{:S(2)}, u32[]{:S(2)}) collective-permute-start(bf16[64,1464]{1,0:T(8,128)(2,1)S(1)} %collective-permute-done.refs_0_), channel_id=1, source_target_pairs={{0,1},{1,0},{2,3},{3,2},{4,5},{5,4},{6,7},{7,6},{8,9},{9,8},{10,11... | collective-permute-start | bytes 562184 | tf_op jit(solution)/shard_map/ppermute | solution.py:307
  9.5 7.1 %collective-permute-start.2 = (bf16[64,1464]{1,0:T(8,128)(2,1)S(1)}, bf16[64,1464]{1,0:T(8,128)(2,1)S(1)}, u32[]{:S(2)}, u32[]{:S(2)}) collective-permute-start(bf16[64,1464]{1,0:T(8,128)(2,1)S(1)} %collective-permute-done.refs_0_), channel_id=1, source_target_pairs={{0,4},{4,8},{8,12},{12,14},{14,10},{10,6},{6,2},{2,0},{1,5},{5,9},... | collective-permute-start | bytes 562184 | tf_op jit(solution)/shard_map/ppermute | solution.py:305
  11.6 5.0 %collective-permute-start.4 = (bf16[64,1464]{1,0:T(8,128)(2,1)S(1)}, bf16[64,1464]{1,0:T(8,128)(2,1)S(1)}, u32[]{:S(2)}, u32[]{:S(2)}) collective-permute-start(bf16[64,1464]{1,0:T(8,128)(2,1)S(1)} %collective-permute-done.1.refs_1_), channel_id=1, source_target_pairs={{0,1},{1,0},{2,3},{3,2},{4,5},{5,4},{6,7},{7,6},{8,9},{9,8},{10,11... | collective-permute-start | bytes 562184 | tf_op jit(solution)/shard_map/ppermute | solution.py:307
  11.6 7.3 %collective-permute-start.6 = (bf16[64,1464]{1,0:T(8,128)(2,1)S(1)}, bf16[64,1464]{1,0:T(8,128)(2,1)S(1)}, u32[]{:S(2)}, u32[]{:S(2)}) collective-permute-start(bf16[64,1464]{1,0:T(8,128)(2,1)S(1)} %collective-permute-done.1.refs_1_), channel_id=1, source_target_pairs={{4,0},{8,4},{12,8},{14,12},{10,14},{6,10},{2,6},{0,2},{5,1},{9,5},... | collective-permute-start | bytes 562184 | tf_op jit(solution)/shard_map/ppermute | solution.py:306
  16.6 6.3 %collective-permute-start.9 = (bf16[64,1464]{1,0:T(8,128)(2,1)S(1)}, bf16[64,1464]{1,0:T(8,128)(2,1)S(1)}, u32[]{:S(2)}, u32[]{:S(2)}) collective-permute-start(bf16[64,1464]{1,0:T(8,128)(2,1)S(1)} %collective-permute-done.2.refs_2_), channel_id=1, source_target_pairs={{0,4},{4,8},{8,12},{12,14},{14,10},{10,6},{6,2},{2,0},{1,5},{5,9},... | collective-permute-start | bytes 562184 | tf_op jit(solution)/shard_map/ppermute | solution.py:305
  18.4 4.4 %collective-permute-start.7 = (bf16[64,1464]{1,0:T(8,128)(2,1)S(1)}, bf16[64,1464]{1,0:T(8,128)(2,1)S(1)}, u32[]{:S(2)}, u32[]{:S(2)}) collective-permute-start(bf16[64,1464]{1,0:T(8,128)(2,1)S(1)} %collective-permute-done.2.refs_2_), channel_id=1, source_target_pairs={{0,1},{1,0},{2,3},{3,2},{4,5},{5,4},{6,7},{7,6},{8,9},{9,8},{10,11... | collective-permute-start | bytes 562184 | tf_op jit(solution)/shard_map/ppermute | solution.py:307
  18.9 4.0 %collective-permute-start.8 = (bf16[64,1464]{1,0:T(8,128)(2,1)S(1)}, bf16[64,1464]{1,0:T(8,128)(2,1)S(1)}, u32[]{:S(2)}, u32[]{:S(2)}) collective-permute-start(bf16[64,1464]{1,0:T(8,128)(2,1)S(1)} %collective-permute-done.6.refs_3_), channel_id=1, source_target_pairs={{0,1},{1,0},{2,3},{3,2},{4,5},{5,4},{6,7},{7,6},{8,9},{9,8},{10,11... | collective-permute-start | bytes 562184 | tf_op jit(solution)/shard_map/ppermute | solution.py:307
  19.0 10.1 %collective-permute-start.11 = (bf16[64,1464]{1,0:T(8,128)(2,1)S(1)}, bf16[64,1464]{1,0:T(8,128)(2,1)S(1)}, u32[]{:S(2)}, u32[]{:S(2)}) collective-permute-start(bf16[64,1464]{1,0:T(8,128)(2,1)S(1)} %collective-permute-done.6.refs_3_), channel_id=1, source_target_pairs={{4,0},{8,4},{12,8},{14,12},{10,14},{6,10},{2,6},{0,2},{5,1},{9,5},... | collective-permute-start | bytes 562184 | tf_op jit(solution)/shard_map/ppermute | solution.py:306
  22.9 9.0 %collective-permute-start.13 = (bf16[64,1464]{1,0:T(8,128)(2,1)S(1)}, bf16[64,1464]{1,0:T(8,128)(2,1)S(1)}, u32[]{:S(2)}, u32[]{:S(2)}) collective-permute-start(bf16[64,1464]{1,0:T(8,128)(2,1)S(1)} %collective-permute-done.9.refs_1_), channel_id=1, source_target_pairs={{0,1},{1,0},{2,3},{3,2},{4,5},{5,4},{6,7},{7,6},{8,9},{9,8},{10,11... | collective-permute-start | bytes 562184 | tf_op jit(solution)/shard_map/ppermute | solution.py:314
  22.9 7.3 %collective-permute-start.10 = (bf16[64,1464]{1,0:T(8,128)(2,1)S(1)}, bf16[64,1464]{1,0:T(8,128)(2,1)S(1)}, u32[]{:S(2)}, u32[]{:S(2)}) collective-permute-start(bf16[64,1464]{1,0:T(8,128)(2,1)S(1)} %collective-permute-done.9.refs_1_), channel_id=1, source_target_pairs={{0,4},{4,8},{8,12},{12,14},{14,10},{10,6},{6,2},{2,0},{1,5},{5,9},... | collective-permute-start | bytes 562184 | tf_op jit(solution)/shard_map/ppermute | solution.py:313
  29.1 2.8 %collective-permute-start.14 = (bf16[64,1464]{1,0:T(8,128)(2,1)S(1)}, bf16[64,1464]{1,0:T(8,128)(2,1)S(1)}, u32[]{:S(2)}, u32[]{:S(2)}) collective-permute-start(bf16[64,1464]{1,0:T(8,128)(2,1)S(1)} %collective-permute-done.11.refs_2_), channel_id=1, source_target_pairs={{0,1},{1,0},{2,3},{3,2},{4,5},{5,4},{6,7},{7,6},{8,9},{9,8},{10,11... | collective-permute-start | bytes 562184 | tf_op jit(solution)/shard_map/ppermute | solution.py:318
  30.2 1.7 %collective-permute-start.12 = (bf16[64,1464]{1,0:T(8,128)(2,1)S(1)}, bf16[64,1464]{1,0:T(8,128)(2,1)S(1)}, u32[]{:S(2)}, u32[]{:S(2)}) collective-permute-start(bf16[64,1464]{1,0:T(8,128)(2,1)S(1)} %collective-permute-done.10.refs_0_), channel_id=1, source_target_pairs={{0,1},{1,0},{2,3},{3,2},{4,5},{5,4},{6,7},{7,6},{8,9},{9,8},{10,11... | collective-permute-start | bytes 562184 | tf_op jit(solution)/shard_map/ppermute | solution.py:318
  34.1 1.8 %collective-permute-start.15 = (bf16[64,1440]{1,0:T(8,128)(2,1)S(1)}, bf16[64,1440]{1,0:T(8,128)(2,1)S(1)}, u32[]{:S(2)}, u32[]{:S(2)}) collective-permute-start(bf16[64,1440]{1,0:T(8,128)(2,1)S(1)} %get-tuple-element.62), channel_id=1, source_target_pairs={{0,1},{1,0},{2,3},{3,2},{4,5},{5,4},{6,7},{7,6},{8,9},{9,8},{10,11... | collective-permute-start | bytes 552968 | tf_op jit(solution)/shard_map/ppermute | solution.py:259
  34.7 3.5 %collective-permute-start.17 = (bf16[128,1440]{1,0:T(8,128)(2,1)S(1)}, bf16[128,1440]{1,0:T(8,128)(2,1)S(1)}, u32[]{:S(2)}, u32[]{:S(2)}) collective-permute-start(bf16[128,1440]{1,0:T(8,128)(2,1)S(1)} %get-tuple-element.67), channel_id=1, source_target_pairs={{0,1},{1,0},{2,3},{3,2},{4,5},{5,4},{6,7},{7,6},{8,9},{9,8},{10,11... | collective-permute-start | bytes 1105928 | tf_op jit(solution)/shard_map/ppermute | solution.py:259
  36.0 7.3 %collective-permute-start.18 = (bf16[64,1440]{1,0:T(8,128)(2,1)S(1)}, bf16[64,1440]{1,0:T(8,128)(2,1)S(1)}, u32[]{:S(2)}, u32[]{:S(2)}) collective-permute-start(bf16[64,1440]{1,0:T(8,128)(2,1)S(1)} %fusion), channel_id=1, source_target_pairs={{0,4},{4,8},{8,12},{12,14},{14,10},{10,6},{6,2},{2,0},{1,5},{5,9},... | collective-permute-start | bytes 552968 | tf_op jit(solution)/shard_map/ppermute | solution.py:327
  37.6 7.4 %collective-permute-start.16 = (bf16[128,1440]{1,0:T(8,128)(2,1)S(1)}, bf16[128,1440]{1,0:T(8,128)(2,1)S(1)}, u32[]{:S(2)}, u32[]{:S(2)}) collective-permute-start(bf16[128,1440]{1,0:T(8,128)(2,1)S(1)} %get-tuple-element.63), channel_id=1, source_target_pairs={{0,1},{1,0},{2,3},{3,2},{4,5},{5,4},{6,7},{7,6},{8,9},{9,8},{10,11... | collective-permute-start | bytes 1105928 | tf_op jit(solution)/shard_map/ppermute | solution.py:323
  37.8 14.0 %collective-permute-start.22 = (bf16[128,1440]{1,0:T(8,128)(2,1)S(1)}, bf16[128,1440]{1,0:T(8,128)(2,1)S(1)}, u32[]{:S(2)}, u32[]{:S(2)}) collective-permute-start(bf16[128,1440]{1,0:T(8,128)(2,1)S(1)} %get-tuple-element.74), channel_id=1, source_target_pairs={{0,1},{1,0},{2,3},{3,2},{4,5},{5,4},{6,7},{7,6},{8,9},{9,8},{10,11... | collective-permute-start | bytes 1105928 | tf_op jit(solution)/shard_map/ppermute | solution.py:323
  38.2 7.0 %collective-permute-start.20 = (bf16[64,1440]{1,0:T(8,128)(2,1)S(1)}, bf16[64,1440]{1,0:T(8,128)(2,1)S(1)}, u32[]{:S(2)}, u32[]{:S(2)}) collective-permute-start(bf16[64,1440]{1,0:T(8,128)(2,1)S(1)} %add_convert_fusion.4), channel_id=1, source_target_pairs={{4,0},{8,4},{12,8},{14,12},{10,14},{6,10},{2,6},{0,2},{5,1},{9,5},... | collective-permute-start | bytes 552968 | tf_op jit(solution)/shard_map/ppermute | solution.py:328
  43.4 6.5 %collective-permute-start.19 = (bf16[64,1440]{1,0:T(8,128)(2,1)S(1)}, bf16[64,1440]{1,0:T(8,128)(2,1)S(1)}, u32[]{:S(2)}, u32[]{:S(2)}) collective-permute-start(bf16[64,1440]{1,0:T(8,128)(2,1)S(1)} %add_convert_fusion.6), channel_id=1, source_target_pairs={{0,4},{4,8},{8,12},{12,14},{14,10},{10,6},{6,2},{2,0},{1,5},{5,9},... | collective-permute-start | bytes 552968 | tf_op jit(solution)/shard_map/ppermute | solution.py:327
  45.3 9.2 %collective-permute-start.25 = (bf16[64,1440]{1,0:T(8,128)(2,1)S(1)}, bf16[64,1440]{1,0:T(8,128)(2,1)S(1)}, u32[]{:S(2)}, u32[]{:S(2)}) collective-permute-start(bf16[64,1440]{1,0:T(8,128)(2,1)S(1)} %add_convert_fusion.3), channel_id=1, source_target_pairs={{4,0},{8,4},{12,8},{14,12},{10,14},{6,10},{2,6},{0,2},{5,1},{9,5},... | collective-permute-start | bytes 552968 | tf_op jit(solution)/shard_map/ppermute | solution.py:328
  50.0 5.9 %collective-permute-start.23 = (bf16[64,1440]{1,0:T(8,128)(2,1)S(1)}, bf16[64,1440]{1,0:T(8,128)(2,1)S(1)}, u32[]{:S(2)}, u32[]{:S(2)}) collective-permute-start(bf16[64,1440]{1,0:T(8,128)(2,1)S(1)} %add_convert_fusion.5), channel_id=1, source_target_pairs={{0,4},{4,8},{8,12},{12,14},{14,10},{10,6},{6,2},{2,0},{1,5},{5,9},... | collective-permute-start | bytes 552968 | tf_op jit(solution)/shard_map/ppermute | solution.py:327
  54.5 3.1 %collective-permute-start.21 = (bf16[64,1440]{1,0:T(8,128)(2,1)S(1)}, bf16[64,1440]{1,0:T(8,128)(2,1)S(1)}, u32[]{:S(2)}, u32[]{:S(2)}) collective-permute-start(bf16[64,1440]{1,0:T(8,128)(2,1)S(1)} %get-tuple-element.72), channel_id=1, source_target_pairs={{0,1},{1,0},{2,3},{3,2},{4,5},{5,4},{6,7},{7,6},{8,9},{9,8},{10,11... | collective-permute-start | bytes 552968 | tf_op jit(solution)/shard_map/ppermute | solution.py:332
  54.6 7.3 %collective-permute-start.26 = (bf16[64,1440]{1,0:T(8,128)(2,1)S(1)}, bf16[64,1440]{1,0:T(8,128)(2,1)S(1)}, u32[]{:S(2)}, u32[]{:S(2)}) collective-permute-start(bf16[64,1440]{1,0:T(8,128)(2,1)S(1)} %add_convert_fusion.1), channel_id=1, source_target_pairs={{4,0},{8,4},{12,8},{14,12},{10,14},{6,10},{2,6},{0,2},{5,1},{9,5},... | collective-permute-start | bytes 552968 | tf_op jit(solution)/shard_map/ppermute | solution.py:328
  55.9 6.3 %collective-permute-start.24 = (bf16[64,1440]{1,0:T(8,128)(2,1)S(1)}, bf16[64,1440]{1,0:T(8,128)(2,1)S(1)}, u32[]{:S(2)}, u32[]{:S(2)}) collective-permute-start(bf16[64,1440]{1,0:T(8,128)(2,1)S(1)} %add_convert_fusion.2), channel_id=1, source_target_pairs={{0,4},{4,8},{8,12},{12,14},{14,10},{10,6},{6,2},{2,0},{1,5},{5,9},... | collective-permute-start | bytes 552968 | tf_op jit(solution)/shard_map/ppermute | solution.py:327

commit v9 on v8

--- a/solution.py
+++ b/solution.py
@@ -299,23 +299,21 @@
     came[1] = lax.ppermute(packed, "ep", ahead)
     came[-1] = lax.ppermute(packed, "ep", back)
     across[0] = swap(packed)
-    weights, done = [gate, up], [up]
-    for k in range(2, far):
+    weights, done, near = [gate, up], up, []
+    for k in range(2, far + 1):
         came[k - 1], came[1 - k] = after(came[k - 1], done), after(came[1 - k], done)
         came[k] = lax.ppermute(came[k - 1], "ep", ahead)
-        came[-k] = lax.ppermute(came[1 - k], "ep", back)
+        if k < far:
+            came[-k] = lax.ppermute(came[1 - k], "ep", back)
         across[k - 1], across[1 - k] = swap(came[k - 1]), swap(came[1 - k])
-        done = [across[k - 1], across[1 - k]]
         if k == 2:
-            weights += halve_weights(after(place, (came[1], across[0])), w_down[0])
-            done.append(weights[-1])
-    came[far - 1] = after(came[far - 1], done)
-    came[far] = lax.ppermute(came[far - 1], "ep", ahead)
-    across[far - 1] = swap(came[far - 1])
-    near = run([j for i in range(1, far - 1) for j in (i, -i)])
-    done = near[0][-1]
-    came[far], came[1 - far] = after(came[far], done), after(came[1 - far], done)
-    across[far], across[1 - far] = swap(came[far]), swap(came[1 - far])
+            weights += halve_weights(after(place, came[1]), w_down[0])
+            done = weights[-1]
+        else:
+            near += run([k - 2, 2 - k])
+            done = near[-1][-1]
+    came[far] = after(came[far], done)
+    across[far] = swap(came[far])
     last = [far, far - 1, 1 - far]
     for keys, mine, theirs in zip(([far], last[1:]), *run_expert_in_stages(place, [came[k] for k in last], [across[k] for k in last], swap, weights, n)):
         keep(keys, mine, theirs)

time: 63.2 us -> 62 us (0.981)
  waiting for transfers between devices: 21.2 us -> 18.5 us
  Pallas kernels: 21.1 us -> 22 us
  starting transfers between devices: 19.2 us -> 19.9 us
    ppermute x4, waiting for transfers between devices: 9.73 us -> 14 us  [ring_body(): behind = lax.ppermute(to_ahead, 'ep', ahead).astype(jnp.float32)]
    ppermute x3, waiting for transfers between devices: 4.59 us -> 1.28 us  [ring_body(): lax.ppermute(to_back, 'ep', back).astype(jnp.float32)]
    ppermute x2 -> x3, waiting for transfers between devices: 5.52 us -> 2.37 us  [ring_body(): came[k] = lax.ppermute(came[k - 1], 'ep', ahead)]
    ppermute x2 -> x3, starting transfers between devices: 3.85 us -> 5.64 us  [ring_body(): came[k] = lax.ppermute(came[k - 1], 'ep', ahead)]
    ppermute x4 -> x1, starting transfers between devices: 1.9 us -> 0.23 us  [ring_body(): across[far] = swap(came[far])]
    pallas_call x5 -> x6, Pallas kernels: 12.2 us -> 13.1 us  [call(): pl.pallas_call(kernel, out_shape=out_shape, in_specs=[pl.BlockSpec(memory...]
    ppermute x4 -> x1, waiting for transfers between devices: 0.91 us -> 0.01 us  [ring_body(): across[far] = swap(came[far])]
  transfers between devices with their start and end apart: 27 -> 27, of which waited for: 10 -> 9; matrix products, arithmetic and copies ran while one was open for 1% -> 1% of each run, Pallas kernels for 28% -> 30%
where the time goes in v9:
time: 62 us; the launch traced here: 61.9 us
  Pallas kernels  22 us (35%)
  starting transfers between devices  19.9 us (32%)
  waiting for transfers between devices  18.5 us (30%)
  other arithmetic  1.32 us (2%)
    ppermute x4, waiting for transfers between devices, ring_body(): behind = lax.ppermute(to_ahead, 'ep', ahead).astype(jnp.float32)  14 us
    pallas_call x6, Pallas kernels, call(): pl.pallas_call(kernel, out_shape=out_shape, in_specs=[pl.BlockSpec(memory...  13.1 us
    ppermute x4, starting transfers between devices, ring_body(): behind = lax.ppermute(to_ahead, 'ep', ahead).astype(jnp.float32)  6.6 us
    ppermute x3, starting transfers between devices, ring_body(): came[k] = lax.ppermute(came[k - 1], 'ep', ahead)  5.64 us
    pallas_call x1, Pallas kernels, turn_weights(): pl.pallas_call(turn_kernel, out_shape=[in_vmem((width, hidden))] * 2, in_...  4.79 us
    pallas_call x1, Pallas kernels, halve_weights(): pl.pallas_call(halve_kernel, out_shape=[in_vmem((hidden, width // 2))] *...  3.13 us
    ppermute x1, starting transfers between devices, ring_body(): came[1] = lax.ppermute(packed, 'ep', ahead)  3.08 us
    ppermute x3, waiting for transfers between devices, ring_body(): came[k] = lax.ppermute(came[k - 1], 'ep', ahead)  2.37 us
  transfers between devices with their start and end apart: 27, of which 9 were waited for; matrix products, arithmetic and copies ran while one was open for 1% of the time, Pallas kernels for 30%

profile of v9, /device:TPU:0, one launch (start us, length us, event | category | flops | bytes accessed | tf_op | source)
XLA Modules:
  0.0 61.9 jit_solution(1478347410605498386)
XLA Ops:
  0.0 1.0 %shard_map.64.refs_0_ = bf16[64,1464]{1,0:T(8,128)(2,1)S(1)} custom-call(bf16[64,1440]{1,0:T(8,128)(2,1)} %tokens_in.1, s32[4,64]{1,0:T(4,128)} %bitcast.14, f32[4,64]{1,0:T(4,128)} %bitcast.15), custom_call_target="tpu_custom_call" | custom-call | tf_op jit(solution)/shard_map/pallas_call | solution.py:53
  1.0 3.1 %collective-permute-start = (bf16[64,1464]{1,0:T(8,128)(2,1)S(1)}, bf16[64,1464]{1,0:T(8,128)(2,1)S(1)}, u32[]{:S(2)}, u32[]{:S(2)}) collective-permute-start(bf16[64,1464]{1,0:T(8,128)(2,1)S(1)} %shard_map.64.refs_0_), channel_id=1, source_target_pairs={{0,4},{4,8},{8,12},{12,14},{14,10},{10,6},{6,2},{2,0},{1,5},{5,9},... | collective-permute-start | bytes 562184 | tf_op jit(solution)/shard_map/ppermute | solution.py:299
  4.1 0.0 collective-permute-start.2
  4.1 0.1 pad_add_fusion.after_this.place
  4.2 4.8 %shard_map.65 = (bf16[2880,720]{1,0:T(8,128)(2,1)S(1)}, bf16[2880,720]{1,0:T(8,128)(2,1)S(1)}) custom-call(s32[2]{0:T(128)S(1)} %pad_add_fusion.after_this.place, bf16[720,2880]{1,0:T(8,128)(2,1)} %bitcast.11, bf16[720,2880]{1,0:T(8,128)(2,1)} %bitcast.12), custom_call_target="tpu_custom_call" | custom-call | bytes 16588800 | tf_op jit(solution)/shard_map/pallas_call | solution.py:83
  9.0 0.0 collective-permute-done.refs_0_
  9.0 2.1 %collective-permute-start.1 = (bf16[64,1464]{1,0:T(8,128)(2,1)S(1)}, bf16[64,1464]{1,0:T(8,128)(2,1)S(1)}, u32[]{:S(2)}, u32[]{:S(2)}) collective-permute-start(bf16[64,1464]{1,0:T(8,128)(2,1)S(1)} %collective-permute-done.refs_0_), channel_id=1, source_target_pairs={{0,4},{4,8},{8,12},{12,14},{14,10},{10,6},{6,2},{2,0},{1,5},{5,9},... | collective-permute-start | bytes 562184 | tf_op jit(solution)/shard_map/ppermute | solution.py:305
  11.0 0.0 collective-permute-done.2.refs_1_
  11.1 0.0 collective-permute-start.3
  11.1 0.5 collective-permute-start.8
  11.6 3.1 %shard_map.66 = (bf16[720,1440]{1,0:T(8,128)(2,1)S(1)}, bf16[720,1440]{1,0:T(8,128)(2,1)S(1)}) custom-call(s32[2]{0:T(128)S(1)} %pad_add_fusion.after_this.place, bf16[720,2880]{1,0:T(8,128)(2,1)} %bitcast.13), custom_call_target="tpu_custom_call" | custom-call | bytes 16588800 | tf_op jit(solution)/shard_map/pallas_call | solution.py:120
  14.7 0.7 %collective-permute-done.1.refs_0_ = bf16[64,1464]{1,0:T(8,128)(2,1)S(1)} collective-permute-done((bf16[64,1464]{1,0:T(8,128)(2,1)S(1)}, bf16[64,1464]{1,0:T(8,128)(2,1)S(1)}, u32[]{:S(2)}, u32[]{:S(2)}) %collective-permute-start.1) | collective-permute-done | bytes 187424 | tf_op jit(solution)/shard_map/ppermute | solution.py:305
  15.4 1.7 %collective-permute-start.6 = (bf16[64,1464]{1,0:T(8,128)(2,1)S(1)}, bf16[64,1464]{1,0:T(8,128)(2,1)S(1)}, u32[]{:S(2)}, u32[]{:S(2)}) collective-permute-start(bf16[64,1464]{1,0:T(8,128)(2,1)S(1)} %collective-permute-done.1.refs_0_), channel_id=1, source_target_pairs={{0,4},{4,8},{8,12},{12,14},{14,10},{10,6},{6,2},{2,0},{1,5},{5,9},... | collective-permute-start | bytes 562184 | tf_op jit(solution)/shard_map/ppermute | solution.py:305
  17.1 0.0 collective-permute-start.4
  17.1 0.0 collective-permute-done.3.refs_1_
  17.1 0.3 collective-permute-start.10
  17.4 0.0 collective-permute-done.7.refs_2_
  17.4 0.3 collective-permute-start.5
  17.7 0.0 collective-permute-done.8.refs_3_
  17.7 2.7 %shard_map.68 = (bf16[128,1440]{1,0:T(8,128)(2,1)S(1)}, bf16[128,1440]{1,0:T(8,128)(2,1)S(1)}) custom-call(s32[2]{0:T(128)S(1)} %pad_add_fusion.after_this.place, bf16[64,1464]{1,0:T(8,128)(2,1)S(1)} %collective-permute-done.refs_0_, bf16[64,1464]{1,0:T(8,128)(2,1)S(1)} %collective-permute-done.2.refs_1_, ...), custom_call_target="tpu_custom_call" | custom-call | flops 1592524800 | bytes 12441600 | tf_op jit(solution)/shard_map/pallas_call | solution.py:210
  20.4 1.3 %collective-permute-done.6.refs_1_ = bf16[64,1464]{1,0:T(8,128)(2,1)S(1)} collective-permute-done((bf16[64,1464]{1,0:T(8,128)(2,1)S(1)}, bf16[64,1464]{1,0:T(8,128)(2,1)S(1)}, u32[]{:S(2)}, u32[]{:S(2)}) %collective-permute-start.6) | collective-permute-done | bytes 187424 | tf_op jit(solution)/shard_map/ppermute | solution.py:305
  21.8 1.8 %collective-permute-start.9 = (bf16[64,1464]{1,0:T(8,128)(2,1)S(1)}, bf16[64,1464]{1,0:T(8,128)(2,1)S(1)}, u32[]{:S(2)}, u32[]{:S(2)}) collective-permute-start(bf16[64,1464]{1,0:T(8,128)(2,1)S(1)} %collective-permute-done.6.refs_1_), channel_id=1, source_target_pairs={{0,4},{4,8},{8,12},{12,14},{14,10},{10,6},{6,2},{2,0},{1,5},{5,9},... | collective-permute-start | bytes 562184 | tf_op jit(solution)/shard_map/ppermute | solution.py:305
  23.6 0.0 collective-permute-start.12
  23.6 0.8 %collective-permute-done.10.refs_2_ = bf16[64,1464]{1,0:T(8,128)(2,1)S(1)} collective-permute-done((bf16[64,1464]{1,0:T(8,128)(2,1)S(1)}, bf16[64,1464]{1,0:T(8,128)(2,1)S(1)}, u32[]{:S(2)}, u32[]{:S(2)}) %collective-permute-start.10) | collective-permute-done | bytes 187424 | tf_op jit(solution)/shard_map/ppermute | solution.py:307
  24.5 0.0 collective-permute-start.13
  24.5 0.0 collective-permute-done.4.refs_2_
  24.5 0.0 collective-permute-done.5.refs_3_
  24.5 2.7 %shard_map.67 = (bf16[128,1440]{1,0:T(8,128)(2,1)S(1)}, bf16[128,1440]{1,0:T(8,128)(2,1)S(1)}) custom-call(s32[2]{0:T(128)S(1)} %pad_add_fusion.after_this.place, bf16[64,1464]{1,0:T(8,128)(2,1)S(1)} %collective-permute-done.1.refs_0_, bf16[64,1464]{1,0:T(8,128)(2,1)S(1)} %collective-permute-done.3.refs_1_, ...), custom_call_target="tpu_custom_call" | custom-call | flops 1592524800 | bytes 12441600 | tf_op jit(solution)/shard_map/pallas_call | solution.py:210
  27.2 0.3 collective-permute-done.9.refs_0_
  27.5 0.2 collective-permute-start.11
  27.7 1.6 %shard_map.69 = (f32[192,720]{1,0:T(8,128)S(1)}, f32[192,720]{1,0:T(8,128)S(1)}) custom-call(s32[2]{0:T(128)S(1)} %pad_add_fusion.after_this.place, bf16[64,1464]{1,0:T(8,128)(2,1)S(1)} %collective-permute-done.9.refs_0_, bf16[64,1464]{1,0:T(8,128)(2,1)S(1)} %collective-permute-done.6.refs_1_, bf16[64,1464]{1,0:T(8,128)(2,1)S(1)} %collective-permute-done.10.refs_2_, ...), custom_call_target="tpu_custom_call" | custom-call | flops 796262400 | bytes 6220800 | tf_op jit(solution)/shard_map/pallas_call | solution.py:210
  29.4 0.0 collective-permute-done.13.refs_5_
  29.4 0.0 collective-permute-done.11.refs_3_
  29.4 2.2 %shard_map.70 = (bf16[192,720]{1,0:T(8,128)(2,1)S(1)}, bf16[64,1440]{1,0:T(8,128)(2,1)S(1)}, bf16[128,1440]{1,0:T(8,128)(2,1)S(1)}) custom-call(s32[2]{0:T(128)S(1)} %pad_add_fusion.after_this.place, bf16[64,1464]{1,0:T(8,128)(2,1)S(1)} %collective-permute-done.9.refs_0_, bf16[64,1464]{1,0:T(8,128)(2,1)S(1)} %collective-permute-done.6.refs_1_, ...), custom_call_target="tpu_custom_call" | custom-call | flops 1194393600 | bytes 9331200 | tf_op jit(solution)/shard_map/pallas_call | solution.py:210
  31.6 0.3 collective-permute-start.14
  32.0 0.2 collective-permute-start.20
  32.2 0.3 collective-permute-start.16
  32.5 1.2 %shard_map.71 = (bf16[64,1440]{1,0:T(8,128)(2,1)S(1)}, bf16[128,1440]{1,0:T(8,128)(2,1)S(1)}) custom-call(s32[2]{0:T(128)S(1)} %pad_add_fusion.after_this.place, bf16[64,1464]{1,0:T(8,128)(2,1)S(1)} %collective-permute-done.9.refs_0_, bf16[64,1464]{1,0:T(8,128)(2,1)S(1)} %collective-permute-done.6.refs_1_, ...), custom_call_target="tpu_custom_call" | custom-call | flops 398131200 | bytes 3110400 | tf_op jit(solution)/shard_map/pallas_call | solution.py:210
  33.7 2.0 %collective-permute-start.17 = (bf16[64,1440]{1,0:T(8,128)(2,1)S(1)}, bf16[64,1440]{1,0:T(8,128)(2,1)S(1)}, u32[]{:S(2)}, u32[]{:S(2)}) collective-permute-start(bf16[64,1440]{1,0:T(8,128)(2,1)S(1)} %fusion), channel_id=1, source_target_pairs={{0,4},{4,8},{8,12},{12,14},{14,10},{10,6},{6,2},{2,0},{1,5},{5,9},... | collective-permute-start | bytes 552968 | tf_op jit(solution)/shard_map/ppermute | solution.py:325
  35.7 0.5 collective-permute-start.15
  36.2 4.8 %collective-permute-done.17 = bf16[64,1440]{1,0:T(8,128)(2,1)S(1)} collective-permute-done((bf16[64,1440]{1,0:T(8,128)(2,1)S(1)}, bf16[64,1440]{1,0:T(8,128)(2,1)S(1)}, u32[]{:S(2)}, u32[]{:S(2)}) %collective-permute-start.17) | collective-permute-done | bytes 184352 | tf_op jit(solution)/shard_map/ppermute | solution.py:325
  41.0 0.1 add_convert_fusion.6
  41.1 1.7 %collective-permute-start.18 = (bf16[64,1440]{1,0:T(8,128)(2,1)S(1)}, bf16[64,1440]{1,0:T(8,128)(2,1)S(1)}, u32[]{:S(2)}, u32[]{:S(2)}) collective-permute-start(bf16[64,1440]{1,0:T(8,128)(2,1)S(1)} %add_convert_fusion.6), channel_id=1, source_target_pairs={{0,4},{4,8},{8,12},{12,14},{14,10},{10,6},{6,2},{2,0},{1,5},{5,9},... | collective-permute-start | bytes 552968 | tf_op jit(solution)/shard_map/ppermute | solution.py:325
  42.8 0.5 collective-permute-start.19
  43.3 0.0 collective-permute-done.15
  43.3 4.1 %collective-permute-done.18 = bf16[64,1440]{1,0:T(8,128)(2,1)S(1)} collective-permute-done((bf16[64,1440]{1,0:T(8,128)(2,1)S(1)}, bf16[64,1440]{1,0:T(8,128)(2,1)S(1)}, u32[]{:S(2)}, u32[]{:S(2)}) %collective-permute-start.18) | collective-permute-done | bytes 184352 | tf_op jit(solution)/shard_map/ppermute | solution.py:325
  47.3 0.1 add_convert_fusion.5
  47.4 1.5 %collective-permute-start.23 = (bf16[64,1440]{1,0:T(8,128)(2,1)S(1)}, bf16[64,1440]{1,0:T(8,128)(2,1)S(1)}, u32[]{:S(2)}, u32[]{:S(2)}) collective-permute-start(bf16[64,1440]{1,0:T(8,128)(2,1)S(1)} %add_convert_fusion.5), channel_id=1, source_target_pairs={{0,4},{4,8},{8,12},{12,14},{14,10},{10,6},{6,2},{2,0},{1,5},{5,9},... | collective-permute-start | bytes 552968 | tf_op jit(solution)/shard_map/ppermute | solution.py:325
  48.9 0.1 add_convert_fusion.3
  49.0 0.7 %collective-permute-start.25 = (bf16[64,1440]{1,0:T(8,128)(2,1)S(1)}, bf16[64,1440]{1,0:T(8,128)(2,1)S(1)}, u32[]{:S(2)}, u32[]{:S(2)}) collective-permute-start(bf16[64,1440]{1,0:T(8,128)(2,1)S(1)} %add_convert_fusion.3), channel_id=1, source_target_pairs={{4,0},{8,4},{12,8},{14,12},{10,14},{6,10},{2,6},{0,2},{5,1},{9,5},... | collective-permute-start | bytes 552968 | tf_op jit(solution)/shard_map/ppermute | solution.py:326
  49.6 0.0 collective-permute-done.22
  49.6 0.0 collective-permute-done.20.refs_1_
  49.6 2.7 %shard_map.72 = (bf16[64,1440]{1,0:T(8,128)(2,1)S(1)}, bf16[64,1440]{1,0:T(8,128)(2,1)S(1)}) custom-call(s32[2]{0:T(128)S(1)} %pad_add_fusion.after_this.place, bf16[64,1464]{1,0:T(8,128)(2,1)S(1)} %shard_map.64.refs_0_, bf16[64,1464]{1,0:T(8,128)(2,1)S(1)} %collective-permute-done.20.refs_1_, ...), custom_call_target="tpu_custom_call" | custom-call | flops 1592524800 | bytes 12441600 | tf_op jit(solution)/shard_map/pallas_call | solution.py:210
  52.3 0.1 collective-permute-start.21
  52.4 0.8 %collective-permute-done.23 = bf16[64,1440]{1,0:T(8,128)(2,1)S(1)} collective-permute-done((bf16[64,1440]{1,0:T(8,128)(2,1)S(1)}, bf16[64,1440]{1,0:T(8,128)(2,1)S(1)}, u32[]{:S(2)}, u32[]{:S(2)}) %collective-permute-start.23) | collective-permute-done | bytes 184352 | tf_op jit(solution)/shard_map/ppermute | solution.py:325
  53.1 0.1 add_convert_fusion.2
  53.2 1.5 %collective-permute-start.24 = (bf16[64,1440]{1,0:T(8,128)(2,1)S(1)}, bf16[64,1440]{1,0:T(8,128)(2,1)S(1)}, u32[]{:S(2)}, u32[]{:S(2)}) collective-permute-start(bf16[64,1440]{1,0:T(8,128)(2,1)S(1)} %add_convert_fusion.2), channel_id=1, source_target_pairs={{0,4},{4,8},{8,12},{12,14},{14,10},{10,6},{6,2},{2,0},{1,5},{5,9},... | collective-permute-start | bytes 552968 | tf_op jit(solution)/shard_map/ppermute | solution.py:325
  54.7 0.0 collective-permute-done.25
  54.7 0.1 add_convert_fusion.1
  54.8 0.7 %collective-permute-start.26 = (bf16[64,1440]{1,0:T(8,128)(2,1)S(1)}, bf16[64,1440]{1,0:T(8,128)(2,1)S(1)}, u32[]{:S(2)}, u32[]{:S(2)}) collective-permute-start(bf16[64,1440]{1,0:T(8,128)(2,1)S(1)} %add_convert_fusion.1), channel_id=1, source_target_pairs={{4,0},{8,4},{12,8},{14,12},{10,14},{6,10},{2,6},{0,2},{5,1},{9,5},... | collective-permute-start | bytes 552968 | tf_op jit(solution)/shard_map/ppermute | solution.py:326
  55.4 0.0 collective-permute-done.21
  55.4 4.4 %collective-permute-done.24 = bf16[64,1440]{1,0:T(8,128)(2,1)S(1)} collective-permute-done((bf16[64,1440]{1,0:T(8,128)(2,1)S(1)}, bf16[64,1440]{1,0:T(8,128)(2,1)S(1)}, u32[]{:S(2)}, u32[]{:S(2)}) %collective-permute-start.24) | collective-permute-done | bytes 184352 | tf_op jit(solution)/shard_map/ppermute | solution.py:325
  59.8 1.3 %collective-permute-done.26 = bf16[64,1440]{1,0:T(8,128)(2,1)S(1)} collective-permute-done((bf16[64,1440]{1,0:T(8,128)(2,1)S(1)}, bf16[64,1440]{1,0:T(8,128)(2,1)S(1)}, u32[]{:S(2)}, u32[]{:S(2)}) %collective-permute-start.26) | collective-permute-done | bytes 184352 | tf_op jit(solution)/shard_map/ppermute | solution.py:326
  61.1 0.8 %add_convert_fusion = bf16[64,1440]{1,0:T(8,128)(2,1)} fusion(bf16[64,1440]{1,0:T(8,128)(2,1)S(1)} %collective-permute-done.26, bf16[64,1440]{1,0:T(8,128)(2,1)S(1)} %collective-permute-done.24, bf16[64,1440]{1,0:T(8,128)(2,1)S(1)} %collective-permute-done.21, bf16[64,1440]{1,0:T(8,128)(2,1)S(1)} %get-tuple-element.71), kind=kLoop, calls=%fused_computation | loop fusion | flops 737280 | bytes 921600 | tf_op jit(solution)/shard_map/convert_element_type | solution.py:336
  (8 shorter events, 0.1 us)
Async XLA Ops:
  1.0 8.0 %collective-permute-start = (bf16[64,1464]{1,0:T(8,128)(2,1)S(1)}, bf16[64,1464]{1,0:T(8,128)(2,1)S(1)}, u32[]{:S(2)}, u32[]{:S(2)}) collective-permute-start(bf16[64,1464]{1,0:T(8,128)(2,1)S(1)} %shard_map.64.refs_0_), channel_id=1, source_target_pairs={{0,4},{4,8},{8,12},{12,14},{14,10},{10,6},{6,2},{2,0},{1,5},{5,9},... | collective-permute-start | bytes 562184 | tf_op jit(solution)/shard_map/ppermute | solution.py:299
  4.1 7.0 %collective-permute-start.2 = (bf16[64,1464]{1,0:T(8,128)(2,1)S(1)}, bf16[64,1464]{1,0:T(8,128)(2,1)S(1)}, u32[]{:S(2)}, u32[]{:S(2)}) collective-permute-start(bf16[64,1464]{1,0:T(8,128)(2,1)S(1)} %shard_map.64.refs_0_), channel_id=1, source_target_pairs={{4,0},{8,4},{12,8},{14,12},{10,14},{6,10},{2,6},{0,2},{5,1},{9,5},... | collective-permute-start | bytes 562184 | tf_op jit(solution)/shard_map/ppermute | solution.py:300
  9.0 6.4 %collective-permute-start.1 = (bf16[64,1464]{1,0:T(8,128)(2,1)S(1)}, bf16[64,1464]{1,0:T(8,128)(2,1)S(1)}, u32[]{:S(2)}, u32[]{:S(2)}) collective-permute-start(bf16[64,1464]{1,0:T(8,128)(2,1)S(1)} %collective-permute-done.refs_0_), channel_id=1, source_target_pairs={{0,4},{4,8},{8,12},{12,14},{14,10},{10,6},{6,2},{2,0},{1,5},{5,9},... | collective-permute-start | bytes 562184 | tf_op jit(solution)/shard_map/ppermute | solution.py:305
  11.1 6.1 %collective-permute-start.3 = (bf16[64,1464]{1,0:T(8,128)(2,1)S(1)}, bf16[64,1464]{1,0:T(8,128)(2,1)S(1)}, u32[]{:S(2)}, u32[]{:S(2)}) collective-permute-start(bf16[64,1464]{1,0:T(8,128)(2,1)S(1)} %collective-permute-done.2.refs_1_), channel_id=1, source_target_pairs={{4,0},{8,4},{12,8},{14,12},{10,14},{6,10},{2,6},{0,2},{5,1},{9,5},... | collective-permute-start | bytes 562184 | tf_op jit(solution)/shard_map/ppermute | solution.py:307
  11.1 6.4 %collective-permute-start.7 = (bf16[64,1464]{1,0:T(8,128)(2,1)S(1)}, bf16[64,1464]{1,0:T(8,128)(2,1)S(1)}, u32[]{:S(2)}, u32[]{:S(2)}) collective-permute-start(bf16[64,1464]{1,0:T(8,128)(2,1)S(1)} %collective-permute-done.refs_0_), channel_id=1, source_target_pairs={{0,1},{1,0},{2,3},{3,2},{4,5},{5,4},{6,7},{7,6},{8,9},{9,8},{10,11... | collective-permute-start | bytes 562184 | tf_op jit(solution)/shard_map/ppermute | solution.py:308
  11.1 6.7 %collective-permute-start.8 = (bf16[64,1464]{1,0:T(8,128)(2,1)S(1)}, bf16[64,1464]{1,0:T(8,128)(2,1)S(1)}, u32[]{:S(2)}, u32[]{:S(2)}) collective-permute-start(bf16[64,1464]{1,0:T(8,128)(2,1)S(1)} %collective-permute-done.2.refs_1_), channel_id=1, source_target_pairs={{0,1},{1,0},{2,3},{3,2},{4,5},{5,4},{6,7},{7,6},{8,9},{9,8},{10,11... | collective-permute-start | bytes 562184 | tf_op jit(solution)/shard_map/ppermute | solution.py:308
  15.4 6.4 %collective-permute-start.6 = (bf16[64,1464]{1,0:T(8,128)(2,1)S(1)}, bf16[64,1464]{1,0:T(8,128)(2,1)S(1)}, u32[]{:S(2)}, u32[]{:S(2)}) collective-permute-start(bf16[64,1464]{1,0:T(8,128)(2,1)S(1)} %collective-permute-done.1.refs_0_), channel_id=1, source_target_pairs={{0,4},{4,8},{8,12},{12,14},{14,10},{10,6},{6,2},{2,0},{1,5},{5,9},... | collective-permute-start | bytes 562184 | tf_op jit(solution)/shard_map/ppermute | solution.py:305
  17.1 7.3 %collective-permute-start.4 = (bf16[64,1464]{1,0:T(8,128)(2,1)S(1)}, bf16[64,1464]{1,0:T(8,128)(2,1)S(1)}, u32[]{:S(2)}, u32[]{:S(2)}) collective-permute-start(bf16[64,1464]{1,0:T(8,128)(2,1)S(1)} %collective-permute-done.1.refs_0_), channel_id=1, source_target_pairs={{0,1},{1,0},{2,3},{3,2},{4,5},{5,4},{6,7},{7,6},{8,9},{9,8},{10,11... | collective-permute-start | bytes 562184 | tf_op jit(solution)/shard_map/ppermute | solution.py:308
  17.1 7.3 %collective-permute-start.10 = (bf16[64,1464]{1,0:T(8,128)(2,1)S(1)}, bf16[64,1464]{1,0:T(8,128)(2,1)S(1)}, u32[]{:S(2)}, u32[]{:S(2)}) collective-permute-start(bf16[64,1464]{1,0:T(8,128)(2,1)S(1)} %collective-permute-done.3.refs_1_), channel_id=1, source_target_pairs={{4,0},{8,4},{12,8},{14,12},{10,14},{6,10},{2,6},{0,2},{5,1},{9,5},... | collective-permute-start | bytes 562184 | tf_op jit(solution)/shard_map/ppermute | solution.py:307
  17.4 7.0 %collective-permute-start.5 = (bf16[64,1464]{1,0:T(8,128)(2,1)S(1)}, bf16[64,1464]{1,0:T(8,128)(2,1)S(1)}, u32[]{:S(2)}, u32[]{:S(2)}) collective-permute-start(bf16[64,1464]{1,0:T(8,128)(2,1)S(1)} %collective-permute-done.3.refs_1_), channel_id=1, source_target_pairs={{0,1},{1,0},{2,3},{3,2},{4,5},{5,4},{6,7},{7,6},{8,9},{9,8},{10,11... | collective-permute-start | bytes 562184 | tf_op jit(solution)/shard_map/ppermute | solution.py:308
  21.8 5.7 %collective-permute-start.9 = (bf16[64,1464]{1,0:T(8,128)(2,1)S(1)}, bf16[64,1464]{1,0:T(8,128)(2,1)S(1)}, u32[]{:S(2)}, u32[]{:S(2)}) collective-permute-start(bf16[64,1464]{1,0:T(8,128)(2,1)S(1)} %collective-permute-done.6.refs_1_), channel_id=1, source_target_pairs={{0,4},{4,8},{8,12},{12,14},{14,10},{10,6},{6,2},{2,0},{1,5},{5,9},... | collective-permute-start | bytes 562184 | tf_op jit(solution)/shard_map/ppermute | solution.py:305
  23.6 5.8 %collective-permute-start.12 = (bf16[64,1464]{1,0:T(8,128)(2,1)S(1)}, bf16[64,1464]{1,0:T(8,128)(2,1)S(1)}, u32[]{:S(2)}, u32[]{:S(2)}) collective-permute-start(bf16[64,1464]{1,0:T(8,128)(2,1)S(1)} %collective-permute-done.6.refs_1_), channel_id=1, source_target_pairs={{0,1},{1,0},{2,3},{3,2},{4,5},{5,4},{6,7},{7,6},{8,9},{9,8},{10,11... | collective-permute-start | bytes 562184 | tf_op jit(solution)/shard_map/ppermute | solution.py:308
  24.5 4.9 %collective-permute-start.13 = (bf16[64,1464]{1,0:T(8,128)(2,1)S(1)}, bf16[64,1464]{1,0:T(8,128)(2,1)S(1)}, u32[]{:S(2)}, u32[]{:S(2)}) collective-permute-start(bf16[64,1464]{1,0:T(8,128)(2,1)S(1)} %collective-permute-done.10.refs_2_), channel_id=1, source_target_pairs={{0,1},{1,0},{2,3},{3,2},{4,5},{5,4},{6,7},{7,6},{8,9},{9,8},{10,11... | collective-permute-start | bytes 562184 | tf_op jit(solution)/shard_map/ppermute | solution.py:308
  27.5 1.9 %collective-permute-start.11 = (bf16[64,1464]{1,0:T(8,128)(2,1)S(1)}, bf16[64,1464]{1,0:T(8,128)(2,1)S(1)}, u32[]{:S(2)}, u32[]{:S(2)}) collective-permute-start(bf16[64,1464]{1,0:T(8,128)(2,1)S(1)} %collective-permute-done.9.refs_0_), channel_id=1, source_target_pairs={{0,1},{1,0},{2,3},{3,2},{4,5},{5,4},{6,7},{7,6},{8,9},{9,8},{10,11... | collective-permute-start | bytes 562184 | tf_op jit(solution)/shard_map/ppermute | solution.py:316
  31.6 2.0 %collective-permute-start.14 = (bf16[64,1440]{1,0:T(8,128)(2,1)S(1)}, bf16[64,1440]{1,0:T(8,128)(2,1)S(1)}, u32[]{:S(2)}, u32[]{:S(2)}) collective-permute-start(bf16[64,1440]{1,0:T(8,128)(2,1)S(1)} %get-tuple-element.62), channel_id=1, source_target_pairs={{0,1},{1,0},{2,3},{3,2},{4,5},{5,4},{6,7},{7,6},{8,9},{9,8},{10,11... | collective-permute-start | bytes 552968 | tf_op jit(solution)/shard_map/ppermute | solution.py:259
  32.0 17.7 %collective-permute-start.20 = (bf16[64,1464]{1,0:T(8,128)(2,1)S(1)}, bf16[64,1464]{1,0:T(8,128)(2,1)S(1)}, u32[]{:S(2)}, u32[]{:S(2)}) collective-permute-start(bf16[64,1464]{1,0:T(8,128)(2,1)S(1)} %shard_map.64.refs_0_), channel_id=1, source_target_pairs={{0,1},{1,0},{2,3},{3,2},{4,5},{5,4},{6,7},{7,6},{8,9},{9,8},{10,11... | collective-permute-start | bytes 562184 | tf_op jit(solution)/shard_map/ppermute | solution.py:301
  32.2 4.0 %collective-permute-start.16 = (bf16[128,1440]{1,0:T(8,128)(2,1)S(1)}, bf16[128,1440]{1,0:T(8,128)(2,1)S(1)}, u32[]{:S(2)}, u32[]{:S(2)}) collective-permute-start(bf16[128,1440]{1,0:T(8,128)(2,1)S(1)} %get-tuple-element.67), channel_id=1, source_target_pairs={{0,1},{1,0},{2,3},{3,2},{4,5},{5,4},{6,7},{7,6},{8,9},{9,8},{10,11... | collective-permute-start | bytes 1105928 | tf_op jit(solution)/shard_map/ppermute | solution.py:259
  33.7 7.3 %collective-permute-start.17 = (bf16[64,1440]{1,0:T(8,128)(2,1)S(1)}, bf16[64,1440]{1,0:T(8,128)(2,1)S(1)}, u32[]{:S(2)}, u32[]{:S(2)}) collective-permute-start(bf16[64,1440]{1,0:T(8,128)(2,1)S(1)} %fusion), channel_id=1, source_target_pairs={{0,4},{4,8},{8,12},{12,14},{14,10},{10,6},{6,2},{2,0},{1,5},{5,9},... | collective-permute-start | bytes 552968 | tf_op jit(solution)/shard_map/ppermute | solution.py:325
  35.7 13.9 %collective-permute-start.22 = (bf16[128,1440]{1,0:T(8,128)(2,1)S(1)}, bf16[128,1440]{1,0:T(8,128)(2,1)S(1)}, u32[]{:S(2)}, u32[]{:S(2)}) collective-permute-start(bf16[128,1440]{1,0:T(8,128)(2,1)S(1)} %get-tuple-element.74), channel_id=1, source_target_pairs={{0,1},{1,0},{2,3},{3,2},{4,5},{5,4},{6,7},{7,6},{8,9},{9,8},{10,11... | collective-permute-start | bytes 1105928 | tf_op jit(solution)/shard_map/ppermute | solution.py:321
  35.7 7.5 %collective-permute-start.15 = (bf16[128,1440]{1,0:T(8,128)(2,1)S(1)}, bf16[128,1440]{1,0:T(8,128)(2,1)S(1)}, u32[]{:S(2)}, u32[]{:S(2)}) collective-permute-start(bf16[128,1440]{1,0:T(8,128)(2,1)S(1)} %get-tuple-element.63), channel_id=1, source_target_pairs={{0,1},{1,0},{2,3},{3,2},{4,5},{5,4},{6,7},{7,6},{8,9},{9,8},{10,11... | collective-permute-start | bytes 1105928 | tf_op jit(solution)/shard_map/ppermute | solution.py:321
  41.1 6.3 %collective-permute-start.18 = (bf16[64,1440]{1,0:T(8,128)(2,1)S(1)}, bf16[64,1440]{1,0:T(8,128)(2,1)S(1)}, u32[]{:S(2)}, u32[]{:S(2)}) collective-permute-start(bf16[64,1440]{1,0:T(8,128)(2,1)S(1)} %add_convert_fusion.6), channel_id=1, source_target_pairs={{0,4},{4,8},{8,12},{12,14},{14,10},{10,6},{6,2},{2,0},{1,5},{5,9},... | collective-permute-start | bytes 552968 | tf_op jit(solution)/shard_map/ppermute | solution.py:325
  42.8 6.1 %collective-permute-start.19 = (bf16[64,1440]{1,0:T(8,128)(2,1)S(1)}, bf16[64,1440]{1,0:T(8,128)(2,1)S(1)}, u32[]{:S(2)}, u32[]{:S(2)}) collective-permute-start(bf16[64,1440]{1,0:T(8,128)(2,1)S(1)} %add_convert_fusion.4), channel_id=1, source_target_pairs={{4,0},{8,4},{12,8},{14,12},{10,14},{6,10},{2,6},{0,2},{5,1},{9,5},... | collective-permute-start | bytes 552968 | tf_op jit(solution)/shard_map/ppermute | solution.py:326
  47.4 5.7 %collective-permute-start.23 = (bf16[64,1440]{1,0:T(8,128)(2,1)S(1)}, bf16[64,1440]{1,0:T(8,128)(2,1)S(1)}, u32[]{:S(2)}, u32[]{:S(2)}) collective-permute-start(bf16[64,1440]{1,0:T(8,128)(2,1)S(1)} %add_convert_fusion.5), channel_id=1, source_target_pairs={{0,4},{4,8},{8,12},{12,14},{14,10},{10,6},{6,2},{2,0},{1,5},{5,9},... | collective-permute-start | bytes 552968 | tf_op jit(solution)/shard_map/ppermute | solution.py:325
  49.0 5.7 %collective-permute-start.25 = (bf16[64,1440]{1,0:T(8,128)(2,1)S(1)}, bf16[64,1440]{1,0:T(8,128)(2,1)S(1)}, u32[]{:S(2)}, u32[]{:S(2)}) collective-permute-start(bf16[64,1440]{1,0:T(8,128)(2,1)S(1)} %add_convert_fusion.3), channel_id=1, source_target_pairs={{4,0},{8,4},{12,8},{14,12},{10,14},{6,10},{2,6},{0,2},{5,1},{9,5},... | collective-permute-start | bytes 552968 | tf_op jit(solution)/shard_map/ppermute | solution.py:326
  52.3 3.1 %collective-permute-start.21 = (bf16[64,1440]{1,0:T(8,128)(2,1)S(1)}, bf16[64,1440]{1,0:T(8,128)(2,1)S(1)}, u32[]{:S(2)}, u32[]{:S(2)}) collective-permute-start(bf16[64,1440]{1,0:T(8,128)(2,1)S(1)} %get-tuple-element.72), channel_id=1, source_target_pairs={{0,1},{1,0},{2,3},{3,2},{4,5},{5,4},{6,7},{7,6},{8,9},{9,8},{10,11... | collective-permute-start | bytes 552968 | tf_op jit(solution)/shard_map/ppermute | solution.py:330
  53.2 6.6 %collective-permute-start.24 = (bf16[64,1440]{1,0:T(8,128)(2,1)S(1)}, bf16[64,1440]{1,0:T(8,128)(2,1)S(1)}, u32[]{:S(2)}, u32[]{:S(2)}) collective-permute-start(bf16[64,1440]{1,0:T(8,128)(2,1)S(1)} %add_convert_fusion.2), channel_id=1, source_target_pairs={{0,4},{4,8},{8,12},{12,14},{14,10},{10,6},{6,2},{2,0},{1,5},{5,9},... | collective-permute-start | bytes 552968 | tf_op jit(solution)/shard_map/ppermute | solution.py:325
  54.8 6.3 %collective-permute-start.26 = (bf16[64,1440]{1,0:T(8,128)(2,1)S(1)}, bf16[64,1440]{1,0:T(8,128)(2,1)S(1)}, u32[]{:S(2)}, u32[]{:S(2)}) collective-permute-start(bf16[64,1440]{1,0:T(8,128)(2,1)S(1)} %add_convert_fusion.1), channel_id=1, source_target_pairs={{4,0},{8,4},{12,8},{14,12},{10,14},{6,10},{2,6},{0,2},{5,1},{9,5},... | collective-permute-start | bytes 552968 | tf_op jit(solution)/shard_map/ppermute | solution.py:326

commit v10 on v9

--- a/solution.py
+++ b/solution.py
@@ -296,37 +296,45 @@
             start = span.stop
             value[k] = mine[span].astype(jnp.float32) + theirs[span].astype(jnp.float32)
 
-    came[1] = lax.ppermute(packed, "ep", ahead)
-    came[-1] = lax.ppermute(packed, "ep", back)
     across[0] = swap(packed)
     weights, done, near = [gate, up], up, []
-    for k in range(2, far + 1):
-        came[k - 1], came[1 - k] = after(came[k - 1], done), after(came[1 - k], done)
-        came[k] = lax.ppermute(came[k - 1], "ep", ahead)
-        if k < far:
-            came[-k] = lax.ppermute(came[1 - k], "ep", back)
-        across[k - 1], across[1 - k] = swap(came[k - 1]), swap(came[1 - k])
+    for k in range(1, far + 1):
+        came[k - 1] = after(came[k - 1], done) if k > 1 else packed
+        if k < far - 1:
+            came[k] = lax.ppermute(came[k - 1], "ep", ahead)
+        if k != far - 1:
+            j = min(k, far - 1)
+            came[1 - j] = after(came[1 - j], done if k < far else (done, came[k - 1])) if k > 1 else packed
+            came[-j] = lax.ppermute(came[1 - j], "ep", back)
+        if k >= far - 1:
+            came[k] = lax.ppermute(came[k - 1], "ep", ahead)
+        if k > 1:
+            across[k - 1] = swap(came[k - 1])
+        if 1 < k < far:
+            across[1 - k] = swap(came[1 - k])
         if k == 2:
             weights += halve_weights(after(place, came[1]), w_down[0])
             done = weights[-1]
-        else:
-            near += run([k - 2, 2 - k])
+        elif k > 2:
+            near += run([k - 2, 2 - k], across[0] if k == 3 else None)
             done = near[-1][-1]
-    came[far] = after(came[far], done)
-    across[far] = swap(came[far])
-    last = [far, far - 1, 1 - far]
-    for keys, mine, theirs in zip(([far], last[1:]), *run_expert_in_stages(place, [came[k] for k in last], [across[k] for k in last], swap, weights, n)):
-        keep(keys, mine, theirs)
-    for keys, mine, theirs in near:
-        keep(keys, mine, swap(after(theirs, value[far])))
+    last = [far, 1 - far]
+    for k in last:
+        came[k] = after(came[k], done)
+        across[k] = swap(came[k])
+    mine, theirs = run_expert_in_stages(place, [came[k] for k in last], [across[k] for k in last], swap, weights, n)
+    for k, m, t in zip(last, mine, theirs):
+        keep([k], m, t)
+    for keys, m, t in near:
+        keep(keys, m, swap(after(t, value[far])))
 
     to_ahead, to_back = value[far].astype(jnp.bfloat16), None
     for k in range(far - 1, -1, -1):
         behind = lax.ppermute(to_ahead, "ep", ahead).astype(jnp.float32)
         front = 0.0 if to_back is None else lax.ppermute(to_back, "ep", back).astype(jnp.float32)
         done = None
-        if k == 1:
-            ((keys, mine, done),) = run([0], (to_ahead, to_back))
+        if k == far - 1:
+            ((keys, mine, done),) = run([k, 0], to_ahead)
             keep(keys, mine, swap(done))
         if k:
             to_ahead = (value[-k] + behind).astype(jnp.bfloat16)

time: 62 us -> 62.3 us (level)
  waiting for transfers between devices: 18.5 us -> 20.7 us
  starting transfers between devices: 19.9 us -> 18.8 us
  Pallas kernels: 22 us -> 21.1 us
    ppermute x4, starting transfers between devices: 6.6 us -> 3.6 us  [ring_body(): behind = lax.ppermute(to_ahead, 'ep', ahead).astype(jnp.float32)]
    ppermute x3, starting transfers between devices: 1.78 us -> 3.83 us  [ring_body(): lax.ppermute(to_back, 'ep', back).astype(jnp.float32)]
    ppermute x13 -> x12, waiting for transfers between devices: 0.88 us -> 2.9 us  [the longest x3 2.88 us: ring_body(): came[-j] = lax.ppermute(came[1 - j], 'ep', back)]
    ppermute x3 -> x4, starting transfers between devices: 5.64 us -> 7.26 us  [ring_body(): came[k] = lax.ppermute(came[k - 1], 'ep', ahead)]
    ppermute x13 -> x12, starting transfers between devices: 4.92 us -> 3.69 us  [the longest x3 1.72 us: ring_body(): came[-j] = lax.ppermute(came[1 - j], 'ep', back)]
    pallas_call x6, Pallas kernels: 13.1 us -> 12.2 us  [call(): pl.pallas_call(kernel, out_shape=out_shape, in_specs=[pl.BlockSpec(memory...]
    ppermute x3 -> x4, waiting for transfers between devices: 2.37 us -> 2.55 us  [ring_body(): came[k] = lax.ppermute(came[k - 1], 'ep', ahead)]
  transfers between devices with their start and end apart: 27 -> 27, of which waited for: 9 -> 10; matrix products, arithmetic and copies ran while one was open for 1% -> 1% of each run, Pallas kernels for 30% -> 30%
where the time goes in v10:
time: 62.3 us; the launch traced here: 62.2 us
  Pallas kernels  21.1 us (34%)
  waiting for transfers between devices  20.7 us (33%)
  starting transfers between devices  18.8 us (30%)
  other arithmetic  1.32 us (2%)
    ppermute x4, waiting for transfers between devices, ring_body(): behind = lax.ppermute(to_ahead, 'ep', ahead).astype(jnp.float32)  14.3 us
    pallas_call x6, Pallas kernels, call(): pl.pallas_call(kernel, out_shape=out_shape, in_specs=[pl.BlockSpec(memory...  12.2 us
    ppermute x4, starting transfers between devices, ring_body(): came[k] = lax.ppermute(came[k - 1], 'ep', ahead)  7.26 us
    pallas_call x1, Pallas kernels, turn_weights(): pl.pallas_call(turn_kernel, out_shape=[in_vmem((width, hidden))] * 2, in_...  4.79 us
    ppermute x3, starting transfers between devices, ring_body(): lax.ppermute(to_back, 'ep', back).astype(jnp.float32)  3.83 us
    ppermute x4, starting transfers between devices, ring_body(): behind = lax.ppermute(to_ahead, 'ep', ahead).astype(jnp.float32)  3.6 us
    pallas_call x1, Pallas kernels, halve_weights(): pl.pallas_call(halve_kernel, out_shape=[in_vmem((hidden, width // 2))] *...  3.13 us
    ppermute x3, waiting for transfers between devices, ring_body(): came[-j] = lax.ppermute(came[1 - j], 'ep', back)  2.88 us
  transfers between devices with their start and end apart: 27, of which 10 were waited for; matrix products, arithmetic and copies ran while one was open for 1% of the time, Pallas kernels for 30%

profile of v10, /device:TPU:0, one launch (start us, length us, event | category | flops | bytes accessed | tf_op | source)
XLA Modules:
  0.0 62.2 jit_solution(16125963555329293626)
XLA Ops:
  0.0 1.0 %shard_map.64.refs_1_ = bf16[64,1464]{1,0:T(8,128)(2,1)S(1)} custom-call(bf16[64,1440]{1,0:T(8,128)(2,1)} %tokens_in.1, s32[4,64]{1,0:T(4,128)} %bitcast.14, f32[4,64]{1,0:T(4,128)} %bitcast.15), custom_call_target="tpu_custom_call" | custom-call | tf_op jit(solution)/shard_map/pallas_call | solution.py:53
  1.0 3.1 %collective-permute-start = (bf16[64,1464]{1,0:T(8,128)(2,1)S(1)}, bf16[64,1464]{1,0:T(8,128)(2,1)S(1)}, u32[]{:S(2)}, u32[]{:S(2)}) collective-permute-start(bf16[64,1464]{1,0:T(8,128)(2,1)S(1)} %shard_map.64.refs_1_), channel_id=1, source_target_pairs={{0,4},{4,8},{8,12},{12,14},{14,10},{10,6},{6,2},{2,0},{1,5},{5,9},... | collective-permute-start | bytes 562184 | tf_op jit(solution)/shard_map/ppermute | solution.py:304
  4.1 0.0 collective-permute-start.4
  4.1 0.1 pad_add_fusion.after_this.place
  4.2 4.8 %shard_map.65 = (bf16[2880,720]{1,0:T(8,128)(2,1)S(1)}, bf16[2880,720]{1,0:T(8,128)(2,1)S(1)}) custom-call(s32[2]{0:T(128)S(1)} %pad_add_fusion.after_this.place, bf16[720,2880]{1,0:T(8,128)(2,1)} %bitcast.11, bf16[720,2880]{1,0:T(8,128)(2,1)} %bitcast.12), custom_call_target="tpu_custom_call" | custom-call | bytes 16588800 | tf_op jit(solution)/shard_map/pallas_call | solution.py:83
  9.0 0.0 collective-permute-done.refs_0_
  9.0 2.1 %collective-permute-start.1 = (bf16[64,1464]{1,0:T(8,128)(2,1)S(1)}, bf16[64,1464]{1,0:T(8,128)(2,1)S(1)}, u32[]{:S(2)}, u32[]{:S(2)}) collective-permute-start(bf16[64,1464]{1,0:T(8,128)(2,1)S(1)} %collective-permute-done.refs_0_), channel_id=1, source_target_pairs={{0,4},{4,8},{8,12},{12,14},{14,10},{10,6},{6,2},{2,0},{1,5},{5,9},... | collective-permute-start | bytes 562184 | tf_op jit(solution)/shard_map/ppermute | solution.py:304
  11.0 0.0 collective-permute-start.3
  11.1 0.0 collective-permute-done.4.refs_1_
  11.1 0.1 collective-permute-start.8
  11.1 0.4 collective-permute-start.5
  11.6 0.1 collective-permute-start.6
  11.6 3.1 %shard_map.66 = (bf16[720,1440]{1,0:T(8,128)(2,1)S(1)}, bf16[720,1440]{1,0:T(8,128)(2,1)S(1)}) custom-call(s32[2]{0:T(128)S(1)} %pad_add_fusion.after_this.place, bf16[720,2880]{1,0:T(8,128)(2,1)} %bitcast.13), custom_call_target="tpu_custom_call" | custom-call | bytes 16588800 | tf_op jit(solution)/shard_map/pallas_call | solution.py:120
  14.8 0.6 collective-permute-done.1.refs_0_
  15.4 1.7 %collective-permute-start.2 = (bf16[64,1464]{1,0:T(8,128)(2,1)S(1)}, bf16[64,1464]{1,0:T(8,128)(2,1)S(1)}, u32[]{:S(2)}, u32[]{:S(2)}) collective-permute-start(bf16[64,1464]{1,0:T(8,128)(2,1)S(1)} %collective-permute-done.1.refs_0_), channel_id=1, source_target_pairs={{0,4},{4,8},{8,12},{12,14},{14,10},{10,6},{6,2},{2,0},{1,5},{5,9},... | collective-permute-start | bytes 562184 | tf_op jit(solution)/shard_map/ppermute | solution.py:310
  17.1 0.0 collective-permute-done.3.refs_3_
  17.1 0.0 collective-permute-start.9
  17.1 1.2 %collective-permute-done.8.refs_1_ = bf16[64,1464]{1,0:T(8,128)(2,1)S(1)} collective-permute-done((bf16[64,1464]{1,0:T(8,128)(2,1)S(1)}, bf16[64,1464]{1,0:T(8,128)(2,1)S(1)}, u32[]{:S(2)}, u32[]{:S(2)}) %collective-permute-start.8) | collective-permute-done | bytes 187424 | tf_op jit(solution)/shard_map/ppermute | solution.py:308
  18.4 0.0 collective-permute-start.10
  18.4 0.0 collective-permute-done.5.refs_2_
  18.4 2.7 %shard_map.67 = (bf16[128,1440]{1,0:T(8,128)(2,1)S(1)}, bf16[128,1440]{1,0:T(8,128)(2,1)S(1)}) custom-call(s32[2]{0:T(128)S(1)} %pad_add_fusion.after_this.place, bf16[64,1464]{1,0:T(8,128)(2,1)S(1)} %collective-permute-done.refs_0_, bf16[64,1464]{1,0:T(8,128)(2,1)S(1)} %collective-permute-done.4.refs_1_, ...), custom_call_target="tpu_custom_call" | custom-call | flops 1592524800 | bytes 12441600 | tf_op jit(solution)/shard_map/pallas_call | solution.py:210
  21.1 1.0 %collective-permute-done.2.refs_0_ = bf16[64,1464]{1,0:T(8,128)(2,1)S(1)} collective-permute-done((bf16[64,1464]{1,0:T(8,128)(2,1)S(1)}, bf16[64,1464]{1,0:T(8,128)(2,1)S(1)}, u32[]{:S(2)}, u32[]{:S(2)}) %collective-permute-start.2) | collective-permute-done | bytes 187424 | tf_op jit(solution)/shard_map/ppermute | solution.py:310
  22.1 1.7 %collective-permute-start.11 = (bf16[64,1464]{1,0:T(8,128)(2,1)S(1)}, bf16[64,1464]{1,0:T(8,128)(2,1)S(1)}, u32[]{:S(2)}, u32[]{:S(2)}) collective-permute-start(bf16[64,1464]{1,0:T(8,128)(2,1)S(1)} %collective-permute-done.8.refs_1_), channel_id=1, source_target_pairs={{4,0},{8,4},{12,8},{14,12},{10,14},{6,10},{2,6},{0,2},{5,1},{9,5},... | collective-permute-start | bytes 562184 | tf_op jit(solution)/shard_map/ppermute | solution.py:308
  23.7 0.4 collective-permute-start.7
  24.1 0.0 collective-permute-done.9.refs_2_
  24.1 0.0 collective-permute-done.10.refs_3_
  24.1 2.7 %shard_map.68 = (bf16[128,1440]{1,0:T(8,128)(2,1)S(1)}, bf16[128,1440]{1,0:T(8,128)(2,1)S(1)}) custom-call(s32[2]{0:T(128)S(1)} %pad_add_fusion.after_this.place, bf16[64,1464]{1,0:T(8,128)(2,1)S(1)} %collective-permute-done.1.refs_0_, bf16[64,1464]{1,0:T(8,128)(2,1)S(1)} %collective-permute-done.8.refs_1_, ...), custom_call_target="tpu_custom_call" | custom-call | flops 1592524800 | bytes 12441600 | tf_op jit(solution)/shard_map/pallas_call | solution.py:210
  26.8 1.6 %collective-permute-done.11.refs_1_ = bf16[64,1464]{1,0:T(8,128)(2,1)S(1)} collective-permute-done((bf16[64,1464]{1,0:T(8,128)(2,1)S(1)}, bf16[64,1464]{1,0:T(8,128)(2,1)S(1)}, u32[]{:S(2)}, u32[]{:S(2)}) %collective-permute-start.11) | collective-permute-done | bytes 187424 | tf_op jit(solution)/shard_map/ppermute | solution.py:308
  28.5 0.9 %collective-permute-done.7.refs_0_ = bf16[64,1464]{1,0:T(8,128)(2,1)S(1)} collective-permute-done((bf16[64,1464]{1,0:T(8,128)(2,1)S(1)}, bf16[64,1464]{1,0:T(8,128)(2,1)S(1)}, u32[]{:S(2)}, u32[]{:S(2)}) %collective-permute-start.7) | collective-permute-done | bytes 187424 | tf_op jit(solution)/shard_map/ppermute | solution.py:310
  29.4 0.0 collective-permute-start.13
  29.4 0.5 collective-permute-start.12
  29.9 1.3 %shard_map.69 = (f32[128,720]{1,0:T(8,128)S(1)}, f32[128,720]{1,0:T(8,128)S(1)}) custom-call(s32[2]{0:T(128)S(1)} %pad_add_fusion.after_this.place, bf16[64,1464]{1,0:T(8,128)(2,1)S(1)} %collective-permute-done.7.refs_0_, bf16[64,1464]{1,0:T(8,128)(2,1)S(1)} %collective-permute-done.11.refs_1_, ...), custom_call_target="tpu_custom_call" | custom-call | flops 530841600 | bytes 4147200 | tf_op jit(solution)/shard_map/pallas_call | solution.py:210
  31.3 1.8 %shard_map.70 = (bf16[128,720]{1,0:T(8,128)(2,1)S(1)}, bf16[64,1440]{1,0:T(8,128)(2,1)S(1)}, bf16[64,1440]{1,0:T(8,128)(2,1)S(1)}) custom-call(s32[2]{0:T(128)S(1)} %pad_add_fusion.after_this.place, bf16[64,1464]{1,0:T(8,128)(2,1)S(1)} %collective-permute-done.7.refs_0_, bf16[64,1464]{1,0:T(8,128)(2,1)S(1)} %collective-permute-done.11.refs_1_, ...), custom_call_target="tpu_custom_call" | custom-call | flops 796262400 | bytes 6220800 | tf_op jit(solution)/shard_map/pallas_call | solution.py:210
  33.0 0.2 collective-permute-start.14
  33.2 0.4 collective-permute-start.15
  33.6 0.1 collective-permute-start.19
  33.7 1.0 %shard_map.71 = (bf16[64,1440]{1,0:T(8,128)(2,1)S(1)}, bf16[64,1440]{1,0:T(8,128)(2,1)S(1)}) custom-call(s32[2]{0:T(128)S(1)} %pad_add_fusion.after_this.place, bf16[64,1464]{1,0:T(8,128)(2,1)S(1)} %collective-permute-done.7.refs_0_, bf16[64,1464]{1,0:T(8,128)(2,1)S(1)} %collective-permute-done.11.refs_1_, bf16[128,720]{1,0:T(8,128)(2,1)S(1)} %get-tuple-element.61.refs_2_, ...), custom_call_target="tpu_custom_call" | custom-call | flops 265420800 | bytes 2073600 | tf_op jit(solution)/shard_map/pallas_call | solution.py:210
  34.8 1.0 %collective-permute-start.20 = (bf16[64,1440]{1,0:T(8,128)(2,1)S(1)}, bf16[64,1440]{1,0:T(8,128)(2,1)S(1)}, u32[]{:S(2)}, u32[]{:S(2)}) collective-permute-start(bf16[64,1440]{1,0:T(8,128)(2,1)S(1)} %fusion), channel_id=1, source_target_pairs={{0,4},{4,8},{8,12},{12,14},{14,10},{10,6},{6,2},{2,0},{1,5},{5,9},... | collective-permute-start | bytes 552968 | tf_op jit(solution)/shard_map/ppermute | solution.py:333
  35.8 2.7 %shard_map.72 = (bf16[128,1440]{1,0:T(8,128)(2,1)S(1)}, bf16[128,1440]{1,0:T(8,128)(2,1)S(1)}) custom-call(s32[2]{0:T(128)S(1)} %pad_add_fusion.after_this.place, bf16[64,1464]{1,0:T(8,128)(2,1)S(1)} %collective-permute-done.2.refs_0_, bf16[64,1464]{1,0:T(8,128)(2,1)S(1)} %shard_map.64.refs_1_, bf16[64,1464]{1,0:T(8,128)(2,1)S(1)} %collective-permute-done.15.refs_2_, ...), custom_call_target="tpu_custom_call" | custom-call | flops 1592524800 | bytes 12441600 | tf_op jit(solution)/shard_map/pallas_call | solution.py:210
  38.5 0.2 collective-permute-start.16
  38.8 0.4 collective-permute-start.17
  39.1 0.2 collective-permute-start.18
  39.3 0.0 collective-permute-done.19
  39.3 3.0 %collective-permute-done.20 = bf16[64,1440]{1,0:T(8,128)(2,1)S(1)} collective-permute-done((bf16[64,1440]{1,0:T(8,128)(2,1)S(1)}, bf16[64,1440]{1,0:T(8,128)(2,1)S(1)}, u32[]{:S(2)}, u32[]{:S(2)}) %collective-permute-start.20) | collective-permute-done | bytes 184352 | tf_op jit(solution)/shard_map/ppermute | solution.py:333
  42.3 0.1 add_convert_fusion.6
  42.4 0.9 %collective-permute-start.21 = (bf16[64,1440]{1,0:T(8,128)(2,1)S(1)}, bf16[64,1440]{1,0:T(8,128)(2,1)S(1)}, u32[]{:S(2)}, u32[]{:S(2)}) collective-permute-start(bf16[64,1440]{1,0:T(8,128)(2,1)S(1)} %add_convert_fusion.6), channel_id=1, source_target_pairs={{0,4},{4,8},{8,12},{12,14},{14,10},{10,6},{6,2},{2,0},{1,5},{5,9},... | collective-permute-start | bytes 552968 | tf_op jit(solution)/shard_map/ppermute | solution.py:333
  43.2 0.0 collective-permute-done.16
  43.3 0.0 collective-permute-done.18
  43.3 1.3 %collective-permute-start.24 = (bf16[64,1440]{1,0:T(8,128)(2,1)S(1)}, bf16[64,1440]{1,0:T(8,128)(2,1)S(1)}, u32[]{:S(2)}, u32[]{:S(2)}) collective-permute-start(bf16[64,1440]{1,0:T(8,128)(2,1)S(1)} %add_convert_fusion.3), channel_id=1, source_target_pairs={{4,0},{8,4},{12,8},{14,12},{10,14},{6,10},{2,6},{0,2},{5,1},{9,5},... | collective-permute-start | bytes 552968 | tf_op jit(solution)/shard_map/ppermute | solution.py:334
  44.6 4.3 %collective-permute-done.21 = bf16[64,1440]{1,0:T(8,128)(2,1)S(1)} collective-permute-done((bf16[64,1440]{1,0:T(8,128)(2,1)S(1)}, bf16[64,1440]{1,0:T(8,128)(2,1)S(1)}, u32[]{:S(2)}, u32[]{:S(2)}) %collective-permute-start.21) | collective-permute-done | bytes 184352 | tf_op jit(solution)/shard_map/ppermute | solution.py:333
  48.9 0.1 add_convert_fusion.5
  48.9 0.9 %collective-permute-start.22 = (bf16[64,1440]{1,0:T(8,128)(2,1)S(1)}, bf16[64,1440]{1,0:T(8,128)(2,1)S(1)}, u32[]{:S(2)}, u32[]{:S(2)}) collective-permute-start(bf16[64,1440]{1,0:T(8,128)(2,1)S(1)} %add_convert_fusion.5), channel_id=1, source_target_pairs={{0,4},{4,8},{8,12},{12,14},{14,10},{10,6},{6,2},{2,0},{1,5},{5,9},... | collective-permute-start | bytes 552968 | tf_op jit(solution)/shard_map/ppermute | solution.py:333
  49.8 0.0 collective-permute-done.24
  49.8 0.1 add_convert_fusion.2
  49.9 1.3 %collective-permute-start.25 = (bf16[64,1440]{1,0:T(8,128)(2,1)S(1)}, bf16[64,1440]{1,0:T(8,128)(2,1)S(1)}, u32[]{:S(2)}, u32[]{:S(2)}) collective-permute-start(bf16[64,1440]{1,0:T(8,128)(2,1)S(1)} %add_convert_fusion.2), channel_id=1, source_target_pairs={{4,0},{8,4},{12,8},{14,12},{10,14},{6,10},{2,6},{0,2},{5,1},{9,5},... | collective-permute-start | bytes 552968 | tf_op jit(solution)/shard_map/ppermute | solution.py:334
  51.2 3.5 %collective-permute-done.22 = bf16[64,1440]{1,0:T(8,128)(2,1)S(1)} collective-permute-done((bf16[64,1440]{1,0:T(8,128)(2,1)S(1)}, bf16[64,1440]{1,0:T(8,128)(2,1)S(1)}, u32[]{:S(2)}, u32[]{:S(2)}) %collective-permute-start.22) | collective-permute-done | bytes 184352 | tf_op jit(solution)/shard_map/ppermute | solution.py:333
  54.7 0.1 add_convert_fusion.4
  54.7 0.9 %collective-permute-start.23 = (bf16[64,1440]{1,0:T(8,128)(2,1)S(1)}, bf16[64,1440]{1,0:T(8,128)(2,1)S(1)}, u32[]{:S(2)}, u32[]{:S(2)}) collective-permute-start(bf16[64,1440]{1,0:T(8,128)(2,1)S(1)} %add_convert_fusion.4), channel_id=1, source_target_pairs={{0,4},{4,8},{8,12},{12,14},{14,10},{10,6},{6,2},{2,0},{1,5},{5,9},... | collective-permute-start | bytes 552968 | tf_op jit(solution)/shard_map/ppermute | solution.py:333
  55.6 0.0 collective-permute-done.25
  55.6 0.1 add_convert_fusion.1
  55.7 1.3 %collective-permute-start.26 = (bf16[64,1440]{1,0:T(8,128)(2,1)S(1)}, bf16[64,1440]{1,0:T(8,128)(2,1)S(1)}, u32[]{:S(2)}, u32[]{:S(2)}) collective-permute-start(bf16[64,1440]{1,0:T(8,128)(2,1)S(1)} %add_convert_fusion.1), channel_id=1, source_target_pairs={{4,0},{8,4},{12,8},{14,12},{10,14},{6,10},{2,6},{0,2},{5,1},{9,5},... | collective-permute-start | bytes 552968 | tf_op jit(solution)/shard_map/ppermute | solution.py:334
  57.0 3.5 %collective-permute-done.23 = bf16[64,1440]{1,0:T(8,128)(2,1)S(1)} collective-permute-done((bf16[64,1440]{1,0:T(8,128)(2,1)S(1)}, bf16[64,1440]{1,0:T(8,128)(2,1)S(1)}, u32[]{:S(2)}, u32[]{:S(2)}) %collective-permute-start.23) | collective-permute-done | bytes 184352 | tf_op jit(solution)/shard_map/ppermute | solution.py:333
  60.5 0.9 %collective-permute-done.26 = bf16[64,1440]{1,0:T(8,128)(2,1)S(1)} collective-permute-done((bf16[64,1440]{1,0:T(8,128)(2,1)S(1)}, bf16[64,1440]{1,0:T(8,128)(2,1)S(1)}, u32[]{:S(2)}, u32[]{:S(2)}) %collective-permute-start.26) | collective-permute-done | bytes 184352 | tf_op jit(solution)/shard_map/ppermute | solution.py:334
  61.4 0.8 %add_convert_fusion = bf16[64,1440]{1,0:T(8,128)(2,1)} fusion(bf16[64,1440]{1,0:T(8,128)(2,1)S(1)} %collective-permute-done.26, bf16[64,1440]{1,0:T(8,128)(2,1)S(1)} %collective-permute-done.23, bf16[128,1440]{1,0:T(8,128)(2,1)S(1)} %collective-permute-done.16, bf16[128,1440]{1,0:T(8,128)(2,1)S(1)} %get-tuple-element.67), kind=kLoop, calls=%fused_computation | loop fusion | flops 737280 | bytes 921600 | tf_op jit(solution)/shard_map/convert_element_type | solution.py:344
  (8 shorter events, 0.1 us)
Async XLA Ops:
  1.0 8.0 %collective-permute-start = (bf16[64,1464]{1,0:T(8,128)(2,1)S(1)}, bf16[64,1464]{1,0:T(8,128)(2,1)S(1)}, u32[]{:S(2)}, u32[]{:S(2)}) collective-permute-start(bf16[64,1464]{1,0:T(8,128)(2,1)S(1)} %shard_map.64.refs_1_), channel_id=1, source_target_pairs={{0,4},{4,8},{8,12},{12,14},{14,10},{10,6},{6,2},{2,0},{1,5},{5,9},... | collective-permute-start | bytes 562184 | tf_op jit(solution)/shard_map/ppermute | solution.py:304
  4.1 7.0 %collective-permute-start.4 = (bf16[64,1464]{1,0:T(8,128)(2,1)S(1)}, bf16[64,1464]{1,0:T(8,128)(2,1)S(1)}, u32[]{:S(2)}, u32[]{:S(2)}) collective-permute-start(bf16[64,1464]{1,0:T(8,128)(2,1)S(1)} %shard_map.64.refs_1_), channel_id=1, source_target_pairs={{4,0},{8,4},{12,8},{14,12},{10,14},{6,10},{2,6},{0,2},{5,1},{9,5},... | collective-permute-start | bytes 562184 | tf_op jit(solution)/shard_map/ppermute | solution.py:308
  9.0 6.4 %collective-permute-start.1 = (bf16[64,1464]{1,0:T(8,128)(2,1)S(1)}, bf16[64,1464]{1,0:T(8,128)(2,1)S(1)}, u32[]{:S(2)}, u32[]{:S(2)}) collective-permute-start(bf16[64,1464]{1,0:T(8,128)(2,1)S(1)} %collective-permute-done.refs_0_), channel_id=1, source_target_pairs={{0,4},{4,8},{8,12},{12,14},{14,10},{10,6},{6,2},{2,0},{1,5},{5,9},... | collective-permute-start | bytes 562184 | tf_op jit(solution)/shard_map/ppermute | solution.py:304
  11.0 6.1 %collective-permute-start.3 = (bf16[64,1464]{1,0:T(8,128)(2,1)S(1)}, bf16[64,1464]{1,0:T(8,128)(2,1)S(1)}, u32[]{:S(2)}, u32[]{:S(2)}) collective-permute-start(bf16[64,1464]{1,0:T(8,128)(2,1)S(1)} %shard_map.64.refs_1_), channel_id=1, source_target_pairs={{0,1},{1,0},{2,3},{3,2},{4,5},{5,4},{6,7},{7,6},{8,9},{9,8},{10,11... | collective-permute-start | bytes 562184 | tf_op jit(solution)/shard_map/ppermute | solution.py:299
  11.1 7.3 %collective-permute-start.8 = (bf16[64,1464]{1,0:T(8,128)(2,1)S(1)}, bf16[64,1464]{1,0:T(8,128)(2,1)S(1)}, u32[]{:S(2)}, u32[]{:S(2)}) collective-permute-start(bf16[64,1464]{1,0:T(8,128)(2,1)S(1)} %collective-permute-done.4.refs_1_), channel_id=1, source_target_pairs={{4,0},{8,4},{12,8},{14,12},{10,14},{6,10},{2,6},{0,2},{5,1},{9,5},... | collective-permute-start | bytes 562184 | tf_op jit(solution)/shard_map/ppermute | solution.py:308
  11.1 7.3 %collective-permute-start.5 = (bf16[64,1464]{1,0:T(8,128)(2,1)S(1)}, bf16[64,1464]{1,0:T(8,128)(2,1)S(1)}, u32[]{:S(2)}, u32[]{:S(2)}) collective-permute-start(bf16[64,1464]{1,0:T(8,128)(2,1)S(1)} %collective-permute-done.refs_0_), channel_id=1, source_target_pairs={{0,1},{1,0},{2,3},{3,2},{4,5},{5,4},{6,7},{7,6},{8,9},{9,8},{10,11... | collective-permute-start | bytes 562184 | tf_op jit(solution)/shard_map/ppermute | solution.py:312
  11.6 6.8 %collective-permute-start.6 = (bf16[64,1464]{1,0:T(8,128)(2,1)S(1)}, bf16[64,1464]{1,0:T(8,128)(2,1)S(1)}, u32[]{:S(2)}, u32[]{:S(2)}) collective-permute-start(bf16[64,1464]{1,0:T(8,128)(2,1)S(1)} %collective-permute-done.4.refs_1_), channel_id=1, source_target_pairs={{0,1},{1,0},{2,3},{3,2},{4,5},{5,4},{6,7},{7,6},{8,9},{9,8},{10,11... | collective-permute-start | bytes 562184 | tf_op jit(solution)/shard_map/ppermute | solution.py:314
  15.4 6.7 %collective-permute-start.2 = (bf16[64,1464]{1,0:T(8,128)(2,1)S(1)}, bf16[64,1464]{1,0:T(8,128)(2,1)S(1)}, u32[]{:S(2)}, u32[]{:S(2)}) collective-permute-start(bf16[64,1464]{1,0:T(8,128)(2,1)S(1)} %collective-permute-done.1.refs_0_), channel_id=1, source_target_pairs={{0,4},{4,8},{8,12},{12,14},{14,10},{10,6},{6,2},{2,0},{1,5},{5,9},... | collective-permute-start | bytes 562184 | tf_op jit(solution)/shard_map/ppermute | solution.py:310
  17.1 7.0 %collective-permute-start.9 = (bf16[64,1464]{1,0:T(8,128)(2,1)S(1)}, bf16[64,1464]{1,0:T(8,128)(2,1)S(1)}, u32[]{:S(2)}, u32[]{:S(2)}) collective-permute-start(bf16[64,1464]{1,0:T(8,128)(2,1)S(1)} %collective-permute-done.1.refs_0_), channel_id=1, source_target_pairs={{0,1},{1,0},{2,3},{3,2},{4,5},{5,4},{6,7},{7,6},{8,9},{9,8},{10,11... | collective-permute-start | bytes 562184 | tf_op jit(solution)/shard_map/ppermute | solution.py:312
  18.4 5.8 %collective-permute-start.10 = (bf16[64,1464]{1,0:T(8,128)(2,1)S(1)}, bf16[64,1464]{1,0:T(8,128)(2,1)S(1)}, u32[]{:S(2)}, u32[]{:S(2)}) collective-permute-start(bf16[64,1464]{1,0:T(8,128)(2,1)S(1)} %collective-permute-done.8.refs_1_), channel_id=1, source_target_pairs={{0,1},{1,0},{2,3},{3,2},{4,5},{5,4},{6,7},{7,6},{8,9},{9,8},{10,11... | collective-permute-start | bytes 562184 | tf_op jit(solution)/shard_map/ppermute | solution.py:314
  22.1 6.4 %collective-permute-start.11 = (bf16[64,1464]{1,0:T(8,128)(2,1)S(1)}, bf16[64,1464]{1,0:T(8,128)(2,1)S(1)}, u32[]{:S(2)}, u32[]{:S(2)}) collective-permute-start(bf16[64,1464]{1,0:T(8,128)(2,1)S(1)} %collective-permute-done.8.refs_1_), channel_id=1, source_target_pairs={{4,0},{8,4},{12,8},{14,12},{10,14},{6,10},{2,6},{0,2},{5,1},{9,5},... | collective-permute-start | bytes 562184 | tf_op jit(solution)/shard_map/ppermute | solution.py:308
  23.7 5.7 %collective-permute-start.7 = (bf16[64,1464]{1,0:T(8,128)(2,1)S(1)}, bf16[64,1464]{1,0:T(8,128)(2,1)S(1)}, u32[]{:S(2)}, u32[]{:S(2)}) collective-permute-start(bf16[64,1464]{1,0:T(8,128)(2,1)S(1)} %collective-permute-done.2.refs_0_), channel_id=1, source_target_pairs={{0,4},{4,8},{8,12},{12,14},{14,10},{10,6},{6,2},{2,0},{1,5},{5,9},... | collective-permute-start | bytes 562184 | tf_op jit(solution)/shard_map/ppermute | solution.py:310
  29.4 1.8 %collective-permute-start.13 = (bf16[64,1464]{1,0:T(8,128)(2,1)S(1)}, bf16[64,1464]{1,0:T(8,128)(2,1)S(1)}, u32[]{:S(2)}, u32[]{:S(2)}) collective-permute-start(bf16[64,1464]{1,0:T(8,128)(2,1)S(1)} %collective-permute-done.11.refs_1_), channel_id=1, source_target_pairs={{0,1},{1,0},{2,3},{3,2},{4,5},{5,4},{6,7},{7,6},{8,9},{9,8},{10,11... | collective-permute-start | bytes 562184 | tf_op jit(solution)/shard_map/ppermute | solution.py:324
  29.4 1.9 %collective-permute-start.12 = (bf16[64,1464]{1,0:T(8,128)(2,1)S(1)}, bf16[64,1464]{1,0:T(8,128)(2,1)S(1)}, u32[]{:S(2)}, u32[]{:S(2)}) collective-permute-start(bf16[64,1464]{1,0:T(8,128)(2,1)S(1)} %collective-permute-done.7.refs_0_), channel_id=1, source_target_pairs={{0,1},{1,0},{2,3},{3,2},{4,5},{5,4},{6,7},{7,6},{8,9},{9,8},{10,11... | collective-permute-start | bytes 562184 | tf_op jit(solution)/shard_map/ppermute | solution.py:324
  33.0 1.7 %collective-permute-start.14 = (bf16[64,1440]{1,0:T(8,128)(2,1)S(1)}, bf16[64,1440]{1,0:T(8,128)(2,1)S(1)}, u32[]{:S(2)}, u32[]{:S(2)}) collective-permute-start(bf16[64,1440]{1,0:T(8,128)(2,1)S(1)} %get-tuple-element.63), channel_id=1, source_target_pairs={{0,1},{1,0},{2,3},{3,2},{4,5},{5,4},{6,7},{7,6},{8,9},{9,8},{10,11... | collective-permute-start | bytes 552968 | tf_op jit(solution)/shard_map/ppermute | solution.py:259
  33.2 2.6 %collective-permute-start.15 = (bf16[64,1464]{1,0:T(8,128)(2,1)S(1)}, bf16[64,1464]{1,0:T(8,128)(2,1)S(1)}, u32[]{:S(2)}, u32[]{:S(2)}) collective-permute-start(bf16[64,1464]{1,0:T(8,128)(2,1)S(1)} %collective-permute-done.2.refs_0_), channel_id=1, source_target_pairs={{0,1},{1,0},{2,3},{3,2},{4,5},{5,4},{6,7},{7,6},{8,9},{9,8},{10,11... | collective-permute-start | bytes 562184 | tf_op jit(solution)/shard_map/ppermute | solution.py:312
  33.6 5.7 %collective-permute-start.19 = (bf16[64,1440]{1,0:T(8,128)(2,1)S(1)}, bf16[64,1440]{1,0:T(8,128)(2,1)S(1)}, u32[]{:S(2)}, u32[]{:S(2)}) collective-permute-start(bf16[64,1440]{1,0:T(8,128)(2,1)S(1)} %get-tuple-element.78), channel_id=1, source_target_pairs={{0,1},{1,0},{2,3},{3,2},{4,5},{5,4},{6,7},{7,6},{8,9},{9,8},{10,11... | collective-permute-start | bytes 552968 | tf_op jit(solution)/shard_map/ppermute | solution.py:259
  34.8 7.5 %collective-permute-start.20 = (bf16[64,1440]{1,0:T(8,128)(2,1)S(1)}, bf16[64,1440]{1,0:T(8,128)(2,1)S(1)}, u32[]{:S(2)}, u32[]{:S(2)}) collective-permute-start(bf16[64,1440]{1,0:T(8,128)(2,1)S(1)} %fusion), channel_id=1, source_target_pairs={{0,4},{4,8},{8,12},{12,14},{14,10},{10,6},{6,2},{2,0},{1,5},{5,9},... | collective-permute-start | bytes 552968 | tf_op jit(solution)/shard_map/ppermute | solution.py:333
  38.5 4.7 %collective-permute-start.16 = (bf16[128,1440]{1,0:T(8,128)(2,1)S(1)}, bf16[128,1440]{1,0:T(8,128)(2,1)S(1)}, u32[]{:S(2)}, u32[]{:S(2)}) collective-permute-start(bf16[128,1440]{1,0:T(8,128)(2,1)S(1)} %get-tuple-element.66), channel_id=1, source_target_pairs={{0,1},{1,0},{2,3},{3,2},{4,5},{5,4},{6,7},{7,6},{8,9},{9,8},{10,11... | collective-permute-start | bytes 1105928 | tf_op jit(solution)/shard_map/ppermute | solution.py:338
  38.8 10.2 %collective-permute-start.17 = (bf16[128,1440]{1,0:T(8,128)(2,1)S(1)}, bf16[128,1440]{1,0:T(8,128)(2,1)S(1)}, u32[]{:S(2)}, u32[]{:S(2)}) collective-permute-start(bf16[128,1440]{1,0:T(8,128)(2,1)S(1)} %get-tuple-element.70), channel_id=1, source_target_pairs={{0,1},{1,0},{2,3},{3,2},{4,5},{5,4},{6,7},{7,6},{8,9},{9,8},{10,11... | collective-permute-start | bytes 1105928 | tf_op jit(solution)/shard_map/ppermute | solution.py:329
  39.1 4.1 %collective-permute-start.18 = (bf16[128,1440]{1,0:T(8,128)(2,1)S(1)}, bf16[128,1440]{1,0:T(8,128)(2,1)S(1)}, u32[]{:S(2)}, u32[]{:S(2)}) collective-permute-start(bf16[128,1440]{1,0:T(8,128)(2,1)S(1)} %get-tuple-element.74), channel_id=1, source_target_pairs={{0,1},{1,0},{2,3},{3,2},{4,5},{5,4},{6,7},{7,6},{8,9},{9,8},{10,11... | collective-permute-start | bytes 1105928 | tf_op jit(solution)/shard_map/ppermute | solution.py:329
  42.4 6.5 %collective-permute-start.21 = (bf16[64,1440]{1,0:T(8,128)(2,1)S(1)}, bf16[64,1440]{1,0:T(8,128)(2,1)S(1)}, u32[]{:S(2)}, u32[]{:S(2)}) collective-permute-start(bf16[64,1440]{1,0:T(8,128)(2,1)S(1)} %add_convert_fusion.6), channel_id=1, source_target_pairs={{0,4},{4,8},{8,12},{12,14},{14,10},{10,6},{6,2},{2,0},{1,5},{5,9},... | collective-permute-start | bytes 552968 | tf_op jit(solution)/shard_map/ppermute | solution.py:333
  43.3 6.5 %collective-permute-start.24 = (bf16[64,1440]{1,0:T(8,128)(2,1)S(1)}, bf16[64,1440]{1,0:T(8,128)(2,1)S(1)}, u32[]{:S(2)}, u32[]{:S(2)}) collective-permute-start(bf16[64,1440]{1,0:T(8,128)(2,1)S(1)} %add_convert_fusion.3), channel_id=1, source_target_pairs={{4,0},{8,4},{12,8},{14,12},{10,14},{6,10},{2,6},{0,2},{5,1},{9,5},... | collective-permute-start | bytes 552968 | tf_op jit(solution)/shard_map/ppermute | solution.py:334
  48.9 5.7 %collective-permute-start.22 = (bf16[64,1440]{1,0:T(8,128)(2,1)S(1)}, bf16[64,1440]{1,0:T(8,128)(2,1)S(1)}, u32[]{:S(2)}, u32[]{:S(2)}) collective-permute-start(bf16[64,1440]{1,0:T(8,128)(2,1)S(1)} %add_convert_fusion.5), channel_id=1, source_target_pairs={{0,4},{4,8},{8,12},{12,14},{14,10},{10,6},{6,2},{2,0},{1,5},{5,9},... | collective-permute-start | bytes 552968 | tf_op jit(solution)/shard_map/ppermute | solution.py:333
  49.9 5.7 %collective-permute-start.25 = (bf16[64,1440]{1,0:T(8,128)(2,1)S(1)}, bf16[64,1440]{1,0:T(8,128)(2,1)S(1)}, u32[]{:S(2)}, u32[]{:S(2)}) collective-permute-start(bf16[64,1440]{1,0:T(8,128)(2,1)S(1)} %add_convert_fusion.2), channel_id=1, source_target_pairs={{4,0},{8,4},{12,8},{14,12},{10,14},{6,10},{2,6},{0,2},{5,1},{9,5},... | collective-permute-start | bytes 552968 | tf_op jit(solution)/shard_map/ppermute | solution.py:334
  54.7 5.7 %collective-permute-start.23 = (bf16[64,1440]{1,0:T(8,128)(2,1)S(1)}, bf16[64,1440]{1,0:T(8,128)(2,1)S(1)}, u32[]{:S(2)}, u32[]{:S(2)}) collective-permute-start(bf16[64,1440]{1,0:T(8,128)(2,1)S(1)} %add_convert_fusion.4), channel_id=1, source_target_pairs={{0,4},{4,8},{8,12},{12,14},{14,10},{10,6},{6,2},{2,0},{1,5},{5,9},... | collective-permute-start | bytes 552968 | tf_op jit(solution)/shard_map/ppermute | solution.py:333
  55.7 5.7 %collective-permute-start.26 = (bf16[64,1440]{1,0:T(8,128)(2,1)S(1)}, bf16[64,1440]{1,0:T(8,128)(2,1)S(1)}, u32[]{:S(2)}, u32[]{:S(2)}) collective-permute-start(bf16[64,1440]{1,0:T(8,128)(2,1)S(1)} %add_convert_fusion.1), channel_id=1, source_target_pairs={{4,0},{8,4},{12,8},{14,12},{10,14},{6,10},{2,6},{0,2},{5,1},{9,5},... | collective-permute-start | bytes 552968 | tf_op jit(solution)/shard_map/ppermute | solution.py:334

commit v11 on v9

--- a/solution.py
+++ b/solution.py
@@ -268,6 +268,22 @@
     return mine, theirs
 
 
+def add_kernel(*refs):
+    *terms, out = refs
+    out[...] = sum(t[...].astype(jnp.float32) for t in terms).astype(out.dtype)
+
+
+def add(*terms):
+    vmem = pl.BlockSpec(memory_space=pltpu.VMEM)
+    return pl.pallas_call(
+        add_kernel,
+        out_shape=in_vmem(terms[0].shape),
+        in_specs=[vmem] * len(terms),
+        out_specs=vmem,
+        cost_estimate=pl.CostEstimate(flops=0, bytes_accessed=12 << 20, transcendentals=0),
+    )(*[hold(t) for t in terms])
+
+
 def ring_body(tokens, expert_ids, gate_probs, w_gate, w_up, w_down):
     n = lax.axis_size("ep")
     rows = tokens.shape[0]
@@ -280,7 +296,7 @@
     packed = pack(tokens, expert_ids, gate_probs, n)
     gate, up = turn_weights(after(place, packed), w_gate[0].T, w_up[0].T)
 
-    came, across, value = {0: packed}, {}, {}
+    came, across, value, parts = {0: packed}, {}, {}, {}
 
     def run(keys, wait_for=None):
         at = place if wait_for is None else after(place, wait_for)
@@ -294,6 +310,7 @@
             mine, theirs = pairs[i % 2]
             span = slice(start, start + came[k].shape[0])
             start = span.stop
+            parts[k] = mine[span], theirs[span]
             value[k] = mine[span].astype(jnp.float32) + theirs[span].astype(jnp.float32)
 
     came[1] = lax.ppermute(packed, "ep", ahead)
@@ -310,7 +327,7 @@
             weights += halve_weights(after(place, came[1]), w_down[0])
             done = weights[-1]
         else:
-            near += run([k - 2, 2 - k])
+            near += run([k - 2, 2 - k], across[0] if k == 3 else None)
             done = near[-1][-1]
     came[far] = after(came[far], done)
     across[far] = swap(came[far])
@@ -320,20 +337,19 @@
     for keys, mine, theirs in near:
         keep(keys, mine, swap(after(theirs, value[far])))
 
-    to_ahead, to_back = value[far].astype(jnp.bfloat16), None
+    to_ahead = value[far].astype(jnp.bfloat16)
+    to_back = (value[far - 1]).astype(jnp.bfloat16)
     for k in range(far - 1, -1, -1):
-        behind = lax.ppermute(to_ahead, "ep", ahead).astype(jnp.float32)
-        front = 0.0 if to_back is None else lax.ppermute(to_back, "ep", back).astype(jnp.float32)
-        done = None
-        if k == 1:
-            ((keys, mine, done),) = run([0], (to_ahead, to_back))
+        behind = lax.ppermute(to_ahead, "ep", ahead)
+        if k == far - 1:
+            ((keys, mine, done),) = run([0], to_ahead)
             keep(keys, mine, swap(done))
+        else:
+            to_back = done = add(*parts[k], after(front, to_ahead))
         if k:
-            to_ahead = (value[-k] + behind).astype(jnp.bfloat16)
-            to_back = (value[k] + front).astype(jnp.bfloat16)
-        if done is not None:
-            to_ahead, to_back = after(to_ahead, done), after(to_back, done)
-    return (value[0] + behind + front).astype(jnp.bfloat16)
+            front = lax.ppermute(to_back, "ep", back)
+            to_ahead = (value[-k] + after(behind, done).astype(jnp.float32)).astype(jnp.bfloat16)
+    return (to_back.astype(jnp.float32) + behind.astype(jnp.float32)).astype(jnp.bfloat16)
 
 
 def swiglu_expert(rows, gate_part, up_part, down_part):

time: 62 us -> 61.1 us (0.985)
  starting transfers between devices: 19.9 us -> 18.8 us
    ppermute x7, waiting for transfers between devices: 15.3 us -> 13.7 us  [the longest x3 7.78 us: ring_body(): front = lax.ppermute(to_back, 'ep', back)]
    ppermute x2, waiting for transfers between devices: 0.85 us -> 2.3 us  [ring_body(): came[-k] = lax.ppermute(came[1 - k], 'ep', back)]
    convert_element_type x8 -> x6, other arithmetic: 1.24 us -> 1.05 us  [the longest x1 0.72 us: ring_body(): (to_back.astype(jnp.float32) + behind.astype(jnp.float32)).astype(jnp.bfl...]
  transfers between devices with their start and end apart: 27 -> 27, of which waited for: 9 -> 12; matrix products, arithmetic and copies ran while one was open for 1% -> 1% of each run, Pallas kernels for 30% -> 31%
where the time goes in v11:
time: 61.1 us; the launch traced here: 60.9 us
  Pallas kernels  22.2 us (36%)
  starting transfers between devices  18.8 us (31%)
  waiting for transfers between devices  18.5 us (30%)
  other arithmetic  1.12 us (2%)
    pallas_call x6, Pallas kernels, call(): pl.pallas_call(kernel, out_shape=out_shape, in_specs=[pl.BlockSpec(memory...  13.1 us
    ppermute x3, waiting for transfers between devices, ring_body(): front = lax.ppermute(to_back, 'ep', back)  7.78 us
    ppermute x4, starting transfers between devices, ring_body(): behind = lax.ppermute(to_ahead, 'ep', ahead)  7.34 us
    ppermute x4, waiting for transfers between devices, ring_body(): behind = lax.ppermute(to_ahead, 'ep', ahead)  5.92 us
    ppermute x3, starting transfers between devices, ring_body(): came[k] = lax.ppermute(came[k - 1], 'ep', ahead)  5.56 us
    pallas_call x1, Pallas kernels, turn_weights(): pl.pallas_call(turn_kernel, out_shape=[in_vmem((width, hidden))] * 2, in_...  4.79 us
    pallas_call x1, Pallas kernels, halve_weights(): pl.pallas_call(halve_kernel, out_shape=[in_vmem((hidden, width // 2))] *...  3.13 us
    ppermute x1, starting transfers between devices, ring_body(): came[1] = lax.ppermute(packed, 'ep', ahead)  3.08 us
  transfers between devices with their start and end apart: 27, of which 12 were waited for; matrix products, arithmetic and copies ran while one was open for 1% of the time, Pallas kernels for 31%

profile of v11, /device:TPU:0, one launch (start us, length us, event | category | flops | bytes accessed | tf_op | source)
XLA Modules:
  0.0 60.9 jit_solution(5305601409299772980)
XLA Ops:
  0.0 1.0 %shard_map.64.refs_0_ = bf16[64,1464]{1,0:T(8,128)(2,1)S(1)} custom-call(bf16[64,1440]{1,0:T(8,128)(2,1)} %tokens_in.1, s32[4,64]{1,0:T(4,128)} %bitcast.14, f32[4,64]{1,0:T(4,128)} %bitcast.15), custom_call_target="tpu_custom_call" | custom-call | tf_op jit(solution)/shard_map/pallas_call | solution.py:53
  1.0 3.1 %collective-permute-start = (bf16[64,1464]{1,0:T(8,128)(2,1)S(1)}, bf16[64,1464]{1,0:T(8,128)(2,1)S(1)}, u32[]{:S(2)}, u32[]{:S(2)}) collective-permute-start(bf16[64,1464]{1,0:T(8,128)(2,1)S(1)} %shard_map.64.refs_0_), channel_id=1, source_target_pairs={{0,4},{4,8},{8,12},{12,14},{14,10},{10,6},{6,2},{2,0},{1,5},{5,9},... | collective-permute-start | bytes 562184 | tf_op jit(solution)/shard_map/ppermute | solution.py:316
  4.1 0.0 collective-permute-start.4
  4.1 0.1 pad_add_fusion.after_this.place
  4.2 4.8 %shard_map.65 = (bf16[2880,720]{1,0:T(8,128)(2,1)S(1)}, bf16[2880,720]{1,0:T(8,128)(2,1)S(1)}) custom-call(s32[2]{0:T(128)S(1)} %pad_add_fusion.after_this.place, bf16[720,2880]{1,0:T(8,128)(2,1)} %bitcast.11, bf16[720,2880]{1,0:T(8,128)(2,1)} %bitcast.12), custom_call_target="tpu_custom_call" | custom-call | bytes 16588800 | tf_op jit(solution)/shard_map/pallas_call | solution.py:83
  9.0 0.0 collective-permute-done.refs_0_
  9.0 2.1 %collective-permute-start.1 = (bf16[64,1464]{1,0:T(8,128)(2,1)S(1)}, bf16[64,1464]{1,0:T(8,128)(2,1)S(1)}, u32[]{:S(2)}, u32[]{:S(2)}) collective-permute-start(bf16[64,1464]{1,0:T(8,128)(2,1)S(1)} %collective-permute-done.refs_0_), channel_id=1, source_target_pairs={{0,4},{4,8},{8,12},{12,14},{14,10},{10,6},{6,2},{2,0},{1,5},{5,9},... | collective-permute-start | bytes 562184 | tf_op jit(solution)/shard_map/ppermute | solution.py:322
  11.0 0.0 collective-permute-start.3
  11.1 0.1 collective-permute-start.8
  11.1 0.4 collective-permute-start.5
  11.6 0.1 collective-permute-start.6
  11.6 3.1 %shard_map.66 = (bf16[720,1440]{1,0:T(8,128)(2,1)S(1)}, bf16[720,1440]{1,0:T(8,128)(2,1)S(1)}) custom-call(s32[2]{0:T(128)S(1)} %pad_add_fusion.after_this.place, bf16[720,2880]{1,0:T(8,128)(2,1)} %bitcast.13), custom_call_target="tpu_custom_call" | custom-call | bytes 16588800 | tf_op jit(solution)/shard_map/pallas_call | solution.py:120
  14.8 0.6 collective-permute-done.1.refs_0_
  15.4 1.7 %collective-permute-start.2 = (bf16[64,1464]{1,0:T(8,128)(2,1)S(1)}, bf16[64,1464]{1,0:T(8,128)(2,1)S(1)}, u32[]{:S(2)}, u32[]{:S(2)}) collective-permute-start(bf16[64,1464]{1,0:T(8,128)(2,1)S(1)} %collective-permute-done.1.refs_0_), channel_id=1, source_target_pairs={{0,4},{4,8},{8,12},{12,14},{14,10},{10,6},{6,2},{2,0},{1,5},{5,9},... | collective-permute-start | bytes 562184 | tf_op jit(solution)/shard_map/ppermute | solution.py:322
  17.1 0.0 collective-permute-done.3.refs_1_
  17.1 0.0 collective-permute-start.9
  17.1 1.2 %collective-permute-done.8.refs_1_ = bf16[64,1464]{1,0:T(8,128)(2,1)S(1)} collective-permute-done((bf16[64,1464]{1,0:T(8,128)(2,1)S(1)}, bf16[64,1464]{1,0:T(8,128)(2,1)S(1)}, u32[]{:S(2)}, u32[]{:S(2)}) %collective-permute-start.8) | collective-permute-done | bytes 187424 | tf_op jit(solution)/shard_map/ppermute | solution.py:324
  18.4 0.3 collective-permute-start.11
  18.7 0.0 collective-permute-done.5.refs_2_
  18.7 0.0 collective-permute-start.10
  18.7 0.0 collective-permute-done.6.refs_3_
  18.7 2.7 %shard_map.67 = (bf16[128,1440]{1,0:T(8,128)(2,1)S(1)}, bf16[128,1440]{1,0:T(8,128)(2,1)S(1)}) custom-call(s32[2]{0:T(128)S(1)} %pad_add_fusion.after_this.place, bf16[64,1464]{1,0:T(8,128)(2,1)S(1)} %collective-permute-done.refs_0_, bf16[64,1464]{1,0:T(8,128)(2,1)S(1)} %collective-permute-done.4.refs_1_, ...), custom_call_target="tpu_custom_call" | custom-call | flops 1592524800 | bytes 12441600 | tf_op jit(solution)/shard_map/pallas_call | solution.py:210
  21.4 0.7 %collective-permute-done.2.refs_1_ = bf16[64,1464]{1,0:T(8,128)(2,1)S(1)} collective-permute-done((bf16[64,1464]{1,0:T(8,128)(2,1)S(1)}, bf16[64,1464]{1,0:T(8,128)(2,1)S(1)}, u32[]{:S(2)}, u32[]{:S(2)}) %collective-permute-start.2) | collective-permute-done | bytes 187424 | tf_op jit(solution)/shard_map/ppermute | solution.py:322
  22.1 1.7 %collective-permute-start.7 = (bf16[64,1464]{1,0:T(8,128)(2,1)S(1)}, bf16[64,1464]{1,0:T(8,128)(2,1)S(1)}, u32[]{:S(2)}, u32[]{:S(2)}) collective-permute-start(bf16[64,1464]{1,0:T(8,128)(2,1)S(1)} %collective-permute-done.2.refs_1_), channel_id=1, source_target_pairs={{0,4},{4,8},{8,12},{12,14},{14,10},{10,6},{6,2},{2,0},{1,5},{5,9},... | collective-permute-start | bytes 562184 | tf_op jit(solution)/shard_map/ppermute | solution.py:322
  23.8 0.0 collective-permute-start.13
  23.8 1.1 %collective-permute-done.11.refs_2_ = bf16[64,1464]{1,0:T(8,128)(2,1)S(1)} collective-permute-done((bf16[64,1464]{1,0:T(8,128)(2,1)S(1)}, bf16[64,1464]{1,0:T(8,128)(2,1)S(1)}, u32[]{:S(2)}, u32[]{:S(2)}) %collective-permute-start.11) | collective-permute-done | bytes 187424 | tf_op jit(solution)/shard_map/ppermute | solution.py:324
  24.9 2.7 %shard_map.68 = (bf16[128,1440]{1,0:T(8,128)(2,1)S(1)}, bf16[128,1440]{1,0:T(8,128)(2,1)S(1)}) custom-call(s32[2]{0:T(128)S(1)} %pad_add_fusion.after_this.place, bf16[64,1464]{1,0:T(8,128)(2,1)S(1)} %collective-permute-done.1.refs_0_, bf16[64,1464]{1,0:T(8,128)(2,1)S(1)} %collective-permute-done.8.refs_1_, ...), custom_call_target="tpu_custom_call" | custom-call | flops 1592524800 | bytes 12441600 | tf_op jit(solution)/shard_map/pallas_call | solution.py:210
  27.6 1.1 %collective-permute-done.7.refs_0_ = bf16[64,1464]{1,0:T(8,128)(2,1)S(1)} collective-permute-done((bf16[64,1464]{1,0:T(8,128)(2,1)S(1)}, bf16[64,1464]{1,0:T(8,128)(2,1)S(1)}, u32[]{:S(2)}, u32[]{:S(2)}) %collective-permute-start.7) | collective-permute-done | bytes 187424 | tf_op jit(solution)/shard_map/ppermute | solution.py:322
  28.7 0.0 collective-permute-start.12
  28.8 1.6 %shard_map.69 = (f32[192,720]{1,0:T(8,128)S(1)}, f32[192,720]{1,0:T(8,128)S(1)}) custom-call(s32[2]{0:T(128)S(1)} %pad_add_fusion.after_this.place, bf16[64,1464]{1,0:T(8,128)(2,1)S(1)} %collective-permute-done.7.refs_0_, bf16[64,1464]{1,0:T(8,128)(2,1)S(1)} %collective-permute-done.2.refs_1_, bf16[64,1464]{1,0:T(8,128)(2,1)S(1)} %collective-permute-done.11.refs_2_, ...), custom_call_target="tpu_custom_call" | custom-call | flops 796262400 | bytes 6220800 | tf_op jit(solution)/shard_map/pallas_call | solution.py:210
  30.4 0.0 collective-permute-done.14.refs_5_
  30.4 0.0 collective-permute-done.12.refs_3_
  30.4 2.2 %shard_map.70 = (bf16[192,720]{1,0:T(8,128)(2,1)S(1)}, bf16[64,1440]{1,0:T(8,128)(2,1)S(1)}, bf16[128,1440]{1,0:T(8,128)(2,1)S(1)}) custom-call(s32[2]{0:T(128)S(1)} %pad_add_fusion.after_this.place, bf16[64,1464]{1,0:T(8,128)(2,1)S(1)} %collective-permute-done.7.refs_0_, bf16[64,1464]{1,0:T(8,128)(2,1)S(1)} %collective-permute-done.2.refs_1_, ...), custom_call_target="tpu_custom_call" | custom-call | flops 1194393600 | bytes 9331200 | tf_op jit(solution)/shard_map/pallas_call | solution.py:210
  32.6 0.6 collective-permute-start.15
  33.2 0.1 collective-permute-start.19
  33.3 1.2 %shard_map.71 = (bf16[64,1440]{1,0:T(8,128)(2,1)S(1)}, bf16[128,1440]{1,0:T(8,128)(2,1)S(1)}) custom-call(s32[2]{0:T(128)S(1)} %pad_add_fusion.after_this.place, bf16[64,1464]{1,0:T(8,128)(2,1)S(1)} %collective-permute-done.7.refs_0_, bf16[64,1464]{1,0:T(8,128)(2,1)S(1)} %collective-permute-done.2.refs_1_, ...), custom_call_target="tpu_custom_call" | custom-call | flops 398131200 | bytes 3110400 | tf_op jit(solution)/shard_map/pallas_call | solution.py:210
  34.5 2.0 %collective-permute-start.21 = (bf16[64,1440]{1,0:T(8,128)(2,1)S(1)}, bf16[64,1440]{1,0:T(8,128)(2,1)S(1)}, u32[]{:S(2)}, u32[]{:S(2)}) collective-permute-start(bf16[64,1440]{1,0:T(8,128)(2,1)S(1)} %fusion), channel_id=1, source_target_pairs={{0,4},{4,8},{8,12},{12,14},{14,10},{10,6},{6,2},{2,0},{1,5},{5,9},... | collective-permute-start | bytes 552968 | tf_op jit(solution)/shard_map/ppermute | solution.py:343
  36.5 0.2 collective-permute-start.18
  36.7 2.7 %shard_map.72 = (bf16[64,1440]{1,0:T(8,128)(2,1)S(1)}, bf16[64,1440]{1,0:T(8,128)(2,1)S(1)}) custom-call(s32[2]{0:T(128)S(1)} %pad_add_fusion.after_this.place, bf16[64,1464]{1,0:T(8,128)(2,1)S(1)} %shard_map.64.refs_0_, bf16[64,1464]{1,0:T(8,128)(2,1)S(1)} %collective-permute-done.3.refs_1_, ...), custom_call_target="tpu_custom_call" | custom-call | flops 1592524800 | bytes 12441600 | tf_op jit(solution)/shard_map/pallas_call | solution.py:210
  39.4 0.1 add_convert_fusion.4
  39.4 0.3 collective-permute-start.20
  39.8 2.3 %collective-permute-done.21 = bf16[64,1440]{1,0:T(8,128)(2,1)S(1)} collective-permute-done((bf16[64,1440]{1,0:T(8,128)(2,1)S(1)}, bf16[64,1440]{1,0:T(8,128)(2,1)S(1)}, u32[]{:S(2)}, u32[]{:S(2)}) %collective-permute-start.21) | collective-permute-done | bytes 184352 | tf_op jit(solution)/shard_map/ppermute | solution.py:343
  42.0 0.1 add_convert_fusion.3
  42.1 1.8 %collective-permute-start.23 = (bf16[64,1440]{1,0:T(8,128)(2,1)S(1)}, bf16[64,1440]{1,0:T(8,128)(2,1)S(1)}, u32[]{:S(2)}, u32[]{:S(2)}) collective-permute-start(bf16[64,1440]{1,0:T(8,128)(2,1)S(1)} %add_convert_fusion.3), channel_id=1, source_target_pairs={{0,4},{4,8},{8,12},{12,14},{14,10},{10,6},{6,2},{2,0},{1,5},{5,9},... | collective-permute-start | bytes 552968 | tf_op jit(solution)/shard_map/ppermute | solution.py:343
  43.9 0.1 collective-permute-start.17
  44.0 2.6 %collective-permute-done.20.refs_2_ = bf16[64,1440]{1,0:T(8,128)(2,1)S(1)} collective-permute-done((bf16[64,1440]{1,0:T(8,128)(2,1)S(1)}, bf16[64,1440]{1,0:T(8,128)(2,1)S(1)}, u32[]{:S(2)}, u32[]{:S(2)}) %collective-permute-start.20) | collective-permute-done | bytes 184352 | tf_op jit(solution)/shard_map/ppermute | solution.py:350
  46.6 0.0 collective-permute-done.18
  46.6 0.1 shard_map.73
  46.7 0.3 collective-permute-start.22
  47.1 1.6 %collective-permute-done.23 = bf16[64,1440]{1,0:T(8,128)(2,1)S(1)} collective-permute-done((bf16[64,1440]{1,0:T(8,128)(2,1)S(1)}, bf16[64,1440]{1,0:T(8,128)(2,1)S(1)}, u32[]{:S(2)}, u32[]{:S(2)}) %collective-permute-start.23) | collective-permute-done | bytes 184352 | tf_op jit(solution)/shard_map/ppermute | solution.py:343
  48.6 0.1 add_convert_fusion.2
  48.7 1.8 %collective-permute-start.25 = (bf16[64,1440]{1,0:T(8,128)(2,1)S(1)}, bf16[64,1440]{1,0:T(8,128)(2,1)S(1)}, u32[]{:S(2)}, u32[]{:S(2)}) collective-permute-start(bf16[64,1440]{1,0:T(8,128)(2,1)S(1)} %add_convert_fusion.2), channel_id=1, source_target_pairs={{0,4},{4,8},{8,12},{12,14},{14,10},{10,6},{6,2},{2,0},{1,5},{5,9},... | collective-permute-start | bytes 552968 | tf_op jit(solution)/shard_map/ppermute | solution.py:343
  50.5 0.1 collective-permute-start.16
  50.6 2.5 %collective-permute-done.22.refs_2_ = bf16[64,1440]{1,0:T(8,128)(2,1)S(1)} collective-permute-done((bf16[64,1440]{1,0:T(8,128)(2,1)S(1)}, bf16[64,1440]{1,0:T(8,128)(2,1)S(1)}, u32[]{:S(2)}, u32[]{:S(2)}) %collective-permute-start.22) | collective-permute-done | bytes 184352 | tf_op jit(solution)/shard_map/ppermute | solution.py:350
  53.1 0.1 shard_map.74
  53.2 0.3 collective-permute-start.24
  53.5 0.9 %collective-permute-done.25 = bf16[64,1440]{1,0:T(8,128)(2,1)S(1)} collective-permute-done((bf16[64,1440]{1,0:T(8,128)(2,1)S(1)}, bf16[64,1440]{1,0:T(8,128)(2,1)S(1)}, u32[]{:S(2)}, u32[]{:S(2)}) %collective-permute-start.25) | collective-permute-done | bytes 184352 | tf_op jit(solution)/shard_map/ppermute | solution.py:343
  54.4 0.1 add_convert_fusion.1
  54.5 1.8 %collective-permute-start.26 = (bf16[64,1440]{1,0:T(8,128)(2,1)S(1)}, bf16[64,1440]{1,0:T(8,128)(2,1)S(1)}, u32[]{:S(2)}, u32[]{:S(2)}) collective-permute-start(bf16[64,1440]{1,0:T(8,128)(2,1)S(1)} %add_convert_fusion.1), channel_id=1, source_target_pairs={{0,4},{4,8},{8,12},{12,14},{14,10},{10,6},{6,2},{2,0},{1,5},{5,9},... | collective-permute-start | bytes 552968 | tf_op jit(solution)/shard_map/ppermute | solution.py:343
  56.3 2.6 %collective-permute-done.24.refs_2_ = bf16[64,1440]{1,0:T(8,128)(2,1)S(1)} collective-permute-done((bf16[64,1440]{1,0:T(8,128)(2,1)S(1)}, bf16[64,1440]{1,0:T(8,128)(2,1)S(1)}, u32[]{:S(2)}, u32[]{:S(2)}) %collective-permute-start.24) | collective-permute-done | bytes 184352 | tf_op jit(solution)/shard_map/ppermute | solution.py:350
  58.9 0.0 collective-permute-done.16.refs_1_
  58.9 0.1 shard_map.75
  59.0 1.2 %collective-permute-done.26 = bf16[64,1440]{1,0:T(8,128)(2,1)S(1)} collective-permute-done((bf16[64,1440]{1,0:T(8,128)(2,1)S(1)}, bf16[64,1440]{1,0:T(8,128)(2,1)S(1)}, u32[]{:S(2)}, u32[]{:S(2)}) %collective-permute-start.26) | collective-permute-done | bytes 184352 | tf_op jit(solution)/shard_map/ppermute | solution.py:343
  60.2 0.7 %add_convert_fusion = bf16[64,1440]{1,0:T(8,128)(2,1)} fusion(bf16[64,1440]{1,0:T(8,128)(2,1)S(1)} %collective-permute-done.26, bf16[64,1440]{1,0:T(8,128)(2,1)S(1)} %shard_map.75), kind=kLoop, calls=%fused_computation | loop fusion | flops 368640 | bytes 552960 | tf_op jit(solution)/shard_map/convert_element_type | solution.py:352
  (13 shorter events, 0.1 us)
Async XLA Ops:
  1.0 8.0 %collective-permute-start = (bf16[64,1464]{1,0:T(8,128)(2,1)S(1)}, bf16[64,1464]{1,0:T(8,128)(2,1)S(1)}, u32[]{:S(2)}, u32[]{:S(2)}) collective-permute-start(bf16[64,1464]{1,0:T(8,128)(2,1)S(1)} %shard_map.64.refs_0_), channel_id=1, source_target_pairs={{0,4},{4,8},{8,12},{12,14},{14,10},{10,6},{6,2},{2,0},{1,5},{5,9},... | collective-permute-start | bytes 562184 | tf_op jit(solution)/shard_map/ppermute | solution.py:316
  4.1 7.0 %collective-permute-start.4 = (bf16[64,1464]{1,0:T(8,128)(2,1)S(1)}, bf16[64,1464]{1,0:T(8,128)(2,1)S(1)}, u32[]{:S(2)}, u32[]{:S(2)}) collective-permute-start(bf16[64,1464]{1,0:T(8,128)(2,1)S(1)} %shard_map.64.refs_0_), channel_id=1, source_target_pairs={{4,0},{8,4},{12,8},{14,12},{10,14},{6,10},{2,6},{0,2},{5,1},{9,5},... | collective-permute-start | bytes 562184 | tf_op jit(solution)/shard_map/ppermute | solution.py:317
  9.0 6.4 %collective-permute-start.1 = (bf16[64,1464]{1,0:T(8,128)(2,1)S(1)}, bf16[64,1464]{1,0:T(8,128)(2,1)S(1)}, u32[]{:S(2)}, u32[]{:S(2)}) collective-permute-start(bf16[64,1464]{1,0:T(8,128)(2,1)S(1)} %collective-permute-done.refs_0_), channel_id=1, source_target_pairs={{0,4},{4,8},{8,12},{12,14},{14,10},{10,6},{6,2},{2,0},{1,5},{5,9},... | collective-permute-start | bytes 562184 | tf_op jit(solution)/shard_map/ppermute | solution.py:322
  11.0 6.1 %collective-permute-start.3 = (bf16[64,1464]{1,0:T(8,128)(2,1)S(1)}, bf16[64,1464]{1,0:T(8,128)(2,1)S(1)}, u32[]{:S(2)}, u32[]{:S(2)}) collective-permute-start(bf16[64,1464]{1,0:T(8,128)(2,1)S(1)} %shard_map.64.refs_0_), channel_id=1, source_target_pairs={{0,1},{1,0},{2,3},{3,2},{4,5},{5,4},{6,7},{7,6},{8,9},{9,8},{10,11... | collective-permute-start | bytes 562184 | tf_op jit(solution)/shard_map/ppermute | solution.py:318
  11.1 7.3 %collective-permute-start.8 = (bf16[64,1464]{1,0:T(8,128)(2,1)S(1)}, bf16[64,1464]{1,0:T(8,128)(2,1)S(1)}, u32[]{:S(2)}, u32[]{:S(2)}) collective-permute-start(bf16[64,1464]{1,0:T(8,128)(2,1)S(1)} %collective-permute-done.4.refs_1_), channel_id=1, source_target_pairs={{4,0},{8,4},{12,8},{14,12},{10,14},{6,10},{2,6},{0,2},{5,1},{9,5},... | collective-permute-start | bytes 562184 | tf_op jit(solution)/shard_map/ppermute | solution.py:324
  11.1 7.5 %collective-permute-start.5 = (bf16[64,1464]{1,0:T(8,128)(2,1)S(1)}, bf16[64,1464]{1,0:T(8,128)(2,1)S(1)}, u32[]{:S(2)}, u32[]{:S(2)}) collective-permute-start(bf16[64,1464]{1,0:T(8,128)(2,1)S(1)} %collective-permute-done.refs_0_), channel_id=1, source_target_pairs={{0,1},{1,0},{2,3},{3,2},{4,5},{5,4},{6,7},{7,6},{8,9},{9,8},{10,11... | collective-permute-start | bytes 562184 | tf_op jit(solution)/shard_map/ppermute | solution.py:325
  11.6 7.1 %collective-permute-start.6 = (bf16[64,1464]{1,0:T(8,128)(2,1)S(1)}, bf16[64,1464]{1,0:T(8,128)(2,1)S(1)}, u32[]{:S(2)}, u32[]{:S(2)}) collective-permute-start(bf16[64,1464]{1,0:T(8,128)(2,1)S(1)} %collective-permute-done.4.refs_1_), channel_id=1, source_target_pairs={{0,1},{1,0},{2,3},{3,2},{4,5},{5,4},{6,7},{7,6},{8,9},{9,8},{10,11... | collective-permute-start | bytes 562184 | tf_op jit(solution)/shard_map/ppermute | solution.py:325
  15.4 6.7 %collective-permute-start.2 = (bf16[64,1464]{1,0:T(8,128)(2,1)S(1)}, bf16[64,1464]{1,0:T(8,128)(2,1)S(1)}, u32[]{:S(2)}, u32[]{:S(2)}) collective-permute-start(bf16[64,1464]{1,0:T(8,128)(2,1)S(1)} %collective-permute-done.1.refs_0_), channel_id=1, source_target_pairs={{0,4},{4,8},{8,12},{12,14},{14,10},{10,6},{6,2},{2,0},{1,5},{5,9},... | collective-permute-start | bytes 562184 | tf_op jit(solution)/shard_map/ppermute | solution.py:322
  17.1 7.8 %collective-permute-start.9 = (bf16[64,1464]{1,0:T(8,128)(2,1)S(1)}, bf16[64,1464]{1,0:T(8,128)(2,1)S(1)}, u32[]{:S(2)}, u32[]{:S(2)}) collective-permute-start(bf16[64,1464]{1,0:T(8,128)(2,1)S(1)} %collective-permute-done.1.refs_0_), channel_id=1, source_target_pairs={{0,1},{1,0},{2,3},{3,2},{4,5},{5,4},{6,7},{7,6},{8,9},{9,8},{10,11... | collective-permute-start | bytes 562184 | tf_op jit(solution)/shard_map/ppermute | solution.py:325
  18.4 6.5 %collective-permute-start.11 = (bf16[64,1464]{1,0:T(8,128)(2,1)S(1)}, bf16[64,1464]{1,0:T(8,128)(2,1)S(1)}, u32[]{:S(2)}, u32[]{:S(2)}) collective-permute-start(bf16[64,1464]{1,0:T(8,128)(2,1)S(1)} %collective-permute-done.8.refs_1_), channel_id=1, source_target_pairs={{4,0},{8,4},{12,8},{14,12},{10,14},{6,10},{2,6},{0,2},{5,1},{9,5},... | collective-permute-start | bytes 562184 | tf_op jit(solution)/shard_map/ppermute | solution.py:324
  18.7 6.3 %collective-permute-start.10 = (bf16[64,1464]{1,0:T(8,128)(2,1)S(1)}, bf16[64,1464]{1,0:T(8,128)(2,1)S(1)}, u32[]{:S(2)}, u32[]{:S(2)}) collective-permute-start(bf16[64,1464]{1,0:T(8,128)(2,1)S(1)} %collective-permute-done.8.refs_1_), channel_id=1, source_target_pairs={{0,1},{1,0},{2,3},{3,2},{4,5},{5,4},{6,7},{7,6},{8,9},{9,8},{10,11... | collective-permute-start | bytes 562184 | tf_op jit(solution)/shard_map/ppermute | solution.py:325
  22.1 6.7 %collective-permute-start.7 = (bf16[64,1464]{1,0:T(8,128)(2,1)S(1)}, bf16[64,1464]{1,0:T(8,128)(2,1)S(1)}, u32[]{:S(2)}, u32[]{:S(2)}) collective-permute-start(bf16[64,1464]{1,0:T(8,128)(2,1)S(1)} %collective-permute-done.2.refs_1_), channel_id=1, source_target_pairs={{0,4},{4,8},{8,12},{12,14},{14,10},{10,6},{6,2},{2,0},{1,5},{5,9},... | collective-permute-start | bytes 562184 | tf_op jit(solution)/shard_map/ppermute | solution.py:322
  23.8 6.6 %collective-permute-start.13 = (bf16[64,1464]{1,0:T(8,128)(2,1)S(1)}, bf16[64,1464]{1,0:T(8,128)(2,1)S(1)}, u32[]{:S(2)}, u32[]{:S(2)}) collective-permute-start(bf16[64,1464]{1,0:T(8,128)(2,1)S(1)} %collective-permute-done.2.refs_1_), channel_id=1, source_target_pairs={{0,1},{1,0},{2,3},{3,2},{4,5},{5,4},{6,7},{7,6},{8,9},{9,8},{10,11... | collective-permute-start | bytes 562184 | tf_op jit(solution)/shard_map/ppermute | solution.py:325
  24.9 5.5 %collective-permute-start.14 = (bf16[64,1464]{1,0:T(8,128)(2,1)S(1)}, bf16[64,1464]{1,0:T(8,128)(2,1)S(1)}, u32[]{:S(2)}, u32[]{:S(2)}) collective-permute-start(bf16[64,1464]{1,0:T(8,128)(2,1)S(1)} %collective-permute-done.11.refs_2_), channel_id=1, source_target_pairs={{0,1},{1,0},{2,3},{3,2},{4,5},{5,4},{6,7},{7,6},{8,9},{9,8},{10,11... | collective-permute-start | bytes 562184 | tf_op jit(solution)/shard_map/ppermute | solution.py:325
  28.7 1.7 %collective-permute-start.12 = (bf16[64,1464]{1,0:T(8,128)(2,1)S(1)}, bf16[64,1464]{1,0:T(8,128)(2,1)S(1)}, u32[]{:S(2)}, u32[]{:S(2)}) collective-permute-start(bf16[64,1464]{1,0:T(8,128)(2,1)S(1)} %collective-permute-done.7.refs_0_), channel_id=1, source_target_pairs={{0,1},{1,0},{2,3},{3,2},{4,5},{5,4},{6,7},{7,6},{8,9},{9,8},{10,11... | collective-permute-start | bytes 562184 | tf_op jit(solution)/shard_map/ppermute | solution.py:333
  32.6 1.8 %collective-permute-start.15 = (bf16[64,1440]{1,0:T(8,128)(2,1)S(1)}, bf16[64,1440]{1,0:T(8,128)(2,1)S(1)}, u32[]{:S(2)}, u32[]{:S(2)}) collective-permute-start(bf16[64,1440]{1,0:T(8,128)(2,1)S(1)} %get-tuple-element.67), channel_id=1, source_target_pairs={{0,1},{1,0},{2,3},{3,2},{4,5},{5,4},{6,7},{7,6},{8,9},{9,8},{10,11... | collective-permute-start | bytes 552968 | tf_op jit(solution)/shard_map/ppermute | solution.py:259
  33.2 6.1 %collective-permute-start.19 = (bf16[128,1440]{1,0:T(8,128)(2,1)S(1)}, bf16[128,1440]{1,0:T(8,128)(2,1)S(1)}, u32[]{:S(2)}, u32[]{:S(2)}) collective-permute-start(bf16[128,1440]{1,0:T(8,128)(2,1)S(1)} %get-tuple-element.76), channel_id=1, source_target_pairs={{0,1},{1,0},{2,3},{3,2},{4,5},{5,4},{6,7},{7,6},{8,9},{9,8},{10,11... | collective-permute-start | bytes 1105928 | tf_op jit(solution)/shard_map/ppermute | solution.py:259
  34.5 7.5 %collective-permute-start.21 = (bf16[64,1440]{1,0:T(8,128)(2,1)S(1)}, bf16[64,1440]{1,0:T(8,128)(2,1)S(1)}, u32[]{:S(2)}, u32[]{:S(2)}) collective-permute-start(bf16[64,1440]{1,0:T(8,128)(2,1)S(1)} %fusion), channel_id=1, source_target_pairs={{0,4},{4,8},{8,12},{12,14},{14,10},{10,6},{6,2},{2,0},{1,5},{5,9},... | collective-permute-start | bytes 552968 | tf_op jit(solution)/shard_map/ppermute | solution.py:343
  36.5 10.1 %collective-permute-start.18 = (bf16[128,1440]{1,0:T(8,128)(2,1)S(1)}, bf16[128,1440]{1,0:T(8,128)(2,1)S(1)}, u32[]{:S(2)}, u32[]{:S(2)}) collective-permute-start(bf16[128,1440]{1,0:T(8,128)(2,1)S(1)} %get-tuple-element.74), channel_id=1, source_target_pairs={{0,1},{1,0},{2,3},{3,2},{4,5},{5,4},{6,7},{7,6},{8,9},{9,8},{10,11... | collective-permute-start | bytes 1105928 | tf_op jit(solution)/shard_map/ppermute | solution.py:338
  39.4 7.2 %collective-permute-start.20 = (bf16[64,1440]{1,0:T(8,128)(2,1)S(1)}, bf16[64,1440]{1,0:T(8,128)(2,1)S(1)}, u32[]{:S(2)}, u32[]{:S(2)}) collective-permute-start(bf16[64,1440]{1,0:T(8,128)(2,1)S(1)} %add_convert_fusion.4), channel_id=1, source_target_pairs={{4,0},{8,4},{12,8},{14,12},{10,14},{6,10},{2,6},{0,2},{5,1},{9,5},... | collective-permute-start | bytes 552968 | tf_op jit(solution)/shard_map/ppermute | solution.py:350
  42.1 6.5 %collective-permute-start.23 = (bf16[64,1440]{1,0:T(8,128)(2,1)S(1)}, bf16[64,1440]{1,0:T(8,128)(2,1)S(1)}, u32[]{:S(2)}, u32[]{:S(2)}) collective-permute-start(bf16[64,1440]{1,0:T(8,128)(2,1)S(1)} %add_convert_fusion.3), channel_id=1, source_target_pairs={{0,4},{4,8},{8,12},{12,14},{14,10},{10,6},{6,2},{2,0},{1,5},{5,9},... | collective-permute-start | bytes 552968 | tf_op jit(solution)/shard_map/ppermute | solution.py:343
  43.9 6.7 %collective-permute-start.17 = (bf16[128,1440]{1,0:T(8,128)(2,1)S(1)}, bf16[128,1440]{1,0:T(8,128)(2,1)S(1)}, u32[]{:S(2)}, u32[]{:S(2)}) collective-permute-start(bf16[128,1440]{1,0:T(8,128)(2,1)S(1)} %get-tuple-element.72), channel_id=1, source_target_pairs={{0,1},{1,0},{2,3},{3,2},{4,5},{5,4},{6,7},{7,6},{8,9},{9,8},{10,11... | collective-permute-start | bytes 1105928 | tf_op jit(solution)/shard_map/ppermute | solution.py:338
  46.7 6.4 %collective-permute-start.22 = (bf16[64,1440]{1,0:T(8,128)(2,1)S(1)}, bf16[64,1440]{1,0:T(8,128)(2,1)S(1)}, u32[]{:S(2)}, u32[]{:S(2)}) collective-permute-start(bf16[64,1440]{1,0:T(8,128)(2,1)S(1)} %shard_map.73), channel_id=1, source_target_pairs={{4,0},{8,4},{12,8},{14,12},{10,14},{6,10},{2,6},{0,2},{5,1},{9,5},... | collective-permute-start | bytes 552968 | tf_op jit(solution)/shard_map/ppermute | solution.py:350
  48.7 5.7 %collective-permute-start.25 = (bf16[64,1440]{1,0:T(8,128)(2,1)S(1)}, bf16[64,1440]{1,0:T(8,128)(2,1)S(1)}, u32[]{:S(2)}, u32[]{:S(2)}) collective-permute-start(bf16[64,1440]{1,0:T(8,128)(2,1)S(1)} %add_convert_fusion.2), channel_id=1, source_target_pairs={{0,4},{4,8},{8,12},{12,14},{14,10},{10,6},{6,2},{2,0},{1,5},{5,9},... | collective-permute-start | bytes 552968 | tf_op jit(solution)/shard_map/ppermute | solution.py:343
  50.5 8.4 %collective-permute-start.16 = (bf16[64,1440]{1,0:T(8,128)(2,1)S(1)}, bf16[64,1440]{1,0:T(8,128)(2,1)S(1)}, u32[]{:S(2)}, u32[]{:S(2)}) collective-permute-start(bf16[64,1440]{1,0:T(8,128)(2,1)S(1)} %get-tuple-element.70), channel_id=1, source_target_pairs={{0,1},{1,0},{2,3},{3,2},{4,5},{5,4},{6,7},{7,6},{8,9},{9,8},{10,11... | collective-permute-start | bytes 552968 | tf_op jit(solution)/shard_map/ppermute | solution.py:346
  53.2 5.7 %collective-permute-start.24 = (bf16[64,1440]{1,0:T(8,128)(2,1)S(1)}, bf16[64,1440]{1,0:T(8,128)(2,1)S(1)}, u32[]{:S(2)}, u32[]{:S(2)}) collective-permute-start(bf16[64,1440]{1,0:T(8,128)(2,1)S(1)} %shard_map.74), channel_id=1, source_target_pairs={{4,0},{8,4},{12,8},{14,12},{10,14},{6,10},{2,6},{0,2},{5,1},{9,5},... | collective-permute-start | bytes 552968 | tf_op jit(solution)/shard_map/ppermute | solution.py:350
  54.5 5.7 %collective-permute-start.26 = (bf16[64,1440]{1,0:T(8,128)(2,1)S(1)}, bf16[64,1440]{1,0:T(8,128)(2,1)S(1)}, u32[]{:S(2)}, u32[]{:S(2)}) collective-permute-start(bf16[64,1440]{1,0:T(8,128)(2,1)S(1)} %add_convert_fusion.1), channel_id=1, source_target_pairs={{0,4},{4,8},{8,12},{12,14},{14,10},{10,6},{6,2},{2,0},{1,5},{5,9},... | collective-permute-start | bytes 552968 | tf_op jit(solution)/shard_map/ppermute | solution.py:343

commit v12 on v11

--- a/solution.py
+++ b/solution.py
@@ -237,7 +237,7 @@
     return outs[:pairs], outs[pairs:]
 
 
-def run_expert_in_stages(place, own, across, swap, weights, n_experts):
+def run_expert_in_stages(place, own, across, swap, weights, n_experts, last_place):
     gate, up, down_mine, down_theirs = weights
     width, hidden = gate.shape
     half = width // 2
@@ -259,7 +259,7 @@
     theirs = [swap(a) for a in theirs]
     mine = call(
         functools.partial(third_kernel, n_blocks, n_experts),
-        place,
+        last_place,
         (*own, units, down_mine),
         outs,
         [],
@@ -332,10 +332,12 @@
     came[far] = after(came[far], done)
     across[far] = swap(came[far])
     last = [far, far - 1, 1 - far]
-    for keys, mine, theirs in zip(([far], last[1:]), *run_expert_in_stages(place, [came[k] for k in last], [across[k] for k in last], swap, weights, n)):
+    near = [(keys, mine, swap(after(theirs, came[far]))) for keys, mine, theirs in near]
+    stages = run_expert_in_stages(
+        place, [came[k] for k in last], [across[k] for k in last], swap, weights, n, after(place, [theirs for *_, theirs in near])
+    )
+    for keys, mine, theirs in (*zip(([far], last[1:]), *stages), *near):
         keep(keys, mine, theirs)
-    for keys, mine, theirs in near:
-        keep(keys, mine, swap(after(theirs, value[far])))
 
     to_ahead = value[far].astype(jnp.bfloat16)
     to_back = (value[far - 1]).astype(jnp.bfloat16)

time: 61.1 us -> 61.2 us (level)
    ppermute x3, waiting for transfers between devices: 7.78 us -> 6.34 us  [ring_body(): front = lax.ppermute(to_back, 'ep', back)]
    ppermute x4, waiting for transfers between devices: 5.92 us -> 7.31 us  [ring_body(): behind = lax.ppermute(to_ahead, 'ep', ahead)]
    ppermute x3, waiting for transfers between devices: 2.43 us -> 1.57 us  [ring_body(): came[k] = lax.ppermute(came[k - 1], 'ep', ahead)]
    ppermute x2, waiting for transfers between devices: 2.3 us -> 3.09 us  [ring_body(): came[-k] = lax.ppermute(came[1 - k], 'ep', back)]
  transfers between devices with their start and end apart: 27 -> 27, of which waited for: 12 -> 12; matrix products, arithmetic and copies ran while one was open for 1% -> 1% of each run, Pallas kernels for 31% -> 35%
where the time goes in v12:
time: 61.2 us; the launch traced here: 61.1 us
  Pallas kernels  22.2 us (36%)
  starting transfers between devices  19.1 us (31%)
  waiting for transfers between devices  18.3 us (30%)
  other arithmetic  1.12 us (2%)
    pallas_call x6, Pallas kernels, call(): pl.pallas_call(kernel, out_shape=out_shape, in_specs=[pl.BlockSpec(memory...  13.1 us
    ppermute x4, waiting for transfers between devices, ring_body(): behind = lax.ppermute(to_ahead, 'ep', ahead)  7.31 us
    ppermute x4, starting transfers between devices, ring_body(): behind = lax.ppermute(to_ahead, 'ep', ahead)  6.96 us
    ppermute x3, waiting for transfers between devices, ring_body(): front = lax.ppermute(to_back, 'ep', back)  6.34 us
    ppermute x3, starting transfers between devices, ring_body(): came[k] = lax.ppermute(came[k - 1], 'ep', ahead)  5.56 us
    pallas_call x1, Pallas kernels, turn_weights(): pl.pallas_call(turn_kernel, out_shape=[in_vmem((width, hidden))] * 2, in_...  4.79 us
    pallas_call x1, Pallas kernels, halve_weights(): pl.pallas_call(halve_kernel, out_shape=[in_vmem((hidden, width // 2))] *...  3.13 us
    ppermute x2, waiting for transfers between devices, ring_body(): came[-k] = lax.ppermute(came[1 - k], 'ep', back)  3.09 us
  transfers between devices with their start and end apart: 27, of which 12 were waited for; matrix products, arithmetic and copies ran while one was open for 1% of the time, Pallas kernels for 35%

profile of v12, /device:TPU:0, one launch (start us, length us, event | category | flops | bytes accessed | tf_op | source)
XLA Modules:
  0.0 61.1 jit_solution(3373379023772617420)
XLA Ops:
  0.0 1.0 %shard_map.64.refs_0_ = bf16[64,1464]{1,0:T(8,128)(2,1)S(1)} custom-call(bf16[64,1440]{1,0:T(8,128)(2,1)} %tokens_in.1, s32[4,64]{1,0:T(4,128)} %bitcast.14, f32[4,64]{1,0:T(4,128)} %bitcast.15), custom_call_target="tpu_custom_call" | custom-call | tf_op jit(solution)/shard_map/pallas_call | solution.py:53
  1.0 3.1 %collective-permute-start.1 = (bf16[64,1464]{1,0:T(8,128)(2,1)S(1)}, bf16[64,1464]{1,0:T(8,128)(2,1)S(1)}, u32[]{:S(2)}, u32[]{:S(2)}) collective-permute-start(bf16[64,1464]{1,0:T(8,128)(2,1)S(1)} %shard_map.64.refs_0_), channel_id=1, source_target_pairs={{0,4},{4,8},{8,12},{12,14},{14,10},{10,6},{6,2},{2,0},{1,5},{5,9},... | collective-permute-start | bytes 562184 | tf_op jit(solution)/shard_map/ppermute | solution.py:316
  4.1 0.1 pad_add_fusion.after_this.place
  4.2 4.8 %shard_map.65 = (bf16[2880,720]{1,0:T(8,128)(2,1)S(1)}, bf16[2880,720]{1,0:T(8,128)(2,1)S(1)}) custom-call(s32[2]{0:T(128)S(1)} %pad_add_fusion.after_this.place, bf16[720,2880]{1,0:T(8,128)(2,1)} %bitcast.11, bf16[720,2880]{1,0:T(8,128)(2,1)} %bitcast.12), custom_call_target="tpu_custom_call" | custom-call | bytes 16588800 | tf_op jit(solution)/shard_map/pallas_call | solution.py:83
  9.0 2.1 %collective-permute-start.5 = (bf16[64,1464]{1,0:T(8,128)(2,1)S(1)}, bf16[64,1464]{1,0:T(8,128)(2,1)S(1)}, u32[]{:S(2)}, u32[]{:S(2)}) collective-permute-start(bf16[64,1464]{1,0:T(8,128)(2,1)S(1)} %collective-permute-done.1.refs_0_), channel_id=1, source_target_pairs={{0,4},{4,8},{8,12},{12,14},{14,10},{10,6},{6,2},{2,0},{1,5},{5,9},... | collective-permute-start | bytes 562184 | tf_op jit(solution)/shard_map/ppermute | solution.py:322
  11.0 0.0 collective-permute-start
  11.1 0.0 collective-permute-done.2.refs_1_
  11.1 0.1 collective-permute-start.8
  11.1 0.4 collective-permute-start.3
  11.6 0.1 collective-permute-start.4
  11.6 3.1 %shard_map.66 = (bf16[720,1440]{1,0:T(8,128)(2,1)S(1)}, bf16[720,1440]{1,0:T(8,128)(2,1)S(1)}) custom-call(s32[2]{0:T(128)S(1)} %pad_add_fusion.after_this.place, bf16[720,2880]{1,0:T(8,128)(2,1)} %bitcast.13), custom_call_target="tpu_custom_call" | custom-call | bytes 16588800 | tf_op jit(solution)/shard_map/pallas_call | solution.py:120
  14.8 0.6 collective-permute-done.5.refs_0_
  15.4 1.7 %collective-permute-start.6 = (bf16[64,1464]{1,0:T(8,128)(2,1)S(1)}, bf16[64,1464]{1,0:T(8,128)(2,1)S(1)}, u32[]{:S(2)}, u32[]{:S(2)}) collective-permute-start(bf16[64,1464]{1,0:T(8,128)(2,1)S(1)} %collective-permute-done.5.refs_0_), channel_id=1, source_target_pairs={{0,4},{4,8},{8,12},{12,14},{14,10},{10,6},{6,2},{2,0},{1,5},{5,9},... | collective-permute-start | bytes 562184 | tf_op jit(solution)/shard_map/ppermute | solution.py:322
  17.1 0.0 collective-permute-done.refs_1_
  17.1 0.0 collective-permute-start.9
  17.1 1.2 %collective-permute-done.8.refs_1_ = bf16[64,1464]{1,0:T(8,128)(2,1)S(1)} collective-permute-done((bf16[64,1464]{1,0:T(8,128)(2,1)S(1)}, bf16[64,1464]{1,0:T(8,128)(2,1)S(1)}, u32[]{:S(2)}, u32[]{:S(2)}) %collective-permute-start.8) | collective-permute-done | bytes 187424 | tf_op jit(solution)/shard_map/ppermute | solution.py:324
  18.4 0.0 collective-permute-start.10
  18.4 0.0 collective-permute-done.3.refs_2_
  18.4 0.3 collective-permute-start.13
  18.7 0.0 collective-permute-done.4.refs_3_
  18.7 2.7 %shard_map.67 = (bf16[128,1440]{1,0:T(8,128)(2,1)S(1)}, bf16[128,1440]{1,0:T(8,128)(2,1)S(1)}) custom-call(s32[2]{0:T(128)S(1)} %pad_add_fusion.after_this.place, bf16[64,1464]{1,0:T(8,128)(2,1)S(1)} %collective-permute-done.1.refs_0_, bf16[64,1464]{1,0:T(8,128)(2,1)S(1)} %collective-permute-done.2.refs_1_, ...), custom_call_target="tpu_custom_call" | custom-call | flops 1592524800 | bytes 12441600 | tf_op jit(solution)/shard_map/pallas_call | solution.py:210
  21.4 0.7 %collective-permute-done.6.refs_1_ = bf16[64,1464]{1,0:T(8,128)(2,1)S(1)} collective-permute-done((bf16[64,1464]{1,0:T(8,128)(2,1)S(1)}, bf16[64,1464]{1,0:T(8,128)(2,1)S(1)}, u32[]{:S(2)}, u32[]{:S(2)}) %collective-permute-start.6) | collective-permute-done | bytes 187424 | tf_op jit(solution)/shard_map/ppermute | solution.py:322
  22.1 1.7 %collective-permute-start.7 = (bf16[64,1464]{1,0:T(8,128)(2,1)S(1)}, bf16[64,1464]{1,0:T(8,128)(2,1)S(1)}, u32[]{:S(2)}, u32[]{:S(2)}) collective-permute-start(bf16[64,1464]{1,0:T(8,128)(2,1)S(1)} %collective-permute-done.6.refs_1_), channel_id=1, source_target_pairs={{0,4},{4,8},{8,12},{12,14},{14,10},{10,6},{6,2},{2,0},{1,5},{5,9},... | collective-permute-start | bytes 562184 | tf_op jit(solution)/shard_map/ppermute | solution.py:322
  23.8 1.9 %collective-permute-done.13.refs_2_ = bf16[64,1464]{1,0:T(8,128)(2,1)S(1)} collective-permute-done((bf16[64,1464]{1,0:T(8,128)(2,1)S(1)}, bf16[64,1464]{1,0:T(8,128)(2,1)S(1)}, u32[]{:S(2)}, u32[]{:S(2)}) %collective-permute-start.13) | collective-permute-done | bytes 187424 | tf_op jit(solution)/shard_map/ppermute | solution.py:324
  25.7 0.0 collective-permute-start.16
  25.7 0.0 collective-permute-done.9.refs_2_
  25.7 2.7 %shard_map.68 = (bf16[128,1440]{1,0:T(8,128)(2,1)S(1)}, bf16[128,1440]{1,0:T(8,128)(2,1)S(1)}) custom-call(s32[2]{0:T(128)S(1)} %pad_add_fusion.after_this.place, bf16[64,1464]{1,0:T(8,128)(2,1)S(1)} %collective-permute-done.5.refs_0_, bf16[64,1464]{1,0:T(8,128)(2,1)S(1)} %collective-permute-done.8.refs_1_, ...), custom_call_target="tpu_custom_call" | custom-call | flops 1592524800 | bytes 12441600 | tf_op jit(solution)/shard_map/pallas_call | solution.py:210
  28.4 0.3 collective-permute-done.7.refs_0_
  28.7 0.3 collective-permute-start.14
  29.0 0.2 collective-permute-start.12
  29.2 0.3 collective-permute-start.11
  29.5 1.6 %shard_map.69 = (f32[192,720]{1,0:T(8,128)S(1)}, f32[192,720]{1,0:T(8,128)S(1)}) custom-call(s32[2]{0:T(128)S(1)} %pad_add_fusion.after_this.place, bf16[64,1464]{1,0:T(8,128)(2,1)S(1)} %collective-permute-done.7.refs_0_, bf16[64,1464]{1,0:T(8,128)(2,1)S(1)} %collective-permute-done.6.refs_1_, bf16[64,1464]{1,0:T(8,128)(2,1)S(1)} %collective-permute-done.13.refs_2_, ...), custom_call_target="tpu_custom_call" | custom-call | flops 796262400 | bytes 6220800 | tf_op jit(solution)/shard_map/pallas_call | solution.py:210
  31.1 0.0 collective-permute-done.16.refs_5_
  31.2 2.2 %shard_map.70 = (bf16[192,720]{1,0:T(8,128)(2,1)S(1)}, bf16[64,1440]{1,0:T(8,128)(2,1)S(1)}, bf16[128,1440]{1,0:T(8,128)(2,1)S(1)}) custom-call(s32[2]{0:T(128)S(1)} %pad_add_fusion.after_this.place, bf16[64,1464]{1,0:T(8,128)(2,1)S(1)} %collective-permute-done.7.refs_0_, bf16[64,1464]{1,0:T(8,128)(2,1)S(1)} %collective-permute-done.6.refs_1_, ...), custom_call_target="tpu_custom_call" | custom-call | flops 1194393600 | bytes 9331200 | tf_op jit(solution)/shard_map/pallas_call | solution.py:210
  33.4 0.2 collective-permute-start.17
  33.6 0.3 collective-permute-start.19
  34.0 0.0 collective-permute-done.11
  34.0 1.2 %shard_map.71 = (bf16[64,1440]{1,0:T(8,128)(2,1)S(1)}, bf16[128,1440]{1,0:T(8,128)(2,1)S(1)}) custom-call(s32[2]{0:T(128)S(1)} %pad_add_fusion.after_this.place, bf16[64,1464]{1,0:T(8,128)(2,1)S(1)} %collective-permute-done.7.refs_0_, bf16[64,1464]{1,0:T(8,128)(2,1)S(1)} %collective-permute-done.6.refs_1_, ...), custom_call_target="tpu_custom_call" | custom-call | flops 398131200 | bytes 3110400 | tf_op jit(solution)/shard_map/pallas_call | solution.py:210
  35.1 0.0 collective-permute-done.17
  35.2 1.6 %collective-permute-start.21 = (bf16[64,1440]{1,0:T(8,128)(2,1)S(1)}, bf16[64,1440]{1,0:T(8,128)(2,1)S(1)}, u32[]{:S(2)}, u32[]{:S(2)}) collective-permute-start(bf16[64,1440]{1,0:T(8,128)(2,1)S(1)} %add_convert_fusion.5), channel_id=1, source_target_pairs={{0,4},{4,8},{8,12},{12,14},{14,10},{10,6},{6,2},{2,0},{1,5},{5,9},... | collective-permute-start | bytes 552968 | tf_op jit(solution)/shard_map/ppermute | solution.py:345
  36.8 2.7 %shard_map.72 = (bf16[64,1440]{1,0:T(8,128)(2,1)S(1)}, bf16[64,1440]{1,0:T(8,128)(2,1)S(1)}) custom-call(s32[2]{0:T(128)S(1)} %pad_add_fusion.after_this.place, bf16[64,1464]{1,0:T(8,128)(2,1)S(1)} %shard_map.64.refs_0_, bf16[64,1464]{1,0:T(8,128)(2,1)S(1)} %collective-permute-done.refs_1_, ...), custom_call_target="tpu_custom_call" | custom-call | flops 1592524800 | bytes 12441600 | tf_op jit(solution)/shard_map/pallas_call | solution.py:210
  39.5 0.0 collective-permute-done.19
  39.5 0.1 add_convert_fusion.4
  39.6 0.5 collective-permute-start.20
  40.1 2.2 %collective-permute-done.21 = bf16[64,1440]{1,0:T(8,128)(2,1)S(1)} collective-permute-done((bf16[64,1440]{1,0:T(8,128)(2,1)S(1)}, bf16[64,1440]{1,0:T(8,128)(2,1)S(1)}, u32[]{:S(2)}, u32[]{:S(2)}) %collective-permute-start.21) | collective-permute-done | bytes 184352 | tf_op jit(solution)/shard_map/ppermute | solution.py:345
  42.2 0.1 add_convert_fusion.3
  42.3 1.8 %collective-permute-start.23 = (bf16[64,1440]{1,0:T(8,128)(2,1)S(1)}, bf16[64,1440]{1,0:T(8,128)(2,1)S(1)}, u32[]{:S(2)}, u32[]{:S(2)}) collective-permute-start(bf16[64,1440]{1,0:T(8,128)(2,1)S(1)} %add_convert_fusion.3), channel_id=1, source_target_pairs={{0,4},{4,8},{8,12},{12,14},{14,10},{10,6},{6,2},{2,0},{1,5},{5,9},... | collective-permute-start | bytes 552968 | tf_op jit(solution)/shard_map/ppermute | solution.py:345
  44.2 2.3 %collective-permute-done.20.refs_2_ = bf16[64,1440]{1,0:T(8,128)(2,1)S(1)} collective-permute-done((bf16[64,1440]{1,0:T(8,128)(2,1)S(1)}, bf16[64,1440]{1,0:T(8,128)(2,1)S(1)}, u32[]{:S(2)}, u32[]{:S(2)}) %collective-permute-start.20) | collective-permute-done | bytes 184352 | tf_op jit(solution)/shard_map/ppermute | solution.py:352
  46.5 0.1 shard_map.73
  46.6 0.3 collective-permute-start.22
  46.9 1.8 %collective-permute-done.23 = bf16[64,1440]{1,0:T(8,128)(2,1)S(1)} collective-permute-done((bf16[64,1440]{1,0:T(8,128)(2,1)S(1)}, bf16[64,1440]{1,0:T(8,128)(2,1)S(1)}, u32[]{:S(2)}, u32[]{:S(2)}) %collective-permute-start.23) | collective-permute-done | bytes 184352 | tf_op jit(solution)/shard_map/ppermute | solution.py:345
  48.8 0.1 add_convert_fusion.2
  48.8 1.8 %collective-permute-start.25 = (bf16[64,1440]{1,0:T(8,128)(2,1)S(1)}, bf16[64,1440]{1,0:T(8,128)(2,1)S(1)}, u32[]{:S(2)}, u32[]{:S(2)}) collective-permute-start(bf16[64,1440]{1,0:T(8,128)(2,1)S(1)} %add_convert_fusion.2), channel_id=1, source_target_pairs={{0,4},{4,8},{8,12},{12,14},{14,10},{10,6},{6,2},{2,0},{1,5},{5,9},... | collective-permute-start | bytes 552968 | tf_op jit(solution)/shard_map/ppermute | solution.py:345
  50.6 0.1 collective-permute-start.18
  50.7 1.9 %collective-permute-done.22.refs_2_ = bf16[64,1440]{1,0:T(8,128)(2,1)S(1)} collective-permute-done((bf16[64,1440]{1,0:T(8,128)(2,1)S(1)}, bf16[64,1440]{1,0:T(8,128)(2,1)S(1)}, u32[]{:S(2)}, u32[]{:S(2)}) %collective-permute-start.22) | collective-permute-done | bytes 184352 | tf_op jit(solution)/shard_map/ppermute | solution.py:352
  52.7 0.1 shard_map.74
  52.7 0.3 collective-permute-start.24
  53.1 1.5 %collective-permute-done.25 = bf16[64,1440]{1,0:T(8,128)(2,1)S(1)} collective-permute-done((bf16[64,1440]{1,0:T(8,128)(2,1)S(1)}, bf16[64,1440]{1,0:T(8,128)(2,1)S(1)}, u32[]{:S(2)}, u32[]{:S(2)}) %collective-permute-start.25) | collective-permute-done | bytes 184352 | tf_op jit(solution)/shard_map/ppermute | solution.py:345
  54.6 0.1 add_convert_fusion.1
  54.6 1.8 %collective-permute-start.26 = (bf16[64,1440]{1,0:T(8,128)(2,1)S(1)}, bf16[64,1440]{1,0:T(8,128)(2,1)S(1)}, u32[]{:S(2)}, u32[]{:S(2)}) collective-permute-start(bf16[64,1440]{1,0:T(8,128)(2,1)S(1)} %add_convert_fusion.1), channel_id=1, source_target_pairs={{0,4},{4,8},{8,12},{12,14},{14,10},{10,6},{6,2},{2,0},{1,5},{5,9},... | collective-permute-start | bytes 552968 | tf_op jit(solution)/shard_map/ppermute | solution.py:345
  56.4 2.1 %collective-permute-done.24.refs_2_ = bf16[64,1440]{1,0:T(8,128)(2,1)S(1)} collective-permute-done((bf16[64,1440]{1,0:T(8,128)(2,1)S(1)}, bf16[64,1440]{1,0:T(8,128)(2,1)S(1)}, u32[]{:S(2)}, u32[]{:S(2)}) %collective-permute-start.24) | collective-permute-done | bytes 184352 | tf_op jit(solution)/shard_map/ppermute | solution.py:352
  58.5 0.1 shard_map.75
  58.5 1.8 %collective-permute-done.26 = bf16[64,1440]{1,0:T(8,128)(2,1)S(1)} collective-permute-done((bf16[64,1440]{1,0:T(8,128)(2,1)S(1)}, bf16[64,1440]{1,0:T(8,128)(2,1)S(1)}, u32[]{:S(2)}, u32[]{:S(2)}) %collective-permute-start.26) | collective-permute-done | bytes 184352 | tf_op jit(solution)/shard_map/ppermute | solution.py:345
  60.4 0.7 %add_convert_fusion = bf16[64,1440]{1,0:T(8,128)(2,1)} fusion(bf16[64,1440]{1,0:T(8,128)(2,1)S(1)} %collective-permute-done.26, bf16[64,1440]{1,0:T(8,128)(2,1)S(1)} %shard_map.75), kind=kLoop, calls=%fused_computation | loop fusion | flops 368640 | bytes 552960 | tf_op jit(solution)/shard_map/convert_element_type | solution.py:354
  (13 shorter events, 0.1 us)
Async XLA Ops:
  1.0 8.0 %collective-permute-start.1 = (bf16[64,1464]{1,0:T(8,128)(2,1)S(1)}, bf16[64,1464]{1,0:T(8,128)(2,1)S(1)}, u32[]{:S(2)}, u32[]{:S(2)}) collective-permute-start(bf16[64,1464]{1,0:T(8,128)(2,1)S(1)} %shard_map.64.refs_0_), channel_id=1, source_target_pairs={{0,4},{4,8},{8,12},{12,14},{14,10},{10,6},{6,2},{2,0},{1,5},{5,9},... | collective-permute-start | bytes 562184 | tf_op jit(solution)/shard_map/ppermute | solution.py:316
  4.1 7.0 %collective-permute-start.2 = (bf16[64,1464]{1,0:T(8,128)(2,1)S(1)}, bf16[64,1464]{1,0:T(8,128)(2,1)S(1)}, u32[]{:S(2)}, u32[]{:S(2)}) collective-permute-start(bf16[64,1464]{1,0:T(8,128)(2,1)S(1)} %shard_map.64.refs_0_), channel_id=1, source_target_pairs={{4,0},{8,4},{12,8},{14,12},{10,14},{6,10},{2,6},{0,2},{5,1},{9,5},... | collective-permute-start | bytes 562184 | tf_op jit(solution)/shard_map/ppermute | solution.py:317
  9.0 6.4 %collective-permute-start.5 = (bf16[64,1464]{1,0:T(8,128)(2,1)S(1)}, bf16[64,1464]{1,0:T(8,128)(2,1)S(1)}, u32[]{:S(2)}, u32[]{:S(2)}) collective-permute-start(bf16[64,1464]{1,0:T(8,128)(2,1)S(1)} %collective-permute-done.1.refs_0_), channel_id=1, source_target_pairs={{0,4},{4,8},{8,12},{12,14},{14,10},{10,6},{6,2},{2,0},{1,5},{5,9},... | collective-permute-start | bytes 562184 | tf_op jit(solution)/shard_map/ppermute | solution.py:322
  11.0 6.1 %collective-permute-start = (bf16[64,1464]{1,0:T(8,128)(2,1)S(1)}, bf16[64,1464]{1,0:T(8,128)(2,1)S(1)}, u32[]{:S(2)}, u32[]{:S(2)}) collective-permute-start(bf16[64,1464]{1,0:T(8,128)(2,1)S(1)} %shard_map.64.refs_0_), channel_id=1, source_target_pairs={{0,1},{1,0},{2,3},{3,2},{4,5},{5,4},{6,7},{7,6},{8,9},{9,8},{10,11... | collective-permute-start | bytes 562184 | tf_op jit(solution)/shard_map/ppermute | solution.py:318
  11.1 7.3 %collective-permute-start.8 = (bf16[64,1464]{1,0:T(8,128)(2,1)S(1)}, bf16[64,1464]{1,0:T(8,128)(2,1)S(1)}, u32[]{:S(2)}, u32[]{:S(2)}) collective-permute-start(bf16[64,1464]{1,0:T(8,128)(2,1)S(1)} %collective-permute-done.2.refs_1_), channel_id=1, source_target_pairs={{4,0},{8,4},{12,8},{14,12},{10,14},{6,10},{2,6},{0,2},{5,1},{9,5},... | collective-permute-start | bytes 562184 | tf_op jit(solution)/shard_map/ppermute | solution.py:324
  11.1 7.3 %collective-permute-start.3 = (bf16[64,1464]{1,0:T(8,128)(2,1)S(1)}, bf16[64,1464]{1,0:T(8,128)(2,1)S(1)}, u32[]{:S(2)}, u32[]{:S(2)}) collective-permute-start(bf16[64,1464]{1,0:T(8,128)(2,1)S(1)} %collective-permute-done.1.refs_0_), channel_id=1, source_target_pairs={{0,1},{1,0},{2,3},{3,2},{4,5},{5,4},{6,7},{7,6},{8,9},{9,8},{10,11... | collective-permute-start | bytes 562184 | tf_op jit(solution)/shard_map/ppermute | solution.py:325
  11.6 7.1 %collective-permute-start.4 = (bf16[64,1464]{1,0:T(8,128)(2,1)S(1)}, bf16[64,1464]{1,0:T(8,128)(2,1)S(1)}, u32[]{:S(2)}, u32[]{:S(2)}) collective-permute-start(bf16[64,1464]{1,0:T(8,128)(2,1)S(1)} %collective-permute-done.2.refs_1_), channel_id=1, source_target_pairs={{0,1},{1,0},{2,3},{3,2},{4,5},{5,4},{6,7},{7,6},{8,9},{9,8},{10,11... | collective-permute-start | bytes 562184 | tf_op jit(solution)/shard_map/ppermute | solution.py:325
  15.4 6.7 %collective-permute-start.6 = (bf16[64,1464]{1,0:T(8,128)(2,1)S(1)}, bf16[64,1464]{1,0:T(8,128)(2,1)S(1)}, u32[]{:S(2)}, u32[]{:S(2)}) collective-permute-start(bf16[64,1464]{1,0:T(8,128)(2,1)S(1)} %collective-permute-done.5.refs_0_), channel_id=1, source_target_pairs={{0,4},{4,8},{8,12},{12,14},{14,10},{10,6},{6,2},{2,0},{1,5},{5,9},... | collective-permute-start | bytes 562184 | tf_op jit(solution)/shard_map/ppermute | solution.py:322
  17.1 8.6 %collective-permute-start.9 = (bf16[64,1464]{1,0:T(8,128)(2,1)S(1)}, bf16[64,1464]{1,0:T(8,128)(2,1)S(1)}, u32[]{:S(2)}, u32[]{:S(2)}) collective-permute-start(bf16[64,1464]{1,0:T(8,128)(2,1)S(1)} %collective-permute-done.5.refs_0_), channel_id=1, source_target_pairs={{0,1},{1,0},{2,3},{3,2},{4,5},{5,4},{6,7},{7,6},{8,9},{9,8},{10,11... | collective-permute-start | bytes 562184 | tf_op jit(solution)/shard_map/ppermute | solution.py:325
  18.4 7.3 %collective-permute-start.10 = (bf16[64,1464]{1,0:T(8,128)(2,1)S(1)}, bf16[64,1464]{1,0:T(8,128)(2,1)S(1)}, u32[]{:S(2)}, u32[]{:S(2)}) collective-permute-start(bf16[64,1464]{1,0:T(8,128)(2,1)S(1)} %collective-permute-done.8.refs_1_), channel_id=1, source_target_pairs={{0,1},{1,0},{2,3},{3,2},{4,5},{5,4},{6,7},{7,6},{8,9},{9,8},{10,11... | collective-permute-start | bytes 562184 | tf_op jit(solution)/shard_map/ppermute | solution.py:325
  18.4 7.3 %collective-permute-start.13 = (bf16[64,1464]{1,0:T(8,128)(2,1)S(1)}, bf16[64,1464]{1,0:T(8,128)(2,1)S(1)}, u32[]{:S(2)}, u32[]{:S(2)}) collective-permute-start(bf16[64,1464]{1,0:T(8,128)(2,1)S(1)} %collective-permute-done.8.refs_1_), channel_id=1, source_target_pairs={{4,0},{8,4},{12,8},{14,12},{10,14},{6,10},{2,6},{0,2},{5,1},{9,5},... | collective-permute-start | bytes 562184 | tf_op jit(solution)/shard_map/ppermute | solution.py:324
  22.1 6.6 %collective-permute-start.7 = (bf16[64,1464]{1,0:T(8,128)(2,1)S(1)}, bf16[64,1464]{1,0:T(8,128)(2,1)S(1)}, u32[]{:S(2)}, u32[]{:S(2)}) collective-permute-start(bf16[64,1464]{1,0:T(8,128)(2,1)S(1)} %collective-permute-done.6.refs_1_), channel_id=1, source_target_pairs={{0,4},{4,8},{8,12},{12,14},{14,10},{10,6},{6,2},{2,0},{1,5},{5,9},... | collective-permute-start | bytes 562184 | tf_op jit(solution)/shard_map/ppermute | solution.py:322
  23.8 7.3 %collective-permute-start.15 = (bf16[64,1464]{1,0:T(8,128)(2,1)S(1)}, bf16[64,1464]{1,0:T(8,128)(2,1)S(1)}, u32[]{:S(2)}, u32[]{:S(2)}) collective-permute-start(bf16[64,1464]{1,0:T(8,128)(2,1)S(1)} %collective-permute-done.6.refs_1_), channel_id=1, source_target_pairs={{0,1},{1,0},{2,3},{3,2},{4,5},{5,4},{6,7},{7,6},{8,9},{9,8},{10,11... | collective-permute-start | bytes 562184 | tf_op jit(solution)/shard_map/ppermute | solution.py:325
  25.7 5.4 %collective-permute-start.16 = (bf16[64,1464]{1,0:T(8,128)(2,1)S(1)}, bf16[64,1464]{1,0:T(8,128)(2,1)S(1)}, u32[]{:S(2)}, u32[]{:S(2)}) collective-permute-start(bf16[64,1464]{1,0:T(8,128)(2,1)S(1)} %collective-permute-done.13.refs_2_), channel_id=1, source_target_pairs={{0,1},{1,0},{2,3},{3,2},{4,5},{5,4},{6,7},{7,6},{8,9},{9,8},{10,11... | collective-permute-start | bytes 562184 | tf_op jit(solution)/shard_map/ppermute | solution.py:325
  28.7 2.5 %collective-permute-start.14 = (bf16[64,1464]{1,0:T(8,128)(2,1)S(1)}, bf16[64,1464]{1,0:T(8,128)(2,1)S(1)}, u32[]{:S(2)}, u32[]{:S(2)}) collective-permute-start(bf16[64,1464]{1,0:T(8,128)(2,1)S(1)} %collective-permute-done.7.refs_0_), channel_id=1, source_target_pairs={{0,1},{1,0},{2,3},{3,2},{4,5},{5,4},{6,7},{7,6},{8,9},{9,8},{10,11... | collective-permute-start | bytes 562184 | tf_op jit(solution)/shard_map/ppermute | solution.py:333
  29.0 5.0 %collective-permute-start.12 = (bf16[128,1440]{1,0:T(8,128)(2,1)S(1)}, bf16[128,1440]{1,0:T(8,128)(2,1)S(1)}, u32[]{:S(2)}, u32[]{:S(2)}) collective-permute-start(bf16[128,1440]{1,0:T(8,128)(2,1)S(1)} %get-tuple-element.64), channel_id=1, source_target_pairs={{0,1},{1,0},{2,3},{3,2},{4,5},{5,4},{6,7},{7,6},{8,9},{9,8},{10,11... | collective-permute-start | bytes 1105928 | tf_op jit(solution)/shard_map/ppermute | solution.py:335
  29.2 4.8 %collective-permute-start.11 = (bf16[128,1440]{1,0:T(8,128)(2,1)S(1)}, bf16[128,1440]{1,0:T(8,128)(2,1)S(1)}, u32[]{:S(2)}, u32[]{:S(2)}) collective-permute-start(bf16[128,1440]{1,0:T(8,128)(2,1)S(1)} %get-tuple-element.63), channel_id=1, source_target_pairs={{0,1},{1,0},{2,3},{3,2},{4,5},{5,4},{6,7},{7,6},{8,9},{9,8},{10,11... | collective-permute-start | bytes 1105928 | tf_op jit(solution)/shard_map/ppermute | solution.py:335
  33.4 1.8 %collective-permute-start.17 = (bf16[64,1440]{1,0:T(8,128)(2,1)S(1)}, bf16[64,1440]{1,0:T(8,128)(2,1)S(1)}, u32[]{:S(2)}, u32[]{:S(2)}) collective-permute-start(bf16[64,1440]{1,0:T(8,128)(2,1)S(1)} %get-tuple-element.71), channel_id=1, source_target_pairs={{0,1},{1,0},{2,3},{3,2},{4,5},{5,4},{6,7},{7,6},{8,9},{9,8},{10,11... | collective-permute-start | bytes 552968 | tf_op jit(solution)/shard_map/ppermute | solution.py:259
  33.6 5.9 %collective-permute-start.19 = (bf16[128,1440]{1,0:T(8,128)(2,1)S(1)}, bf16[128,1440]{1,0:T(8,128)(2,1)S(1)}, u32[]{:S(2)}, u32[]{:S(2)}) collective-permute-start(bf16[128,1440]{1,0:T(8,128)(2,1)S(1)} %get-tuple-element.78), channel_id=1, source_target_pairs={{0,1},{1,0},{2,3},{3,2},{4,5},{5,4},{6,7},{7,6},{8,9},{9,8},{10,11... | collective-permute-start | bytes 1105928 | tf_op jit(solution)/shard_map/ppermute | solution.py:259
  35.2 7.0 %collective-permute-start.21 = (bf16[64,1440]{1,0:T(8,128)(2,1)S(1)}, bf16[64,1440]{1,0:T(8,128)(2,1)S(1)}, u32[]{:S(2)}, u32[]{:S(2)}) collective-permute-start(bf16[64,1440]{1,0:T(8,128)(2,1)S(1)} %add_convert_fusion.5), channel_id=1, source_target_pairs={{0,4},{4,8},{8,12},{12,14},{14,10},{10,6},{6,2},{2,0},{1,5},{5,9},... | collective-permute-start | bytes 552968 | tf_op jit(solution)/shard_map/ppermute | solution.py:345
  39.6 6.9 %collective-permute-start.20 = (bf16[64,1440]{1,0:T(8,128)(2,1)S(1)}, bf16[64,1440]{1,0:T(8,128)(2,1)S(1)}, u32[]{:S(2)}, u32[]{:S(2)}) collective-permute-start(bf16[64,1440]{1,0:T(8,128)(2,1)S(1)} %add_convert_fusion.4), channel_id=1, source_target_pairs={{4,0},{8,4},{12,8},{14,12},{10,14},{6,10},{2,6},{0,2},{5,1},{9,5},... | collective-permute-start | bytes 552968 | tf_op jit(solution)/shard_map/ppermute | solution.py:352
  42.3 6.4 %collective-permute-start.23 = (bf16[64,1440]{1,0:T(8,128)(2,1)S(1)}, bf16[64,1440]{1,0:T(8,128)(2,1)S(1)}, u32[]{:S(2)}, u32[]{:S(2)}) collective-permute-start(bf16[64,1440]{1,0:T(8,128)(2,1)S(1)} %add_convert_fusion.3), channel_id=1, source_target_pairs={{0,4},{4,8},{8,12},{12,14},{14,10},{10,6},{6,2},{2,0},{1,5},{5,9},... | collective-permute-start | bytes 552968 | tf_op jit(solution)/shard_map/ppermute | solution.py:345
  46.6 6.1 %collective-permute-start.22 = (bf16[64,1440]{1,0:T(8,128)(2,1)S(1)}, bf16[64,1440]{1,0:T(8,128)(2,1)S(1)}, u32[]{:S(2)}, u32[]{:S(2)}) collective-permute-start(bf16[64,1440]{1,0:T(8,128)(2,1)S(1)} %shard_map.73), channel_id=1, source_target_pairs={{4,0},{8,4},{12,8},{14,12},{10,14},{6,10},{2,6},{0,2},{5,1},{9,5},... | collective-permute-start | bytes 552968 | tf_op jit(solution)/shard_map/ppermute | solution.py:352
  48.8 5.7 %collective-permute-start.25 = (bf16[64,1440]{1,0:T(8,128)(2,1)S(1)}, bf16[64,1440]{1,0:T(8,128)(2,1)S(1)}, u32[]{:S(2)}, u32[]{:S(2)}) collective-permute-start(bf16[64,1440]{1,0:T(8,128)(2,1)S(1)} %add_convert_fusion.2), channel_id=1, source_target_pairs={{0,4},{4,8},{8,12},{12,14},{14,10},{10,6},{6,2},{2,0},{1,5},{5,9},... | collective-permute-start | bytes 552968 | tf_op jit(solution)/shard_map/ppermute | solution.py:345
  50.6 7.8 %collective-permute-start.18 = (bf16[64,1440]{1,0:T(8,128)(2,1)S(1)}, bf16[64,1440]{1,0:T(8,128)(2,1)S(1)}, u32[]{:S(2)}, u32[]{:S(2)}) collective-permute-start(bf16[64,1440]{1,0:T(8,128)(2,1)S(1)} %get-tuple-element.74), channel_id=1, source_target_pairs={{0,1},{1,0},{2,3},{3,2},{4,5},{5,4},{6,7},{7,6},{8,9},{9,8},{10,11... | collective-permute-start | bytes 552968 | tf_op jit(solution)/shard_map/ppermute | solution.py:348
  52.7 5.7 %collective-permute-start.24 = (bf16[64,1440]{1,0:T(8,128)(2,1)S(1)}, bf16[64,1440]{1,0:T(8,128)(2,1)S(1)}, u32[]{:S(2)}, u32[]{:S(2)}) collective-permute-start(bf16[64,1440]{1,0:T(8,128)(2,1)S(1)} %shard_map.74), channel_id=1, source_target_pairs={{4,0},{8,4},{12,8},{14,12},{10,14},{6,10},{2,6},{0,2},{5,1},{9,5},... | collective-permute-start | bytes 552968 | tf_op jit(solution)/shard_map/ppermute | solution.py:352
  54.6 5.7 %collective-permute-start.26 = (bf16[64,1440]{1,0:T(8,128)(2,1)S(1)}, bf16[64,1440]{1,0:T(8,128)(2,1)S(1)}, u32[]{:S(2)}, u32[]{:S(2)}) collective-permute-start(bf16[64,1440]{1,0:T(8,128)(2,1)S(1)} %add_convert_fusion.1), channel_id=1, source_target_pairs={{0,4},{4,8},{8,12},{12,14},{14,10},{10,6},{6,2},{2,0},{1,5},{5,9},... | collective-permute-start | bytes 552968 | tf_op jit(solution)/shard_map/ppermute | solution.py:345

commit v13 on v11

--- a/solution.py
+++ b/solution.py
@@ -315,7 +315,6 @@
 
     came[1] = lax.ppermute(packed, "ep", ahead)
     came[-1] = lax.ppermute(packed, "ep", back)
-    across[0] = swap(packed)
     weights, done, near = [gate, up], up, []
     for k in range(2, far + 1):
         came[k - 1], came[1 - k] = after(came[k - 1], done), after(came[1 - k], done)
@@ -327,7 +326,7 @@
             weights += halve_weights(after(place, came[1]), w_down[0])
             done = weights[-1]
         else:
-            near += run([k - 2, 2 - k], across[0] if k == 3 else None)
+            near += run([k - 2, 2 - k])
             done = near[-1][-1]
     came[far] = after(came[far], done)
     across[far] = swap(came[far])
@@ -341,13 +340,17 @@
     to_back = (value[far - 1]).astype(jnp.bfloat16)
     for k in range(far - 1, -1, -1):
         behind = lax.ppermute(to_ahead, "ep", ahead)
-        if k == far - 1:
-            ((keys, mine, done),) = run([0], to_ahead)
-            keep(keys, mine, swap(done))
-        else:
+        done = to_ahead
+        if k < far - 1:
             to_back = done = add(*parts[k], after(front, to_ahead))
         if k:
             front = lax.ppermute(to_back, "ep", back)
+        if k == 2:
+            across[0] = swap(after(packed, to_ahead))
+        if k == 1:
+            ((keys, mine, done),) = run([0], done)
+            keep(keys, mine, swap(done))
+        if k:
             to_ahead = (value[-k] + after(behind, done).astype(jnp.float32)).astype(jnp.bfloat16)
     return (to_back.astype(jnp.float32) + behind.astype(jnp.float32)).astype(jnp.bfloat16)
 

time: 61.1 us -> 72.9 us (1.19)
  local copies, waits for them, and re-layouts: 0.06 us -> 9.57 us
  other arithmetic: 1.12 us -> 3.27 us
  waiting for transfers between devices: 18.5 us -> 16.6 us
  Pallas kernels: 22.2 us -> 23.1 us
  starting transfers between devices: 18.8 us -> 19.6 us
    ppermute x3, waiting for transfers between devices: 7.78 us -> 0.01 us  [ring_body(): front = lax.ppermute(to_back, 'ep', back)]
    unnamed x0 -> x20, local copies, waits for them, and re-layouts: none -> 7.66 us
    ppermute x4, waiting for transfers between devices: 5.92 us -> 13.4 us  [ring_body(): behind = lax.ppermute(to_ahead, 'ep', ahead)]
    convert_element_type x3, other arithmetic: 0.22 us -> 2.37 us  [ring_body(): (value[-k] + after(behind, done).astype(jnp.float32)).astype(jnp.bfloat16)]
    slice x4, local copies, waits for them, and re-layouts: 0.06 us -> 1.91 us  [keep(): parts[k] = (mine[span], theirs[span])]
    ppermute x2, waiting for transfers between devices: 2.3 us -> 0.84 us  [ring_body(): came[-k] = lax.ppermute(came[1 - k], 'ep', back)]
    pallas_call x6, Pallas kernels: 13.1 us -> 14 us  [call(): pl.pallas_call(kernel, out_shape=out_shape, in_specs=[pl.BlockSpec(memory...]
  transfers between devices with their start and end apart: 27 -> 27, of which waited for: 12 -> 7; matrix products, arithmetic and copies ran while one was open for 1% -> 6% of each run, Pallas kernels for 31% -> 27%
where the time goes in v13:
time: 72.9 us; the launch traced here: 72.5 us
  Pallas kernels  23.1 us (32%)
  starting transfers between devices  19.6 us (27%)
  waiting for transfers between devices  16.6 us (23%)
  local copies, waits for them, and re-layouts  9.57 us (13%)
  other arithmetic  3.27 us (4%)
    pallas_call x6, Pallas kernels, call(): pl.pallas_call(kernel, out_shape=out_shape, in_specs=[pl.BlockSpec(memory...  14 us
    ppermute x4, waiting for transfers between devices, ring_body(): behind = lax.ppermute(to_ahead, 'ep', ahead)  13.4 us
    unnamed x20, local copies, waits for them, and re-layouts  7.66 us
    ppermute x4, starting transfers between devices, ring_body(): behind = lax.ppermute(to_ahead, 'ep', ahead)  7.37 us
    ppermute x3, starting transfers between devices, ring_body(): came[k] = lax.ppermute(came[k - 1], 'ep', ahead)  5.64 us
    pallas_call x1, Pallas kernels, turn_weights(): pl.pallas_call(turn_kernel, out_shape=[in_vmem((width, hidden))] * 2, in_...  4.79 us
    pallas_call x1, Pallas kernels, halve_weights(): pl.pallas_call(halve_kernel, out_shape=[in_vmem((hidden, width // 2))] *...  3.13 us
    ppermute x1, starting transfers between devices, ring_body(): came[1] = lax.ppermute(packed, 'ep', ahead)  3.08 us
  transfers between devices with their start and end apart: 27, of which 7 were waited for; matrix products, arithmetic and copies ran while one was open for 6% of the time, Pallas kernels for 27%

profile of v13, /device:TPU:0, one launch (start us, length us, event | category | flops | bytes accessed | tf_op | source)
XLA Modules:
  0.0 72.5 jit_solution(13385607304084280589)
XLA Ops:
  0.0 1.0 %shard_map.64.refs_0_ = bf16[64,1464]{1,0:T(8,128)(2,1)S(1)} custom-call(bf16[64,1440]{1,0:T(8,128)(2,1)} %tokens_in.1, s32[4,64]{1,0:T(4,128)} %bitcast.14, f32[4,64]{1,0:T(4,128)} %bitcast.15), custom_call_target="tpu_custom_call" | custom-call | tf_op jit(solution)/shard_map/pallas_call | solution.py:53
  1.0 3.1 %collective-permute-start = (bf16[64,1464]{1,0:T(8,128)(2,1)S(1)}, bf16[64,1464]{1,0:T(8,128)(2,1)S(1)}, u32[]{:S(2)}, u32[]{:S(2)}) collective-permute-start(bf16[64,1464]{1,0:T(8,128)(2,1)S(1)} %shard_map.64.refs_0_), channel_id=1, source_target_pairs={{0,4},{4,8},{8,12},{12,14},{14,10},{10,6},{6,2},{2,0},{1,5},{5,9},... | collective-permute-start | bytes 562184 | tf_op jit(solution)/shard_map/ppermute | solution.py:316
  4.1 0.1 pad_add_fusion.after_this.place
  4.2 4.8 %shard_map.65 = (bf16[2880,720]{1,0:T(8,128)(2,1)S(1)}, bf16[2880,720]{1,0:T(8,128)(2,1)S(1)}) custom-call(s32[2]{0:T(128)S(1)} %pad_add_fusion.after_this.place, bf16[720,2880]{1,0:T(8,128)(2,1)} %bitcast.11, bf16[720,2880]{1,0:T(8,128)(2,1)} %bitcast.12), custom_call_target="tpu_custom_call" | custom-call | bytes 16588800 | tf_op jit(solution)/shard_map/pallas_call | solution.py:83
  9.0 2.1 %collective-permute-start.4 = (bf16[64,1464]{1,0:T(8,128)(2,1)S(1)}, bf16[64,1464]{1,0:T(8,128)(2,1)S(1)}, u32[]{:S(2)}, u32[]{:S(2)}) collective-permute-start(bf16[64,1464]{1,0:T(8,128)(2,1)S(1)} %collective-permute-done.refs_0_), channel_id=1, source_target_pairs={{0,4},{4,8},{8,12},{12,14},{14,10},{10,6},{6,2},{2,0},{1,5},{5,9},... | collective-permute-start | bytes 562184 | tf_op jit(solution)/shard_map/ppermute | solution.py:321
  11.1 0.0 collective-permute-done.1.refs_1_
  11.1 0.0 collective-permute-start.7
  11.1 0.0 collective-permute-start.2
  11.1 0.5 collective-permute-start.3
  11.6 3.1 %shard_map.66 = (bf16[720,1440]{1,0:T(8,128)(2,1)S(1)}, bf16[720,1440]{1,0:T(8,128)(2,1)S(1)}) custom-call(s32[2]{0:T(128)S(1)} %pad_add_fusion.after_this.place, bf16[720,2880]{1,0:T(8,128)(2,1)} %bitcast.13), custom_call_target="tpu_custom_call" | custom-call | bytes 16588800 | tf_op jit(solution)/shard_map/pallas_call | solution.py:120
  14.7 0.7 collective-permute-done.4.refs_0_
  15.4 1.7 %collective-permute-start.5 = (bf16[64,1464]{1,0:T(8,128)(2,1)S(1)}, bf16[64,1464]{1,0:T(8,128)(2,1)S(1)}, u32[]{:S(2)}, u32[]{:S(2)}) collective-permute-start(bf16[64,1464]{1,0:T(8,128)(2,1)S(1)} %collective-permute-done.4.refs_0_), channel_id=1, source_target_pairs={{0,4},{4,8},{8,12},{12,14},{14,10},{10,6},{6,2},{2,0},{1,5},{5,9},... | collective-permute-start | bytes 562184 | tf_op jit(solution)/shard_map/ppermute | solution.py:321
  17.1 0.0 collective-permute-start.8
  17.2 0.0 collective-permute-done.7.refs_1_
  17.2 0.3 collective-permute-start.10
  17.4 0.0 collective-permute-done.2.refs_2_
  17.4 0.3 collective-permute-start.9
  17.7 0.0 collective-permute-done.3.refs_3_
  17.7 3.2 %shard_map.67 = (bf16[128,1440]{1,0:T(8,128)(2,1)S(1)}, bf16[128,1440]{1,0:T(8,128)(2,1)}) custom-call(s32[2]{0:T(128)S(1)} %pad_add_fusion.after_this.place, bf16[64,1464]{1,0:T(8,128)(2,1)S(1)} %collective-permute-done.refs_0_, bf16[64,1464]{1,0:T(8,128)(2,1)S(1)} %collective-permute-done.1.refs_1_, bf16[64,1464]{1,0:T(8,128)(2,1)S(1)} %collective-permute-done.2.refs_2_, ...), custom_call_target="tpu_custom_call" | custom-call | flops 1592524800 | bytes 12441600 | tf_op jit(solution)/shard_map/pallas_call | solution.py:210
  20.9 0.7 %copy-done.6 = bf16[128,1440]{1,0:T(8,128)(2,1)} copy-done((bf16[128,1440]{1,0:T(8,128)(2,1)}, bf16[128,1440]{1,0:T(8,128)(2,1)S(1)}, u32[]{:S(2)}) %copy-start.6) | copy-done | bytes 368664
  21.6 0.2 collective-permute-done.5.refs_1_
  21.8 1.8 %collective-permute-start.6 = (bf16[64,1464]{1,0:T(8,128)(2,1)S(1)}, bf16[64,1464]{1,0:T(8,128)(2,1)S(1)}, u32[]{:S(2)}, u32[]{:S(2)}) collective-permute-start(bf16[64,1464]{1,0:T(8,128)(2,1)S(1)} %collective-permute-done.5.refs_1_), channel_id=1, source_target_pairs={{0,4},{4,8},{8,12},{12,14},{14,10},{10,6},{6,2},{2,0},{1,5},{5,9},... | collective-permute-start | bytes 562184 | tf_op jit(solution)/shard_map/ppermute | solution.py:321
  23.6 0.0 collective-permute-start.12
  23.6 0.8 %collective-permute-done.10.refs_2_ = bf16[64,1464]{1,0:T(8,128)(2,1)S(1)} collective-permute-done((bf16[64,1464]{1,0:T(8,128)(2,1)S(1)}, bf16[64,1464]{1,0:T(8,128)(2,1)S(1)}, u32[]{:S(2)}, u32[]{:S(2)}) %collective-permute-start.10) | collective-permute-done | bytes 187424 | tf_op jit(solution)/shard_map/ppermute | solution.py:323
  24.5 0.0 collective-permute-start.13
  24.5 0.0 collective-permute-done.8.refs_2_
  24.5 0.0 collective-permute-done.9.refs_3_
  24.5 2.7 %shard_map.68 = (bf16[128,1440]{1,0:T(8,128)(2,1)S(1)}, bf16[128,1440]{1,0:T(8,128)(2,1)S(1)}) custom-call(s32[2]{0:T(128)S(1)} %pad_add_fusion.after_this.place, bf16[64,1464]{1,0:T(8,128)(2,1)S(1)} %collective-permute-done.4.refs_0_, bf16[64,1464]{1,0:T(8,128)(2,1)S(1)} %collective-permute-done.7.refs_1_, ...), custom_call_target="tpu_custom_call" | custom-call | flops 1592524800 | bytes 12441600 | tf_op jit(solution)/shard_map/pallas_call | solution.py:210
  27.2 1.5 %collective-permute-done.6.refs_0_ = bf16[64,1464]{1,0:T(8,128)(2,1)S(1)} collective-permute-done((bf16[64,1464]{1,0:T(8,128)(2,1)S(1)}, bf16[64,1464]{1,0:T(8,128)(2,1)S(1)}, u32[]{:S(2)}, u32[]{:S(2)}) %collective-permute-start.6) | collective-permute-done | bytes 187424 | tf_op jit(solution)/shard_map/ppermute | solution.py:321
  28.7 0.0 collective-permute-start.11
  28.7 1.6 %shard_map.69 = (f32[192,720]{1,0:T(8,128)S(1)}, f32[192,720]{1,0:T(8,128)S(1)}) custom-call(s32[2]{0:T(128)S(1)} %pad_add_fusion.after_this.place, bf16[64,1464]{1,0:T(8,128)(2,1)S(1)} %collective-permute-done.6.refs_0_, bf16[64,1464]{1,0:T(8,128)(2,1)S(1)} %collective-permute-done.5.refs_1_, bf16[64,1464]{1,0:T(8,128)(2,1)S(1)} %collective-permute-done.10.refs_2_, ...), custom_call_target="tpu_custom_call" | custom-call | flops 796262400 | bytes 6220800 | tf_op jit(solution)/shard_map/pallas_call | solution.py:210
  30.3 0.0 collective-permute-done.13.refs_5_
  30.4 2.2 %shard_map.70 = (bf16[192,720]{1,0:T(8,128)(2,1)S(1)}, bf16[64,1440]{1,0:T(8,128)(2,1)S(1)}, bf16[128,1440]{1,0:T(8,128)(2,1)S(1)}) custom-call(s32[2]{0:T(128)S(1)} %pad_add_fusion.after_this.place, bf16[64,1464]{1,0:T(8,128)(2,1)S(1)} %collective-permute-done.6.refs_0_, bf16[64,1464]{1,0:T(8,128)(2,1)S(1)} %collective-permute-done.5.refs_1_, ...), custom_call_target="tpu_custom_call" | custom-call | flops 1194393600 | bytes 9331200 | tf_op jit(solution)/shard_map/pallas_call | solution.py:210
  32.6 0.6 collective-permute-start.14
  33.2 0.1 collective-permute-start.17
  33.2 1.2 %shard_map.71 = (bf16[64,1440]{1,0:T(8,128)(2,1)S(1)}, bf16[128,1440]{1,0:T(8,128)(2,1)S(1)}) custom-call(s32[2]{0:T(128)S(1)} %pad_add_fusion.after_this.place, bf16[64,1464]{1,0:T(8,128)(2,1)S(1)} %collective-permute-done.6.refs_0_, bf16[64,1464]{1,0:T(8,128)(2,1)S(1)} %collective-permute-done.5.refs_1_, ...), custom_call_target="tpu_custom_call" | custom-call | flops 398131200 | bytes 3110400 | tf_op jit(solution)/shard_map/pallas_call | solution.py:210
  34.5 2.0 %collective-permute-start.19 = (bf16[64,1440]{1,0:T(8,128)(2,1)S(1)}, bf16[64,1440]{1,0:T(8,128)(2,1)S(1)}, u32[]{:S(2)}, u32[]{:S(2)}) collective-permute-start(bf16[64,1440]{1,0:T(8,128)(2,1)S(1)} %fusion), channel_id=1, source_target_pairs={{0,4},{4,8},{8,12},{12,14},{14,10},{10,6},{6,2},{2,0},{1,5},{5,9},... | collective-permute-start | bytes 552968 | tf_op jit(solution)/shard_map/ppermute | solution.py:342
  36.5 0.2 collective-permute-start.16
  36.7 0.3 collective-permute-start.18
  37.0 5.0 %collective-permute-done.19 = bf16[64,1440]{1,0:T(8,128)(2,1)S(1)} collective-permute-done((bf16[64,1440]{1,0:T(8,128)(2,1)S(1)}, bf16[64,1440]{1,0:T(8,128)(2,1)S(1)}, u32[]{:S(2)}, u32[]{:S(2)}) %collective-permute-start.19) | collective-permute-done | bytes 184352 | tf_op jit(solution)/shard_map/ppermute | solution.py:342
  42.0 0.1 add_convert_fusion.3
  42.0 1.8 %collective-permute-start.21 = (bf16[64,1440]{1,0:T(8,128)(2,1)S(1)}, bf16[64,1440]{1,0:T(8,128)(2,1)}, u32[]{:S(2)}, u32[]{:S(2)}) collective-permute-start(bf16[64,1440]{1,0:T(8,128)(2,1)S(1)} %add_convert_fusion.3), channel_id=1, source_target_pairs={{0,4},{4,8},{8,12},{12,14},{14,10},{10,6},{6,2},{2,0},{1,5},{5,9},... | collective-permute-start | bytes 552968 | tf_op jit(solution)/shard_map/ppermute | solution.py:342
  43.9 0.1 collective-permute-start.15
  43.9 0.5 collective-permute-start.22
  44.4 0.8 %copy-done.9 = bf16[128,1440]{1,0:T(8,128)(2,1)} copy-done((bf16[128,1440]{1,0:T(8,128)(2,1)}, bf16[128,1440]{1,0:T(8,128)(2,1)S(1)}, u32[]{:S(2)}) %copy-start.9) | copy-done | bytes 368664
  45.2 0.1 shard_map.72
  45.3 0.3 collective-permute-start.20
  45.6 3.0 %collective-permute-done.21 = bf16[64,1440]{1,0:T(8,128)(2,1)} collective-permute-done((bf16[64,1440]{1,0:T(8,128)(2,1)S(1)}, bf16[64,1440]{1,0:T(8,128)(2,1)}, u32[]{:S(2)}, u32[]{:S(2)}) %collective-permute-start.21) | collective-permute-done | bytes 184352 | tf_op jit(solution)/shard_map/ppermute | solution.py:342
  48.7 1.2 %add_convert_fusion.2 = bf16[64,1440]{1,0:T(8,128)(2,1)S(1)} fusion(bf16[64,1440]{1,0:T(8,128)(2,1)} %collective-permute-done.21, bf16[128,1440]{1,0:T(8,128)(2,1)} %copy-done.9, bf16[128,1440]{1,0:T(8,128)(2,1)} %copy-done.8), kind=kLoop, calls=%fused_computation.2 | loop fusion | flops 552960 | bytes 737280 | tf_op jit(solution)/shard_map/convert_element_type | solution.py:354
  49.9 1.8 %collective-permute-start.25 = (bf16[64,1440]{1,0:T(8,128)(2,1)S(1)}, bf16[64,1440]{1,0:T(8,128)(2,1)}, u32[]{:S(2)}, u32[]{:S(2)}) collective-permute-start(bf16[64,1440]{1,0:T(8,128)(2,1)S(1)} %add_convert_fusion.2), channel_id=1, source_target_pairs={{0,4},{4,8},{8,12},{12,14},{14,10},{10,6},{6,2},{2,0},{1,5},{5,9},... | collective-permute-start | bytes 552968 | tf_op jit(solution)/shard_map/ppermute | solution.py:342
  51.7 0.9 %slice.36.refs_0_ = bf16[64,1440]{1,0:T(8,128)(2,1)S(1)} slice(bf16[128,1440]{1,0:T(8,128)(2,1)} %copy-done.6), slice={[0:64], [0:1440]} | slice | bytes 368640 | tf_op jit(solution)/shard_map/slice | solution.py:313
  52.6 0.9 %slice.48.refs_1_ = bf16[64,1440]{1,0:T(8,128)(2,1)S(1)} slice(bf16[128,1440]{1,0:T(8,128)(2,1)} %collective-permute-done.15), slice={[0:64], [0:1440]} | slice | bytes 368640 | tf_op jit(solution)/shard_map/slice | solution.py:313
  53.6 0.1 shard_map.73
  53.6 0.3 collective-permute-start.24
  54.0 2.3 %copy-done.1 = bf16[2880,720]{1,0:T(8,128)(2,1)S(1)} copy-done((bf16[2880,720]{1,0:T(8,128)(2,1)S(1)}, bf16[2880,720]{1,0:T(8,128)(2,1)}, u32[]{:S(2)}) %copy-start.1) | copy-done | bytes 4147224
  56.2 2.3 %copy-done.3 = bf16[2880,720]{1,0:T(8,128)(2,1)S(1)} copy-done((bf16[2880,720]{1,0:T(8,128)(2,1)S(1)}, bf16[2880,720]{1,0:T(8,128)(2,1)}, u32[]{:S(2)}) %copy-start.3) | copy-done | bytes 4147224
  58.5 1.6 %copy-done.5 = bf16[720,1440]{1,0:T(8,128)(2,1)S(1)} copy-done((bf16[720,1440]{1,0:T(8,128)(2,1)S(1)}, bf16[720,1440]{1,0:T(8,128)(2,1)}, u32[]{:S(2)}) %copy-start.5) | copy-done | bytes 2073624
  60.1 3.1 %shard_map.74 = (bf16[64,1440]{1,0:T(8,128)(2,1)S(1)}, bf16[64,1440]{1,0:T(8,128)(2,1)S(1)}) custom-call(s32[2]{0:T(128)S(1)} %pad_add_fusion.after_this.place, bf16[64,1464]{1,0:T(8,128)(2,1)S(1)} %shard_map.64.refs_0_, bf16[64,1464]{1,0:T(8,128)(2,1)} %collective-permute-done.22.refs_1_, bf16[2880,720]{1,0:T(8,128)(2,1)S(1)} %copy-done.1, ...), custom_call_target="tpu_custom_call" | custom-call | flops 1592524800 | bytes 12441600 | tf_op jit(solution)/shard_map/pallas_call | solution.py:210
  63.2 0.1 collective-permute-start.23
  63.3 1.1 %add_convert_fusion.1 = bf16[64,1440]{1,0:T(8,128)(2,1)S(1)} fusion(bf16[64,1440]{1,0:T(8,128)(2,1)} %collective-permute-done.25, bf16[128,1440]{1,0:T(8,128)(2,1)} %collective-permute-done.15, bf16[128,1440]{1,0:T(8,128)(2,1)S(1)} %copy-done.7), kind=kLoop, calls=%fused_computation.1 | loop fusion | flops 552960 | bytes 737280 | tf_op jit(solution)/shard_map/convert_element_type | solution.py:354
  64.4 1.8 %collective-permute-start.26 = (bf16[64,1440]{1,0:T(8,128)(2,1)S(1)}, bf16[64,1440]{1,0:T(8,128)(2,1)S(1)}, u32[]{:S(2)}, u32[]{:S(2)}) collective-permute-start(bf16[64,1440]{1,0:T(8,128)(2,1)S(1)} %add_convert_fusion.1), channel_id=1, source_target_pairs={{0,4},{4,8},{8,12},{12,14},{14,10},{10,6},{6,2},{2,0},{1,5},{5,9},... | collective-permute-start | bytes 552968 | tf_op jit(solution)/shard_map/ppermute | solution.py:342
  66.2 0.1 shard_map.75
  66.3 5.5 %collective-permute-done.26 = bf16[64,1440]{1,0:T(8,128)(2,1)S(1)} collective-permute-done((bf16[64,1440]{1,0:T(8,128)(2,1)S(1)}, bf16[64,1440]{1,0:T(8,128)(2,1)S(1)}, u32[]{:S(2)}, u32[]{:S(2)}) %collective-permute-start.26) | collective-permute-done | bytes 184352 | tf_op jit(solution)/shard_map/ppermute | solution.py:342
  71.8 0.7 %add_convert_fusion = bf16[64,1440]{1,0:T(8,128)(2,1)} fusion(bf16[64,1440]{1,0:T(8,128)(2,1)S(1)} %collective-permute-done.26, bf16[64,1440]{1,0:T(8,128)(2,1)S(1)} %shard_map.75), kind=kLoop, calls=%fused_computation | loop fusion | flops 368640 | bytes 552960 | tf_op jit(solution)/shard_map/convert_element_type | solution.py:355
  (33 shorter events, 0.2 us)
Async XLA Ops:
  1.0 8.0 %collective-permute-start = (bf16[64,1464]{1,0:T(8,128)(2,1)S(1)}, bf16[64,1464]{1,0:T(8,128)(2,1)S(1)}, u32[]{:S(2)}, u32[]{:S(2)}) collective-permute-start(bf16[64,1464]{1,0:T(8,128)(2,1)S(1)} %shard_map.64.refs_0_), channel_id=1, source_target_pairs={{0,4},{4,8},{8,12},{12,14},{14,10},{10,6},{6,2},{2,0},{1,5},{5,9},... | collective-permute-start | bytes 562184 | tf_op jit(solution)/shard_map/ppermute | solution.py:316
  4.1 7.0 %collective-permute-start.1 = (bf16[64,1464]{1,0:T(8,128)(2,1)S(1)}, bf16[64,1464]{1,0:T(8,128)(2,1)S(1)}, u32[]{:S(2)}, u32[]{:S(2)}) collective-permute-start(bf16[64,1464]{1,0:T(8,128)(2,1)S(1)} %shard_map.64.refs_0_), channel_id=1, source_target_pairs={{4,0},{8,4},{12,8},{14,12},{10,14},{6,10},{2,6},{0,2},{5,1},{9,5},... | collective-permute-start | bytes 562184 | tf_op jit(solution)/shard_map/ppermute | solution.py:317
  9.0 21.4 %copy-start = (bf16[2880,720]{1,0:T(8,128)(2,1)}, bf16[2880,720]{1,0:T(8,128)(2,1)S(1)}, u32[]{:S(2)}) copy-start(bf16[2880,720]{1,0:T(8,128)(2,1)S(1)} %get-tuple-element.51.refs_4_.refs_3_.refs_8_.refs_2_) | copy-start | bytes 12441604
  9.0 21.4 %copy-start.2 = (bf16[2880,720]{1,0:T(8,128)(2,1)}, bf16[2880,720]{1,0:T(8,128)(2,1)S(1)}, u32[]{:S(2)}) copy-start(bf16[2880,720]{1,0:T(8,128)(2,1)S(1)} %get-tuple-element.48.refs_5_.refs_4_.refs_9_.refs_3_) | copy-start | bytes 12441604
  9.0 6.4 %collective-permute-start.4 = (bf16[64,1464]{1,0:T(8,128)(2,1)S(1)}, bf16[64,1464]{1,0:T(8,128)(2,1)S(1)}, u32[]{:S(2)}, u32[]{:S(2)}) collective-permute-start(bf16[64,1464]{1,0:T(8,128)(2,1)S(1)} %collective-permute-done.refs_0_), channel_id=1, source_target_pairs={{0,4},{4,8},{8,12},{12,14},{14,10},{10,6},{6,2},{2,0},{1,5},{5,9},... | collective-permute-start | bytes 562184 | tf_op jit(solution)/shard_map/ppermute | solution.py:321
  11.1 6.1 %collective-permute-start.7 = (bf16[64,1464]{1,0:T(8,128)(2,1)S(1)}, bf16[64,1464]{1,0:T(8,128)(2,1)S(1)}, u32[]{:S(2)}, u32[]{:S(2)}) collective-permute-start(bf16[64,1464]{1,0:T(8,128)(2,1)S(1)} %collective-permute-done.1.refs_1_), channel_id=1, source_target_pairs={{4,0},{8,4},{12,8},{14,12},{10,14},{6,10},{2,6},{0,2},{5,1},{9,5},... | collective-permute-start | bytes 562184 | tf_op jit(solution)/shard_map/ppermute | solution.py:323
  11.1 6.4 %collective-permute-start.2 = (bf16[64,1464]{1,0:T(8,128)(2,1)S(1)}, bf16[64,1464]{1,0:T(8,128)(2,1)S(1)}, u32[]{:S(2)}, u32[]{:S(2)}) collective-permute-start(bf16[64,1464]{1,0:T(8,128)(2,1)S(1)} %collective-permute-done.refs_0_), channel_id=1, source_target_pairs={{0,1},{1,0},{2,3},{3,2},{4,5},{5,4},{6,7},{7,6},{8,9},{9,8},{10,11... | collective-permute-start | bytes 562184 | tf_op jit(solution)/shard_map/ppermute | solution.py:324
  11.1 6.7 %collective-permute-start.3 = (bf16[64,1464]{1,0:T(8,128)(2,1)S(1)}, bf16[64,1464]{1,0:T(8,128)(2,1)S(1)}, u32[]{:S(2)}, u32[]{:S(2)}) collective-permute-start(bf16[64,1464]{1,0:T(8,128)(2,1)S(1)} %collective-permute-done.1.refs_1_), channel_id=1, source_target_pairs={{0,1},{1,0},{2,3},{3,2},{4,5},{5,4},{6,7},{7,6},{8,9},{9,8},{10,11... | collective-permute-start | bytes 562184 | tf_op jit(solution)/shard_map/ppermute | solution.py:324
  14.7 15.6 %copy-start.4 = (bf16[720,1440]{1,0:T(8,128)(2,1)}, bf16[720,1440]{1,0:T(8,128)(2,1)S(1)}, u32[]{:S(2)}) copy-start(bf16[720,1440]{1,0:T(8,128)(2,1)S(1)} %get-tuple-element.54.refs_7_.refs_10_.refs_5_) | copy-start | bytes 6220804
  15.4 6.4 %collective-permute-start.5 = (bf16[64,1464]{1,0:T(8,128)(2,1)S(1)}, bf16[64,1464]{1,0:T(8,128)(2,1)S(1)}, u32[]{:S(2)}, u32[]{:S(2)}) collective-permute-start(bf16[64,1464]{1,0:T(8,128)(2,1)S(1)} %collective-permute-done.4.refs_0_), channel_id=1, source_target_pairs={{0,4},{4,8},{8,12},{12,14},{14,10},{10,6},{6,2},{2,0},{1,5},{5,9},... | collective-permute-start | bytes 562184 | tf_op jit(solution)/shard_map/ppermute | solution.py:321
  17.1 7.3 %collective-permute-start.8 = (bf16[64,1464]{1,0:T(8,128)(2,1)S(1)}, bf16[64,1464]{1,0:T(8,128)(2,1)S(1)}, u32[]{:S(2)}, u32[]{:S(2)}) collective-permute-start(bf16[64,1464]{1,0:T(8,128)(2,1)S(1)} %collective-permute-done.4.refs_0_), channel_id=1, source_target_pairs={{0,1},{1,0},{2,3},{3,2},{4,5},{5,4},{6,7},{7,6},{8,9},{9,8},{10,11... | collective-permute-start | bytes 562184 | tf_op jit(solution)/shard_map/ppermute | solution.py:324
  17.2 7.3 %collective-permute-start.10 = (bf16[64,1464]{1,0:T(8,128)(2,1)S(1)}, bf16[64,1464]{1,0:T(8,128)(2,1)S(1)}, u32[]{:S(2)}, u32[]{:S(2)}) collective-permute-start(bf16[64,1464]{1,0:T(8,128)(2,1)S(1)} %collective-permute-done.7.refs_1_), channel_id=1, source_target_pairs={{4,0},{8,4},{12,8},{14,12},{10,14},{6,10},{2,6},{0,2},{5,1},{9,5},... | collective-permute-start | bytes 562184 | tf_op jit(solution)/shard_map/ppermute | solution.py:323
  17.4 7.0 %collective-permute-start.9 = (bf16[64,1464]{1,0:T(8,128)(2,1)S(1)}, bf16[64,1464]{1,0:T(8,128)(2,1)S(1)}, u32[]{:S(2)}, u32[]{:S(2)}) collective-permute-start(bf16[64,1464]{1,0:T(8,128)(2,1)S(1)} %collective-permute-done.7.refs_1_), channel_id=1, source_target_pairs={{0,1},{1,0},{2,3},{3,2},{4,5},{5,4},{6,7},{7,6},{8,9},{9,8},{10,11... | collective-permute-start | bytes 562184 | tf_op jit(solution)/shard_map/ppermute | solution.py:324
  20.9 0.7 %copy-start.6 = (bf16[128,1440]{1,0:T(8,128)(2,1)}, bf16[128,1440]{1,0:T(8,128)(2,1)S(1)}, u32[]{:S(2)}) copy-start(bf16[128,1440]{1,0:T(8,128)(2,1)S(1)} %get-tuple-element.85) | copy-start | bytes 1105924
  21.8 6.9 %collective-permute-start.6 = (bf16[64,1464]{1,0:T(8,128)(2,1)S(1)}, bf16[64,1464]{1,0:T(8,128)(2,1)S(1)}, u32[]{:S(2)}, u32[]{:S(2)}) collective-permute-start(bf16[64,1464]{1,0:T(8,128)(2,1)S(1)} %collective-permute-done.5.refs_1_), channel_id=1, source_target_pairs={{0,4},{4,8},{8,12},{12,14},{14,10},{10,6},{6,2},{2,0},{1,5},{5,9},... | collective-permute-start | bytes 562184 | tf_op jit(solution)/shard_map/ppermute | solution.py:321
  23.6 6.7 %collective-permute-start.12 = (bf16[64,1464]{1,0:T(8,128)(2,1)S(1)}, bf16[64,1464]{1,0:T(8,128)(2,1)S(1)}, u32[]{:S(2)}, u32[]{:S(2)}) collective-permute-start(bf16[64,1464]{1,0:T(8,128)(2,1)S(1)} %collective-permute-done.5.refs_1_), channel_id=1, source_target_pairs={{0,1},{1,0},{2,3},{3,2},{4,5},{5,4},{6,7},{7,6},{8,9},{9,8},{10,11... | collective-permute-start | bytes 562184 | tf_op jit(solution)/shard_map/ppermute | solution.py:324
  24.5 5.8 %collective-permute-start.13 = (bf16[64,1464]{1,0:T(8,128)(2,1)S(1)}, bf16[64,1464]{1,0:T(8,128)(2,1)S(1)}, u32[]{:S(2)}, u32[]{:S(2)}) collective-permute-start(bf16[64,1464]{1,0:T(8,128)(2,1)S(1)} %collective-permute-done.10.refs_2_), channel_id=1, source_target_pairs={{0,1},{1,0},{2,3},{3,2},{4,5},{5,4},{6,7},{7,6},{8,9},{9,8},{10,11... | collective-permute-start | bytes 562184 | tf_op jit(solution)/shard_map/ppermute | solution.py:324
  27.2 16.7 %copy-start.8 = (bf16[128,1440]{1,0:T(8,128)(2,1)}, bf16[128,1440]{1,0:T(8,128)(2,1)S(1)}, u32[]{:S(2)}) copy-start(bf16[128,1440]{1,0:T(8,128)(2,1)S(1)} %get-tuple-element.77) | copy-start | bytes 1105924
  28.7 1.7 %collective-permute-start.11 = (bf16[64,1464]{1,0:T(8,128)(2,1)S(1)}, bf16[64,1464]{1,0:T(8,128)(2,1)S(1)}, u32[]{:S(2)}, u32[]{:S(2)}) collective-permute-start(bf16[64,1464]{1,0:T(8,128)(2,1)S(1)} %collective-permute-done.6.refs_0_), channel_id=1, source_target_pairs={{0,1},{1,0},{2,3},{3,2},{4,5},{5,4},{6,7},{7,6},{8,9},{9,8},{10,11... | collective-permute-start | bytes 562184 | tf_op jit(solution)/shard_map/ppermute | solution.py:332
  32.6 1.8 %collective-permute-start.14 = (bf16[64,1440]{1,0:T(8,128)(2,1)S(1)}, bf16[64,1440]{1,0:T(8,128)(2,1)S(1)}, u32[]{:S(2)}, u32[]{:S(2)}) collective-permute-start(bf16[64,1440]{1,0:T(8,128)(2,1)S(1)} %get-tuple-element.67), channel_id=1, source_target_pairs={{0,1},{1,0},{2,3},{3,2},{4,5},{5,4},{6,7},{7,6},{8,9},{9,8},{10,11... | collective-permute-start | bytes 552968 | tf_op jit(solution)/shard_map/ppermute | solution.py:259
  33.2 3.5 %collective-permute-start.17 = (bf16[128,1440]{1,0:T(8,128)(2,1)S(1)}, bf16[128,1440]{1,0:T(8,128)(2,1)S(1)}, u32[]{:S(2)}, u32[]{:S(2)}) collective-permute-start(bf16[128,1440]{1,0:T(8,128)(2,1)S(1)} %get-tuple-element.72), channel_id=1, source_target_pairs={{0,1},{1,0},{2,3},{3,2},{4,5},{5,4},{6,7},{7,6},{8,9},{9,8},{10,11... | collective-permute-start | bytes 1105928 | tf_op jit(solution)/shard_map/ppermute | solution.py:259
  34.5 7.5 %collective-permute-start.19 = (bf16[64,1440]{1,0:T(8,128)(2,1)S(1)}, bf16[64,1440]{1,0:T(8,128)(2,1)S(1)}, u32[]{:S(2)}, u32[]{:S(2)}) collective-permute-start(bf16[64,1440]{1,0:T(8,128)(2,1)S(1)} %fusion), channel_id=1, source_target_pairs={{0,4},{4,8},{8,12},{12,14},{14,10},{10,6},{6,2},{2,0},{1,5},{5,9},... | collective-permute-start | bytes 552968 | tf_op jit(solution)/shard_map/ppermute | solution.py:342
  36.5 8.0 %collective-permute-start.16 = (bf16[128,1440]{1,0:T(8,128)(2,1)S(1)}, bf16[128,1440]{1,0:T(8,128)(2,1)S(1)}, u32[]{:S(2)}, u32[]{:S(2)}) collective-permute-start(bf16[128,1440]{1,0:T(8,128)(2,1)S(1)} %get-tuple-element.70), channel_id=1, source_target_pairs={{0,1},{1,0},{2,3},{3,2},{4,5},{5,4},{6,7},{7,6},{8,9},{9,8},{10,11... | collective-permute-start | bytes 1105928 | tf_op jit(solution)/shard_map/ppermute | solution.py:337
  36.7 7.8 %collective-permute-start.18 = (bf16[64,1440]{1,0:T(8,128)(2,1)S(1)}, bf16[64,1440]{1,0:T(8,128)(2,1)S(1)}, u32[]{:S(2)}, u32[]{:S(2)}) collective-permute-start(bf16[64,1440]{1,0:T(8,128)(2,1)S(1)} %add_convert_fusion.4), channel_id=1, source_target_pairs={{4,0},{8,4},{12,8},{14,12},{10,14},{6,10},{2,6},{0,2},{5,1},{9,5},... | collective-permute-start | bytes 552968 | tf_op jit(solution)/shard_map/ppermute | solution.py:347
  42.0 6.6 %collective-permute-start.21 = (bf16[64,1440]{1,0:T(8,128)(2,1)S(1)}, bf16[64,1440]{1,0:T(8,128)(2,1)}, u32[]{:S(2)}, u32[]{:S(2)}) collective-permute-start(bf16[64,1440]{1,0:T(8,128)(2,1)S(1)} %add_convert_fusion.3), channel_id=1, source_target_pairs={{0,4},{4,8},{8,12},{12,14},{14,10},{10,6},{6,2},{2,0},{1,5},{5,9},... | collective-permute-start | bytes 552968 | tf_op jit(solution)/shard_map/ppermute | solution.py:342
  43.9 8.7 %collective-permute-start.15 = (bf16[128,1440]{1,0:T(8,128)(2,1)}, bf16[128,1440]{1,0:T(8,128)(2,1)}, u32[]{:S(2)}, u32[]{:S(2)}) collective-permute-start(bf16[128,1440]{1,0:T(8,128)(2,1)} %get-tuple-element.68), channel_id=1, source_target_pairs={{0,1},{1,0},{2,3},{3,2},{4,5},{5,4},{6,7},{7,6},{8,9},{9,8},{10,11... | collective-permute-start | bytes 1105928 | tf_op jit(solution)/shard_map/ppermute | solution.py:337
  43.9 10.0 %collective-permute-start.22 = (bf16[64,1464]{1,0:T(8,128)(2,1)S(1)}, bf16[64,1464]{1,0:T(8,128)(2,1)}, u32[]{:S(2)}, u32[]{:S(2)}) collective-permute-start(bf16[64,1464]{1,0:T(8,128)(2,1)S(1)} %shard_map.64.refs_0_), channel_id=1, source_target_pairs={{0,1},{1,0},{2,3},{3,2},{4,5},{5,4},{6,7},{7,6},{8,9},{9,8},{10,11... | collective-permute-start | bytes 562184 | tf_op jit(solution)/shard_map/ppermute | solution.py:349
  44.4 0.8 %copy-start.9 = (bf16[128,1440]{1,0:T(8,128)(2,1)}, bf16[128,1440]{1,0:T(8,128)(2,1)S(1)}, u32[]{:S(2)}) copy-start(bf16[128,1440]{1,0:T(8,128)(2,1)S(1)} %collective-permute-done.16) | copy-start | bytes 1105924
  45.3 8.2 %collective-permute-start.20 = (bf16[64,1440]{1,0:T(8,128)(2,1)S(1)}, bf16[64,1440]{1,0:T(8,128)(2,1)S(1)}, u32[]{:S(2)}, u32[]{:S(2)}) collective-permute-start(bf16[64,1440]{1,0:T(8,128)(2,1)S(1)} %shard_map.72), channel_id=1, source_target_pairs={{4,0},{8,4},{12,8},{14,12},{10,14},{6,10},{2,6},{0,2},{5,1},{9,5},... | collective-permute-start | bytes 552968 | tf_op jit(solution)/shard_map/ppermute | solution.py:347
  49.9 13.4 %collective-permute-start.25 = (bf16[64,1440]{1,0:T(8,128)(2,1)S(1)}, bf16[64,1440]{1,0:T(8,128)(2,1)}, u32[]{:S(2)}, u32[]{:S(2)}) collective-permute-start(bf16[64,1440]{1,0:T(8,128)(2,1)S(1)} %add_convert_fusion.2), channel_id=1, source_target_pairs={{0,4},{4,8},{8,12},{12,14},{14,10},{10,6},{6,2},{2,0},{1,5},{5,9},... | collective-permute-start | bytes 552968 | tf_op jit(solution)/shard_map/ppermute | solution.py:342
  53.6 12.6 %collective-permute-start.24 = (bf16[64,1440]{1,0:T(8,128)(2,1)S(1)}, bf16[64,1440]{1,0:T(8,128)(2,1)S(1)}, u32[]{:S(2)}, u32[]{:S(2)}) collective-permute-start(bf16[64,1440]{1,0:T(8,128)(2,1)S(1)} %shard_map.73), channel_id=1, source_target_pairs={{4,0},{8,4},{12,8},{14,12},{10,14},{6,10},{2,6},{0,2},{5,1},{9,5},... | collective-permute-start | bytes 552968 | tf_op jit(solution)/shard_map/ppermute | solution.py:347
  54.0 2.3 %copy-start.1 = (bf16[2880,720]{1,0:T(8,128)(2,1)S(1)}, bf16[2880,720]{1,0:T(8,128)(2,1)}, u32[]{:S(2)}) copy-start(bf16[2880,720]{1,0:T(8,128)(2,1)} %copy-done) | copy-start | bytes 12441604
  56.2 2.3 %copy-start.3 = (bf16[2880,720]{1,0:T(8,128)(2,1)S(1)}, bf16[2880,720]{1,0:T(8,128)(2,1)}, u32[]{:S(2)}) copy-start(bf16[2880,720]{1,0:T(8,128)(2,1)} %copy-done.2) | copy-start | bytes 12441604
  58.5 1.6 %copy-start.5 = (bf16[720,1440]{1,0:T(8,128)(2,1)S(1)}, bf16[720,1440]{1,0:T(8,128)(2,1)}, u32[]{:S(2)}) copy-start(bf16[720,1440]{1,0:T(8,128)(2,1)} %copy-done.4) | copy-start | bytes 6220804
  60.1 3.2 %copy-start.7 = (bf16[128,1440]{1,0:T(8,128)(2,1)S(1)}, bf16[128,1440]{1,0:T(8,128)(2,1)}, u32[]{:S(2)}) copy-start(bf16[128,1440]{1,0:T(8,128)(2,1)} %copy-done.6) | copy-start | bytes 1105924
  63.2 3.0 %collective-permute-start.23 = (bf16[64,1440]{1,0:T(8,128)(2,1)S(1)}, bf16[64,1440]{1,0:T(8,128)(2,1)S(1)}, u32[]{:S(2)}, u32[]{:S(2)}) collective-permute-start(bf16[64,1440]{1,0:T(8,128)(2,1)S(1)} %get-tuple-element.84), channel_id=1, source_target_pairs={{0,1},{1,0},{2,3},{3,2},{4,5},{5,4},{6,7},{7,6},{8,9},{9,8},{10,11... | collective-permute-start | bytes 552968 | tf_op jit(solution)/shard_map/ppermute | solution.py:352
  64.4 7.3 %collective-permute-start.26 = (bf16[64,1440]{1,0:T(8,128)(2,1)S(1)}, bf16[64,1440]{1,0:T(8,128)(2,1)S(1)}, u32[]{:S(2)}, u32[]{:S(2)}) collective-permute-start(bf16[64,1440]{1,0:T(8,128)(2,1)S(1)} %add_convert_fusion.1), channel_id=1, source_target_pairs={{0,4},{4,8},{8,12},{12,14},{14,10},{10,6},{6,2},{2,0},{1,5},{5,9},... | collective-permute-start | bytes 552968 | tf_op jit(solution)/shard_map/ppermute | solution.py:342

commit v14 on v11

--- a/solution.py
+++ b/solution.py
@@ -315,7 +315,6 @@
 
     came[1] = lax.ppermute(packed, "ep", ahead)
     came[-1] = lax.ppermute(packed, "ep", back)
-    across[0] = swap(packed)
     weights, done, near = [gate, up], up, []
     for k in range(2, far + 1):
         came[k - 1], came[1 - k] = after(came[k - 1], done), after(came[1 - k], done)
@@ -327,10 +326,11 @@
             weights += halve_weights(after(place, came[1]), w_down[0])
             done = weights[-1]
         else:
-            near += run([k - 2, 2 - k], across[0] if k == 3 else None)
+            near += run([k - 2, 2 - k])
             done = near[-1][-1]
     came[far] = after(came[far], done)
     across[far] = swap(came[far])
+    across[0] = swap(after(packed, came[far]))
     last = [far, far - 1, 1 - far]
     for keys, mine, theirs in zip(([far], last[1:]), *run_expert_in_stages(place, [came[k] for k in last], [across[k] for k in last], swap, weights, n)):
         keep(keys, mine, theirs)

time: 61.1 us -> 59.8 us (0.979)
  waiting for transfers between devices: 18.5 us -> 17.3 us
    ppermute x3, waiting for transfers between devices: 7.78 us -> 9.99 us  [ring_body(): front = lax.ppermute(to_back, 'ep', back)]
    ppermute x4, waiting for transfers between devices: 5.92 us -> 4.03 us  [ring_body(): behind = lax.ppermute(to_ahead, 'ep', ahead)]
    ppermute x2, waiting for transfers between devices: 2.3 us -> 0.85 us  [ring_body(): came[-k] = lax.ppermute(came[1 - k], 'ep', back)]
    ppermute x4, starting transfers between devices: 7.34 us -> 6.71 us  [ring_body(): behind = lax.ppermute(to_ahead, 'ep', ahead)]
  transfers between devices with their start and end apart: 27 -> 27, of which waited for: 12 -> 11; matrix products, arithmetic and copies ran while one was open for 1% -> 1% of each run, Pallas kernels for 31% -> 32%
where the time goes in v14:
time: 59.8 us; the launch traced here: 59.7 us
  Pallas kernels  22.2 us (37%)
  starting transfers between devices  18.8 us (31%)
  waiting for transfers between devices  17.3 us (29%)
  other arithmetic  1.12 us (2%)
    pallas_call x6, Pallas kernels, call(): pl.pallas_call(kernel, out_shape=out_shape, in_specs=[pl.BlockSpec(memory...  13.1 us
    ppermute x3, waiting for transfers between devices, ring_body(): front = lax.ppermute(to_back, 'ep', back)  9.99 us
    ppermute x4, starting transfers between devices, ring_body(): behind = lax.ppermute(to_ahead, 'ep', ahead)  6.71 us
    ppermute x3, starting transfers between devices, ring_body(): came[k] = lax.ppermute(came[k - 1], 'ep', ahead)  5.64 us
    pallas_call x1, Pallas kernels, turn_weights(): pl.pallas_call(turn_kernel, out_shape=[in_vmem((width, hidden))] * 2, in_...  4.79 us
    ppermute x4, waiting for transfers between devices, ring_body(): behind = lax.ppermute(to_ahead, 'ep', ahead)  4.03 us
    pallas_call x1, Pallas kernels, halve_weights(): pl.pallas_call(halve_kernel, out_shape=[in_vmem((hidden, width // 2))] *...  3.13 us
    ppermute x1, starting transfers between devices, ring_body(): came[1] = lax.ppermute(packed, 'ep', ahead)  3.08 us
  transfers between devices with their start and end apart: 27, of which 11 were waited for; matrix products, arithmetic and copies ran while one was open for 1% of the time, Pallas kernels for 32%

profile of v14, /device:TPU:0, one launch (start us, length us, event | category | flops | bytes accessed | tf_op | source)
XLA Modules:
  0.0 59.7 jit_solution(12259582853489772992)
XLA Ops:
  0.0 1.0 %shard_map.64.refs_0_ = bf16[64,1464]{1,0:T(8,128)(2,1)S(1)} custom-call(bf16[64,1440]{1,0:T(8,128)(2,1)} %tokens_in.1, s32[4,64]{1,0:T(4,128)} %bitcast.14, f32[4,64]{1,0:T(4,128)} %bitcast.15), custom_call_target="tpu_custom_call" | custom-call | tf_op jit(solution)/shard_map/pallas_call | solution.py:53
  1.0 3.1 %collective-permute-start = (bf16[64,1464]{1,0:T(8,128)(2,1)S(1)}, bf16[64,1464]{1,0:T(8,128)(2,1)S(1)}, u32[]{:S(2)}, u32[]{:S(2)}) collective-permute-start(bf16[64,1464]{1,0:T(8,128)(2,1)S(1)} %shard_map.64.refs_0_), channel_id=1, source_target_pairs={{0,4},{4,8},{8,12},{12,14},{14,10},{10,6},{6,2},{2,0},{1,5},{5,9},... | collective-permute-start | bytes 562184 | tf_op jit(solution)/shard_map/ppermute | solution.py:316
  4.1 0.0 collective-permute-start.3
  4.1 0.1 pad_add_fusion.after_this.place
  4.2 4.8 %shard_map.65 = (bf16[2880,720]{1,0:T(8,128)(2,1)S(1)}, bf16[2880,720]{1,0:T(8,128)(2,1)S(1)}) custom-call(s32[2]{0:T(128)S(1)} %pad_add_fusion.after_this.place, bf16[720,2880]{1,0:T(8,128)(2,1)} %bitcast.11, bf16[720,2880]{1,0:T(8,128)(2,1)} %bitcast.12), custom_call_target="tpu_custom_call" | custom-call | bytes 16588800 | tf_op jit(solution)/shard_map/pallas_call | solution.py:83
  9.0 0.0 collective-permute-done.refs_0_
  9.0 2.1 %collective-permute-start.1 = (bf16[64,1464]{1,0:T(8,128)(2,1)S(1)}, bf16[64,1464]{1,0:T(8,128)(2,1)S(1)}, u32[]{:S(2)}, u32[]{:S(2)}) collective-permute-start(bf16[64,1464]{1,0:T(8,128)(2,1)S(1)} %collective-permute-done.refs_0_), channel_id=1, source_target_pairs={{0,4},{4,8},{8,12},{12,14},{14,10},{10,6},{6,2},{2,0},{1,5},{5,9},... | collective-permute-start | bytes 562184 | tf_op jit(solution)/shard_map/ppermute | solution.py:321
  11.0 0.0 collective-permute-done.3.refs_1_
  11.1 0.0 collective-permute-start.7
  11.1 0.0 collective-permute-start.4
  11.1 0.5 collective-permute-start.5
  11.6 3.1 %shard_map.66 = (bf16[720,1440]{1,0:T(8,128)(2,1)S(1)}, bf16[720,1440]{1,0:T(8,128)(2,1)S(1)}) custom-call(s32[2]{0:T(128)S(1)} %pad_add_fusion.after_this.place, bf16[720,2880]{1,0:T(8,128)(2,1)} %bitcast.13), custom_call_target="tpu_custom_call" | custom-call | bytes 16588800 | tf_op jit(solution)/shard_map/pallas_call | solution.py:120
  14.7 0.7 %collective-permute-done.1.refs_0_ = bf16[64,1464]{1,0:T(8,128)(2,1)S(1)} collective-permute-done((bf16[64,1464]{1,0:T(8,128)(2,1)S(1)}, bf16[64,1464]{1,0:T(8,128)(2,1)S(1)}, u32[]{:S(2)}, u32[]{:S(2)}) %collective-permute-start.1) | collective-permute-done | bytes 187424 | tf_op jit(solution)/shard_map/ppermute | solution.py:321
  15.4 1.7 %collective-permute-start.2 = (bf16[64,1464]{1,0:T(8,128)(2,1)S(1)}, bf16[64,1464]{1,0:T(8,128)(2,1)S(1)}, u32[]{:S(2)}, u32[]{:S(2)}) collective-permute-start(bf16[64,1464]{1,0:T(8,128)(2,1)S(1)} %collective-permute-done.1.refs_0_), channel_id=1, source_target_pairs={{0,4},{4,8},{8,12},{12,14},{14,10},{10,6},{6,2},{2,0},{1,5},{5,9},... | collective-permute-start | bytes 562184 | tf_op jit(solution)/shard_map/ppermute | solution.py:321
  17.1 0.3 collective-permute-start.10
  17.4 0.0 collective-permute-done.4.refs_2_
  17.4 0.3 collective-permute-start.9
  17.7 2.7 %shard_map.67 = (bf16[128,1440]{1,0:T(8,128)(2,1)S(1)}, bf16[128,1440]{1,0:T(8,128)(2,1)S(1)}) custom-call(s32[2]{0:T(128)S(1)} %pad_add_fusion.after_this.place, bf16[64,1464]{1,0:T(8,128)(2,1)S(1)} %collective-permute-done.refs_0_, bf16[64,1464]{1,0:T(8,128)(2,1)S(1)} %collective-permute-done.3.refs_1_, ...), custom_call_target="tpu_custom_call" | custom-call | flops 1592524800 | bytes 12441600 | tf_op jit(solution)/shard_map/pallas_call | solution.py:210
  20.4 1.3 %collective-permute-done.2.refs_1_ = bf16[64,1464]{1,0:T(8,128)(2,1)S(1)} collective-permute-done((bf16[64,1464]{1,0:T(8,128)(2,1)S(1)}, bf16[64,1464]{1,0:T(8,128)(2,1)S(1)}, u32[]{:S(2)}, u32[]{:S(2)}) %collective-permute-start.2) | collective-permute-done | bytes 187424 | tf_op jit(solution)/shard_map/ppermute | solution.py:321
  21.8 1.8 %collective-permute-start.6 = (bf16[64,1464]{1,0:T(8,128)(2,1)S(1)}, bf16[64,1464]{1,0:T(8,128)(2,1)S(1)}, u32[]{:S(2)}, u32[]{:S(2)}) collective-permute-start(bf16[64,1464]{1,0:T(8,128)(2,1)S(1)} %collective-permute-done.2.refs_1_), channel_id=1, source_target_pairs={{0,4},{4,8},{8,12},{12,14},{14,10},{10,6},{6,2},{2,0},{1,5},{5,9},... | collective-permute-start | bytes 562184 | tf_op jit(solution)/shard_map/ppermute | solution.py:321
  23.6 0.0 collective-permute-start.12
  23.6 0.8 %collective-permute-done.10.refs_2_ = bf16[64,1464]{1,0:T(8,128)(2,1)S(1)} collective-permute-done((bf16[64,1464]{1,0:T(8,128)(2,1)S(1)}, bf16[64,1464]{1,0:T(8,128)(2,1)S(1)}, u32[]{:S(2)}, u32[]{:S(2)}) %collective-permute-start.10) | collective-permute-done | bytes 187424 | tf_op jit(solution)/shard_map/ppermute | solution.py:323
  24.5 0.0 collective-permute-done.9.refs_3_
  24.5 2.7 %shard_map.68 = (bf16[128,1440]{1,0:T(8,128)(2,1)S(1)}, bf16[128,1440]{1,0:T(8,128)(2,1)S(1)}) custom-call(s32[2]{0:T(128)S(1)} %pad_add_fusion.after_this.place, bf16[64,1464]{1,0:T(8,128)(2,1)S(1)} %collective-permute-done.1.refs_0_, bf16[64,1464]{1,0:T(8,128)(2,1)S(1)} %collective-permute-done.7.refs_1_, ...), custom_call_target="tpu_custom_call" | custom-call | flops 1592524800 | bytes 12441600 | tf_op jit(solution)/shard_map/pallas_call | solution.py:210
  27.2 0.3 collective-permute-done.6.refs_0_
  27.5 0.2 collective-permute-start.11
  27.8 1.6 %shard_map.69 = (f32[192,720]{1,0:T(8,128)S(1)}, f32[192,720]{1,0:T(8,128)S(1)}) custom-call(s32[2]{0:T(128)S(1)} %pad_add_fusion.after_this.place, bf16[64,1464]{1,0:T(8,128)(2,1)S(1)} %collective-permute-done.6.refs_0_, bf16[64,1464]{1,0:T(8,128)(2,1)S(1)} %collective-permute-done.2.refs_1_, bf16[64,1464]{1,0:T(8,128)(2,1)S(1)} %collective-permute-done.10.refs_2_, ...), custom_call_target="tpu_custom_call" | custom-call | flops 796262400 | bytes 6220800 | tf_op jit(solution)/shard_map/pallas_call | solution.py:210
  29.4 0.0 collective-permute-done.13.refs_5_
  29.4 0.0 collective-permute-done.12.refs_4_
  29.4 2.2 %shard_map.70 = (bf16[192,720]{1,0:T(8,128)(2,1)S(1)}, bf16[64,1440]{1,0:T(8,128)(2,1)S(1)}, bf16[128,1440]{1,0:T(8,128)(2,1)S(1)}) custom-call(s32[2]{0:T(128)S(1)} %pad_add_fusion.after_this.place, bf16[64,1464]{1,0:T(8,128)(2,1)S(1)} %collective-permute-done.6.refs_0_, bf16[64,1464]{1,0:T(8,128)(2,1)S(1)} %collective-permute-done.2.refs_1_, ...), custom_call_target="tpu_custom_call" | custom-call | flops 1194393600 | bytes 9331200 | tf_op jit(solution)/shard_map/pallas_call | solution.py:210
  31.6 0.3 collective-permute-start.14
  32.0 0.2 collective-permute-start.15
  32.2 0.3 collective-permute-start.19
  32.5 1.2 %shard_map.71 = (bf16[64,1440]{1,0:T(8,128)(2,1)S(1)}, bf16[128,1440]{1,0:T(8,128)(2,1)S(1)}) custom-call(s32[2]{0:T(128)S(1)} %pad_add_fusion.after_this.place, bf16[64,1464]{1,0:T(8,128)(2,1)S(1)} %collective-permute-done.6.refs_0_, bf16[64,1464]{1,0:T(8,128)(2,1)S(1)} %collective-permute-done.2.refs_1_, ...), custom_call_target="tpu_custom_call" | custom-call | flops 398131200 | bytes 3110400 | tf_op jit(solution)/shard_map/pallas_call | solution.py:210
  33.7 2.0 %collective-permute-start.21 = (bf16[64,1440]{1,0:T(8,128)(2,1)S(1)}, bf16[64,1440]{1,0:T(8,128)(2,1)S(1)}, u32[]{:S(2)}, u32[]{:S(2)}) collective-permute-start(bf16[64,1440]{1,0:T(8,128)(2,1)S(1)} %fusion), channel_id=1, source_target_pairs={{0,4},{4,8},{8,12},{12,14},{14,10},{10,6},{6,2},{2,0},{1,5},{5,9},... | collective-permute-start | bytes 552968 | tf_op jit(solution)/shard_map/ppermute | solution.py:343
  35.7 0.0 collective-permute-start.18
  35.7 0.0 collective-permute-done.15.refs_1_
  35.7 2.7 %shard_map.72 = (bf16[64,1440]{1,0:T(8,128)(2,1)S(1)}, bf16[64,1440]{1,0:T(8,128)(2,1)S(1)}) custom-call(s32[2]{0:T(128)S(1)} %pad_add_fusion.after_this.place, bf16[64,1464]{1,0:T(8,128)(2,1)S(1)} %shard_map.64.refs_0_, bf16[64,1464]{1,0:T(8,128)(2,1)S(1)} %collective-permute-done.15.refs_1_, ...), custom_call_target="tpu_custom_call" | custom-call | flops 1592524800 | bytes 12441600 | tf_op jit(solution)/shard_map/pallas_call | solution.py:210
  38.4 0.0 collective-permute-done.19
  38.4 0.1 add_convert_fusion.4
  38.5 0.3 collective-permute-start.20
  38.8 2.2 %collective-permute-done.21 = bf16[64,1440]{1,0:T(8,128)(2,1)S(1)} collective-permute-done((bf16[64,1440]{1,0:T(8,128)(2,1)S(1)}, bf16[64,1440]{1,0:T(8,128)(2,1)S(1)}, u32[]{:S(2)}, u32[]{:S(2)}) %collective-permute-start.21) | collective-permute-done | bytes 184352 | tf_op jit(solution)/shard_map/ppermute | solution.py:343
  41.0 0.1 add_convert_fusion.3
  41.1 1.7 %collective-permute-start.23 = (bf16[64,1440]{1,0:T(8,128)(2,1)S(1)}, bf16[64,1440]{1,0:T(8,128)(2,1)S(1)}, u32[]{:S(2)}, u32[]{:S(2)}) collective-permute-start(bf16[64,1440]{1,0:T(8,128)(2,1)S(1)} %add_convert_fusion.3), channel_id=1, source_target_pairs={{0,4},{4,8},{8,12},{12,14},{14,10},{10,6},{6,2},{2,0},{1,5},{5,9},... | collective-permute-start | bytes 552968 | tf_op jit(solution)/shard_map/ppermute | solution.py:343
  42.8 0.1 collective-permute-start.17
  42.8 3.0 %collective-permute-done.20.refs_2_ = bf16[64,1440]{1,0:T(8,128)(2,1)S(1)} collective-permute-done((bf16[64,1440]{1,0:T(8,128)(2,1)S(1)}, bf16[64,1440]{1,0:T(8,128)(2,1)S(1)}, u32[]{:S(2)}, u32[]{:S(2)}) %collective-permute-start.20) | collective-permute-done | bytes 184352 | tf_op jit(solution)/shard_map/ppermute | solution.py:350
  45.8 0.0 collective-permute-done.18
  45.9 0.1 shard_map.73
  45.9 0.3 collective-permute-start.22
  46.3 1.1 %collective-permute-done.23 = bf16[64,1440]{1,0:T(8,128)(2,1)S(1)} collective-permute-done((bf16[64,1440]{1,0:T(8,128)(2,1)S(1)}, bf16[64,1440]{1,0:T(8,128)(2,1)S(1)}, u32[]{:S(2)}, u32[]{:S(2)}) %collective-permute-start.23) | collective-permute-done | bytes 184352 | tf_op jit(solution)/shard_map/ppermute | solution.py:343
  47.4 0.1 add_convert_fusion.2
  47.4 1.5 %collective-permute-start.25 = (bf16[64,1440]{1,0:T(8,128)(2,1)S(1)}, bf16[64,1440]{1,0:T(8,128)(2,1)S(1)}, u32[]{:S(2)}, u32[]{:S(2)}) collective-permute-start(bf16[64,1440]{1,0:T(8,128)(2,1)S(1)} %add_convert_fusion.2), channel_id=1, source_target_pairs={{0,4},{4,8},{8,12},{12,14},{14,10},{10,6},{6,2},{2,0},{1,5},{5,9},... | collective-permute-start | bytes 552968 | tf_op jit(solution)/shard_map/ppermute | solution.py:343
  48.9 0.1 collective-permute-start.16
  49.0 0.0 collective-permute-done.17
  49.0 3.5 %collective-permute-done.22.refs_2_ = bf16[64,1440]{1,0:T(8,128)(2,1)S(1)} collective-permute-done((bf16[64,1440]{1,0:T(8,128)(2,1)S(1)}, bf16[64,1440]{1,0:T(8,128)(2,1)S(1)}, u32[]{:S(2)}, u32[]{:S(2)}) %collective-permute-start.22) | collective-permute-done | bytes 184352 | tf_op jit(solution)/shard_map/ppermute | solution.py:350
  52.5 0.1 shard_map.74
  52.6 0.4 collective-permute-start.24
  53.0 0.2 collective-permute-done.25
  53.2 0.1 add_convert_fusion.1
  53.2 1.6 %collective-permute-start.26 = (bf16[64,1440]{1,0:T(8,128)(2,1)S(1)}, bf16[64,1440]{1,0:T(8,128)(2,1)S(1)}, u32[]{:S(2)}, u32[]{:S(2)}) collective-permute-start(bf16[64,1440]{1,0:T(8,128)(2,1)S(1)} %add_convert_fusion.1), channel_id=1, source_target_pairs={{0,4},{4,8},{8,12},{12,14},{14,10},{10,6},{6,2},{2,0},{1,5},{5,9},... | collective-permute-start | bytes 552968 | tf_op jit(solution)/shard_map/ppermute | solution.py:343
  54.8 3.5 %collective-permute-done.24.refs_2_ = bf16[64,1440]{1,0:T(8,128)(2,1)S(1)} collective-permute-done((bf16[64,1440]{1,0:T(8,128)(2,1)S(1)}, bf16[64,1440]{1,0:T(8,128)(2,1)S(1)}, u32[]{:S(2)}, u32[]{:S(2)}) %collective-permute-start.24) | collective-permute-done | bytes 184352 | tf_op jit(solution)/shard_map/ppermute | solution.py:350
  58.3 0.1 shard_map.75
  58.4 0.5 collective-permute-done.26
  59.0 0.7 %add_convert_fusion = bf16[64,1440]{1,0:T(8,128)(2,1)} fusion(bf16[64,1440]{1,0:T(8,128)(2,1)S(1)} %collective-permute-done.26, bf16[64,1440]{1,0:T(8,128)(2,1)S(1)} %shard_map.75), kind=kLoop, calls=%fused_computation | loop fusion | flops 368640 | bytes 552960 | tf_op jit(solution)/shard_map/convert_element_type | solution.py:352
  (13 shorter events, 0.1 us)
Async XLA Ops:
  1.0 8.0 %collective-permute-start = (bf16[64,1464]{1,0:T(8,128)(2,1)S(1)}, bf16[64,1464]{1,0:T(8,128)(2,1)S(1)}, u32[]{:S(2)}, u32[]{:S(2)}) collective-permute-start(bf16[64,1464]{1,0:T(8,128)(2,1)S(1)} %shard_map.64.refs_0_), channel_id=1, source_target_pairs={{0,4},{4,8},{8,12},{12,14},{14,10},{10,6},{6,2},{2,0},{1,5},{5,9},... | collective-permute-start | bytes 562184 | tf_op jit(solution)/shard_map/ppermute | solution.py:316
  4.1 7.0 %collective-permute-start.3 = (bf16[64,1464]{1,0:T(8,128)(2,1)S(1)}, bf16[64,1464]{1,0:T(8,128)(2,1)S(1)}, u32[]{:S(2)}, u32[]{:S(2)}) collective-permute-start(bf16[64,1464]{1,0:T(8,128)(2,1)S(1)} %shard_map.64.refs_0_), channel_id=1, source_target_pairs={{4,0},{8,4},{12,8},{14,12},{10,14},{6,10},{2,6},{0,2},{5,1},{9,5},... | collective-permute-start | bytes 562184 | tf_op jit(solution)/shard_map/ppermute | solution.py:317
  9.0 6.4 %collective-permute-start.1 = (bf16[64,1464]{1,0:T(8,128)(2,1)S(1)}, bf16[64,1464]{1,0:T(8,128)(2,1)S(1)}, u32[]{:S(2)}, u32[]{:S(2)}) collective-permute-start(bf16[64,1464]{1,0:T(8,128)(2,1)S(1)} %collective-permute-done.refs_0_), channel_id=1, source_target_pairs={{0,4},{4,8},{8,12},{12,14},{14,10},{10,6},{6,2},{2,0},{1,5},{5,9},... | collective-permute-start | bytes 562184 | tf_op jit(solution)/shard_map/ppermute | solution.py:321
  11.1 6.1 %collective-permute-start.7 = (bf16[64,1464]{1,0:T(8,128)(2,1)S(1)}, bf16[64,1464]{1,0:T(8,128)(2,1)S(1)}, u32[]{:S(2)}, u32[]{:S(2)}) collective-permute-start(bf16[64,1464]{1,0:T(8,128)(2,1)S(1)} %collective-permute-done.3.refs_1_), channel_id=1, source_target_pairs={{4,0},{8,4},{12,8},{14,12},{10,14},{6,10},{2,6},{0,2},{5,1},{9,5},... | collective-permute-start | bytes 562184 | tf_op jit(solution)/shard_map/ppermute | solution.py:323
  11.1 6.4 %collective-permute-start.4 = (bf16[64,1464]{1,0:T(8,128)(2,1)S(1)}, bf16[64,1464]{1,0:T(8,128)(2,1)S(1)}, u32[]{:S(2)}, u32[]{:S(2)}) collective-permute-start(bf16[64,1464]{1,0:T(8,128)(2,1)S(1)} %collective-permute-done.refs_0_), channel_id=1, source_target_pairs={{0,1},{1,0},{2,3},{3,2},{4,5},{5,4},{6,7},{7,6},{8,9},{9,8},{10,11... | collective-permute-start | bytes 562184 | tf_op jit(solution)/shard_map/ppermute | solution.py:324
  11.1 6.7 %collective-permute-start.5 = (bf16[64,1464]{1,0:T(8,128)(2,1)S(1)}, bf16[64,1464]{1,0:T(8,128)(2,1)S(1)}, u32[]{:S(2)}, u32[]{:S(2)}) collective-permute-start(bf16[64,1464]{1,0:T(8,128)(2,1)S(1)} %collective-permute-done.3.refs_1_), channel_id=1, source_target_pairs={{0,1},{1,0},{2,3},{3,2},{4,5},{5,4},{6,7},{7,6},{8,9},{9,8},{10,11... | collective-permute-start | bytes 562184 | tf_op jit(solution)/shard_map/ppermute | solution.py:324
  15.4 6.4 %collective-permute-start.2 = (bf16[64,1464]{1,0:T(8,128)(2,1)S(1)}, bf16[64,1464]{1,0:T(8,128)(2,1)S(1)}, u32[]{:S(2)}, u32[]{:S(2)}) collective-permute-start(bf16[64,1464]{1,0:T(8,128)(2,1)S(1)} %collective-permute-done.1.refs_0_), channel_id=1, source_target_pairs={{0,4},{4,8},{8,12},{12,14},{14,10},{10,6},{6,2},{2,0},{1,5},{5,9},... | collective-permute-start | bytes 562184 | tf_op jit(solution)/shard_map/ppermute | solution.py:321
  17.1 7.3 %collective-permute-start.8 = (bf16[64,1464]{1,0:T(8,128)(2,1)S(1)}, bf16[64,1464]{1,0:T(8,128)(2,1)S(1)}, u32[]{:S(2)}, u32[]{:S(2)}) collective-permute-start(bf16[64,1464]{1,0:T(8,128)(2,1)S(1)} %collective-permute-done.1.refs_0_), channel_id=1, source_target_pairs={{0,1},{1,0},{2,3},{3,2},{4,5},{5,4},{6,7},{7,6},{8,9},{9,8},{10,11... | collective-permute-start | bytes 562184 | tf_op jit(solution)/shard_map/ppermute | solution.py:324
  17.1 7.3 %collective-permute-start.10 = (bf16[64,1464]{1,0:T(8,128)(2,1)S(1)}, bf16[64,1464]{1,0:T(8,128)(2,1)S(1)}, u32[]{:S(2)}, u32[]{:S(2)}) collective-permute-start(bf16[64,1464]{1,0:T(8,128)(2,1)S(1)} %collective-permute-done.7.refs_1_), channel_id=1, source_target_pairs={{4,0},{8,4},{12,8},{14,12},{10,14},{6,10},{2,6},{0,2},{5,1},{9,5},... | collective-permute-start | bytes 562184 | tf_op jit(solution)/shard_map/ppermute | solution.py:323
  17.4 7.0 %collective-permute-start.9 = (bf16[64,1464]{1,0:T(8,128)(2,1)S(1)}, bf16[64,1464]{1,0:T(8,128)(2,1)S(1)}, u32[]{:S(2)}, u32[]{:S(2)}) collective-permute-start(bf16[64,1464]{1,0:T(8,128)(2,1)S(1)} %collective-permute-done.7.refs_1_), channel_id=1, source_target_pairs={{0,1},{1,0},{2,3},{3,2},{4,5},{5,4},{6,7},{7,6},{8,9},{9,8},{10,11... | collective-permute-start | bytes 562184 | tf_op jit(solution)/shard_map/ppermute | solution.py:324
  21.8 5.7 %collective-permute-start.6 = (bf16[64,1464]{1,0:T(8,128)(2,1)S(1)}, bf16[64,1464]{1,0:T(8,128)(2,1)S(1)}, u32[]{:S(2)}, u32[]{:S(2)}) collective-permute-start(bf16[64,1464]{1,0:T(8,128)(2,1)S(1)} %collective-permute-done.2.refs_1_), channel_id=1, source_target_pairs={{0,4},{4,8},{8,12},{12,14},{14,10},{10,6},{6,2},{2,0},{1,5},{5,9},... | collective-permute-start | bytes 562184 | tf_op jit(solution)/shard_map/ppermute | solution.py:321
  23.6 5.8 %collective-permute-start.12 = (bf16[64,1464]{1,0:T(8,128)(2,1)S(1)}, bf16[64,1464]{1,0:T(8,128)(2,1)S(1)}, u32[]{:S(2)}, u32[]{:S(2)}) collective-permute-start(bf16[64,1464]{1,0:T(8,128)(2,1)S(1)} %collective-permute-done.2.refs_1_), channel_id=1, source_target_pairs={{0,1},{1,0},{2,3},{3,2},{4,5},{5,4},{6,7},{7,6},{8,9},{9,8},{10,11... | collective-permute-start | bytes 562184 | tf_op jit(solution)/shard_map/ppermute | solution.py:324
  24.5 4.9 %collective-permute-start.13 = (bf16[64,1464]{1,0:T(8,128)(2,1)S(1)}, bf16[64,1464]{1,0:T(8,128)(2,1)S(1)}, u32[]{:S(2)}, u32[]{:S(2)}) collective-permute-start(bf16[64,1464]{1,0:T(8,128)(2,1)S(1)} %collective-permute-done.10.refs_2_), channel_id=1, source_target_pairs={{0,1},{1,0},{2,3},{3,2},{4,5},{5,4},{6,7},{7,6},{8,9},{9,8},{10,11... | collective-permute-start | bytes 562184 | tf_op jit(solution)/shard_map/ppermute | solution.py:324
  27.5 1.9 %collective-permute-start.11 = (bf16[64,1464]{1,0:T(8,128)(2,1)S(1)}, bf16[64,1464]{1,0:T(8,128)(2,1)S(1)}, u32[]{:S(2)}, u32[]{:S(2)}) collective-permute-start(bf16[64,1464]{1,0:T(8,128)(2,1)S(1)} %collective-permute-done.6.refs_0_), channel_id=1, source_target_pairs={{0,1},{1,0},{2,3},{3,2},{4,5},{5,4},{6,7},{7,6},{8,9},{9,8},{10,11... | collective-permute-start | bytes 562184 | tf_op jit(solution)/shard_map/ppermute | solution.py:332
  31.6 2.0 %collective-permute-start.14 = (bf16[64,1440]{1,0:T(8,128)(2,1)S(1)}, bf16[64,1440]{1,0:T(8,128)(2,1)S(1)}, u32[]{:S(2)}, u32[]{:S(2)}) collective-permute-start(bf16[64,1440]{1,0:T(8,128)(2,1)S(1)} %get-tuple-element.66), channel_id=1, source_target_pairs={{0,1},{1,0},{2,3},{3,2},{4,5},{5,4},{6,7},{7,6},{8,9},{9,8},{10,11... | collective-permute-start | bytes 552968 | tf_op jit(solution)/shard_map/ppermute | solution.py:259
  32.0 3.8 %collective-permute-start.15 = (bf16[64,1464]{1,0:T(8,128)(2,1)S(1)}, bf16[64,1464]{1,0:T(8,128)(2,1)S(1)}, u32[]{:S(2)}, u32[]{:S(2)}) collective-permute-start(bf16[64,1464]{1,0:T(8,128)(2,1)S(1)} %shard_map.64.refs_0_), channel_id=1, source_target_pairs={{0,1},{1,0},{2,3},{3,2},{4,5},{5,4},{6,7},{7,6},{8,9},{9,8},{10,11... | collective-permute-start | bytes 562184 | tf_op jit(solution)/shard_map/ppermute | solution.py:333
  32.2 6.2 %collective-permute-start.19 = (bf16[128,1440]{1,0:T(8,128)(2,1)S(1)}, bf16[128,1440]{1,0:T(8,128)(2,1)S(1)}, u32[]{:S(2)}, u32[]{:S(2)}) collective-permute-start(bf16[128,1440]{1,0:T(8,128)(2,1)S(1)} %get-tuple-element.76), channel_id=1, source_target_pairs={{0,1},{1,0},{2,3},{3,2},{4,5},{5,4},{6,7},{7,6},{8,9},{9,8},{10,11... | collective-permute-start | bytes 1105928 | tf_op jit(solution)/shard_map/ppermute | solution.py:259
  33.7 7.3 %collective-permute-start.21 = (bf16[64,1440]{1,0:T(8,128)(2,1)S(1)}, bf16[64,1440]{1,0:T(8,128)(2,1)S(1)}, u32[]{:S(2)}, u32[]{:S(2)}) collective-permute-start(bf16[64,1440]{1,0:T(8,128)(2,1)S(1)} %fusion), channel_id=1, source_target_pairs={{0,4},{4,8},{8,12},{12,14},{14,10},{10,6},{6,2},{2,0},{1,5},{5,9},... | collective-permute-start | bytes 552968 | tf_op jit(solution)/shard_map/ppermute | solution.py:343
  35.7 10.1 %collective-permute-start.18 = (bf16[128,1440]{1,0:T(8,128)(2,1)S(1)}, bf16[128,1440]{1,0:T(8,128)(2,1)S(1)}, u32[]{:S(2)}, u32[]{:S(2)}) collective-permute-start(bf16[128,1440]{1,0:T(8,128)(2,1)S(1)} %get-tuple-element.74), channel_id=1, source_target_pairs={{0,1},{1,0},{2,3},{3,2},{4,5},{5,4},{6,7},{7,6},{8,9},{9,8},{10,11... | collective-permute-start | bytes 1105928 | tf_op jit(solution)/shard_map/ppermute | solution.py:338
  38.5 7.4 %collective-permute-start.20 = (bf16[64,1440]{1,0:T(8,128)(2,1)S(1)}, bf16[64,1440]{1,0:T(8,128)(2,1)S(1)}, u32[]{:S(2)}, u32[]{:S(2)}) collective-permute-start(bf16[64,1440]{1,0:T(8,128)(2,1)S(1)} %add_convert_fusion.4), channel_id=1, source_target_pairs={{4,0},{8,4},{12,8},{14,12},{10,14},{6,10},{2,6},{0,2},{5,1},{9,5},... | collective-permute-start | bytes 552968 | tf_op jit(solution)/shard_map/ppermute | solution.py:350
  41.1 6.3 %collective-permute-start.23 = (bf16[64,1440]{1,0:T(8,128)(2,1)S(1)}, bf16[64,1440]{1,0:T(8,128)(2,1)S(1)}, u32[]{:S(2)}, u32[]{:S(2)}) collective-permute-start(bf16[64,1440]{1,0:T(8,128)(2,1)S(1)} %add_convert_fusion.3), channel_id=1, source_target_pairs={{0,4},{4,8},{8,12},{12,14},{14,10},{10,6},{6,2},{2,0},{1,5},{5,9},... | collective-permute-start | bytes 552968 | tf_op jit(solution)/shard_map/ppermute | solution.py:343
  42.8 6.3 %collective-permute-start.17 = (bf16[128,1440]{1,0:T(8,128)(2,1)S(1)}, bf16[128,1440]{1,0:T(8,128)(2,1)S(1)}, u32[]{:S(2)}, u32[]{:S(2)}) collective-permute-start(bf16[128,1440]{1,0:T(8,128)(2,1)S(1)} %get-tuple-element.72), channel_id=1, source_target_pairs={{0,1},{1,0},{2,3},{3,2},{4,5},{5,4},{6,7},{7,6},{8,9},{9,8},{10,11... | collective-permute-start | bytes 1105928 | tf_op jit(solution)/shard_map/ppermute | solution.py:338
  45.9 6.6 %collective-permute-start.22 = (bf16[64,1440]{1,0:T(8,128)(2,1)S(1)}, bf16[64,1440]{1,0:T(8,128)(2,1)S(1)}, u32[]{:S(2)}, u32[]{:S(2)}) collective-permute-start(bf16[64,1440]{1,0:T(8,128)(2,1)S(1)} %shard_map.73), channel_id=1, source_target_pairs={{4,0},{8,4},{12,8},{14,12},{10,14},{6,10},{2,6},{0,2},{5,1},{9,5},... | collective-permute-start | bytes 552968 | tf_op jit(solution)/shard_map/ppermute | solution.py:350
  47.4 5.7 %collective-permute-start.25 = (bf16[64,1440]{1,0:T(8,128)(2,1)S(1)}, bf16[64,1440]{1,0:T(8,128)(2,1)S(1)}, u32[]{:S(2)}, u32[]{:S(2)}) collective-permute-start(bf16[64,1440]{1,0:T(8,128)(2,1)S(1)} %add_convert_fusion.2), channel_id=1, source_target_pairs={{0,4},{4,8},{8,12},{12,14},{14,10},{10,6},{6,2},{2,0},{1,5},{5,9},... | collective-permute-start | bytes 552968 | tf_op jit(solution)/shard_map/ppermute | solution.py:343
  48.9 9.4 %collective-permute-start.16 = (bf16[64,1440]{1,0:T(8,128)(2,1)S(1)}, bf16[64,1440]{1,0:T(8,128)(2,1)S(1)}, u32[]{:S(2)}, u32[]{:S(2)}) collective-permute-start(bf16[64,1440]{1,0:T(8,128)(2,1)S(1)} %get-tuple-element.70), channel_id=1, source_target_pairs={{0,1},{1,0},{2,3},{3,2},{4,5},{5,4},{6,7},{7,6},{8,9},{9,8},{10,11... | collective-permute-start | bytes 552968 | tf_op jit(solution)/shard_map/ppermute | solution.py:346
  52.6 5.7 %collective-permute-start.24 = (bf16[64,1440]{1,0:T(8,128)(2,1)S(1)}, bf16[64,1440]{1,0:T(8,128)(2,1)S(1)}, u32[]{:S(2)}, u32[]{:S(2)}) collective-permute-start(bf16[64,1440]{1,0:T(8,128)(2,1)S(1)} %shard_map.74), channel_id=1, source_target_pairs={{4,0},{8,4},{12,8},{14,12},{10,14},{6,10},{2,6},{0,2},{5,1},{9,5},... | collective-permute-start | bytes 552968 | tf_op jit(solution)/shard_map/ppermute | solution.py:350
  53.2 5.7 %collective-permute-start.26 = (bf16[64,1440]{1,0:T(8,128)(2,1)S(1)}, bf16[64,1440]{1,0:T(8,128)(2,1)S(1)}, u32[]{:S(2)}, u32[]{:S(2)}) collective-permute-start(bf16[64,1440]{1,0:T(8,128)(2,1)S(1)} %add_convert_fusion.1), channel_id=1, source_target_pairs={{0,4},{4,8},{8,12},{12,14},{14,10},{10,6},{6,2},{2,0},{1,5},{5,9},... | collective-permute-start | bytes 552968 | tf_op jit(solution)/shard_map/ppermute | solution.py:343

commit v15 on v14

--- a/solution.py
+++ b/solution.py
@@ -20,6 +20,23 @@
 
 def after(x, done):
     return lax.optimization_barrier((x, done))[0]
+
+
+def tiles_of(rows, columns):
+    whole, rest = divmod(columns, 128)
+    parts = 1
+    while rest and 128 // (2 * parts) >= rest and rows % (32 * parts) == 0:
+        parts *= 2
+    return whole, rest, parts, whole * rows + (rows // parts if rest else 0)
+
+
+def tile_places(rows, columns):
+    whole, rest, parts, size = tiles_of(rows, columns)
+    for j in range(whole):
+        yield slice(0, rows), slice(128 * j, 128 * j + 128), slice(j * rows, (j + 1) * rows), slice(0, 128)
+    for q in range(parts if rest else 0):
+        share, lane = rows // parts, q * (128 // parts)
+        yield slice(q * share, (q + 1) * share), slice(128 * whole, columns), slice(whole * rows, size), slice(lane, lane + rest)
 
 
 def pack_kernel(n_experts, tokens_in, ids_in, probs_in, packed, tokens, ids, probs, sems):
@@ -42,9 +59,15 @@
         term = rest.astype(jnp.bfloat16).astype(jnp.float32)
         terms.append(term)
         rest = rest - term
-    packed[:, half:] = jnp.concatenate(terms, axis=0).T.astype(jnp.bfloat16)
+    terms = jnp.concatenate(terms, axis=0).T.astype(jnp.bfloat16)
     copies[2].wait()
-    packed[:, :half] = tokens[...]
+    for r, c, at, lanes in tile_places(rows, half + terms.shape[1]):
+        if c.stop <= half:
+            packed[at, lanes] = tokens[r, c]
+        else:
+            split = lanes.start + half - c.start
+            packed[at, lanes.start : split] = tokens[r, c.start : half]
+            packed[at, split : lanes.stop] = terms[r, :]
 
 
 def pack(tokens, expert_ids, gate_probs, n_experts):
@@ -52,7 +75,7 @@
     args = (tokens, expert_ids.T, gate_probs.T)
     return pl.pallas_call(
         functools.partial(pack_kernel, n_experts),
-        out_shape=in_vmem((rows, half + SPLITS * n_experts)),
+        out_shape=in_vmem((tiles_of(rows, half + SPLITS * n_experts)[-1], 128)),
         in_specs=[pl.BlockSpec(memory_space=pltpu.HBM)] * 3,
         out_specs=pl.BlockSpec(memory_space=pltpu.VMEM),
         scratch_shapes=[pltpu.VMEM(a.shape, a.dtype) for a in args] + [pltpu.SemaphoreType.DMA((3,))],
@@ -128,13 +151,15 @@
     )(place, pltpu.with_memory_space_constraint(w_down, pltpu.HBM))
 
 
-def gather_rows(blocks, x, width):
-    start = 0
-    for block in blocks:
-        x[start : start + block.shape[0], :] = block[:, :width]
-        start += block.shape[0]
+def gather_rows(blocks, x, rows, columns):
+    half = x.shape[1]
+    for i, block in enumerate(blocks):
+        for r, c, at, lanes in tile_places(rows, columns):
+            stop = min(c.stop, half)
+            x[i * rows + r.start : i * rows + r.stop, c.start : stop] = block[at, lanes.start : lanes.start + stop - c.start]
+    start = len(blocks) * rows
     if start < x.shape[0]:
-        x[start:, :] = jnp.zeros((x.shape[0] - start, width), x.dtype)
+        x[start:, :] = jnp.zeros((x.shape[0] - start, half), x.dtype)
 
 
 def project(x, lane, w):
@@ -146,63 +171,70 @@
     return (gated / (1.0 + jnp.exp(-gated)) * lifted).astype(jnp.bfloat16)
 
 
-def gate_weights(blocks, half, expert, n_experts):
+def gate_weights(blocks, half, expert, n_experts, rows):
+    columns = half + SPLITS * n_experts
     weights = []
     for block in blocks:
-        terms = block[:, half:].astype(jnp.float32)
-        column = lax.broadcasted_iota(jnp.int32, terms.shape, 1)
-        weights.append(jnp.sum(jnp.where(lax.rem(column, n_experts) == expert, terms, 0.0), axis=1, keepdims=True))
+        pieces = []
+        for _, c, at, lanes in tile_places(rows, columns):
+            if c.stop == columns:
+                terms = block[at, lanes.start + half - c.start : lanes.stop].astype(jnp.float32)
+                column = lax.broadcasted_iota(jnp.int32, terms.shape, 1)
+                pieces.append(jnp.sum(jnp.where(lax.rem(column, n_experts) == expert, terms, 0.0), axis=1, keepdims=True))
+        weights.append(jnp.concatenate(pieces, axis=0))
     return weights
 
 
 def lower(hidden, w, weights, *outs):
     value = jnp.dot(hidden, w[...], preferred_element_type=jnp.float32)
-    places = [(out, at) for out in outs for at in range(0, out.shape[0], weights[0].shape[0])]
-    start = 0
-    for weight, (out, at) in zip(weights, places):
-        rows = weight.shape[0]
-        out[at : at + rows] = (value[start : start + rows] * weight).astype(jnp.bfloat16)
-        start += rows
-
-
-def expert_kernel(n_blocks, n_experts, place, *refs):
+    rows, half = weights[0].shape[0], w.shape[1]
+    size = tiles_of(rows, half)[-1]
+    places = [(out, start) for out in outs for start in range(0, out.shape[0], size)]
+    for i, (weight, (out, start)) in enumerate(zip(weights, places)):
+        scaled = (value[i * rows : (i + 1) * rows] * weight).astype(jnp.bfloat16)
+        for r, c, at, lanes in tile_places(rows, half):
+            out[start + at.start : start + at.stop, lanes] = scaled[r, c]
+
+
+def expert_kernel(n_blocks, n_experts, rows, place, *refs):
     own, across = refs[:n_blocks], refs[n_blocks : 2 * n_blocks]
     w_gate, w_up, down_mine, down_theirs, *outs, x_own, x_across = refs[2 * n_blocks :]
     lane, expert = place[0], place[1]
     half = x_own.shape[1]
-    gather_rows(own, x_own, half)
-    gather_rows(across, x_across, half)
+    columns = half + SPLITS * n_experts
+    gather_rows(own, x_own, rows, columns)
+    gather_rows(across, x_across, rows, columns)
     gated = project(x_own, lane, w_gate) + project(x_across, 1 - lane, w_gate)
     lifted = project(x_own, lane, w_up) + project(x_across, 1 - lane, w_up)
     hidden = activate(gated, lifted)
-    weights = gate_weights(own, half, expert, n_experts)
+    weights = gate_weights(own, half, expert, n_experts, rows)
     mine, theirs = outs[: len(outs) // 2], outs[len(outs) // 2 :]
     lower(hidden, down_theirs, weights, *theirs)
     lower(hidden, down_mine, weights, *mine)
 
 
-def first_kernel(n_blocks, place, *refs):
+def first_kernel(n_blocks, n_experts, rows, place, *refs):
     own = refs[:n_blocks]
     w_gate, w_up, gated, lifted, x = refs[n_blocks:]
-    gather_rows(own, x, x.shape[1])
+    gather_rows(own, x, rows, x.shape[1] + SPLITS * n_experts)
     gated[...] = project(x, place[0], w_gate)
     lifted[...] = project(x, place[0], w_up)
 
 
-def second_kernel(n_blocks, n_experts, place, *refs):
+def second_kernel(n_blocks, n_experts, rows, place, *refs):
     own, across = refs[:n_blocks], refs[n_blocks : 2 * n_blocks]
     gated, lifted, w_gate, w_up, down_theirs, hidden, *theirs, x = refs[2 * n_blocks :]
     half = x.shape[1]
-    gather_rows(across, x, half)
+    gather_rows(across, x, rows, half + SPLITS * n_experts)
     there = 1 - place[0]
     hidden[...] = activate(gated[...] + project(x, there, w_gate), lifted[...] + project(x, there, w_up))
-    lower(hidden[...], down_theirs, gate_weights(own, half, place[1], n_experts), *theirs)
-
-
-def third_kernel(n_blocks, n_experts, place, *refs):
+    lower(hidden[...], down_theirs, gate_weights(own, half, place[1], n_experts, rows), *theirs)
+
+
+def third_kernel(n_blocks, n_experts, rows, place, *refs):
     own = refs[:n_blocks]
     hidden, down_mine, *mine = refs[n_blocks:]
-    lower(hidden[...], down_mine, gate_weights(own, mine[0].shape[1], place[1], n_experts), *mine)
+    lower(hidden[...], down_mine, gate_weights(own, down_mine.shape[1], place[1], n_experts, rows), *mine)
 
 
 def call(kernel, place, args, out_shape, scratch_shapes, flops):
@@ -222,34 +254,34 @@
     return max(rows, 128)
 
 
-def run_expert(place, own, across, weights, n_experts):
+def run_expert(place, own, across, weights, n_experts, block_rows):
     width, hidden = weights[0].shape
     half = width // 2
-    rows, pairs = sum(a.shape[0] for a in own), max(1, len(own) // 2)
+    rows, pairs = len(own) * block_rows, max(1, len(own) // 2)
     outs = call(
-        functools.partial(expert_kernel, len(own), n_experts),
+        functools.partial(expert_kernel, len(own), n_experts, block_rows),
         place,
         (*own, *across, *weights),
-        [in_vmem((rows // pairs, half))] * (2 * pairs),
+        [in_vmem((len(own) // pairs * tiles_of(block_rows, half)[-1], 128))] * (2 * pairs),
         [pltpu.VMEM((padded(rows), half), jnp.bfloat16)] * 2,
         6 * padded(rows) * hidden * width,
     )
     return outs[:pairs], outs[pairs:]
 
 
-def run_expert_in_stages(place, own, across, swap, weights, n_experts):
+def run_expert_in_stages(place, own, across, swap, weights, n_experts, block_rows):
     gate, up, down_mine, down_theirs = weights
     width, hidden = gate.shape
     half = width // 2
-    rows, n_blocks = sum(a.shape[0] for a in own), len(own)
-    first = own[0].shape[0]
+    n_blocks = len(own)
+    rows, size = n_blocks * block_rows, tiles_of(block_rows, half)[-1]
     products = [in_vmem((padded(rows), hidden), jnp.float32)] * 2
-    outs = [in_vmem((first, half)), in_vmem((rows - first, half))]
+    outs = [in_vmem((size, 128)), in_vmem(((n_blocks - 1) * size, 128))]
     x = [pltpu.VMEM((padded(rows), half), jnp.bfloat16)]
     flops = 2 * padded(rows) * hidden * width
-    gated, lifted = call(functools.partial(first_kernel, n_blocks), place, (*own, gate, up), products, x, flops)
+    gated, lifted = call(functools.partial(first_kernel, n_blocks, n_experts, block_rows), place, (*own, gate, up), products, x, flops)
     units, *theirs = call(
-        functools.partial(second_kernel, n_blocks, n_experts),
+        functools.partial(second_kernel, n_blocks, n_experts, block_rows),
         place,
         (*own, *across, gated, lifted, gate, up, down_theirs),
         [in_vmem((padded(rows), hidden)), *outs],
@@ -258,7 +290,7 @@
     )
     theirs = [swap(a) for a in theirs]
     mine = call(
-        functools.partial(third_kernel, n_blocks, n_experts),
+        functools.partial(third_kernel, n_blocks, n_experts, block_rows),
         place,
         (*own, units, down_mine),
         outs,
@@ -284,9 +316,27 @@
     )(*[hold(t) for t in terms])
 
 
+def finish_kernel(a, b, out):
+    rows, half = out.shape
+    for r, c, at, lanes in tile_places(rows, half):
+        total = a[at, lanes].astype(jnp.float32) + b[at, lanes].astype(jnp.float32)
+        out[r, c] = total.astype(out.dtype)
+
+
+def finish(a, b, rows, half):
+    vmem = pl.BlockSpec(memory_space=pltpu.VMEM)
+    return pl.pallas_call(
+        finish_kernel,
+        out_shape=jax.ShapeDtypeStruct((rows, half), jnp.bfloat16),
+        in_specs=[vmem] * 2,
+        out_specs=vmem,
+    )(hold(a), hold(b))
+
+
 def ring_body(tokens, expert_ids, gate_probs, w_gate, w_up, w_down):
     n = lax.axis_size("ep")
-    rows = tokens.shape[0]
+    rows, half = tokens.shape
+    size = tiles_of(rows, half)[-1]
     order = list(range(0, n, 2)) + list(range(n - 1, 0, -2))
     ahead = [(order[i], order[(i + 1) % n]) for i in range(n)]
     back = [(b, a) for a, b in ahead]
@@ -300,7 +350,7 @@
 
     def run(keys, wait_for=None):
         at = place if wait_for is None else after(place, wait_for)
-        mine, theirs = run_expert(at, [came[k] for k in keys], [across[k] for k in keys], weights, n)
+        mine, theirs = run_expert(at, [came[k] for k in keys], [across[k] for k in keys], weights, n, rows)
         return [(keys[2 * i : 2 * i + 2], *pair) for i, pair in enumerate(zip(mine, theirs))]
 
     def keep(keys, mine, theirs):
@@ -308,7 +358,7 @@
         start = 0
         for i, k in enumerate(keys):
             mine, theirs = pairs[i % 2]
-            span = slice(start, start + came[k].shape[0])
+            span = slice(start, start + size)
             start = span.stop
             parts[k] = mine[span], theirs[span]
             value[k] = mine[span].astype(jnp.float32) + theirs[span].astype(jnp.float32)
@@ -332,7 +382,7 @@
     across[far] = swap(came[far])
     across[0] = swap(after(packed, came[far]))
     last = [far, far - 1, 1 - far]
-    for keys, mine, theirs in zip(([far], last[1:]), *run_expert_in_stages(place, [came[k] for k in last], [across[k] for k in last], swap, weights, n)):
+    for keys, mine, theirs in zip(([far], last[1:]), *run_expert_in_stages(place, [came[k] for k in last], [across[k] for k in last], swap, weights, n, rows)):
         keep(keys, mine, theirs)
     for keys, mine, theirs in near:
         keep(keys, mine, swap(after(theirs, value[far])))
@@ -349,7 +399,7 @@
         if k:
             front = lax.ppermute(to_back, "ep", back)
             to_ahead = (value[-k] + after(behind, done).astype(jnp.float32)).astype(jnp.bfloat16)
-    return (to_back.astype(jnp.float32) + behind.astype(jnp.float32)).astype(jnp.bfloat16)
+    return finish(to_back, behind, rows, half)
 
 
 def swiglu_expert(rows, gate_part, up_part, down_part):
@@ -425,7 +475,7 @@
 
     def body(tokens, expert_ids, *rest):
         n, top = lax.axis_size("ep"), expert_ids.shape[1]
-        small = n <= 4 * top and n % 2 == 0 and n >= 6 and lax.axis_size("tp") == 2
+        small = n <= 4 * top and n % 2 == 0 and n >= 8 and lax.axis_size("tp") == 2 and tokens.shape[1] % 128 + SPLITS * n <= 128
         return (ring_body if small else slot_body)(tokens, expert_ids, *rest)
 
     return jax.shard_map(body, mesh=mesh, in_specs=in_specs, out_specs=out_specs, check_vma=False)

time: 59.8 us -> 59 us (0.987)
  waiting for transfers between devices: 17.3 us -> 15.5 us
  Pallas kernels: 22.2 us -> 23.4 us
  other arithmetic: 1.12 us -> 0.43 us
    ppermute x4, waiting for transfers between devices: 4.03 us -> 2.56 us  [ring_body(): behind = lax.ppermute(to_ahead, 'ep', ahead)]
    pallas_call x0 -> x1, Pallas kernels: none -> 0.75 us  [finish(): pl.pallas_call(finish_kernel, out_shape=jax.ShapeDtypeStruct((rows, half)...]
    convert_element_type x1 -> x0, other arithmetic: 0.72 us -> none  [ring_body(): (to_back.astype(jnp.float32) + behind.astype(jnp.float32)).astype(jnp.bfl...]
  transfers between devices with their start and end apart: 27 -> 27, of which waited for: 11 -> 10; matrix products, arithmetic and copies ran while one was open for 1% -> 1% of each run, Pallas kernels for 32% -> 33%
where the time goes in v15:
time: 59 us; the launch traced here: 58.8 us
  Pallas kernels  23.4 us (40%)
  starting transfers between devices  19.2 us (33%)
  waiting for transfers between devices  15.5 us (26%)
    pallas_call x6, Pallas kernels, call(): pl.pallas_call(kernel, out_shape=out_shape, in_specs=[pl.BlockSpec(memory...  13.5 us
    ppermute x3, waiting for transfers between devices, ring_body(): front = lax.ppermute(to_back, 'ep', back)  9.92 us
    ppermute x4, starting transfers between devices, ring_body(): behind = lax.ppermute(to_ahead, 'ep', ahead)  7.18 us
    ppermute x3, starting transfers between devices, ring_body(): came[k] = lax.ppermute(came[k - 1], 'ep', ahead)  5.64 us
    pallas_call x1, Pallas kernels, turn_weights(): pl.pallas_call(turn_kernel, out_shape=[in_vmem((width, hidden))] * 2, in_...  4.79 us
    pallas_call x1, Pallas kernels, halve_weights(): pl.pallas_call(halve_kernel, out_shape=[in_vmem((hidden, width // 2))] *...  3.13 us
    ppermute x1, starting transfers between devices, ring_body(): came[1] = lax.ppermute(packed, 'ep', ahead)  3.08 us
    ppermute x4, waiting for transfers between devices, ring_body(): behind = lax.ppermute(to_ahead, 'ep', ahead)  2.56 us
  transfers between devices with their start and end apart: 27, of which 10 were waited for; matrix products, arithmetic and copies ran while one was open for 1% of the time, Pallas kernels for 33%

profile of v15, /device:TPU:0, one launch (start us, length us, event | category | flops | bytes accessed | tf_op | source)
XLA Modules:
  0.0 58.8 jit_solution(4357102010109765410)
XLA Ops:
  0.0 1.1 %shard_map.64.refs_0_ = bf16[736,128]{1,0:T(8,128)(2,1)S(1)} custom-call(bf16[64,1440]{1,0:T(8,128)(2,1)} %tokens_in.1, s32[4,64]{1,0:T(4,128)} %bitcast.14, f32[4,64]{1,0:T(4,128)} %bitcast.15), custom_call_target="tpu_custom_call" | custom-call | tf_op jit(solution)/shard_map/pallas_call | solution.py:76
  1.1 3.1 %collective-permute-start = (bf16[736,128]{1,0:T(8,128)(2,1)S(1)}, bf16[736,128]{1,0:T(8,128)(2,1)S(1)}, u32[]{:S(2)}, u32[]{:S(2)}) collective-permute-start(bf16[736,128]{1,0:T(8,128)(2,1)S(1)} %shard_map.64.refs_0_), channel_id=1, source_target_pairs={{0,4},{4,8},{8,12},{12,14},{14,10},{10,6},{6,2},{2,0},{1,5},{5,9},... | collective-permute-start | bytes 565256 | tf_op jit(solution)/shard_map/ppermute | solution.py:366
  4.2 0.0 collective-permute-start.3
  4.2 0.1 pad_add_fusion.after_this.place
  4.3 4.8 %shard_map.65 = (bf16[2880,720]{1,0:T(8,128)(2,1)S(1)}, bf16[2880,720]{1,0:T(8,128)(2,1)S(1)}) custom-call(s32[2]{0:T(128)S(1)} %pad_add_fusion.after_this.place, bf16[720,2880]{1,0:T(8,128)(2,1)} %bitcast.11, bf16[720,2880]{1,0:T(8,128)(2,1)} %bitcast.12), custom_call_target="tpu_custom_call" | custom-call | bytes 16588800 | tf_op jit(solution)/shard_map/pallas_call | solution.py:106
  9.1 0.0 collective-permute-done.refs_0_
  9.1 2.1 %collective-permute-start.1 = (bf16[736,128]{1,0:T(8,128)(2,1)S(1)}, bf16[736,128]{1,0:T(8,128)(2,1)S(1)}, u32[]{:S(2)}, u32[]{:S(2)}) collective-permute-start(bf16[736,128]{1,0:T(8,128)(2,1)S(1)} %collective-permute-done.refs_0_), channel_id=1, source_target_pairs={{0,4},{4,8},{8,12},{12,14},{14,10},{10,6},{6,2},{2,0},{1,5},{5,9},... | collective-permute-start | bytes 565256 | tf_op jit(solution)/shard_map/ppermute | solution.py:371
  11.1 0.0 collective-permute-done.3.refs_1_
  11.1 0.0 collective-permute-start.7
  11.2 0.5 collective-permute-start.5
  11.7 3.1 %shard_map.66 = (bf16[720,1440]{1,0:T(8,128)(2,1)S(1)}, bf16[720,1440]{1,0:T(8,128)(2,1)S(1)}) custom-call(s32[2]{0:T(128)S(1)} %pad_add_fusion.after_this.place, bf16[720,2880]{1,0:T(8,128)(2,1)} %bitcast.13), custom_call_target="tpu_custom_call" | custom-call | bytes 16588800 | tf_op jit(solution)/shard_map/pallas_call | solution.py:143
  14.8 0.5 collective-permute-done.1.refs_0_
  15.3 1.7 %collective-permute-start.2 = (bf16[736,128]{1,0:T(8,128)(2,1)S(1)}, bf16[736,128]{1,0:T(8,128)(2,1)S(1)}, u32[]{:S(2)}, u32[]{:S(2)}) collective-permute-start(bf16[736,128]{1,0:T(8,128)(2,1)S(1)} %collective-permute-done.1.refs_0_), channel_id=1, source_target_pairs={{0,4},{4,8},{8,12},{12,14},{14,10},{10,6},{6,2},{2,0},{1,5},{5,9},... | collective-permute-start | bytes 565256 | tf_op jit(solution)/shard_map/ppermute | solution.py:371
  17.0 0.0 collective-permute-start.8
  17.0 0.0 collective-permute-done.7.refs_1_
  17.1 0.3 collective-permute-start.10
  17.3 0.3 collective-permute-start.9
  17.6 0.0 collective-permute-done.5.refs_3_
  17.6 2.8 %shard_map.67 = (bf16[1440,128]{1,0:T(8,128)(2,1)S(1)}, bf16[1440,128]{1,0:T(8,128)(2,1)S(1)}) custom-call(s32[2]{0:T(128)S(1)} %pad_add_fusion.after_this.place, bf16[736,128]{1,0:T(8,128)(2,1)S(1)} %collective-permute-done.refs_0_, bf16[736,128]{1,0:T(8,128)(2,1)S(1)} %collective-permute-done.3.refs_1_, ...), custom_call_target="tpu_custom_call" | custom-call | flops 1592524800 | bytes 12441600 | tf_op jit(solution)/shard_map/pallas_call | solution.py:242
  20.4 1.3 %collective-permute-done.2.refs_1_ = bf16[736,128]{1,0:T(8,128)(2,1)S(1)} collective-permute-done((bf16[736,128]{1,0:T(8,128)(2,1)S(1)}, bf16[736,128]{1,0:T(8,128)(2,1)S(1)}, u32[]{:S(2)}, u32[]{:S(2)}) %collective-permute-start.2) | collective-permute-done | bytes 188448 | tf_op jit(solution)/shard_map/ppermute | solution.py:371
  21.7 1.8 %collective-permute-start.6 = (bf16[736,128]{1,0:T(8,128)(2,1)S(1)}, bf16[736,128]{1,0:T(8,128)(2,1)S(1)}, u32[]{:S(2)}, u32[]{:S(2)}) collective-permute-start(bf16[736,128]{1,0:T(8,128)(2,1)S(1)} %collective-permute-done.2.refs_1_), channel_id=1, source_target_pairs={{0,4},{4,8},{8,12},{12,14},{14,10},{10,6},{6,2},{2,0},{1,5},{5,9},... | collective-permute-start | bytes 565256 | tf_op jit(solution)/shard_map/ppermute | solution.py:371
  23.5 0.0 collective-permute-start.12
  23.5 0.7 %collective-permute-done.10.refs_2_ = bf16[736,128]{1,0:T(8,128)(2,1)S(1)} collective-permute-done((bf16[736,128]{1,0:T(8,128)(2,1)S(1)}, bf16[736,128]{1,0:T(8,128)(2,1)S(1)}, u32[]{:S(2)}, u32[]{:S(2)}) %collective-permute-start.10) | collective-permute-done | bytes 188448 | tf_op jit(solution)/shard_map/ppermute | solution.py:373
  24.2 0.0 collective-permute-done.9.refs_3_
  24.2 2.8 %shard_map.68 = (bf16[1440,128]{1,0:T(8,128)(2,1)S(1)}, bf16[1440,128]{1,0:T(8,128)(2,1)S(1)}) custom-call(s32[2]{0:T(128)S(1)} %pad_add_fusion.after_this.place, bf16[736,128]{1,0:T(8,128)(2,1)S(1)} %collective-permute-done.1.refs_0_, bf16[736,128]{1,0:T(8,128)(2,1)S(1)} %collective-permute-done.7.refs_1_, ...), custom_call_target="tpu_custom_call" | custom-call | flops 1592524800 | bytes 12441600 | tf_op jit(solution)/shard_map/pallas_call | solution.py:242
  27.0 0.5 collective-permute-done.6.refs_0_
  27.5 0.1 collective-permute-start.11
  27.5 1.7 %shard_map.69 = (f32[192,720]{1,0:T(8,128)S(1)}, f32[192,720]{1,0:T(8,128)S(1)}) custom-call(s32[2]{0:T(128)S(1)} %pad_add_fusion.after_this.place, bf16[736,128]{1,0:T(8,128)(2,1)S(1)} %collective-permute-done.6.refs_0_, bf16[736,128]{1,0:T(8,128)(2,1)S(1)} %collective-permute-done.2.refs_1_, bf16[736,128]{1,0:T(8,128)(2,1)S(1)} %collective-permute-done.10.refs_2_, ...), custom_call_target="tpu_custom_call" | custom-call | flops 796262400 | bytes 6220800 | tf_op jit(solution)/shard_map/pallas_call | solution.py:242
  29.2 0.0 collective-permute-done.13.refs_5_
  29.2 0.0 collective-permute-done.11.refs_3_
  29.2 2.3 %shard_map.70 = (bf16[192,720]{1,0:T(8,128)(2,1)S(1)}, bf16[720,128]{1,0:T(8,128)(2,1)S(1)}, bf16[1440,128]{1,0:T(8,128)(2,1)S(1)}) custom-call(s32[2]{0:T(128)S(1)} %pad_add_fusion.after_this.place, bf16[736,128]{1,0:T(8,128)(2,1)S(1)} %collective-permute-done.6.refs_0_, bf16[736,128]{1,0:T(8,128)(2,1)S(1)} %collective-permute-done.2.refs_1_, ...), custom_call_target="tpu_custom_call" | custom-call | flops 1194393600 | bytes 9331200 | tf_op jit(solution)/shard_map/pallas_call | solution.py:242
  31.5 0.5 collective-permute-start.14
  32.0 0.1 collective-permute-start.15
  32.1 0.4 collective-permute-start.19
  32.5 1.3 %shard_map.71 = (bf16[720,128]{1,0:T(8,128)(2,1)S(1)}, bf16[1440,128]{1,0:T(8,128)(2,1)S(1)}) custom-call(s32[2]{0:T(128)S(1)} %pad_add_fusion.after_this.place, bf16[736,128]{1,0:T(8,128)(2,1)S(1)} %collective-permute-done.6.refs_0_, bf16[736,128]{1,0:T(8,128)(2,1)S(1)} %collective-permute-done.2.refs_1_, ...), custom_call_target="tpu_custom_call" | custom-call | flops 398131200 | bytes 3110400 | tf_op jit(solution)/shard_map/pallas_call | solution.py:242
  33.8 0.0 collective-permute-done.14
  33.8 0.1 fusion
  33.9 1.8 %collective-permute-start.21 = (bf16[720,128]{1,0:T(8,128)(2,1)S(1)}, bf16[720,128]{1,0:T(8,128)(2,1)S(1)}, u32[]{:S(2)}, u32[]{:S(2)}) collective-permute-start(bf16[720,128]{1,0:T(8,128)(2,1)S(1)} %fusion), channel_id=1, source_target_pairs={{0,4},{4,8},{8,12},{12,14},{14,10},{10,6},{6,2},{2,0},{1,5},{5,9},... | collective-permute-start | bytes 552968 | tf_op jit(solution)/shard_map/ppermute | solution.py:393
  35.7 0.0 collective-permute-start.18
  35.7 0.0 collective-permute-done.15.refs_1_
  35.7 2.7 %shard_map.72 = (bf16[720,128]{1,0:T(8,128)(2,1)S(1)}, bf16[720,128]{1,0:T(8,128)(2,1)S(1)}) custom-call(s32[2]{0:T(128)S(1)} %pad_add_fusion.after_this.place, bf16[736,128]{1,0:T(8,128)(2,1)S(1)} %shard_map.64.refs_0_, bf16[736,128]{1,0:T(8,128)(2,1)S(1)} %collective-permute-done.15.refs_1_, ...), custom_call_target="tpu_custom_call" | custom-call | flops 1592524800 | bytes 12441600 | tf_op jit(solution)/shard_map/pallas_call | solution.py:242
  38.4 0.0 collective-permute-done.19
  38.4 0.1 add_convert_fusion.3
  38.5 0.3 collective-permute-start.20
  38.8 1.7 %collective-permute-done.21 = bf16[720,128]{1,0:T(8,128)(2,1)S(1)} collective-permute-done((bf16[720,128]{1,0:T(8,128)(2,1)S(1)}, bf16[720,128]{1,0:T(8,128)(2,1)S(1)}, u32[]{:S(2)}, u32[]{:S(2)}) %collective-permute-start.21) | collective-permute-done | bytes 184352 | tf_op jit(solution)/shard_map/ppermute | solution.py:393
  40.6 0.1 add_convert_fusion.2
  40.6 1.8 %collective-permute-start.23 = (bf16[720,128]{1,0:T(8,128)(2,1)S(1)}, bf16[720,128]{1,0:T(8,128)(2,1)S(1)}, u32[]{:S(2)}, u32[]{:S(2)}) collective-permute-start(bf16[720,128]{1,0:T(8,128)(2,1)S(1)} %add_convert_fusion.2), channel_id=1, source_target_pairs={{0,4},{4,8},{8,12},{12,14},{14,10},{10,6},{6,2},{2,0},{1,5},{5,9},... | collective-permute-start | bytes 552968 | tf_op jit(solution)/shard_map/ppermute | solution.py:393
  42.5 0.1 collective-permute-start.17
  42.5 3.0 %collective-permute-done.20.refs_2_ = bf16[720,128]{1,0:T(8,128)(2,1)S(1)} collective-permute-done((bf16[720,128]{1,0:T(8,128)(2,1)S(1)}, bf16[720,128]{1,0:T(8,128)(2,1)S(1)}, u32[]{:S(2)}, u32[]{:S(2)}) %collective-permute-start.20) | collective-permute-done | bytes 184352 | tf_op jit(solution)/shard_map/ppermute | solution.py:400
  45.6 0.1 shard_map.73
  45.7 0.3 collective-permute-start.22
  46.0 0.5 collective-permute-done.23
  46.5 0.1 add_convert_fusion.1
  46.6 1.8 %collective-permute-start.25 = (bf16[720,128]{1,0:T(8,128)(2,1)S(1)}, bf16[720,128]{1,0:T(8,128)(2,1)S(1)}, u32[]{:S(2)}, u32[]{:S(2)}) collective-permute-start(bf16[720,128]{1,0:T(8,128)(2,1)S(1)} %add_convert_fusion.1), channel_id=1, source_target_pairs={{0,4},{4,8},{8,12},{12,14},{14,10},{10,6},{6,2},{2,0},{1,5},{5,9},... | collective-permute-start | bytes 552968 | tf_op jit(solution)/shard_map/ppermute | solution.py:393
  48.4 0.1 collective-permute-start.16
  48.5 3.5 %collective-permute-done.22.refs_2_ = bf16[720,128]{1,0:T(8,128)(2,1)S(1)} collective-permute-done((bf16[720,128]{1,0:T(8,128)(2,1)S(1)}, bf16[720,128]{1,0:T(8,128)(2,1)S(1)}, u32[]{:S(2)}, u32[]{:S(2)}) %collective-permute-start.22) | collective-permute-done | bytes 184352 | tf_op jit(solution)/shard_map/ppermute | solution.py:400
  52.0 0.1 shard_map.74
  52.1 0.3 collective-permute-start.24
  52.4 0.1 add_convert_fusion
  52.5 1.8 %collective-permute-start.26 = (bf16[720,128]{1,0:T(8,128)(2,1)S(1)}, bf16[720,128]{1,0:T(8,128)(2,1)S(1)}, u32[]{:S(2)}, u32[]{:S(2)}) collective-permute-start(bf16[720,128]{1,0:T(8,128)(2,1)S(1)} %add_convert_fusion), channel_id=1, source_target_pairs={{0,4},{4,8},{8,12},{12,14},{14,10},{10,6},{6,2},{2,0},{1,5},{5,9},... | collective-permute-start | bytes 552968 | tf_op jit(solution)/shard_map/ppermute | solution.py:393
  54.3 3.4 %collective-permute-done.24.refs_2_ = bf16[720,128]{1,0:T(8,128)(2,1)S(1)} collective-permute-done((bf16[720,128]{1,0:T(8,128)(2,1)S(1)}, bf16[720,128]{1,0:T(8,128)(2,1)S(1)}, u32[]{:S(2)}, u32[]{:S(2)}) %collective-permute-start.24) | collective-permute-done | bytes 184352 | tf_op jit(solution)/shard_map/ppermute | solution.py:400
  57.7 0.1 shard_map.75.a
  57.7 0.3 collective-permute-done.26.b
  58.1 0.8 %shard_map.76 = bf16[64,1440]{1,0:T(8,128)(2,1)} custom-call(bf16[720,128]{1,0:T(8,128)(2,1)S(1)} %shard_map.75.a, bf16[720,128]{1,0:T(8,128)(2,1)S(1)} %collective-permute-done.26.b), custom_call_target="tpu_custom_call" | custom-call | tf_op jit(solution)/shard_map/pallas_call | solution.py:328
  (13 shorter events, 0.1 us)
Async XLA Ops:
  1.1 8.0 %collective-permute-start = (bf16[736,128]{1,0:T(8,128)(2,1)S(1)}, bf16[736,128]{1,0:T(8,128)(2,1)S(1)}, u32[]{:S(2)}, u32[]{:S(2)}) collective-permute-start(bf16[736,128]{1,0:T(8,128)(2,1)S(1)} %shard_map.64.refs_0_), channel_id=1, source_target_pairs={{0,4},{4,8},{8,12},{12,14},{14,10},{10,6},{6,2},{2,0},{1,5},{5,9},... | collective-permute-start | bytes 565256 | tf_op jit(solution)/shard_map/ppermute | solution.py:366
  4.2 7.0 %collective-permute-start.3 = (bf16[736,128]{1,0:T(8,128)(2,1)S(1)}, bf16[736,128]{1,0:T(8,128)(2,1)S(1)}, u32[]{:S(2)}, u32[]{:S(2)}) collective-permute-start(bf16[736,128]{1,0:T(8,128)(2,1)S(1)} %shard_map.64.refs_0_), channel_id=1, source_target_pairs={{4,0},{8,4},{12,8},{14,12},{10,14},{6,10},{2,6},{0,2},{5,1},{9,5},... | collective-permute-start | bytes 565256 | tf_op jit(solution)/shard_map/ppermute | solution.py:367
  9.1 6.2 %collective-permute-start.1 = (bf16[736,128]{1,0:T(8,128)(2,1)S(1)}, bf16[736,128]{1,0:T(8,128)(2,1)S(1)}, u32[]{:S(2)}, u32[]{:S(2)}) collective-permute-start(bf16[736,128]{1,0:T(8,128)(2,1)S(1)} %collective-permute-done.refs_0_), channel_id=1, source_target_pairs={{0,4},{4,8},{8,12},{12,14},{14,10},{10,6},{6,2},{2,0},{1,5},{5,9},... | collective-permute-start | bytes 565256 | tf_op jit(solution)/shard_map/ppermute | solution.py:371
  11.1 5.9 %collective-permute-start.7 = (bf16[736,128]{1,0:T(8,128)(2,1)S(1)}, bf16[736,128]{1,0:T(8,128)(2,1)S(1)}, u32[]{:S(2)}, u32[]{:S(2)}) collective-permute-start(bf16[736,128]{1,0:T(8,128)(2,1)S(1)} %collective-permute-done.3.refs_1_), channel_id=1, source_target_pairs={{4,0},{8,4},{12,8},{14,12},{10,14},{6,10},{2,6},{0,2},{5,1},{9,5},... | collective-permute-start | bytes 565256 | tf_op jit(solution)/shard_map/ppermute | solution.py:373
  11.1 6.2 %collective-permute-start.4 = (bf16[736,128]{1,0:T(8,128)(2,1)S(1)}, bf16[736,128]{1,0:T(8,128)(2,1)S(1)}, u32[]{:S(2)}, u32[]{:S(2)}) collective-permute-start(bf16[736,128]{1,0:T(8,128)(2,1)S(1)} %collective-permute-done.refs_0_), channel_id=1, source_target_pairs={{0,1},{1,0},{2,3},{3,2},{4,5},{5,4},{6,7},{7,6},{8,9},{9,8},{10,11... | collective-permute-start | bytes 565256 | tf_op jit(solution)/shard_map/ppermute | solution.py:374
  11.2 6.5 %collective-permute-start.5 = (bf16[736,128]{1,0:T(8,128)(2,1)S(1)}, bf16[736,128]{1,0:T(8,128)(2,1)S(1)}, u32[]{:S(2)}, u32[]{:S(2)}) collective-permute-start(bf16[736,128]{1,0:T(8,128)(2,1)S(1)} %collective-permute-done.3.refs_1_), channel_id=1, source_target_pairs={{0,1},{1,0},{2,3},{3,2},{4,5},{5,4},{6,7},{7,6},{8,9},{9,8},{10,11... | collective-permute-start | bytes 565256 | tf_op jit(solution)/shard_map/ppermute | solution.py:374
  15.3 6.4 %collective-permute-start.2 = (bf16[736,128]{1,0:T(8,128)(2,1)S(1)}, bf16[736,128]{1,0:T(8,128)(2,1)S(1)}, u32[]{:S(2)}, u32[]{:S(2)}) collective-permute-start(bf16[736,128]{1,0:T(8,128)(2,1)S(1)} %collective-permute-done.1.refs_0_), channel_id=1, source_target_pairs={{0,4},{4,8},{8,12},{12,14},{14,10},{10,6},{6,2},{2,0},{1,5},{5,9},... | collective-permute-start | bytes 565256 | tf_op jit(solution)/shard_map/ppermute | solution.py:371
  17.0 7.2 %collective-permute-start.8 = (bf16[736,128]{1,0:T(8,128)(2,1)S(1)}, bf16[736,128]{1,0:T(8,128)(2,1)S(1)}, u32[]{:S(2)}, u32[]{:S(2)}) collective-permute-start(bf16[736,128]{1,0:T(8,128)(2,1)S(1)} %collective-permute-done.1.refs_0_), channel_id=1, source_target_pairs={{0,1},{1,0},{2,3},{3,2},{4,5},{5,4},{6,7},{7,6},{8,9},{9,8},{10,11... | collective-permute-start | bytes 565256 | tf_op jit(solution)/shard_map/ppermute | solution.py:374
  17.1 7.1 %collective-permute-start.10 = (bf16[736,128]{1,0:T(8,128)(2,1)S(1)}, bf16[736,128]{1,0:T(8,128)(2,1)S(1)}, u32[]{:S(2)}, u32[]{:S(2)}) collective-permute-start(bf16[736,128]{1,0:T(8,128)(2,1)S(1)} %collective-permute-done.7.refs_1_), channel_id=1, source_target_pairs={{4,0},{8,4},{12,8},{14,12},{10,14},{6,10},{2,6},{0,2},{5,1},{9,5},... | collective-permute-start | bytes 565256 | tf_op jit(solution)/shard_map/ppermute | solution.py:373
  17.3 6.9 %collective-permute-start.9 = (bf16[736,128]{1,0:T(8,128)(2,1)S(1)}, bf16[736,128]{1,0:T(8,128)(2,1)S(1)}, u32[]{:S(2)}, u32[]{:S(2)}) collective-permute-start(bf16[736,128]{1,0:T(8,128)(2,1)S(1)} %collective-permute-done.7.refs_1_), channel_id=1, source_target_pairs={{0,1},{1,0},{2,3},{3,2},{4,5},{5,4},{6,7},{7,6},{8,9},{9,8},{10,11... | collective-permute-start | bytes 565256 | tf_op jit(solution)/shard_map/ppermute | solution.py:374
  21.7 5.8 %collective-permute-start.6 = (bf16[736,128]{1,0:T(8,128)(2,1)S(1)}, bf16[736,128]{1,0:T(8,128)(2,1)S(1)}, u32[]{:S(2)}, u32[]{:S(2)}) collective-permute-start(bf16[736,128]{1,0:T(8,128)(2,1)S(1)} %collective-permute-done.2.refs_1_), channel_id=1, source_target_pairs={{0,4},{4,8},{8,12},{12,14},{14,10},{10,6},{6,2},{2,0},{1,5},{5,9},... | collective-permute-start | bytes 565256 | tf_op jit(solution)/shard_map/ppermute | solution.py:371
  23.5 5.7 %collective-permute-start.12 = (bf16[736,128]{1,0:T(8,128)(2,1)S(1)}, bf16[736,128]{1,0:T(8,128)(2,1)S(1)}, u32[]{:S(2)}, u32[]{:S(2)}) collective-permute-start(bf16[736,128]{1,0:T(8,128)(2,1)S(1)} %collective-permute-done.2.refs_1_), channel_id=1, source_target_pairs={{0,1},{1,0},{2,3},{3,2},{4,5},{5,4},{6,7},{7,6},{8,9},{9,8},{10,11... | collective-permute-start | bytes 565256 | tf_op jit(solution)/shard_map/ppermute | solution.py:374
  24.2 5.0 %collective-permute-start.13 = (bf16[736,128]{1,0:T(8,128)(2,1)S(1)}, bf16[736,128]{1,0:T(8,128)(2,1)S(1)}, u32[]{:S(2)}, u32[]{:S(2)}) collective-permute-start(bf16[736,128]{1,0:T(8,128)(2,1)S(1)} %collective-permute-done.10.refs_2_), channel_id=1, source_target_pairs={{0,1},{1,0},{2,3},{3,2},{4,5},{5,4},{6,7},{7,6},{8,9},{9,8},{10,11... | collective-permute-start | bytes 565256 | tf_op jit(solution)/shard_map/ppermute | solution.py:374
  27.5 1.7 %collective-permute-start.11 = (bf16[736,128]{1,0:T(8,128)(2,1)S(1)}, bf16[736,128]{1,0:T(8,128)(2,1)S(1)}, u32[]{:S(2)}, u32[]{:S(2)}) collective-permute-start(bf16[736,128]{1,0:T(8,128)(2,1)S(1)} %collective-permute-done.6.refs_0_), channel_id=1, source_target_pairs={{0,1},{1,0},{2,3},{3,2},{4,5},{5,4},{6,7},{7,6},{8,9},{9,8},{10,11... | collective-permute-start | bytes 565256 | tf_op jit(solution)/shard_map/ppermute | solution.py:382
  31.5 2.3 %collective-permute-start.14 = (bf16[720,128]{1,0:T(8,128)(2,1)S(1)}, bf16[720,128]{1,0:T(8,128)(2,1)S(1)}, u32[]{:S(2)}, u32[]{:S(2)}) collective-permute-start(bf16[720,128]{1,0:T(8,128)(2,1)S(1)} %get-tuple-element.66), channel_id=1, source_target_pairs={{0,1},{1,0},{2,3},{3,2},{4,5},{5,4},{6,7},{7,6},{8,9},{9,8},{10,11... | collective-permute-start | bytes 552968 | tf_op jit(solution)/shard_map/ppermute | solution.py:291
  32.0 3.7 %collective-permute-start.15 = (bf16[736,128]{1,0:T(8,128)(2,1)S(1)}, bf16[736,128]{1,0:T(8,128)(2,1)S(1)}, u32[]{:S(2)}, u32[]{:S(2)}) collective-permute-start(bf16[736,128]{1,0:T(8,128)(2,1)S(1)} %shard_map.64.refs_0_), channel_id=1, source_target_pairs={{0,1},{1,0},{2,3},{3,2},{4,5},{5,4},{6,7},{7,6},{8,9},{9,8},{10,11... | collective-permute-start | bytes 565256 | tf_op jit(solution)/shard_map/ppermute | solution.py:383
  32.1 6.3 %collective-permute-start.19 = (bf16[1440,128]{1,0:T(8,128)(2,1)S(1)}, bf16[1440,128]{1,0:T(8,128)(2,1)S(1)}, u32[]{:S(2)}, u32[]{:S(2)}) collective-permute-start(bf16[1440,128]{1,0:T(8,128)(2,1)S(1)} %get-tuple-element.76), channel_id=1, source_target_pairs={{0,1},{1,0},{2,3},{3,2},{4,5},{5,4},{6,7},{7,6},{8,9},{9,8},{10,11... | collective-permute-start | bytes 1105928 | tf_op jit(solution)/shard_map/ppermute | solution.py:291
  33.9 6.7 %collective-permute-start.21 = (bf16[720,128]{1,0:T(8,128)(2,1)S(1)}, bf16[720,128]{1,0:T(8,128)(2,1)S(1)}, u32[]{:S(2)}, u32[]{:S(2)}) collective-permute-start(bf16[720,128]{1,0:T(8,128)(2,1)S(1)} %fusion), channel_id=1, source_target_pairs={{0,4},{4,8},{8,12},{12,14},{14,10},{10,6},{6,2},{2,0},{1,5},{5,9},... | collective-permute-start | bytes 552968 | tf_op jit(solution)/shard_map/ppermute | solution.py:393
  35.7 6.9 %collective-permute-start.18 = (bf16[1440,128]{1,0:T(8,128)(2,1)S(1)}, bf16[1440,128]{1,0:T(8,128)(2,1)S(1)}, u32[]{:S(2)}, u32[]{:S(2)}) collective-permute-start(bf16[1440,128]{1,0:T(8,128)(2,1)S(1)} %get-tuple-element.74), channel_id=1, source_target_pairs={{0,1},{1,0},{2,3},{3,2},{4,5},{5,4},{6,7},{7,6},{8,9},{9,8},{10,11... | collective-permute-start | bytes 1105928 | tf_op jit(solution)/shard_map/ppermute | solution.py:388
  38.5 7.1 %collective-permute-start.20 = (bf16[720,128]{1,0:T(8,128)(2,1)S(1)}, bf16[720,128]{1,0:T(8,128)(2,1)S(1)}, u32[]{:S(2)}, u32[]{:S(2)}) collective-permute-start(bf16[720,128]{1,0:T(8,128)(2,1)S(1)} %add_convert_fusion.3), channel_id=1, source_target_pairs={{4,0},{8,4},{12,8},{14,12},{10,14},{6,10},{2,6},{0,2},{5,1},{9,5},... | collective-permute-start | bytes 552968 | tf_op jit(solution)/shard_map/ppermute | solution.py:400
  40.6 5.8 %collective-permute-start.23 = (bf16[720,128]{1,0:T(8,128)(2,1)S(1)}, bf16[720,128]{1,0:T(8,128)(2,1)S(1)}, u32[]{:S(2)}, u32[]{:S(2)}) collective-permute-start(bf16[720,128]{1,0:T(8,128)(2,1)S(1)} %add_convert_fusion.2), channel_id=1, source_target_pairs={{0,4},{4,8},{8,12},{12,14},{14,10},{10,6},{6,2},{2,0},{1,5},{5,9},... | collective-permute-start | bytes 552968 | tf_op jit(solution)/shard_map/ppermute | solution.py:393
  42.5 6.0 %collective-permute-start.17 = (bf16[1440,128]{1,0:T(8,128)(2,1)S(1)}, bf16[1440,128]{1,0:T(8,128)(2,1)S(1)}, u32[]{:S(2)}, u32[]{:S(2)}) collective-permute-start(bf16[1440,128]{1,0:T(8,128)(2,1)S(1)} %get-tuple-element.72), channel_id=1, source_target_pairs={{0,1},{1,0},{2,3},{3,2},{4,5},{5,4},{6,7},{7,6},{8,9},{9,8},{10,11... | collective-permute-start | bytes 1105928 | tf_op jit(solution)/shard_map/ppermute | solution.py:388
  45.7 6.3 %collective-permute-start.22 = (bf16[720,128]{1,0:T(8,128)(2,1)S(1)}, bf16[720,128]{1,0:T(8,128)(2,1)S(1)}, u32[]{:S(2)}, u32[]{:S(2)}) collective-permute-start(bf16[720,128]{1,0:T(8,128)(2,1)S(1)} %shard_map.73), channel_id=1, source_target_pairs={{4,0},{8,4},{12,8},{14,12},{10,14},{6,10},{2,6},{0,2},{5,1},{9,5},... | collective-permute-start | bytes 552968 | tf_op jit(solution)/shard_map/ppermute | solution.py:400
  46.6 5.8 %collective-permute-start.25 = (bf16[720,128]{1,0:T(8,128)(2,1)S(1)}, bf16[720,128]{1,0:T(8,128)(2,1)S(1)}, u32[]{:S(2)}, u32[]{:S(2)}) collective-permute-start(bf16[720,128]{1,0:T(8,128)(2,1)S(1)} %add_convert_fusion.1), channel_id=1, source_target_pairs={{0,4},{4,8},{8,12},{12,14},{14,10},{10,6},{6,2},{2,0},{1,5},{5,9},... | collective-permute-start | bytes 552968 | tf_op jit(solution)/shard_map/ppermute | solution.py:393
  48.4 9.3 %collective-permute-start.16 = (bf16[720,128]{1,0:T(8,128)(2,1)S(1)}, bf16[720,128]{1,0:T(8,128)(2,1)S(1)}, u32[]{:S(2)}, u32[]{:S(2)}) collective-permute-start(bf16[720,128]{1,0:T(8,128)(2,1)S(1)} %get-tuple-element.70), channel_id=1, source_target_pairs={{0,1},{1,0},{2,3},{3,2},{4,5},{5,4},{6,7},{7,6},{8,9},{9,8},{10,11... | collective-permute-start | bytes 552968 | tf_op jit(solution)/shard_map/ppermute | solution.py:396
  52.1 5.6 %collective-permute-start.24 = (bf16[720,128]{1,0:T(8,128)(2,1)S(1)}, bf16[720,128]{1,0:T(8,128)(2,1)S(1)}, u32[]{:S(2)}, u32[]{:S(2)}) collective-permute-start(bf16[720,128]{1,0:T(8,128)(2,1)S(1)} %shard_map.74), channel_id=1, source_target_pairs={{4,0},{8,4},{12,8},{14,12},{10,14},{6,10},{2,6},{0,2},{5,1},{9,5},... | collective-permute-start | bytes 552968 | tf_op jit(solution)/shard_map/ppermute | solution.py:400
  52.5 5.6 %collective-permute-start.26 = (bf16[720,128]{1,0:T(8,128)(2,1)S(1)}, bf16[720,128]{1,0:T(8,128)(2,1)S(1)}, u32[]{:S(2)}, u32[]{:S(2)}) collective-permute-start(bf16[720,128]{1,0:T(8,128)(2,1)S(1)} %add_convert_fusion), channel_id=1, source_target_pairs={{0,4},{4,8},{8,12},{12,14},{14,10},{10,6},{6,2},{2,0},{1,5},{5,9},... | collective-permute-start | bytes 552968 | tf_op jit(solution)/shard_map/ppermute | solution.py:393

commit v16 on v15

--- a/solution.py
+++ b/solution.py
@@ -223,18 +223,21 @@
 
 def second_kernel(n_blocks, n_experts, rows, place, *refs):
     own, across = refs[:n_blocks], refs[n_blocks : 2 * n_blocks]
-    gated, lifted, w_gate, w_up, down_theirs, hidden, *theirs, x = refs[2 * n_blocks :]
+    gated, lifted, w_gate, w_up, down_theirs, hidden, theirs, x = refs[2 * n_blocks :]
     half = x.shape[1]
     gather_rows(across, x, rows, half + SPLITS * n_experts)
     there = 1 - place[0]
     hidden[...] = activate(gated[...] + project(x, there, w_gate), lifted[...] + project(x, there, w_up))
-    lower(hidden[...], down_theirs, gate_weights(own, half, place[1], n_experts, rows), *theirs)
-
-
-def third_kernel(n_blocks, n_experts, rows, place, *refs):
-    own = refs[:n_blocks]
-    hidden, down_mine, *mine = refs[n_blocks:]
-    lower(hidden[...], down_mine, gate_weights(own, down_mine.shape[1], place[1], n_experts, rows), *mine)
+    lower(hidden[:rows], down_theirs, gate_weights(own[:1], half, place[1], n_experts, rows), theirs)
+
+
+def last_kernel(n_blocks, n_experts, rows, skipped, place, *refs):
+    own, hidden = refs[:n_blocks], refs[n_blocks]
+    after_downs = n_blocks + 1 + (len(refs) - n_blocks - 1) // 2
+    downs, outs = refs[n_blocks + 1 : after_downs], refs[after_downs:]
+    units = hidden[skipped * rows : (skipped + n_blocks) * rows]
+    for down, out in zip(downs, outs):
+        lower(units, down, gate_weights(own, down.shape[1], place[1], n_experts, rows), out)
 
 
 def call(kernel, place, args, out_shape, scratch_shapes, flops):
@@ -276,28 +279,34 @@
     n_blocks = len(own)
     rows, size = n_blocks * block_rows, tiles_of(block_rows, half)[-1]
     products = [in_vmem((padded(rows), hidden), jnp.float32)] * 2
-    outs = [in_vmem((size, 128)), in_vmem(((n_blocks - 1) * size, 128))]
     x = [pltpu.VMEM((padded(rows), half), jnp.bfloat16)]
     flops = 2 * padded(rows) * hidden * width
     gated, lifted = call(functools.partial(first_kernel, n_blocks, n_experts, block_rows), place, (*own, gate, up), products, x, flops)
-    units, *theirs = call(
+    units, theirs = call(
         functools.partial(second_kernel, n_blocks, n_experts, block_rows),
         place,
         (*own, *across, gated, lifted, gate, up, down_theirs),
-        [in_vmem((padded(rows), hidden)), *outs],
+        [in_vmem((padded(rows), hidden)), in_vmem((size, 128))],
         x,
         flops + flops // 2,
     )
-    theirs = [swap(a) for a in theirs]
-    mine = call(
-        functools.partial(third_kernel, n_blocks, n_experts, block_rows),
-        place,
-        (*own, units, down_mine),
-        outs,
-        [],
-        flops // 2,
-    )
-    return mine, theirs
+    theirs = swap(theirs)
+    (mine,) = call(
+        functools.partial(last_kernel, 1, n_experts, block_rows, 0), place, (own[0], units, down_mine), [in_vmem((size, 128))], [], flops // 6
+    )
+
+    def others(place):
+        rest = n_blocks - 1
+        return call(
+            functools.partial(last_kernel, rest, n_experts, block_rows, 1),
+            place,
+            (*own[1:], units, down_theirs, down_mine),
+            [in_vmem((rest * size, 128))] * 2,
+            [],
+            flops // 2,
+        )
+
+    return mine, theirs, others
 
 
 def add_kernel(*refs):
@@ -382,8 +391,11 @@
     across[far] = swap(came[far])
     across[0] = swap(after(packed, came[far]))
     last = [far, far - 1, 1 - far]
-    for keys, mine, theirs in zip(([far], last[1:]), *run_expert_in_stages(place, [came[k] for k in last], [across[k] for k in last], swap, weights, n, rows)):
-        keep(keys, mine, theirs)
+    mine, theirs, others = run_expert_in_stages(place, [came[k] for k in last], [across[k] for k in last], swap, weights, n, rows)
+    keep([far], mine, theirs)
+    theirs, mine = others(after(place, value[far]))
+    quarter = theirs.shape[0] // 4
+    keep(last[1:], mine, jnp.concatenate([swap(theirs[i * quarter : (i + 1) * quarter]) for i in range(4)], axis=0))
     for keys, mine, theirs in near:
         keep(keys, mine, swap(after(theirs, value[far])))
 

time: 59 us -> 61 us (1.034)
  Pallas kernels: 23.4 us -> 24.6 us
  starting transfers between devices: 19.2 us -> 20.3 us
    ppermute x4, waiting for transfers between devices: 2.56 us -> 0.55 us  [ring_body(): behind = lax.ppermute(to_ahead, 'ep', ahead)]
    ppermute x3, waiting for transfers between devices: 9.92 us -> 11.8 us  [ring_body(): front = lax.ppermute(to_back, 'ep', back)]
    pallas_call x6 -> x7, Pallas kernels: 13.5 us -> 14.6 us  [call(): pl.pallas_call(kernel, out_shape=out_shape, in_specs=[pl.BlockSpec(memory...]
    ppermute x2 -> x5, starting transfers between devices: 0.95 us -> 1.37 us  [the longest x4 1.09 us: ring_body(): swap(theirs[i * quarter:(i + 1) * quarter])]
  transfers between devices with their start and end apart: 27 -> 30, of which waited for: 10 -> 8; matrix products, arithmetic and copies ran while one was open for 1% -> 1% of each run, Pallas kernels for 33% -> 34%
where the time goes in v16:
time: 61 us; the launch traced here: 60.8 us
  Pallas kernels  24.6 us (40%)
  starting transfers between devices  20.3 us (33%)
  waiting for transfers between devices  15.2 us (25%)
    pallas_call x7, Pallas kernels, call(): pl.pallas_call(kernel, out_shape=out_shape, in_specs=[pl.BlockSpec(memory...  14.6 us
    ppermute x3, waiting for transfers between devices, ring_body(): front = lax.ppermute(to_back, 'ep', back)  11.8 us
    ppermute x4, starting transfers between devices, ring_body(): behind = lax.ppermute(to_ahead, 'ep', ahead)  6.94 us
    ppermute x3, starting transfers between devices, ring_body(): came[k] = lax.ppermute(came[k - 1], 'ep', ahead)  5.64 us
    pallas_call x1, Pallas kernels, turn_weights(): pl.pallas_call(turn_kernel, out_shape=[in_vmem((width, hidden))] * 2, in_...  4.79 us
    pallas_call x1, Pallas kernels, halve_weights(): pl.pallas_call(halve_kernel, out_shape=[in_vmem((hidden, width // 2))] *...  3.13 us
    ppermute x1, starting transfers between devices, ring_body(): came[1] = lax.ppermute(packed, 'ep', ahead)  3.08 us
    ppermute x3, waiting for transfers between devices, ring_body(): came[k] = lax.ppermute(came[k - 1], 'ep', ahead)  2.13 us
  transfers between devices with their start and end apart: 30, of which 8 were waited for; matrix products, arithmetic and copies ran while one was open for 1% of the time, Pallas kernels for 34%

profile of v16, /device:TPU:0, one launch (start us, length us, event | category | flops | bytes accessed | tf_op | source)
XLA Modules:
  0.0 60.8 jit_solution(820455012218953122)
XLA Ops:
  0.0 1.1 %shard_map.64.refs_0_ = bf16[736,128]{1,0:T(8,128)(2,1)S(1)} custom-call(bf16[64,1440]{1,0:T(8,128)(2,1)} %tokens_in.1, s32[4,64]{1,0:T(4,128)} %bitcast.14, f32[4,64]{1,0:T(4,128)} %bitcast.15), custom_call_target="tpu_custom_call" | custom-call | tf_op jit(solution)/shard_map/pallas_call | solution.py:76
  1.1 3.1 %collective-permute-start = (bf16[736,128]{1,0:T(8,128)(2,1)S(1)}, bf16[736,128]{1,0:T(8,128)(2,1)S(1)}, u32[]{:S(2)}, u32[]{:S(2)}) collective-permute-start(bf16[736,128]{1,0:T(8,128)(2,1)S(1)} %shard_map.64.refs_0_), channel_id=1, source_target_pairs={{0,4},{4,8},{8,12},{12,14},{14,10},{10,6},{6,2},{2,0},{1,5},{5,9},... | collective-permute-start | bytes 565256 | tf_op jit(solution)/shard_map/ppermute | solution.py:375
  4.2 0.0 collective-permute-start.3
  4.2 0.1 pad_add_fusion.after_this.place
  4.3 4.8 %shard_map.65 = (bf16[2880,720]{1,0:T(8,128)(2,1)S(1)}, bf16[2880,720]{1,0:T(8,128)(2,1)S(1)}) custom-call(s32[2]{0:T(128)S(1)} %pad_add_fusion.after_this.place, bf16[720,2880]{1,0:T(8,128)(2,1)} %bitcast.11, bf16[720,2880]{1,0:T(8,128)(2,1)} %bitcast.12), custom_call_target="tpu_custom_call" | custom-call | bytes 16588800 | tf_op jit(solution)/shard_map/pallas_call | solution.py:106
  9.1 0.0 collective-permute-done.refs_0_
  9.1 2.1 %collective-permute-start.1 = (bf16[736,128]{1,0:T(8,128)(2,1)S(1)}, bf16[736,128]{1,0:T(8,128)(2,1)S(1)}, u32[]{:S(2)}, u32[]{:S(2)}) collective-permute-start(bf16[736,128]{1,0:T(8,128)(2,1)S(1)} %collective-permute-done.refs_0_), channel_id=1, source_target_pairs={{0,4},{4,8},{8,12},{12,14},{14,10},{10,6},{6,2},{2,0},{1,5},{5,9},... | collective-permute-start | bytes 565256 | tf_op jit(solution)/shard_map/ppermute | solution.py:380
  11.1 0.0 collective-permute-start.7
  11.1 0.0 collective-permute-start.4
  11.2 0.5 collective-permute-start.5
  11.7 3.1 %shard_map.66 = (bf16[720,1440]{1,0:T(8,128)(2,1)S(1)}, bf16[720,1440]{1,0:T(8,128)(2,1)S(1)}) custom-call(s32[2]{0:T(128)S(1)} %pad_add_fusion.after_this.place, bf16[720,2880]{1,0:T(8,128)(2,1)} %bitcast.13), custom_call_target="tpu_custom_call" | custom-call | bytes 16588800 | tf_op jit(solution)/shard_map/pallas_call | solution.py:143
  14.8 0.5 collective-permute-done.1.refs_0_
  15.3 1.7 %collective-permute-start.2 = (bf16[736,128]{1,0:T(8,128)(2,1)S(1)}, bf16[736,128]{1,0:T(8,128)(2,1)S(1)}, u32[]{:S(2)}, u32[]{:S(2)}) collective-permute-start(bf16[736,128]{1,0:T(8,128)(2,1)S(1)} %collective-permute-done.1.refs_0_), channel_id=1, source_target_pairs={{0,4},{4,8},{8,12},{12,14},{14,10},{10,6},{6,2},{2,0},{1,5},{5,9},... | collective-permute-start | bytes 565256 | tf_op jit(solution)/shard_map/ppermute | solution.py:380
  17.0 0.0 collective-permute-start.8
  17.0 0.0 collective-permute-done.7.refs_1_
  17.1 0.3 collective-permute-start.10
  17.3 0.0 collective-permute-done.4.refs_2_
  17.3 0.3 collective-permute-start.9
  17.6 0.0 collective-permute-done.5.refs_3_
  17.6 2.8 %shard_map.67 = (bf16[1440,128]{1,0:T(8,128)(2,1)S(1)}, bf16[1440,128]{1,0:T(8,128)(2,1)S(1)}) custom-call(s32[2]{0:T(128)S(1)} %pad_add_fusion.after_this.place, bf16[736,128]{1,0:T(8,128)(2,1)S(1)} %collective-permute-done.refs_0_, bf16[736,128]{1,0:T(8,128)(2,1)S(1)} %collective-permute-done.3.refs_1_, ...), custom_call_target="tpu_custom_call" | custom-call | flops 1592524800 | bytes 12441600 | tf_op jit(solution)/shard_map/pallas_call | solution.py:245
  20.4 1.3 %collective-permute-done.2.refs_1_.refs_0_ = bf16[736,128]{1,0:T(8,128)(2,1)S(1)} collective-permute-done((bf16[736,128]{1,0:T(8,128)(2,1)S(1)}, bf16[736,128]{1,0:T(8,128)(2,1)S(1)}, u32[]{:S(2)}, u32[]{:S(2)}) %collective-permute-start.2) | collective-permute-done | bytes 188448 | tf_op jit(solution)/shard_map/ppermute | solution.py:380
  21.7 1.8 %collective-permute-start.6 = (bf16[736,128]{1,0:T(8,128)(2,1)S(1)}, bf16[736,128]{1,0:T(8,128)(2,1)S(1)}, u32[]{:S(2)}, u32[]{:S(2)}) collective-permute-start(bf16[736,128]{1,0:T(8,128)(2,1)S(1)} %collective-permute-done.2.refs_1_.refs_0_), channel_id=1, source_target_pairs={{0,4},{4,8},{8,12},{12,14},{14,10},{10,6},{6,2},{2,0},{1,5},{5,9},... | collective-permute-start | bytes 565256 | tf_op jit(solution)/shard_map/ppermute | solution.py:380
  23.5 0.7 %collective-permute-done.10.refs_2_.refs_1_ = bf16[736,128]{1,0:T(8,128)(2,1)S(1)} collective-permute-done((bf16[736,128]{1,0:T(8,128)(2,1)S(1)}, bf16[736,128]{1,0:T(8,128)(2,1)S(1)}, u32[]{:S(2)}, u32[]{:S(2)}) %collective-permute-start.10) | collective-permute-done | bytes 188448 | tf_op jit(solution)/shard_map/ppermute | solution.py:382
  24.2 2.8 %shard_map.68 = (bf16[1440,128]{1,0:T(8,128)(2,1)S(1)}, bf16[1440,128]{1,0:T(8,128)(2,1)S(1)}) custom-call(s32[2]{0:T(128)S(1)} %pad_add_fusion.after_this.place, bf16[736,128]{1,0:T(8,128)(2,1)S(1)} %collective-permute-done.1.refs_0_, bf16[736,128]{1,0:T(8,128)(2,1)S(1)} %collective-permute-done.7.refs_1_, ...), custom_call_target="tpu_custom_call" | custom-call | flops 1592524800 | bytes 12441600 | tf_op jit(solution)/shard_map/pallas_call | solution.py:245
  27.0 0.3 collective-permute-done.6.refs_0_
  27.3 0.2 collective-permute-start.11
  27.6 1.7 %shard_map.69 = (f32[192,720]{1,0:T(8,128)S(1)}, f32[192,720]{1,0:T(8,128)S(1)}) custom-call(s32[2]{0:T(128)S(1)} %pad_add_fusion.after_this.place, bf16[736,128]{1,0:T(8,128)(2,1)S(1)} %collective-permute-done.6.refs_0_, bf16[736,128]{1,0:T(8,128)(2,1)S(1)} %collective-permute-done.2.refs_1_.refs_0_, ...), custom_call_target="tpu_custom_call" | custom-call | flops 796262400 | bytes 6220800 | tf_op jit(solution)/shard_map/pallas_call | solution.py:245
  29.2 0.0 collective-permute-done.12.refs_4_
  29.2 0.0 collective-permute-done.11.refs_3_
  29.2 2.2 %shard_map.70 = (bf16[192,720]{1,0:T(8,128)(2,1)S(1)}, bf16[720,128]{1,0:T(8,128)(2,1)S(1)}) custom-call(s32[2]{0:T(128)S(1)} %pad_add_fusion.after_this.place, bf16[736,128]{1,0:T(8,128)(2,1)S(1)} %collective-permute-done.6.refs_0_, bf16[736,128]{1,0:T(8,128)(2,1)S(1)} %collective-permute-done.2.refs_1_.refs_0_, ...), custom_call_target="tpu_custom_call" | custom-call | flops 1194393600 | bytes 9331200 | tf_op jit(solution)/shard_map/pallas_call | solution.py:245
  31.4 0.3 collective-permute-start.14
  31.7 0.2 collective-permute-start.15
  31.9 1.1 %shard_map.71 = bf16[720,128]{1,0:T(8,128)(2,1)S(1)} custom-call(s32[2]{0:T(128)S(1)} %pad_add_fusion.after_this.place, bf16[736,128]{1,0:T(8,128)(2,1)S(1)} %collective-permute-done.6.refs_0_, bf16[192,720]{1,0:T(8,128)(2,1)S(1)} %get-tuple-element.64.refs_1_.refs_2_, bf16[720,1440]{1,0:T(8,128)(2,1)S(1)} %get-tuple-element.55.refs_6_.refs_2_.refs_4_), custom_call_target="tpu_custom_call" | custom-call | flops 132710400 | bytes 1036800 | tf_op jit(solution)/shard_map/pallas_call | solution.py:245
  33.1 0.1 fusion
  33.1 1.9 %collective-permute-start.24 = (bf16[720,128]{1,0:T(8,128)(2,1)S(1)}, bf16[720,128]{1,0:T(8,128)(2,1)S(1)}, u32[]{:S(2)}, u32[]{:S(2)}) collective-permute-start(bf16[720,128]{1,0:T(8,128)(2,1)S(1)} %fusion), channel_id=1, source_target_pairs={{0,4},{4,8},{8,12},{12,14},{14,10},{10,6},{6,2},{2,0},{1,5},{5,9},... | collective-permute-start | bytes 552968 | tf_op jit(solution)/shard_map/ppermute | solution.py:405
  35.0 1.4 %shard_map.73 = (bf16[1440,128]{1,0:T(8,128)(2,1)S(1)}, bf16[1440,128]{1,0:T(8,128)(2,1)S(1)}) custom-call(s32[2]{0:T(128)S(1)} %pad_add_fusion.after_this.place, bf16[736,128]{1,0:T(8,128)(2,1)S(1)} %collective-permute-done.2.refs_1_.refs_0_, bf16[736,128]{1,0:T(8,128)(2,1)S(1)} %collective-permute-done.10.refs_2_.refs_1_, ...), custom_call_target="tpu_custom_call" | custom-call | flops 398131200 | bytes 3110400 | tf_op jit(solution)/shard_map/pallas_call | solution.py:245
  36.4 0.2 collective-permute-start.19
  36.7 0.3 collective-permute-start.20
  37.0 0.2 collective-permute-start.22
  37.2 0.0 collective-permute-done.15.refs_1_
  37.2 0.3 collective-permute-start.23
  37.5 2.7 %shard_map.72 = (bf16[720,128]{1,0:T(8,128)(2,1)S(1)}, bf16[720,128]{1,0:T(8,128)(2,1)S(1)}) custom-call(s32[2]{0:T(128)S(1)} %pad_add_fusion.after_this.place, bf16[736,128]{1,0:T(8,128)(2,1)S(1)} %shard_map.64.refs_0_, bf16[736,128]{1,0:T(8,128)(2,1)S(1)} %collective-permute-done.15.refs_1_, ...), custom_call_target="tpu_custom_call" | custom-call | flops 1592524800 | bytes 12441600 | tf_op jit(solution)/shard_map/pallas_call | solution.py:245
  40.3 0.0 collective-permute-done.19
  40.3 0.2 collective-permute-start.18
  40.5 0.1 add_convert_fusion.3
  40.6 0.3 collective-permute-start.21
  41.0 0.1 add_convert_fusion.2
  41.0 1.8 %collective-permute-start.26 = (bf16[720,128]{1,0:T(8,128)(2,1)S(1)}, bf16[720,128]{1,0:T(8,128)(2,1)S(1)}, u32[]{:S(2)}, u32[]{:S(2)}) collective-permute-start(bf16[720,128]{1,0:T(8,128)(2,1)S(1)} %add_convert_fusion.2), channel_id=1, source_target_pairs={{0,4},{4,8},{8,12},{12,14},{14,10},{10,6},{6,2},{2,0},{1,5},{5,9},... | collective-permute-start | bytes 552968 | tf_op jit(solution)/shard_map/ppermute | solution.py:405
  42.8 0.1 collective-permute-start.17
  42.9 4.6 %collective-permute-done.21.refs_2_ = bf16[720,128]{1,0:T(8,128)(2,1)S(1)} collective-permute-done((bf16[720,128]{1,0:T(8,128)(2,1)S(1)}, bf16[720,128]{1,0:T(8,128)(2,1)S(1)}, u32[]{:S(2)}, u32[]{:S(2)}) %collective-permute-start.21) | collective-permute-done | bytes 184352 | tf_op jit(solution)/shard_map/ppermute | solution.py:412
  47.6 0.1 shard_map.74
  47.7 0.4 collective-permute-start.25
  48.1 0.1 add_convert_fusion.1
  48.2 1.7 %collective-permute-start.28 = (bf16[720,128]{1,0:T(8,128)(2,1)S(1)}, bf16[720,128]{1,0:T(8,128)(2,1)S(1)}, u32[]{:S(2)}, u32[]{:S(2)}) collective-permute-start(bf16[720,128]{1,0:T(8,128)(2,1)S(1)} %add_convert_fusion.1), channel_id=1, source_target_pairs={{0,4},{4,8},{8,12},{12,14},{14,10},{10,6},{6,2},{2,0},{1,5},{5,9},... | collective-permute-start | bytes 552968 | tf_op jit(solution)/shard_map/ppermute | solution.py:405
  49.9 0.1 collective-permute-start.16
  50.0 3.8 %collective-permute-done.25.refs_2_ = bf16[720,128]{1,0:T(8,128)(2,1)S(1)} collective-permute-done((bf16[720,128]{1,0:T(8,128)(2,1)S(1)}, bf16[720,128]{1,0:T(8,128)(2,1)S(1)}, u32[]{:S(2)}, u32[]{:S(2)}) %collective-permute-start.25) | collective-permute-done | bytes 184352 | tf_op jit(solution)/shard_map/ppermute | solution.py:412
  53.8 0.1 shard_map.75
  53.9 0.5 collective-permute-start.27
  54.4 0.1 add_convert_fusion
  54.5 1.6 %collective-permute-start.29 = (bf16[720,128]{1,0:T(8,128)(2,1)S(1)}, bf16[720,128]{1,0:T(8,128)(2,1)S(1)}, u32[]{:S(2)}, u32[]{:S(2)}) collective-permute-start(bf16[720,128]{1,0:T(8,128)(2,1)S(1)} %add_convert_fusion), channel_id=1, source_target_pairs={{0,4},{4,8},{8,12},{12,14},{14,10},{10,6},{6,2},{2,0},{1,5},{5,9},... | collective-permute-start | bytes 552968 | tf_op jit(solution)/shard_map/ppermute | solution.py:405
  56.1 3.4 %collective-permute-done.27.refs_2_ = bf16[720,128]{1,0:T(8,128)(2,1)S(1)} collective-permute-done((bf16[720,128]{1,0:T(8,128)(2,1)S(1)}, bf16[720,128]{1,0:T(8,128)(2,1)S(1)}, u32[]{:S(2)}, u32[]{:S(2)}) %collective-permute-start.27) | collective-permute-done | bytes 184352 | tf_op jit(solution)/shard_map/ppermute | solution.py:412
  59.5 0.1 shard_map.76.a
  59.5 0.5 collective-permute-done.29.b
  60.1 0.8 %shard_map.77 = bf16[64,1440]{1,0:T(8,128)(2,1)} custom-call(bf16[720,128]{1,0:T(8,128)(2,1)S(1)} %shard_map.76.a, bf16[720,128]{1,0:T(8,128)(2,1)S(1)} %collective-permute-done.29.b), custom_call_target="tpu_custom_call" | custom-call | tf_op jit(solution)/shard_map/pallas_call | solution.py:337
  (22 shorter events, 0.1 us)
Async XLA Ops:
  1.1 8.0 %collective-permute-start = (bf16[736,128]{1,0:T(8,128)(2,1)S(1)}, bf16[736,128]{1,0:T(8,128)(2,1)S(1)}, u32[]{:S(2)}, u32[]{:S(2)}) collective-permute-start(bf16[736,128]{1,0:T(8,128)(2,1)S(1)} %shard_map.64.refs_0_), channel_id=1, source_target_pairs={{0,4},{4,8},{8,12},{12,14},{14,10},{10,6},{6,2},{2,0},{1,5},{5,9},... | collective-permute-start | bytes 565256 | tf_op jit(solution)/shard_map/ppermute | solution.py:375
  4.2 7.0 %collective-permute-start.3 = (bf16[736,128]{1,0:T(8,128)(2,1)S(1)}, bf16[736,128]{1,0:T(8,128)(2,1)S(1)}, u32[]{:S(2)}, u32[]{:S(2)}) collective-permute-start(bf16[736,128]{1,0:T(8,128)(2,1)S(1)} %shard_map.64.refs_0_), channel_id=1, source_target_pairs={{4,0},{8,4},{12,8},{14,12},{10,14},{6,10},{2,6},{0,2},{5,1},{9,5},... | collective-permute-start | bytes 565256 | tf_op jit(solution)/shard_map/ppermute | solution.py:376
  9.1 6.2 %collective-permute-start.1 = (bf16[736,128]{1,0:T(8,128)(2,1)S(1)}, bf16[736,128]{1,0:T(8,128)(2,1)S(1)}, u32[]{:S(2)}, u32[]{:S(2)}) collective-permute-start(bf16[736,128]{1,0:T(8,128)(2,1)S(1)} %collective-permute-done.refs_0_), channel_id=1, source_target_pairs={{0,4},{4,8},{8,12},{12,14},{14,10},{10,6},{6,2},{2,0},{1,5},{5,9},... | collective-permute-start | bytes 565256 | tf_op jit(solution)/shard_map/ppermute | solution.py:380
  11.1 5.9 %collective-permute-start.7 = (bf16[736,128]{1,0:T(8,128)(2,1)S(1)}, bf16[736,128]{1,0:T(8,128)(2,1)S(1)}, u32[]{:S(2)}, u32[]{:S(2)}) collective-permute-start(bf16[736,128]{1,0:T(8,128)(2,1)S(1)} %collective-permute-done.3.refs_1_), channel_id=1, source_target_pairs={{4,0},{8,4},{12,8},{14,12},{10,14},{6,10},{2,6},{0,2},{5,1},{9,5},... | collective-permute-start | bytes 565256 | tf_op jit(solution)/shard_map/ppermute | solution.py:382
  11.1 6.2 %collective-permute-start.4 = (bf16[736,128]{1,0:T(8,128)(2,1)S(1)}, bf16[736,128]{1,0:T(8,128)(2,1)S(1)}, u32[]{:S(2)}, u32[]{:S(2)}) collective-permute-start(bf16[736,128]{1,0:T(8,128)(2,1)S(1)} %collective-permute-done.refs_0_), channel_id=1, source_target_pairs={{0,1},{1,0},{2,3},{3,2},{4,5},{5,4},{6,7},{7,6},{8,9},{9,8},{10,11... | collective-permute-start | bytes 565256 | tf_op jit(solution)/shard_map/ppermute | solution.py:383
  11.2 6.5 %collective-permute-start.5 = (bf16[736,128]{1,0:T(8,128)(2,1)S(1)}, bf16[736,128]{1,0:T(8,128)(2,1)S(1)}, u32[]{:S(2)}, u32[]{:S(2)}) collective-permute-start(bf16[736,128]{1,0:T(8,128)(2,1)S(1)} %collective-permute-done.3.refs_1_), channel_id=1, source_target_pairs={{0,1},{1,0},{2,3},{3,2},{4,5},{5,4},{6,7},{7,6},{8,9},{9,8},{10,11... | collective-permute-start | bytes 565256 | tf_op jit(solution)/shard_map/ppermute | solution.py:383
  15.3 6.4 %collective-permute-start.2 = (bf16[736,128]{1,0:T(8,128)(2,1)S(1)}, bf16[736,128]{1,0:T(8,128)(2,1)S(1)}, u32[]{:S(2)}, u32[]{:S(2)}) collective-permute-start(bf16[736,128]{1,0:T(8,128)(2,1)S(1)} %collective-permute-done.1.refs_0_), channel_id=1, source_target_pairs={{0,4},{4,8},{8,12},{12,14},{14,10},{10,6},{6,2},{2,0},{1,5},{5,9},... | collective-permute-start | bytes 565256 | tf_op jit(solution)/shard_map/ppermute | solution.py:380
  17.0 7.2 %collective-permute-start.8 = (bf16[736,128]{1,0:T(8,128)(2,1)S(1)}, bf16[736,128]{1,0:T(8,128)(2,1)S(1)}, u32[]{:S(2)}, u32[]{:S(2)}) collective-permute-start(bf16[736,128]{1,0:T(8,128)(2,1)S(1)} %collective-permute-done.1.refs_0_), channel_id=1, source_target_pairs={{0,1},{1,0},{2,3},{3,2},{4,5},{5,4},{6,7},{7,6},{8,9},{9,8},{10,11... | collective-permute-start | bytes 565256 | tf_op jit(solution)/shard_map/ppermute | solution.py:383
  17.1 7.1 %collective-permute-start.10 = (bf16[736,128]{1,0:T(8,128)(2,1)S(1)}, bf16[736,128]{1,0:T(8,128)(2,1)S(1)}, u32[]{:S(2)}, u32[]{:S(2)}) collective-permute-start(bf16[736,128]{1,0:T(8,128)(2,1)S(1)} %collective-permute-done.7.refs_1_), channel_id=1, source_target_pairs={{4,0},{8,4},{12,8},{14,12},{10,14},{6,10},{2,6},{0,2},{5,1},{9,5},... | collective-permute-start | bytes 565256 | tf_op jit(solution)/shard_map/ppermute | solution.py:382
  17.3 6.9 %collective-permute-start.9 = (bf16[736,128]{1,0:T(8,128)(2,1)S(1)}, bf16[736,128]{1,0:T(8,128)(2,1)S(1)}, u32[]{:S(2)}, u32[]{:S(2)}) collective-permute-start(bf16[736,128]{1,0:T(8,128)(2,1)S(1)} %collective-permute-done.7.refs_1_), channel_id=1, source_target_pairs={{0,1},{1,0},{2,3},{3,2},{4,5},{5,4},{6,7},{7,6},{8,9},{9,8},{10,11... | collective-permute-start | bytes 565256 | tf_op jit(solution)/shard_map/ppermute | solution.py:383
  21.7 5.6 %collective-permute-start.6 = (bf16[736,128]{1,0:T(8,128)(2,1)S(1)}, bf16[736,128]{1,0:T(8,128)(2,1)S(1)}, u32[]{:S(2)}, u32[]{:S(2)}) collective-permute-start(bf16[736,128]{1,0:T(8,128)(2,1)S(1)} %collective-permute-done.2.refs_1_.refs_0_), channel_id=1, source_target_pairs={{0,4},{4,8},{8,12},{12,14},{14,10},{10,6},{6,2},{2,0},{1,5},{5,9},... | collective-permute-start | bytes 565256 | tf_op jit(solution)/shard_map/ppermute | solution.py:380
  23.5 5.7 %collective-permute-start.12 = (bf16[736,128]{1,0:T(8,128)(2,1)S(1)}, bf16[736,128]{1,0:T(8,128)(2,1)S(1)}, u32[]{:S(2)}, u32[]{:S(2)}) collective-permute-start(bf16[736,128]{1,0:T(8,128)(2,1)S(1)} %collective-permute-done.2.refs_1_.refs_0_), channel_id=1, source_target_pairs={{0,1},{1,0},{2,3},{3,2},{4,5},{5,4},{6,7},{7,6},{8,9},{9,8},{10,11... | collective-permute-start | bytes 565256 | tf_op jit(solution)/shard_map/ppermute | solution.py:383
  24.2 5.0 %collective-permute-start.13 = (bf16[736,128]{1,0:T(8,128)(2,1)S(1)}, bf16[736,128]{1,0:T(8,128)(2,1)S(1)}, u32[]{:S(2)}, u32[]{:S(2)}) collective-permute-start(bf16[736,128]{1,0:T(8,128)(2,1)S(1)} %collective-permute-done.10.refs_2_.refs_1_), channel_id=1, source_target_pairs={{0,1},{1,0},{2,3},{3,2},{4,5},{5,4},{6,7},{7,6},{8,9},{9,8},{10,11... | collective-permute-start | bytes 565256 | tf_op jit(solution)/shard_map/ppermute | solution.py:383
  27.3 1.9 %collective-permute-start.11 = (bf16[736,128]{1,0:T(8,128)(2,1)S(1)}, bf16[736,128]{1,0:T(8,128)(2,1)S(1)}, u32[]{:S(2)}, u32[]{:S(2)}) collective-permute-start(bf16[736,128]{1,0:T(8,128)(2,1)S(1)} %collective-permute-done.6.refs_0_), channel_id=1, source_target_pairs={{0,1},{1,0},{2,3},{3,2},{4,5},{5,4},{6,7},{7,6},{8,9},{9,8},{10,11... | collective-permute-start | bytes 565256 | tf_op jit(solution)/shard_map/ppermute | solution.py:391
  31.4 1.6 %collective-permute-start.14 = (bf16[720,128]{1,0:T(8,128)(2,1)S(1)}, bf16[720,128]{1,0:T(8,128)(2,1)S(1)}, u32[]{:S(2)}, u32[]{:S(2)}) collective-permute-start(bf16[720,128]{1,0:T(8,128)(2,1)S(1)} %get-tuple-element.65), channel_id=1, source_target_pairs={{0,1},{1,0},{2,3},{3,2},{4,5},{5,4},{6,7},{7,6},{8,9},{9,8},{10,11... | collective-permute-start | bytes 552968 | tf_op jit(solution)/shard_map/ppermute | solution.py:293
  31.7 5.5 %collective-permute-start.15 = (bf16[736,128]{1,0:T(8,128)(2,1)S(1)}, bf16[736,128]{1,0:T(8,128)(2,1)S(1)}, u32[]{:S(2)}, u32[]{:S(2)}) collective-permute-start(bf16[736,128]{1,0:T(8,128)(2,1)S(1)} %shard_map.64.refs_0_), channel_id=1, source_target_pairs={{0,1},{1,0},{2,3},{3,2},{4,5},{5,4},{6,7},{7,6},{8,9},{9,8},{10,11... | collective-permute-start | bytes 565256 | tf_op jit(solution)/shard_map/ppermute | solution.py:392
  33.1 7.8 %collective-permute-start.24 = (bf16[720,128]{1,0:T(8,128)(2,1)S(1)}, bf16[720,128]{1,0:T(8,128)(2,1)S(1)}, u32[]{:S(2)}, u32[]{:S(2)}) collective-permute-start(bf16[720,128]{1,0:T(8,128)(2,1)S(1)} %fusion), channel_id=1, source_target_pairs={{0,4},{4,8},{8,12},{12,14},{14,10},{10,6},{6,2},{2,0},{1,5},{5,9},... | collective-permute-start | bytes 552968 | tf_op jit(solution)/shard_map/ppermute | solution.py:405
  36.4 3.8 %collective-permute-start.19 = (bf16[360,128]{1,0:T(8,128)(2,1)S(1)}, bf16[360,128]{1,0:T(8,128)(2,1)S(1)}, u32[]{:S(2)}, u32[]{:S(2)}) collective-permute-start(bf16[360,128]{1,0:T(8,128)(2,1)S(1)} %get-tuple-element.92), channel_id=1, source_target_pairs={{0,1},{1,0},{2,3},{3,2},{4,5},{5,4},{6,7},{7,6},{8,9},{9,8},{10,11... | collective-permute-start | bytes 276488 | tf_op jit(solution)/shard_map/ppermute | solution.py:398
  36.7 3.8 %collective-permute-start.20 = (bf16[360,128]{1,0:T(8,128)(2,1)S(1)}, bf16[360,128]{1,0:T(8,128)(2,1)S(1)}, u32[]{:S(2)}, u32[]{:S(2)}) collective-permute-start(bf16[360,128]{1,0:T(8,128)(2,1)S(1)} %get-tuple-element.91), channel_id=1, source_target_pairs={{0,1},{1,0},{2,3},{3,2},{4,5},{5,4},{6,7},{7,6},{8,9},{9,8},{10,11... | collective-permute-start | bytes 276488 | tf_op jit(solution)/shard_map/ppermute | solution.py:398
  37.0 3.5 %collective-permute-start.22 = (bf16[360,128]{1,0:T(8,128)(2,1)S(1)}, bf16[360,128]{1,0:T(8,128)(2,1)S(1)}, u32[]{:S(2)}, u32[]{:S(2)}) collective-permute-start(bf16[360,128]{1,0:T(8,128)(2,1)S(1)} %get-tuple-element.89), channel_id=1, source_target_pairs={{0,1},{1,0},{2,3},{3,2},{4,5},{5,4},{6,7},{7,6},{8,9},{9,8},{10,11... | collective-permute-start | bytes 276488 | tf_op jit(solution)/shard_map/ppermute | solution.py:398
  37.2 3.3 %collective-permute-start.23 = (bf16[360,128]{1,0:T(8,128)(2,1)S(1)}, bf16[360,128]{1,0:T(8,128)(2,1)S(1)}, u32[]{:S(2)}, u32[]{:S(2)}) collective-permute-start(bf16[360,128]{1,0:T(8,128)(2,1)S(1)} %get-tuple-element.90), channel_id=1, source_target_pairs={{0,1},{1,0},{2,3},{3,2},{4,5},{5,4},{6,7},{7,6},{8,9},{9,8},{10,11... | collective-permute-start | bytes 276488 | tf_op jit(solution)/shard_map/ppermute | solution.py:398
  40.3 7.3 %collective-permute-start.18 = (bf16[1440,128]{1,0:T(8,128)(2,1)S(1)}, bf16[1440,128]{1,0:T(8,128)(2,1)S(1)}, u32[]{:S(2)}, u32[]{:S(2)}) collective-permute-start(bf16[1440,128]{1,0:T(8,128)(2,1)S(1)} %get-tuple-element.73), channel_id=1, source_target_pairs={{0,1},{1,0},{2,3},{3,2},{4,5},{5,4},{6,7},{7,6},{8,9},{9,8},{10,11... | collective-permute-start | bytes 1105928 | tf_op jit(solution)/shard_map/ppermute | solution.py:400
  40.6 6.9 %collective-permute-start.21 = (bf16[720,128]{1,0:T(8,128)(2,1)S(1)}, bf16[720,128]{1,0:T(8,128)(2,1)S(1)}, u32[]{:S(2)}, u32[]{:S(2)}) collective-permute-start(bf16[720,128]{1,0:T(8,128)(2,1)S(1)} %add_convert_fusion.3), channel_id=1, source_target_pairs={{4,0},{8,4},{12,8},{14,12},{10,14},{6,10},{2,6},{0,2},{5,1},{9,5},... | collective-permute-start | bytes 552968 | tf_op jit(solution)/shard_map/ppermute | solution.py:412
  41.0 7.1 %collective-permute-start.26 = (bf16[720,128]{1,0:T(8,128)(2,1)S(1)}, bf16[720,128]{1,0:T(8,128)(2,1)S(1)}, u32[]{:S(2)}, u32[]{:S(2)}) collective-permute-start(bf16[720,128]{1,0:T(8,128)(2,1)S(1)} %add_convert_fusion.2), channel_id=1, source_target_pairs={{0,4},{4,8},{8,12},{12,14},{14,10},{10,6},{6,2},{2,0},{1,5},{5,9},... | collective-permute-start | bytes 552968 | tf_op jit(solution)/shard_map/ppermute | solution.py:405
  42.8 7.1 %collective-permute-start.17 = (bf16[1440,128]{1,0:T(8,128)(2,1)S(1)}, bf16[1440,128]{1,0:T(8,128)(2,1)S(1)}, u32[]{:S(2)}, u32[]{:S(2)}) collective-permute-start(bf16[1440,128]{1,0:T(8,128)(2,1)S(1)} %get-tuple-element.71), channel_id=1, source_target_pairs={{0,1},{1,0},{2,3},{3,2},{4,5},{5,4},{6,7},{7,6},{8,9},{9,8},{10,11... | collective-permute-start | bytes 1105928 | tf_op jit(solution)/shard_map/ppermute | solution.py:400
  47.7 6.1 %collective-permute-start.25 = (bf16[720,128]{1,0:T(8,128)(2,1)S(1)}, bf16[720,128]{1,0:T(8,128)(2,1)S(1)}, u32[]{:S(2)}, u32[]{:S(2)}) collective-permute-start(bf16[720,128]{1,0:T(8,128)(2,1)S(1)} %shard_map.74), channel_id=1, source_target_pairs={{4,0},{8,4},{12,8},{14,12},{10,14},{6,10},{2,6},{0,2},{5,1},{9,5},... | collective-permute-start | bytes 552968 | tf_op jit(solution)/shard_map/ppermute | solution.py:412
  48.2 6.2 %collective-permute-start.28 = (bf16[720,128]{1,0:T(8,128)(2,1)S(1)}, bf16[720,128]{1,0:T(8,128)(2,1)S(1)}, u32[]{:S(2)}, u32[]{:S(2)}) collective-permute-start(bf16[720,128]{1,0:T(8,128)(2,1)S(1)} %add_convert_fusion.1), channel_id=1, source_target_pairs={{0,4},{4,8},{8,12},{12,14},{14,10},{10,6},{6,2},{2,0},{1,5},{5,9},... | collective-permute-start | bytes 552968 | tf_op jit(solution)/shard_map/ppermute | solution.py:405
  49.9 9.6 %collective-permute-start.16 = (bf16[720,128]{1,0:T(8,128)(2,1)S(1)}, bf16[720,128]{1,0:T(8,128)(2,1)S(1)}, u32[]{:S(2)}, u32[]{:S(2)}) collective-permute-start(bf16[720,128]{1,0:T(8,128)(2,1)S(1)} %get-tuple-element.69), channel_id=1, source_target_pairs={{0,1},{1,0},{2,3},{3,2},{4,5},{5,4},{6,7},{7,6},{8,9},{9,8},{10,11... | collective-permute-start | bytes 552968 | tf_op jit(solution)/shard_map/ppermute | solution.py:408
  53.9 5.6 %collective-permute-start.27 = (bf16[720,128]{1,0:T(8,128)(2,1)S(1)}, bf16[720,128]{1,0:T(8,128)(2,1)S(1)}, u32[]{:S(2)}, u32[]{:S(2)}) collective-permute-start(bf16[720,128]{1,0:T(8,128)(2,1)S(1)} %shard_map.75), channel_id=1, source_target_pairs={{4,0},{8,4},{12,8},{14,12},{10,14},{6,10},{2,6},{0,2},{5,1},{9,5},... | collective-permute-start | bytes 552968 | tf_op jit(solution)/shard_map/ppermute | solution.py:412
  54.5 5.6 %collective-permute-start.29 = (bf16[720,128]{1,0:T(8,128)(2,1)S(1)}, bf16[720,128]{1,0:T(8,128)(2,1)S(1)}, u32[]{:S(2)}, u32[]{:S(2)}) collective-permute-start(bf16[720,128]{1,0:T(8,128)(2,1)S(1)} %add_convert_fusion), channel_id=1, source_target_pairs={{0,4},{4,8},{8,12},{12,14},{14,10},{10,6},{6,2},{2,0},{1,5},{5,9},... | collective-permute-start | bytes 552968 | tf_op jit(solution)/shard_map/ppermute | solution.py:405

commit v17 on v15

--- a/solution.py
+++ b/solution.py
@@ -384,15 +384,15 @@
     last = [far, far - 1, 1 - far]
     for keys, mine, theirs in zip(([far], last[1:]), *run_expert_in_stages(place, [came[k] for k in last], [across[k] for k in last], swap, weights, n, rows)):
         keep(keys, mine, theirs)
+
+    to_ahead = value[far].astype(jnp.bfloat16)
+    to_back = value[far - 1].astype(jnp.bfloat16)
     for keys, mine, theirs in near:
-        keep(keys, mine, swap(after(theirs, value[far])))
-
-    to_ahead = value[far].astype(jnp.bfloat16)
-    to_back = (value[far - 1]).astype(jnp.bfloat16)
+        keep(keys, mine, swap(after(theirs, to_back)))
     for k in range(far - 1, -1, -1):
         behind = lax.ppermute(to_ahead, "ep", ahead)
         if k == far - 1:
-            ((keys, mine, done),) = run([0], to_ahead)
+            ((keys, mine, done),) = run([0], (to_ahead, to_back))
             keep(keys, mine, swap(done))
         else:
             to_back = done = add(*parts[k], after(front, to_ahead))

time: 59 us -> 58.7 us (level)
    ppermute x3, waiting for transfers between devices: 9.92 us -> 3.32 us  [ring_body(): front = lax.ppermute(to_back, 'ep', back)]
    ppermute x4, waiting for transfers between devices: 2.56 us -> 8.9 us  [ring_body(): behind = lax.ppermute(to_ahead, 'ep', ahead)]
where the time goes in v17:
time: 58.7 us; the launch traced here: 58.6 us
  Pallas kernels  23.4 us (40%)
  starting transfers between devices  19.2 us (33%)
  waiting for transfers between devices  15.2 us (26%)
    pallas_call x6, Pallas kernels, call(): pl.pallas_call(kernel, out_shape=out_shape, in_specs=[pl.BlockSpec(memory...  13.5 us
    ppermute x4, waiting for transfers between devices, ring_body(): behind = lax.ppermute(to_ahead, 'ep', ahead)  8.9 us
    ppermute x4, starting transfers between devices, ring_body(): behind = lax.ppermute(to_ahead, 'ep', ahead)  7.18 us
    ppermute x3, starting transfers between devices, ring_body(): came[k] = lax.ppermute(came[k - 1], 'ep', ahead)  5.64 us
    pallas_call x1, Pallas kernels, turn_weights(): pl.pallas_call(turn_kernel, out_shape=[in_vmem((width, hidden))] * 2, in_...  4.79 us
    ppermute x3, waiting for transfers between devices, ring_body(): front = lax.ppermute(to_back, 'ep', back)  3.32 us
    pallas_call x1, Pallas kernels, halve_weights(): pl.pallas_call(halve_kernel, out_shape=[in_vmem((hidden, width // 2))] *...  3.13 us
    ppermute x1, starting transfers between devices, ring_body(): came[1] = lax.ppermute(packed, 'ep', ahead)  3.08 us
  transfers between devices with their start and end apart: 27, of which 10 were waited for; matrix products, arithmetic and copies ran while one was open for 1% of the time, Pallas kernels for 33%

profile of v17, /device:TPU:0, one launch (start us, length us, event | category | flops | bytes accessed | tf_op | source)
XLA Modules:
  0.0 58.6 jit_solution(7842587471460178553)
XLA Ops:
  0.0 1.1 %shard_map.64.refs_0_ = bf16[736,128]{1,0:T(8,128)(2,1)S(1)} custom-call(bf16[64,1440]{1,0:T(8,128)(2,1)} %tokens_in.1, s32[4,64]{1,0:T(4,128)} %bitcast.14, f32[4,64]{1,0:T(4,128)} %bitcast.15), custom_call_target="tpu_custom_call" | custom-call | tf_op jit(solution)/shard_map/pallas_call | solution.py:76
  1.1 3.1 %collective-permute-start = (bf16[736,128]{1,0:T(8,128)(2,1)S(1)}, bf16[736,128]{1,0:T(8,128)(2,1)S(1)}, u32[]{:S(2)}, u32[]{:S(2)}) collective-permute-start(bf16[736,128]{1,0:T(8,128)(2,1)S(1)} %shard_map.64.refs_0_), channel_id=1, source_target_pairs={{0,4},{4,8},{8,12},{12,14},{14,10},{10,6},{6,2},{2,0},{1,5},{5,9},... | collective-permute-start | bytes 565256 | tf_op jit(solution)/shard_map/ppermute | solution.py:366
  4.2 0.0 collective-permute-start.3
  4.2 0.1 pad_add_fusion.after_this.place
  4.3 4.8 %shard_map.65 = (bf16[2880,720]{1,0:T(8,128)(2,1)S(1)}, bf16[2880,720]{1,0:T(8,128)(2,1)S(1)}) custom-call(s32[2]{0:T(128)S(1)} %pad_add_fusion.after_this.place, bf16[720,2880]{1,0:T(8,128)(2,1)} %bitcast.11, bf16[720,2880]{1,0:T(8,128)(2,1)} %bitcast.12), custom_call_target="tpu_custom_call" | custom-call | bytes 16588800 | tf_op jit(solution)/shard_map/pallas_call | solution.py:106
  9.1 2.1 %collective-permute-start.1 = (bf16[736,128]{1,0:T(8,128)(2,1)S(1)}, bf16[736,128]{1,0:T(8,128)(2,1)S(1)}, u32[]{:S(2)}, u32[]{:S(2)}) collective-permute-start(bf16[736,128]{1,0:T(8,128)(2,1)S(1)} %collective-permute-done.refs_0_), channel_id=1, source_target_pairs={{0,4},{4,8},{8,12},{12,14},{14,10},{10,6},{6,2},{2,0},{1,5},{5,9},... | collective-permute-start | bytes 565256 | tf_op jit(solution)/shard_map/ppermute | solution.py:371
  11.1 0.0 collective-permute-done.3.refs_1_
  11.1 0.0 collective-permute-start.7
  11.2 0.5 collective-permute-start.5
  11.7 3.1 %shard_map.66 = (bf16[720,1440]{1,0:T(8,128)(2,1)S(1)}, bf16[720,1440]{1,0:T(8,128)(2,1)S(1)}) custom-call(s32[2]{0:T(128)S(1)} %pad_add_fusion.after_this.place, bf16[720,2880]{1,0:T(8,128)(2,1)} %bitcast.13), custom_call_target="tpu_custom_call" | custom-call | bytes 16588800 | tf_op jit(solution)/shard_map/pallas_call | solution.py:143
  14.8 0.5 collective-permute-done.1.refs_0_
  15.3 1.7 %collective-permute-start.2 = (bf16[736,128]{1,0:T(8,128)(2,1)S(1)}, bf16[736,128]{1,0:T(8,128)(2,1)S(1)}, u32[]{:S(2)}, u32[]{:S(2)}) collective-permute-start(bf16[736,128]{1,0:T(8,128)(2,1)S(1)} %collective-permute-done.1.refs_0_), channel_id=1, source_target_pairs={{0,4},{4,8},{8,12},{12,14},{14,10},{10,6},{6,2},{2,0},{1,5},{5,9},... | collective-permute-start | bytes 565256 | tf_op jit(solution)/shard_map/ppermute | solution.py:371
  17.0 0.0 collective-permute-start.8
  17.0 0.0 collective-permute-done.7.refs_1_
  17.1 0.3 collective-permute-start.10
  17.3 0.3 collective-permute-start.9
  17.6 0.0 collective-permute-done.5.refs_3_
  17.6 2.8 %shard_map.67 = (bf16[1440,128]{1,0:T(8,128)(2,1)S(1)}, bf16[1440,128]{1,0:T(8,128)(2,1)S(1)}) custom-call(s32[2]{0:T(128)S(1)} %pad_add_fusion.after_this.place, bf16[736,128]{1,0:T(8,128)(2,1)S(1)} %collective-permute-done.refs_0_, bf16[736,128]{1,0:T(8,128)(2,1)S(1)} %collective-permute-done.3.refs_1_, ...), custom_call_target="tpu_custom_call" | custom-call | flops 1592524800 | bytes 12441600 | tf_op jit(solution)/shard_map/pallas_call | solution.py:242
  20.4 1.3 %collective-permute-done.2.refs_1_ = bf16[736,128]{1,0:T(8,128)(2,1)S(1)} collective-permute-done((bf16[736,128]{1,0:T(8,128)(2,1)S(1)}, bf16[736,128]{1,0:T(8,128)(2,1)S(1)}, u32[]{:S(2)}, u32[]{:S(2)}) %collective-permute-start.2) | collective-permute-done | bytes 188448 | tf_op jit(solution)/shard_map/ppermute | solution.py:371
  21.7 1.8 %collective-permute-start.6 = (bf16[736,128]{1,0:T(8,128)(2,1)S(1)}, bf16[736,128]{1,0:T(8,128)(2,1)S(1)}, u32[]{:S(2)}, u32[]{:S(2)}) collective-permute-start(bf16[736,128]{1,0:T(8,128)(2,1)S(1)} %collective-permute-done.2.refs_1_), channel_id=1, source_target_pairs={{0,4},{4,8},{8,12},{12,14},{14,10},{10,6},{6,2},{2,0},{1,5},{5,9},... | collective-permute-start | bytes 565256 | tf_op jit(solution)/shard_map/ppermute | solution.py:371
  23.5 0.0 collective-permute-start.12
  23.5 0.7 %collective-permute-done.10.refs_2_ = bf16[736,128]{1,0:T(8,128)(2,1)S(1)} collective-permute-done((bf16[736,128]{1,0:T(8,128)(2,1)S(1)}, bf16[736,128]{1,0:T(8,128)(2,1)S(1)}, u32[]{:S(2)}, u32[]{:S(2)}) %collective-permute-start.10) | collective-permute-done | bytes 188448 | tf_op jit(solution)/shard_map/ppermute | solution.py:373
  24.2 0.0 collective-permute-done.8.refs_2_
  24.2 0.0 collective-permute-done.9.refs_3_
  24.2 2.8 %shard_map.68 = (bf16[1440,128]{1,0:T(8,128)(2,1)S(1)}, bf16[1440,128]{1,0:T(8,128)(2,1)S(1)}) custom-call(s32[2]{0:T(128)S(1)} %pad_add_fusion.after_this.place, bf16[736,128]{1,0:T(8,128)(2,1)S(1)} %collective-permute-done.1.refs_0_, bf16[736,128]{1,0:T(8,128)(2,1)S(1)} %collective-permute-done.7.refs_1_, ...), custom_call_target="tpu_custom_call" | custom-call | flops 1592524800 | bytes 12441600 | tf_op jit(solution)/shard_map/pallas_call | solution.py:242
  27.0 0.5 collective-permute-done.6.refs_0_
  27.5 0.1 collective-permute-start.11
  27.5 1.7 %shard_map.69 = (f32[192,720]{1,0:T(8,128)S(1)}, f32[192,720]{1,0:T(8,128)S(1)}) custom-call(s32[2]{0:T(128)S(1)} %pad_add_fusion.after_this.place, bf16[736,128]{1,0:T(8,128)(2,1)S(1)} %collective-permute-done.6.refs_0_, bf16[736,128]{1,0:T(8,128)(2,1)S(1)} %collective-permute-done.2.refs_1_, bf16[736,128]{1,0:T(8,128)(2,1)S(1)} %collective-permute-done.10.refs_2_, ...), custom_call_target="tpu_custom_call" | custom-call | flops 796262400 | bytes 6220800 | tf_op jit(solution)/shard_map/pallas_call | solution.py:242
  29.2 0.0 collective-permute-done.13.refs_5_
  29.2 2.3 %shard_map.70 = (bf16[192,720]{1,0:T(8,128)(2,1)S(1)}, bf16[720,128]{1,0:T(8,128)(2,1)S(1)}, bf16[1440,128]{1,0:T(8,128)(2,1)S(1)}) custom-call(s32[2]{0:T(128)S(1)} %pad_add_fusion.after_this.place, bf16[736,128]{1,0:T(8,128)(2,1)S(1)} %collective-permute-done.6.refs_0_, bf16[736,128]{1,0:T(8,128)(2,1)S(1)} %collective-permute-done.2.refs_1_, ...), custom_call_target="tpu_custom_call" | custom-call | flops 1194393600 | bytes 9331200 | tf_op jit(solution)/shard_map/pallas_call | solution.py:242
  31.5 0.5 collective-permute-start.14
  32.0 0.1 collective-permute-start.15
  32.1 0.4 collective-permute-start.16
  32.5 1.3 %shard_map.71 = (bf16[720,128]{1,0:T(8,128)(2,1)S(1)}, bf16[1440,128]{1,0:T(8,128)(2,1)S(1)}) custom-call(s32[2]{0:T(128)S(1)} %pad_add_fusion.after_this.place, bf16[736,128]{1,0:T(8,128)(2,1)S(1)} %collective-permute-done.6.refs_0_, bf16[736,128]{1,0:T(8,128)(2,1)S(1)} %collective-permute-done.2.refs_1_, ...), custom_call_target="tpu_custom_call" | custom-call | flops 398131200 | bytes 3110400 | tf_op jit(solution)/shard_map/pallas_call | solution.py:242
  33.8 0.0 collective-permute-done.14
  33.8 0.1 add_convert_fusion.4
  33.9 1.8 %collective-permute-start.21 = (bf16[720,128]{1,0:T(8,128)(2,1)S(1)}, bf16[720,128]{1,0:T(8,128)(2,1)S(1)}, u32[]{:S(2)}, u32[]{:S(2)}) collective-permute-start(bf16[720,128]{1,0:T(8,128)(2,1)S(1)} %add_convert_fusion.4), channel_id=1, source_target_pairs={{0,4},{4,8},{8,12},{12,14},{14,10},{10,6},{6,2},{2,0},{1,5},{5,9},... | collective-permute-start | bytes 552968 | tf_op jit(solution)/shard_map/ppermute | solution.py:393
  35.7 0.0 collective-permute-done.15
  35.7 0.1 add_convert_fusion.3
  35.7 0.3 collective-permute-start.20
  36.1 2.7 %shard_map.72 = (bf16[720,128]{1,0:T(8,128)(2,1)S(1)}, bf16[720,128]{1,0:T(8,128)(2,1)S(1)}) custom-call(s32[2]{0:T(128)S(1)} %pad_add_fusion.after_this.place, bf16[736,128]{1,0:T(8,128)(2,1)S(1)} %shard_map.64.refs_0_, bf16[736,128]{1,0:T(8,128)(2,1)S(1)} %collective-permute-done.16.refs_1_, ...), custom_call_target="tpu_custom_call" | custom-call | flops 1592524800 | bytes 12441600 | tf_op jit(solution)/shard_map/pallas_call | solution.py:242
  38.8 1.8 %collective-permute-done.21 = bf16[720,128]{1,0:T(8,128)(2,1)S(1)} collective-permute-done((bf16[720,128]{1,0:T(8,128)(2,1)S(1)}, bf16[720,128]{1,0:T(8,128)(2,1)S(1)}, u32[]{:S(2)}, u32[]{:S(2)}) %collective-permute-start.21) | collective-permute-done | bytes 184352 | tf_op jit(solution)/shard_map/ppermute | solution.py:393
  40.6 0.1 add_convert_fusion.2
  40.6 1.8 %collective-permute-start.23 = (bf16[720,128]{1,0:T(8,128)(2,1)S(1)}, bf16[720,128]{1,0:T(8,128)(2,1)S(1)}, u32[]{:S(2)}, u32[]{:S(2)}) collective-permute-start(bf16[720,128]{1,0:T(8,128)(2,1)S(1)} %add_convert_fusion.2), channel_id=1, source_target_pairs={{0,4},{4,8},{8,12},{12,14},{14,10},{10,6},{6,2},{2,0},{1,5},{5,9},... | collective-permute-start | bytes 552968 | tf_op jit(solution)/shard_map/ppermute | solution.py:393
  42.5 0.1 collective-permute-start.18
  42.5 0.0 collective-permute-done.20.refs_2_
  42.5 0.0 collective-permute-done.19
  42.6 0.1 shard_map.73
  42.7 0.3 collective-permute-start.22
  43.0 3.5 %collective-permute-done.23 = bf16[720,128]{1,0:T(8,128)(2,1)S(1)} collective-permute-done((bf16[720,128]{1,0:T(8,128)(2,1)S(1)}, bf16[720,128]{1,0:T(8,128)(2,1)S(1)}, u32[]{:S(2)}, u32[]{:S(2)}) %collective-permute-start.23) | collective-permute-done | bytes 184352 | tf_op jit(solution)/shard_map/ppermute | solution.py:393
  46.5 0.1 add_convert_fusion.1
  46.6 1.8 %collective-permute-start.25 = (bf16[720,128]{1,0:T(8,128)(2,1)S(1)}, bf16[720,128]{1,0:T(8,128)(2,1)S(1)}, u32[]{:S(2)}, u32[]{:S(2)}) collective-permute-start(bf16[720,128]{1,0:T(8,128)(2,1)S(1)} %add_convert_fusion.1), channel_id=1, source_target_pairs={{0,4},{4,8},{8,12},{12,14},{14,10},{10,6},{6,2},{2,0},{1,5},{5,9},... | collective-permute-start | bytes 552968 | tf_op jit(solution)/shard_map/ppermute | solution.py:393
  48.4 0.1 collective-permute-start.17
  48.5 1.2 %collective-permute-done.22.refs_2_ = bf16[720,128]{1,0:T(8,128)(2,1)S(1)} collective-permute-done((bf16[720,128]{1,0:T(8,128)(2,1)S(1)}, bf16[720,128]{1,0:T(8,128)(2,1)S(1)}, u32[]{:S(2)}, u32[]{:S(2)}) %collective-permute-start.22) | collective-permute-done | bytes 184352 | tf_op jit(solution)/shard_map/ppermute | solution.py:400
  49.7 0.1 shard_map.74
  49.8 0.3 collective-permute-start.24
  50.1 2.0 %collective-permute-done.25 = bf16[720,128]{1,0:T(8,128)(2,1)S(1)} collective-permute-done((bf16[720,128]{1,0:T(8,128)(2,1)S(1)}, bf16[720,128]{1,0:T(8,128)(2,1)S(1)}, u32[]{:S(2)}, u32[]{:S(2)}) %collective-permute-start.25) | collective-permute-done | bytes 184352 | tf_op jit(solution)/shard_map/ppermute | solution.py:393
  52.1 0.1 add_convert_fusion
  52.2 1.8 %collective-permute-start.26 = (bf16[720,128]{1,0:T(8,128)(2,1)S(1)}, bf16[720,128]{1,0:T(8,128)(2,1)S(1)}, u32[]{:S(2)}, u32[]{:S(2)}) collective-permute-start(bf16[720,128]{1,0:T(8,128)(2,1)S(1)} %add_convert_fusion), channel_id=1, source_target_pairs={{0,4},{4,8},{8,12},{12,14},{14,10},{10,6},{6,2},{2,0},{1,5},{5,9},... | collective-permute-start | bytes 552968 | tf_op jit(solution)/shard_map/ppermute | solution.py:393
  54.0 2.1 %collective-permute-done.24.refs_2_ = bf16[720,128]{1,0:T(8,128)(2,1)S(1)} collective-permute-done((bf16[720,128]{1,0:T(8,128)(2,1)S(1)}, bf16[720,128]{1,0:T(8,128)(2,1)S(1)}, u32[]{:S(2)}, u32[]{:S(2)}) %collective-permute-start.24) | collective-permute-done | bytes 184352 | tf_op jit(solution)/shard_map/ppermute | solution.py:400
  56.1 0.0 collective-permute-done.17.refs_1_
  56.1 0.1 shard_map.75.a
  56.2 1.7 %collective-permute-done.26.b = bf16[720,128]{1,0:T(8,128)(2,1)S(1)} collective-permute-done((bf16[720,128]{1,0:T(8,128)(2,1)S(1)}, bf16[720,128]{1,0:T(8,128)(2,1)S(1)}, u32[]{:S(2)}, u32[]{:S(2)}) %collective-permute-start.26) | collective-permute-done | bytes 184352 | tf_op jit(solution)/shard_map/ppermute | solution.py:393
  57.8 0.8 %shard_map.76 = bf16[64,1440]{1,0:T(8,128)(2,1)} custom-call(bf16[720,128]{1,0:T(8,128)(2,1)S(1)} %shard_map.75.a, bf16[720,128]{1,0:T(8,128)(2,1)S(1)} %collective-permute-done.26.b), custom_call_target="tpu_custom_call" | custom-call | tf_op jit(solution)/shard_map/pallas_call | solution.py:328
  (13 shorter events, 0.1 us)
Async XLA Ops:
  1.1 8.0 %collective-permute-start = (bf16[736,128]{1,0:T(8,128)(2,1)S(1)}, bf16[736,128]{1,0:T(8,128)(2,1)S(1)}, u32[]{:S(2)}, u32[]{:S(2)}) collective-permute-start(bf16[736,128]{1,0:T(8,128)(2,1)S(1)} %shard_map.64.refs_0_), channel_id=1, source_target_pairs={{0,4},{4,8},{8,12},{12,14},{14,10},{10,6},{6,2},{2,0},{1,5},{5,9},... | collective-permute-start | bytes 565256 | tf_op jit(solution)/shard_map/ppermute | solution.py:366
  4.2 7.0 %collective-permute-start.3 = (bf16[736,128]{1,0:T(8,128)(2,1)S(1)}, bf16[736,128]{1,0:T(8,128)(2,1)S(1)}, u32[]{:S(2)}, u32[]{:S(2)}) collective-permute-start(bf16[736,128]{1,0:T(8,128)(2,1)S(1)} %shard_map.64.refs_0_), channel_id=1, source_target_pairs={{4,0},{8,4},{12,8},{14,12},{10,14},{6,10},{2,6},{0,2},{5,1},{9,5},... | collective-permute-start | bytes 565256 | tf_op jit(solution)/shard_map/ppermute | solution.py:367
  9.1 6.2 %collective-permute-start.1 = (bf16[736,128]{1,0:T(8,128)(2,1)S(1)}, bf16[736,128]{1,0:T(8,128)(2,1)S(1)}, u32[]{:S(2)}, u32[]{:S(2)}) collective-permute-start(bf16[736,128]{1,0:T(8,128)(2,1)S(1)} %collective-permute-done.refs_0_), channel_id=1, source_target_pairs={{0,4},{4,8},{8,12},{12,14},{14,10},{10,6},{6,2},{2,0},{1,5},{5,9},... | collective-permute-start | bytes 565256 | tf_op jit(solution)/shard_map/ppermute | solution.py:371
  11.1 5.9 %collective-permute-start.7 = (bf16[736,128]{1,0:T(8,128)(2,1)S(1)}, bf16[736,128]{1,0:T(8,128)(2,1)S(1)}, u32[]{:S(2)}, u32[]{:S(2)}) collective-permute-start(bf16[736,128]{1,0:T(8,128)(2,1)S(1)} %collective-permute-done.3.refs_1_), channel_id=1, source_target_pairs={{4,0},{8,4},{12,8},{14,12},{10,14},{6,10},{2,6},{0,2},{5,1},{9,5},... | collective-permute-start | bytes 565256 | tf_op jit(solution)/shard_map/ppermute | solution.py:373
  11.1 6.2 %collective-permute-start.4 = (bf16[736,128]{1,0:T(8,128)(2,1)S(1)}, bf16[736,128]{1,0:T(8,128)(2,1)S(1)}, u32[]{:S(2)}, u32[]{:S(2)}) collective-permute-start(bf16[736,128]{1,0:T(8,128)(2,1)S(1)} %collective-permute-done.refs_0_), channel_id=1, source_target_pairs={{0,1},{1,0},{2,3},{3,2},{4,5},{5,4},{6,7},{7,6},{8,9},{9,8},{10,11... | collective-permute-start | bytes 565256 | tf_op jit(solution)/shard_map/ppermute | solution.py:374
  11.2 6.5 %collective-permute-start.5 = (bf16[736,128]{1,0:T(8,128)(2,1)S(1)}, bf16[736,128]{1,0:T(8,128)(2,1)S(1)}, u32[]{:S(2)}, u32[]{:S(2)}) collective-permute-start(bf16[736,128]{1,0:T(8,128)(2,1)S(1)} %collective-permute-done.3.refs_1_), channel_id=1, source_target_pairs={{0,1},{1,0},{2,3},{3,2},{4,5},{5,4},{6,7},{7,6},{8,9},{9,8},{10,11... | collective-permute-start | bytes 565256 | tf_op jit(solution)/shard_map/ppermute | solution.py:374
  15.3 6.4 %collective-permute-start.2 = (bf16[736,128]{1,0:T(8,128)(2,1)S(1)}, bf16[736,128]{1,0:T(8,128)(2,1)S(1)}, u32[]{:S(2)}, u32[]{:S(2)}) collective-permute-start(bf16[736,128]{1,0:T(8,128)(2,1)S(1)} %collective-permute-done.1.refs_0_), channel_id=1, source_target_pairs={{0,4},{4,8},{8,12},{12,14},{14,10},{10,6},{6,2},{2,0},{1,5},{5,9},... | collective-permute-start | bytes 565256 | tf_op jit(solution)/shard_map/ppermute | solution.py:371
  17.0 7.2 %collective-permute-start.8 = (bf16[736,128]{1,0:T(8,128)(2,1)S(1)}, bf16[736,128]{1,0:T(8,128)(2,1)S(1)}, u32[]{:S(2)}, u32[]{:S(2)}) collective-permute-start(bf16[736,128]{1,0:T(8,128)(2,1)S(1)} %collective-permute-done.1.refs_0_), channel_id=1, source_target_pairs={{0,1},{1,0},{2,3},{3,2},{4,5},{5,4},{6,7},{7,6},{8,9},{9,8},{10,11... | collective-permute-start | bytes 565256 | tf_op jit(solution)/shard_map/ppermute | solution.py:374
  17.1 7.1 %collective-permute-start.10 = (bf16[736,128]{1,0:T(8,128)(2,1)S(1)}, bf16[736,128]{1,0:T(8,128)(2,1)S(1)}, u32[]{:S(2)}, u32[]{:S(2)}) collective-permute-start(bf16[736,128]{1,0:T(8,128)(2,1)S(1)} %collective-permute-done.7.refs_1_), channel_id=1, source_target_pairs={{4,0},{8,4},{12,8},{14,12},{10,14},{6,10},{2,6},{0,2},{5,1},{9,5},... | collective-permute-start | bytes 565256 | tf_op jit(solution)/shard_map/ppermute | solution.py:373
  17.3 6.9 %collective-permute-start.9 = (bf16[736,128]{1,0:T(8,128)(2,1)S(1)}, bf16[736,128]{1,0:T(8,128)(2,1)S(1)}, u32[]{:S(2)}, u32[]{:S(2)}) collective-permute-start(bf16[736,128]{1,0:T(8,128)(2,1)S(1)} %collective-permute-done.7.refs_1_), channel_id=1, source_target_pairs={{0,1},{1,0},{2,3},{3,2},{4,5},{5,4},{6,7},{7,6},{8,9},{9,8},{10,11... | collective-permute-start | bytes 565256 | tf_op jit(solution)/shard_map/ppermute | solution.py:374
  21.7 5.8 %collective-permute-start.6 = (bf16[736,128]{1,0:T(8,128)(2,1)S(1)}, bf16[736,128]{1,0:T(8,128)(2,1)S(1)}, u32[]{:S(2)}, u32[]{:S(2)}) collective-permute-start(bf16[736,128]{1,0:T(8,128)(2,1)S(1)} %collective-permute-done.2.refs_1_), channel_id=1, source_target_pairs={{0,4},{4,8},{8,12},{12,14},{14,10},{10,6},{6,2},{2,0},{1,5},{5,9},... | collective-permute-start | bytes 565256 | tf_op jit(solution)/shard_map/ppermute | solution.py:371
  23.5 5.7 %collective-permute-start.12 = (bf16[736,128]{1,0:T(8,128)(2,1)S(1)}, bf16[736,128]{1,0:T(8,128)(2,1)S(1)}, u32[]{:S(2)}, u32[]{:S(2)}) collective-permute-start(bf16[736,128]{1,0:T(8,128)(2,1)S(1)} %collective-permute-done.2.refs_1_), channel_id=1, source_target_pairs={{0,1},{1,0},{2,3},{3,2},{4,5},{5,4},{6,7},{7,6},{8,9},{9,8},{10,11... | collective-permute-start | bytes 565256 | tf_op jit(solution)/shard_map/ppermute | solution.py:374
  24.2 5.0 %collective-permute-start.13 = (bf16[736,128]{1,0:T(8,128)(2,1)S(1)}, bf16[736,128]{1,0:T(8,128)(2,1)S(1)}, u32[]{:S(2)}, u32[]{:S(2)}) collective-permute-start(bf16[736,128]{1,0:T(8,128)(2,1)S(1)} %collective-permute-done.10.refs_2_), channel_id=1, source_target_pairs={{0,1},{1,0},{2,3},{3,2},{4,5},{5,4},{6,7},{7,6},{8,9},{9,8},{10,11... | collective-permute-start | bytes 565256 | tf_op jit(solution)/shard_map/ppermute | solution.py:374
  27.5 1.7 %collective-permute-start.11 = (bf16[736,128]{1,0:T(8,128)(2,1)S(1)}, bf16[736,128]{1,0:T(8,128)(2,1)S(1)}, u32[]{:S(2)}, u32[]{:S(2)}) collective-permute-start(bf16[736,128]{1,0:T(8,128)(2,1)S(1)} %collective-permute-done.6.refs_0_), channel_id=1, source_target_pairs={{0,1},{1,0},{2,3},{3,2},{4,5},{5,4},{6,7},{7,6},{8,9},{9,8},{10,11... | collective-permute-start | bytes 565256 | tf_op jit(solution)/shard_map/ppermute | solution.py:382
  31.5 2.3 %collective-permute-start.14 = (bf16[720,128]{1,0:T(8,128)(2,1)S(1)}, bf16[720,128]{1,0:T(8,128)(2,1)S(1)}, u32[]{:S(2)}, u32[]{:S(2)}) collective-permute-start(bf16[720,128]{1,0:T(8,128)(2,1)S(1)} %get-tuple-element.66), channel_id=1, source_target_pairs={{0,1},{1,0},{2,3},{3,2},{4,5},{5,4},{6,7},{7,6},{8,9},{9,8},{10,11... | collective-permute-start | bytes 552968 | tf_op jit(solution)/shard_map/ppermute | solution.py:291
  32.0 3.7 %collective-permute-start.15 = (bf16[1440,128]{1,0:T(8,128)(2,1)S(1)}, bf16[1440,128]{1,0:T(8,128)(2,1)S(1)}, u32[]{:S(2)}, u32[]{:S(2)}) collective-permute-start(bf16[1440,128]{1,0:T(8,128)(2,1)S(1)} %get-tuple-element.68), channel_id=1, source_target_pairs={{0,1},{1,0},{2,3},{3,2},{4,5},{5,4},{6,7},{7,6},{8,9},{9,8},{10,11... | collective-permute-start | bytes 1105928 | tf_op jit(solution)/shard_map/ppermute | solution.py:291
  32.1 4.0 %collective-permute-start.16 = (bf16[736,128]{1,0:T(8,128)(2,1)S(1)}, bf16[736,128]{1,0:T(8,128)(2,1)S(1)}, u32[]{:S(2)}, u32[]{:S(2)}) collective-permute-start(bf16[736,128]{1,0:T(8,128)(2,1)S(1)} %shard_map.64.refs_0_), channel_id=1, source_target_pairs={{0,1},{1,0},{2,3},{3,2},{4,5},{5,4},{6,7},{7,6},{8,9},{9,8},{10,11... | collective-permute-start | bytes 565256 | tf_op jit(solution)/shard_map/ppermute | solution.py:383
  33.9 6.7 %collective-permute-start.21 = (bf16[720,128]{1,0:T(8,128)(2,1)S(1)}, bf16[720,128]{1,0:T(8,128)(2,1)S(1)}, u32[]{:S(2)}, u32[]{:S(2)}) collective-permute-start(bf16[720,128]{1,0:T(8,128)(2,1)S(1)} %add_convert_fusion.4), channel_id=1, source_target_pairs={{0,4},{4,8},{8,12},{12,14},{14,10},{10,6},{6,2},{2,0},{1,5},{5,9},... | collective-permute-start | bytes 552968 | tf_op jit(solution)/shard_map/ppermute | solution.py:393
  35.7 6.8 %collective-permute-start.20 = (bf16[720,128]{1,0:T(8,128)(2,1)S(1)}, bf16[720,128]{1,0:T(8,128)(2,1)S(1)}, u32[]{:S(2)}, u32[]{:S(2)}) collective-permute-start(bf16[720,128]{1,0:T(8,128)(2,1)S(1)} %add_convert_fusion.3), channel_id=1, source_target_pairs={{4,0},{8,4},{12,8},{14,12},{10,14},{6,10},{2,6},{0,2},{5,1},{9,5},... | collective-permute-start | bytes 552968 | tf_op jit(solution)/shard_map/ppermute | solution.py:400
  36.1 6.5 %collective-permute-start.19 = (bf16[1440,128]{1,0:T(8,128)(2,1)S(1)}, bf16[1440,128]{1,0:T(8,128)(2,1)S(1)}, u32[]{:S(2)}, u32[]{:S(2)}) collective-permute-start(bf16[1440,128]{1,0:T(8,128)(2,1)S(1)} %get-tuple-element.76), channel_id=1, source_target_pairs={{0,1},{1,0},{2,3},{3,2},{4,5},{5,4},{6,7},{7,6},{8,9},{9,8},{10,11... | collective-permute-start | bytes 1105928 | tf_op jit(solution)/shard_map/ppermute | solution.py:391
  40.6 5.8 %collective-permute-start.23 = (bf16[720,128]{1,0:T(8,128)(2,1)S(1)}, bf16[720,128]{1,0:T(8,128)(2,1)S(1)}, u32[]{:S(2)}, u32[]{:S(2)}) collective-permute-start(bf16[720,128]{1,0:T(8,128)(2,1)S(1)} %add_convert_fusion.2), channel_id=1, source_target_pairs={{0,4},{4,8},{8,12},{12,14},{14,10},{10,6},{6,2},{2,0},{1,5},{5,9},... | collective-permute-start | bytes 552968 | tf_op jit(solution)/shard_map/ppermute | solution.py:393
  42.5 6.0 %collective-permute-start.18 = (bf16[1440,128]{1,0:T(8,128)(2,1)S(1)}, bf16[1440,128]{1,0:T(8,128)(2,1)S(1)}, u32[]{:S(2)}, u32[]{:S(2)}) collective-permute-start(bf16[1440,128]{1,0:T(8,128)(2,1)S(1)} %get-tuple-element.74), channel_id=1, source_target_pairs={{0,1},{1,0},{2,3},{3,2},{4,5},{5,4},{6,7},{7,6},{8,9},{9,8},{10,11... | collective-permute-start | bytes 1105928 | tf_op jit(solution)/shard_map/ppermute | solution.py:391
  42.7 7.1 %collective-permute-start.22 = (bf16[720,128]{1,0:T(8,128)(2,1)S(1)}, bf16[720,128]{1,0:T(8,128)(2,1)S(1)}, u32[]{:S(2)}, u32[]{:S(2)}) collective-permute-start(bf16[720,128]{1,0:T(8,128)(2,1)S(1)} %shard_map.73), channel_id=1, source_target_pairs={{4,0},{8,4},{12,8},{14,12},{10,14},{6,10},{2,6},{0,2},{5,1},{9,5},... | collective-permute-start | bytes 552968 | tf_op jit(solution)/shard_map/ppermute | solution.py:400
  46.6 5.6 %collective-permute-start.25 = (bf16[720,128]{1,0:T(8,128)(2,1)S(1)}, bf16[720,128]{1,0:T(8,128)(2,1)S(1)}, u32[]{:S(2)}, u32[]{:S(2)}) collective-permute-start(bf16[720,128]{1,0:T(8,128)(2,1)S(1)} %add_convert_fusion.1), channel_id=1, source_target_pairs={{0,4},{4,8},{8,12},{12,14},{14,10},{10,6},{6,2},{2,0},{1,5},{5,9},... | collective-permute-start | bytes 552968 | tf_op jit(solution)/shard_map/ppermute | solution.py:393
  48.4 7.7 %collective-permute-start.17 = (bf16[720,128]{1,0:T(8,128)(2,1)S(1)}, bf16[720,128]{1,0:T(8,128)(2,1)S(1)}, u32[]{:S(2)}, u32[]{:S(2)}) collective-permute-start(bf16[720,128]{1,0:T(8,128)(2,1)S(1)} %get-tuple-element.72), channel_id=1, source_target_pairs={{0,1},{1,0},{2,3},{3,2},{4,5},{5,4},{6,7},{7,6},{8,9},{9,8},{10,11... | collective-permute-start | bytes 552968 | tf_op jit(solution)/shard_map/ppermute | solution.py:396
  49.8 6.3 %collective-permute-start.24 = (bf16[720,128]{1,0:T(8,128)(2,1)S(1)}, bf16[720,128]{1,0:T(8,128)(2,1)S(1)}, u32[]{:S(2)}, u32[]{:S(2)}) collective-permute-start(bf16[720,128]{1,0:T(8,128)(2,1)S(1)} %shard_map.74), channel_id=1, source_target_pairs={{4,0},{8,4},{12,8},{14,12},{10,14},{6,10},{2,6},{0,2},{5,1},{9,5},... | collective-permute-start | bytes 552968 | tf_op jit(solution)/shard_map/ppermute | solution.py:400
  52.2 5.6 %collective-permute-start.26 = (bf16[720,128]{1,0:T(8,128)(2,1)S(1)}, bf16[720,128]{1,0:T(8,128)(2,1)S(1)}, u32[]{:S(2)}, u32[]{:S(2)}) collective-permute-start(bf16[720,128]{1,0:T(8,128)(2,1)S(1)} %add_convert_fusion), channel_id=1, source_target_pairs={{0,4},{4,8},{8,12},{12,14},{14,10},{10,6},{6,2},{2,0},{1,5},{5,9},... | collective-permute-start | bytes 552968 | tf_op jit(solution)/shard_map/ppermute | solution.py:393

commit v18 on v17

--- a/solution.py
+++ b/solution.py
@@ -94,10 +94,12 @@
         for j, (start, stop) in enumerate(pieces(src.shape[0])):
             span = pl.ds(start, stop - start)
             steps.append((pltpu.make_async_copy(src.at[span], buf.at[span], sems.at[i, j]), buf, out, start, stop))
-    for copy, *_ in steps:
+    for copy, *_ in steps[:2]:
         copy.start()
-    for copy, buf, out, start, stop in steps:
+    for i, (copy, buf, out, start, stop) in enumerate(steps):
         copy.wait()
+        if i + 2 < len(steps):
+            steps[i + 2][0].start()
         out[:, start:stop] = buf[start:stop, :].T
 
 

time: 58.7 us -> 59.2 us (level)
  transfers between devices with their start and end apart: 27 -> 27, of which waited for: 10 -> 10; matrix products, arithmetic and copies ran while one was open for 1% -> 1% of each run, Pallas kernels for 33% -> 34%
where the time goes in v18:
time: 59.2 us; the launch traced here: 59.1 us
  Pallas kernels  23.9 us (40%)
  starting transfers between devices  19.2 us (32%)
  waiting for transfers between devices  15.3 us (26%)
    pallas_call x6, Pallas kernels, call(): pl.pallas_call(kernel, out_shape=out_shape, in_specs=[pl.BlockSpec(memory...  13.5 us
    ppermute x4, waiting for transfers between devices, ring_body(): behind = lax.ppermute(to_ahead, 'ep', ahead)  8.92 us
    ppermute x4, starting transfers between devices, ring_body(): behind = lax.ppermute(to_ahead, 'ep', ahead)  7.13 us
    ppermute x3, starting transfers between devices, ring_body(): came[k] = lax.ppermute(came[k - 1], 'ep', ahead)  5.64 us
    pallas_call x1, Pallas kernels, turn_weights(): pl.pallas_call(turn_kernel, out_shape=[in_vmem((width, hidden))] * 2, in_...  5.29 us
    ppermute x3, waiting for transfers between devices, ring_body(): front = lax.ppermute(to_back, 'ep', back)  3.32 us
    pallas_call x1, Pallas kernels, halve_weights(): pl.pallas_call(halve_kernel, out_shape=[in_vmem((hidden, width // 2))] *...  3.13 us
    ppermute x1, starting transfers between devices, ring_body(): came[1] = lax.ppermute(packed, 'ep', ahead)  3.08 us
  transfers between devices with their start and end apart: 27, of which 10 were waited for; matrix products, arithmetic and copies ran while one was open for 1% of the time, Pallas kernels for 34%

profile of v18, /device:TPU:0, one launch (start us, length us, event | category | flops | bytes accessed | tf_op | source)
XLA Modules:
  0.0 59.1 jit_solution(17196465348311367573)
XLA Ops:
  0.0 1.1 %shard_map.64.refs_0_ = bf16[736,128]{1,0:T(8,128)(2,1)S(1)} custom-call(bf16[64,1440]{1,0:T(8,128)(2,1)} %tokens_in.1, s32[4,64]{1,0:T(4,128)} %bitcast.14, f32[4,64]{1,0:T(4,128)} %bitcast.15), custom_call_target="tpu_custom_call" | custom-call | tf_op jit(solution)/shard_map/pallas_call | solution.py:76
  1.1 3.1 %collective-permute-start = (bf16[736,128]{1,0:T(8,128)(2,1)S(1)}, bf16[736,128]{1,0:T(8,128)(2,1)S(1)}, u32[]{:S(2)}, u32[]{:S(2)}) collective-permute-start(bf16[736,128]{1,0:T(8,128)(2,1)S(1)} %shard_map.64.refs_0_), channel_id=1, source_target_pairs={{0,4},{4,8},{8,12},{12,14},{14,10},{10,6},{6,2},{2,0},{1,5},{5,9},... | collective-permute-start | bytes 565256 | tf_op jit(solution)/shard_map/ppermute | solution.py:368
  4.2 0.0 collective-permute-start.3
  4.2 0.1 pad_add_fusion.after_this.place
  4.3 5.3 %shard_map.65 = (bf16[2880,720]{1,0:T(8,128)(2,1)S(1)}, bf16[2880,720]{1,0:T(8,128)(2,1)S(1)}) custom-call(s32[2]{0:T(128)S(1)} %pad_add_fusion.after_this.place, bf16[720,2880]{1,0:T(8,128)(2,1)} %bitcast.11, bf16[720,2880]{1,0:T(8,128)(2,1)} %bitcast.12), custom_call_target="tpu_custom_call" | custom-call | bytes 16588800 | tf_op jit(solution)/shard_map/pallas_call | solution.py:108
  9.6 0.0 collective-permute-done.refs_0_
  9.6 2.1 %collective-permute-start.1 = (bf16[736,128]{1,0:T(8,128)(2,1)S(1)}, bf16[736,128]{1,0:T(8,128)(2,1)S(1)}, u32[]{:S(2)}, u32[]{:S(2)}) collective-permute-start(bf16[736,128]{1,0:T(8,128)(2,1)S(1)} %collective-permute-done.refs_0_), channel_id=1, source_target_pairs={{0,4},{4,8},{8,12},{12,14},{14,10},{10,6},{6,2},{2,0},{1,5},{5,9},... | collective-permute-start | bytes 565256 | tf_op jit(solution)/shard_map/ppermute | solution.py:373
  11.6 0.0 collective-permute-done.3.refs_1_
  11.6 0.0 collective-permute-start.7
  11.6 0.0 collective-permute-start.4
  11.7 0.5 collective-permute-start.5
  12.2 3.1 %shard_map.66 = (bf16[720,1440]{1,0:T(8,128)(2,1)S(1)}, bf16[720,1440]{1,0:T(8,128)(2,1)S(1)}) custom-call(s32[2]{0:T(128)S(1)} %pad_add_fusion.after_this.place, bf16[720,2880]{1,0:T(8,128)(2,1)} %bitcast.13), custom_call_target="tpu_custom_call" | custom-call | bytes 16588800 | tf_op jit(solution)/shard_map/pallas_call | solution.py:145
  15.3 0.5 collective-permute-done.1.refs_0_
  15.8 1.7 %collective-permute-start.2 = (bf16[736,128]{1,0:T(8,128)(2,1)S(1)}, bf16[736,128]{1,0:T(8,128)(2,1)S(1)}, u32[]{:S(2)}, u32[]{:S(2)}) collective-permute-start(bf16[736,128]{1,0:T(8,128)(2,1)S(1)} %collective-permute-done.1.refs_0_), channel_id=1, source_target_pairs={{0,4},{4,8},{8,12},{12,14},{14,10},{10,6},{6,2},{2,0},{1,5},{5,9},... | collective-permute-start | bytes 565256 | tf_op jit(solution)/shard_map/ppermute | solution.py:373
  17.5 0.0 collective-permute-start.8
  17.6 0.3 collective-permute-start.10
  17.8 0.0 collective-permute-done.4.refs_2_
  17.8 0.3 collective-permute-start.9
  18.1 2.8 %shard_map.67 = (bf16[1440,128]{1,0:T(8,128)(2,1)S(1)}, bf16[1440,128]{1,0:T(8,128)(2,1)S(1)}) custom-call(s32[2]{0:T(128)S(1)} %pad_add_fusion.after_this.place, bf16[736,128]{1,0:T(8,128)(2,1)S(1)} %collective-permute-done.refs_0_, bf16[736,128]{1,0:T(8,128)(2,1)S(1)} %collective-permute-done.3.refs_1_, ...), custom_call_target="tpu_custom_call" | custom-call | flops 1592524800 | bytes 12441600 | tf_op jit(solution)/shard_map/pallas_call | solution.py:244
  20.9 1.3 %collective-permute-done.2.refs_1_ = bf16[736,128]{1,0:T(8,128)(2,1)S(1)} collective-permute-done((bf16[736,128]{1,0:T(8,128)(2,1)S(1)}, bf16[736,128]{1,0:T(8,128)(2,1)S(1)}, u32[]{:S(2)}, u32[]{:S(2)}) %collective-permute-start.2) | collective-permute-done | bytes 188448 | tf_op jit(solution)/shard_map/ppermute | solution.py:373
  22.2 1.8 %collective-permute-start.6 = (bf16[736,128]{1,0:T(8,128)(2,1)S(1)}, bf16[736,128]{1,0:T(8,128)(2,1)S(1)}, u32[]{:S(2)}, u32[]{:S(2)}) collective-permute-start(bf16[736,128]{1,0:T(8,128)(2,1)S(1)} %collective-permute-done.2.refs_1_), channel_id=1, source_target_pairs={{0,4},{4,8},{8,12},{12,14},{14,10},{10,6},{6,2},{2,0},{1,5},{5,9},... | collective-permute-start | bytes 565256 | tf_op jit(solution)/shard_map/ppermute | solution.py:373
  24.0 0.7 %collective-permute-done.10.refs_2_ = bf16[736,128]{1,0:T(8,128)(2,1)S(1)} collective-permute-done((bf16[736,128]{1,0:T(8,128)(2,1)S(1)}, bf16[736,128]{1,0:T(8,128)(2,1)S(1)}, u32[]{:S(2)}, u32[]{:S(2)}) %collective-permute-start.10) | collective-permute-done | bytes 188448 | tf_op jit(solution)/shard_map/ppermute | solution.py:375
  24.7 0.0 collective-permute-start.13
  24.7 0.0 collective-permute-done.8.refs_2_
  24.7 2.8 %shard_map.68 = (bf16[1440,128]{1,0:T(8,128)(2,1)S(1)}, bf16[1440,128]{1,0:T(8,128)(2,1)S(1)}) custom-call(s32[2]{0:T(128)S(1)} %pad_add_fusion.after_this.place, bf16[736,128]{1,0:T(8,128)(2,1)S(1)} %collective-permute-done.1.refs_0_, bf16[736,128]{1,0:T(8,128)(2,1)S(1)} %collective-permute-done.7.refs_1_, ...), custom_call_target="tpu_custom_call" | custom-call | flops 1592524800 | bytes 12441600 | tf_op jit(solution)/shard_map/pallas_call | solution.py:244
  27.5 0.5 collective-permute-done.6.refs_0_
  28.0 0.1 collective-permute-start.11
  28.1 1.7 %shard_map.69 = (f32[192,720]{1,0:T(8,128)S(1)}, f32[192,720]{1,0:T(8,128)S(1)}) custom-call(s32[2]{0:T(128)S(1)} %pad_add_fusion.after_this.place, bf16[736,128]{1,0:T(8,128)(2,1)S(1)} %collective-permute-done.6.refs_0_, bf16[736,128]{1,0:T(8,128)(2,1)S(1)} %collective-permute-done.2.refs_1_, bf16[736,128]{1,0:T(8,128)(2,1)S(1)} %collective-permute-done.10.refs_2_, ...), custom_call_target="tpu_custom_call" | custom-call | flops 796262400 | bytes 6220800 | tf_op jit(solution)/shard_map/pallas_call | solution.py:244
  29.7 0.0 collective-permute-done.13.refs_5_
  29.7 0.0 collective-permute-done.12.refs_4_
  29.8 2.3 %shard_map.70 = (bf16[192,720]{1,0:T(8,128)(2,1)S(1)}, bf16[720,128]{1,0:T(8,128)(2,1)S(1)}, bf16[1440,128]{1,0:T(8,128)(2,1)S(1)}) custom-call(s32[2]{0:T(128)S(1)} %pad_add_fusion.after_this.place, bf16[736,128]{1,0:T(8,128)(2,1)S(1)} %collective-permute-done.6.refs_0_, bf16[736,128]{1,0:T(8,128)(2,1)S(1)} %collective-permute-done.2.refs_1_, ...), custom_call_target="tpu_custom_call" | custom-call | flops 1194393600 | bytes 9331200 | tf_op jit(solution)/shard_map/pallas_call | solution.py:244
  32.0 0.5 collective-permute-start.14
  32.5 0.1 collective-permute-start.15
  32.6 0.4 collective-permute-start.16
  33.0 1.3 %shard_map.71 = (bf16[720,128]{1,0:T(8,128)(2,1)S(1)}, bf16[1440,128]{1,0:T(8,128)(2,1)S(1)}) custom-call(s32[2]{0:T(128)S(1)} %pad_add_fusion.after_this.place, bf16[736,128]{1,0:T(8,128)(2,1)S(1)} %collective-permute-done.6.refs_0_, bf16[736,128]{1,0:T(8,128)(2,1)S(1)} %collective-permute-done.2.refs_1_, ...), custom_call_target="tpu_custom_call" | custom-call | flops 398131200 | bytes 3110400 | tf_op jit(solution)/shard_map/pallas_call | solution.py:244
  34.3 0.0 collective-permute-done.14
  34.3 0.1 add_convert_fusion.4
  34.4 1.8 %collective-permute-start.21 = (bf16[720,128]{1,0:T(8,128)(2,1)S(1)}, bf16[720,128]{1,0:T(8,128)(2,1)S(1)}, u32[]{:S(2)}, u32[]{:S(2)}) collective-permute-start(bf16[720,128]{1,0:T(8,128)(2,1)S(1)} %add_convert_fusion.4), channel_id=1, source_target_pairs={{0,4},{4,8},{8,12},{12,14},{14,10},{10,6},{6,2},{2,0},{1,5},{5,9},... | collective-permute-start | bytes 552968 | tf_op jit(solution)/shard_map/ppermute | solution.py:395
  36.2 0.0 collective-permute-done.15
  36.2 0.1 add_convert_fusion.3
  36.2 0.3 collective-permute-start.20
  36.6 2.7 %shard_map.72 = (bf16[720,128]{1,0:T(8,128)(2,1)S(1)}, bf16[720,128]{1,0:T(8,128)(2,1)S(1)}) custom-call(s32[2]{0:T(128)S(1)} %pad_add_fusion.after_this.place, bf16[736,128]{1,0:T(8,128)(2,1)S(1)} %shard_map.64.refs_0_, bf16[736,128]{1,0:T(8,128)(2,1)S(1)} %collective-permute-done.16.refs_1_, ...), custom_call_target="tpu_custom_call" | custom-call | flops 1592524800 | bytes 12441600 | tf_op jit(solution)/shard_map/pallas_call | solution.py:244
  39.3 1.8 %collective-permute-done.21 = bf16[720,128]{1,0:T(8,128)(2,1)S(1)} collective-permute-done((bf16[720,128]{1,0:T(8,128)(2,1)S(1)}, bf16[720,128]{1,0:T(8,128)(2,1)S(1)}, u32[]{:S(2)}, u32[]{:S(2)}) %collective-permute-start.21) | collective-permute-done | bytes 184352 | tf_op jit(solution)/shard_map/ppermute | solution.py:395
  41.1 0.1 add_convert_fusion.2
  41.1 1.8 %collective-permute-start.23 = (bf16[720,128]{1,0:T(8,128)(2,1)S(1)}, bf16[720,128]{1,0:T(8,128)(2,1)S(1)}, u32[]{:S(2)}, u32[]{:S(2)}) collective-permute-start(bf16[720,128]{1,0:T(8,128)(2,1)S(1)} %add_convert_fusion.2), channel_id=1, source_target_pairs={{0,4},{4,8},{8,12},{12,14},{14,10},{10,6},{6,2},{2,0},{1,5},{5,9},... | collective-permute-start | bytes 552968 | tf_op jit(solution)/shard_map/ppermute | solution.py:395
  42.9 0.1 collective-permute-start.18
  43.0 0.0 collective-permute-done.19
  43.1 0.1 shard_map.73
  43.1 0.3 collective-permute-start.22
  43.5 3.5 %collective-permute-done.23 = bf16[720,128]{1,0:T(8,128)(2,1)S(1)} collective-permute-done((bf16[720,128]{1,0:T(8,128)(2,1)S(1)}, bf16[720,128]{1,0:T(8,128)(2,1)S(1)}, u32[]{:S(2)}, u32[]{:S(2)}) %collective-permute-start.23) | collective-permute-done | bytes 184352 | tf_op jit(solution)/shard_map/ppermute | solution.py:395
  47.0 0.1 add_convert_fusion.1
  47.1 1.8 %collective-permute-start.25 = (bf16[720,128]{1,0:T(8,128)(2,1)S(1)}, bf16[720,128]{1,0:T(8,128)(2,1)S(1)}, u32[]{:S(2)}, u32[]{:S(2)}) collective-permute-start(bf16[720,128]{1,0:T(8,128)(2,1)S(1)} %add_convert_fusion.1), channel_id=1, source_target_pairs={{0,4},{4,8},{8,12},{12,14},{14,10},{10,6},{6,2},{2,0},{1,5},{5,9},... | collective-permute-start | bytes 552968 | tf_op jit(solution)/shard_map/ppermute | solution.py:395
  48.9 0.1 collective-permute-start.17
  48.9 0.0 collective-permute-done.18
  49.0 1.2 %collective-permute-done.22.refs_2_ = bf16[720,128]{1,0:T(8,128)(2,1)S(1)} collective-permute-done((bf16[720,128]{1,0:T(8,128)(2,1)S(1)}, bf16[720,128]{1,0:T(8,128)(2,1)S(1)}, u32[]{:S(2)}, u32[]{:S(2)}) %collective-permute-start.22) | collective-permute-done | bytes 184352 | tf_op jit(solution)/shard_map/ppermute | solution.py:402
  50.2 0.1 shard_map.74
  50.3 0.3 collective-permute-start.24
  50.6 2.0 %collective-permute-done.25 = bf16[720,128]{1,0:T(8,128)(2,1)S(1)} collective-permute-done((bf16[720,128]{1,0:T(8,128)(2,1)S(1)}, bf16[720,128]{1,0:T(8,128)(2,1)S(1)}, u32[]{:S(2)}, u32[]{:S(2)}) %collective-permute-start.25) | collective-permute-done | bytes 184352 | tf_op jit(solution)/shard_map/ppermute | solution.py:395
  52.7 0.1 add_convert_fusion
  52.7 1.8 %collective-permute-start.26 = (bf16[720,128]{1,0:T(8,128)(2,1)S(1)}, bf16[720,128]{1,0:T(8,128)(2,1)S(1)}, u32[]{:S(2)}, u32[]{:S(2)}) collective-permute-start(bf16[720,128]{1,0:T(8,128)(2,1)S(1)} %add_convert_fusion), channel_id=1, source_target_pairs={{0,4},{4,8},{8,12},{12,14},{14,10},{10,6},{6,2},{2,0},{1,5},{5,9},... | collective-permute-start | bytes 552968 | tf_op jit(solution)/shard_map/ppermute | solution.py:395
  54.5 2.1 %collective-permute-done.24.refs_2_ = bf16[720,128]{1,0:T(8,128)(2,1)S(1)} collective-permute-done((bf16[720,128]{1,0:T(8,128)(2,1)S(1)}, bf16[720,128]{1,0:T(8,128)(2,1)S(1)}, u32[]{:S(2)}, u32[]{:S(2)}) %collective-permute-start.24) | collective-permute-done | bytes 184352 | tf_op jit(solution)/shard_map/ppermute | solution.py:402
  56.6 0.1 shard_map.75.a
  56.7 1.7 %collective-permute-done.26.b = bf16[720,128]{1,0:T(8,128)(2,1)S(1)} collective-permute-done((bf16[720,128]{1,0:T(8,128)(2,1)S(1)}, bf16[720,128]{1,0:T(8,128)(2,1)S(1)}, u32[]{:S(2)}, u32[]{:S(2)}) %collective-permute-start.26) | collective-permute-done | bytes 184352 | tf_op jit(solution)/shard_map/ppermute | solution.py:395
  58.3 0.8 %shard_map.76 = bf16[64,1440]{1,0:T(8,128)(2,1)} custom-call(bf16[720,128]{1,0:T(8,128)(2,1)S(1)} %shard_map.75.a, bf16[720,128]{1,0:T(8,128)(2,1)S(1)} %collective-permute-done.26.b), custom_call_target="tpu_custom_call" | custom-call | tf_op jit(solution)/shard_map/pallas_call | solution.py:330
  (13 shorter events, 0.1 us)
Async XLA Ops:
  1.1 8.5 %collective-permute-start = (bf16[736,128]{1,0:T(8,128)(2,1)S(1)}, bf16[736,128]{1,0:T(8,128)(2,1)S(1)}, u32[]{:S(2)}, u32[]{:S(2)}) collective-permute-start(bf16[736,128]{1,0:T(8,128)(2,1)S(1)} %shard_map.64.refs_0_), channel_id=1, source_target_pairs={{0,4},{4,8},{8,12},{12,14},{14,10},{10,6},{6,2},{2,0},{1,5},{5,9},... | collective-permute-start | bytes 565256 | tf_op jit(solution)/shard_map/ppermute | solution.py:368
  4.2 7.5 %collective-permute-start.3 = (bf16[736,128]{1,0:T(8,128)(2,1)S(1)}, bf16[736,128]{1,0:T(8,128)(2,1)S(1)}, u32[]{:S(2)}, u32[]{:S(2)}) collective-permute-start(bf16[736,128]{1,0:T(8,128)(2,1)S(1)} %shard_map.64.refs_0_), channel_id=1, source_target_pairs={{4,0},{8,4},{12,8},{14,12},{10,14},{6,10},{2,6},{0,2},{5,1},{9,5},... | collective-permute-start | bytes 565256 | tf_op jit(solution)/shard_map/ppermute | solution.py:369
  9.6 6.2 %collective-permute-start.1 = (bf16[736,128]{1,0:T(8,128)(2,1)S(1)}, bf16[736,128]{1,0:T(8,128)(2,1)S(1)}, u32[]{:S(2)}, u32[]{:S(2)}) collective-permute-start(bf16[736,128]{1,0:T(8,128)(2,1)S(1)} %collective-permute-done.refs_0_), channel_id=1, source_target_pairs={{0,4},{4,8},{8,12},{12,14},{14,10},{10,6},{6,2},{2,0},{1,5},{5,9},... | collective-permute-start | bytes 565256 | tf_op jit(solution)/shard_map/ppermute | solution.py:373
  11.6 5.9 %collective-permute-start.7 = (bf16[736,128]{1,0:T(8,128)(2,1)S(1)}, bf16[736,128]{1,0:T(8,128)(2,1)S(1)}, u32[]{:S(2)}, u32[]{:S(2)}) collective-permute-start(bf16[736,128]{1,0:T(8,128)(2,1)S(1)} %collective-permute-done.3.refs_1_), channel_id=1, source_target_pairs={{4,0},{8,4},{12,8},{14,12},{10,14},{6,10},{2,6},{0,2},{5,1},{9,5},... | collective-permute-start | bytes 565256 | tf_op jit(solution)/shard_map/ppermute | solution.py:375
  11.6 6.2 %collective-permute-start.4 = (bf16[736,128]{1,0:T(8,128)(2,1)S(1)}, bf16[736,128]{1,0:T(8,128)(2,1)S(1)}, u32[]{:S(2)}, u32[]{:S(2)}) collective-permute-start(bf16[736,128]{1,0:T(8,128)(2,1)S(1)} %collective-permute-done.refs_0_), channel_id=1, source_target_pairs={{0,1},{1,0},{2,3},{3,2},{4,5},{5,4},{6,7},{7,6},{8,9},{9,8},{10,11... | collective-permute-start | bytes 565256 | tf_op jit(solution)/shard_map/ppermute | solution.py:376
  11.7 6.5 %collective-permute-start.5 = (bf16[736,128]{1,0:T(8,128)(2,1)S(1)}, bf16[736,128]{1,0:T(8,128)(2,1)S(1)}, u32[]{:S(2)}, u32[]{:S(2)}) collective-permute-start(bf16[736,128]{1,0:T(8,128)(2,1)S(1)} %collective-permute-done.3.refs_1_), channel_id=1, source_target_pairs={{0,1},{1,0},{2,3},{3,2},{4,5},{5,4},{6,7},{7,6},{8,9},{9,8},{10,11... | collective-permute-start | bytes 565256 | tf_op jit(solution)/shard_map/ppermute | solution.py:376
  15.8 6.4 %collective-permute-start.2 = (bf16[736,128]{1,0:T(8,128)(2,1)S(1)}, bf16[736,128]{1,0:T(8,128)(2,1)S(1)}, u32[]{:S(2)}, u32[]{:S(2)}) collective-permute-start(bf16[736,128]{1,0:T(8,128)(2,1)S(1)} %collective-permute-done.1.refs_0_), channel_id=1, source_target_pairs={{0,4},{4,8},{8,12},{12,14},{14,10},{10,6},{6,2},{2,0},{1,5},{5,9},... | collective-permute-start | bytes 565256 | tf_op jit(solution)/shard_map/ppermute | solution.py:373
  17.5 7.2 %collective-permute-start.8 = (bf16[736,128]{1,0:T(8,128)(2,1)S(1)}, bf16[736,128]{1,0:T(8,128)(2,1)S(1)}, u32[]{:S(2)}, u32[]{:S(2)}) collective-permute-start(bf16[736,128]{1,0:T(8,128)(2,1)S(1)} %collective-permute-done.1.refs_0_), channel_id=1, source_target_pairs={{0,1},{1,0},{2,3},{3,2},{4,5},{5,4},{6,7},{7,6},{8,9},{9,8},{10,11... | collective-permute-start | bytes 565256 | tf_op jit(solution)/shard_map/ppermute | solution.py:376
  17.6 7.1 %collective-permute-start.10 = (bf16[736,128]{1,0:T(8,128)(2,1)S(1)}, bf16[736,128]{1,0:T(8,128)(2,1)S(1)}, u32[]{:S(2)}, u32[]{:S(2)}) collective-permute-start(bf16[736,128]{1,0:T(8,128)(2,1)S(1)} %collective-permute-done.7.refs_1_), channel_id=1, source_target_pairs={{4,0},{8,4},{12,8},{14,12},{10,14},{6,10},{2,6},{0,2},{5,1},{9,5},... | collective-permute-start | bytes 565256 | tf_op jit(solution)/shard_map/ppermute | solution.py:375
  17.8 6.9 %collective-permute-start.9 = (bf16[736,128]{1,0:T(8,128)(2,1)S(1)}, bf16[736,128]{1,0:T(8,128)(2,1)S(1)}, u32[]{:S(2)}, u32[]{:S(2)}) collective-permute-start(bf16[736,128]{1,0:T(8,128)(2,1)S(1)} %collective-permute-done.7.refs_1_), channel_id=1, source_target_pairs={{0,1},{1,0},{2,3},{3,2},{4,5},{5,4},{6,7},{7,6},{8,9},{9,8},{10,11... | collective-permute-start | bytes 565256 | tf_op jit(solution)/shard_map/ppermute | solution.py:376
  22.2 5.8 %collective-permute-start.6 = (bf16[736,128]{1,0:T(8,128)(2,1)S(1)}, bf16[736,128]{1,0:T(8,128)(2,1)S(1)}, u32[]{:S(2)}, u32[]{:S(2)}) collective-permute-start(bf16[736,128]{1,0:T(8,128)(2,1)S(1)} %collective-permute-done.2.refs_1_), channel_id=1, source_target_pairs={{0,4},{4,8},{8,12},{12,14},{14,10},{10,6},{6,2},{2,0},{1,5},{5,9},... | collective-permute-start | bytes 565256 | tf_op jit(solution)/shard_map/ppermute | solution.py:373
  24.0 5.7 %collective-permute-start.12 = (bf16[736,128]{1,0:T(8,128)(2,1)S(1)}, bf16[736,128]{1,0:T(8,128)(2,1)S(1)}, u32[]{:S(2)}, u32[]{:S(2)}) collective-permute-start(bf16[736,128]{1,0:T(8,128)(2,1)S(1)} %collective-permute-done.2.refs_1_), channel_id=1, source_target_pairs={{0,1},{1,0},{2,3},{3,2},{4,5},{5,4},{6,7},{7,6},{8,9},{9,8},{10,11... | collective-permute-start | bytes 565256 | tf_op jit(solution)/shard_map/ppermute | solution.py:376
  24.7 5.0 %collective-permute-start.13 = (bf16[736,128]{1,0:T(8,128)(2,1)S(1)}, bf16[736,128]{1,0:T(8,128)(2,1)S(1)}, u32[]{:S(2)}, u32[]{:S(2)}) collective-permute-start(bf16[736,128]{1,0:T(8,128)(2,1)S(1)} %collective-permute-done.10.refs_2_), channel_id=1, source_target_pairs={{0,1},{1,0},{2,3},{3,2},{4,5},{5,4},{6,7},{7,6},{8,9},{9,8},{10,11... | collective-permute-start | bytes 565256 | tf_op jit(solution)/shard_map/ppermute | solution.py:376
  28.0 1.7 %collective-permute-start.11 = (bf16[736,128]{1,0:T(8,128)(2,1)S(1)}, bf16[736,128]{1,0:T(8,128)(2,1)S(1)}, u32[]{:S(2)}, u32[]{:S(2)}) collective-permute-start(bf16[736,128]{1,0:T(8,128)(2,1)S(1)} %collective-permute-done.6.refs_0_), channel_id=1, source_target_pairs={{0,1},{1,0},{2,3},{3,2},{4,5},{5,4},{6,7},{7,6},{8,9},{9,8},{10,11... | collective-permute-start | bytes 565256 | tf_op jit(solution)/shard_map/ppermute | solution.py:384
  32.0 2.3 %collective-permute-start.14 = (bf16[720,128]{1,0:T(8,128)(2,1)S(1)}, bf16[720,128]{1,0:T(8,128)(2,1)S(1)}, u32[]{:S(2)}, u32[]{:S(2)}) collective-permute-start(bf16[720,128]{1,0:T(8,128)(2,1)S(1)} %get-tuple-element.66), channel_id=1, source_target_pairs={{0,1},{1,0},{2,3},{3,2},{4,5},{5,4},{6,7},{7,6},{8,9},{9,8},{10,11... | collective-permute-start | bytes 552968 | tf_op jit(solution)/shard_map/ppermute | solution.py:293
  32.5 3.6 %collective-permute-start.15 = (bf16[1440,128]{1,0:T(8,128)(2,1)S(1)}, bf16[1440,128]{1,0:T(8,128)(2,1)S(1)}, u32[]{:S(2)}, u32[]{:S(2)}) collective-permute-start(bf16[1440,128]{1,0:T(8,128)(2,1)S(1)} %get-tuple-element.68), channel_id=1, source_target_pairs={{0,1},{1,0},{2,3},{3,2},{4,5},{5,4},{6,7},{7,6},{8,9},{9,8},{10,11... | collective-permute-start | bytes 1105928 | tf_op jit(solution)/shard_map/ppermute | solution.py:293
  32.6 4.0 %collective-permute-start.16 = (bf16[736,128]{1,0:T(8,128)(2,1)S(1)}, bf16[736,128]{1,0:T(8,128)(2,1)S(1)}, u32[]{:S(2)}, u32[]{:S(2)}) collective-permute-start(bf16[736,128]{1,0:T(8,128)(2,1)S(1)} %shard_map.64.refs_0_), channel_id=1, source_target_pairs={{0,1},{1,0},{2,3},{3,2},{4,5},{5,4},{6,7},{7,6},{8,9},{9,8},{10,11... | collective-permute-start | bytes 565256 | tf_op jit(solution)/shard_map/ppermute | solution.py:385
  34.4 6.7 %collective-permute-start.21 = (bf16[720,128]{1,0:T(8,128)(2,1)S(1)}, bf16[720,128]{1,0:T(8,128)(2,1)S(1)}, u32[]{:S(2)}, u32[]{:S(2)}) collective-permute-start(bf16[720,128]{1,0:T(8,128)(2,1)S(1)} %add_convert_fusion.4), channel_id=1, source_target_pairs={{0,4},{4,8},{8,12},{12,14},{14,10},{10,6},{6,2},{2,0},{1,5},{5,9},... | collective-permute-start | bytes 552968 | tf_op jit(solution)/shard_map/ppermute | solution.py:395
  36.2 6.8 %collective-permute-start.20 = (bf16[720,128]{1,0:T(8,128)(2,1)S(1)}, bf16[720,128]{1,0:T(8,128)(2,1)S(1)}, u32[]{:S(2)}, u32[]{:S(2)}) collective-permute-start(bf16[720,128]{1,0:T(8,128)(2,1)S(1)} %add_convert_fusion.3), channel_id=1, source_target_pairs={{4,0},{8,4},{12,8},{14,12},{10,14},{6,10},{2,6},{0,2},{5,1},{9,5},... | collective-permute-start | bytes 552968 | tf_op jit(solution)/shard_map/ppermute | solution.py:402
  36.6 6.5 %collective-permute-start.19 = (bf16[1440,128]{1,0:T(8,128)(2,1)S(1)}, bf16[1440,128]{1,0:T(8,128)(2,1)S(1)}, u32[]{:S(2)}, u32[]{:S(2)}) collective-permute-start(bf16[1440,128]{1,0:T(8,128)(2,1)S(1)} %get-tuple-element.76), channel_id=1, source_target_pairs={{0,1},{1,0},{2,3},{3,2},{4,5},{5,4},{6,7},{7,6},{8,9},{9,8},{10,11... | collective-permute-start | bytes 1105928 | tf_op jit(solution)/shard_map/ppermute | solution.py:393
  41.1 5.8 %collective-permute-start.23 = (bf16[720,128]{1,0:T(8,128)(2,1)S(1)}, bf16[720,128]{1,0:T(8,128)(2,1)S(1)}, u32[]{:S(2)}, u32[]{:S(2)}) collective-permute-start(bf16[720,128]{1,0:T(8,128)(2,1)S(1)} %add_convert_fusion.2), channel_id=1, source_target_pairs={{0,4},{4,8},{8,12},{12,14},{14,10},{10,6},{6,2},{2,0},{1,5},{5,9},... | collective-permute-start | bytes 552968 | tf_op jit(solution)/shard_map/ppermute | solution.py:395
  42.9 6.0 %collective-permute-start.18 = (bf16[1440,128]{1,0:T(8,128)(2,1)S(1)}, bf16[1440,128]{1,0:T(8,128)(2,1)S(1)}, u32[]{:S(2)}, u32[]{:S(2)}) collective-permute-start(bf16[1440,128]{1,0:T(8,128)(2,1)S(1)} %get-tuple-element.74), channel_id=1, source_target_pairs={{0,1},{1,0},{2,3},{3,2},{4,5},{5,4},{6,7},{7,6},{8,9},{9,8},{10,11... | collective-permute-start | bytes 1105928 | tf_op jit(solution)/shard_map/ppermute | solution.py:393
  43.1 7.1 %collective-permute-start.22 = (bf16[720,128]{1,0:T(8,128)(2,1)S(1)}, bf16[720,128]{1,0:T(8,128)(2,1)S(1)}, u32[]{:S(2)}, u32[]{:S(2)}) collective-permute-start(bf16[720,128]{1,0:T(8,128)(2,1)S(1)} %shard_map.73), channel_id=1, source_target_pairs={{4,0},{8,4},{12,8},{14,12},{10,14},{6,10},{2,6},{0,2},{5,1},{9,5},... | collective-permute-start | bytes 552968 | tf_op jit(solution)/shard_map/ppermute | solution.py:402
  47.1 5.6 %collective-permute-start.25 = (bf16[720,128]{1,0:T(8,128)(2,1)S(1)}, bf16[720,128]{1,0:T(8,128)(2,1)S(1)}, u32[]{:S(2)}, u32[]{:S(2)}) collective-permute-start(bf16[720,128]{1,0:T(8,128)(2,1)S(1)} %add_convert_fusion.1), channel_id=1, source_target_pairs={{0,4},{4,8},{8,12},{12,14},{14,10},{10,6},{6,2},{2,0},{1,5},{5,9},... | collective-permute-start | bytes 552968 | tf_op jit(solution)/shard_map/ppermute | solution.py:395
  48.9 7.7 %collective-permute-start.17 = (bf16[720,128]{1,0:T(8,128)(2,1)S(1)}, bf16[720,128]{1,0:T(8,128)(2,1)S(1)}, u32[]{:S(2)}, u32[]{:S(2)}) collective-permute-start(bf16[720,128]{1,0:T(8,128)(2,1)S(1)} %get-tuple-element.72), channel_id=1, source_target_pairs={{0,1},{1,0},{2,3},{3,2},{4,5},{5,4},{6,7},{7,6},{8,9},{9,8},{10,11... | collective-permute-start | bytes 552968 | tf_op jit(solution)/shard_map/ppermute | solution.py:398
  50.3 6.3 %collective-permute-start.24 = (bf16[720,128]{1,0:T(8,128)(2,1)S(1)}, bf16[720,128]{1,0:T(8,128)(2,1)S(1)}, u32[]{:S(2)}, u32[]{:S(2)}) collective-permute-start(bf16[720,128]{1,0:T(8,128)(2,1)S(1)} %shard_map.74), channel_id=1, source_target_pairs={{4,0},{8,4},{12,8},{14,12},{10,14},{6,10},{2,6},{0,2},{5,1},{9,5},... | collective-permute-start | bytes 552968 | tf_op jit(solution)/shard_map/ppermute | solution.py:402
  52.7 5.6 %collective-permute-start.26 = (bf16[720,128]{1,0:T(8,128)(2,1)S(1)}, bf16[720,128]{1,0:T(8,128)(2,1)S(1)}, u32[]{:S(2)}, u32[]{:S(2)}) collective-permute-start(bf16[720,128]{1,0:T(8,128)(2,1)S(1)} %add_convert_fusion), channel_id=1, source_target_pairs={{0,4},{4,8},{8,12},{12,14},{14,10},{10,6},{6,2},{2,0},{1,5},{5,9},... | collective-permute-start | bytes 552968 | tf_op jit(solution)/shard_map/ppermute | solution.py:395

commit v19 on v17

--- a/solution.py
+++ b/solution.py
@@ -83,9 +83,12 @@
     )(*[pltpu.with_memory_space_constraint(a, pltpu.HBM) for a in args])
 
 
+PIECES = 3
+
+
 def pieces(hidden):
-    first = -(-hidden // 256) * 128
-    return ((0, first), (first, hidden))
+    step = -(-hidden // (128 * PIECES)) * 128
+    return [(min(i * step, hidden), min((i + 1) * step, hidden)) for i in range(PIECES)]
 
 
 def turn_kernel(after_this, gate_in, up_in, gate, up, gate_buf, up_buf, sems):
@@ -108,7 +111,7 @@
         out_shape=[in_vmem((width, hidden))] * 2,
         in_specs=[pl.BlockSpec(memory_space=pltpu.SMEM)] + [pl.BlockSpec(memory_space=pltpu.HBM)] * 2,
         out_specs=[pl.BlockSpec(memory_space=pltpu.VMEM)] * 2,
-        scratch_shapes=[pltpu.VMEM((hidden, width), jnp.bfloat16)] * 2 + [pltpu.SemaphoreType.DMA((2, 2))],
+        scratch_shapes=[pltpu.VMEM((hidden, width), jnp.bfloat16)] * 2 + [pltpu.SemaphoreType.DMA((2, PIECES))],
         compiler_params=pltpu.CompilerParams(vmem_limit_bytes=32 << 20),
         cost_estimate=pl.CostEstimate(flops=0, bytes_accessed=8 * hidden * width, transcendentals=0),
     )(after_this, *[pltpu.with_memory_space_constraint(w, pltpu.HBM) for w in weights])
@@ -145,7 +148,7 @@
         out_shape=[in_vmem((hidden, width // 2))] * 2,
         in_specs=[pl.BlockSpec(memory_space=pltpu.SMEM), pl.BlockSpec(memory_space=pltpu.HBM)],
         out_specs=[pl.BlockSpec(memory_space=pltpu.VMEM)] * 2,
-        scratch_shapes=[pltpu.VMEM((hidden, width), jnp.bfloat16), pltpu.SemaphoreType.DMA((2,))],
+        scratch_shapes=[pltpu.VMEM((hidden, width), jnp.bfloat16), pltpu.SemaphoreType.DMA((PIECES,))],
         compiler_params=pltpu.CompilerParams(vmem_limit_bytes=32 << 20),
         cost_estimate=pl.CostEstimate(flops=0, bytes_accessed=8 * hidden * width, transcendentals=0),
     )(place, pltpu.with_memory_space_constraint(w_down, pltpu.HBM))

time: 58.7 us -> 58.6 us (level)
  no operation moved by 1% of the time
where the time goes in v19:
time: 58.6 us; the launch traced here: 58.5 us
  Pallas kernels  23.2 us (40%)
  starting transfers between devices  19.2 us (33%)
  waiting for transfers between devices  15.4 us (26%)
    pallas_call x6, Pallas kernels, call(): pl.pallas_call(kernel, out_shape=out_shape, in_specs=[pl.BlockSpec(memory...  13.5 us
    ppermute x4, waiting for transfers between devices, ring_body(): behind = lax.ppermute(to_ahead, 'ep', ahead)  8.91 us
    ppermute x4, starting transfers between devices, ring_body(): behind = lax.ppermute(to_ahead, 'ep', ahead)  7.15 us
    ppermute x3, starting transfers between devices, ring_body(): came[k] = lax.ppermute(came[k - 1], 'ep', ahead)  5.64 us
    pallas_call x1, Pallas kernels, turn_weights(): pl.pallas_call(turn_kernel, out_shape=[in_vmem((width, hidden))] * 2, in_...  4.68 us
    ppermute x3, waiting for transfers between devices, ring_body(): front = lax.ppermute(to_back, 'ep', back)  3.32 us
    ppermute x1, starting transfers between devices, ring_body(): came[1] = lax.ppermute(packed, 'ep', ahead)  3.08 us
    pallas_call x1, Pallas kernels, halve_weights(): pl.pallas_call(halve_kernel, out_shape=[in_vmem((hidden, width // 2))] *...  2.99 us
  transfers between devices with their start and end apart: 27, of which 10 were waited for; matrix products, arithmetic and copies ran while one was open for 1% of the time, Pallas kernels for 33%

profile of v19, /device:TPU:0, one launch (start us, length us, event | category | flops | bytes accessed | tf_op | source)
XLA Modules:
  0.0 58.5 jit_solution(16680668576193969746)
XLA Ops:
  0.0 1.1 %shard_map.64.refs_0_ = bf16[736,128]{1,0:T(8,128)(2,1)S(1)} custom-call(bf16[64,1440]{1,0:T(8,128)(2,1)} %tokens_in.1, s32[4,64]{1,0:T(4,128)} %bitcast.14, f32[4,64]{1,0:T(4,128)} %bitcast.15), custom_call_target="tpu_custom_call" | custom-call | tf_op jit(solution)/shard_map/pallas_call | solution.py:76
  1.1 3.1 %collective-permute-start = (bf16[736,128]{1,0:T(8,128)(2,1)S(1)}, bf16[736,128]{1,0:T(8,128)(2,1)S(1)}, u32[]{:S(2)}, u32[]{:S(2)}) collective-permute-start(bf16[736,128]{1,0:T(8,128)(2,1)S(1)} %shard_map.64.refs_0_), channel_id=1, source_target_pairs={{0,4},{4,8},{8,12},{12,14},{14,10},{10,6},{6,2},{2,0},{1,5},{5,9},... | collective-permute-start | bytes 565256 | tf_op jit(solution)/shard_map/ppermute | solution.py:369
  4.2 0.0 collective-permute-start.3
  4.2 0.1 pad_add_fusion.after_this.place
  4.3 4.7 %shard_map.65 = (bf16[2880,720]{1,0:T(8,128)(2,1)S(1)}, bf16[2880,720]{1,0:T(8,128)(2,1)S(1)}) custom-call(s32[2]{0:T(128)S(1)} %pad_add_fusion.after_this.place, bf16[720,2880]{1,0:T(8,128)(2,1)} %bitcast.11, bf16[720,2880]{1,0:T(8,128)(2,1)} %bitcast.12), custom_call_target="tpu_custom_call" | custom-call | bytes 16588800 | tf_op jit(solution)/shard_map/pallas_call | solution.py:109
  8.9 0.0 collective-permute-done.refs_0_
  8.9 2.1 %collective-permute-start.1 = (bf16[736,128]{1,0:T(8,128)(2,1)S(1)}, bf16[736,128]{1,0:T(8,128)(2,1)S(1)}, u32[]{:S(2)}, u32[]{:S(2)}) collective-permute-start(bf16[736,128]{1,0:T(8,128)(2,1)S(1)} %collective-permute-done.refs_0_), channel_id=1, source_target_pairs={{0,4},{4,8},{8,12},{12,14},{14,10},{10,6},{6,2},{2,0},{1,5},{5,9},... | collective-permute-start | bytes 565256 | tf_op jit(solution)/shard_map/ppermute | solution.py:374
  11.0 0.0 collective-permute-done.3.refs_1_
  11.0 0.0 collective-permute-start.7
  11.0 0.0 collective-permute-start.4
  11.0 0.5 collective-permute-start.5
  11.5 3.0 %shard_map.66 = (bf16[720,1440]{1,0:T(8,128)(2,1)S(1)}, bf16[720,1440]{1,0:T(8,128)(2,1)S(1)}) custom-call(s32[2]{0:T(128)S(1)} %pad_add_fusion.after_this.place, bf16[720,2880]{1,0:T(8,128)(2,1)} %bitcast.13), custom_call_target="tpu_custom_call" | custom-call | bytes 16588800 | tf_op jit(solution)/shard_map/pallas_call | solution.py:146
  14.5 0.6 %collective-permute-done.1.refs_0_ = bf16[736,128]{1,0:T(8,128)(2,1)S(1)} collective-permute-done((bf16[736,128]{1,0:T(8,128)(2,1)S(1)}, bf16[736,128]{1,0:T(8,128)(2,1)S(1)}, u32[]{:S(2)}, u32[]{:S(2)}) %collective-permute-start.1) | collective-permute-done | bytes 188448 | tf_op jit(solution)/shard_map/ppermute | solution.py:374
  15.2 1.7 %collective-permute-start.2 = (bf16[736,128]{1,0:T(8,128)(2,1)S(1)}, bf16[736,128]{1,0:T(8,128)(2,1)S(1)}, u32[]{:S(2)}, u32[]{:S(2)}) collective-permute-start(bf16[736,128]{1,0:T(8,128)(2,1)S(1)} %collective-permute-done.1.refs_0_), channel_id=1, source_target_pairs={{0,4},{4,8},{8,12},{12,14},{14,10},{10,6},{6,2},{2,0},{1,5},{5,9},... | collective-permute-start | bytes 565256 | tf_op jit(solution)/shard_map/ppermute | solution.py:374
  16.9 0.0 collective-permute-done.7.refs_1_
  16.9 0.3 collective-permute-start.10
  17.2 0.0 collective-permute-done.4.refs_2_
  17.2 0.3 collective-permute-start.9
  17.5 2.8 %shard_map.67 = (bf16[1440,128]{1,0:T(8,128)(2,1)S(1)}, bf16[1440,128]{1,0:T(8,128)(2,1)S(1)}) custom-call(s32[2]{0:T(128)S(1)} %pad_add_fusion.after_this.place, bf16[736,128]{1,0:T(8,128)(2,1)S(1)} %collective-permute-done.refs_0_, bf16[736,128]{1,0:T(8,128)(2,1)S(1)} %collective-permute-done.3.refs_1_, ...), custom_call_target="tpu_custom_call" | custom-call | flops 1592524800 | bytes 12441600 | tf_op jit(solution)/shard_map/pallas_call | solution.py:245
  20.3 1.1 %collective-permute-done.2.refs_1_ = bf16[736,128]{1,0:T(8,128)(2,1)S(1)} collective-permute-done((bf16[736,128]{1,0:T(8,128)(2,1)S(1)}, bf16[736,128]{1,0:T(8,128)(2,1)S(1)}, u32[]{:S(2)}, u32[]{:S(2)}) %collective-permute-start.2) | collective-permute-done | bytes 188448 | tf_op jit(solution)/shard_map/ppermute | solution.py:374
  21.4 1.8 %collective-permute-start.6 = (bf16[736,128]{1,0:T(8,128)(2,1)S(1)}, bf16[736,128]{1,0:T(8,128)(2,1)S(1)}, u32[]{:S(2)}, u32[]{:S(2)}) collective-permute-start(bf16[736,128]{1,0:T(8,128)(2,1)S(1)} %collective-permute-done.2.refs_1_), channel_id=1, source_target_pairs={{0,4},{4,8},{8,12},{12,14},{14,10},{10,6},{6,2},{2,0},{1,5},{5,9},... | collective-permute-start | bytes 565256 | tf_op jit(solution)/shard_map/ppermute | solution.py:374
  23.3 0.8 %collective-permute-done.10.refs_2_ = bf16[736,128]{1,0:T(8,128)(2,1)S(1)} collective-permute-done((bf16[736,128]{1,0:T(8,128)(2,1)S(1)}, bf16[736,128]{1,0:T(8,128)(2,1)S(1)}, u32[]{:S(2)}, u32[]{:S(2)}) %collective-permute-start.10) | collective-permute-done | bytes 188448 | tf_op jit(solution)/shard_map/ppermute | solution.py:376
  24.1 0.0 collective-permute-start.13
  24.1 0.0 collective-permute-done.8.refs_2_
  24.1 2.8 %shard_map.68 = (bf16[1440,128]{1,0:T(8,128)(2,1)S(1)}, bf16[1440,128]{1,0:T(8,128)(2,1)S(1)}) custom-call(s32[2]{0:T(128)S(1)} %pad_add_fusion.after_this.place, bf16[736,128]{1,0:T(8,128)(2,1)S(1)} %collective-permute-done.1.refs_0_, bf16[736,128]{1,0:T(8,128)(2,1)S(1)} %collective-permute-done.7.refs_1_, ...), custom_call_target="tpu_custom_call" | custom-call | flops 1592524800 | bytes 12441600 | tf_op jit(solution)/shard_map/pallas_call | solution.py:245
  26.9 0.5 collective-permute-done.6.refs_0_
  27.4 0.1 collective-permute-start.11
  27.4 1.7 %shard_map.69 = (f32[192,720]{1,0:T(8,128)S(1)}, f32[192,720]{1,0:T(8,128)S(1)}) custom-call(s32[2]{0:T(128)S(1)} %pad_add_fusion.after_this.place, bf16[736,128]{1,0:T(8,128)(2,1)S(1)} %collective-permute-done.6.refs_0_, bf16[736,128]{1,0:T(8,128)(2,1)S(1)} %collective-permute-done.2.refs_1_, bf16[736,128]{1,0:T(8,128)(2,1)S(1)} %collective-permute-done.10.refs_2_, ...), custom_call_target="tpu_custom_call" | custom-call | flops 796262400 | bytes 6220800 | tf_op jit(solution)/shard_map/pallas_call | solution.py:245
  29.1 0.0 collective-permute-done.13.refs_5_
  29.1 0.0 collective-permute-done.11.refs_3_
  29.1 2.3 %shard_map.70 = (bf16[192,720]{1,0:T(8,128)(2,1)S(1)}, bf16[720,128]{1,0:T(8,128)(2,1)S(1)}, bf16[1440,128]{1,0:T(8,128)(2,1)S(1)}) custom-call(s32[2]{0:T(128)S(1)} %pad_add_fusion.after_this.place, bf16[736,128]{1,0:T(8,128)(2,1)S(1)} %collective-permute-done.6.refs_0_, bf16[736,128]{1,0:T(8,128)(2,1)S(1)} %collective-permute-done.2.refs_1_, ...), custom_call_target="tpu_custom_call" | custom-call | flops 1194393600 | bytes 9331200 | tf_op jit(solution)/shard_map/pallas_call | solution.py:245
  31.4 0.5 collective-permute-start.14
  31.9 0.1 collective-permute-start.15
  32.0 0.4 collective-permute-start.16
  32.4 1.3 %shard_map.71 = (bf16[720,128]{1,0:T(8,128)(2,1)S(1)}, bf16[1440,128]{1,0:T(8,128)(2,1)S(1)}) custom-call(s32[2]{0:T(128)S(1)} %pad_add_fusion.after_this.place, bf16[736,128]{1,0:T(8,128)(2,1)S(1)} %collective-permute-done.6.refs_0_, bf16[736,128]{1,0:T(8,128)(2,1)S(1)} %collective-permute-done.2.refs_1_, ...), custom_call_target="tpu_custom_call" | custom-call | flops 398131200 | bytes 3110400 | tf_op jit(solution)/shard_map/pallas_call | solution.py:245
  33.7 0.1 add_convert_fusion.4
  33.8 1.8 %collective-permute-start.21 = (bf16[720,128]{1,0:T(8,128)(2,1)S(1)}, bf16[720,128]{1,0:T(8,128)(2,1)S(1)}, u32[]{:S(2)}, u32[]{:S(2)}) collective-permute-start(bf16[720,128]{1,0:T(8,128)(2,1)S(1)} %add_convert_fusion.4), channel_id=1, source_target_pairs={{0,4},{4,8},{8,12},{12,14},{14,10},{10,6},{6,2},{2,0},{1,5},{5,9},... | collective-permute-start | bytes 552968 | tf_op jit(solution)/shard_map/ppermute | solution.py:396
  35.6 0.1 add_convert_fusion.3
  35.6 0.3 collective-permute-start.20
  36.0 0.0 collective-permute-start.19
  36.0 0.0 collective-permute-done.16.refs_1_
  36.0 2.7 %shard_map.72 = (bf16[720,128]{1,0:T(8,128)(2,1)S(1)}, bf16[720,128]{1,0:T(8,128)(2,1)S(1)}) custom-call(s32[2]{0:T(128)S(1)} %pad_add_fusion.after_this.place, bf16[736,128]{1,0:T(8,128)(2,1)S(1)} %shard_map.64.refs_0_, bf16[736,128]{1,0:T(8,128)(2,1)S(1)} %collective-permute-done.16.refs_1_, ...), custom_call_target="tpu_custom_call" | custom-call | flops 1592524800 | bytes 12441600 | tf_op jit(solution)/shard_map/pallas_call | solution.py:245
  38.7 1.8 %collective-permute-done.21 = bf16[720,128]{1,0:T(8,128)(2,1)S(1)} collective-permute-done((bf16[720,128]{1,0:T(8,128)(2,1)S(1)}, bf16[720,128]{1,0:T(8,128)(2,1)S(1)}, u32[]{:S(2)}, u32[]{:S(2)}) %collective-permute-start.21) | collective-permute-done | bytes 184352 | tf_op jit(solution)/shard_map/ppermute | solution.py:396
  40.4 0.1 add_convert_fusion.2
  40.5 1.8 %collective-permute-start.23 = (bf16[720,128]{1,0:T(8,128)(2,1)S(1)}, bf16[720,128]{1,0:T(8,128)(2,1)S(1)}, u32[]{:S(2)}, u32[]{:S(2)}) collective-permute-start(bf16[720,128]{1,0:T(8,128)(2,1)S(1)} %add_convert_fusion.2), channel_id=1, source_target_pairs={{0,4},{4,8},{8,12},{12,14},{14,10},{10,6},{6,2},{2,0},{1,5},{5,9},... | collective-permute-start | bytes 552968 | tf_op jit(solution)/shard_map/ppermute | solution.py:396
  42.3 0.1 collective-permute-start.18
  42.4 0.0 collective-permute-done.20.refs_2_
  42.4 0.0 collective-permute-done.19
  42.5 0.1 shard_map.73
  42.5 0.3 collective-permute-start.22
  42.9 3.5 %collective-permute-done.23 = bf16[720,128]{1,0:T(8,128)(2,1)S(1)} collective-permute-done((bf16[720,128]{1,0:T(8,128)(2,1)S(1)}, bf16[720,128]{1,0:T(8,128)(2,1)S(1)}, u32[]{:S(2)}, u32[]{:S(2)}) %collective-permute-start.23) | collective-permute-done | bytes 184352 | tf_op jit(solution)/shard_map/ppermute | solution.py:396
  46.4 0.1 add_convert_fusion.1
  46.4 1.8 %collective-permute-start.25 = (bf16[720,128]{1,0:T(8,128)(2,1)S(1)}, bf16[720,128]{1,0:T(8,128)(2,1)S(1)}, u32[]{:S(2)}, u32[]{:S(2)}) collective-permute-start(bf16[720,128]{1,0:T(8,128)(2,1)S(1)} %add_convert_fusion.1), channel_id=1, source_target_pairs={{0,4},{4,8},{8,12},{12,14},{14,10},{10,6},{6,2},{2,0},{1,5},{5,9},... | collective-permute-start | bytes 552968 | tf_op jit(solution)/shard_map/ppermute | solution.py:396
  48.2 0.1 collective-permute-start.17
  48.4 1.2 %collective-permute-done.22.refs_2_ = bf16[720,128]{1,0:T(8,128)(2,1)S(1)} collective-permute-done((bf16[720,128]{1,0:T(8,128)(2,1)S(1)}, bf16[720,128]{1,0:T(8,128)(2,1)S(1)}, u32[]{:S(2)}, u32[]{:S(2)}) %collective-permute-start.22) | collective-permute-done | bytes 184352 | tf_op jit(solution)/shard_map/ppermute | solution.py:403
  49.6 0.1 shard_map.74
  49.7 0.3 collective-permute-start.24
  50.0 2.0 %collective-permute-done.25 = bf16[720,128]{1,0:T(8,128)(2,1)S(1)} collective-permute-done((bf16[720,128]{1,0:T(8,128)(2,1)S(1)}, bf16[720,128]{1,0:T(8,128)(2,1)S(1)}, u32[]{:S(2)}, u32[]{:S(2)}) %collective-permute-start.25) | collective-permute-done | bytes 184352 | tf_op jit(solution)/shard_map/ppermute | solution.py:396
  52.0 0.1 add_convert_fusion
  52.1 1.8 %collective-permute-start.26 = (bf16[720,128]{1,0:T(8,128)(2,1)S(1)}, bf16[720,128]{1,0:T(8,128)(2,1)S(1)}, u32[]{:S(2)}, u32[]{:S(2)}) collective-permute-start(bf16[720,128]{1,0:T(8,128)(2,1)S(1)} %add_convert_fusion), channel_id=1, source_target_pairs={{0,4},{4,8},{8,12},{12,14},{14,10},{10,6},{6,2},{2,0},{1,5},{5,9},... | collective-permute-start | bytes 552968 | tf_op jit(solution)/shard_map/ppermute | solution.py:396
  53.9 2.1 %collective-permute-done.24.refs_2_ = bf16[720,128]{1,0:T(8,128)(2,1)S(1)} collective-permute-done((bf16[720,128]{1,0:T(8,128)(2,1)S(1)}, bf16[720,128]{1,0:T(8,128)(2,1)S(1)}, u32[]{:S(2)}, u32[]{:S(2)}) %collective-permute-start.24) | collective-permute-done | bytes 184352 | tf_op jit(solution)/shard_map/ppermute | solution.py:403
  56.0 0.1 shard_map.75.a
  56.0 1.7 %collective-permute-done.26.b = bf16[720,128]{1,0:T(8,128)(2,1)S(1)} collective-permute-done((bf16[720,128]{1,0:T(8,128)(2,1)S(1)}, bf16[720,128]{1,0:T(8,128)(2,1)S(1)}, u32[]{:S(2)}, u32[]{:S(2)}) %collective-permute-start.26) | collective-permute-done | bytes 184352 | tf_op jit(solution)/shard_map/ppermute | solution.py:396
  57.7 0.8 %shard_map.76 = bf16[64,1440]{1,0:T(8,128)(2,1)} custom-call(bf16[720,128]{1,0:T(8,128)(2,1)S(1)} %shard_map.75.a, bf16[720,128]{1,0:T(8,128)(2,1)S(1)} %collective-permute-done.26.b), custom_call_target="tpu_custom_call" | custom-call | tf_op jit(solution)/shard_map/pallas_call | solution.py:331
  (13 shorter events, 0.1 us)
Async XLA Ops:
  1.1 7.8 %collective-permute-start = (bf16[736,128]{1,0:T(8,128)(2,1)S(1)}, bf16[736,128]{1,0:T(8,128)(2,1)S(1)}, u32[]{:S(2)}, u32[]{:S(2)}) collective-permute-start(bf16[736,128]{1,0:T(8,128)(2,1)S(1)} %shard_map.64.refs_0_), channel_id=1, source_target_pairs={{0,4},{4,8},{8,12},{12,14},{14,10},{10,6},{6,2},{2,0},{1,5},{5,9},... | collective-permute-start | bytes 565256 | tf_op jit(solution)/shard_map/ppermute | solution.py:369
  4.2 6.9 %collective-permute-start.3 = (bf16[736,128]{1,0:T(8,128)(2,1)S(1)}, bf16[736,128]{1,0:T(8,128)(2,1)S(1)}, u32[]{:S(2)}, u32[]{:S(2)}) collective-permute-start(bf16[736,128]{1,0:T(8,128)(2,1)S(1)} %shard_map.64.refs_0_), channel_id=1, source_target_pairs={{4,0},{8,4},{12,8},{14,12},{10,14},{6,10},{2,6},{0,2},{5,1},{9,5},... | collective-permute-start | bytes 565256 | tf_op jit(solution)/shard_map/ppermute | solution.py:370
  8.9 6.2 %collective-permute-start.1 = (bf16[736,128]{1,0:T(8,128)(2,1)S(1)}, bf16[736,128]{1,0:T(8,128)(2,1)S(1)}, u32[]{:S(2)}, u32[]{:S(2)}) collective-permute-start(bf16[736,128]{1,0:T(8,128)(2,1)S(1)} %collective-permute-done.refs_0_), channel_id=1, source_target_pairs={{0,4},{4,8},{8,12},{12,14},{14,10},{10,6},{6,2},{2,0},{1,5},{5,9},... | collective-permute-start | bytes 565256 | tf_op jit(solution)/shard_map/ppermute | solution.py:374
  11.0 5.9 %collective-permute-start.7 = (bf16[736,128]{1,0:T(8,128)(2,1)S(1)}, bf16[736,128]{1,0:T(8,128)(2,1)S(1)}, u32[]{:S(2)}, u32[]{:S(2)}) collective-permute-start(bf16[736,128]{1,0:T(8,128)(2,1)S(1)} %collective-permute-done.3.refs_1_), channel_id=1, source_target_pairs={{4,0},{8,4},{12,8},{14,12},{10,14},{6,10},{2,6},{0,2},{5,1},{9,5},... | collective-permute-start | bytes 565256 | tf_op jit(solution)/shard_map/ppermute | solution.py:376
  11.0 6.2 %collective-permute-start.4 = (bf16[736,128]{1,0:T(8,128)(2,1)S(1)}, bf16[736,128]{1,0:T(8,128)(2,1)S(1)}, u32[]{:S(2)}, u32[]{:S(2)}) collective-permute-start(bf16[736,128]{1,0:T(8,128)(2,1)S(1)} %collective-permute-done.refs_0_), channel_id=1, source_target_pairs={{0,1},{1,0},{2,3},{3,2},{4,5},{5,4},{6,7},{7,6},{8,9},{9,8},{10,11... | collective-permute-start | bytes 565256 | tf_op jit(solution)/shard_map/ppermute | solution.py:377
  11.0 6.5 %collective-permute-start.5 = (bf16[736,128]{1,0:T(8,128)(2,1)S(1)}, bf16[736,128]{1,0:T(8,128)(2,1)S(1)}, u32[]{:S(2)}, u32[]{:S(2)}) collective-permute-start(bf16[736,128]{1,0:T(8,128)(2,1)S(1)} %collective-permute-done.3.refs_1_), channel_id=1, source_target_pairs={{0,1},{1,0},{2,3},{3,2},{4,5},{5,4},{6,7},{7,6},{8,9},{9,8},{10,11... | collective-permute-start | bytes 565256 | tf_op jit(solution)/shard_map/ppermute | solution.py:377
  15.2 6.2 %collective-permute-start.2 = (bf16[736,128]{1,0:T(8,128)(2,1)S(1)}, bf16[736,128]{1,0:T(8,128)(2,1)S(1)}, u32[]{:S(2)}, u32[]{:S(2)}) collective-permute-start(bf16[736,128]{1,0:T(8,128)(2,1)S(1)} %collective-permute-done.1.refs_0_), channel_id=1, source_target_pairs={{0,4},{4,8},{8,12},{12,14},{14,10},{10,6},{6,2},{2,0},{1,5},{5,9},... | collective-permute-start | bytes 565256 | tf_op jit(solution)/shard_map/ppermute | solution.py:374
  16.9 7.2 %collective-permute-start.8 = (bf16[736,128]{1,0:T(8,128)(2,1)S(1)}, bf16[736,128]{1,0:T(8,128)(2,1)S(1)}, u32[]{:S(2)}, u32[]{:S(2)}) collective-permute-start(bf16[736,128]{1,0:T(8,128)(2,1)S(1)} %collective-permute-done.1.refs_0_), channel_id=1, source_target_pairs={{0,1},{1,0},{2,3},{3,2},{4,5},{5,4},{6,7},{7,6},{8,9},{9,8},{10,11... | collective-permute-start | bytes 565256 | tf_op jit(solution)/shard_map/ppermute | solution.py:377
  16.9 7.1 %collective-permute-start.10 = (bf16[736,128]{1,0:T(8,128)(2,1)S(1)}, bf16[736,128]{1,0:T(8,128)(2,1)S(1)}, u32[]{:S(2)}, u32[]{:S(2)}) collective-permute-start(bf16[736,128]{1,0:T(8,128)(2,1)S(1)} %collective-permute-done.7.refs_1_), channel_id=1, source_target_pairs={{4,0},{8,4},{12,8},{14,12},{10,14},{6,10},{2,6},{0,2},{5,1},{9,5},... | collective-permute-start | bytes 565256 | tf_op jit(solution)/shard_map/ppermute | solution.py:376
  17.2 6.9 %collective-permute-start.9 = (bf16[736,128]{1,0:T(8,128)(2,1)S(1)}, bf16[736,128]{1,0:T(8,128)(2,1)S(1)}, u32[]{:S(2)}, u32[]{:S(2)}) collective-permute-start(bf16[736,128]{1,0:T(8,128)(2,1)S(1)} %collective-permute-done.7.refs_1_), channel_id=1, source_target_pairs={{0,1},{1,0},{2,3},{3,2},{4,5},{5,4},{6,7},{7,6},{8,9},{9,8},{10,11... | collective-permute-start | bytes 565256 | tf_op jit(solution)/shard_map/ppermute | solution.py:377
  21.4 5.9 %collective-permute-start.6 = (bf16[736,128]{1,0:T(8,128)(2,1)S(1)}, bf16[736,128]{1,0:T(8,128)(2,1)S(1)}, u32[]{:S(2)}, u32[]{:S(2)}) collective-permute-start(bf16[736,128]{1,0:T(8,128)(2,1)S(1)} %collective-permute-done.2.refs_1_), channel_id=1, source_target_pairs={{0,4},{4,8},{8,12},{12,14},{14,10},{10,6},{6,2},{2,0},{1,5},{5,9},... | collective-permute-start | bytes 565256 | tf_op jit(solution)/shard_map/ppermute | solution.py:374
  23.3 5.9 %collective-permute-start.12 = (bf16[736,128]{1,0:T(8,128)(2,1)S(1)}, bf16[736,128]{1,0:T(8,128)(2,1)S(1)}, u32[]{:S(2)}, u32[]{:S(2)}) collective-permute-start(bf16[736,128]{1,0:T(8,128)(2,1)S(1)} %collective-permute-done.2.refs_1_), channel_id=1, source_target_pairs={{0,1},{1,0},{2,3},{3,2},{4,5},{5,4},{6,7},{7,6},{8,9},{9,8},{10,11... | collective-permute-start | bytes 565256 | tf_op jit(solution)/shard_map/ppermute | solution.py:377
  24.1 5.0 %collective-permute-start.13 = (bf16[736,128]{1,0:T(8,128)(2,1)S(1)}, bf16[736,128]{1,0:T(8,128)(2,1)S(1)}, u32[]{:S(2)}, u32[]{:S(2)}) collective-permute-start(bf16[736,128]{1,0:T(8,128)(2,1)S(1)} %collective-permute-done.10.refs_2_), channel_id=1, source_target_pairs={{0,1},{1,0},{2,3},{3,2},{4,5},{5,4},{6,7},{7,6},{8,9},{9,8},{10,11... | collective-permute-start | bytes 565256 | tf_op jit(solution)/shard_map/ppermute | solution.py:377
  27.4 1.7 %collective-permute-start.11 = (bf16[736,128]{1,0:T(8,128)(2,1)S(1)}, bf16[736,128]{1,0:T(8,128)(2,1)S(1)}, u32[]{:S(2)}, u32[]{:S(2)}) collective-permute-start(bf16[736,128]{1,0:T(8,128)(2,1)S(1)} %collective-permute-done.6.refs_0_), channel_id=1, source_target_pairs={{0,1},{1,0},{2,3},{3,2},{4,5},{5,4},{6,7},{7,6},{8,9},{9,8},{10,11... | collective-permute-start | bytes 565256 | tf_op jit(solution)/shard_map/ppermute | solution.py:385
  31.4 2.3 %collective-permute-start.14 = (bf16[720,128]{1,0:T(8,128)(2,1)S(1)}, bf16[720,128]{1,0:T(8,128)(2,1)S(1)}, u32[]{:S(2)}, u32[]{:S(2)}) collective-permute-start(bf16[720,128]{1,0:T(8,128)(2,1)S(1)} %get-tuple-element.66), channel_id=1, source_target_pairs={{0,1},{1,0},{2,3},{3,2},{4,5},{5,4},{6,7},{7,6},{8,9},{9,8},{10,11... | collective-permute-start | bytes 552968 | tf_op jit(solution)/shard_map/ppermute | solution.py:294
  31.9 3.6 %collective-permute-start.15 = (bf16[1440,128]{1,0:T(8,128)(2,1)S(1)}, bf16[1440,128]{1,0:T(8,128)(2,1)S(1)}, u32[]{:S(2)}, u32[]{:S(2)}) collective-permute-start(bf16[1440,128]{1,0:T(8,128)(2,1)S(1)} %get-tuple-element.68), channel_id=1, source_target_pairs={{0,1},{1,0},{2,3},{3,2},{4,5},{5,4},{6,7},{7,6},{8,9},{9,8},{10,11... | collective-permute-start | bytes 1105928 | tf_op jit(solution)/shard_map/ppermute | solution.py:294
  32.0 4.0 %collective-permute-start.16 = (bf16[736,128]{1,0:T(8,128)(2,1)S(1)}, bf16[736,128]{1,0:T(8,128)(2,1)S(1)}, u32[]{:S(2)}, u32[]{:S(2)}) collective-permute-start(bf16[736,128]{1,0:T(8,128)(2,1)S(1)} %shard_map.64.refs_0_), channel_id=1, source_target_pairs={{0,1},{1,0},{2,3},{3,2},{4,5},{5,4},{6,7},{7,6},{8,9},{9,8},{10,11... | collective-permute-start | bytes 565256 | tf_op jit(solution)/shard_map/ppermute | solution.py:386
  33.8 6.7 %collective-permute-start.21 = (bf16[720,128]{1,0:T(8,128)(2,1)S(1)}, bf16[720,128]{1,0:T(8,128)(2,1)S(1)}, u32[]{:S(2)}, u32[]{:S(2)}) collective-permute-start(bf16[720,128]{1,0:T(8,128)(2,1)S(1)} %add_convert_fusion.4), channel_id=1, source_target_pairs={{0,4},{4,8},{8,12},{12,14},{14,10},{10,6},{6,2},{2,0},{1,5},{5,9},... | collective-permute-start | bytes 552968 | tf_op jit(solution)/shard_map/ppermute | solution.py:396
  35.6 6.8 %collective-permute-start.20 = (bf16[720,128]{1,0:T(8,128)(2,1)S(1)}, bf16[720,128]{1,0:T(8,128)(2,1)S(1)}, u32[]{:S(2)}, u32[]{:S(2)}) collective-permute-start(bf16[720,128]{1,0:T(8,128)(2,1)S(1)} %add_convert_fusion.3), channel_id=1, source_target_pairs={{4,0},{8,4},{12,8},{14,12},{10,14},{6,10},{2,6},{0,2},{5,1},{9,5},... | collective-permute-start | bytes 552968 | tf_op jit(solution)/shard_map/ppermute | solution.py:403
  36.0 6.5 %collective-permute-start.19 = (bf16[1440,128]{1,0:T(8,128)(2,1)S(1)}, bf16[1440,128]{1,0:T(8,128)(2,1)S(1)}, u32[]{:S(2)}, u32[]{:S(2)}) collective-permute-start(bf16[1440,128]{1,0:T(8,128)(2,1)S(1)} %get-tuple-element.76), channel_id=1, source_target_pairs={{0,1},{1,0},{2,3},{3,2},{4,5},{5,4},{6,7},{7,6},{8,9},{9,8},{10,11... | collective-permute-start | bytes 1105928 | tf_op jit(solution)/shard_map/ppermute | solution.py:394
  40.5 5.8 %collective-permute-start.23 = (bf16[720,128]{1,0:T(8,128)(2,1)S(1)}, bf16[720,128]{1,0:T(8,128)(2,1)S(1)}, u32[]{:S(2)}, u32[]{:S(2)}) collective-permute-start(bf16[720,128]{1,0:T(8,128)(2,1)S(1)} %add_convert_fusion.2), channel_id=1, source_target_pairs={{0,4},{4,8},{8,12},{12,14},{14,10},{10,6},{6,2},{2,0},{1,5},{5,9},... | collective-permute-start | bytes 552968 | tf_op jit(solution)/shard_map/ppermute | solution.py:396
  42.3 6.0 %collective-permute-start.18 = (bf16[1440,128]{1,0:T(8,128)(2,1)S(1)}, bf16[1440,128]{1,0:T(8,128)(2,1)S(1)}, u32[]{:S(2)}, u32[]{:S(2)}) collective-permute-start(bf16[1440,128]{1,0:T(8,128)(2,1)S(1)} %get-tuple-element.74), channel_id=1, source_target_pairs={{0,1},{1,0},{2,3},{3,2},{4,5},{5,4},{6,7},{7,6},{8,9},{9,8},{10,11... | collective-permute-start | bytes 1105928 | tf_op jit(solution)/shard_map/ppermute | solution.py:394
  42.5 7.1 %collective-permute-start.22 = (bf16[720,128]{1,0:T(8,128)(2,1)S(1)}, bf16[720,128]{1,0:T(8,128)(2,1)S(1)}, u32[]{:S(2)}, u32[]{:S(2)}) collective-permute-start(bf16[720,128]{1,0:T(8,128)(2,1)S(1)} %shard_map.73), channel_id=1, source_target_pairs={{4,0},{8,4},{12,8},{14,12},{10,14},{6,10},{2,6},{0,2},{5,1},{9,5},... | collective-permute-start | bytes 552968 | tf_op jit(solution)/shard_map/ppermute | solution.py:403
  46.4 5.6 %collective-permute-start.25 = (bf16[720,128]{1,0:T(8,128)(2,1)S(1)}, bf16[720,128]{1,0:T(8,128)(2,1)S(1)}, u32[]{:S(2)}, u32[]{:S(2)}) collective-permute-start(bf16[720,128]{1,0:T(8,128)(2,1)S(1)} %add_convert_fusion.1), channel_id=1, source_target_pairs={{0,4},{4,8},{8,12},{12,14},{14,10},{10,6},{6,2},{2,0},{1,5},{5,9},... | collective-permute-start | bytes 552968 | tf_op jit(solution)/shard_map/ppermute | solution.py:396
  48.2 7.7 %collective-permute-start.17 = (bf16[720,128]{1,0:T(8,128)(2,1)S(1)}, bf16[720,128]{1,0:T(8,128)(2,1)S(1)}, u32[]{:S(2)}, u32[]{:S(2)}) collective-permute-start(bf16[720,128]{1,0:T(8,128)(2,1)S(1)} %get-tuple-element.72), channel_id=1, source_target_pairs={{0,1},{1,0},{2,3},{3,2},{4,5},{5,4},{6,7},{7,6},{8,9},{9,8},{10,11... | collective-permute-start | bytes 552968 | tf_op jit(solution)/shard_map/ppermute | solution.py:399
  49.7 6.3 %collective-permute-start.24 = (bf16[720,128]{1,0:T(8,128)(2,1)S(1)}, bf16[720,128]{1,0:T(8,128)(2,1)S(1)}, u32[]{:S(2)}, u32[]{:S(2)}) collective-permute-start(bf16[720,128]{1,0:T(8,128)(2,1)S(1)} %shard_map.74), channel_id=1, source_target_pairs={{4,0},{8,4},{12,8},{14,12},{10,14},{6,10},{2,6},{0,2},{5,1},{9,5},... | collective-permute-start | bytes 552968 | tf_op jit(solution)/shard_map/ppermute | solution.py:403
  52.1 5.6 %collective-permute-start.26 = (bf16[720,128]{1,0:T(8,128)(2,1)S(1)}, bf16[720,128]{1,0:T(8,128)(2,1)S(1)}, u32[]{:S(2)}, u32[]{:S(2)}) collective-permute-start(bf16[720,128]{1,0:T(8,128)(2,1)S(1)} %add_convert_fusion), channel_id=1, source_target_pairs={{0,4},{4,8},{8,12},{12,14},{14,10},{10,6},{6,2},{2,0},{1,5},{5,9},... | collective-permute-start | bytes 552968 | tf_op jit(solution)/shard_map/ppermute | solution.py:396

commit v20 on v19

--- a/solution.py
+++ b/solution.py
@@ -83,7 +83,7 @@
     )(*[pltpu.with_memory_space_constraint(a, pltpu.HBM) for a in args])
 
 
-PIECES = 3
+PIECES = 6
 
 
 def pieces(hidden):

time: 58.6 us -> 58.7 us (level)
  no operation moved by 1% of the time
where the time goes in v20:
time: 58.7 us; the launch traced here: 58.6 us
  Pallas kernels  23.2 us (40%)
  starting transfers between devices  19.2 us (33%)
  waiting for transfers between devices  15.5 us (26%)
    pallas_call x6, Pallas kernels, call(): pl.pallas_call(kernel, out_shape=out_shape, in_specs=[pl.BlockSpec(memory...  13.5 us
    ppermute x4, waiting for transfers between devices, ring_body(): behind = lax.ppermute(to_ahead, 'ep', ahead)  8.92 us
    ppermute x4, starting transfers between devices, ring_body(): behind = lax.ppermute(to_ahead, 'ep', ahead)  7.13 us
    ppermute x3, starting transfers between devices, ring_body(): came[k] = lax.ppermute(came[k - 1], 'ep', ahead)  5.64 us
    pallas_call x1, Pallas kernels, turn_weights(): pl.pallas_call(turn_kernel, out_shape=[in_vmem((width, hidden))] * 2, in_...  4.79 us
    ppermute x3, waiting for transfers between devices, ring_body(): front = lax.ppermute(to_back, 'ep', back)  3.32 us
    ppermute x1, starting transfers between devices, ring_body(): came[1] = lax.ppermute(packed, 'ep', ahead)  3.08 us
    pallas_call x1, Pallas kernels, halve_weights(): pl.pallas_call(halve_kernel, out_shape=[in_vmem((hidden, width // 2))] *...  2.92 us
  transfers between devices with their start and end apart: 27, of which 10 were waited for; matrix products, arithmetic and copies ran while one was open for 1% of the time, Pallas kernels for 33%

profile of v20, /device:TPU:0, one launch (start us, length us, event | category | flops | bytes accessed | tf_op | source)
XLA Modules:
  0.0 58.6 jit_solution(2240229246077685127)
XLA Ops:
  0.0 1.1 %shard_map.64.refs_0_ = bf16[736,128]{1,0:T(8,128)(2,1)S(1)} custom-call(bf16[64,1440]{1,0:T(8,128)(2,1)} %tokens_in.1, s32[4,64]{1,0:T(4,128)} %bitcast.14, f32[4,64]{1,0:T(4,128)} %bitcast.15), custom_call_target="tpu_custom_call" | custom-call | tf_op jit(solution)/shard_map/pallas_call | solution.py:76
  1.1 3.1 %collective-permute-start = (bf16[736,128]{1,0:T(8,128)(2,1)S(1)}, bf16[736,128]{1,0:T(8,128)(2,1)S(1)}, u32[]{:S(2)}, u32[]{:S(2)}) collective-permute-start(bf16[736,128]{1,0:T(8,128)(2,1)S(1)} %shard_map.64.refs_0_), channel_id=1, source_target_pairs={{0,4},{4,8},{8,12},{12,14},{14,10},{10,6},{6,2},{2,0},{1,5},{5,9},... | collective-permute-start | bytes 565256 | tf_op jit(solution)/shard_map/ppermute | solution.py:369
  4.2 0.0 collective-permute-start.3
  4.2 0.1 pad_add_fusion.after_this.place
  4.3 4.8 %shard_map.65 = (bf16[2880,720]{1,0:T(8,128)(2,1)S(1)}, bf16[2880,720]{1,0:T(8,128)(2,1)S(1)}) custom-call(s32[2]{0:T(128)S(1)} %pad_add_fusion.after_this.place, bf16[720,2880]{1,0:T(8,128)(2,1)} %bitcast.11, bf16[720,2880]{1,0:T(8,128)(2,1)} %bitcast.12), custom_call_target="tpu_custom_call" | custom-call | bytes 16588800 | tf_op jit(solution)/shard_map/pallas_call | solution.py:109
  9.0 0.0 collective-permute-done.refs_0_
  9.1 2.1 %collective-permute-start.1 = (bf16[736,128]{1,0:T(8,128)(2,1)S(1)}, bf16[736,128]{1,0:T(8,128)(2,1)S(1)}, u32[]{:S(2)}, u32[]{:S(2)}) collective-permute-start(bf16[736,128]{1,0:T(8,128)(2,1)S(1)} %collective-permute-done.refs_0_), channel_id=1, source_target_pairs={{0,4},{4,8},{8,12},{12,14},{14,10},{10,6},{6,2},{2,0},{1,5},{5,9},... | collective-permute-start | bytes 565256 | tf_op jit(solution)/shard_map/ppermute | solution.py:374
  11.1 0.0 collective-permute-start.7
  11.1 0.0 collective-permute-start.4
  11.2 0.5 collective-permute-start.5
  11.7 2.9 %shard_map.66 = (bf16[720,1440]{1,0:T(8,128)(2,1)S(1)}, bf16[720,1440]{1,0:T(8,128)(2,1)S(1)}) custom-call(s32[2]{0:T(128)S(1)} %pad_add_fusion.after_this.place, bf16[720,2880]{1,0:T(8,128)(2,1)} %bitcast.13), custom_call_target="tpu_custom_call" | custom-call | bytes 16588800 | tf_op jit(solution)/shard_map/pallas_call | solution.py:146
  14.6 0.7 %collective-permute-done.1.refs_0_ = bf16[736,128]{1,0:T(8,128)(2,1)S(1)} collective-permute-done((bf16[736,128]{1,0:T(8,128)(2,1)S(1)}, bf16[736,128]{1,0:T(8,128)(2,1)S(1)}, u32[]{:S(2)}, u32[]{:S(2)}) %collective-permute-start.1) | collective-permute-done | bytes 188448 | tf_op jit(solution)/shard_map/ppermute | solution.py:374
  15.3 1.7 %collective-permute-start.2 = (bf16[736,128]{1,0:T(8,128)(2,1)S(1)}, bf16[736,128]{1,0:T(8,128)(2,1)S(1)}, u32[]{:S(2)}, u32[]{:S(2)}) collective-permute-start(bf16[736,128]{1,0:T(8,128)(2,1)S(1)} %collective-permute-done.1.refs_0_), channel_id=1, source_target_pairs={{0,4},{4,8},{8,12},{12,14},{14,10},{10,6},{6,2},{2,0},{1,5},{5,9},... | collective-permute-start | bytes 565256 | tf_op jit(solution)/shard_map/ppermute | solution.py:374
  17.0 0.0 collective-permute-start.8
  17.0 0.0 collective-permute-done.7.refs_1_
  17.0 0.3 collective-permute-start.10
  17.3 0.0 collective-permute-done.4.refs_2_
  17.3 0.3 collective-permute-start.9
  17.6 2.8 %shard_map.67 = (bf16[1440,128]{1,0:T(8,128)(2,1)S(1)}, bf16[1440,128]{1,0:T(8,128)(2,1)S(1)}) custom-call(s32[2]{0:T(128)S(1)} %pad_add_fusion.after_this.place, bf16[736,128]{1,0:T(8,128)(2,1)S(1)} %collective-permute-done.refs_0_, bf16[736,128]{1,0:T(8,128)(2,1)S(1)} %collective-permute-done.3.refs_1_, ...), custom_call_target="tpu_custom_call" | custom-call | flops 1592524800 | bytes 12441600 | tf_op jit(solution)/shard_map/pallas_call | solution.py:245
  20.4 1.1 %collective-permute-done.2.refs_1_ = bf16[736,128]{1,0:T(8,128)(2,1)S(1)} collective-permute-done((bf16[736,128]{1,0:T(8,128)(2,1)S(1)}, bf16[736,128]{1,0:T(8,128)(2,1)S(1)}, u32[]{:S(2)}, u32[]{:S(2)}) %collective-permute-start.2) | collective-permute-done | bytes 188448 | tf_op jit(solution)/shard_map/ppermute | solution.py:374
  21.5 1.8 %collective-permute-start.6 = (bf16[736,128]{1,0:T(8,128)(2,1)S(1)}, bf16[736,128]{1,0:T(8,128)(2,1)S(1)}, u32[]{:S(2)}, u32[]{:S(2)}) collective-permute-start(bf16[736,128]{1,0:T(8,128)(2,1)S(1)} %collective-permute-done.2.refs_1_), channel_id=1, source_target_pairs={{0,4},{4,8},{8,12},{12,14},{14,10},{10,6},{6,2},{2,0},{1,5},{5,9},... | collective-permute-start | bytes 565256 | tf_op jit(solution)/shard_map/ppermute | solution.py:374
  23.3 0.0 collective-permute-start.12
  23.3 0.9 %collective-permute-done.10.refs_2_ = bf16[736,128]{1,0:T(8,128)(2,1)S(1)} collective-permute-done((bf16[736,128]{1,0:T(8,128)(2,1)S(1)}, bf16[736,128]{1,0:T(8,128)(2,1)S(1)}, u32[]{:S(2)}, u32[]{:S(2)}) %collective-permute-start.10) | collective-permute-done | bytes 188448 | tf_op jit(solution)/shard_map/ppermute | solution.py:376
  24.2 0.0 collective-permute-start.13
  24.2 2.8 %shard_map.68 = (bf16[1440,128]{1,0:T(8,128)(2,1)S(1)}, bf16[1440,128]{1,0:T(8,128)(2,1)S(1)}) custom-call(s32[2]{0:T(128)S(1)} %pad_add_fusion.after_this.place, bf16[736,128]{1,0:T(8,128)(2,1)S(1)} %collective-permute-done.1.refs_0_, bf16[736,128]{1,0:T(8,128)(2,1)S(1)} %collective-permute-done.7.refs_1_, ...), custom_call_target="tpu_custom_call" | custom-call | flops 1592524800 | bytes 12441600 | tf_op jit(solution)/shard_map/pallas_call | solution.py:245
  27.0 0.5 collective-permute-done.6.refs_0_
  27.5 0.1 collective-permute-start.11
  27.6 1.7 %shard_map.69 = (f32[192,720]{1,0:T(8,128)S(1)}, f32[192,720]{1,0:T(8,128)S(1)}) custom-call(s32[2]{0:T(128)S(1)} %pad_add_fusion.after_this.place, bf16[736,128]{1,0:T(8,128)(2,1)S(1)} %collective-permute-done.6.refs_0_, bf16[736,128]{1,0:T(8,128)(2,1)S(1)} %collective-permute-done.2.refs_1_, bf16[736,128]{1,0:T(8,128)(2,1)S(1)} %collective-permute-done.10.refs_2_, ...), custom_call_target="tpu_custom_call" | custom-call | flops 796262400 | bytes 6220800 | tf_op jit(solution)/shard_map/pallas_call | solution.py:245
  29.2 0.0 collective-permute-done.13.refs_5_
  29.2 0.0 collective-permute-done.12.refs_4_
  29.2 2.3 %shard_map.70 = (bf16[192,720]{1,0:T(8,128)(2,1)S(1)}, bf16[720,128]{1,0:T(8,128)(2,1)S(1)}, bf16[1440,128]{1,0:T(8,128)(2,1)S(1)}) custom-call(s32[2]{0:T(128)S(1)} %pad_add_fusion.after_this.place, bf16[736,128]{1,0:T(8,128)(2,1)S(1)} %collective-permute-done.6.refs_0_, bf16[736,128]{1,0:T(8,128)(2,1)S(1)} %collective-permute-done.2.refs_1_, ...), custom_call_target="tpu_custom_call" | custom-call | flops 1194393600 | bytes 9331200 | tf_op jit(solution)/shard_map/pallas_call | solution.py:245
  31.5 0.5 collective-permute-start.14
  32.0 0.1 collective-permute-start.15
  32.1 0.4 collective-permute-start.16
  32.5 1.3 %shard_map.71 = (bf16[720,128]{1,0:T(8,128)(2,1)S(1)}, bf16[1440,128]{1,0:T(8,128)(2,1)S(1)}) custom-call(s32[2]{0:T(128)S(1)} %pad_add_fusion.after_this.place, bf16[736,128]{1,0:T(8,128)(2,1)S(1)} %collective-permute-done.6.refs_0_, bf16[736,128]{1,0:T(8,128)(2,1)S(1)} %collective-permute-done.2.refs_1_, ...), custom_call_target="tpu_custom_call" | custom-call | flops 398131200 | bytes 3110400 | tf_op jit(solution)/shard_map/pallas_call | solution.py:245
  33.8 0.0 collective-permute-done.14
  33.8 0.1 add_convert_fusion.4
  33.9 1.8 %collective-permute-start.21 = (bf16[720,128]{1,0:T(8,128)(2,1)S(1)}, bf16[720,128]{1,0:T(8,128)(2,1)S(1)}, u32[]{:S(2)}, u32[]{:S(2)}) collective-permute-start(bf16[720,128]{1,0:T(8,128)(2,1)S(1)} %add_convert_fusion.4), channel_id=1, source_target_pairs={{0,4},{4,8},{8,12},{12,14},{14,10},{10,6},{6,2},{2,0},{1,5},{5,9},... | collective-permute-start | bytes 552968 | tf_op jit(solution)/shard_map/ppermute | solution.py:396
  35.7 0.0 collective-permute-done.15
  35.7 0.1 add_convert_fusion.3
  35.7 0.3 collective-permute-start.20
  36.1 2.7 %shard_map.72 = (bf16[720,128]{1,0:T(8,128)(2,1)S(1)}, bf16[720,128]{1,0:T(8,128)(2,1)S(1)}) custom-call(s32[2]{0:T(128)S(1)} %pad_add_fusion.after_this.place, bf16[736,128]{1,0:T(8,128)(2,1)S(1)} %shard_map.64.refs_0_, bf16[736,128]{1,0:T(8,128)(2,1)S(1)} %collective-permute-done.16.refs_1_, ...), custom_call_target="tpu_custom_call" | custom-call | flops 1592524800 | bytes 12441600 | tf_op jit(solution)/shard_map/pallas_call | solution.py:245
  38.8 1.8 %collective-permute-done.21 = bf16[720,128]{1,0:T(8,128)(2,1)S(1)} collective-permute-done((bf16[720,128]{1,0:T(8,128)(2,1)S(1)}, bf16[720,128]{1,0:T(8,128)(2,1)S(1)}, u32[]{:S(2)}, u32[]{:S(2)}) %collective-permute-start.21) | collective-permute-done | bytes 184352 | tf_op jit(solution)/shard_map/ppermute | solution.py:396
  40.6 0.1 add_convert_fusion.2
  40.6 1.8 %collective-permute-start.23 = (bf16[720,128]{1,0:T(8,128)(2,1)S(1)}, bf16[720,128]{1,0:T(8,128)(2,1)S(1)}, u32[]{:S(2)}, u32[]{:S(2)}) collective-permute-start(bf16[720,128]{1,0:T(8,128)(2,1)S(1)} %add_convert_fusion.2), channel_id=1, source_target_pairs={{0,4},{4,8},{8,12},{12,14},{14,10},{10,6},{6,2},{2,0},{1,5},{5,9},... | collective-permute-start | bytes 552968 | tf_op jit(solution)/shard_map/ppermute | solution.py:396
  42.4 0.1 collective-permute-start.18
  42.6 0.1 shard_map.73
  42.6 0.3 collective-permute-start.22
  43.0 3.5 %collective-permute-done.23 = bf16[720,128]{1,0:T(8,128)(2,1)S(1)} collective-permute-done((bf16[720,128]{1,0:T(8,128)(2,1)S(1)}, bf16[720,128]{1,0:T(8,128)(2,1)S(1)}, u32[]{:S(2)}, u32[]{:S(2)}) %collective-permute-start.23) | collective-permute-done | bytes 184352 | tf_op jit(solution)/shard_map/ppermute | solution.py:396
  46.5 0.1 add_convert_fusion.1
  46.6 1.8 %collective-permute-start.25 = (bf16[720,128]{1,0:T(8,128)(2,1)S(1)}, bf16[720,128]{1,0:T(8,128)(2,1)S(1)}, u32[]{:S(2)}, u32[]{:S(2)}) collective-permute-start(bf16[720,128]{1,0:T(8,128)(2,1)S(1)} %add_convert_fusion.1), channel_id=1, source_target_pairs={{0,4},{4,8},{8,12},{12,14},{14,10},{10,6},{6,2},{2,0},{1,5},{5,9},... | collective-permute-start | bytes 552968 | tf_op jit(solution)/shard_map/ppermute | solution.py:396
  48.4 0.1 collective-permute-start.17
  48.4 0.0 collective-permute-done.18
  48.5 1.2 %collective-permute-done.22.refs_2_ = bf16[720,128]{1,0:T(8,128)(2,1)S(1)} collective-permute-done((bf16[720,128]{1,0:T(8,128)(2,1)S(1)}, bf16[720,128]{1,0:T(8,128)(2,1)S(1)}, u32[]{:S(2)}, u32[]{:S(2)}) %collective-permute-start.22) | collective-permute-done | bytes 184352 | tf_op jit(solution)/shard_map/ppermute | solution.py:403
  49.7 0.1 shard_map.74
  49.8 0.3 collective-permute-start.24
  50.1 2.0 %collective-permute-done.25 = bf16[720,128]{1,0:T(8,128)(2,1)S(1)} collective-permute-done((bf16[720,128]{1,0:T(8,128)(2,1)S(1)}, bf16[720,128]{1,0:T(8,128)(2,1)S(1)}, u32[]{:S(2)}, u32[]{:S(2)}) %collective-permute-start.25) | collective-permute-done | bytes 184352 | tf_op jit(solution)/shard_map/ppermute | solution.py:396
  52.1 0.1 add_convert_fusion
  52.2 1.8 %collective-permute-start.26 = (bf16[720,128]{1,0:T(8,128)(2,1)S(1)}, bf16[720,128]{1,0:T(8,128)(2,1)S(1)}, u32[]{:S(2)}, u32[]{:S(2)}) collective-permute-start(bf16[720,128]{1,0:T(8,128)(2,1)S(1)} %add_convert_fusion), channel_id=1, source_target_pairs={{0,4},{4,8},{8,12},{12,14},{14,10},{10,6},{6,2},{2,0},{1,5},{5,9},... | collective-permute-start | bytes 552968 | tf_op jit(solution)/shard_map/ppermute | solution.py:396
  54.0 2.1 %collective-permute-done.24.refs_2_ = bf16[720,128]{1,0:T(8,128)(2,1)S(1)} collective-permute-done((bf16[720,128]{1,0:T(8,128)(2,1)S(1)}, bf16[720,128]{1,0:T(8,128)(2,1)S(1)}, u32[]{:S(2)}, u32[]{:S(2)}) %collective-permute-start.24) | collective-permute-done | bytes 184352 | tf_op jit(solution)/shard_map/ppermute | solution.py:403
  56.1 0.0 collective-permute-done.17.refs_1_
  56.1 0.1 shard_map.75.a
  56.2 1.7 %collective-permute-done.26.b = bf16[720,128]{1,0:T(8,128)(2,1)S(1)} collective-permute-done((bf16[720,128]{1,0:T(8,128)(2,1)S(1)}, bf16[720,128]{1,0:T(8,128)(2,1)S(1)}, u32[]{:S(2)}, u32[]{:S(2)}) %collective-permute-start.26) | collective-permute-done | bytes 184352 | tf_op jit(solution)/shard_map/ppermute | solution.py:396
  57.8 0.8 %shard_map.76 = bf16[64,1440]{1,0:T(8,128)(2,1)} custom-call(bf16[720,128]{1,0:T(8,128)(2,1)S(1)} %shard_map.75.a, bf16[720,128]{1,0:T(8,128)(2,1)S(1)} %collective-permute-done.26.b), custom_call_target="tpu_custom_call" | custom-call | tf_op jit(solution)/shard_map/pallas_call | solution.py:331
  (13 shorter events, 0.1 us)
Async XLA Ops:
  1.1 8.0 %collective-permute-start = (bf16[736,128]{1,0:T(8,128)(2,1)S(1)}, bf16[736,128]{1,0:T(8,128)(2,1)S(1)}, u32[]{:S(2)}, u32[]{:S(2)}) collective-permute-start(bf16[736,128]{1,0:T(8,128)(2,1)S(1)} %shard_map.64.refs_0_), channel_id=1, source_target_pairs={{0,4},{4,8},{8,12},{12,14},{14,10},{10,6},{6,2},{2,0},{1,5},{5,9},... | collective-permute-start | bytes 565256 | tf_op jit(solution)/shard_map/ppermute | solution.py:369
  4.2 7.0 %collective-permute-start.3 = (bf16[736,128]{1,0:T(8,128)(2,1)S(1)}, bf16[736,128]{1,0:T(8,128)(2,1)S(1)}, u32[]{:S(2)}, u32[]{:S(2)}) collective-permute-start(bf16[736,128]{1,0:T(8,128)(2,1)S(1)} %shard_map.64.refs_0_), channel_id=1, source_target_pairs={{4,0},{8,4},{12,8},{14,12},{10,14},{6,10},{2,6},{0,2},{5,1},{9,5},... | collective-permute-start | bytes 565256 | tf_op jit(solution)/shard_map/ppermute | solution.py:370
  9.1 6.2 %collective-permute-start.1 = (bf16[736,128]{1,0:T(8,128)(2,1)S(1)}, bf16[736,128]{1,0:T(8,128)(2,1)S(1)}, u32[]{:S(2)}, u32[]{:S(2)}) collective-permute-start(bf16[736,128]{1,0:T(8,128)(2,1)S(1)} %collective-permute-done.refs_0_), channel_id=1, source_target_pairs={{0,4},{4,8},{8,12},{12,14},{14,10},{10,6},{6,2},{2,0},{1,5},{5,9},... | collective-permute-start | bytes 565256 | tf_op jit(solution)/shard_map/ppermute | solution.py:374
  11.1 5.9 %collective-permute-start.7 = (bf16[736,128]{1,0:T(8,128)(2,1)S(1)}, bf16[736,128]{1,0:T(8,128)(2,1)S(1)}, u32[]{:S(2)}, u32[]{:S(2)}) collective-permute-start(bf16[736,128]{1,0:T(8,128)(2,1)S(1)} %collective-permute-done.3.refs_1_), channel_id=1, source_target_pairs={{4,0},{8,4},{12,8},{14,12},{10,14},{6,10},{2,6},{0,2},{5,1},{9,5},... | collective-permute-start | bytes 565256 | tf_op jit(solution)/shard_map/ppermute | solution.py:376
  11.1 6.2 %collective-permute-start.4 = (bf16[736,128]{1,0:T(8,128)(2,1)S(1)}, bf16[736,128]{1,0:T(8,128)(2,1)S(1)}, u32[]{:S(2)}, u32[]{:S(2)}) collective-permute-start(bf16[736,128]{1,0:T(8,128)(2,1)S(1)} %collective-permute-done.refs_0_), channel_id=1, source_target_pairs={{0,1},{1,0},{2,3},{3,2},{4,5},{5,4},{6,7},{7,6},{8,9},{9,8},{10,11... | collective-permute-start | bytes 565256 | tf_op jit(solution)/shard_map/ppermute | solution.py:377
  11.2 6.5 %collective-permute-start.5 = (bf16[736,128]{1,0:T(8,128)(2,1)S(1)}, bf16[736,128]{1,0:T(8,128)(2,1)S(1)}, u32[]{:S(2)}, u32[]{:S(2)}) collective-permute-start(bf16[736,128]{1,0:T(8,128)(2,1)S(1)} %collective-permute-done.3.refs_1_), channel_id=1, source_target_pairs={{0,1},{1,0},{2,3},{3,2},{4,5},{5,4},{6,7},{7,6},{8,9},{9,8},{10,11... | collective-permute-start | bytes 565256 | tf_op jit(solution)/shard_map/ppermute | solution.py:377
  15.3 6.2 %collective-permute-start.2 = (bf16[736,128]{1,0:T(8,128)(2,1)S(1)}, bf16[736,128]{1,0:T(8,128)(2,1)S(1)}, u32[]{:S(2)}, u32[]{:S(2)}) collective-permute-start(bf16[736,128]{1,0:T(8,128)(2,1)S(1)} %collective-permute-done.1.refs_0_), channel_id=1, source_target_pairs={{0,4},{4,8},{8,12},{12,14},{14,10},{10,6},{6,2},{2,0},{1,5},{5,9},... | collective-permute-start | bytes 565256 | tf_op jit(solution)/shard_map/ppermute | solution.py:374
  17.0 7.2 %collective-permute-start.8 = (bf16[736,128]{1,0:T(8,128)(2,1)S(1)}, bf16[736,128]{1,0:T(8,128)(2,1)S(1)}, u32[]{:S(2)}, u32[]{:S(2)}) collective-permute-start(bf16[736,128]{1,0:T(8,128)(2,1)S(1)} %collective-permute-done.1.refs_0_), channel_id=1, source_target_pairs={{0,1},{1,0},{2,3},{3,2},{4,5},{5,4},{6,7},{7,6},{8,9},{9,8},{10,11... | collective-permute-start | bytes 565256 | tf_op jit(solution)/shard_map/ppermute | solution.py:377
  17.0 7.1 %collective-permute-start.10 = (bf16[736,128]{1,0:T(8,128)(2,1)S(1)}, bf16[736,128]{1,0:T(8,128)(2,1)S(1)}, u32[]{:S(2)}, u32[]{:S(2)}) collective-permute-start(bf16[736,128]{1,0:T(8,128)(2,1)S(1)} %collective-permute-done.7.refs_1_), channel_id=1, source_target_pairs={{4,0},{8,4},{12,8},{14,12},{10,14},{6,10},{2,6},{0,2},{5,1},{9,5},... | collective-permute-start | bytes 565256 | tf_op jit(solution)/shard_map/ppermute | solution.py:376
  17.3 6.9 %collective-permute-start.9 = (bf16[736,128]{1,0:T(8,128)(2,1)S(1)}, bf16[736,128]{1,0:T(8,128)(2,1)S(1)}, u32[]{:S(2)}, u32[]{:S(2)}) collective-permute-start(bf16[736,128]{1,0:T(8,128)(2,1)S(1)} %collective-permute-done.7.refs_1_), channel_id=1, source_target_pairs={{0,1},{1,0},{2,3},{3,2},{4,5},{5,4},{6,7},{7,6},{8,9},{9,8},{10,11... | collective-permute-start | bytes 565256 | tf_op jit(solution)/shard_map/ppermute | solution.py:377
  21.5 6.0 %collective-permute-start.6 = (bf16[736,128]{1,0:T(8,128)(2,1)S(1)}, bf16[736,128]{1,0:T(8,128)(2,1)S(1)}, u32[]{:S(2)}, u32[]{:S(2)}) collective-permute-start(bf16[736,128]{1,0:T(8,128)(2,1)S(1)} %collective-permute-done.2.refs_1_), channel_id=1, source_target_pairs={{0,4},{4,8},{8,12},{12,14},{14,10},{10,6},{6,2},{2,0},{1,5},{5,9},... | collective-permute-start | bytes 565256 | tf_op jit(solution)/shard_map/ppermute | solution.py:374
  23.3 5.9 %collective-permute-start.12 = (bf16[736,128]{1,0:T(8,128)(2,1)S(1)}, bf16[736,128]{1,0:T(8,128)(2,1)S(1)}, u32[]{:S(2)}, u32[]{:S(2)}) collective-permute-start(bf16[736,128]{1,0:T(8,128)(2,1)S(1)} %collective-permute-done.2.refs_1_), channel_id=1, source_target_pairs={{0,1},{1,0},{2,3},{3,2},{4,5},{5,4},{6,7},{7,6},{8,9},{9,8},{10,11... | collective-permute-start | bytes 565256 | tf_op jit(solution)/shard_map/ppermute | solution.py:377
  24.2 5.0 %collective-permute-start.13 = (bf16[736,128]{1,0:T(8,128)(2,1)S(1)}, bf16[736,128]{1,0:T(8,128)(2,1)S(1)}, u32[]{:S(2)}, u32[]{:S(2)}) collective-permute-start(bf16[736,128]{1,0:T(8,128)(2,1)S(1)} %collective-permute-done.10.refs_2_), channel_id=1, source_target_pairs={{0,1},{1,0},{2,3},{3,2},{4,5},{5,4},{6,7},{7,6},{8,9},{9,8},{10,11... | collective-permute-start | bytes 565256 | tf_op jit(solution)/shard_map/ppermute | solution.py:377
  27.5 1.7 %collective-permute-start.11 = (bf16[736,128]{1,0:T(8,128)(2,1)S(1)}, bf16[736,128]{1,0:T(8,128)(2,1)S(1)}, u32[]{:S(2)}, u32[]{:S(2)}) collective-permute-start(bf16[736,128]{1,0:T(8,128)(2,1)S(1)} %collective-permute-done.6.refs_0_), channel_id=1, source_target_pairs={{0,1},{1,0},{2,3},{3,2},{4,5},{5,4},{6,7},{7,6},{8,9},{9,8},{10,11... | collective-permute-start | bytes 565256 | tf_op jit(solution)/shard_map/ppermute | solution.py:385
  31.5 2.3 %collective-permute-start.14 = (bf16[720,128]{1,0:T(8,128)(2,1)S(1)}, bf16[720,128]{1,0:T(8,128)(2,1)S(1)}, u32[]{:S(2)}, u32[]{:S(2)}) collective-permute-start(bf16[720,128]{1,0:T(8,128)(2,1)S(1)} %get-tuple-element.66), channel_id=1, source_target_pairs={{0,1},{1,0},{2,3},{3,2},{4,5},{5,4},{6,7},{7,6},{8,9},{9,8},{10,11... | collective-permute-start | bytes 552968 | tf_op jit(solution)/shard_map/ppermute | solution.py:294
  32.0 3.6 %collective-permute-start.15 = (bf16[1440,128]{1,0:T(8,128)(2,1)S(1)}, bf16[1440,128]{1,0:T(8,128)(2,1)S(1)}, u32[]{:S(2)}, u32[]{:S(2)}) collective-permute-start(bf16[1440,128]{1,0:T(8,128)(2,1)S(1)} %get-tuple-element.68), channel_id=1, source_target_pairs={{0,1},{1,0},{2,3},{3,2},{4,5},{5,4},{6,7},{7,6},{8,9},{9,8},{10,11... | collective-permute-start | bytes 1105928 | tf_op jit(solution)/shard_map/ppermute | solution.py:294
  32.1 4.0 %collective-permute-start.16 = (bf16[736,128]{1,0:T(8,128)(2,1)S(1)}, bf16[736,128]{1,0:T(8,128)(2,1)S(1)}, u32[]{:S(2)}, u32[]{:S(2)}) collective-permute-start(bf16[736,128]{1,0:T(8,128)(2,1)S(1)} %shard_map.64.refs_0_), channel_id=1, source_target_pairs={{0,1},{1,0},{2,3},{3,2},{4,5},{5,4},{6,7},{7,6},{8,9},{9,8},{10,11... | collective-permute-start | bytes 565256 | tf_op jit(solution)/shard_map/ppermute | solution.py:386
  33.9 6.7 %collective-permute-start.21 = (bf16[720,128]{1,0:T(8,128)(2,1)S(1)}, bf16[720,128]{1,0:T(8,128)(2,1)S(1)}, u32[]{:S(2)}, u32[]{:S(2)}) collective-permute-start(bf16[720,128]{1,0:T(8,128)(2,1)S(1)} %add_convert_fusion.4), channel_id=1, source_target_pairs={{0,4},{4,8},{8,12},{12,14},{14,10},{10,6},{6,2},{2,0},{1,5},{5,9},... | collective-permute-start | bytes 552968 | tf_op jit(solution)/shard_map/ppermute | solution.py:396
  35.7 6.8 %collective-permute-start.20 = (bf16[720,128]{1,0:T(8,128)(2,1)S(1)}, bf16[720,128]{1,0:T(8,128)(2,1)S(1)}, u32[]{:S(2)}, u32[]{:S(2)}) collective-permute-start(bf16[720,128]{1,0:T(8,128)(2,1)S(1)} %add_convert_fusion.3), channel_id=1, source_target_pairs={{4,0},{8,4},{12,8},{14,12},{10,14},{6,10},{2,6},{0,2},{5,1},{9,5},... | collective-permute-start | bytes 552968 | tf_op jit(solution)/shard_map/ppermute | solution.py:403
  36.1 6.5 %collective-permute-start.19 = (bf16[1440,128]{1,0:T(8,128)(2,1)S(1)}, bf16[1440,128]{1,0:T(8,128)(2,1)S(1)}, u32[]{:S(2)}, u32[]{:S(2)}) collective-permute-start(bf16[1440,128]{1,0:T(8,128)(2,1)S(1)} %get-tuple-element.76), channel_id=1, source_target_pairs={{0,1},{1,0},{2,3},{3,2},{4,5},{5,4},{6,7},{7,6},{8,9},{9,8},{10,11... | collective-permute-start | bytes 1105928 | tf_op jit(solution)/shard_map/ppermute | solution.py:394
  40.6 5.8 %collective-permute-start.23 = (bf16[720,128]{1,0:T(8,128)(2,1)S(1)}, bf16[720,128]{1,0:T(8,128)(2,1)S(1)}, u32[]{:S(2)}, u32[]{:S(2)}) collective-permute-start(bf16[720,128]{1,0:T(8,128)(2,1)S(1)} %add_convert_fusion.2), channel_id=1, source_target_pairs={{0,4},{4,8},{8,12},{12,14},{14,10},{10,6},{6,2},{2,0},{1,5},{5,9},... | collective-permute-start | bytes 552968 | tf_op jit(solution)/shard_map/ppermute | solution.py:396
  42.4 6.0 %collective-permute-start.18 = (bf16[1440,128]{1,0:T(8,128)(2,1)S(1)}, bf16[1440,128]{1,0:T(8,128)(2,1)S(1)}, u32[]{:S(2)}, u32[]{:S(2)}) collective-permute-start(bf16[1440,128]{1,0:T(8,128)(2,1)S(1)} %get-tuple-element.74), channel_id=1, source_target_pairs={{0,1},{1,0},{2,3},{3,2},{4,5},{5,4},{6,7},{7,6},{8,9},{9,8},{10,11... | collective-permute-start | bytes 1105928 | tf_op jit(solution)/shard_map/ppermute | solution.py:394
  42.6 7.1 %collective-permute-start.22 = (bf16[720,128]{1,0:T(8,128)(2,1)S(1)}, bf16[720,128]{1,0:T(8,128)(2,1)S(1)}, u32[]{:S(2)}, u32[]{:S(2)}) collective-permute-start(bf16[720,128]{1,0:T(8,128)(2,1)S(1)} %shard_map.73), channel_id=1, source_target_pairs={{4,0},{8,4},{12,8},{14,12},{10,14},{6,10},{2,6},{0,2},{5,1},{9,5},... | collective-permute-start | bytes 552968 | tf_op jit(solution)/shard_map/ppermute | solution.py:403
  46.6 5.6 %collective-permute-start.25 = (bf16[720,128]{1,0:T(8,128)(2,1)S(1)}, bf16[720,128]{1,0:T(8,128)(2,1)S(1)}, u32[]{:S(2)}, u32[]{:S(2)}) collective-permute-start(bf16[720,128]{1,0:T(8,128)(2,1)S(1)} %add_convert_fusion.1), channel_id=1, source_target_pairs={{0,4},{4,8},{8,12},{12,14},{14,10},{10,6},{6,2},{2,0},{1,5},{5,9},... | collective-permute-start | bytes 552968 | tf_op jit(solution)/shard_map/ppermute | solution.py:396
  48.4 7.7 %collective-permute-start.17 = (bf16[720,128]{1,0:T(8,128)(2,1)S(1)}, bf16[720,128]{1,0:T(8,128)(2,1)S(1)}, u32[]{:S(2)}, u32[]{:S(2)}) collective-permute-start(bf16[720,128]{1,0:T(8,128)(2,1)S(1)} %get-tuple-element.72), channel_id=1, source_target_pairs={{0,1},{1,0},{2,3},{3,2},{4,5},{5,4},{6,7},{7,6},{8,9},{9,8},{10,11... | collective-permute-start | bytes 552968 | tf_op jit(solution)/shard_map/ppermute | solution.py:399
  49.8 6.3 %collective-permute-start.24 = (bf16[720,128]{1,0:T(8,128)(2,1)S(1)}, bf16[720,128]{1,0:T(8,128)(2,1)S(1)}, u32[]{:S(2)}, u32[]{:S(2)}) collective-permute-start(bf16[720,128]{1,0:T(8,128)(2,1)S(1)} %shard_map.74), channel_id=1, source_target_pairs={{4,0},{8,4},{12,8},{14,12},{10,14},{6,10},{2,6},{0,2},{5,1},{9,5},... | collective-permute-start | bytes 552968 | tf_op jit(solution)/shard_map/ppermute | solution.py:403
  52.2 5.6 %collective-permute-start.26 = (bf16[720,128]{1,0:T(8,128)(2,1)S(1)}, bf16[720,128]{1,0:T(8,128)(2,1)S(1)}, u32[]{:S(2)}, u32[]{:S(2)}) collective-permute-start(bf16[720,128]{1,0:T(8,128)(2,1)S(1)} %add_convert_fusion), channel_id=1, source_target_pairs={{0,4},{4,8},{8,12},{12,14},{14,10},{10,6},{6,2},{2,0},{1,5},{5,9},... | collective-permute-start | bytes 552968 | tf_op jit(solution)/shard_map/ppermute | solution.py:396
